TPU v7x, 32 devices: a whole 2x2x4 slice. The times are simulated.
32 devices in a mesh: groups: 2 (over y), col: 4 (over z), row: 2 (over x), side: 2 (over core).
Axes of the slice: x: 2, y: 2, z: 4, core: 2. Of those that a mesh axis runs over, the one named last changes fastest.
Arguments:
- hidden_in: bfloat16 [256, 8192], P(('groups', 'col'), 'row'), parts along dimension 0, may hold values from -40 to 40
- norm_gain: bfloat16 [8192], P('row'), may hold values from 0.099609375 to 1.8984375
- qkv_weight: bfloat16 [8192, 10240], P('row', 'col'), may hold values from -0.0625 to 0.0625
- out_weight: bfloat16 [8192, 8192], P('row', 'col'), may hold values from -0.0625 to 0.0625
- key_cache: bfloat16 [256, 64, 1024], P(('groups', 'col'), None, 'row'), parts along dimension 0, may hold values from -320 to 320
- value_cache: bfloat16 [256, 64, 1024], P(('groups', 'col'), None, 'row'), parts along dimension 0, may hold values from -4 to 4
- cache_lengths: int32 [256], P(('groups', 'col')), parts along dimension 0, may hold values from 1 to 64, 4096 in all
- slot_request: int32 [256], P('groups'), parts along dimension 0, may hold values from 0 to 127, each once
Outputs:
- layer_rows: bfloat16 [2, 256, 8192], P('side', ('groups', 'col'), 'row'), parts along dimension 1
There are 2 independent parts, one for each index of `groups`. A program takes and returns all parts, laid end to end along the dimension named above; an argument that names none is the same for every part. Nothing has to cross between parts.
Inputs may be any that keep to these rules, and one draw needn't show every extreme that they name: Slot s of cache_lengths, key_cache and value_cache belongs to request slot_request[s]; every request has exactly one slot. Positions from cache_lengths[s] on are not filled; some slot is full in every draw.
All inputs are finite; a program needn't handle non-finite values. No bound on the sum of `cache_lengths` on one device may be relied on, other than what follows from the above.
Results may differ from a plain program's by a relative error of at most 0.035.
Values may be sent and summed in bfloat16 or wider, within the bound.
No kernel may reach another device: no remote copies, remote signals or barrier semaphores. Data moves between devices by JAX's collectives and lax.ppermute only.
A program may use at most 128 MiB of HBM per device.

v0:
```python
import jax
import jax.numpy as jnp
from jax import lax
from jax.sharding import PartitionSpec as P

D = 8192
HEADS = 64
KV_HEADS = 8
HEAD_DIM = 128
QKV = 10240


EPSILON = 1e-05
THETA = 500000.0


def swapped(value, axis, bit):
    mask = 2**bit
    pairs = [(source, source ^ mask) for source in range(lax.axis_size(axis))]
    return lax.ppermute(value, axis, pairs)


def rope_tables(lengths, head_dim):
    half_dim = head_dim // 2
    inv_freq = jnp.exp(
        -jnp.log(jnp.float32(THETA)) * jnp.arange(half_dim, dtype=jnp.float32) / half_dim
    )
    phases = lengths.astype(jnp.float32)[:, None] * inv_freq[None, :]
    return (jnp.cos(phases), jnp.sin(phases))


def rotate(vector, cos_vals, sine_vals):
    half_dim = vector.shape[-1] // 2
    front_half = vector[..., :half_dim]
    back_half = vector[..., half_dim:]
    return jnp.concatenate(
        [
            front_half * cos_vals - back_half * sine_vals,
            back_half * cos_vals + front_half * sine_vals,
        ],
        axis=-1,
    )


def attend(packed, key_block, value_block, lengths):
    slot_count = packed.shape[0]
    cache_size = key_block.shape[1]
    groups = key_block.shape[2] // HEAD_DIM
    per_group = HEADS // KV_HEADS
    grouped = packed.reshape(slot_count, groups, per_group + 2, HEAD_DIM)
    cos_vals, sine_vals = rope_tables(lengths, HEAD_DIM)
    queries = rotate(
        grouped[:, :, :per_group].astype(jnp.float32),
        cos_vals[:, None, None, :],
        sine_vals[:, None, None, :],
    ).astype(jnp.bfloat16)
    new_keys = rotate(
        grouped[:, :, per_group].astype(jnp.float32), cos_vals[:, None, :], sine_vals[:, None, :]
    ).astype(jnp.bfloat16)
    new_values = grouped[:, :, per_group + 1]
    cache_keys = key_block.reshape(slot_count, cache_size, groups, HEAD_DIM)
    cache_values = value_block.reshape(slot_count, cache_size, groups, HEAD_DIM)
    factor = HEAD_DIM ** (-0.5)
    cache_scores = (
        jnp.einsum("sghd,slgd->sghl", queries, cache_keys, preferred_element_type=jnp.float32)
        * factor
    )
    own_scores = (
        jnp.einsum("sghd,sgd->sgh", queries, new_keys, preferred_element_type=jnp.float32) * factor
    )
    in_cache = lax.broadcasted_iota(jnp.int32, (slot_count, cache_size), 1) < lengths[:, None]
    cache_scores = jnp.where(in_cache[:, None, None, :], cache_scores, -1e30)
    row_max = jnp.maximum(jnp.max(cache_scores, axis=-1), own_scores)
    cache_exp = jnp.exp(cache_scores - row_max[..., None])
    own_exp = jnp.exp(own_scores - row_max)
    denominator = jnp.sum(cache_exp, axis=-1) + own_exp
    cache_weight = (cache_exp / denominator[..., None]).astype(jnp.bfloat16)
    own_weight = (own_exp / denominator).astype(jnp.bfloat16)
    combined = jnp.einsum(
        "sghl,slgd->sghd", cache_weight, cache_values, preferred_element_type=jnp.float32
    )
    combined = (
        combined
        + own_weight.astype(jnp.float32)[..., None] * new_values.astype(jnp.float32)[:, :, None, :]
    )
    return combined.astype(jnp.bfloat16).reshape(slot_count, groups * per_group * HEAD_DIM)


def per_device(
    hidden_in,
    norm_gain,
    qkv_weight,
    out_weight,
    key_cache,
    value_cache,
    cache_lengths,
    slot_request,
):
    side_index = lax.axis_index("side")
    is_weight = side_index == 0
    col_count = lax.axis_size("col")
    row_count = lax.axis_size("row")
    group_cols = col_count // row_count
    in_half = qkv_weight.shape[1] // 2
    out_half = out_weight.shape[1] // 2
    residual = hidden_in.astype(jnp.float32)
    square_sums = lax.psum(jnp.sum(residual * residual, axis=1), "row")
    normed = (
        residual
        * lax.rsqrt(square_sums[:, None] / D + EPSILON)
        * norm_gain.astype(jnp.float32)[None, :]
    ).astype(jnp.bfloat16)
    in_weight = lax.dynamic_slice_in_dim(qkv_weight, side_index * in_half, in_half, 1)
    partial_in = jnp.dot(
        lax.all_gather(normed, "col", axis=0, tiled=True),
        in_weight,
        preferred_element_type=jnp.float32,
    )
    in_slots = jnp.take(partial_in, slot_request, axis=0)
    own_width = QKV // row_count
    summed = lax.psum(in_slots.astype(jnp.bfloat16), "row")
    spread = lax.all_to_all(summed, "col", split_axis=0, concat_axis=1, tiled=True)
    own_columns = lax.dynamic_slice_in_dim(
        spread.reshape(spread.shape[0], col_count, in_half),
        lax.axis_index("row") * group_cols,
        group_cols,
        1,
    )
    slot_half = key_cache.shape[0] // 2
    halves = lax.all_to_all(
        own_columns[:, :, None, :], "side", split_axis=0, concat_axis=2, tiled=True
    )
    arrived = halves.reshape(slot_half, own_width)
    first_slot = side_index * slot_half
    key_part = lax.dynamic_slice_in_dim(key_cache, first_slot, slot_half, 0)
    value_part = lax.dynamic_slice_in_dim(value_cache, first_slot, slot_half, 0)
    length_part = lax.dynamic_slice_in_dim(cache_lengths, first_slot, slot_half, 0)
    attended = attend(arrived, key_part, value_part, length_part)
    out_cols = lax.dynamic_slice_in_dim(out_weight, side_index * out_half, out_half, 1)
    collected = lax.all_gather(attended, ("col", "side"), axis=0, tiled=True)
    out_slots = jnp.dot(collected, out_cols, preferred_element_type=jnp.float32)
    inverse = jnp.argsort(slot_request)
    out_requests = jnp.take(out_slots, inverse, axis=0)
    spread_out = lax.all_to_all(
        out_requests.astype(jnp.bfloat16), "col", split_axis=0, concat_axis=1, tiled=True
    ).astype(out_requests.dtype)
    out_view = spread_out.reshape(spread_out.shape[0], col_count, out_half)
    summed_out = lax.psum_scatter(
        out_view.astype(jnp.bfloat16), "row", scatter_dimension=1, tiled=True
    ).astype(jnp.float32)
    req_rows = hidden_in.shape[0]
    residual_view = residual.reshape(req_rows, group_cols, 2, out_half)
    residual_half = lax.dynamic_index_in_dim(residual_view, side_index, 2, keepdims=False)
    own_hidden = (residual_half + summed_out).astype(jnp.bfloat16)
    payload = jnp.where(is_weight, attended, own_hidden.reshape(attended.shape))
    received = swapped(payload, "side", 0)
    hidden = jnp.stack([own_hidden, received.reshape(own_hidden.shape)], axis=2).reshape(
        req_rows, residual.shape[1]
    )
    attention_rows = jnp.concatenate([received, attended], axis=0)
    result = jnp.where(is_weight, hidden, attention_rows)
    return result[None]


def solution(mesh):
    placed = (
        P(("groups", "col"), "row"),
        P("row"),
        P("row", "col"),
        P("row", "col"),
        P(("groups", "col"), None, "row"),
        P(("groups", "col"), None, "row"),
        P(("groups", "col")),
        P("groups"),
    )
    return jax.shard_map(
        per_device,
        mesh=mesh,
        in_specs=placed,
        out_specs=P("side", ("groups", "col"), "row"),
        check_vma=False,
    )
```

profile of v0, /device:TPU:0, one launch (start us, length us, event | category | flops | bytes accessed | tf_op | source)
XLA Modules:
  0.0 160.1 jit_solution(10407784582039779955)
XLA Ops:
  6.5 0.7 convert_element_type.54
  7.2 1.1 multiply_reduce_fusion
  8.4 5.8 %psum.14 = f32[32]{0:T(128)S(1)} all-reduce(f32[32]{0:T(128)S(1)} %multiply_reduce_fusion), channel_id=1, replica_groups=mesh['groups'=2,'col'=4,'row'=2,'side'=2] {'row'}, use_global_device_ids=true, to_apply=%region_2.3 | all-reduce | flops 32 | bytes 256 | tf_op jit(solution)/shard_map/psum | solution.py:107
  14.2 1.8 %multiply_convert_fusion = bf16[32,4096]{1,0:T(8,128)(2,1)} fusion(f32[4096]{0:T(1024)S(1)} %convert_element_type.54, f32[32]{0:T(128)S(1)} %add_rsqrt_fusion, bf16[32,4096]{1,0:T(8,128)(2,1)} %param.8), kind=kLoop, calls=%fused_computation.18 | loop fusion | flops 524288 | bytes 540800 | tf_op jit(solution)/shard_map/convert_element_type | solution.py:112
  16.1 0.7 compare_select_fusion
  16.7 0.7 compare_and_fusion
  17.4 28.5 %all-gather.3.cloned.1.call-done = bf16[128,4096]{1,0:T(8,128)(2,1)} async-done(((bf16[32,4096]{1,0:T(8,128)(2,1)}), bf16[128,4096]{1,0:T(8,128)(2,1)}) %all-gather.3.cloned.1.call-update) | async-done | bytes 1048592 | tf_op jit(solution)/shard_map/all_gather | solution.py:115
  45.9 5.9 %fusion = bf16[128,1280]{1,0:T(8,128)(2,1)S(1)} fusion(bf16[128,4096]{1,0:T(8,128)(2,1)} %all-gather.3.cloned.1.call-done, bf16[4096,2560]{1,0:T(8,128)(2,1)} %param.10, s32[]{:T(128)S(6)} %select_n.68), kind=kOutput, calls=%fused_computation.2 | convolution fusion | flops 1342177280 | bytes 11862020 | tf_op jit(solution)/shard_map/dot_general | solution.py:114
  51.8 0.9 gather_fusion
  52.7 0.9 select_convert_fusion
  53.6 0.1 fusion.22
  53.7 1.9 %dynamic-slice_bitcast_fusion = (bf16[16,8,4,8,128]{4,3,2,1,0:T(8,128)(2,1)S(1)}, bf16[16,8,4,8,128]{4,3,2,1,0:T(8,128)(2,1)S(1)}) fusion(bf16[32,64,512]{2,1,0:T(8,128)(2,1)} %param.13, s32[]{:T(128)S(6)} %select_n.66, bf16[32,64,512]{2,1,0:T(8,128)(2,1)} %param.12), kind=kLoop, calls=%fused_computation.14 | loop fusion | bytes 4194308
  55.6 21.9 %all-reduce.2.cloned.1.call-done = bf16[4,32,1280]{2,1,0:T(8,128)(2,1)} async-done(((bf16[4,32,1280]{2,1,0:T(8,128)(2,1)}), bf16[4,32,1280]{2,1,0:T(8,128)(2,1)}) %all-reduce.2.cloned.1.call-update) | async-done | bytes 327696 | tf_op jit(solution)/shard_map/psum | solution.py:121
  77.5 4.6 %all-to-all-start = ((bf16[4,32,1280]{2,1,0:T(8,128)(2,1)}), bf16[4,32,1280]{2,1,0:T(8,128)(2,1)S(1)}, u32[]{:S(2)}, u32[]{:S(2)}) async-start(bf16[4,32,1280]{2,1,0:T(8,128)(2,1)} %all-reduce.2.cloned.1.call-done), calls=%async_computation | async-start | bytes 655360 | tf_op jit(solution)/shard_map/all_to_all | solution.py:122
  82.1 0.1 iota_compare_fusion
  82.2 0.1 multiply_cosine_fusion
  82.3 10.1 %all-to-all-done = bf16[4,32,1280]{2,1,0:T(8,128)(2,1)S(1)} async-done(((bf16[4,32,1280]{2,1,0:T(8,128)(2,1)}), bf16[4,32,1280]{2,1,0:T(8,128)(2,1)S(1)}, u32[]{:S(2)}, u32[]{:S(2)}) %all-to-all-start) | async-done | bytes 327712 | tf_op jit(solution)/shard_map/all_to_all | solution.py:122
  92.4 0.2 copy.32
  92.6 3.8 %all_to_all.41 = bf16[32,2,1,1280]{3,1,2,0:T(2,128)(2,1)S(1)} all-to-all(bf16[32,2,1,1280]{3,1,2,0:T(2,128)(2,1)S(1)} %copy.32), channel_id=1, replica_groups=mesh['groups'=2,'col'=4,'row'=2,'side'=2] {'side'}, dimensions={0} | all-to-all | bytes 327680 | tf_op jit(solution)/shard_map/all_to_all | solution.py:130
  96.5 0.1 reshape_reshape.3
  96.7 0.1 subtract_convert_fusion.1
  96.8 0.1 subtract_convert_fusion
  96.9 0.1 maximum_bitcast_fusion
  97.0 0.3 fusion.14
  97.3 0.8 fusion.23
  98.1 0.3 fusion.11
  98.5 0.5 fusion.5
  98.9 0.7 copy.64
  99.7 2.5 %sort.17 = (s32[128]{0:T(128)}, s32[128]{0:T(128)S(1)}) sort(s32[128]{0:T(128)S(1)} %copy-done.2, s32[128]{0:T(128)S(1)} %iota.16), dimensions={0}, to_apply=%region_0.0 | sort | flops 896 | bytes 2048 | tf_op jit(solution)/shard_map/jit(argsort)/sort | solution.py:142
  102.3 0.1 broadcast_in_dim.56
  102.4 17.6 %all-gather.5.cloned.1.call-done = bf16[128,4096]{1,0:T(8,128)(2,1)} async-done(((bf16[16,4096]{1,0:T(8,128)(2,1)}), bf16[128,4096]{1,0:T(8,128)(2,1)}) %all-gather.5.cloned.1.call-update) | async-done | bytes 1048592 | tf_op jit(solution)/shard_map/all_gather | solution.py:140
  120.0 5.0 %fusion.2 = bf16[128,1024]{1,0:T(8,128)(2,1)S(1)} fusion(bf16[128,4096]{1,0:T(8,128)(2,1)} %all-gather.5.cloned.1.call-done, bf16[4096,2048]{1,0:T(8,128)(2,1)} %param.11, s32[]{:T(128)S(6)} %select_n.72), kind=kOutput, calls=%fused_computation.4 | convolution fusion | flops 1073741824 | bytes 9699332 | tf_op jit(solution)/shard_map/dot_general | solution.py:141
  125.0 0.9 gather_fusion.1
  125.9 0.1 select_convert_fusion.1
  126.0 12.6 %all_to_all.42 = bf16[4,32,1024]{2,1,0:T(8,128)(2,1)} all-to-all(bf16[4,32,1024]{2,1,0:T(8,128)(2,1)S(1)} %select_convert_fusion.1), channel_id=1, replica_groups=mesh['groups'=2,'col'=4,'row'=2,'side'=2] {'col'}, dimensions={0} | all-to-all | bytes 524288 | tf_op jit(solution)/shard_map/all_to_all | solution.py:144
  138.6 0.5 reshape.201
  139.1 0.3 constant_dynamic-slice_fusion
  139.4 10.1 %reduce-scatter.2.cloned.1.call-done = bf16[32,2,1024]{2,0,1:T(8,128)(2,1)} async-done(((bf16[32,4,1024]{2,0,1:T(8,128)(2,1)}), bf16[32,2,1024]{2,0,1:T(8,128)(2,1)}) %reduce-scatter.2.cloned.1.call-update) | async-done | bytes 131088 | tf_op jit(solution)/shard_map/reduce_scatter | solution.py:148
  149.5 1.0 fusion.10
  150.5 0.1 copy.38
  150.6 0.1 reshape.205
  150.8 0.1 collective-permute-start
  150.8 0.1 concatenate.25
  150.9 1.3 collective-permute-done
  152.2 0.1 stack_reshape.3
  152.3 0.3 copy.40
  152.6 0.2 reshape.206
  152.8 0.8 maximum_select_fusion
  (31 shorter events, 0.5 us)
Async XLA Ops:
  6.5 47.0 %copy-start.1 = (s32[32]{0:T(128)S(1)}, s32[32]{0:T(128)}, u32[]{:S(2)}) copy-start(s32[32]{0:T(128)} %param.14) | copy-start | bytes 388
  6.5 39.4 %all-gather.3.cloned.1.call-start = ((), (), s32[]{:S(2)}) async-start(), calls=%async_computation.4 | async-start | bytes 1310720 | tf_op jit(solution)/shard_map/all_gather | solution.py:115
  16.0 61.5 %all-reduce.2.cloned.1.call-start = ((), (), s32[]{:S(2)}) async-start(), calls=%async_computation.5 | async-start | bytes 655360 | tf_op jit(solution)/shard_map/psum | solution.py:121
  51.8 47.9 %copy-start.2 = (s32[128]{0:T(128)S(1)}, s32[128]{0:T(128)}, u32[]{:S(2)}) copy-start(s32[128]{0:T(128)} %param.15) | copy-start | bytes 1540
  77.5 14.9 %all-to-all-start = ((bf16[4,32,1280]{2,1,0:T(8,128)(2,1)}), bf16[4,32,1280]{2,1,0:T(8,128)(2,1)S(1)}, u32[]{:S(2)}, u32[]{:S(2)}) async-start(bf16[4,32,1280]{2,1,0:T(8,128)(2,1)} %all-reduce.2.cloned.1.call-done), calls=%async_computation | async-start | bytes 655360 | tf_op jit(solution)/shard_map/all_to_all | solution.py:122
  82.1 37.9 %all-gather.5.cloned.1.call-start = ((), (), s32[]{:S(2)}) async-start(), calls=%async_computation.6 | async-start | bytes 1179648 | tf_op jit(solution)/shard_map/all_gather | solution.py:140
  96.6 42.0 %copy-start = (bf16[32,4096]{1,0:T(8,128)(2,1)S(1)}, bf16[32,4096]{1,0:T(8,128)(2,1)}, u32[]{:S(2)}) copy-start(bf16[32,4096]{1,0:T(8,128)(2,1)} %param.8) | copy-start | bytes 786436
  99.7 49.8 %reduce-scatter.2.cloned.1.call-start = ((), (), s32[]{:S(2)}) async-start(), calls=%async_computation.7 | async-start | bytes 393216 | tf_op jit(solution)/shard_map/reduce_scatter | solution.py:148
  150.8 1.4 collective-permute-start
Sparse Core Ops, SparseCore 0:
  16.1 29.7 all-gather.2
  53.7 23.7 all-reduce.1
  99.8 20.1 all-gather.4
  138.7 10.7 reduce-scatter.1
where the time goes:
time: 161 us; the launch traced here: 160 us
  waiting for transfers between devices  89.5 us (56%)
  blocking collectives  22.3 us (14%)
  between operations  13.4 us (8%)
  matrix products  12.4 us (8%)
  other arithmetic  11.3 us (7%)
  local copies, waits for them, and re-layouts  6.42 us (4%)
  starting transfers between devices  4.76 us (3%)
    all_gather x1, waiting for transfers between devices, per_device(): lax.all_gather(normed, 'col', axis=0, tiled=True)  28.5 us
    psum x1, waiting for transfers between devices, per_device(): summed = lax.psum(in_slots.astype(jnp.bfloat16), 'row')  21.9 us
    all_gather x1, waiting for transfers between devices, per_device(): collected = lax.all_gather(attended, ('col', 'side'), axis=0, tiled=True)  17.6 us
    all_to_all x1, blocking collectives, per_device(): lax.all_to_all(out_requests.astype(jnp.bfloat16), 'col', split_axis=0, co...  12.6 us
    all_to_all x1, waiting for transfers between devices, per_device(): lax.all_to_all(summed, 'col', split_axis=0, concat_axis=1, tiled=True)  10.1 us
    reduce_scatter x1, waiting for transfers between devices, per_device(): lax.psum_scatter(out_view.astype(jnp.bfloat16), 'row', scatter_dimension=...  10.1 us
    dot_general x1, matrix products, per_device(): jnp.dot(lax.all_gather(normed, 'col', axis=0, tiled=True), in_weight, pre...  5.87 us
    psum x1, blocking collectives, per_device(): square_sums = lax.psum(jnp.sum(residual * residual, axis=1), 'row')  5.84 us
  transfers between devices with their start and end apart: 6, of which 6 were waited for; matrix products, arithmetic and copies ran while one was open for 4% of the time, Pallas kernels for 0%

commit v1 on v0

--- a/solution.py
+++ b/solution.py
@@ -1,6 +1,10 @@
+import functools
+
 import jax
 import jax.numpy as jnp
 from jax import lax
+from jax.experimental import pallas as pl
+from jax.experimental.pallas import tpu as pltpu
 from jax.sharding import PartitionSpec as P
 
 D = 8192
@@ -86,7 +90,7 @@
     return combined.astype(jnp.bfloat16).reshape(slot_count, groups * per_group * HEAD_DIM)
 
 
-def per_device(
+def general_plan(
     hidden_in,
     norm_gain,
     qkv_weight,
@@ -162,6 +166,404 @@
     return result[None]
 
 
+GROUP = HEADS // KV_HEADS
+GROUP_WIDTH = (GROUP + 2) * HEAD_DIM
+OUT_WIDTH = GROUP * HEAD_DIM
+SLOTS = 8
+VMEM = pl.BlockSpec(memory_space=pltpu.VMEM)
+SMEM = pl.BlockSpec(memory_space=pltpu.SMEM)
+HBM = pl.BlockSpec(memory_space=pl.ANY)
+MIB = 2**20
+
+
+def call(kernel, out_shape, in_specs, out_specs, flops, size, scratch=(), limit=16):
+    return pl.pallas_call(
+        kernel,
+        out_shape=out_shape,
+        in_specs=in_specs,
+        out_specs=out_specs,
+        scratch_shapes=list(scratch),
+        compiler_params=pltpu.CompilerParams(vmem_limit_bytes=limit * MIB),
+        cost_estimate=pl.CostEstimate(flops=flops, bytes_accessed=size, transcendentals=0),
+    )
+
+
+def in_vmem(value):
+    return pltpu.with_memory_space_constraint(value, pltpu.VMEM)
+
+
+def struct(shape, dtype=jnp.bfloat16):
+    return jax.ShapeDtypeStruct(shape, dtype)
+
+
+def moved(value, axis, mask):
+    pairs = [(source, source ^ mask) for source in range(lax.axis_size(axis))]
+    return lax.ppermute(value, axis, pairs)
+
+
+def stage_in_kernel(place, weight, staged, sem):
+    depth = staged.shape[0]
+    first = pl.multiple_of(place[0] * depth, depth)
+    copy = pltpu.make_async_copy(weight.at[pl.ds(first, depth), :], staged, sem)
+    copy.start()
+    copy.wait()
+
+
+def stage_rest_kernel(place, weight, keys, values, staged, key_part, value_part, sems):
+    pairs = staged.shape[0] // OUT_WIDTH
+    copies = []
+    for j in range(pairs):
+        head = 2 * j + place[0]
+        row = pl.multiple_of(head * OUT_WIDTH, OUT_WIDTH)
+        lane = pl.multiple_of(head * HEAD_DIM, HEAD_DIM)
+        for source, target in ((keys, key_part), (values, value_part)):
+            copies.append(
+                (
+                    source.at[:, :, pl.ds(lane, HEAD_DIM)],
+                    target.at[:, :, pl.ds(j * HEAD_DIM, HEAD_DIM)],
+                )
+            )
+        copies.append(
+            (weight.at[pl.ds(row, OUT_WIDTH), :], staged.at[pl.ds(j * OUT_WIDTH, OUT_WIDTH), :])
+        )
+    copies = [
+        pltpu.make_async_copy(source, target, sems.at[i])
+        for i, (source, target) in enumerate(copies)
+    ]
+    for copy in copies:
+        copy.start()
+    for copy in copies:
+        copy.wait()
+
+
+def square_kernel(hidden, total):
+    values = hidden[...].astype(jnp.float32)
+    sums = jnp.sum(values * values, axis=1, keepdims=True)
+    total[...] = jnp.broadcast_to(sums, total.shape)
+
+
+def one_hot(place, slots, request_axis_size):
+    col = place[1]
+    blocks, rows, _ = slots.shape
+    lane = lax.broadcasted_iota(jnp.int32, (rows, request_axis_size), 1)
+    request = (lax.div(lane, rows) ^ col) * rows + lax.rem(lane, rows)
+    parts = [
+        jnp.where(slots[col ^ block] == request, 1.0, 0.0) for block in range(blocks)
+    ]
+    return jnp.concatenate(parts, axis=0)
+
+
+def dot_columns(rows, weight, first, out, width):
+    def step(i, carry):
+        start = pl.multiple_of(i * width, width)
+        part = jnp.dot(
+            rows,
+            weight[:, pl.ds(pl.multiple_of(first + start, width), width)],
+            preferred_element_type=jnp.float32,
+        )
+        out[:, pl.ds(start, width)] = part.astype(out.dtype)
+        return carry
+
+    lax.fori_loop(0, out.shape[1] // width, step, 0)
+
+
+def project_kernel(count, transpose, scaled, place, slots, *refs):
+    blocks = refs[:count]
+    refs = refs[count:]
+    if scaled:
+        scales, gain, refs = refs[:count], refs[count], refs[count + 1 :]
+    weight, give, permuted = refs
+    side = place[0]
+    rows, depth = blocks[0].shape
+    parts = []
+    for i, block in enumerate(blocks):
+        value = block[...]
+        if scaled:
+            gains = gain[:, pl.ds(pl.multiple_of(side * depth, depth), depth)]
+            value = (
+                value.astype(jnp.float32) * scales[i][:, :1] * gains.astype(jnp.float32)
+            ).astype(jnp.bfloat16)
+        parts.append(value)
+    gathered = jnp.concatenate(parts, axis=0)
+    chosen = one_hot(place, slots, rows * count)
+    chosen = (chosen.T if transpose else chosen).astype(jnp.bfloat16)
+    order = jnp.dot(chosen, gathered, preferred_element_type=jnp.float32).astype(jnp.bfloat16)
+    permuted[...] = order
+    dot_columns(order, weight, (1 - side) * give.shape[1], give, 256)
+
+
+def own_kernel(place, permuted, weight, own):
+    dot_columns(permuted[...], weight, place[0] * own.shape[1], own, 256)
+
+
+def project(place, slots, blocks, scales, gain, weight, transpose):
+    count = len(blocks)
+    rows, depth = blocks[0].shape
+    rows = rows * count
+    half = weight.shape[1] // 2
+    flops = 2 * rows * depth * half
+    scaled = scales is not None
+    extra = [*scales, gain] if scaled else []
+    give, permuted = call(
+        functools.partial(project_kernel, count, transpose, scaled),
+        [struct((rows, half)), struct((rows, depth))],
+        [SMEM, VMEM] + [VMEM] * (count + len(extra) + 1),
+        [VMEM, VMEM],
+        flops,
+        depth * half * 2,
+    )(place, slots, *blocks, *extra, in_vmem(weight))
+    received = moved(give, "side", 1)
+    own = call(
+        own_kernel,
+        struct((rows, half), jnp.float32),
+        [SMEM, VMEM, VMEM],
+        VMEM,
+        flops,
+        depth * half * 2,
+    )(place, permuted, in_vmem(weight))
+    total = (own + received.astype(jnp.float32)).astype(jnp.bfloat16)
+    return total.reshape(count, rows // count, half)
+
+
+def rotated(vector, cosine, sine):
+    return vector * cosine + pltpu.roll(vector, HEAD_DIM // 2, 1) * sine
+
+
+def attend_all(count, place, cosine, sine, lengths, *refs):
+    kept, (arrived, keys, values, out) = refs[:count], refs[count:]
+    others, pairs, rows, _ = arrived.shape
+    cache = keys.shape[1]
+    base = place[2]
+    low = place[1] % pairs
+    factor = HEAD_DIM ** (-0.5)
+    cosines, sines = cosine[...], sine[...]
+    lane = lax.broadcasted_iota(jnp.int32, (SLOTS, SLOTS * cache), 1)
+    slot = lax.broadcasted_iota(jnp.int32, (SLOTS, SLOTS * cache), 0)
+    for pair in range(pairs):
+        column = low ^ pair
+        total = jnp.zeros(arrived.shape[2:], jnp.float32)
+        for chunk in range(count // pairs):
+            part = kept[chunk * pairs + pair][...].astype(jnp.float32)
+            total = total + jnp.where(base == chunk, part, 0.0)
+        for other in range(others):
+            total = total + arrived[other, pair].astype(jnp.float32)
+        total = total.astype(jnp.bfloat16).astype(jnp.float32)
+        heads = [total[:, h * HEAD_DIM : (h + 1) * HEAD_DIM] for h in range(GROUP + 2)]
+        queries = [
+            rotated(head, cosines, sines).astype(jnp.bfloat16).astype(jnp.float32)
+            for head in heads[:GROUP]
+        ]
+        new_key = rotated(heads[GROUP], cosines, sines).astype(jnp.bfloat16).astype(jnp.float32)
+        new_value = heads[GROUP + 1]
+        own = [jnp.sum(query * new_key, axis=1, keepdims=True) * factor for query in queries]
+        lanes = pl.ds(pl.multiple_of(column * HEAD_DIM, HEAD_DIM), HEAD_DIM)
+        results = []
+        for start in range(0, rows, SLOTS):
+            part = slice(start, start + SLOTS)
+            query = jnp.concatenate([head[part] for head in queries], axis=0)
+            key = keys[start : start + SLOTS, :, lanes].reshape(SLOTS * cache, HEAD_DIM)
+            value = values[start : start + SLOTS, :, lanes].reshape(SLOTS * cache, HEAD_DIM)
+            scores = (
+                lax.dot_general(
+                    query.astype(jnp.bfloat16),
+                    key,
+                    (((1,), (1,)), ((), ())),
+                    preferred_element_type=jnp.float32,
+                )
+                * factor
+            ).reshape(GROUP, SLOTS, SLOTS * cache)
+            position = lane - slot * cache
+            filled = (position >= 0) & (position < lengths[part])
+            scores = jnp.where(filled[None], scores, -1e30)
+            own_score = jnp.concatenate([head[part] for head in own], axis=0).reshape(
+                GROUP, SLOTS, 1
+            )
+            highest = jnp.maximum(jnp.max(scores, axis=2, keepdims=True), own_score)
+            weights = jnp.exp(scores - highest)
+            own_weight = jnp.exp(own_score - highest)
+            inverse = 1.0 / (jnp.sum(weights, axis=2, keepdims=True) + own_weight)
+            probs = (weights * inverse).astype(jnp.bfloat16)
+            own_prob = (own_weight * inverse).astype(jnp.bfloat16).astype(jnp.float32)
+            mixed = jnp.dot(
+                probs.reshape(GROUP * SLOTS, SLOTS * cache),
+                value,
+                preferred_element_type=jnp.float32,
+            ).reshape(GROUP, SLOTS, HEAD_DIM)
+            results.append(mixed + own_prob * new_value[part][None])
+        for head in range(GROUP):
+            joined = jnp.concatenate([result[head] for result in results], axis=0)
+            at = pl.multiple_of(column * OUT_WIDTH + head * HEAD_DIM, HEAD_DIM)
+            out[:, pl.ds(at, HEAD_DIM)] = joined.astype(jnp.bfloat16)
+
+
+def finish_kernel(count, others, place, hidden, attended, given, *refs):
+    kept, refs = refs[:count], refs[count:]
+    near, refs = refs[0], refs[1:]
+    same, cross, out = refs[:others], refs[others : 2 * others], refs[2 * others]
+    pairs, _, width = near.shape
+    base = place[2]
+    low = place[1] % pairs
+
+    @pl.when(place[0] == 0)
+    def _():
+        for pair in range(pairs):
+            column = low ^ pair
+            total = jnp.zeros(near.shape[1:], jnp.float32)
+            for chunk in range(count // pairs):
+                part = kept[chunk * pairs + pair][...].astype(jnp.float32)
+                total = total + jnp.where(base == chunk, part, 0.0)
+            for ref in same:
+                total = total + ref[pair].astype(jnp.float32)
+            first = pl.ds(pl.multiple_of(column * 2 * width, width), width)
+            out[0, :, first] = (hidden[:, first].astype(jnp.float32) + total).astype(jnp.bfloat16)
+            total = near[pair].astype(jnp.float32)
+            for ref in cross:
+                total = total + ref[pair].astype(jnp.float32)
+            second = pl.ds(pl.multiple_of((column * 2 + 1) * width, width), width)
+            out[0, :, second] = (hidden[:, second].astype(jnp.float32) + total).astype(
+                jnp.bfloat16
+            )
+
+    @pl.when(place[0] != 0)
+    def _():
+        size = OUT_WIDTH
+        for j in range(attended.shape[1] // size):
+            out[0, :, 2 * j * size : (2 * j + 1) * size] = given[:, j * size : (j + 1) * size]
+            out[0, :, (2 * j + 1) * size : (2 * j + 2) * size] = attended[
+                :, j * size : (j + 1) * size
+            ]
+
+
+def chunk_of(blocks, pairs, index):
+    chunks = [jnp.stack(blocks[i : i + pairs]) for i in range(0, len(blocks), pairs)]
+    chosen = chunks[0]
+    for i, chunk in enumerate(chunks[1:], 1):
+        chosen = jnp.where(index == i, chunk, chosen)
+    return chosen
+
+
+def paired_plan(
+    hidden_in, norm_gain, qkv_weight, out_weight, key_cache, value_cache, cache_lengths, slot_request
+):
+    col_count, row_count = lax.axis_size("col"), lax.axis_size("row")
+    pairs = col_count // row_count
+    side, col, row = (lax.axis_index(name) for name in ("side", "col", "row"))
+    base = lax.div(col, pairs) ^ row
+    place = jnp.stack([side, col, base]).astype(jnp.int32)
+    rows, depth = hidden_in.shape
+    half = depth // 2
+    cache = key_cache.shape[1]
+    slots = slot_request.reshape(col_count, rows, 1)
+
+    own_part = lax.dynamic_slice_in_dim(hidden_in, side * half, half, 1)
+    blocks = [own_part] + [moved(own_part, "col", mask) for mask in range(1, col_count)]
+    squares = call(
+        square_kernel, struct((rows, 128), jnp.float32), [VMEM], VMEM, rows * depth * 2, rows * depth * 2
+    )(hidden_in)
+    total = squares
+    for mask in range(1, row_count):
+        total = total + moved(squares, "row", mask)
+    scale = lax.rsqrt(total / D + EPSILON)
+    scales = [scale] + [moved(scale, "col", mask) for mask in range(1, col_count)]
+
+    weight_in = call(
+        stage_in_kernel,
+        pltpu.VMEM((half, qkv_weight.shape[1]), jnp.bfloat16),
+        [SMEM, HBM],
+        VMEM,
+        0,
+        half * qkv_weight.shape[1] * 2,
+        [pltpu.SemaphoreType.DMA],
+    )(place, qkv_weight)
+    weight_out, key_part, value_part = call(
+        stage_rest_kernel,
+        [
+            pltpu.VMEM((half, out_weight.shape[1]), jnp.bfloat16),
+            pltpu.VMEM((rows, cache, pairs * HEAD_DIM), jnp.bfloat16),
+            pltpu.VMEM((rows, cache, pairs * HEAD_DIM), jnp.bfloat16),
+        ],
+        [SMEM, HBM, HBM, HBM],
+        [VMEM, VMEM, VMEM],
+        0,
+        half * out_weight.shape[1] * 2 + 4 * rows * cache * pairs * HEAD_DIM,
+        [pltpu.SemaphoreType.DMA((3 * pairs,))],
+    )(place, out_weight, key_cache, value_cache)
+
+    products = project(
+        place, slots, blocks, scales, norm_gain.reshape(1, depth), weight_in, False
+    )
+    products = [products[0]] + [
+        moved(products[mask], "col", mask) for mask in range(1, col_count)
+    ]
+    arrived = jnp.stack(
+        [
+            moved(chunk_of(products, pairs, base ^ mask), "row", mask)
+            for mask in range(1, row_count)
+        ]
+    )
+
+    cosine, sine = rope_tables(cache_lengths, HEAD_DIM)
+    attended = call(
+        functools.partial(attend_all, col_count),
+        struct((rows, half)),
+        [SMEM] + [VMEM] * (3 + col_count + 3),
+        VMEM,
+        4 * rows * half * cache,
+        0,
+    )(
+        place,
+        jnp.concatenate([cosine, cosine], axis=1),
+        jnp.concatenate([-sine, sine], axis=1),
+        cache_lengths.reshape(rows, 1),
+        *products,
+        arrived,
+        in_vmem(key_part),
+        in_vmem(value_part),
+    )
+
+    given = lax.ppermute(attended, "side", [(0, 1)])
+    blocks = [attended] + [moved(attended, "col", mask) for mask in range(1, col_count)]
+    products = project(place, slots, blocks, None, None, weight_out, True)
+    products = [products[0]] + [
+        moved(products[mask], "col", mask) for mask in range(1, col_count)
+    ]
+    near = lax.ppermute(chunk_of(products, pairs, base), "side", [(1, 0)])
+    same, cross = [], []
+    for mask in range(1, row_count):
+        chunk = chunk_of(products, pairs, base ^ mask)
+        for target, side_from in ((same, 0), (cross, 1)):
+            target.append(
+                lax.ppermute(
+                    chunk,
+                    ("row", "side"),
+                    [(2 * r + side_from, 2 * (r ^ mask)) for r in range(row_count)],
+                )
+            )
+    return call(
+        functools.partial(finish_kernel, col_count, row_count - 1),
+        struct((1, rows, depth)),
+        [SMEM] + [VMEM] * (3 + col_count + 1 + 2 * (row_count - 1)),
+        VMEM,
+        rows * depth * 4,
+        rows * depth * 8,
+    )(place, hidden_in, attended, given, *products, near, *same, *cross)
+
+
+def per_device(*args):
+    hidden_in, _, qkv_weight, out_weight, key_cache = args[:5]
+    col_count, row_count = lax.axis_size("col"), lax.axis_size("row")
+    fits = (
+        lax.axis_size("side") == 2
+        and qkv_weight.shape[1] == 2 * GROUP_WIDTH
+        and col_count % row_count == 0
+        and col_count & (col_count - 1) == 0
+        and hidden_in.shape[0] % 16 == 0
+        and key_cache.shape[1] % 16 == 0
+        and hidden_in.shape[1] == 2 * OUT_WIDTH * (col_count // row_count)
+    )
+    return paired_plan(*args) if fits else general_plan(*args)
+
+
 def solution(mesh):
     placed = (
         P(("groups", "col"), "row"),

time: 161 us -> 107 us (0.66)
  waiting for transfers between devices: 89.5 us -> 26.5 us
  starting transfers between devices: 4.76 us -> 35.2 us
  blocking collectives: 22.3 us -> 0 us
  local copies, waits for them, and re-layouts: 6.42 us -> 25.9 us
  Pallas kernels: 0 us -> 18.4 us
  between operations: 13.4 us -> 0.28 us
  matrix products: 12.4 us -> 0 us
  other arithmetic: 11.3 us -> 0.48 us
    all_gather x2 -> x0, waiting for transfers between devices: 46.1 us -> none  [the longest x1 28.5 us: per_device(): lax.all_gather(normed, 'col', axis=0, tiled=True)]
    ppermute x1 -> x23, starting transfers between devices: 0.07 us -> 35.2 us  [the longest x19 27.7 us: moved(): return lax.ppermute(value, axis, pairs)]
    ppermute x1 -> x23, waiting for transfers between devices: 1.27 us -> 26.5 us  [the longest x19 21.5 us: moved(): return lax.ppermute(value, axis, pairs)]
    psum x1 -> x0, waiting for transfers between devices: 21.9 us -> none  [per_device(): summed = lax.psum(in_slots.astype(jnp.bfloat16), 'row')]
    unnamed x8 -> x18, local copies, waits for them, and re-layouts: 2.64 us -> 23.3 us
    pallas_call x0 -> x9, Pallas kernels: none -> 18.4 us  [the longest x2 5.56 us: project(): call(functools.partial(project_kernel, count, transpose, scaled), [struct...]
    all_to_all x2 -> x0, blocking collectives: 16.5 us -> none  [the longest x1 12.6 us: per_device(): lax.all_to_all(out_requests.astype(jnp.bfloat16), 'col', split_axis=0, co...]
    dot_general x5 -> x0, matrix products: 12.4 us -> none  [the longest x1 5.87 us: per_device(): jnp.dot(lax.all_gather(normed, 'col', axis=0, tiled=True), in_weight, pre...]
  transfers between devices with their start and end apart: 6 -> 23, of which waited for: 6 -> 10; matrix products, arithmetic and copies ran while one was open for 4% -> 3% of each run, Pallas kernels for 0% -> 6%
where the time goes in v1:
time: 107 us
  starting transfers between devices  35.2 us (33%)
  waiting for transfers between devices  26.5 us (25%)
  local copies, waits for them, and re-layouts  25.9 us (24%)
  Pallas kernels  18.4 us (17%)
    ppermute x19, starting transfers between devices, moved(): return lax.ppermute(value, axis, pairs)  27.7 us
    unnamed x18, local copies, waits for them, and re-layouts  23.3 us
    ppermute x19, waiting for transfers between devices, moved(): return lax.ppermute(value, axis, pairs)  21.5 us
    pallas_call x2, Pallas kernels, project(): call(functools.partial(project_kernel, count, transpose, scaled), [struct...  5.56 us
    ppermute x2, waiting for transfers between devices, paired_plan(): lax.ppermute(chunk, ('row', 'side'), [(2 * r + side_from, 2 * (r ^ mask))...  4.97 us
    ppermute x2, starting transfers between devices, paired_plan(): lax.ppermute(chunk, ('row', 'side'), [(2 * r + side_from, 2 * (r ^ mask))...  4.68 us
    pallas_call x1, Pallas kernels, paired_plan(): call(functools.partial(attend_all, col_count), struct((rows, half)), [SME...  4.5 us
    pallas_call x2, Pallas kernels, project(): call(own_kernel, struct((rows, half), jnp.float32), [SMEM, VMEM, VMEM], V...  4.03 us
  transfers between devices with their start and end apart: 23, of which 10 were waited for; matrix products, arithmetic and copies ran while one was open for 3% of the time, Pallas kernels for 6%

profile of v1, /device:TPU:0, one launch (start us, length us, event | category | flops | bytes accessed | tf_op | source)
XLA Modules:
  0.0 106.8 jit_solution(13750311253363122041)
XLA Ops:
  0.0 0.9 copy-done.6
  1.0 0.1 shard_map.82
  1.1 2.9 %collective-permute-start.3 = (f32[32,128]{1,0:T(8,128)S(1)}, f32[32,128]{1,0:T(8,128)S(1)}, u32[]{:S(2)}, u32[]{:S(2)}) collective-permute-start(f32[32,128]{1,0:T(8,128)S(1)} %shard_map.82), channel_id=1, source_target_pairs={{0,2},{2,0},{1,3},{3,1},{4,6},{6,4},{5,7},{7,5},{8,10},{10,8},{9,1... | collective-permute-start | bytes 49160 | tf_op jit(solution)/shard_map/ppermute | solution.py:201
  4.0 0.9 constant_dynamic-slice_fusion.refs_0_
  4.9 1.6 %collective-permute-start = (bf16[32,2048]{1,0:T(8,128)(2,1)S(1)}, bf16[32,2048]{1,0:T(8,128)(2,1)S(1)}, u32[]{:S(2)}, u32[]{:S(2)}) collective-permute-start(bf16[32,2048]{1,0:T(8,128)(2,1)S(1)} %constant_dynamic-slice_fusion.refs_0_), channel_id=1, source_target_pairs={{0,4},{4,0},{8,12},{12,8},{1,5},{5,1},{9,13},{13,9},{2,6},{6,2},{1... | collective-permute-start | bytes 393224 | tf_op jit(solution)/shard_map/ppermute | solution.py:201
  6.6 2.6 %collective-permute-start.1 = (bf16[32,2048]{1,0:T(8,128)(2,1)S(1)}, bf16[32,2048]{1,0:T(8,128)(2,1)S(1)}, u32[]{:S(2)}, u32[]{:S(2)}) collective-permute-start(bf16[32,2048]{1,0:T(8,128)(2,1)S(1)} %constant_dynamic-slice_fusion.refs_0_), channel_id=1, source_target_pairs={{0,8},{4,12},{8,0},{12,4},{1,9},{5,13},{9,1},{13,5},{2,10},{6,14},... | collective-permute-start | bytes 393224 | tf_op jit(solution)/shard_map/ppermute | solution.py:201
  9.2 0.2 collective-permute-start.2
  9.4 0.7 collective-permute-start.4
  10.2 3.5 %collective-permute-start.5 = (f32[32,128]{1,0:T(8,128)S(1)}, f32[32,128]{1,0:T(8,128)S(1)}, u32[]{:S(2)}, u32[]{:S(2)}) collective-permute-start(f32[32,128]{1,0:T(8,128)S(1)} %add_rsqrt_fusion.refs_4_), channel_id=1, source_target_pairs={{0,8},{4,12},{8,0},{12,4},{1,9},{5,13},{9,1},{13,5},{2,10},{6,14},... | collective-permute-start | bytes 49160 | tf_op jit(solution)/shard_map/ppermute | solution.py:201
  13.6 1.6 %collective-permute-done.4.refs_5_ = f32[32,128]{1,0:T(8,128)S(1)} collective-permute-done((f32[32,128]{1,0:T(8,128)S(1)}, f32[32,128]{1,0:T(8,128)S(1)}, u32[]{:S(2)}, u32[]{:S(2)}) %collective-permute-start.4) | collective-permute-done | bytes 16416 | tf_op jit(solution)/shard_map/ppermute | solution.py:201
  15.2 2.5 %collective-permute-start.6 = (f32[32,128]{1,0:T(8,128)S(1)}, f32[32,128]{1,0:T(8,128)S(1)}, u32[]{:S(2)}, u32[]{:S(2)}) collective-permute-start(f32[32,128]{1,0:T(8,128)S(1)} %add_rsqrt_fusion.refs_4_), channel_id=1, source_target_pairs={{0,12},{4,8},{8,4},{12,0},{1,13},{5,9},{9,5},{13,1},{2,14},{6,10},... | collective-permute-start | bytes 49160 | tf_op jit(solution)/shard_map/ppermute | solution.py:201
  17.8 0.9 reshape.36.slots
  18.6 0.7 reshape.35.refs_8_
  19.3 7.0 %copy-done.2 = bf16[4096,2560]{1,0:T(8,128)(2,1)S(1)} copy-done((bf16[4096,2560]{1,0:T(8,128)(2,1)S(1)}, bf16[4096,2560]{1,0:T(8,128)(2,1)}, u32[]{:S(2)}) %copy-start.2) | copy-done | bytes 20971544
  26.3 1.3 %shard_map.83.refs_9_.weight = bf16[2048,2560]{1,0:T(8,128)(2,1)S(1)} custom-call(s32[3]{0:T(128)S(1)} %pad_add_fusion.place, bf16[4096,2560]{1,0:T(8,128)(2,1)S(1)} %copy-done.2), custom_call_target="tpu_custom_call" | custom-call | bytes 10485760 | tf_op jit(solution)/shard_map/pallas_call | solution.py:469
  27.6 3.3 %shard_map.84 = (bf16[128,1280]{1,0:T(8,128)(2,1)}, bf16[128,2048]{1,0:T(8,128)(2,1)S(1)}) custom-call(s32[3]{0:T(128)S(1)} %pad_add_fusion.place, s32[4,32,1]{2,1,0:T(8,128)S(1)} %reshape.36.slots, bf16[32,2048]{1,0:T(8,128)(2,1)S(1)} %constant_dynamic-slice_fusion.refs_0_, bf16[32,2048]{1,0:T(8,128)(2,1)S(1)} %collective-permute-done.refs_1_, ...), custom_call_target="tpu_custom_call" | custom-call | flops 671088640 | bytes 5242880 | tf_op jit(solution)/shard_map/pallas_call | solution.py:307
  30.9 4.0 %copy-done = bf16[2048,2560]{1,0:T(8,128)(2,1)} copy-done((bf16[2048,2560]{1,0:T(8,128)(2,1)}, bf16[2048,2560]{1,0:T(8,128)(2,1)S(1)}, u32[]{:S(2)}) %copy-start) | copy-done | bytes 10485784
  35.0 4.0 %copy-done.1 = bf16[2048,2560]{1,0:T(8,128)(2,1)S(1)} copy-done((bf16[2048,2560]{1,0:T(8,128)(2,1)S(1)}, bf16[2048,2560]{1,0:T(8,128)(2,1)}, u32[]{:S(2)}) %copy-start.1) | copy-done | bytes 10485784
  38.9 2.2 %shard_map.85 = f32[128,1280]{1,0:T(8,128)S(1)} custom-call(s32[3]{0:T(128)S(1)} %pad_add_fusion.place, bf16[128,2048]{1,0:T(8,128)(2,1)S(1)} %get-tuple-element.12.permuted, bf16[2048,2560]{1,0:T(8,128)(2,1)S(1)} %copy-done.1), custom_call_target="tpu_custom_call" | custom-call | flops 671088640 | bytes 5242880 | tf_op jit(solution)/shard_map/pallas_call | solution.py:316
  41.2 1.5 %collective-permute-start.9 = (bf16[32,1280]{1,0:T(8,128)(2,1)S(1)}, bf16[32,1280]{1,0:T(8,128)(2,1)S(1)}, u32[]{:S(2)}, u32[]{:S(2)}) collective-permute-start(bf16[32,1280]{1,0:T(8,128)(2,1)S(1)} %get-tuple-element.21), channel_id=1, source_target_pairs={{0,8},{4,12},{8,0},{12,4},{1,9},{5,13},{9,1},{13,5},{2,10},{6,14},... | collective-permute-start | bytes 245768 | tf_op jit(solution)/shard_map/ppermute | solution.py:201
  42.7 2.5 %collective-permute-start.10 = (bf16[32,1280]{1,0:T(8,128)(2,1)S(1)}, bf16[32,1280]{1,0:T(8,128)(2,1)S(1)}, u32[]{:S(2)}, u32[]{:S(2)}) collective-permute-start(bf16[32,1280]{1,0:T(8,128)(2,1)S(1)} %get-tuple-element.20), channel_id=1, source_target_pairs={{0,12},{4,8},{8,4},{12,0},{1,13},{5,9},{9,5},{13,1},{2,14},{6,10},... | collective-permute-start | bytes 245768 | tf_op jit(solution)/shard_map/ppermute | solution.py:201
  45.2 5.7 %collective-permute-done.9.refs_2_ = bf16[32,1280]{1,0:T(8,128)(2,1)S(1)} collective-permute-done((bf16[32,1280]{1,0:T(8,128)(2,1)S(1)}, bf16[32,1280]{1,0:T(8,128)(2,1)S(1)}, u32[]{:S(2)}, u32[]{:S(2)}) %collective-permute-start.9) | collective-permute-done | bytes 81952 | tf_op jit(solution)/shard_map/ppermute | solution.py:201
  51.0 0.9 collective-permute-done.8.refs_1_
  51.9 0.6 collective-permute-start.11
  52.8 5.8 %copy-done.3 = bf16[4096,2048]{1,0:T(8,128)(2,1)S(1)} copy-done((bf16[4096,2048]{1,0:T(8,128)(2,1)S(1)}, bf16[4096,2048]{1,0:T(8,128)(2,1)}, u32[]{:S(2)}) %copy-start.3) | copy-done | bytes 16777240
  58.5 1.6 %copy-done.5 = bf16[32,64,512]{2,1,0:T(8,128)(2,1)S(1)} copy-done((bf16[32,64,512]{2,1,0:T(8,128)(2,1)S(1)}, bf16[32,64,512]{2,1,0:T(8,128)(2,1)}, u32[]{:S(2)}) %copy-start.5) | copy-done | bytes 2097176
  60.1 1.5 %shard_map.86 = (bf16[2048,2048]{1,0:T(8,128)(2,1)S(1)}, bf16[32,64,256]{2,1,0:T(8,128)(2,1)S(1)}, bf16[32,64,256]{2,1,0:T(8,128)(2,1)S(1)}) custom-call(s32[3]{0:T(128)S(1)} %pad_add_fusion.place, bf16[4096,2048]{1,0:T(8,128)(2,1)S(1)} %copy-done.3, bf16[32,64,512]{2,1,0:T(8,128)(2,1)S(1)} %copy-done.4, bf16[32,64,512]{2,1,0:T(8,128)(2,1)S(1)} %copy-done.5), custom_call_target="tpu_custom_call" | custom-call | bytes 10485760 | tf_op jit(solution)/shard_map/pallas_call | solution.py:478
  61.7 4.5 %shard_map.87.refs_0_.attended = bf16[32,2048]{1,0:T(8,128)(2,1)S(1)} custom-call(s32[3]{0:T(128)S(1)} %pad_add_fusion.place, f32[32,128]{1,0:T(8,128)S(1)} %get-tuple-element.34.cosine, f32[32,128]{1,0:T(8,128)S(1)} %get-tuple-element.35.sine, s32[32,1]{1,0:T(8,128)S(1)} %copy.10.lengths, bf16[32,1280]{1,0:T(8,128)(2,1)S(1)} %get-tuple-element.23.refs_0_, ...), custom_call_target="tpu_custom_call" | custom-call | flops 16777216 | tf_op jit(solution)/shard_map/pallas_call | solution.py:506
  66.3 1.1 %collective-permute-start.13 = (bf16[32,2048]{1,0:T(8,128)(2,1)S(1)}, bf16[32,2048]{1,0:T(8,128)(2,1)S(1)}, u32[]{:S(2)}, u32[]{:S(2)}) collective-permute-start(bf16[32,2048]{1,0:T(8,128)(2,1)S(1)} %shard_map.87.refs_0_.attended), channel_id=1, source_target_pairs={{0,4},{4,0},{8,12},{12,8},{1,5},{5,1},{9,13},{13,9},{2,6},{6,2},{1... | collective-permute-start | bytes 393224 | tf_op jit(solution)/shard_map/ppermute | solution.py:201
  67.3 0.9 collective-permute-start.14
  68.3 2.5 %collective-permute-start.15 = (bf16[32,2048]{1,0:T(8,128)(2,1)S(1)}, bf16[32,2048]{1,0:T(8,128)(2,1)S(1)}, u32[]{:S(2)}, u32[]{:S(2)}) collective-permute-start(bf16[32,2048]{1,0:T(8,128)(2,1)S(1)} %shard_map.87.refs_0_.attended), channel_id=1, source_target_pairs={{0,12},{4,8},{8,4},{12,0},{1,13},{5,9},{9,5},{13,1},{2,14},{6,10},... | collective-permute-start | bytes 393224 | tf_op jit(solution)/shard_map/ppermute | solution.py:201
  70.7 2.3 %collective-permute-done.13.refs_1_ = bf16[32,2048]{1,0:T(8,128)(2,1)S(1)} collective-permute-done((bf16[32,2048]{1,0:T(8,128)(2,1)S(1)}, bf16[32,2048]{1,0:T(8,128)(2,1)S(1)}, u32[]{:S(2)}, u32[]{:S(2)}) %collective-permute-start.13) | collective-permute-done | bytes 131104 | tf_op jit(solution)/shard_map/ppermute | solution.py:201
  73.0 6.6 %collective-permute-done.14.refs_2_ = bf16[32,2048]{1,0:T(8,128)(2,1)S(1)} collective-permute-done((bf16[32,2048]{1,0:T(8,128)(2,1)S(1)}, bf16[32,2048]{1,0:T(8,128)(2,1)S(1)}, u32[]{:S(2)}, u32[]{:S(2)}) %collective-permute-start.14) | collective-permute-done | bytes 131104 | tf_op jit(solution)/shard_map/ppermute | solution.py:201
  79.6 2.3 %shard_map.88 = (bf16[128,1024]{1,0:T(8,128)(2,1)S(1)}, bf16[128,2048]{1,0:T(8,128)(2,1)S(1)}) custom-call(s32[3]{0:T(128)S(1)} %pad_add_fusion.place, s32[4,32,1]{2,1,0:T(8,128)S(1)} %reshape.36.slots, bf16[32,2048]{1,0:T(8,128)(2,1)S(1)} %shard_map.87.refs_0_.attended, bf16[32,2048]{1,0:T(8,128)(2,1)S(1)} %collective-permute-done.13.refs_1_, ...), custom_call_target="tpu_custom_call" | custom-call | flops 536870912 | bytes 4194304 | tf_op jit(solution)/shard_map/pallas_call | solution.py:307
  81.9 1.9 %shard_map.89 = f32[128,1024]{1,0:T(8,128)S(1)} custom-call(s32[3]{0:T(128)S(1)} %pad_add_fusion.place, bf16[128,2048]{1,0:T(8,128)(2,1)S(1)} %get-tuple-element.17.permuted, bf16[2048,2048]{1,0:T(8,128)(2,1)S(1)} %get-tuple-element.16.refs_4_.weight), custom_call_target="tpu_custom_call" | custom-call | flops 536870912 | bytes 4194304 | tf_op jit(solution)/shard_map/pallas_call | solution.py:316
  83.9 1.7 %collective-permute-start.19 = (bf16[32,1024]{1,0:T(8,128)(2,1)S(1)}, bf16[32,1024]{1,0:T(8,128)(2,1)S(1)}, u32[]{:S(2)}, u32[]{:S(2)}) collective-permute-start(bf16[32,1024]{1,0:T(8,128)(2,1)S(1)} %get-tuple-element.27), channel_id=1, source_target_pairs={{0,12},{4,8},{8,4},{12,0},{1,13},{5,9},{9,5},{13,1},{2,14},{6,10},... | collective-permute-start | bytes 196616 | tf_op jit(solution)/shard_map/ppermute | solution.py:201
  85.6 1.1 collective-permute-start.17
  86.7 1.7 %collective-permute-start.18 = (bf16[32,1024]{1,0:T(8,128)(2,1)S(1)}, bf16[32,1024]{1,0:T(8,128)(2,1)S(1)}, u32[]{:S(2)}, u32[]{:S(2)}) collective-permute-start(bf16[32,1024]{1,0:T(8,128)(2,1)S(1)} %get-tuple-element.28), channel_id=1, source_target_pairs={{0,8},{4,12},{8,0},{12,4},{1,9},{5,13},{9,1},{13,5},{2,10},{6,14},... | collective-permute-start | bytes 196616 | tf_op jit(solution)/shard_map/ppermute | solution.py:201
  88.4 1.6 %collective-permute-start.12 = (bf16[32,2048]{1,0:T(8,128)(2,1)S(1)}, bf16[32,2048]{1,0:T(8,128)(2,1)S(1)}, u32[]{:S(2)}, u32[]{:S(2)}) collective-permute-start(bf16[32,2048]{1,0:T(8,128)(2,1)S(1)} %shard_map.87.refs_0_.attended), channel_id=1, source_target_pairs={{0,1},{2,3},{4,5},{6,7},{8,9},{10,11},{12,13},{14,15},{16,17},{18,... | collective-permute-start | bytes 393224 | tf_op jit(solution)/shard_map/ppermute | solution.py:524
  89.9 0.8 collective-permute-done.19.refs_3_
  90.7 0.5 collective-permute-done.17.refs_1_
  91.3 3.1 %collective-permute-done.18.refs_2_ = bf16[32,1024]{1,0:T(8,128)(2,1)S(1)} collective-permute-done((bf16[32,1024]{1,0:T(8,128)(2,1)S(1)}, bf16[32,1024]{1,0:T(8,128)(2,1)S(1)}, u32[]{:S(2)}, u32[]{:S(2)}) %collective-permute-start.18) | collective-permute-done | bytes 65568 | tf_op jit(solution)/shard_map/ppermute | solution.py:201
  94.4 1.3 %collective-permute-start.20 = (bf16[2,32,1024]{2,1,0:T(8,128)(2,1)S(1)}, bf16[2,32,1024]{2,1,0:T(8,128)(2,1)S(1)}, u32[]{:S(2)}, u32[]{:S(2)}) collective-permute-start(bf16[2,32,1024]{2,1,0:T(8,128)(2,1)S(1)} %get-tuple-element.25), channel_id=1, source_target_pairs={{1,0},{3,2},{5,4},{7,6},{9,8},{11,10},{13,12},{15,14},{17,16},{19,... | collective-permute-start | bytes 393224 | tf_op jit(solution)/shard_map/ppermute | solution.py:530
  95.7 3.4 %collective-permute-start.21 = (bf16[2,32,1024]{2,1,0:T(8,128)(2,1)S(1)}, bf16[2,32,1024]{2,1,0:T(8,128)(2,1)S(1)}, u32[]{:S(2)}, u32[]{:S(2)}) collective-permute-start(bf16[2,32,1024]{2,1,0:T(8,128)(2,1)S(1)} %get-tuple-element.24), channel_id=1, source_target_pairs={{0,2},{2,0},{4,6},{6,4},{8,10},{10,8},{12,14},{14,12},{16,18},{18,... | collective-permute-start | bytes 393224 | tf_op jit(solution)/shard_map/ppermute | solution.py:536
  99.1 1.3 %collective-permute-start.22 = (bf16[2,32,1024]{2,1,0:T(8,128)(2,1)S(1)}, bf16[2,32,1024]{2,1,0:T(8,128)(2,1)S(1)}, u32[]{:S(2)}, u32[]{:S(2)}) collective-permute-start(bf16[2,32,1024]{2,1,0:T(8,128)(2,1)S(1)} %get-tuple-element.24), channel_id=1, source_target_pairs={{1,2},{3,0},{5,6},{7,4},{9,10},{11,8},{13,14},{15,12},{17,18},{19,... | collective-permute-start | bytes 393224 | tf_op jit(solution)/shard_map/ppermute | solution.py:536
  100.4 2.1 %collective-permute-done.21.refs_5_ = bf16[2,32,1024]{2,1,0:T(8,128)(2,1)S(1)} collective-permute-done((bf16[2,32,1024]{2,1,0:T(8,128)(2,1)S(1)}, bf16[2,32,1024]{2,1,0:T(8,128)(2,1)S(1)}, u32[]{:S(2)}, u32[]{:S(2)}) %collective-permute-start.21) | collective-permute-done | bytes 131104 | tf_op jit(solution)/shard_map/ppermute | solution.py:536
  102.6 2.8 %collective-permute-done.22.refs_6_ = bf16[2,32,1024]{2,1,0:T(8,128)(2,1)S(1)} collective-permute-done((bf16[2,32,1024]{2,1,0:T(8,128)(2,1)S(1)}, bf16[2,32,1024]{2,1,0:T(8,128)(2,1)S(1)}, u32[]{:S(2)}, u32[]{:S(2)}) %collective-permute-start.22) | collective-permute-done | bytes 131104 | tf_op jit(solution)/shard_map/ppermute | solution.py:536
  105.4 1.4 %shard_map.90 = bf16[1,32,4096]{2,1,0:T(8,128)(2,1)} custom-call(s32[3]{0:T(128)S(1)} %pad_add_fusion.place, bf16[32,4096]{1,0:T(8,128)(2,1)S(1)} %copy-done.7, bf16[32,2048]{1,0:T(8,128)(2,1)S(1)} %shard_map.87.refs_0_.attended, bf16[32,2048]{1,0:T(8,128)(2,1)S(1)} %collective-permute-done.12.given, bf16[32,1024]{1,0:T(8,128)(2,1)S(1)} %get-tuple-element.30.refs_0_, ...), custom_call_target="tpu_custom_call" | custom-call | flops 524288 | bytes 1048576 | tf_op jit(solution)/shard_map/pallas_call | solution.py:542
  (41 shorter events, 0.8 us)
Async XLA Ops:
  0.0 0.9 copy-start.6
  1.1 8.3 %collective-permute-start.3 = (f32[32,128]{1,0:T(8,128)S(1)}, f32[32,128]{1,0:T(8,128)S(1)}, u32[]{:S(2)}, u32[]{:S(2)}) collective-permute-start(f32[32,128]{1,0:T(8,128)S(1)} %shard_map.82), channel_id=1, source_target_pairs={{0,2},{2,0},{1,3},{3,1},{4,6},{6,4},{5,7},{7,5},{8,10},{10,8},{9,1... | collective-permute-start | bytes 49160 | tf_op jit(solution)/shard_map/ppermute | solution.py:201
  4.9 22.7 %collective-permute-start = (bf16[32,2048]{1,0:T(8,128)(2,1)S(1)}, bf16[32,2048]{1,0:T(8,128)(2,1)S(1)}, u32[]{:S(2)}, u32[]{:S(2)}) collective-permute-start(bf16[32,2048]{1,0:T(8,128)(2,1)S(1)} %constant_dynamic-slice_fusion.refs_0_), channel_id=1, source_target_pairs={{0,4},{4,0},{8,12},{12,8},{1,5},{5,1},{9,13},{13,9},{2,6},{6,2},{1... | collective-permute-start | bytes 393224 | tf_op jit(solution)/shard_map/ppermute | solution.py:201
  6.6 21.0 %collective-permute-start.1 = (bf16[32,2048]{1,0:T(8,128)(2,1)S(1)}, bf16[32,2048]{1,0:T(8,128)(2,1)S(1)}, u32[]{:S(2)}, u32[]{:S(2)}) collective-permute-start(bf16[32,2048]{1,0:T(8,128)(2,1)S(1)} %constant_dynamic-slice_fusion.refs_0_), channel_id=1, source_target_pairs={{0,8},{4,12},{8,0},{12,4},{1,9},{5,13},{9,1},{13,5},{2,10},{6,14},... | collective-permute-start | bytes 393224 | tf_op jit(solution)/shard_map/ppermute | solution.py:201
  9.2 18.5 %collective-permute-start.2 = (bf16[32,2048]{1,0:T(8,128)(2,1)S(1)}, bf16[32,2048]{1,0:T(8,128)(2,1)S(1)}, u32[]{:S(2)}, u32[]{:S(2)}) collective-permute-start(bf16[32,2048]{1,0:T(8,128)(2,1)S(1)} %constant_dynamic-slice_fusion.refs_0_), channel_id=1, source_target_pairs={{0,12},{4,8},{8,4},{12,0},{1,13},{5,9},{9,5},{13,1},{2,14},{6,10},... | collective-permute-start | bytes 393224 | tf_op jit(solution)/shard_map/ppermute | solution.py:201
  9.4 5.8 %collective-permute-start.4 = (f32[32,128]{1,0:T(8,128)S(1)}, f32[32,128]{1,0:T(8,128)S(1)}, u32[]{:S(2)}, u32[]{:S(2)}) collective-permute-start(f32[32,128]{1,0:T(8,128)S(1)} %add_rsqrt_fusion.refs_4_), channel_id=1, source_target_pairs={{0,4},{4,0},{8,12},{12,8},{1,5},{5,1},{9,13},{13,9},{2,6},{6,2},{1... | collective-permute-start | bytes 49160 | tf_op jit(solution)/shard_map/ppermute | solution.py:201
  10.2 17.4 %collective-permute-start.5 = (f32[32,128]{1,0:T(8,128)S(1)}, f32[32,128]{1,0:T(8,128)S(1)}, u32[]{:S(2)}, u32[]{:S(2)}) collective-permute-start(f32[32,128]{1,0:T(8,128)S(1)} %add_rsqrt_fusion.refs_4_), channel_id=1, source_target_pairs={{0,8},{4,12},{8,0},{12,4},{1,9},{5,13},{9,1},{13,5},{2,10},{6,14},... | collective-permute-start | bytes 49160 | tf_op jit(solution)/shard_map/ppermute | solution.py:201
  15.2 12.4 %collective-permute-start.6 = (f32[32,128]{1,0:T(8,128)S(1)}, f32[32,128]{1,0:T(8,128)S(1)}, u32[]{:S(2)}, u32[]{:S(2)}) collective-permute-start(f32[32,128]{1,0:T(8,128)S(1)} %add_rsqrt_fusion.refs_4_), channel_id=1, source_target_pairs={{0,12},{4,8},{8,4},{12,0},{1,13},{5,9},{9,5},{13,1},{2,14},{6,10},... | collective-permute-start | bytes 49160 | tf_op jit(solution)/shard_map/ppermute | solution.py:201
  19.3 7.0 %copy-start.2 = (bf16[4096,2560]{1,0:T(8,128)(2,1)S(1)}, bf16[4096,2560]{1,0:T(8,128)(2,1)}, u32[]{:S(2)}) copy-start(bf16[4096,2560]{1,0:T(8,128)(2,1)} %weight.2) | copy-start | bytes 62914564
  27.6 7.4 %copy-start.8 = (s32[32]{0:T(128)S(1)}, s32[32]{0:T(128)}, u32[]{:S(2)}) copy-start(s32[32]{0:T(128)} %param.14) | copy-start | bytes 388
  27.6 25.2 %copy-start.4 = (bf16[32,64,512]{2,1,0:T(8,128)(2,1)S(1)}, bf16[32,64,512]{2,1,0:T(8,128)(2,1)}, u32[]{:S(2)}) copy-start(bf16[32,64,512]{2,1,0:T(8,128)(2,1)} %keys.1) | copy-start | bytes 6291460
  30.9 4.0 %copy-start = (bf16[2048,2560]{1,0:T(8,128)(2,1)}, bf16[2048,2560]{1,0:T(8,128)(2,1)S(1)}, u32[]{:S(2)}) copy-start(bf16[2048,2560]{1,0:T(8,128)(2,1)S(1)} %shard_map.83.refs_9_.weight) | copy-start | bytes 31457284
  34.9 6.2 %collective-permute-start.7 = (bf16[128,1280]{1,0:T(8,128)(2,1)}, bf16[128,1280]{1,0:T(8,128)(2,1)S(1)}, u32[]{:S(2)}, u32[]{:S(2)}) collective-permute-start(bf16[128,1280]{1,0:T(8,128)(2,1)} %get-tuple-element.13), channel_id=1, source_target_pairs={{0,1},{1,0},{2,3},{3,2},{4,5},{5,4},{6,7},{7,6},{8,9},{9,8},{10,11... | collective-permute-start | bytes 983048 | tf_op jit(solution)/shard_map/ppermute | solution.py:201
  35.0 4.0 %copy-start.1 = (bf16[2048,2560]{1,0:T(8,128)(2,1)S(1)}, bf16[2048,2560]{1,0:T(8,128)(2,1)}, u32[]{:S(2)}) copy-start(bf16[2048,2560]{1,0:T(8,128)(2,1)} %copy-done) | copy-start | bytes 31457284
  41.2 9.8 %collective-permute-start.9 = (bf16[32,1280]{1,0:T(8,128)(2,1)S(1)}, bf16[32,1280]{1,0:T(8,128)(2,1)S(1)}, u32[]{:S(2)}, u32[]{:S(2)}) collective-permute-start(bf16[32,1280]{1,0:T(8,128)(2,1)S(1)} %get-tuple-element.21), channel_id=1, source_target_pairs={{0,8},{4,12},{8,0},{12,4},{1,9},{5,13},{9,1},{13,5},{2,10},{6,14},... | collective-permute-start | bytes 245768 | tf_op jit(solution)/shard_map/ppermute | solution.py:201
  42.7 8.2 %collective-permute-start.10 = (bf16[32,1280]{1,0:T(8,128)(2,1)S(1)}, bf16[32,1280]{1,0:T(8,128)(2,1)S(1)}, u32[]{:S(2)}, u32[]{:S(2)}) collective-permute-start(bf16[32,1280]{1,0:T(8,128)(2,1)S(1)} %get-tuple-element.20), channel_id=1, source_target_pairs={{0,12},{4,8},{8,4},{12,0},{1,13},{5,9},{9,5},{13,1},{2,14},{6,10},... | collective-permute-start | bytes 245768 | tf_op jit(solution)/shard_map/ppermute | solution.py:201
  45.2 6.7 %collective-permute-start.8 = (bf16[32,1280]{1,0:T(8,128)(2,1)S(1)}, bf16[32,1280]{1,0:T(8,128)(2,1)S(1)}, u32[]{:S(2)}, u32[]{:S(2)}) collective-permute-start(bf16[32,1280]{1,0:T(8,128)(2,1)S(1)} %get-tuple-element.22), channel_id=1, source_target_pairs={{0,4},{4,0},{8,12},{12,8},{1,5},{5,1},{9,13},{13,9},{2,6},{6,2},{1... | collective-permute-start | bytes 245768 | tf_op jit(solution)/shard_map/ppermute | solution.py:201
  51.9 9.8 %collective-permute-start.11 = (bf16[2,32,1280]{2,1,0:T(8,128)(2,1)S(1)}, bf16[2,32,1280]{2,1,0:T(8,128)(2,1)S(1)}, u32[]{:S(2)}, u32[]{:S(2)}) collective-permute-start(bf16[2,32,1280]{2,1,0:T(8,128)(2,1)S(1)} %maximum_select_fusion), channel_id=1, source_target_pairs={{0,2},{2,0},{1,3},{3,1},{4,6},{6,4},{5,7},{7,5},{8,10},{10,8},{9,1... | collective-permute-start | bytes 491528 | tf_op jit(solution)/shard_map/ppermute | solution.py:201
  52.8 5.8 %copy-start.3 = (bf16[4096,2048]{1,0:T(8,128)(2,1)S(1)}, bf16[4096,2048]{1,0:T(8,128)(2,1)}, u32[]{:S(2)}) copy-start(bf16[4096,2048]{1,0:T(8,128)(2,1)} %weight.3) | copy-start | bytes 50331652
  58.5 1.6 %copy-start.5 = (bf16[32,64,512]{2,1,0:T(8,128)(2,1)S(1)}, bf16[32,64,512]{2,1,0:T(8,128)(2,1)}, u32[]{:S(2)}) copy-start(bf16[32,64,512]{2,1,0:T(8,128)(2,1)} %values.1) | copy-start | bytes 6291460
  66.2 39.1 %copy-start.7 = (bf16[32,4096]{1,0:T(8,128)(2,1)S(1)}, bf16[32,4096]{1,0:T(8,128)(2,1)}, u32[]{:S(2)}) copy-start(bf16[32,4096]{1,0:T(8,128)(2,1)} %hidden.3) | copy-start | bytes 786436
  66.3 6.7 %collective-permute-start.13 = (bf16[32,2048]{1,0:T(8,128)(2,1)S(1)}, bf16[32,2048]{1,0:T(8,128)(2,1)S(1)}, u32[]{:S(2)}, u32[]{:S(2)}) collective-permute-start(bf16[32,2048]{1,0:T(8,128)(2,1)S(1)} %shard_map.87.refs_0_.attended), channel_id=1, source_target_pairs={{0,4},{4,0},{8,12},{12,8},{1,5},{5,1},{9,13},{13,9},{2,6},{6,2},{1... | collective-permute-start | bytes 393224 | tf_op jit(solution)/shard_map/ppermute | solution.py:201
  67.3 12.2 %collective-permute-start.14 = (bf16[32,2048]{1,0:T(8,128)(2,1)S(1)}, bf16[32,2048]{1,0:T(8,128)(2,1)S(1)}, u32[]{:S(2)}, u32[]{:S(2)}) collective-permute-start(bf16[32,2048]{1,0:T(8,128)(2,1)S(1)} %shard_map.87.refs_0_.attended), channel_id=1, source_target_pairs={{0,8},{4,12},{8,0},{12,4},{1,9},{5,13},{9,1},{13,5},{2,10},{6,14},... | collective-permute-start | bytes 393224 | tf_op jit(solution)/shard_map/ppermute | solution.py:201
  68.3 11.3 %collective-permute-start.15 = (bf16[32,2048]{1,0:T(8,128)(2,1)S(1)}, bf16[32,2048]{1,0:T(8,128)(2,1)S(1)}, u32[]{:S(2)}, u32[]{:S(2)}) collective-permute-start(bf16[32,2048]{1,0:T(8,128)(2,1)S(1)} %shard_map.87.refs_0_.attended), channel_id=1, source_target_pairs={{0,12},{4,8},{8,4},{12,0},{1,13},{5,9},{9,5},{13,1},{2,14},{6,10},... | collective-permute-start | bytes 393224 | tf_op jit(solution)/shard_map/ppermute | solution.py:201
  81.8 2.0 %collective-permute-start.16 = (bf16[128,1024]{1,0:T(8,128)(2,1)S(1)}, bf16[128,1024]{1,0:T(8,128)(2,1)S(1)}, u32[]{:S(2)}, u32[]{:S(2)}) collective-permute-start(bf16[128,1024]{1,0:T(8,128)(2,1)S(1)} %get-tuple-element.18), channel_id=1, source_target_pairs={{0,1},{1,0},{2,3},{3,2},{4,5},{5,4},{6,7},{7,6},{8,9},{9,8},{10,11... | collective-permute-start | bytes 786440 | tf_op jit(solution)/shard_map/ppermute | solution.py:201
  83.9 6.8 %collective-permute-start.19 = (bf16[32,1024]{1,0:T(8,128)(2,1)S(1)}, bf16[32,1024]{1,0:T(8,128)(2,1)S(1)}, u32[]{:S(2)}, u32[]{:S(2)}) collective-permute-start(bf16[32,1024]{1,0:T(8,128)(2,1)S(1)} %get-tuple-element.27), channel_id=1, source_target_pairs={{0,12},{4,8},{8,4},{12,0},{1,13},{5,9},{9,5},{13,1},{2,14},{6,10},... | collective-permute-start | bytes 196616 | tf_op jit(solution)/shard_map/ppermute | solution.py:201
  85.6 5.6 %collective-permute-start.17 = (bf16[32,1024]{1,0:T(8,128)(2,1)S(1)}, bf16[32,1024]{1,0:T(8,128)(2,1)S(1)}, u32[]{:S(2)}, u32[]{:S(2)}) collective-permute-start(bf16[32,1024]{1,0:T(8,128)(2,1)S(1)} %get-tuple-element.29), channel_id=1, source_target_pairs={{0,4},{4,0},{8,12},{12,8},{1,5},{5,1},{9,13},{13,9},{2,6},{6,2},{1... | collective-permute-start | bytes 196616 | tf_op jit(solution)/shard_map/ppermute | solution.py:201
  86.7 7.7 %collective-permute-start.18 = (bf16[32,1024]{1,0:T(8,128)(2,1)S(1)}, bf16[32,1024]{1,0:T(8,128)(2,1)S(1)}, u32[]{:S(2)}, u32[]{:S(2)}) collective-permute-start(bf16[32,1024]{1,0:T(8,128)(2,1)S(1)} %get-tuple-element.28), channel_id=1, source_target_pairs={{0,8},{4,12},{8,0},{12,4},{1,9},{5,13},{9,1},{13,5},{2,10},{6,14},... | collective-permute-start | bytes 196616 | tf_op jit(solution)/shard_map/ppermute | solution.py:201
  88.4 12.0 %collective-permute-start.12 = (bf16[32,2048]{1,0:T(8,128)(2,1)S(1)}, bf16[32,2048]{1,0:T(8,128)(2,1)S(1)}, u32[]{:S(2)}, u32[]{:S(2)}) collective-permute-start(bf16[32,2048]{1,0:T(8,128)(2,1)S(1)} %shard_map.87.refs_0_.attended), channel_id=1, source_target_pairs={{0,1},{2,3},{4,5},{6,7},{8,9},{10,11},{12,13},{14,15},{16,17},{18,... | collective-permute-start | bytes 393224 | tf_op jit(solution)/shard_map/ppermute | solution.py:524
  94.4 6.0 %collective-permute-start.20 = (bf16[2,32,1024]{2,1,0:T(8,128)(2,1)S(1)}, bf16[2,32,1024]{2,1,0:T(8,128)(2,1)S(1)}, u32[]{:S(2)}, u32[]{:S(2)}) collective-permute-start(bf16[2,32,1024]{2,1,0:T(8,128)(2,1)S(1)} %get-tuple-element.25), channel_id=1, source_target_pairs={{1,0},{3,2},{5,4},{7,6},{9,8},{11,10},{13,12},{15,14},{17,16},{19,... | collective-permute-start | bytes 393224 | tf_op jit(solution)/shard_map/ppermute | solution.py:530
  95.7 6.9 %collective-permute-start.21 = (bf16[2,32,1024]{2,1,0:T(8,128)(2,1)S(1)}, bf16[2,32,1024]{2,1,0:T(8,128)(2,1)S(1)}, u32[]{:S(2)}, u32[]{:S(2)}) collective-permute-start(bf16[2,32,1024]{2,1,0:T(8,128)(2,1)S(1)} %get-tuple-element.24), channel_id=1, source_target_pairs={{0,2},{2,0},{4,6},{6,4},{8,10},{10,8},{12,14},{14,12},{16,18},{18,... | collective-permute-start | bytes 393224 | tf_op jit(solution)/shard_map/ppermute | solution.py:536
  99.1 6.3 %collective-permute-start.22 = (bf16[2,32,1024]{2,1,0:T(8,128)(2,1)S(1)}, bf16[2,32,1024]{2,1,0:T(8,128)(2,1)S(1)}, u32[]{:S(2)}, u32[]{:S(2)}) collective-permute-start(bf16[2,32,1024]{2,1,0:T(8,128)(2,1)S(1)} %get-tuple-element.24), channel_id=1, source_target_pairs={{1,2},{3,0},{5,6},{7,4},{9,10},{11,8},{13,14},{15,12},{17,18},{19,... | collective-permute-start | bytes 393224 | tf_op jit(solution)/shard_map/ppermute | solution.py:536

commit v2 on v1

--- a/solution.py
+++ b/solution.py
@@ -192,6 +192,10 @@
     return pltpu.with_memory_space_constraint(value, pltpu.VMEM)
 
 
+def in_hbm(value):
+    return pltpu.with_memory_space_constraint(value, pltpu.HBM)
+
+
 def struct(shape, dtype=jnp.bfloat16):
     return jax.ShapeDtypeStruct(shape, dtype)
 
@@ -236,24 +240,24 @@
         copy.wait()
 
 
-def square_kernel(hidden, total):
-    values = hidden[...].astype(jnp.float32)
-    sums = jnp.sum(values * values, axis=1, keepdims=True)
-    total[...] = jnp.broadcast_to(sums, total.shape)
-
-
-def one_hot(place, slots, request_axis_size):
-    col = place[1]
+def one_hot(slots, slot_base, request_base):
     blocks, rows, _ = slots.shape
-    lane = lax.broadcasted_iota(jnp.int32, (rows, request_axis_size), 1)
-    request = (lax.div(lane, rows) ^ col) * rows + lax.rem(lane, rows)
-    parts = [
-        jnp.where(slots[col ^ block] == request, 1.0, 0.0) for block in range(blocks)
-    ]
+    lane = lax.broadcasted_iota(jnp.int32, (rows, blocks * rows), 1)
+    request = (lax.div(lane, rows) ^ request_base) * rows + lax.rem(lane, rows)
+    parts = [jnp.where(slots[slot_base ^ i] == request, 1.0, 0.0) for i in range(blocks)]
     return jnp.concatenate(parts, axis=0)
 
 
-def dot_columns(rows, weight, first, out, width):
+def pieces(sums):
+    high = sums.astype(jnp.bfloat16).astype(jnp.float32)
+    middle = (sums - high).astype(jnp.bfloat16).astype(jnp.float32)
+    low = sums - high - middle
+    lane = lax.broadcasted_iota(jnp.int32, (sums.shape[0], HEAD_DIM), 1)
+    parts = jnp.where(lane == 0, high, jnp.where(lane == 1, middle, low))
+    return jnp.where(lane < 3, parts, 0.0).astype(jnp.bfloat16)
+
+
+def dot_columns(rows, weight, first, out, size, width):
     def step(i, carry):
         start = pl.multiple_of(i * width, width)
         part = jnp.dot(
@@ -264,49 +268,50 @@
         out[:, pl.ds(start, width)] = part.astype(out.dtype)
         return carry
 
-    lax.fori_loop(0, out.shape[1] // width, step, 0)
-
-
-def project_kernel(count, transpose, scaled, place, slots, *refs):
-    blocks = refs[:count]
-    refs = refs[count:]
-    if scaled:
-        scales, gain, refs = refs[:count], refs[count], refs[count + 1 :]
-    weight, give, permuted = refs
+    lax.fori_loop(0, size // width, step, 0)
+
+
+def in_kernel(count, place, slots, *refs):
+    blocks, (gain, weight, give, permuted) = refs[:count], refs[count:]
     side = place[0]
-    rows, depth = blocks[0].shape
-    parts = []
-    for i, block in enumerate(blocks):
-        value = block[...]
-        if scaled:
-            gains = gain[:, pl.ds(pl.multiple_of(side * depth, depth), depth)]
-            value = (
-                value.astype(jnp.float32) * scales[i][:, :1] * gains.astype(jnp.float32)
-            ).astype(jnp.bfloat16)
-        parts.append(value)
-    gathered = jnp.concatenate(parts, axis=0)
-    chosen = one_hot(place, slots, rows * count)
-    chosen = (chosen.T if transpose else chosen).astype(jnp.bfloat16)
-    order = jnp.dot(chosen, gathered, preferred_element_type=jnp.float32).astype(jnp.bfloat16)
+    depth = blocks[0].shape[1]
+    half = weight.shape[1] // 2
+    gains = gain[:, pl.ds(pl.multiple_of(side * depth, depth), depth)].astype(jnp.float32)
+    values = jnp.concatenate([block[...].astype(jnp.float32) for block in blocks], axis=0)
+    sums = pieces(jnp.sum(values * values, axis=1, keepdims=True))
+    chosen = one_hot(slots, place[2], place[1]).astype(jnp.bfloat16)
+    order = jnp.dot(
+        chosen, (values * gains).astype(jnp.bfloat16), preferred_element_type=jnp.float32
+    ).astype(jnp.bfloat16)
     permuted[...] = order
-    dot_columns(order, weight, (1 - side) * give.shape[1], give, 256)
+    give[:, half:] = jnp.dot(chosen, sums, preferred_element_type=jnp.float32).astype(jnp.bfloat16)
+    dot_columns(order, weight, (1 - side) * half, give, half, 256)
+
+
+def out_kernel(count, place, slots, *refs):
+    blocks, (weight, give, permuted) = refs[:count], refs[count:]
+    half = weight.shape[1] // 2
+    values = jnp.concatenate([block[...] for block in blocks], axis=0)
+    chosen = one_hot(slots, place[1], place[2]).T.astype(jnp.bfloat16)
+    order = jnp.dot(chosen, values, preferred_element_type=jnp.float32).astype(jnp.bfloat16)
+    permuted[...] = order
+    dot_columns(order, weight, (1 - place[0]) * half, give, half, 256)
 
 
 def own_kernel(place, permuted, weight, own):
-    dot_columns(permuted[...], weight, place[0] * own.shape[1], own, 256)
-
-
-def project(place, slots, blocks, scales, gain, weight, transpose):
+    half = own.shape[1]
+    dot_columns(permuted[...], weight, place[0] * half, own, half, 256)
+
+
+def project(kernel, place, slots, blocks, extra, weight, more):
     count = len(blocks)
     rows, depth = blocks[0].shape
     rows = rows * count
     half = weight.shape[1] // 2
     flops = 2 * rows * depth * half
-    scaled = scales is not None
-    extra = [*scales, gain] if scaled else []
     give, permuted = call(
-        functools.partial(project_kernel, count, transpose, scaled),
-        [struct((rows, half)), struct((rows, depth))],
+        functools.partial(kernel, count),
+        [struct((rows, half + more)), struct((rows, depth))],
         [SMEM, VMEM] + [VMEM] * (count + len(extra) + 1),
         [VMEM, VMEM],
         flops,
@@ -321,32 +326,62 @@
         flops,
         depth * half * 2,
     )(place, permuted, in_vmem(weight))
-    total = (own + received.astype(jnp.float32)).astype(jnp.bfloat16)
-    return total.reshape(count, rows // count, half)
+    total = (own + received[:, :half].astype(jnp.float32)).astype(jnp.bfloat16)
+    return total.reshape(count, rows // count, half), give, received
+
+
+def gathered(value, axis):
+    blocks = {0: value}
+    mask = lax.axis_size(axis) // 2
+    while mask:
+        blocks |= {known | mask: moved(block, axis, mask) for known, block in blocks.items()}
+        mask //= 2
+    return [blocks[i] for i in sorted(blocks)]
+
+
+def spread(products):
+    col_count, row_count = lax.axis_size("col"), lax.axis_size("row")
+    pairs = col_count // row_count
+    return [
+        lax.ppermute(
+            products[j],
+            ("col", "row"),
+            [
+                (
+                    col * row_count + row,
+                    ((row * pairs + col % pairs) ^ j) * row_count + col // pairs,
+                )
+                for col in range(col_count)
+                for row in range(row_count)
+            ],
+        )
+        for j in range(col_count)
+    ]
 
 
 def rotated(vector, cosine, sine):
     return vector * cosine + pltpu.roll(vector, HEAD_DIM // 2, 1) * sine
 
 
-def attend_all(count, place, cosine, sine, lengths, *refs):
-    kept, (arrived, keys, values, out) = refs[:count], refs[count:]
-    others, pairs, rows, _ = arrived.shape
-    cache = keys.shape[1]
-    base = place[2]
+def attend_all(count, others, place, cosine, sine, lengths, *refs):
+    blocks, sums, (keys, values, out) = refs[:count], refs[count : count + others], refs[-3:]
+    pairs = keys.shape[2] // HEAD_DIM
+    rows, cache = keys.shape[:2]
     low = place[1] % pairs
+    squares = sums[0][...]
+    for ref in sums[1:]:
+        squares = squares + ref[...]
+    scale = lax.rsqrt(jnp.sum(squares, axis=1, keepdims=True) / D + EPSILON)
     factor = HEAD_DIM ** (-0.5)
     cosines, sines = cosine[...], sine[...]
     lane = lax.broadcasted_iota(jnp.int32, (SLOTS, SLOTS * cache), 1)
     slot = lax.broadcasted_iota(jnp.int32, (SLOTS, SLOTS * cache), 0)
     for pair in range(pairs):
         column = low ^ pair
-        total = jnp.zeros(arrived.shape[2:], jnp.float32)
-        for chunk in range(count // pairs):
-            part = kept[chunk * pairs + pair][...].astype(jnp.float32)
-            total = total + jnp.where(base == chunk, part, 0.0)
-        for other in range(others):
-            total = total + arrived[other, pair].astype(jnp.float32)
+        total = blocks[pair][...].astype(jnp.float32)
+        for i in range(pair + pairs, count, pairs):
+            total = total + blocks[i][...].astype(jnp.float32)
+        total = total * scale
         total = total.astype(jnp.bfloat16).astype(jnp.float32)
         heads = [total[:, h * HEAD_DIM : (h + 1) * HEAD_DIM] for h in range(GROUP + 2)]
         queries = [
@@ -396,50 +431,34 @@
             out[:, pl.ds(at, HEAD_DIM)] = joined.astype(jnp.bfloat16)
 
 
-def finish_kernel(count, others, place, hidden, attended, given, *refs):
-    kept, refs = refs[:count], refs[count:]
-    near, refs = refs[0], refs[1:]
-    same, cross, out = refs[:others], refs[others : 2 * others], refs[2 * others]
-    pairs, _, width = near.shape
-    base = place[2]
+def sum_kernel(count, place, hidden, attended, *refs):
+    blocks, (keep, send) = refs[:count], refs[count:]
+    rows, width = blocks[0].shape
+    pairs = attended.shape[1] // width
+    side = place[0]
     low = place[1] % pairs
-
-    @pl.when(place[0] == 0)
-    def _():
-        for pair in range(pairs):
-            column = low ^ pair
-            total = jnp.zeros(near.shape[1:], jnp.float32)
-            for chunk in range(count // pairs):
-                part = kept[chunk * pairs + pair][...].astype(jnp.float32)
-                total = total + jnp.where(base == chunk, part, 0.0)
-            for ref in same:
-                total = total + ref[pair].astype(jnp.float32)
-            first = pl.ds(pl.multiple_of(column * 2 * width, width), width)
-            out[0, :, first] = (hidden[:, first].astype(jnp.float32) + total).astype(jnp.bfloat16)
-            total = near[pair].astype(jnp.float32)
-            for ref in cross:
-                total = total + ref[pair].astype(jnp.float32)
-            second = pl.ds(pl.multiple_of((column * 2 + 1) * width, width), width)
-            out[0, :, second] = (hidden[:, second].astype(jnp.float32) + total).astype(
-                jnp.bfloat16
-            )
-
-    @pl.when(place[0] != 0)
-    def _():
-        size = OUT_WIDTH
-        for j in range(attended.shape[1] // size):
-            out[0, :, 2 * j * size : (2 * j + 1) * size] = given[:, j * size : (j + 1) * size]
-            out[0, :, (2 * j + 1) * size : (2 * j + 2) * size] = attended[
-                :, j * size : (j + 1) * size
-            ]
-
-
-def chunk_of(blocks, pairs, index):
-    chunks = [jnp.stack(blocks[i : i + pairs]) for i in range(0, len(blocks), pairs)]
-    chosen = chunks[0]
-    for i, chunk in enumerate(chunks[1:], 1):
-        chosen = jnp.where(index == i, chunk, chosen)
-    return chosen
+    for pair in range(pairs):
+        column = low ^ pair
+        total = blocks[pair][...].astype(jnp.float32)
+        for i in range(pair + pairs, count, pairs):
+            total = total + blocks[i][...].astype(jnp.float32)
+        at = pl.ds(pl.multiple_of((2 * column + side) * width, width), width)
+        hidden_out = (hidden[:, at].astype(jnp.float32) + total).astype(jnp.bfloat16)
+        at = pl.ds(pl.multiple_of(column * width, width), width)
+        attention = attended[:, at]
+        keep[:, at] = jnp.where(side == 0, hidden_out, attention)
+        send[:, at] = jnp.where(side == 0, attention, hidden_out)
+
+
+def join_kernel(place, keep, received, out):
+    side = place[0]
+    width = OUT_WIDTH
+    for j in range(keep.shape[1] // width):
+        part = slice(j * width, (j + 1) * width)
+        out[0, :, pl.ds(pl.multiple_of((2 * j + side) * width, width), width)] = keep[:, part]
+        out[0, :, pl.ds(pl.multiple_of((2 * j + 1 - side) * width, width), width)] = received[
+            :, part
+        ]
 
 
 def paired_plan(
@@ -448,23 +467,14 @@
     col_count, row_count = lax.axis_size("col"), lax.axis_size("row")
     pairs = col_count // row_count
     side, col, row = (lax.axis_index(name) for name in ("side", "col", "row"))
-    base = lax.div(col, pairs) ^ row
-    place = jnp.stack([side, col, base]).astype(jnp.int32)
+    run = row * pairs + lax.rem(col, pairs)
+    place = jnp.stack([side, col, run]).astype(jnp.int32)
     rows, depth = hidden_in.shape
     half = depth // 2
     cache = key_cache.shape[1]
     slots = slot_request.reshape(col_count, rows, 1)
 
-    own_part = lax.dynamic_slice_in_dim(hidden_in, side * half, half, 1)
-    blocks = [own_part] + [moved(own_part, "col", mask) for mask in range(1, col_count)]
-    squares = call(
-        square_kernel, struct((rows, 128), jnp.float32), [VMEM], VMEM, rows * depth * 2, rows * depth * 2
-    )(hidden_in)
-    total = squares
-    for mask in range(1, row_count):
-        total = total + moved(squares, "row", mask)
-    scale = lax.rsqrt(total / D + EPSILON)
-    scales = [scale] + [moved(scale, "col", mask) for mask in range(1, col_count)]
+    blocks = gathered(lax.dynamic_slice_in_dim(hidden_in, side * half, half, 1), "col")
 
     weight_in = call(
         stage_in_kernel,
@@ -474,7 +484,7 @@
         0,
         half * qkv_weight.shape[1] * 2,
         [pltpu.SemaphoreType.DMA],
-    )(place, qkv_weight)
+    )(place, in_hbm(qkv_weight))
     weight_out, key_part, value_part = call(
         stage_rest_kernel,
         [
@@ -487,26 +497,22 @@
         0,
         half * out_weight.shape[1] * 2 + 4 * rows * cache * pairs * HEAD_DIM,
         [pltpu.SemaphoreType.DMA((3 * pairs,))],
-    )(place, out_weight, key_cache, value_cache)
-
-    products = project(
-        place, slots, blocks, scales, norm_gain.reshape(1, depth), weight_in, False
-    )
-    products = [products[0]] + [
-        moved(products[mask], "col", mask) for mask in range(1, col_count)
-    ]
-    arrived = jnp.stack(
-        [
-            moved(chunk_of(products, pairs, base ^ mask), "row", mask)
-            for mask in range(1, row_count)
-        ]
-    )
+    )(place, in_hbm(out_weight), in_hbm(key_cache), in_hbm(value_cache))
+
+    gain = norm_gain.reshape(1, depth)
+    products, given, received = project(
+        in_kernel, place, slots, blocks, [gain], weight_in, HEAD_DIM
+    )
+    products = spread(products)
+    sums = given[:, -HEAD_DIM:].astype(jnp.float32) + received[:, -HEAD_DIM:].astype(jnp.float32)
+    own_sums = lax.dynamic_slice_in_dim(sums, (run ^ col) * rows, rows, 0)
+    all_sums = [own_sums] + [moved(own_sums, "row", mask) for mask in range(1, row_count)]
 
     cosine, sine = rope_tables(cache_lengths, HEAD_DIM)
     attended = call(
-        functools.partial(attend_all, col_count),
+        functools.partial(attend_all, col_count, row_count),
         struct((rows, half)),
-        [SMEM] + [VMEM] * (3 + col_count + 3),
+        [SMEM] + [VMEM] * (3 + col_count + row_count + 2),
         VMEM,
         4 * rows * half * cache,
         0,
@@ -516,37 +522,31 @@
         jnp.concatenate([-sine, sine], axis=1),
         cache_lengths.reshape(rows, 1),
         *products,
-        arrived,
+        *all_sums,
         in_vmem(key_part),
         in_vmem(value_part),
     )
 
-    given = lax.ppermute(attended, "side", [(0, 1)])
-    blocks = [attended] + [moved(attended, "col", mask) for mask in range(1, col_count)]
-    products = project(place, slots, blocks, None, None, weight_out, True)
-    products = [products[0]] + [
-        moved(products[mask], "col", mask) for mask in range(1, col_count)
-    ]
-    near = lax.ppermute(chunk_of(products, pairs, base), "side", [(1, 0)])
-    same, cross = [], []
-    for mask in range(1, row_count):
-        chunk = chunk_of(products, pairs, base ^ mask)
-        for target, side_from in ((same, 0), (cross, 1)):
-            target.append(
-                lax.ppermute(
-                    chunk,
-                    ("row", "side"),
-                    [(2 * r + side_from, 2 * (r ^ mask)) for r in range(row_count)],
-                )
-            )
-    return call(
-        functools.partial(finish_kernel, col_count, row_count - 1),
-        struct((1, rows, depth)),
-        [SMEM] + [VMEM] * (3 + col_count + 1 + 2 * (row_count - 1)),
-        VMEM,
+    products, _, _ = project(
+        out_kernel, place, slots, gathered(attended, "col"), [], weight_out, 0
+    )
+    products = spread(products)
+    keep, send = call(
+        functools.partial(sum_kernel, col_count),
+        [struct((rows, half)), struct((rows, half))],
+        [SMEM] + [VMEM] * (2 + col_count),
+        [VMEM, VMEM],
         rows * depth * 4,
         rows * depth * 8,
-    )(place, hidden_in, attended, given, *products, near, *same, *cross)
+    )(place, hidden_in, attended, *products)
+    return call(
+        join_kernel,
+        struct((1, rows, depth)),
+        [SMEM, VMEM, VMEM],
+        VMEM,
+        0,
+        rows * depth * 4,
+    )(place, keep, moved(send, "side", 1))
 
 
 def per_device(*args):

time: 107 us -> 89.2 us (0.83)
  local copies, waits for them, and re-layouts: 25.9 us -> 10.6 us
  starting transfers between devices: 35.2 us -> 28 us
  Pallas kernels: 18.4 us -> 24.6 us
  waiting for transfers between devices: 26.5 us -> 24.3 us
    ppermute x19 -> x10, starting transfers between devices: 27.7 us -> 10.7 us  [moved(): return lax.ppermute(value, axis, pairs)]
    unnamed x18 -> x8, local copies, waits for them, and re-layouts: 23.3 us -> 7.98 us
    ppermute x4 -> x8, starting transfers between devices: 7.53 us -> 17.3 us  [spread(): lax.ppermute(products[j], ('col', 'row'), [(col * row_count + row, (row *...]
    ppermute x19 -> x10, waiting for transfers between devices: 21.5 us -> 17.9 us  [moved(): return lax.ppermute(value, axis, pairs)]
    pallas_call x1, Pallas kernels: 1.25 us -> 4.53 us  [paired_plan(): call(stage_in_kernel, pltpu.VMEM((half, qkv_weight.shape[1]), jnp.bfloat1...]
    pallas_call x1, Pallas kernels: 1.53 us -> 4.75 us  [paired_plan(): call(stage_rest_kernel, [pltpu.VMEM((half, out_weight.shape[1]), jnp.bflo...]
    ppermute x4 -> x8, waiting for transfers between devices: 4.97 us -> 6.44 us  [spread(): lax.ppermute(products[j], ('col', 'row'), [(col * row_count + row, (row *...]
  transfers between devices with their start and end apart: 23 -> 18, of which waited for: 10 -> 8; matrix products, arithmetic and copies ran while one was open for 3% -> 3% of each run, Pallas kernels for 6% -> 15%
where the time goes in v2:
time: 89.2 us; the launch traced here: 88.9 us
  starting transfers between devices  28 us (31%)
  Pallas kernels  24.6 us (28%)
  waiting for transfers between devices  24.3 us (27%)
  local copies, waits for them, and re-layouts  10.6 us (12%)
  other arithmetic  1.09 us (1%)
    ppermute x10, waiting for transfers between devices, moved(): return lax.ppermute(value, axis, pairs)  17.9 us
    ppermute x8, starting transfers between devices, spread(): lax.ppermute(products[j], ('col', 'row'), [(col * row_count + row, (row *...  17.3 us
    ppermute x10, starting transfers between devices, moved(): return lax.ppermute(value, axis, pairs)  10.7 us
    unnamed x8, local copies, waits for them, and re-layouts  7.98 us
    ppermute x8, waiting for transfers between devices, spread(): lax.ppermute(products[j], ('col', 'row'), [(col * row_count + row, (row *...  6.44 us
    pallas_call x2, Pallas kernels, project(): call(functools.partial(kernel, count), [struct((rows, half + more)), stru...  4.81 us
    pallas_call x1, Pallas kernels, paired_plan(): call(stage_rest_kernel, [pltpu.VMEM((half, out_weight.shape[1]), jnp.bflo...  4.75 us
    pallas_call x1, Pallas kernels, paired_plan(): call(functools.partial(attend_all, col_count, row_count), struct((rows, h...  4.6 us
  transfers between devices with their start and end apart: 18, of which 8 were waited for; matrix products, arithmetic and copies ran while one was open for 3% of the time, Pallas kernels for 15%

profile of v2, /device:TPU:0, one launch (start us, length us, event | category | flops | bytes accessed | tf_op | source)
XLA Modules:
  0.0 88.9 jit_solution(6887747599974263083)
XLA Ops:
  0.0 0.9 %constant_dynamic-slice_fusion.refs_0_ = bf16[32,2048]{1,0:T(8,128)(2,1)S(1)} fusion(bf16[32,4096]{1,0:T(8,128)(2,1)} %hidden.1, s32[]{:T(128)S(6)} %select_n.6), kind=kLoop, calls=%fused_computation.8 | loop fusion | bytes 262148 | tf_op jit(solution)/shard_map/dynamic_slice | solution.py:477
  0.9 4.1 %collective-permute-start.1 = (bf16[32,2048]{1,0:T(8,128)(2,1)S(1)}, bf16[32,2048]{1,0:T(8,128)(2,1)S(1)}, u32[]{:S(2)}, u32[]{:S(2)}) collective-permute-start(bf16[32,2048]{1,0:T(8,128)(2,1)S(1)} %constant_dynamic-slice_fusion.refs_0_), channel_id=1, source_target_pairs={{0,8},{4,12},{8,0},{12,4},{1,9},{5,13},{9,1},{13,5},{2,10},{6,14},... | collective-permute-start | bytes 393224 | tf_op jit(solution)/shard_map/ppermute | solution.py:205
  5.0 1.6 %collective-permute-start = (bf16[32,2048]{1,0:T(8,128)(2,1)S(1)}, bf16[32,2048]{1,0:T(8,128)(2,1)S(1)}, u32[]{:S(2)}, u32[]{:S(2)}) collective-permute-start(bf16[32,2048]{1,0:T(8,128)(2,1)S(1)} %constant_dynamic-slice_fusion.refs_0_), channel_id=1, source_target_pairs={{0,4},{4,0},{8,12},{12,8},{1,5},{5,1},{9,13},{13,9},{2,6},{6,2},{1... | collective-permute-start | bytes 393224 | tf_op jit(solution)/shard_map/ppermute | solution.py:205
  6.6 4.8 %collective-permute-done.1.refs_2_ = bf16[32,2048]{1,0:T(8,128)(2,1)S(1)} collective-permute-done((bf16[32,2048]{1,0:T(8,128)(2,1)S(1)}, bf16[32,2048]{1,0:T(8,128)(2,1)S(1)}, u32[]{:S(2)}, u32[]{:S(2)}) %collective-permute-start.1) | collective-permute-done | bytes 131104 | tf_op jit(solution)/shard_map/ppermute | solution.py:205
  11.4 0.6 collective-permute-start.2
  12.0 0.8 reshape.36.slots
  12.9 0.7 reshape.35.refs_4_
  13.6 0.7 convert_element_type.21
  14.3 0.1 pad_add_fusion.place
  14.4 4.5 %shard_map.82.refs_5_.weight = bf16[2048,2560]{1,0:T(8,128)(2,1)S(1)} custom-call(s32[3]{0:T(128)S(1)} %pad_add_fusion.place, bf16[4096,2560]{1,0:T(8,128)(2,1)} %weight.2), custom_call_target="tpu_custom_call" | custom-call | bytes 10485760 | tf_op jit(solution)/shard_map/pallas_call | solution.py:479
  18.9 4.0 %copy-done = bf16[2048,2560]{1,0:T(8,128)(2,1)} copy-done((bf16[2048,2560]{1,0:T(8,128)(2,1)}, bf16[2048,2560]{1,0:T(8,128)(2,1)S(1)}, u32[]{:S(2)}) %copy-start) | copy-done | bytes 10485784
  22.9 0.0 collective-permute-done.refs_1_
  22.9 0.0 collective-permute-done.2.refs_3_
  22.9 4.0 %copy-done.1 = bf16[2048,2560]{1,0:T(8,128)(2,1)S(1)} copy-done((bf16[2048,2560]{1,0:T(8,128)(2,1)S(1)}, bf16[2048,2560]{1,0:T(8,128)(2,1)}, u32[]{:S(2)}) %copy-start.1) | copy-done | bytes 10485784
  26.9 2.5 %shard_map.83 = (bf16[128,1408]{1,0:T(8,128)(2,1)S(1)}, bf16[128,2048]{1,0:T(8,128)(2,1)S(1)}) custom-call(s32[3]{0:T(128)S(1)} %pad_add_fusion.place, s32[4,32,1]{2,1,0:T(8,128)S(1)} %reshape.36.slots, bf16[32,2048]{1,0:T(8,128)(2,1)S(1)} %constant_dynamic-slice_fusion.refs_0_, bf16[32,2048]{1,0:T(8,128)(2,1)S(1)} %collective-permute-done.refs_1_, ...), custom_call_target="tpu_custom_call" | custom-call | flops 671088640 | bytes 5242880 | tf_op jit(solution)/shard_map/pallas_call | solution.py:312
  29.5 0.1 collective-permute-start.3
  29.5 0.1 fusion
  29.7 2.1 %shard_map.84 = f32[128,1280]{1,0:T(8,128)S(1)} custom-call(s32[3]{0:T(128)S(1)} %pad_add_fusion.place, bf16[128,2048]{1,0:T(8,128)(2,1)S(1)} %get-tuple-element.14.permuted, bf16[2048,2560]{1,0:T(8,128)(2,1)S(1)} %copy-done.1), custom_call_target="tpu_custom_call" | custom-call | flops 671088640 | bytes 5242880 | tf_op jit(solution)/shard_map/pallas_call | solution.py:321
  31.9 0.0 collective-permute-done.3
  31.9 1.5 %collective-permute-start.8 = (f32[32,128]{1,0:T(8,128)S(1)}, f32[32,128]{1,0:T(8,128)S(1)}, u32[]{:S(2)}, u32[]{:S(2)}) collective-permute-start(f32[32,128]{1,0:T(8,128)S(1)} %convert_add_fusion.refs_4_), channel_id=1, source_target_pairs={{0,2},{2,0},{1,3},{3,1},{4,6},{6,4},{5,7},{7,5},{8,10},{10,8},{9,1... | collective-permute-start | bytes 49160 | tf_op jit(solution)/shard_map/ppermute | solution.py:205
  33.4 0.1 add_convert_fusion
  33.5 0.7 collective-permute-start.4
  34.2 1.6 %collective-permute-start.5 = (bf16[32,1280]{1,0:T(8,128)(2,1)S(1)}, bf16[32,1280]{1,0:T(8,128)(2,1)S(1)}, u32[]{:S(2)}, u32[]{:S(2)}) collective-permute-start(bf16[32,1280]{1,0:T(8,128)(2,1)S(1)} %get-tuple-element.25), channel_id=1, source_target_pairs={{0,4},{2,12},{4,0},{6,8},{8,6},{10,14},{12,2},{14,10},{1,5},{3,13}... | collective-permute-start | bytes 245768 | tf_op jit(solution)/shard_map/ppermute | solution.py:346
  35.8 5.5 %collective-permute-start.6 = (bf16[32,1280]{1,0:T(8,128)(2,1)S(1)}, bf16[32,1280]{1,0:T(8,128)(2,1)S(1)}, u32[]{:S(2)}, u32[]{:S(2)}) collective-permute-start(bf16[32,1280]{1,0:T(8,128)(2,1)S(1)} %get-tuple-element.24), channel_id=1, source_target_pairs={{0,8},{2,0},{4,12},{6,4},{8,10},{10,2},{12,14},{14,6},{1,9},{3,1},... | collective-permute-start | bytes 245768 | tf_op jit(solution)/shard_map/ppermute | solution.py:346
  41.3 2.3 %collective-permute-start.7 = (bf16[32,1280]{1,0:T(8,128)(2,1)S(1)}, bf16[32,1280]{1,0:T(8,128)(2,1)S(1)}, u32[]{:S(2)}, u32[]{:S(2)}) collective-permute-start(bf16[32,1280]{1,0:T(8,128)(2,1)S(1)} %get-tuple-element.23), channel_id=1, source_target_pairs={{0,12},{2,4},{4,8},{6,0},{8,14},{10,6},{12,10},{14,2},{1,13},{3,5}... | collective-permute-start | bytes 245768 | tf_op jit(solution)/shard_map/ppermute | solution.py:346
  43.6 0.1 pad_maximum_fusion
  43.7 0.1 copy.10.lengths
  43.8 4.7 %shard_map.85 = (bf16[2048,2048]{1,0:T(8,128)(2,1)S(1)}, bf16[32,64,256]{2,1,0:T(8,128)(2,1)S(1)}, bf16[32,64,256]{2,1,0:T(8,128)(2,1)S(1)}) custom-call(s32[3]{0:T(128)S(1)} %pad_add_fusion.place, bf16[4096,2048]{1,0:T(8,128)(2,1)} %weight.3, bf16[32,64,512]{2,1,0:T(8,128)(2,1)} %keys.1, bf16[32,64,512]{2,1,0:T(8,128)(2,1)} %values.1), custom_call_target="tpu_custom_call" | custom-call | bytes 10485760 | tf_op jit(solution)/shard_map/pallas_call | solution.py:488
  48.6 0.7 collective-permute-done.7.refs_3_
  49.3 4.6 %shard_map.86.refs_0_.attended = bf16[32,2048]{1,0:T(8,128)(2,1)S(1)} custom-call(s32[3]{0:T(128)S(1)} %pad_add_fusion.place, f32[32,128]{1,0:T(8,128)S(1)} %get-tuple-element.34.cosine, f32[32,128]{1,0:T(8,128)S(1)} %get-tuple-element.35.sine, s32[32,1]{1,0:T(8,128)S(1)} %copy.10.lengths, bf16[32,1280]{1,0:T(8,128)(2,1)S(1)} %collective-permute-done.4.refs_0_, ...), custom_call_target="tpu_custom_call" | custom-call | flops 16777216 | tf_op jit(solution)/shard_map/pallas_call | solution.py:512
  53.9 2.6 %collective-permute-start.10 = (bf16[32,2048]{1,0:T(8,128)(2,1)S(1)}, bf16[32,2048]{1,0:T(8,128)(2,1)S(1)}, u32[]{:S(2)}, u32[]{:S(2)}) collective-permute-start(bf16[32,2048]{1,0:T(8,128)(2,1)S(1)} %shard_map.86.refs_0_.attended), channel_id=1, source_target_pairs={{0,8},{4,12},{8,0},{12,4},{1,9},{5,13},{9,1},{13,5},{2,10},{6,14},... | collective-permute-start | bytes 393224 | tf_op jit(solution)/shard_map/ppermute | solution.py:205
  56.6 6.5 %collective-permute-done.10.refs_2_ = bf16[32,2048]{1,0:T(8,128)(2,1)S(1)} collective-permute-done((bf16[32,2048]{1,0:T(8,128)(2,1)S(1)}, bf16[32,2048]{1,0:T(8,128)(2,1)S(1)}, u32[]{:S(2)}, u32[]{:S(2)}) %collective-permute-start.10) | collective-permute-done | bytes 131104 | tf_op jit(solution)/shard_map/ppermute | solution.py:205
  63.1 1.1 %collective-permute-done.9.refs_1_ = bf16[32,2048]{1,0:T(8,128)(2,1)S(1)} collective-permute-done((bf16[32,2048]{1,0:T(8,128)(2,1)S(1)}, bf16[32,2048]{1,0:T(8,128)(2,1)S(1)}, u32[]{:S(2)}, u32[]{:S(2)}) %collective-permute-start.9) | collective-permute-done | bytes 131104 | tf_op jit(solution)/shard_map/ppermute | solution.py:205
  64.2 4.1 %collective-permute-done.11.refs_3_ = bf16[32,2048]{1,0:T(8,128)(2,1)S(1)} collective-permute-done((bf16[32,2048]{1,0:T(8,128)(2,1)S(1)}, bf16[32,2048]{1,0:T(8,128)(2,1)S(1)}, u32[]{:S(2)}, u32[]{:S(2)}) %collective-permute-start.11) | collective-permute-done | bytes 131104 | tf_op jit(solution)/shard_map/ppermute | solution.py:205
  68.3 2.3 %shard_map.87 = (bf16[128,1024]{1,0:T(8,128)(2,1)S(1)}, bf16[128,2048]{1,0:T(8,128)(2,1)S(1)}) custom-call(s32[3]{0:T(128)S(1)} %pad_add_fusion.place, s32[4,32,1]{2,1,0:T(8,128)S(1)} %reshape.36.slots, bf16[32,2048]{1,0:T(8,128)(2,1)S(1)} %shard_map.86.refs_0_.attended, bf16[32,2048]{1,0:T(8,128)(2,1)S(1)} %collective-permute-done.9.refs_1_, ...), custom_call_target="tpu_custom_call" | custom-call | flops 536870912 | bytes 4194304 | tf_op jit(solution)/shard_map/pallas_call | solution.py:312
  70.6 0.1 collective-permute-start.12
  70.7 1.9 %shard_map.88 = f32[128,1024]{1,0:T(8,128)S(1)} custom-call(s32[3]{0:T(128)S(1)} %pad_add_fusion.place, bf16[128,2048]{1,0:T(8,128)(2,1)S(1)} %get-tuple-element.19.permuted, bf16[2048,2048]{1,0:T(8,128)(2,1)S(1)} %get-tuple-element.18.refs_4_.weight), custom_call_target="tpu_custom_call" | custom-call | flops 536870912 | bytes 4194304 | tf_op jit(solution)/shard_map/pallas_call | solution.py:321
  72.6 0.1 add_convert_fusion.1
  72.7 0.7 collective-permute-start.13
  73.3 0.3 collective-permute-start.14
  73.7 5.4 %collective-permute-start.15 = (bf16[32,1024]{1,0:T(8,128)(2,1)S(1)}, bf16[32,1024]{1,0:T(8,128)(2,1)S(1)}, u32[]{:S(2)}, u32[]{:S(2)}) collective-permute-start(bf16[32,1024]{1,0:T(8,128)(2,1)S(1)} %get-tuple-element.28), channel_id=1, source_target_pairs={{0,8},{2,0},{4,12},{6,4},{8,10},{10,2},{12,14},{14,6},{1,9},{3,1},... | collective-permute-start | bytes 196616 | tf_op jit(solution)/shard_map/ppermute | solution.py:346
  79.0 0.8 collective-permute-start.16
  79.9 1.4 %collective-permute-done.15.refs_2_ = bf16[32,1024]{1,0:T(8,128)(2,1)S(1)} collective-permute-done((bf16[32,1024]{1,0:T(8,128)(2,1)S(1)}, bf16[32,1024]{1,0:T(8,128)(2,1)S(1)}, u32[]{:S(2)}, u32[]{:S(2)}) %collective-permute-start.15) | collective-permute-done | bytes 65568 | tf_op jit(solution)/shard_map/ppermute | solution.py:346
  81.3 4.3 %collective-permute-done.16.refs_3_ = bf16[32,1024]{1,0:T(8,128)(2,1)S(1)} collective-permute-done((bf16[32,1024]{1,0:T(8,128)(2,1)S(1)}, bf16[32,1024]{1,0:T(8,128)(2,1)S(1)}, u32[]{:S(2)}, u32[]{:S(2)}) %collective-permute-start.16) | collective-permute-done | bytes 65568 | tf_op jit(solution)/shard_map/ppermute | solution.py:346
  85.6 0.6 shard_map.89
  86.2 0.1 collective-permute-start.17
  86.3 1.3 %collective-permute-done.17.received = bf16[32,2048]{1,0:T(8,128)(2,1)S(1)} collective-permute-done((bf16[32,2048]{1,0:T(8,128)(2,1)S(1)}, bf16[32,2048]{1,0:T(8,128)(2,1)S(1)}, u32[]{:S(2)}, u32[]{:S(2)}) %collective-permute-start.17) | collective-permute-done | bytes 131104 | tf_op jit(solution)/shard_map/ppermute | solution.py:205
  87.6 1.3 %shard_map.90 = bf16[1,32,4096]{2,1,0:T(8,128)(2,1)} custom-call(s32[3]{0:T(128)S(1)} %pad_add_fusion.place, bf16[32,2048]{1,0:T(8,128)(2,1)S(1)} %get-tuple-element.21.keep, bf16[32,2048]{1,0:T(8,128)(2,1)S(1)} %collective-permute-done.17.received), custom_call_target="tpu_custom_call" | custom-call | bytes 524288 | tf_op jit(solution)/shard_map/pallas_call | solution.py:542
  (21 shorter events, 0.1 us)
Async XLA Ops:
  0.9 10.5 %collective-permute-start.1 = (bf16[32,2048]{1,0:T(8,128)(2,1)S(1)}, bf16[32,2048]{1,0:T(8,128)(2,1)S(1)}, u32[]{:S(2)}, u32[]{:S(2)}) collective-permute-start(bf16[32,2048]{1,0:T(8,128)(2,1)S(1)} %constant_dynamic-slice_fusion.refs_0_), channel_id=1, source_target_pairs={{0,8},{4,12},{8,0},{12,4},{1,9},{5,13},{9,1},{13,5},{2,10},{6,14},... | collective-permute-start | bytes 393224 | tf_op jit(solution)/shard_map/ppermute | solution.py:205
  5.0 17.9 %collective-permute-start = (bf16[32,2048]{1,0:T(8,128)(2,1)S(1)}, bf16[32,2048]{1,0:T(8,128)(2,1)S(1)}, u32[]{:S(2)}, u32[]{:S(2)}) collective-permute-start(bf16[32,2048]{1,0:T(8,128)(2,1)S(1)} %constant_dynamic-slice_fusion.refs_0_), channel_id=1, source_target_pairs={{0,4},{4,0},{8,12},{12,8},{1,5},{5,1},{9,13},{13,9},{2,6},{6,2},{1... | collective-permute-start | bytes 393224 | tf_op jit(solution)/shard_map/ppermute | solution.py:205
  11.4 11.5 %collective-permute-start.2 = (bf16[32,2048]{1,0:T(8,128)(2,1)S(1)}, bf16[32,2048]{1,0:T(8,128)(2,1)S(1)}, u32[]{:S(2)}, u32[]{:S(2)}) collective-permute-start(bf16[32,2048]{1,0:T(8,128)(2,1)S(1)} %collective-permute-done.1.refs_2_), channel_id=1, source_target_pairs={{0,4},{4,0},{8,12},{12,8},{1,5},{5,1},{9,13},{13,9},{2,6},{6,2},{1... | collective-permute-start | bytes 393224 | tf_op jit(solution)/shard_map/ppermute | solution.py:205
  18.9 4.0 %copy-start = (bf16[2048,2560]{1,0:T(8,128)(2,1)}, bf16[2048,2560]{1,0:T(8,128)(2,1)S(1)}, u32[]{:S(2)}) copy-start(bf16[2048,2560]{1,0:T(8,128)(2,1)S(1)} %shard_map.82.refs_5_.weight) | copy-start | bytes 31457284
  22.9 20.8 %copy-start.3 = (s32[32]{0:T(128)S(1)}, s32[32]{0:T(128)}, u32[]{:S(2)}) copy-start(s32[32]{0:T(128)} %param.14) | copy-start | bytes 388
  22.9 4.0 %copy-start.1 = (bf16[2048,2560]{1,0:T(8,128)(2,1)S(1)}, bf16[2048,2560]{1,0:T(8,128)(2,1)}, u32[]{:S(2)}) copy-start(bf16[2048,2560]{1,0:T(8,128)(2,1)} %copy-done) | copy-start | bytes 31457284
  29.5 2.4 %collective-permute-start.3 = (bf16[128,1408]{1,0:T(8,128)(2,1)S(1)}, bf16[128,1408]{1,0:T(8,128)(2,1)S(1)}, u32[]{:S(2)}, u32[]{:S(2)}) collective-permute-start(bf16[128,1408]{1,0:T(8,128)(2,1)S(1)} %get-tuple-element.15), channel_id=1, source_target_pairs={{0,1},{1,0},{2,3},{3,2},{4,5},{5,4},{6,7},{7,6},{8,9},{9,8},{10,11... | collective-permute-start | bytes 1081352 | tf_op jit(solution)/shard_map/ppermute | solution.py:205
  31.9 16.7 %collective-permute-start.8 = (f32[32,128]{1,0:T(8,128)S(1)}, f32[32,128]{1,0:T(8,128)S(1)}, u32[]{:S(2)}, u32[]{:S(2)}) collective-permute-start(f32[32,128]{1,0:T(8,128)S(1)} %convert_add_fusion.refs_4_), channel_id=1, source_target_pairs={{0,2},{2,0},{1,3},{3,1},{4,6},{6,4},{5,7},{7,5},{8,10},{10,8},{9,1... | collective-permute-start | bytes 49160 | tf_op jit(solution)/shard_map/ppermute | solution.py:205
  33.5 15.0 %collective-permute-start.4 = (bf16[32,1280]{1,0:T(8,128)(2,1)S(1)}, bf16[32,1280]{1,0:T(8,128)(2,1)S(1)}, u32[]{:S(2)}, u32[]{:S(2)}) collective-permute-start(bf16[32,1280]{1,0:T(8,128)(2,1)S(1)} %get-tuple-element.26), channel_id=1, source_target_pairs={{0,0},{2,8},{4,4},{6,12},{8,2},{10,10},{12,6},{14,14},{1,1},{3,9},... | collective-permute-start | bytes 245768 | tf_op jit(solution)/shard_map/ppermute | solution.py:346
  34.2 14.4 %collective-permute-start.5 = (bf16[32,1280]{1,0:T(8,128)(2,1)S(1)}, bf16[32,1280]{1,0:T(8,128)(2,1)S(1)}, u32[]{:S(2)}, u32[]{:S(2)}) collective-permute-start(bf16[32,1280]{1,0:T(8,128)(2,1)S(1)} %get-tuple-element.25), channel_id=1, source_target_pairs={{0,4},{2,12},{4,0},{6,8},{8,6},{10,14},{12,2},{14,10},{1,5},{3,13}... | collective-permute-start | bytes 245768 | tf_op jit(solution)/shard_map/ppermute | solution.py:346
  35.8 12.8 %collective-permute-start.6 = (bf16[32,1280]{1,0:T(8,128)(2,1)S(1)}, bf16[32,1280]{1,0:T(8,128)(2,1)S(1)}, u32[]{:S(2)}, u32[]{:S(2)}) collective-permute-start(bf16[32,1280]{1,0:T(8,128)(2,1)S(1)} %get-tuple-element.24), channel_id=1, source_target_pairs={{0,8},{2,0},{4,12},{6,4},{8,10},{10,2},{12,14},{14,6},{1,9},{3,1},... | collective-permute-start | bytes 245768 | tf_op jit(solution)/shard_map/ppermute | solution.py:346
  41.3 8.0 %collective-permute-start.7 = (bf16[32,1280]{1,0:T(8,128)(2,1)S(1)}, bf16[32,1280]{1,0:T(8,128)(2,1)S(1)}, u32[]{:S(2)}, u32[]{:S(2)}) collective-permute-start(bf16[32,1280]{1,0:T(8,128)(2,1)S(1)} %get-tuple-element.23), channel_id=1, source_target_pairs={{0,12},{2,4},{4,8},{6,0},{8,14},{10,6},{12,10},{14,2},{1,13},{3,5}... | collective-permute-start | bytes 245768 | tf_op jit(solution)/shard_map/ppermute | solution.py:346
  53.9 31.7 %copy-start.2 = (bf16[32,4096]{1,0:T(8,128)(2,1)S(1)}, bf16[32,4096]{1,0:T(8,128)(2,1)}, u32[]{:S(2)}) copy-start(bf16[32,4096]{1,0:T(8,128)(2,1)} %hidden.1) | copy-start | bytes 786436
  53.9 9.2 %collective-permute-start.10 = (bf16[32,2048]{1,0:T(8,128)(2,1)S(1)}, bf16[32,2048]{1,0:T(8,128)(2,1)S(1)}, u32[]{:S(2)}, u32[]{:S(2)}) collective-permute-start(bf16[32,2048]{1,0:T(8,128)(2,1)S(1)} %shard_map.86.refs_0_.attended), channel_id=1, source_target_pairs={{0,8},{4,12},{8,0},{12,4},{1,9},{5,13},{9,1},{13,5},{2,10},{6,14},... | collective-permute-start | bytes 393224 | tf_op jit(solution)/shard_map/ppermute | solution.py:205
  56.6 7.6 %collective-permute-start.9 = (bf16[32,2048]{1,0:T(8,128)(2,1)S(1)}, bf16[32,2048]{1,0:T(8,128)(2,1)S(1)}, u32[]{:S(2)}, u32[]{:S(2)}) collective-permute-start(bf16[32,2048]{1,0:T(8,128)(2,1)S(1)} %shard_map.86.refs_0_.attended), channel_id=1, source_target_pairs={{0,4},{4,0},{8,12},{12,8},{1,5},{5,1},{9,13},{13,9},{2,6},{6,2},{1... | collective-permute-start | bytes 393224 | tf_op jit(solution)/shard_map/ppermute | solution.py:205
  63.1 5.2 %collective-permute-start.11 = (bf16[32,2048]{1,0:T(8,128)(2,1)S(1)}, bf16[32,2048]{1,0:T(8,128)(2,1)S(1)}, u32[]{:S(2)}, u32[]{:S(2)}) collective-permute-start(bf16[32,2048]{1,0:T(8,128)(2,1)S(1)} %collective-permute-done.10.refs_2_), channel_id=1, source_target_pairs={{0,4},{4,0},{8,12},{12,8},{1,5},{5,1},{9,13},{13,9},{2,6},{6,2},{1... | collective-permute-start | bytes 393224 | tf_op jit(solution)/shard_map/ppermute | solution.py:205
  70.6 2.0 %collective-permute-start.12 = (bf16[128,1024]{1,0:T(8,128)(2,1)S(1)}, bf16[128,1024]{1,0:T(8,128)(2,1)S(1)}, u32[]{:S(2)}, u32[]{:S(2)}) collective-permute-start(bf16[128,1024]{1,0:T(8,128)(2,1)S(1)} %get-tuple-element.20), channel_id=1, source_target_pairs={{0,1},{1,0},{2,3},{3,2},{4,5},{5,4},{6,7},{7,6},{8,9},{9,8},{10,11... | collective-permute-start | bytes 786440 | tf_op jit(solution)/shard_map/ppermute | solution.py:205
  72.7 7.2 %collective-permute-start.13 = (bf16[32,1024]{1,0:T(8,128)(2,1)S(1)}, bf16[32,1024]{1,0:T(8,128)(2,1)S(1)}, u32[]{:S(2)}, u32[]{:S(2)}) collective-permute-start(bf16[32,1024]{1,0:T(8,128)(2,1)S(1)} %get-tuple-element.30), channel_id=1, source_target_pairs={{0,0},{2,8},{4,4},{6,12},{8,2},{10,10},{12,6},{14,14},{1,1},{3,9},... | collective-permute-start | bytes 196616 | tf_op jit(solution)/shard_map/ppermute | solution.py:346
  73.3 6.6 %collective-permute-start.14 = (bf16[32,1024]{1,0:T(8,128)(2,1)S(1)}, bf16[32,1024]{1,0:T(8,128)(2,1)S(1)}, u32[]{:S(2)}, u32[]{:S(2)}) collective-permute-start(bf16[32,1024]{1,0:T(8,128)(2,1)S(1)} %get-tuple-element.29), channel_id=1, source_target_pairs={{0,4},{2,12},{4,0},{6,8},{8,6},{10,14},{12,2},{14,10},{1,5},{3,13}... | collective-permute-start | bytes 196616 | tf_op jit(solution)/shard_map/ppermute | solution.py:346
  73.7 7.7 %collective-permute-start.15 = (bf16[32,1024]{1,0:T(8,128)(2,1)S(1)}, bf16[32,1024]{1,0:T(8,128)(2,1)S(1)}, u32[]{:S(2)}, u32[]{:S(2)}) collective-permute-start(bf16[32,1024]{1,0:T(8,128)(2,1)S(1)} %get-tuple-element.28), channel_id=1, source_target_pairs={{0,8},{2,0},{4,12},{6,4},{8,10},{10,2},{12,14},{14,6},{1,9},{3,1},... | collective-permute-start | bytes 196616 | tf_op jit(solution)/shard_map/ppermute | solution.py:346
  79.0 6.5 %collective-permute-start.16 = (bf16[32,1024]{1,0:T(8,128)(2,1)S(1)}, bf16[32,1024]{1,0:T(8,128)(2,1)S(1)}, u32[]{:S(2)}, u32[]{:S(2)}) collective-permute-start(bf16[32,1024]{1,0:T(8,128)(2,1)S(1)} %get-tuple-element.27), channel_id=1, source_target_pairs={{0,12},{2,4},{4,8},{6,0},{8,14},{10,6},{12,10},{14,2},{1,13},{3,5}... | collective-permute-start | bytes 196616 | tf_op jit(solution)/shard_map/ppermute | solution.py:346
  86.2 1.4 %collective-permute-start.17 = (bf16[32,2048]{1,0:T(8,128)(2,1)S(1)}, bf16[32,2048]{1,0:T(8,128)(2,1)S(1)}, u32[]{:S(2)}, u32[]{:S(2)}) collective-permute-start(bf16[32,2048]{1,0:T(8,128)(2,1)S(1)} %get-tuple-element.22), channel_id=1, source_target_pairs={{0,1},{1,0},{2,3},{3,2},{4,5},{5,4},{6,7},{7,6},{8,9},{9,8},{10,11... | collective-permute-start | bytes 393224 | tf_op jit(solution)/shard_map/ppermute | solution.py:205

commit v3 on v2

--- a/solution.py
+++ b/solution.py
@@ -205,18 +205,48 @@
     return lax.ppermute(value, axis, pairs)
 
 
-def stage_in_kernel(place, weight, staged, sem):
-    depth = staged.shape[0]
-    first = pl.multiple_of(place[0] * depth, depth)
-    copy = pltpu.make_async_copy(weight.at[pl.ds(first, depth), :], staged, sem)
+def slice_kernel(place, source, part, sem):
+    width = part.shape[1]
+    columns = pl.ds(pl.multiple_of(place[0] * width, width), width)
+    copy = pltpu.make_async_copy(source.at[:, columns], part, sem)
     copy.start()
     copy.wait()
 
 
-def stage_rest_kernel(place, weight, keys, values, staged, key_part, value_part, sems):
-    pairs = staged.shape[0] // OUT_WIDTH
+def halves(place, weight, staged, row, target_row, size):
+    width = staged[0].shape[1]
     copies = []
-    for j in range(pairs):
+    for target, half in zip(staged, (1 - place[0], place[0])):
+        columns = pl.ds(pl.multiple_of(half * width, width), width)
+        copies.append(
+            (weight.at[pl.ds(row, size), columns], target.at[pl.ds(target_row, size), :])
+        )
+    return copies
+
+
+def run_copies(copies, sems):
+    copies = [
+        pltpu.make_async_copy(source, target, sems.at[i])
+        for i, (source, target) in enumerate(copies)
+    ]
+    for copy in copies:
+        copy.start()
+    for copy in copies:
+        copy.wait()
+
+
+def stage_in_kernel(place, weight, *refs):
+    give_part, own_part, sems = refs[-3:]
+    depth = own_part.shape[0]
+    first = pl.multiple_of(place[0] * depth, depth)
+    run_copies(halves(place, weight, (give_part, own_part), first, 0, depth), sems)
+
+
+def stage_rest_kernel(
+    place, weight, keys, values, give_part, own_part, key_part, value_part, sems
+):
+    copies = []
+    for j in range(own_part.shape[0] // OUT_WIDTH):
         head = 2 * j + place[0]
         row = pl.multiple_of(head * OUT_WIDTH, OUT_WIDTH)
         lane = pl.multiple_of(head * HEAD_DIM, HEAD_DIM)
@@ -227,17 +257,10 @@
                     target.at[:, :, pl.ds(j * HEAD_DIM, HEAD_DIM)],
                 )
             )
-        copies.append(
-            (weight.at[pl.ds(row, OUT_WIDTH), :], staged.at[pl.ds(j * OUT_WIDTH, OUT_WIDTH), :])
+        copies += halves(
+            place, weight, (give_part, own_part), row, j * OUT_WIDTH, OUT_WIDTH
         )
-    copies = [
-        pltpu.make_async_copy(source, target, sems.at[i])
-        for i, (source, target) in enumerate(copies)
-    ]
-    for copy in copies:
-        copy.start()
-    for copy in copies:
-        copy.wait()
+    run_copies(copies, sems)
 
 
 def one_hot(slots, slot_base, request_base):
@@ -257,25 +280,19 @@
     return jnp.where(lane < 3, parts, 0.0).astype(jnp.bfloat16)
 
 
-def dot_columns(rows, weight, first, out, size, width):
-    def step(i, carry):
-        start = pl.multiple_of(i * width, width)
-        part = jnp.dot(
-            rows,
-            weight[:, pl.ds(pl.multiple_of(first + start, width), width)],
-            preferred_element_type=jnp.float32,
-        )
-        out[:, pl.ds(start, width)] = part.astype(out.dtype)
-        return carry
-
-    lax.fori_loop(0, size // width, step, 0)
+def dot_columns(rows, weight, out):
+    size, width = weight.shape[1], 512
+    for start in range(0, size, width):
+        part = slice(start, min(start + width, size))
+        product = jnp.dot(rows, weight[:, part], preferred_element_type=jnp.float32)
+        out[:, part] = product.astype(out.dtype)
 
 
 def in_kernel(count, place, slots, *refs):
     blocks, (gain, weight, give, permuted) = refs[:count], refs[count:]
     side = place[0]
     depth = blocks[0].shape[1]
-    half = weight.shape[1] // 2
+    half = weight.shape[1]
     gains = gain[:, pl.ds(pl.multiple_of(side * depth, depth), depth)].astype(jnp.float32)
     values = jnp.concatenate([block[...].astype(jnp.float32) for block in blocks], axis=0)
     sums = pieces(jnp.sum(values * values, axis=1, keepdims=True))
@@ -285,29 +302,42 @@
     ).astype(jnp.bfloat16)
     permuted[...] = order
     give[:, half:] = jnp.dot(chosen, sums, preferred_element_type=jnp.float32).astype(jnp.bfloat16)
-    dot_columns(order, weight, (1 - side) * half, give, half, 256)
+    dot_columns(order, weight, give)
 
 
 def out_kernel(count, place, slots, *refs):
     blocks, (weight, give, permuted) = refs[:count], refs[count:]
-    half = weight.shape[1] // 2
     values = jnp.concatenate([block[...] for block in blocks], axis=0)
     chosen = one_hot(slots, place[1], place[2]).T.astype(jnp.bfloat16)
     order = jnp.dot(chosen, values, preferred_element_type=jnp.float32).astype(jnp.bfloat16)
     permuted[...] = order
-    dot_columns(order, weight, (1 - place[0]) * half, give, half, 256)
-
-
-def own_kernel(place, permuted, weight, own):
+    dot_columns(order, weight, give)
+
+
+def merge_kernel(own, given, received, *outs):
+    rows = outs[0].shape[0]
     half = own.shape[1]
-    dot_columns(permuted[...], weight, place[0] * half, own, half, 256)
-
-
-def project(kernel, place, slots, blocks, extra, weight, more):
+    more = given.shape[1] - half
+    for i, out in enumerate(outs):
+        part = slice(i * rows, (i + 1) * rows)
+        total = own[part, :] + received[part, :half].astype(jnp.float32)
+        out[:, :half] = total.astype(jnp.bfloat16)
+        if out.shape[1] > half:
+            out[:, half:] = jnp.concatenate(
+                [given[part, half : half + more // 2], received[part, half : half + more // 2]],
+                axis=1,
+            )
+
+
+def own_kernel(permuted, weight, own):
+    dot_columns(permuted[...], weight, own)
+
+
+def project(kernel, place, slots, blocks, extra, weights, more, pairs):
     count = len(blocks)
     rows, depth = blocks[0].shape
     rows = rows * count
-    half = weight.shape[1] // 2
+    half = weights[0].shape[1]
     flops = 2 * rows * depth * half
     give, permuted = call(
         functools.partial(kernel, count),
@@ -316,18 +346,26 @@
         [VMEM, VMEM],
         flops,
         depth * half * 2,
-    )(place, slots, *blocks, *extra, in_vmem(weight))
+    )(place, slots, *blocks, *extra, in_vmem(weights[0]))
     received = moved(give, "side", 1)
     own = call(
         own_kernel,
         struct((rows, half), jnp.float32),
-        [SMEM, VMEM, VMEM],
+        [VMEM, VMEM],
         VMEM,
         flops,
         depth * half * 2,
-    )(place, permuted, in_vmem(weight))
-    total = (own + received[:, :half].astype(jnp.float32)).astype(jnp.bfloat16)
-    return total.reshape(count, rows // count, half), give, received
+    )(permuted, in_vmem(weights[1]))
+    return call(
+        merge_kernel,
+        [
+            struct((rows // count, half + (0 if i % pairs else more))) for i in range(count)
+        ],
+        [VMEM] * 3,
+        [VMEM] * count,
+        rows * half,
+        rows * half * 8,
+    )(own, give, received)
 
 
 def gathered(value, axis):
@@ -363,54 +401,52 @@
     return vector * cosine + pltpu.roll(vector, HEAD_DIM // 2, 1) * sine
 
 
-def attend_all(count, others, place, cosine, sine, lengths, *refs):
-    blocks, sums, (keys, values, out) = refs[:count], refs[count : count + others], refs[-3:]
+def attend_all(count, place, cosine, sine, lengths, *refs):
+    blocks, (keys, values, out, scores_of, probs_of) = refs[:count], refs[count:]
     pairs = keys.shape[2] // HEAD_DIM
     rows, cache = keys.shape[:2]
     low = place[1] % pairs
-    squares = sums[0][...]
-    for ref in sums[1:]:
-        squares = squares + ref[...]
+    width = GROUP_WIDTH
+    squares = blocks[0][:, width:].astype(jnp.float32)
+    for i in range(pairs, count, pairs):
+        squares = squares + blocks[i][:, width:].astype(jnp.float32)
     scale = lax.rsqrt(jnp.sum(squares, axis=1, keepdims=True) / D + EPSILON)
     factor = HEAD_DIM ** (-0.5)
     cosines, sines = cosine[...], sine[...]
     lane = lax.broadcasted_iota(jnp.int32, (SLOTS, SLOTS * cache), 1)
     slot = lax.broadcasted_iota(jnp.int32, (SLOTS, SLOTS * cache), 0)
+    position = lane - slot * cache
+    runs = [slice(start, start + SLOTS) for start in range(0, rows, SLOTS)]
+    filled = [(position >= 0) & (position < lengths[part]) for part in runs]
+    own, new_values, own_probs = [], [], []
     for pair in range(pairs):
-        column = low ^ pair
-        total = blocks[pair][...].astype(jnp.float32)
+        total = blocks[pair][:, :width].astype(jnp.float32)
         for i in range(pair + pairs, count, pairs):
-            total = total + blocks[i][...].astype(jnp.float32)
-        total = total * scale
-        total = total.astype(jnp.bfloat16).astype(jnp.float32)
+            total = total + blocks[i][:, :width].astype(jnp.float32)
+        total = (total * scale).astype(jnp.bfloat16).astype(jnp.float32)
         heads = [total[:, h * HEAD_DIM : (h + 1) * HEAD_DIM] for h in range(GROUP + 2)]
         queries = [
             rotated(head, cosines, sines).astype(jnp.bfloat16).astype(jnp.float32)
             for head in heads[:GROUP]
         ]
         new_key = rotated(heads[GROUP], cosines, sines).astype(jnp.bfloat16).astype(jnp.float32)
-        new_value = heads[GROUP + 1]
-        own = [jnp.sum(query * new_key, axis=1, keepdims=True) * factor for query in queries]
-        lanes = pl.ds(pl.multiple_of(column * HEAD_DIM, HEAD_DIM), HEAD_DIM)
-        results = []
-        for start in range(0, rows, SLOTS):
-            part = slice(start, start + SLOTS)
+        new_values.append(heads[GROUP + 1])
+        own.append([jnp.sum(query * new_key, axis=1, keepdims=True) * factor for query in queries])
+        lanes = pl.ds(pl.multiple_of((low ^ pair) * HEAD_DIM, HEAD_DIM), HEAD_DIM)
+        for run, part in enumerate(runs):
             query = jnp.concatenate([head[part] for head in queries], axis=0)
-            key = keys[start : start + SLOTS, :, lanes].reshape(SLOTS * cache, HEAD_DIM)
-            value = values[start : start + SLOTS, :, lanes].reshape(SLOTS * cache, HEAD_DIM)
-            scores = (
-                lax.dot_general(
-                    query.astype(jnp.bfloat16),
-                    key,
-                    (((1,), (1,)), ((), ())),
-                    preferred_element_type=jnp.float32,
-                )
-                * factor
-            ).reshape(GROUP, SLOTS, SLOTS * cache)
-            position = lane - slot * cache
-            filled = (position >= 0) & (position < lengths[part])
-            scores = jnp.where(filled[None], scores, -1e30)
-            own_score = jnp.concatenate([head[part] for head in own], axis=0).reshape(
+            key = keys[part, :, lanes].reshape(SLOTS * cache, HEAD_DIM)
+            scores_of[pair, run] = lax.dot_general(
+                query.astype(jnp.bfloat16),
+                key,
+                (((1,), (1,)), ((), ())),
+                preferred_element_type=jnp.float32,
+            )
+    for pair in range(pairs):
+        for run, part in enumerate(runs):
+            scores = (scores_of[pair, run] * factor).reshape(GROUP, SLOTS, SLOTS * cache)
+            scores = jnp.where(filled[run][None], scores, -1e30)
+            own_score = jnp.concatenate([head[part] for head in own[pair]], axis=0).reshape(
                 GROUP, SLOTS, 1
             )
             highest = jnp.maximum(jnp.max(scores, axis=2, keepdims=True), own_score)
@@ -418,16 +454,21 @@
             own_weight = jnp.exp(own_score - highest)
             inverse = 1.0 / (jnp.sum(weights, axis=2, keepdims=True) + own_weight)
             probs = (weights * inverse).astype(jnp.bfloat16)
-            own_prob = (own_weight * inverse).astype(jnp.bfloat16).astype(jnp.float32)
-            mixed = jnp.dot(
-                probs.reshape(GROUP * SLOTS, SLOTS * cache),
-                value,
-                preferred_element_type=jnp.float32,
-            ).reshape(GROUP, SLOTS, HEAD_DIM)
-            results.append(mixed + own_prob * new_value[part][None])
+            probs_of[pair, run] = probs.reshape(GROUP * SLOTS, SLOTS * cache)
+            own_probs.append((own_weight * inverse).astype(jnp.bfloat16).astype(jnp.float32))
+    for pair in range(pairs):
+        lanes = pl.ds(pl.multiple_of((low ^ pair) * HEAD_DIM, HEAD_DIM), HEAD_DIM)
+        results = []
+        for run, part in enumerate(runs):
+            value = values[part, :, lanes].reshape(SLOTS * cache, HEAD_DIM)
+            mixed = jnp.dot(probs_of[pair, run], value, preferred_element_type=jnp.float32)
+            own_prob = own_probs[pair * len(runs) + run]
+            results.append(
+                mixed.reshape(GROUP, SLOTS, HEAD_DIM) + own_prob * new_values[pair][part][None]
+            )
         for head in range(GROUP):
             joined = jnp.concatenate([result[head] for result in results], axis=0)
-            at = pl.multiple_of(column * OUT_WIDTH + head * HEAD_DIM, HEAD_DIM)
+            at = pl.multiple_of((low ^ pair) * OUT_WIDTH + head * HEAD_DIM, HEAD_DIM)
             out[:, pl.ds(at, HEAD_DIM)] = joined.astype(jnp.bfloat16)
 
 
@@ -474,63 +515,72 @@
     cache = key_cache.shape[1]
     slots = slot_request.reshape(col_count, rows, 1)
 
-    blocks = gathered(lax.dynamic_slice_in_dim(hidden_in, side * half, half, 1), "col")
-
-    weight_in = call(
-        stage_in_kernel,
-        pltpu.VMEM((half, qkv_weight.shape[1]), jnp.bfloat16),
+    own_part = call(
+        slice_kernel,
+        struct((rows, half)),
         [SMEM, HBM],
         VMEM,
         0,
-        half * qkv_weight.shape[1] * 2,
+        rows * depth * 2,
         [pltpu.SemaphoreType.DMA],
-    )(place, in_hbm(qkv_weight))
-    weight_out, key_part, value_part = call(
+    )(place, in_hbm(hidden_in))
+    blocks = gathered(own_part, "col")
+
+    gain = norm_gain.reshape(1, depth)
+    cosine, sine = rope_tables(cache_lengths, HEAD_DIM)
+    tables = [
+        jnp.concatenate([cosine, cosine], axis=1),
+        jnp.concatenate([-sine, sine], axis=1),
+        cache_lengths.reshape(rows, 1),
+    ]
+    ready = [slots, gain, *tables]
+    half_in, half_out = qkv_weight.shape[1] // 2, out_weight.shape[1] // 2
+    weights_in = call(
+        stage_in_kernel,
+        [pltpu.VMEM((half, half_in), jnp.bfloat16)] * 2,
+        [SMEM, HBM] + [HBM] * len(ready),
+        [VMEM] * 2,
+        0,
+        half * half_in * 4,
+        [pltpu.SemaphoreType.DMA((2,))],
+    )(place, in_hbm(qkv_weight), *ready)
+    *weights_out, key_part, value_part = call(
         stage_rest_kernel,
-        [
-            pltpu.VMEM((half, out_weight.shape[1]), jnp.bfloat16),
-            pltpu.VMEM((rows, cache, pairs * HEAD_DIM), jnp.bfloat16),
-            pltpu.VMEM((rows, cache, pairs * HEAD_DIM), jnp.bfloat16),
-        ],
+        [pltpu.VMEM((half, half_out), jnp.bfloat16)] * 2
+        + [pltpu.VMEM((rows, cache, pairs * HEAD_DIM), jnp.bfloat16)] * 2,
         [SMEM, HBM, HBM, HBM],
-        [VMEM, VMEM, VMEM],
+        [VMEM] * 4,
         0,
-        half * out_weight.shape[1] * 2 + 4 * rows * cache * pairs * HEAD_DIM,
-        [pltpu.SemaphoreType.DMA((3 * pairs,))],
+        half * half_out * 4 + 4 * rows * cache * pairs * HEAD_DIM,
+        [pltpu.SemaphoreType.DMA((4 * pairs,))],
     )(place, in_hbm(out_weight), in_hbm(key_cache), in_hbm(value_cache))
 
-    gain = norm_gain.reshape(1, depth)
-    products, given, received = project(
-        in_kernel, place, slots, blocks, [gain], weight_in, HEAD_DIM
-    )
-    products = spread(products)
-    sums = given[:, -HEAD_DIM:].astype(jnp.float32) + received[:, -HEAD_DIM:].astype(jnp.float32)
-    own_sums = lax.dynamic_slice_in_dim(sums, (run ^ col) * rows, rows, 0)
-    all_sums = [own_sums] + [moved(own_sums, "row", mask) for mask in range(1, row_count)]
-
-    cosine, sine = rope_tables(cache_lengths, HEAD_DIM)
+    products = spread(
+        project(in_kernel, place, slots, blocks, [gain], weights_in, HEAD_DIM, pairs)
+    )
+
     attended = call(
-        functools.partial(attend_all, col_count, row_count),
+        functools.partial(attend_all, col_count),
         struct((rows, half)),
-        [SMEM] + [VMEM] * (3 + col_count + row_count + 2),
+        [SMEM] + [VMEM] * (3 + col_count + 2),
         VMEM,
         4 * rows * half * cache,
         0,
+        [
+            pltpu.VMEM((pairs, rows // SLOTS, GROUP * SLOTS, SLOTS * cache), jnp.float32),
+            pltpu.VMEM((pairs, rows // SLOTS, GROUP * SLOTS, SLOTS * cache), jnp.bfloat16),
+        ],
     )(
         place,
-        jnp.concatenate([cosine, cosine], axis=1),
-        jnp.concatenate([-sine, sine], axis=1),
-        cache_lengths.reshape(rows, 1),
+        *tables,
         *products,
-        *all_sums,
         in_vmem(key_part),
         in_vmem(value_part),
     )
 
-    products, _, _ = project(
-        out_kernel, place, slots, gathered(attended, "col"), [], weight_out, 0
-    )
-    products = spread(products)
+    products = spread(
+        project(out_kernel, place, slots, gathered(attended, "col"), [], weights_out, 0, pairs)
+    )
     keep, send = call(
         functools.partial(sum_kernel, col_count),
         [struct((rows, half)), struct((rows, half))],

time: 89.2 us -> 74.3 us (0.83)
  local copies, waits for them, and re-layouts: 10.6 us -> 2.3 us
  Pallas kernels: 24.6 us -> 19.9 us
  starting transfers between devices: 28 us -> 25.4 us
  waiting for transfers between devices: 24.3 us -> 25.3 us
    unnamed x8 -> x2, local copies, waits for them, and re-layouts: 7.98 us -> 0.01 us
    pallas_call x5 -> x8, Pallas kernels: 17.9 us -> 14.8 us  [the longest x1 4.77 us: paired_plan(): call(stage_rest_kernel, [pltpu.VMEM((half, half_out), jnp.bfloat16)] * 2...]
    ppermute x10 -> x9, starting transfers between devices: 10.7 us -> 8.05 us  [moved(): return lax.ppermute(value, axis, pairs)]
    pallas_call x2, Pallas kernels: 4.81 us -> 3.18 us  [project(): call(functools.partial(kernel, count), [struct((rows, half + more)), stru...]
    dynamic_slice x1 -> x0, local copies, waits for them, and re-layouts: 0.91 us -> none  [paired_plan(): lax.dynamic_slice_in_dim(hidden_in, side * half, half, 1)]
    ppermute x10 -> x9, waiting for transfers between devices: 17.9 us -> 18.4 us  [moved(): return lax.ppermute(value, axis, pairs)]
  transfers between devices with their start and end apart: 18 -> 17, of which waited for: 8 -> 10; matrix products, arithmetic and copies ran while one was open for 3% -> 4% of each run, Pallas kernels for 15% -> 15%
where the time goes in v3:
time: 74.3 us; the launch traced here: 74.1 us
  starting transfers between devices  25.4 us (34%)
  waiting for transfers between devices  25.3 us (34%)
  Pallas kernels  19.9 us (27%)
  local copies, waits for them, and re-layouts  2.3 us (3%)
  other arithmetic  0.96 us (1%)
    ppermute x9, waiting for transfers between devices, moved(): return lax.ppermute(value, axis, pairs)  18.4 us
    ppermute x8, starting transfers between devices, spread(): lax.ppermute(products[j], ('col', 'row'), [(col * row_count + row, (row *...  17.3 us
    ppermute x9, starting transfers between devices, moved(): return lax.ppermute(value, axis, pairs)  8.05 us
    ppermute x8, waiting for transfers between devices, spread(): lax.ppermute(products[j], ('col', 'row'), [(col * row_count + row, (row *...  6.95 us
    pallas_call x1, Pallas kernels, paired_plan(): call(stage_rest_kernel, [pltpu.VMEM((half, half_out), jnp.bfloat16)] * 2...  4.77 us
    pallas_call x1, Pallas kernels, paired_plan(): call(stage_in_kernel, [pltpu.VMEM((half, half_in), jnp.bfloat16)] * 2, [S...  4.62 us
    pallas_call x2, Pallas kernels, project(): call(functools.partial(kernel, count), [struct((rows, half + more)), stru...  3.18 us
    pallas_call x1, Pallas kernels, paired_plan(): call(functools.partial(attend_all, col_count), struct((rows, half)), [SME...  2.27 us
  transfers between devices with their start and end apart: 17, of which 10 were waited for; matrix products, arithmetic and copies ran while one was open for 4% of the time, Pallas kernels for 15%

profile of v3, /device:TPU:0, one launch (start us, length us, event | category | flops | bytes accessed | tf_op | source)
XLA Modules:
  0.0 74.1 jit_solution(9664141620188641073)
XLA Ops:
  0.0 0.1 pad_add_fusion.place
  0.1 1.5 %shard_map.82.refs_0_ = bf16[32,2048]{1,0:T(8,128)(2,1)S(1)} custom-call(s32[3]{0:T(128)S(1)} %pad_add_fusion.place, bf16[32,4096]{1,0:T(8,128)(2,1)} %hidden.1), custom_call_target="tpu_custom_call" | custom-call | bytes 262144 | tf_op jit(solution)/shard_map/pallas_call | solution.py:518
  1.5 4.1 %collective-permute-start.1 = (bf16[32,2048]{1,0:T(8,128)(2,1)S(1)}, bf16[32,2048]{1,0:T(8,128)(2,1)S(1)}, u32[]{:S(2)}, u32[]{:S(2)}) collective-permute-start(bf16[32,2048]{1,0:T(8,128)(2,1)S(1)} %shard_map.82.refs_0_), channel_id=1, source_target_pairs={{0,8},{4,12},{8,0},{12,4},{1,9},{5,13},{9,1},{13,5},{2,10},{6,14},... | collective-permute-start | bytes 393224 | tf_op jit(solution)/shard_map/ppermute | solution.py:205
  5.6 1.6 %collective-permute-start = (bf16[32,2048]{1,0:T(8,128)(2,1)S(1)}, bf16[32,2048]{1,0:T(8,128)(2,1)S(1)}, u32[]{:S(2)}, u32[]{:S(2)}) collective-permute-start(bf16[32,2048]{1,0:T(8,128)(2,1)S(1)} %shard_map.82.refs_0_), channel_id=1, source_target_pairs={{0,4},{4,0},{8,12},{12,8},{1,5},{5,1},{9,13},{13,9},{2,6},{6,2},{1... | collective-permute-start | bytes 393224 | tf_op jit(solution)/shard_map/ppermute | solution.py:205
  7.2 0.7 convert_element_type.3
  7.9 4.2 %collective-permute-done.1.refs_2_ = bf16[32,2048]{1,0:T(8,128)(2,1)S(1)} collective-permute-done((bf16[32,2048]{1,0:T(8,128)(2,1)S(1)}, bf16[32,2048]{1,0:T(8,128)(2,1)S(1)}, u32[]{:S(2)}, u32[]{:S(2)}) %collective-permute-start.1) | collective-permute-done | bytes 131104 | tf_op jit(solution)/shard_map/ppermute | solution.py:205
  12.1 0.6 collective-permute-start.2
  12.7 0.1 fusion
  12.8 0.9 %reshape.18.refs_0_.slots = s32[4,32,1]{2,1,0:T(8,128)S(1)} reshape(s32[128]{0:T(128)} %param.15) | data formatting | bytes 1024 | tf_op jit(solution)/shard_map/reshape | solution.py:516
  13.7 0.7 %copy.12.refs_4_.lengths = s32[32,1]{1,0:T(8,128)S(1)} copy(s32[32,1]{0,1:T(1,128)} %bitcast.4) | data formatting | bytes 256 | tf_op jit(solution)/shard_map/reshape | solution.py:534
  14.4 0.7 reshape.17.refs_1_.refs_4_
  15.1 0.1 pad_maximum_fusion
  15.2 4.6 %shard_map.83 = (bf16[2048,1280]{1,0:T(8,128)(2,1)S(1)}, bf16[2048,1280]{1,0:T(8,128)(2,1)S(1)}) custom-call(s32[3]{0:T(128)S(1)} %pad_add_fusion.place, bf16[4096,2560]{1,0:T(8,128)(2,1)} %weight.2, s32[4,32,1]{2,1,0:T(8,128)S(1)} %reshape.18.refs_0_.slots, bf16[1,4096]{1,0:T(2,128)(2,1)S(1)} %reshape.17.refs_1_.refs_4_, ...), custom_call_target="tpu_custom_call" | custom-call | bytes 10485760 | tf_op jit(solution)/shard_map/pallas_call | solution.py:538
  19.8 0.0 collective-permute-done.refs_1_
  19.9 1.7 %shard_map.84 = (bf16[128,1408]{1,0:T(8,128)(2,1)S(1)}, bf16[128,2048]{1,0:T(8,128)(2,1)S(1)}) custom-call(s32[3]{0:T(128)S(1)} %pad_add_fusion.place, s32[4,32,1]{2,1,0:T(8,128)S(1)} %reshape.18.refs_0_.slots, bf16[32,2048]{1,0:T(8,128)(2,1)S(1)} %shard_map.82.refs_0_, bf16[32,2048]{1,0:T(8,128)(2,1)S(1)} %collective-permute-done.refs_1_, ...), custom_call_target="tpu_custom_call" | custom-call | flops 671088640 | bytes 5242880 | tf_op jit(solution)/shard_map/pallas_call | solution.py:342
  21.6 0.1 collective-permute-start.3
  21.6 0.9 %shard_map.85.own = f32[128,1280]{1,0:T(8,128)S(1)} custom-call(bf16[128,2048]{1,0:T(8,128)(2,1)S(1)} %get-tuple-element.26.permuted, bf16[2048,1280]{1,0:T(8,128)(2,1)S(1)} %get-tuple-element.27.weight), custom_call_target="tpu_custom_call" | custom-call | flops 671088640 | bytes 5242880 | tf_op jit(solution)/shard_map/pallas_call | solution.py:351
  22.5 0.8 %collective-permute-done.3.received = bf16[128,1408]{1,0:T(8,128)(2,1)S(1)} collective-permute-done((bf16[128,1408]{1,0:T(8,128)(2,1)S(1)}, bf16[128,1408]{1,0:T(8,128)(2,1)S(1)}, u32[]{:S(2)}, u32[]{:S(2)}) %collective-permute-start.3) | collective-permute-done | bytes 360480 | tf_op jit(solution)/shard_map/ppermute | solution.py:205
  23.3 0.1 shard_map.86
  23.4 0.7 collective-permute-start.4
  24.0 5.1 %collective-permute-start.6 = (bf16[32,1408]{1,0:T(8,128)(2,1)S(1)}, bf16[32,1408]{1,0:T(8,128)(2,1)S(1)}, u32[]{:S(2)}, u32[]{:S(2)}) collective-permute-start(bf16[32,1408]{1,0:T(8,128)(2,1)S(1)} %get-tuple-element.31), channel_id=1, source_target_pairs={{0,8},{2,0},{4,12},{6,4},{8,10},{10,2},{12,14},{14,6},{1,9},{3,1},... | collective-permute-start | bytes 270344 | tf_op jit(solution)/shard_map/ppermute | solution.py:384
  29.2 1.5 %collective-permute-start.5 = (bf16[32,1280]{1,0:T(8,128)(2,1)S(1)}, bf16[32,1280]{1,0:T(8,128)(2,1)S(1)}, u32[]{:S(2)}, u32[]{:S(2)}) collective-permute-start(bf16[32,1280]{1,0:T(8,128)(2,1)S(1)} %get-tuple-element.30), channel_id=1, source_target_pairs={{0,4},{2,12},{4,0},{6,8},{8,6},{10,14},{12,2},{14,10},{1,5},{3,13}... | collective-permute-start | bytes 245768 | tf_op jit(solution)/shard_map/ppermute | solution.py:384
  30.7 2.9 %collective-permute-start.7 = (bf16[32,1280]{1,0:T(8,128)(2,1)S(1)}, bf16[32,1280]{1,0:T(8,128)(2,1)S(1)}, u32[]{:S(2)}, u32[]{:S(2)}) collective-permute-start(bf16[32,1280]{1,0:T(8,128)(2,1)S(1)} %get-tuple-element.32), channel_id=1, source_target_pairs={{0,12},{2,4},{4,8},{6,0},{8,14},{10,6},{12,10},{14,2},{1,13},{3,5}... | collective-permute-start | bytes 245768 | tf_op jit(solution)/shard_map/ppermute | solution.py:384
  33.5 4.8 %shard_map.87 = (bf16[2048,1024]{1,0:T(8,128)(2,1)S(1)}, bf16[2048,1024]{1,0:T(8,128)(2,1)S(1)}, bf16[32,64,256]{2,1,0:T(8,128)(2,1)S(1)}, bf16[32,64,256]{2,1,0:T(8,128)(2,1)S(1)}) custom-call(s32[3]{0:T(128)S(1)} %pad_add_fusion.place, bf16[4096,2048]{1,0:T(8,128)(2,1)} %weight.3, bf16[32,64,512]{2,1,0:T(8,128)(2,1)} %keys.1, bf16[32,64,512]{2,1,0:T(8,128)(2,1)} %values.1), custom_call_target="tpu_custom_call" | custom-call | bytes 10485760 | tf_op jit(solution)/shard_map/pallas_call | solution.py:547
  38.3 0.6 collective-permute-done.7.refs_3_
  38.9 0.0 collective-permute-done.4.refs_0_
  38.9 0.0 collective-permute-done.6.refs_2_
  38.9 2.3 %shard_map.88.refs_0_.attended = bf16[32,2048]{1,0:T(8,128)(2,1)S(1)} custom-call(s32[3]{0:T(128)S(1)} %pad_add_fusion.place, f32[32,128]{1,0:T(8,128)S(1)} %get-tuple-element.48.refs_2_.cosine, f32[32,128]{1,0:T(8,128)S(1)} %get-tuple-element.49.refs_3_.sine, s32[32,1]{1,0:T(8,128)S(1)} %copy.12.refs_4_.lengths, ...), custom_call_target="tpu_custom_call" | custom-call | flops 16777216 | tf_op jit(solution)/shard_map/pallas_call | solution.py:562
  41.2 1.1 %collective-permute-start.9 = (bf16[32,2048]{1,0:T(8,128)(2,1)S(1)}, bf16[32,2048]{1,0:T(8,128)(2,1)S(1)}, u32[]{:S(2)}, u32[]{:S(2)}) collective-permute-start(bf16[32,2048]{1,0:T(8,128)(2,1)S(1)} %shard_map.88.refs_0_.attended), channel_id=1, source_target_pairs={{0,8},{4,12},{8,0},{12,4},{1,9},{5,13},{9,1},{13,5},{2,10},{6,14},... | collective-permute-start | bytes 393224 | tf_op jit(solution)/shard_map/ppermute | solution.py:205
  42.2 0.5 collective-permute-start.8
  42.7 6.2 %collective-permute-done.9.refs_2_ = bf16[32,2048]{1,0:T(8,128)(2,1)S(1)} collective-permute-done((bf16[32,2048]{1,0:T(8,128)(2,1)S(1)}, bf16[32,2048]{1,0:T(8,128)(2,1)S(1)}, u32[]{:S(2)}, u32[]{:S(2)}) %collective-permute-start.9) | collective-permute-done | bytes 131104 | tf_op jit(solution)/shard_map/ppermute | solution.py:205
  48.9 0.0 collective-permute-start.10
  48.9 1.1 %collective-permute-done.8.refs_1_ = bf16[32,2048]{1,0:T(8,128)(2,1)S(1)} collective-permute-done((bf16[32,2048]{1,0:T(8,128)(2,1)S(1)}, bf16[32,2048]{1,0:T(8,128)(2,1)S(1)}, u32[]{:S(2)}, u32[]{:S(2)}) %collective-permute-start.8) | collective-permute-done | bytes 131104 | tf_op jit(solution)/shard_map/ppermute | solution.py:205
  50.0 4.0 %collective-permute-done.10.refs_3_ = bf16[32,2048]{1,0:T(8,128)(2,1)S(1)} collective-permute-done((bf16[32,2048]{1,0:T(8,128)(2,1)S(1)}, bf16[32,2048]{1,0:T(8,128)(2,1)S(1)}, u32[]{:S(2)}, u32[]{:S(2)}) %collective-permute-start.10) | collective-permute-done | bytes 131104 | tf_op jit(solution)/shard_map/ppermute | solution.py:205
  54.1 1.5 %shard_map.89 = (bf16[128,1024]{1,0:T(8,128)(2,1)S(1)}, bf16[128,2048]{1,0:T(8,128)(2,1)S(1)}) custom-call(s32[3]{0:T(128)S(1)} %pad_add_fusion.place, s32[4,32,1]{2,1,0:T(8,128)S(1)} %reshape.18.refs_0_.slots, bf16[32,2048]{1,0:T(8,128)(2,1)S(1)} %shard_map.88.refs_0_.attended, bf16[32,2048]{1,0:T(8,128)(2,1)S(1)} %collective-permute-done.8.refs_1_, ...), custom_call_target="tpu_custom_call" | custom-call | flops 536870912 | bytes 4194304 | tf_op jit(solution)/shard_map/pallas_call | solution.py:342
  55.6 0.1 collective-permute-start.11
  55.6 0.8 %shard_map.90.own = f32[128,1024]{1,0:T(8,128)S(1)} custom-call(bf16[128,2048]{1,0:T(8,128)(2,1)S(1)} %get-tuple-element.36.permuted, bf16[2048,1024]{1,0:T(8,128)(2,1)S(1)} %get-tuple-element.37.weight), custom_call_target="tpu_custom_call" | custom-call | flops 536870912 | bytes 4194304 | tf_op jit(solution)/shard_map/pallas_call | solution.py:351
  56.4 0.8 %collective-permute-done.11.received = bf16[128,1024]{1,0:T(8,128)(2,1)S(1)} collective-permute-done((bf16[128,1024]{1,0:T(8,128)(2,1)S(1)}, bf16[128,1024]{1,0:T(8,128)(2,1)S(1)}, u32[]{:S(2)}, u32[]{:S(2)}) %collective-permute-start.11) | collective-permute-done | bytes 262176 | tf_op jit(solution)/shard_map/ppermute | solution.py:205
  57.2 0.7 collective-permute-start.12
  57.9 0.3 collective-permute-start.13
  58.2 5.6 %collective-permute-start.14 = (bf16[32,1024]{1,0:T(8,128)(2,1)S(1)}, bf16[32,1024]{1,0:T(8,128)(2,1)S(1)}, u32[]{:S(2)}, u32[]{:S(2)}) collective-permute-start(bf16[32,1024]{1,0:T(8,128)(2,1)S(1)} %get-tuple-element.41), channel_id=1, source_target_pairs={{0,8},{2,0},{4,12},{6,4},{8,10},{10,2},{12,14},{14,6},{1,9},{3,1},... | collective-permute-start | bytes 196616 | tf_op jit(solution)/shard_map/ppermute | solution.py:384
  63.9 0.5 collective-permute-start.15
  64.4 1.7 %collective-permute-done.14.refs_2_ = bf16[32,1024]{1,0:T(8,128)(2,1)S(1)} collective-permute-done((bf16[32,1024]{1,0:T(8,128)(2,1)S(1)}, bf16[32,1024]{1,0:T(8,128)(2,1)S(1)}, u32[]{:S(2)}, u32[]{:S(2)}) %collective-permute-start.14) | collective-permute-done | bytes 65568 | tf_op jit(solution)/shard_map/ppermute | solution.py:384
  66.1 4.6 %collective-permute-done.15.refs_3_ = bf16[32,1024]{1,0:T(8,128)(2,1)S(1)} collective-permute-done((bf16[32,1024]{1,0:T(8,128)(2,1)S(1)}, bf16[32,1024]{1,0:T(8,128)(2,1)S(1)}, u32[]{:S(2)}, u32[]{:S(2)}) %collective-permute-start.15) | collective-permute-done | bytes 65568 | tf_op jit(solution)/shard_map/ppermute | solution.py:384
  70.7 0.6 shard_map.92
  71.4 0.1 collective-permute-start.16
  71.5 1.3 %collective-permute-done.16.received = bf16[32,2048]{1,0:T(8,128)(2,1)S(1)} collective-permute-done((bf16[32,2048]{1,0:T(8,128)(2,1)S(1)}, bf16[32,2048]{1,0:T(8,128)(2,1)S(1)}, u32[]{:S(2)}, u32[]{:S(2)}) %collective-permute-start.16) | collective-permute-done | bytes 131104 | tf_op jit(solution)/shard_map/ppermute | solution.py:205
  72.8 1.3 %shard_map.93 = bf16[1,32,4096]{2,1,0:T(8,128)(2,1)} custom-call(s32[3]{0:T(128)S(1)} %pad_add_fusion.place, bf16[32,2048]{1,0:T(8,128)(2,1)S(1)} %get-tuple-element.43.keep, bf16[32,2048]{1,0:T(8,128)(2,1)S(1)} %collective-permute-done.16.received), custom_call_target="tpu_custom_call" | custom-call | bytes 524288 | tf_op jit(solution)/shard_map/pallas_call | solution.py:592
  (8 shorter events, 0.1 us)
Async XLA Ops:
  1.5 10.5 %collective-permute-start.1 = (bf16[32,2048]{1,0:T(8,128)(2,1)S(1)}, bf16[32,2048]{1,0:T(8,128)(2,1)S(1)}, u32[]{:S(2)}, u32[]{:S(2)}) collective-permute-start(bf16[32,2048]{1,0:T(8,128)(2,1)S(1)} %shard_map.82.refs_0_), channel_id=1, source_target_pairs={{0,8},{4,12},{8,0},{12,4},{1,9},{5,13},{9,1},{13,5},{2,10},{6,14},... | collective-permute-start | bytes 393224 | tf_op jit(solution)/shard_map/ppermute | solution.py:205
  5.6 14.2 %collective-permute-start = (bf16[32,2048]{1,0:T(8,128)(2,1)S(1)}, bf16[32,2048]{1,0:T(8,128)(2,1)S(1)}, u32[]{:S(2)}, u32[]{:S(2)}) collective-permute-start(bf16[32,2048]{1,0:T(8,128)(2,1)S(1)} %shard_map.82.refs_0_), channel_id=1, source_target_pairs={{0,4},{4,0},{8,12},{12,8},{1,5},{5,1},{9,13},{13,9},{2,6},{6,2},{1... | collective-permute-start | bytes 393224 | tf_op jit(solution)/shard_map/ppermute | solution.py:205
  12.1 7.8 %collective-permute-start.2 = (bf16[32,2048]{1,0:T(8,128)(2,1)S(1)}, bf16[32,2048]{1,0:T(8,128)(2,1)S(1)}, u32[]{:S(2)}, u32[]{:S(2)}) collective-permute-start(bf16[32,2048]{1,0:T(8,128)(2,1)S(1)} %collective-permute-done.1.refs_2_), channel_id=1, source_target_pairs={{0,4},{4,0},{8,12},{12,8},{1,5},{5,1},{9,13},{13,9},{2,6},{6,2},{1... | collective-permute-start | bytes 393224 | tf_op jit(solution)/shard_map/ppermute | solution.py:205
  21.6 1.7 %collective-permute-start.3 = (bf16[128,1408]{1,0:T(8,128)(2,1)S(1)}, bf16[128,1408]{1,0:T(8,128)(2,1)S(1)}, u32[]{:S(2)}, u32[]{:S(2)}) collective-permute-start(bf16[128,1408]{1,0:T(8,128)(2,1)S(1)} %get-tuple-element.28.given), channel_id=1, source_target_pairs={{0,1},{1,0},{2,3},{3,2},{4,5},{5,4},{6,7},{7,6},{8,9},{9,8},{10,11... | collective-permute-start | bytes 1081352 | tf_op jit(solution)/shard_map/ppermute | solution.py:205
  23.4 15.5 %collective-permute-start.4 = (bf16[32,1408]{1,0:T(8,128)(2,1)S(1)}, bf16[32,1408]{1,0:T(8,128)(2,1)S(1)}, u32[]{:S(2)}, u32[]{:S(2)}) collective-permute-start(bf16[32,1408]{1,0:T(8,128)(2,1)S(1)} %get-tuple-element.29), channel_id=1, source_target_pairs={{0,0},{2,8},{4,4},{6,12},{8,2},{10,10},{12,6},{14,14},{1,1},{3,9},... | collective-permute-start | bytes 270344 | tf_op jit(solution)/shard_map/ppermute | solution.py:384
  24.0 14.9 %collective-permute-start.6 = (bf16[32,1408]{1,0:T(8,128)(2,1)S(1)}, bf16[32,1408]{1,0:T(8,128)(2,1)S(1)}, u32[]{:S(2)}, u32[]{:S(2)}) collective-permute-start(bf16[32,1408]{1,0:T(8,128)(2,1)S(1)} %get-tuple-element.31), channel_id=1, source_target_pairs={{0,8},{2,0},{4,12},{6,4},{8,10},{10,2},{12,14},{14,6},{1,9},{3,1},... | collective-permute-start | bytes 270344 | tf_op jit(solution)/shard_map/ppermute | solution.py:384
  29.2 9.1 %collective-permute-start.5 = (bf16[32,1280]{1,0:T(8,128)(2,1)S(1)}, bf16[32,1280]{1,0:T(8,128)(2,1)S(1)}, u32[]{:S(2)}, u32[]{:S(2)}) collective-permute-start(bf16[32,1280]{1,0:T(8,128)(2,1)S(1)} %get-tuple-element.30), channel_id=1, source_target_pairs={{0,4},{2,12},{4,0},{6,8},{8,6},{10,14},{12,2},{14,10},{1,5},{3,13}... | collective-permute-start | bytes 245768 | tf_op jit(solution)/shard_map/ppermute | solution.py:384
  30.7 8.3 %collective-permute-start.7 = (bf16[32,1280]{1,0:T(8,128)(2,1)S(1)}, bf16[32,1280]{1,0:T(8,128)(2,1)S(1)}, u32[]{:S(2)}, u32[]{:S(2)}) collective-permute-start(bf16[32,1280]{1,0:T(8,128)(2,1)S(1)} %get-tuple-element.32), channel_id=1, source_target_pairs={{0,12},{2,4},{4,8},{6,0},{8,14},{10,6},{12,10},{14,2},{1,13},{3,5}... | collective-permute-start | bytes 245768 | tf_op jit(solution)/shard_map/ppermute | solution.py:384
  41.2 7.8 %collective-permute-start.9 = (bf16[32,2048]{1,0:T(8,128)(2,1)S(1)}, bf16[32,2048]{1,0:T(8,128)(2,1)S(1)}, u32[]{:S(2)}, u32[]{:S(2)}) collective-permute-start(bf16[32,2048]{1,0:T(8,128)(2,1)S(1)} %shard_map.88.refs_0_.attended), channel_id=1, source_target_pairs={{0,8},{4,12},{8,0},{12,4},{1,9},{5,13},{9,1},{13,5},{2,10},{6,14},... | collective-permute-start | bytes 393224 | tf_op jit(solution)/shard_map/ppermute | solution.py:205
  42.2 7.8 %collective-permute-start.8 = (bf16[32,2048]{1,0:T(8,128)(2,1)S(1)}, bf16[32,2048]{1,0:T(8,128)(2,1)S(1)}, u32[]{:S(2)}, u32[]{:S(2)}) collective-permute-start(bf16[32,2048]{1,0:T(8,128)(2,1)S(1)} %shard_map.88.refs_0_.attended), channel_id=1, source_target_pairs={{0,4},{4,0},{8,12},{12,8},{1,5},{5,1},{9,13},{13,9},{2,6},{6,2},{1... | collective-permute-start | bytes 393224 | tf_op jit(solution)/shard_map/ppermute | solution.py:205
  48.9 5.1 %collective-permute-start.10 = (bf16[32,2048]{1,0:T(8,128)(2,1)S(1)}, bf16[32,2048]{1,0:T(8,128)(2,1)S(1)}, u32[]{:S(2)}, u32[]{:S(2)}) collective-permute-start(bf16[32,2048]{1,0:T(8,128)(2,1)S(1)} %collective-permute-done.9.refs_2_), channel_id=1, source_target_pairs={{0,4},{4,0},{8,12},{12,8},{1,5},{5,1},{9,13},{13,9},{2,6},{6,2},{1... | collective-permute-start | bytes 393224 | tf_op jit(solution)/shard_map/ppermute | solution.py:205
  54.1 16.7 %copy-start = (bf16[32,4096]{1,0:T(8,128)(2,1)S(1)}, bf16[32,4096]{1,0:T(8,128)(2,1)}, u32[]{:S(2)}) copy-start(bf16[32,4096]{1,0:T(8,128)(2,1)} %hidden.1) | copy-start | bytes 786436
  55.6 1.6 %collective-permute-start.11 = (bf16[128,1024]{1,0:T(8,128)(2,1)S(1)}, bf16[128,1024]{1,0:T(8,128)(2,1)S(1)}, u32[]{:S(2)}, u32[]{:S(2)}) collective-permute-start(bf16[128,1024]{1,0:T(8,128)(2,1)S(1)} %get-tuple-element.38.given), channel_id=1, source_target_pairs={{0,1},{1,0},{2,3},{3,2},{4,5},{5,4},{6,7},{7,6},{8,9},{9,8},{10,11... | collective-permute-start | bytes 786440 | tf_op jit(solution)/shard_map/ppermute | solution.py:205
  57.2 7.2 %collective-permute-start.12 = (bf16[32,1024]{1,0:T(8,128)(2,1)S(1)}, bf16[32,1024]{1,0:T(8,128)(2,1)S(1)}, u32[]{:S(2)}, u32[]{:S(2)}) collective-permute-start(bf16[32,1024]{1,0:T(8,128)(2,1)S(1)} %get-tuple-element.39), channel_id=1, source_target_pairs={{0,0},{2,8},{4,4},{6,12},{8,2},{10,10},{12,6},{14,14},{1,1},{3,9},... | collective-permute-start | bytes 196616 | tf_op jit(solution)/shard_map/ppermute | solution.py:384
  57.9 6.5 %collective-permute-start.13 = (bf16[32,1024]{1,0:T(8,128)(2,1)S(1)}, bf16[32,1024]{1,0:T(8,128)(2,1)S(1)}, u32[]{:S(2)}, u32[]{:S(2)}) collective-permute-start(bf16[32,1024]{1,0:T(8,128)(2,1)S(1)} %get-tuple-element.40), channel_id=1, source_target_pairs={{0,4},{2,12},{4,0},{6,8},{8,6},{10,14},{12,2},{14,10},{1,5},{3,13}... | collective-permute-start | bytes 196616 | tf_op jit(solution)/shard_map/ppermute | solution.py:384
  58.2 7.9 %collective-permute-start.14 = (bf16[32,1024]{1,0:T(8,128)(2,1)S(1)}, bf16[32,1024]{1,0:T(8,128)(2,1)S(1)}, u32[]{:S(2)}, u32[]{:S(2)}) collective-permute-start(bf16[32,1024]{1,0:T(8,128)(2,1)S(1)} %get-tuple-element.41), channel_id=1, source_target_pairs={{0,8},{2,0},{4,12},{6,4},{8,10},{10,2},{12,14},{14,6},{1,9},{3,1},... | collective-permute-start | bytes 196616 | tf_op jit(solution)/shard_map/ppermute | solution.py:384
  63.9 6.9 %collective-permute-start.15 = (bf16[32,1024]{1,0:T(8,128)(2,1)S(1)}, bf16[32,1024]{1,0:T(8,128)(2,1)S(1)}, u32[]{:S(2)}, u32[]{:S(2)}) collective-permute-start(bf16[32,1024]{1,0:T(8,128)(2,1)S(1)} %get-tuple-element.42), channel_id=1, source_target_pairs={{0,12},{2,4},{4,8},{6,0},{8,14},{10,6},{12,10},{14,2},{1,13},{3,5}... | collective-permute-start | bytes 196616 | tf_op jit(solution)/shard_map/ppermute | solution.py:384
  71.4 1.4 %collective-permute-start.16 = (bf16[32,2048]{1,0:T(8,128)(2,1)S(1)}, bf16[32,2048]{1,0:T(8,128)(2,1)S(1)}, u32[]{:S(2)}, u32[]{:S(2)}) collective-permute-start(bf16[32,2048]{1,0:T(8,128)(2,1)S(1)} %get-tuple-element.44), channel_id=1, source_target_pairs={{0,1},{1,0},{2,3},{3,2},{4,5},{5,4},{6,7},{7,6},{8,9},{9,8},{10,11... | collective-permute-start | bytes 393224 | tf_op jit(solution)/shard_map/ppermute | solution.py:205

commit v4 on v3

--- a/solution.py
+++ b/solution.py
@@ -1,4 +1,5 @@
 import functools
+import math
 
 import jax
 import jax.numpy as jnp
@@ -205,12 +206,19 @@
     return lax.ppermute(value, axis, pairs)
 
 
-def slice_kernel(place, source, part, sem):
-    width = part.shape[1]
-    columns = pl.ds(pl.multiple_of(place[0] * width, width), width)
-    copy = pltpu.make_async_copy(source.at[:, columns], part, sem)
-    copy.start()
-    copy.wait()
+def hold_kernel(value, token, out):
+    pass
+
+
+def held(value, token):
+    return pl.pallas_call(
+        hold_kernel,
+        out_shape=pltpu.VMEM(value.shape, value.dtype),
+        in_specs=[VMEM, HBM],
+        out_specs=VMEM,
+        input_output_aliases={0: 0},
+        compiler_params=pltpu.CompilerParams(vmem_limit_bytes=MIB),
+    )(in_vmem(value), token)
 
 
 def halves(place, weight, staged, row, target_row, size):
@@ -236,7 +244,8 @@
 
 
 def stage_in_kernel(place, weight, *refs):
-    give_part, own_part, sems = refs[-3:]
+    give_part, own_part, token, sems = refs[-4:]
+    token[...] = jnp.zeros(token.shape, token.dtype)
     depth = own_part.shape[0]
     first = pl.multiple_of(place[0] * depth, depth)
     run_copies(halves(place, weight, (give_part, own_part), first, 0, depth), sems)
@@ -263,11 +272,16 @@
     run_copies(copies, sems)
 
 
-def one_hot(slots, slot_base, request_base):
-    blocks, rows, _ = slots.shape
-    lane = lax.broadcasted_iota(jnp.int32, (rows, blocks * rows), 1)
-    request = (lax.div(lane, rows) ^ request_base) * rows + lax.rem(lane, rows)
-    parts = [jnp.where(slots[slot_base ^ i] == request, 1.0, 0.0) for i in range(blocks)]
+def one_hot(slots, scratch, blocks, slot_base, request_base):
+    total = slots.shape[0]
+    rows = total // blocks
+    index = lax.broadcasted_iota(jnp.int32, (total, total), 0)
+    request = (lax.div(index, rows) ^ request_base) * rows + lax.rem(index, rows)
+    scratch[...] = jnp.where(slots[...].reshape(1, total) == request, 1.0, 0.0).T
+    parts = [
+        scratch[pl.ds(pl.multiple_of((slot_base ^ i) * rows, rows), rows), :]
+        for i in range(blocks)
+    ]
     return jnp.concatenate(parts, axis=0)
 
 
@@ -288,15 +302,15 @@
         out[:, part] = product.astype(out.dtype)
 
 
-def in_kernel(count, place, slots, *refs):
-    blocks, (gain, weight, give, permuted) = refs[:count], refs[count:]
+def in_kernel(count, blocks, place, slots, *refs):
+    pieces_in, (gain, weight, give, permuted, scratch) = refs[:count], refs[count:]
     side = place[0]
-    depth = blocks[0].shape[1]
+    depth = pieces_in[0].shape[1]
     half = weight.shape[1]
     gains = gain[:, pl.ds(pl.multiple_of(side * depth, depth), depth)].astype(jnp.float32)
-    values = jnp.concatenate([block[...].astype(jnp.float32) for block in blocks], axis=0)
+    values = jnp.concatenate([piece[...].astype(jnp.float32) for piece in pieces_in], axis=0)
     sums = pieces(jnp.sum(values * values, axis=1, keepdims=True))
-    chosen = one_hot(slots, place[2], place[1]).astype(jnp.bfloat16)
+    chosen = one_hot(slots, scratch, blocks, place[2], place[1]).astype(jnp.bfloat16)
     order = jnp.dot(
         chosen, (values * gains).astype(jnp.bfloat16), preferred_element_type=jnp.float32
     ).astype(jnp.bfloat16)
@@ -305,10 +319,10 @@
     dot_columns(order, weight, give)
 
 
-def out_kernel(count, place, slots, *refs):
-    blocks, (weight, give, permuted) = refs[:count], refs[count:]
-    values = jnp.concatenate([block[...] for block in blocks], axis=0)
-    chosen = one_hot(slots, place[1], place[2]).T.astype(jnp.bfloat16)
+def out_kernel(count, blocks, place, slots, *refs):
+    pieces_in, (weight, give, permuted, scratch) = refs[:count], refs[count:]
+    values = jnp.concatenate([piece[...] for piece in pieces_in], axis=0)
+    chosen = one_hot(slots, scratch, blocks, place[1], place[2]).T.astype(jnp.bfloat16)
     order = jnp.dot(chosen, values, preferred_element_type=jnp.float32).astype(jnp.bfloat16)
     permuted[...] = order
     dot_columns(order, weight, give)
@@ -333,20 +347,22 @@
     dot_columns(permuted[...], weight, own)
 
 
-def project(kernel, place, slots, blocks, extra, weights, more, pairs):
-    count = len(blocks)
-    rows, depth = blocks[0].shape
-    rows = rows * count
+def project(kernel, place, slots, pieces_in, extra, weights, more, pairs):
+    count = lax.axis_size("col")
+    parts = len(pieces_in)
+    rows, depth = pieces_in[0].shape
+    rows = rows * parts
     half = weights[0].shape[1]
     flops = 2 * rows * depth * half
     give, permuted = call(
-        functools.partial(kernel, count),
+        functools.partial(kernel, parts, count),
         [struct((rows, half + more)), struct((rows, depth))],
-        [SMEM, VMEM] + [VMEM] * (count + len(extra) + 1),
+        [SMEM, VMEM] + [VMEM] * (parts + len(extra) + 1),
         [VMEM, VMEM],
         flops,
         depth * half * 2,
-    )(place, slots, *blocks, *extra, in_vmem(weights[0]))
+        [pltpu.VMEM((rows, rows), jnp.float32)],
+    )(place, slots, *pieces_in, *extra, in_vmem(weights[0]))
     received = moved(give, "side", 1)
     own = call(
         own_kernel,
@@ -368,13 +384,21 @@
     )(own, give, received)
 
 
-def gathered(value, axis):
-    blocks = {0: value}
+def gathered(parts, axis, token=None):
+    blocks = {0: parts}
     mask = lax.axis_size(axis) // 2
     while mask:
-        blocks |= {known | mask: moved(block, axis, mask) for known, block in blocks.items()}
+        blocks |= {
+            known | mask: [moved(part, axis, mask) for part in block]
+            for known, block in blocks.items()
+        }
+        if token is not None and mask > 1:
+            blocks = {
+                known: [held(part, token) for part in block] if known else block
+                for known, block in blocks.items()
+            }
         mask //= 2
-    return [blocks[i] for i in sorted(blocks)]
+    return [part for i in sorted(blocks) for part in blocks[i]]
 
 
 def spread(products):
@@ -401,28 +425,43 @@
     return vector * cosine + pltpu.roll(vector, HEAD_DIM // 2, 1) * sine
 
 
-def attend_all(count, place, cosine, sine, lengths, *refs):
+def rope(lengths, first, rows):
+    slot = lax.broadcasted_iota(jnp.int32, (rows, HEAD_DIM), 0)
+    length_of = jnp.zeros((rows, HEAD_DIM), jnp.int32)
+    for i in range(rows):
+        length_of = jnp.where(slot == i, lengths[first + i], length_of)
+    lane = lax.broadcasted_iota(jnp.int32, (rows, HEAD_DIM), 1)
+    half = HEAD_DIM // 2
+    step = lax.rem(lane, half).astype(jnp.float32)
+    phases = length_of.astype(jnp.float32) * jnp.exp(-math.log(THETA) * step / half)
+    sine = jnp.sin(phases)
+    return jnp.cos(phases), jnp.where(lane < half, -sine, sine), length_of[:, :1]
+
+
+def attend_all(count, first, place, lengths, *refs):
     blocks, (keys, values, out, scores_of, probs_of) = refs[:count], refs[count:]
     pairs = keys.shape[2] // HEAD_DIM
-    rows, cache = keys.shape[:2]
+    cache = keys.shape[1]
+    rows = out.shape[0]
+    here = slice(first, first + rows)
     low = place[1] % pairs
     width = GROUP_WIDTH
-    squares = blocks[0][:, width:].astype(jnp.float32)
+    squares = blocks[0][here, width:].astype(jnp.float32)
     for i in range(pairs, count, pairs):
-        squares = squares + blocks[i][:, width:].astype(jnp.float32)
+        squares = squares + blocks[i][here, width:].astype(jnp.float32)
     scale = lax.rsqrt(jnp.sum(squares, axis=1, keepdims=True) / D + EPSILON)
     factor = HEAD_DIM ** (-0.5)
-    cosines, sines = cosine[...], sine[...]
+    cosines, sines, length_of = rope(lengths, first, rows)
     lane = lax.broadcasted_iota(jnp.int32, (SLOTS, SLOTS * cache), 1)
     slot = lax.broadcasted_iota(jnp.int32, (SLOTS, SLOTS * cache), 0)
     position = lane - slot * cache
     runs = [slice(start, start + SLOTS) for start in range(0, rows, SLOTS)]
-    filled = [(position >= 0) & (position < lengths[part]) for part in runs]
+    filled = [(position >= 0) & (position < length_of[part]) for part in runs]
     own, new_values, own_probs = [], [], []
     for pair in range(pairs):
-        total = blocks[pair][:, :width].astype(jnp.float32)
+        total = blocks[pair][here, :width].astype(jnp.float32)
         for i in range(pair + pairs, count, pairs):
-            total = total + blocks[i][:, :width].astype(jnp.float32)
+            total = total + blocks[i][here, :width].astype(jnp.float32)
         total = (total * scale).astype(jnp.bfloat16).astype(jnp.float32)
         heads = [total[:, h * HEAD_DIM : (h + 1) * HEAD_DIM] for h in range(GROUP + 2)]
         queries = [
@@ -435,7 +474,7 @@
         lanes = pl.ds(pl.multiple_of((low ^ pair) * HEAD_DIM, HEAD_DIM), HEAD_DIM)
         for run, part in enumerate(runs):
             query = jnp.concatenate([head[part] for head in queries], axis=0)
-            key = keys[part, :, lanes].reshape(SLOTS * cache, HEAD_DIM)
+            key = keys[first + part.start : first + part.stop, :, lanes].reshape(SLOTS * cache, HEAD_DIM)
             scores_of[pair, run] = lax.dot_general(
                 query.astype(jnp.bfloat16),
                 key,
@@ -460,7 +499,7 @@
         lanes = pl.ds(pl.multiple_of((low ^ pair) * HEAD_DIM, HEAD_DIM), HEAD_DIM)
         results = []
         for run, part in enumerate(runs):
-            value = values[part, :, lanes].reshape(SLOTS * cache, HEAD_DIM)
+            value = values[first + part.start : first + part.stop, :, lanes].reshape(SLOTS * cache, HEAD_DIM)
             mixed = jnp.dot(probs_of[pair, run], value, preferred_element_type=jnp.float32)
             own_prob = own_probs[pair * len(runs) + run]
             results.append(
@@ -472,10 +511,10 @@
             out[:, pl.ds(at, HEAD_DIM)] = joined.astype(jnp.bfloat16)
 
 
-def sum_kernel(count, place, hidden, attended, *refs):
-    blocks, (keep, send) = refs[:count], refs[count:]
+def sum_kernel(count, parts, place, hidden, *refs):
+    attended, blocks, (keep, send) = refs[:parts], refs[parts : parts + count], refs[parts + count :]
     rows, width = blocks[0].shape
-    pairs = attended.shape[1] // width
+    pairs = keep.shape[1] // width
     side = place[0]
     low = place[1] % pairs
     for pair in range(pairs):
@@ -486,7 +525,7 @@
         at = pl.ds(pl.multiple_of((2 * column + side) * width, width), width)
         hidden_out = (hidden[:, at].astype(jnp.float32) + total).astype(jnp.bfloat16)
         at = pl.ds(pl.multiple_of(column * width, width), width)
-        attention = attended[:, at]
+        attention = jnp.concatenate([part[:, at] for part in attended], axis=0)
         keep[:, at] = jnp.where(side == 0, hidden_out, attention)
         send[:, at] = jnp.where(side == 0, attention, hidden_out)
 
@@ -513,37 +552,24 @@
     rows, depth = hidden_in.shape
     half = depth // 2
     cache = key_cache.shape[1]
-    slots = slot_request.reshape(col_count, rows, 1)
-
-    own_part = call(
-        slice_kernel,
-        struct((rows, half)),
-        [SMEM, HBM],
-        VMEM,
-        0,
-        rows * depth * 2,
-        [pltpu.SemaphoreType.DMA],
-    )(place, in_hbm(hidden_in))
-    blocks = gathered(own_part, "col")
-
+    parts = 2
+    piece = rows // parts
+
+    own_part = lax.dynamic_slice_in_dim(hidden_in, side * half, half, 1)
     gain = norm_gain.reshape(1, depth)
-    cosine, sine = rope_tables(cache_lengths, HEAD_DIM)
-    tables = [
-        jnp.concatenate([cosine, cosine], axis=1),
-        jnp.concatenate([-sine, sine], axis=1),
-        cache_lengths.reshape(rows, 1),
-    ]
-    ready = [slots, gain, *tables]
     half_in, half_out = qkv_weight.shape[1] // 2, out_weight.shape[1] // 2
-    weights_in = call(
+    *weights_in, token = call(
         stage_in_kernel,
-        [pltpu.VMEM((half, half_in), jnp.bfloat16)] * 2,
-        [SMEM, HBM] + [HBM] * len(ready),
-        [VMEM] * 2,
+        [pltpu.VMEM((half, half_in), jnp.bfloat16)] * 2 + [struct((8, 128), jnp.float32)],
+        [SMEM, HBM, HBM],
+        [VMEM] * 3,
         0,
         half * half_in * 4,
         [pltpu.SemaphoreType.DMA((2,))],
-    )(place, in_hbm(qkv_weight), *ready)
+    )(place, in_hbm(qkv_weight), gain)
+    blocks = gathered(
+        [own_part[i * piece : (i + 1) * piece] for i in range(parts)], "col", token
+    )
     *weights_out, key_part, value_part = call(
         stage_rest_kernel,
         [pltpu.VMEM((half, half_out), jnp.bfloat16)] * 2
@@ -556,39 +582,37 @@
     )(place, in_hbm(out_weight), in_hbm(key_cache), in_hbm(value_cache))
 
     products = spread(
-        project(in_kernel, place, slots, blocks, [gain], weights_in, HEAD_DIM, pairs)
-    )
-
-    attended = call(
-        functools.partial(attend_all, col_count),
-        struct((rows, half)),
-        [SMEM] + [VMEM] * (3 + col_count + 2),
-        VMEM,
-        4 * rows * half * cache,
-        0,
-        [
-            pltpu.VMEM((pairs, rows // SLOTS, GROUP * SLOTS, SLOTS * cache), jnp.float32),
-            pltpu.VMEM((pairs, rows // SLOTS, GROUP * SLOTS, SLOTS * cache), jnp.bfloat16),
-        ],
-    )(
-        place,
-        *tables,
-        *products,
-        in_vmem(key_part),
-        in_vmem(value_part),
-    )
+        project(in_kernel, place, slot_request, blocks, [gain], weights_in, HEAD_DIM, pairs)
+    )
+
+    key_part, value_part = in_vmem(key_part), in_vmem(value_part)
+    runs = (pairs, piece // SLOTS, GROUP * SLOTS, SLOTS * cache)
+    attended = [
+        call(
+            functools.partial(attend_all, col_count, first),
+            struct((piece, half)),
+            [SMEM, SMEM] + [VMEM] * (col_count + 2),
+            VMEM,
+            4 * piece * half * cache,
+            0,
+            [pltpu.VMEM(runs, jnp.float32), pltpu.VMEM(runs, jnp.bfloat16)],
+        )(place, cache_lengths, *products, key_part, value_part)
+        for first in range(0, rows, piece)
+    ]
 
     products = spread(
-        project(out_kernel, place, slots, gathered(attended, "col"), [], weights_out, 0, pairs)
+        project(
+            out_kernel, place, slot_request, gathered(attended, "col"), [], weights_out, 0, pairs
+        )
     )
     keep, send = call(
-        functools.partial(sum_kernel, col_count),
+        functools.partial(sum_kernel, col_count, parts),
         [struct((rows, half)), struct((rows, half))],
-        [SMEM] + [VMEM] * (2 + col_count),
+        [SMEM] + [VMEM] * (1 + parts + col_count),
         [VMEM, VMEM],
         rows * depth * 4,
         rows * depth * 8,
-    )(place, hidden_in, attended, *products)
+    )(place, hidden_in, *attended, *products)
     return call(
         join_kernel,
         struct((1, rows, depth)),
@@ -607,7 +631,7 @@
         and qkv_weight.shape[1] == 2 * GROUP_WIDTH
         and col_count % row_count == 0
         and col_count & (col_count - 1) == 0
-        and hidden_in.shape[0] % 16 == 0
+        and hidden_in.shape[0] % 32 == 0
         and key_cache.shape[1] % 16 == 0
         and hidden_in.shape[1] == 2 * OUT_WIDTH * (col_count // row_count)
     )

time: 74.3 us -> 71.1 us (0.957)
  waiting for transfers between devices: 25.3 us -> 16.5 us
  starting transfers between devices: 25.4 us -> 32.7 us
  other arithmetic: 0.96 us -> 0.08 us
    ppermute x9 -> x15, starting transfers between devices: 8.05 us -> 18 us  [moved(): return lax.ppermute(value, axis, pairs)]
    ppermute x9 -> x15, waiting for transfers between devices: 18.4 us -> 10.5 us  [moved(): return lax.ppermute(value, axis, pairs)]
    ppermute x8, starting transfers between devices: 17.3 us -> 14.7 us  [spread(): lax.ppermute(products[j], ('col', 'row'), [(col * row_count + row, (row *...]
    reshape x2 -> x0, local copies, waits for them, and re-layouts: 1.59 us -> none  [the longest x1 0.85 us: paired_plan(): slots = slot_request.reshape(col_count, rows, 1)]
    ppermute x8, waiting for transfers between devices: 6.95 us -> 5.92 us  [spread(): lax.ppermute(products[j], ('col', 'row'), [(col * row_count + row, (row *...]
    slice x0 -> x1, local copies, waits for them, and re-layouts: none -> 0.88 us  [paired_plan(): own_part[i * piece:(i + 1) * piece]]
    pallas_call x6 -> x8, Pallas kernels: 12.2 us -> 11.8 us  [the longest x1 4.62 us: paired_plan(): call(stage_in_kernel, [pltpu.VMEM((half, half_in), jnp.bfloat16)] * 2 + [...]
  transfers between devices with their start and end apart: 17 -> 23, of which waited for: 10 -> 12; matrix products, arithmetic and copies ran while one was open for 4% -> 1% of each run, Pallas kernels for 15% -> 18%
where the time goes in v4:
time: 71.1 us; the launch traced here: 70.5 us
  starting transfers between devices  32.7 us (46%)
  Pallas kernels  19.6 us (28%)
  waiting for transfers between devices  16.5 us (23%)
  local copies, waits for them, and re-layouts  1.6 us (2%)
    ppermute x15, starting transfers between devices, moved(): return lax.ppermute(value, axis, pairs)  18 us
    ppermute x8, starting transfers between devices, spread(): lax.ppermute(products[j], ('col', 'row'), [(col * row_count + row, (row *...  14.7 us
    ppermute x15, waiting for transfers between devices, moved(): return lax.ppermute(value, axis, pairs)  10.5 us
    ppermute x8, waiting for transfers between devices, spread(): lax.ppermute(products[j], ('col', 'row'), [(col * row_count + row, (row *...  5.92 us
    pallas_call x1, Pallas kernels, paired_plan(): call(stage_rest_kernel, [pltpu.VMEM((half, half_out), jnp.bfloat16)] * 2...  4.77 us
    pallas_call x1, Pallas kernels, paired_plan(): call(stage_in_kernel, [pltpu.VMEM((half, half_in), jnp.bfloat16)] * 2 + [...  4.62 us
    pallas_call x2, Pallas kernels, paired_plan(): call(functools.partial(attend_all, col_count, first), struct((piece, half...  3.29 us
    pallas_call x2, Pallas kernels, project(): call(functools.partial(kernel, parts, count), [struct((rows, half + more)...  3.26 us
  transfers between devices with their start and end apart: 23, of which 12 were waited for; matrix products, arithmetic and copies ran while one was open for 1% of the time, Pallas kernels for 18%

profile of v4, /device:TPU:0, one launch (start us, length us, event | category | flops | bytes accessed | tf_op | source)
XLA Modules:
  0.0 70.5 jit_solution(6152466167887104376)
XLA Ops:
  0.0 0.9 %fusion = (bf16[16,2048]{1,0:T(8,128)(2,1)S(1)}, bf16[16,2048]{1,0:T(8,128)(2,1)S(1)}) fusion(bf16[32,4096]{1,0:T(8,128)(2,1)} %hidden.1, s32[]{:T(128)S(6)} %add.10, s32[]{:T(128)S(6)} %select_n.3), kind=kLoop, calls=%fused_computation.2 | loop fusion | bytes 262152 | tf_op jit(solution)/shard_map/slice | solution.py:571
  0.9 4.1 %collective-permute-start.2 = (bf16[16,2048]{1,0:T(8,128)(2,1)S(1)}, bf16[16,2048]{1,0:T(8,128)(2,1)S(1)}, u32[]{:S(2)}, u32[]{:S(2)}) collective-permute-start(bf16[16,2048]{1,0:T(8,128)(2,1)S(1)} %get-tuple-element.48.refs_0_), channel_id=1, source_target_pairs={{0,8},{4,12},{8,0},{12,4},{1,9},{5,13},{9,1},{13,5},{2,10},{6,14},... | collective-permute-start | bytes 196616 | tf_op jit(solution)/shard_map/ppermute | solution.py:206
  5.0 1.6 %collective-permute-start = (bf16[16,2048]{1,0:T(8,128)(2,1)S(1)}, bf16[16,2048]{1,0:T(8,128)(2,1)S(1)}, u32[]{:S(2)}, u32[]{:S(2)}) collective-permute-start(bf16[16,2048]{1,0:T(8,128)(2,1)S(1)} %get-tuple-element.48.refs_0_), channel_id=1, source_target_pairs={{0,4},{4,0},{8,12},{12,8},{1,5},{5,1},{9,13},{13,9},{2,6},{6,2},{1... | collective-permute-start | bytes 196616 | tf_op jit(solution)/shard_map/ppermute | solution.py:206
  6.6 0.3 collective-permute-start.3
  6.9 0.2 collective-permute-start.1
  7.1 0.7 %reshape.3.refs_0_.refs_8_ = bf16[1,4096]{1,0:T(2,128)(2,1)S(1)} reshape(bf16[4096]{0:T(1024)(128)(2,1)} %param.9) | data formatting | bytes 16384 | tf_op jit(solution)/shard_map/reshape | solution.py:559
  7.8 0.1 pad_add_fusion.place
  7.9 4.6 %shard_map.82 = (bf16[2048,1280]{1,0:T(8,128)(2,1)S(1)}, bf16[2048,1280]{1,0:T(8,128)(2,1)S(1)}, f32[8,128]{1,0:T(8,128)S(1)}) custom-call(s32[3]{0:T(128)S(1)} %pad_add_fusion.place, bf16[4096,2560]{1,0:T(8,128)(2,1)} %weight.2, bf16[1,4096]{1,0:T(2,128)(2,1)S(1)} %reshape.3.refs_0_.refs_8_), custom_call_target="tpu_custom_call" | custom-call | bytes 10485760 | tf_op jit(solution)/shard_map/pallas_call | solution.py:561
  12.5 1.9 %collective-permute-start.4 = (bf16[16,2048]{1,0:T(8,128)(2,1)S(1)}, bf16[16,2048]{1,0:T(8,128)(2,1)S(1)}, u32[]{:S(2)}, u32[]{:S(2)}) collective-permute-start(bf16[16,2048]{1,0:T(8,128)(2,1)S(1)} %shard_map.83.refs_4_), channel_id=1, source_target_pairs={{0,4},{4,0},{8,12},{12,8},{1,5},{5,1},{9,13},{13,9},{2,6},{6,2},{1... | collective-permute-start | bytes 196616 | tf_op jit(solution)/shard_map/ppermute | solution.py:206
  14.4 0.2 collective-permute-start.5
  14.6 2.3 %collective-permute-done.4.refs_6_ = bf16[16,2048]{1,0:T(8,128)(2,1)S(1)} collective-permute-done((bf16[16,2048]{1,0:T(8,128)(2,1)S(1)}, bf16[16,2048]{1,0:T(8,128)(2,1)S(1)}, u32[]{:S(2)}, u32[]{:S(2)}) %collective-permute-start.4) | collective-permute-done | bytes 65568 | tf_op jit(solution)/shard_map/ppermute | solution.py:206
  16.9 1.8 %collective-permute-done.5.refs_7_ = bf16[16,2048]{1,0:T(8,128)(2,1)S(1)} collective-permute-done((bf16[16,2048]{1,0:T(8,128)(2,1)S(1)}, bf16[16,2048]{1,0:T(8,128)(2,1)S(1)}, u32[]{:S(2)}, u32[]{:S(2)}) %collective-permute-start.5) | collective-permute-done | bytes 65568 | tf_op jit(solution)/shard_map/ppermute | solution.py:206
  18.7 1.7 %shard_map.85 = (bf16[128,1408]{1,0:T(8,128)(2,1)S(1)}, bf16[128,2048]{1,0:T(8,128)(2,1)S(1)}) custom-call(s32[3]{0:T(128)S(1)} %pad_add_fusion.place, s32[128]{0:T(128)S(1)} %copy-done.2, bf16[16,2048]{1,0:T(8,128)(2,1)S(1)} %get-tuple-element.48.refs_0_, bf16[16,2048]{1,0:T(8,128)(2,1)S(1)} %get-tuple-element.47.refs_1_, ...), custom_call_target="tpu_custom_call" | custom-call | flops 671088640 | bytes 5242880 | tf_op jit(solution)/shard_map/pallas_call | solution.py:357
  20.5 0.1 collective-permute-start.6
  20.5 0.9 %shard_map.86.own = f32[128,1280]{1,0:T(8,128)S(1)} custom-call(bf16[128,2048]{1,0:T(8,128)(2,1)S(1)} %get-tuple-element.28.permuted, bf16[2048,1280]{1,0:T(8,128)(2,1)S(1)} %get-tuple-element.29.weight), custom_call_target="tpu_custom_call" | custom-call | flops 671088640 | bytes 5242880 | tf_op jit(solution)/shard_map/pallas_call | solution.py:367
  21.4 0.8 %collective-permute-done.6.received = bf16[128,1408]{1,0:T(8,128)(2,1)S(1)} collective-permute-done((bf16[128,1408]{1,0:T(8,128)(2,1)S(1)}, bf16[128,1408]{1,0:T(8,128)(2,1)S(1)}, u32[]{:S(2)}, u32[]{:S(2)}) %collective-permute-start.6) | collective-permute-done | bytes 360480 | tf_op jit(solution)/shard_map/ppermute | solution.py:206
  22.2 0.1 shard_map.87
  22.3 0.7 collective-permute-start.7
  22.9 5.1 %collective-permute-start.9 = (bf16[32,1408]{1,0:T(8,128)(2,1)S(1)}, bf16[32,1408]{1,0:T(8,128)(2,1)S(1)}, u32[]{:S(2)}, u32[]{:S(2)}) collective-permute-start(bf16[32,1408]{1,0:T(8,128)(2,1)S(1)} %get-tuple-element.33), channel_id=1, source_target_pairs={{0,8},{2,0},{4,12},{6,4},{8,10},{10,2},{12,14},{14,6},{1,9},{3,1},... | collective-permute-start | bytes 270344 | tf_op jit(solution)/shard_map/ppermute | solution.py:408
  28.1 0.2 collective-permute-start.10
  28.3 0.5 collective-permute-start.8
  28.8 4.8 %shard_map.88 = (bf16[2048,1024]{1,0:T(8,128)(2,1)S(1)}, bf16[2048,1024]{1,0:T(8,128)(2,1)S(1)}, bf16[32,64,256]{2,1,0:T(8,128)(2,1)S(1)}, bf16[32,64,256]{2,1,0:T(8,128)(2,1)S(1)}) custom-call(s32[3]{0:T(128)S(1)} %pad_add_fusion.place, bf16[4096,2048]{1,0:T(8,128)(2,1)} %weight.3, bf16[32,64,512]{2,1,0:T(8,128)(2,1)} %keys.1, bf16[32,64,512]{2,1,0:T(8,128)(2,1)} %values.1), custom_call_target="tpu_custom_call" | custom-call | bytes 10485760 | tf_op jit(solution)/shard_map/pallas_call | solution.py:573
  33.6 0.7 collective-permute-done.10.refs_3_
  34.2 0.5 collective-permute-done.8.refs_1_
  34.7 1.6 %shard_map.90.refs_1_ = bf16[16,2048]{1,0:T(8,128)(2,1)S(1)} custom-call(s32[3]{0:T(128)S(1)} %pad_add_fusion.place, s32[32]{0:T(128)S(1)} %copy-done.1, bf16[32,1408]{1,0:T(8,128)(2,1)S(1)} %collective-permute-done.7.refs_0_, bf16[32,1280]{1,0:T(8,128)(2,1)S(1)} %collective-permute-done.8.refs_1_, bf16[32,1408]{1,0:T(8,128)(2,1)S(1)} %collective-permute-done.9.refs_2_, ...), custom_call_target="tpu_custom_call" | custom-call | flops 8388608 | tf_op jit(solution)/shard_map/pallas_call | solution.py:591
  36.4 3.4 %collective-permute-start.14 = (bf16[16,2048]{1,0:T(8,128)(2,1)S(1)}, bf16[16,2048]{1,0:T(8,128)(2,1)S(1)}, u32[]{:S(2)}, u32[]{:S(2)}) collective-permute-start(bf16[16,2048]{1,0:T(8,128)(2,1)S(1)} %shard_map.90.refs_1_), channel_id=1, source_target_pairs={{0,8},{4,12},{8,0},{12,4},{1,9},{5,13},{9,1},{13,5},{2,10},{6,14},... | collective-permute-start | bytes 196616 | tf_op jit(solution)/shard_map/ppermute | solution.py:206
  39.8 1.6 %shard_map.89.refs_0_ = bf16[16,2048]{1,0:T(8,128)(2,1)S(1)} custom-call(s32[3]{0:T(128)S(1)} %pad_add_fusion.place, s32[32]{0:T(128)S(1)} %copy-done.1, bf16[32,1408]{1,0:T(8,128)(2,1)S(1)} %collective-permute-done.7.refs_0_, bf16[32,1280]{1,0:T(8,128)(2,1)S(1)} %collective-permute-done.8.refs_1_, bf16[32,1408]{1,0:T(8,128)(2,1)S(1)} %collective-permute-done.9.refs_2_, ...), custom_call_target="tpu_custom_call" | custom-call | flops 8388608 | tf_op jit(solution)/shard_map/pallas_call | solution.py:591
  41.5 1.9 %collective-permute-start.12 = (bf16[16,2048]{1,0:T(8,128)(2,1)S(1)}, bf16[16,2048]{1,0:T(8,128)(2,1)S(1)}, u32[]{:S(2)}, u32[]{:S(2)}) collective-permute-start(bf16[16,2048]{1,0:T(8,128)(2,1)S(1)} %shard_map.90.refs_1_), channel_id=1, source_target_pairs={{0,4},{4,0},{8,12},{12,8},{1,5},{5,1},{9,13},{13,9},{2,6},{6,2},{1... | collective-permute-start | bytes 196616 | tf_op jit(solution)/shard_map/ppermute | solution.py:206
  43.4 0.2 collective-permute-start.11
  43.6 1.8 %collective-permute-start.16 = (bf16[16,2048]{1,0:T(8,128)(2,1)S(1)}, bf16[16,2048]{1,0:T(8,128)(2,1)S(1)}, u32[]{:S(2)}, u32[]{:S(2)}) collective-permute-start(bf16[16,2048]{1,0:T(8,128)(2,1)S(1)} %collective-permute-done.14.refs_5_), channel_id=1, source_target_pairs={{0,4},{4,0},{8,12},{12,8},{1,5},{5,1},{9,13},{13,9},{2,6},{6,2},{1... | collective-permute-start | bytes 196616 | tf_op jit(solution)/shard_map/ppermute | solution.py:206
  45.4 1.3 %collective-permute-done.13.refs_4_ = bf16[16,2048]{1,0:T(8,128)(2,1)S(1)} collective-permute-done((bf16[16,2048]{1,0:T(8,128)(2,1)S(1)}, bf16[16,2048]{1,0:T(8,128)(2,1)S(1)}, u32[]{:S(2)}, u32[]{:S(2)}) %collective-permute-start.13) | collective-permute-done | bytes 65568 | tf_op jit(solution)/shard_map/ppermute | solution.py:206
  46.7 2.1 %collective-permute-start.15 = (bf16[16,2048]{1,0:T(8,128)(2,1)S(1)}, bf16[16,2048]{1,0:T(8,128)(2,1)S(1)}, u32[]{:S(2)}, u32[]{:S(2)}) collective-permute-start(bf16[16,2048]{1,0:T(8,128)(2,1)S(1)} %collective-permute-done.13.refs_4_), channel_id=1, source_target_pairs={{0,4},{4,0},{8,12},{12,8},{1,5},{5,1},{9,13},{13,9},{2,6},{6,2},{1... | collective-permute-start | bytes 196616 | tf_op jit(solution)/shard_map/ppermute | solution.py:206
  48.8 0.6 collective-permute-done.16.refs_7_
  49.4 1.7 %collective-permute-done.15.refs_6_ = bf16[16,2048]{1,0:T(8,128)(2,1)S(1)} collective-permute-done((bf16[16,2048]{1,0:T(8,128)(2,1)S(1)}, bf16[16,2048]{1,0:T(8,128)(2,1)S(1)}, u32[]{:S(2)}, u32[]{:S(2)}) %collective-permute-start.15) | collective-permute-done | bytes 65568 | tf_op jit(solution)/shard_map/ppermute | solution.py:206
  51.1 1.5 %shard_map.91 = (bf16[128,1024]{1,0:T(8,128)(2,1)S(1)}, bf16[128,2048]{1,0:T(8,128)(2,1)S(1)}) custom-call(s32[3]{0:T(128)S(1)} %pad_add_fusion.place, s32[128]{0:T(128)S(1)} %copy-done.2, bf16[16,2048]{1,0:T(8,128)(2,1)S(1)} %shard_map.89.refs_0_, bf16[16,2048]{1,0:T(8,128)(2,1)S(1)} %shard_map.90.refs_1_, ...), custom_call_target="tpu_custom_call" | custom-call | flops 536870912 | bytes 4194304 | tf_op jit(solution)/shard_map/pallas_call | solution.py:357
  52.6 0.1 collective-permute-start.17
  52.7 0.7 %shard_map.92.own = f32[128,1024]{1,0:T(8,128)S(1)} custom-call(bf16[128,2048]{1,0:T(8,128)(2,1)S(1)} %get-tuple-element.38.permuted, bf16[2048,1024]{1,0:T(8,128)(2,1)S(1)} %get-tuple-element.39.weight), custom_call_target="tpu_custom_call" | custom-call | flops 536870912 | bytes 4194304 | tf_op jit(solution)/shard_map/pallas_call | solution.py:367
  53.4 0.8 %collective-permute-done.17.received = bf16[128,1024]{1,0:T(8,128)(2,1)S(1)} collective-permute-done((bf16[128,1024]{1,0:T(8,128)(2,1)S(1)}, bf16[128,1024]{1,0:T(8,128)(2,1)S(1)}, u32[]{:S(2)}, u32[]{:S(2)}) %collective-permute-start.17) | collective-permute-done | bytes 262176 | tf_op jit(solution)/shard_map/ppermute | solution.py:206
  54.3 0.7 collective-permute-start.18
  54.9 2.1 %collective-permute-start.19 = (bf16[32,1024]{1,0:T(8,128)(2,1)S(1)}, bf16[32,1024]{1,0:T(8,128)(2,1)S(1)}, u32[]{:S(2)}, u32[]{:S(2)}) collective-permute-start(bf16[32,1024]{1,0:T(8,128)(2,1)S(1)} %get-tuple-element.42), channel_id=1, source_target_pairs={{0,4},{2,12},{4,0},{6,8},{8,6},{10,14},{12,2},{14,10},{1,5},{3,13}... | collective-permute-start | bytes 196616 | tf_op jit(solution)/shard_map/ppermute | solution.py:408
  57.0 4.1 %collective-permute-start.20 = (bf16[32,1024]{1,0:T(8,128)(2,1)S(1)}, bf16[32,1024]{1,0:T(8,128)(2,1)S(1)}, u32[]{:S(2)}, u32[]{:S(2)}) collective-permute-start(bf16[32,1024]{1,0:T(8,128)(2,1)S(1)} %get-tuple-element.43), channel_id=1, source_target_pairs={{0,8},{2,0},{4,12},{6,4},{8,10},{10,2},{12,14},{14,6},{1,9},{3,1},... | collective-permute-start | bytes 196616 | tf_op jit(solution)/shard_map/ppermute | solution.py:408
  61.1 1.3 %collective-permute-start.21 = (bf16[32,1024]{1,0:T(8,128)(2,1)S(1)}, bf16[32,1024]{1,0:T(8,128)(2,1)S(1)}, u32[]{:S(2)}, u32[]{:S(2)}) collective-permute-start(bf16[32,1024]{1,0:T(8,128)(2,1)S(1)} %get-tuple-element.44), channel_id=1, source_target_pairs={{0,12},{2,4},{4,8},{6,0},{8,14},{10,6},{12,10},{14,2},{1,13},{3,5}... | collective-permute-start | bytes 196616 | tf_op jit(solution)/shard_map/ppermute | solution.py:408
  62.4 3.1 %collective-permute-done.20.refs_4_ = bf16[32,1024]{1,0:T(8,128)(2,1)S(1)} collective-permute-done((bf16[32,1024]{1,0:T(8,128)(2,1)S(1)}, bf16[32,1024]{1,0:T(8,128)(2,1)S(1)}, u32[]{:S(2)}, u32[]{:S(2)}) %collective-permute-start.20) | collective-permute-done | bytes 65568 | tf_op jit(solution)/shard_map/ppermute | solution.py:408
  65.5 1.7 %collective-permute-done.21.refs_5_ = bf16[32,1024]{1,0:T(8,128)(2,1)S(1)} collective-permute-done((bf16[32,1024]{1,0:T(8,128)(2,1)S(1)}, bf16[32,1024]{1,0:T(8,128)(2,1)S(1)}, u32[]{:S(2)}, u32[]{:S(2)}) %collective-permute-start.21) | collective-permute-done | bytes 65568 | tf_op jit(solution)/shard_map/ppermute | solution.py:408
  67.2 0.6 shard_map.94
  67.8 0.1 collective-permute-start.22
  67.9 1.3 %collective-permute-done.22.received = bf16[32,2048]{1,0:T(8,128)(2,1)S(1)} collective-permute-done((bf16[32,2048]{1,0:T(8,128)(2,1)S(1)}, bf16[32,2048]{1,0:T(8,128)(2,1)S(1)}, u32[]{:S(2)}, u32[]{:S(2)}) %collective-permute-start.22) | collective-permute-done | bytes 131104 | tf_op jit(solution)/shard_map/ppermute | solution.py:206
  69.2 1.3 %shard_map.95 = bf16[1,32,4096]{2,1,0:T(8,128)(2,1)} custom-call(s32[3]{0:T(128)S(1)} %pad_add_fusion.place, bf16[32,2048]{1,0:T(8,128)(2,1)S(1)} %get-tuple-element.45.keep, bf16[32,2048]{1,0:T(8,128)(2,1)S(1)} %collective-permute-done.22.received), custom_call_target="tpu_custom_call" | custom-call | bytes 524288 | tf_op jit(solution)/shard_map/pallas_call | solution.py:616
  (21 shorter events, 0.2 us)
Async XLA Ops:
  0.9 11.6 %collective-permute-start.2 = (bf16[16,2048]{1,0:T(8,128)(2,1)S(1)}, bf16[16,2048]{1,0:T(8,128)(2,1)S(1)}, u32[]{:S(2)}, u32[]{:S(2)}) collective-permute-start(bf16[16,2048]{1,0:T(8,128)(2,1)S(1)} %get-tuple-element.48.refs_0_), channel_id=1, source_target_pairs={{0,8},{4,12},{8,0},{12,4},{1,9},{5,13},{9,1},{13,5},{2,10},{6,14},... | collective-permute-start | bytes 196616 | tf_op jit(solution)/shard_map/ppermute | solution.py:206
  5.0 9.7 %collective-permute-start = (bf16[16,2048]{1,0:T(8,128)(2,1)S(1)}, bf16[16,2048]{1,0:T(8,128)(2,1)S(1)}, u32[]{:S(2)}, u32[]{:S(2)}) collective-permute-start(bf16[16,2048]{1,0:T(8,128)(2,1)S(1)} %get-tuple-element.48.refs_0_), channel_id=1, source_target_pairs={{0,4},{4,0},{8,12},{12,8},{1,5},{5,1},{9,13},{13,9},{2,6},{6,2},{1... | collective-permute-start | bytes 196616 | tf_op jit(solution)/shard_map/ppermute | solution.py:206
  6.6 7.9 %collective-permute-start.3 = (bf16[16,2048]{1,0:T(8,128)(2,1)S(1)}, bf16[16,2048]{1,0:T(8,128)(2,1)S(1)}, u32[]{:S(2)}, u32[]{:S(2)}) collective-permute-start(bf16[16,2048]{1,0:T(8,128)(2,1)S(1)} %get-tuple-element.47.refs_1_), channel_id=1, source_target_pairs={{0,8},{4,12},{8,0},{12,4},{1,9},{5,13},{9,1},{13,5},{2,10},{6,14},... | collective-permute-start | bytes 196616 | tf_op jit(solution)/shard_map/ppermute | solution.py:206
  6.9 7.7 %collective-permute-start.1 = (bf16[16,2048]{1,0:T(8,128)(2,1)S(1)}, bf16[16,2048]{1,0:T(8,128)(2,1)S(1)}, u32[]{:S(2)}, u32[]{:S(2)}) collective-permute-start(bf16[16,2048]{1,0:T(8,128)(2,1)S(1)} %get-tuple-element.47.refs_1_), channel_id=1, source_target_pairs={{0,4},{4,0},{8,12},{12,8},{1,5},{5,1},{9,13},{13,9},{2,6},{6,2},{1... | collective-permute-start | bytes 196616 | tf_op jit(solution)/shard_map/ppermute | solution.py:206
  7.9 10.8 %copy-start.2 = (s32[128]{0:T(128)S(1)}, s32[128]{0:T(128)}, u32[]{:S(2)}) copy-start(s32[128]{0:T(128)} %slots.3) | copy-start | bytes 1540
  12.5 4.4 %collective-permute-start.4 = (bf16[16,2048]{1,0:T(8,128)(2,1)S(1)}, bf16[16,2048]{1,0:T(8,128)(2,1)S(1)}, u32[]{:S(2)}, u32[]{:S(2)}) collective-permute-start(bf16[16,2048]{1,0:T(8,128)(2,1)S(1)} %shard_map.83.refs_4_), channel_id=1, source_target_pairs={{0,4},{4,0},{8,12},{12,8},{1,5},{5,1},{9,13},{13,9},{2,6},{6,2},{1... | collective-permute-start | bytes 196616 | tf_op jit(solution)/shard_map/ppermute | solution.py:206
  14.4 4.3 %collective-permute-start.5 = (bf16[16,2048]{1,0:T(8,128)(2,1)S(1)}, bf16[16,2048]{1,0:T(8,128)(2,1)S(1)}, u32[]{:S(2)}, u32[]{:S(2)}) collective-permute-start(bf16[16,2048]{1,0:T(8,128)(2,1)S(1)} %shard_map.84.refs_5_), channel_id=1, source_target_pairs={{0,4},{4,0},{8,12},{12,8},{1,5},{5,1},{9,13},{13,9},{2,6},{6,2},{1... | collective-permute-start | bytes 196616 | tf_op jit(solution)/shard_map/ppermute | solution.py:206
  20.5 1.7 %collective-permute-start.6 = (bf16[128,1408]{1,0:T(8,128)(2,1)S(1)}, bf16[128,1408]{1,0:T(8,128)(2,1)S(1)}, u32[]{:S(2)}, u32[]{:S(2)}) collective-permute-start(bf16[128,1408]{1,0:T(8,128)(2,1)S(1)} %get-tuple-element.30.given), channel_id=1, source_target_pairs={{0,1},{1,0},{2,3},{3,2},{4,5},{5,4},{6,7},{7,6},{8,9},{9,8},{10,11... | collective-permute-start | bytes 1081352 | tf_op jit(solution)/shard_map/ppermute | solution.py:206
  22.3 12.4 %collective-permute-start.7 = (bf16[32,1408]{1,0:T(8,128)(2,1)S(1)}, bf16[32,1408]{1,0:T(8,128)(2,1)S(1)}, u32[]{:S(2)}, u32[]{:S(2)}) collective-permute-start(bf16[32,1408]{1,0:T(8,128)(2,1)S(1)} %get-tuple-element.31), channel_id=1, source_target_pairs={{0,0},{2,8},{4,4},{6,12},{8,2},{10,10},{12,6},{14,14},{1,1},{3,9},... | collective-permute-start | bytes 270344 | tf_op jit(solution)/shard_map/ppermute | solution.py:408
  22.9 11.8 %collective-permute-start.9 = (bf16[32,1408]{1,0:T(8,128)(2,1)S(1)}, bf16[32,1408]{1,0:T(8,128)(2,1)S(1)}, u32[]{:S(2)}, u32[]{:S(2)}) collective-permute-start(bf16[32,1408]{1,0:T(8,128)(2,1)S(1)} %get-tuple-element.33), channel_id=1, source_target_pairs={{0,8},{2,0},{4,12},{6,4},{8,10},{10,2},{12,14},{14,6},{1,9},{3,1},... | collective-permute-start | bytes 270344 | tf_op jit(solution)/shard_map/ppermute | solution.py:408
  28.1 6.2 %collective-permute-start.10 = (bf16[32,1280]{1,0:T(8,128)(2,1)S(1)}, bf16[32,1280]{1,0:T(8,128)(2,1)S(1)}, u32[]{:S(2)}, u32[]{:S(2)}) collective-permute-start(bf16[32,1280]{1,0:T(8,128)(2,1)S(1)} %get-tuple-element.34), channel_id=1, source_target_pairs={{0,12},{2,4},{4,8},{6,0},{8,14},{10,6},{12,10},{14,2},{1,13},{3,5}... | collective-permute-start | bytes 245768 | tf_op jit(solution)/shard_map/ppermute | solution.py:408
  28.3 6.4 %copy-start.1 = (s32[32]{0:T(128)S(1)}, s32[32]{0:T(128)}, u32[]{:S(2)}) copy-start(s32[32]{0:T(128)} %lengths.3) | copy-start | bytes 388
  28.3 6.4 %collective-permute-start.8 = (bf16[32,1280]{1,0:T(8,128)(2,1)S(1)}, bf16[32,1280]{1,0:T(8,128)(2,1)S(1)}, u32[]{:S(2)}, u32[]{:S(2)}) collective-permute-start(bf16[32,1280]{1,0:T(8,128)(2,1)S(1)} %get-tuple-element.32), channel_id=1, source_target_pairs={{0,4},{2,12},{4,0},{6,8},{8,6},{10,14},{12,2},{14,10},{1,5},{3,13}... | collective-permute-start | bytes 245768 | tf_op jit(solution)/shard_map/ppermute | solution.py:408
  36.4 7.2 %collective-permute-start.14 = (bf16[16,2048]{1,0:T(8,128)(2,1)S(1)}, bf16[16,2048]{1,0:T(8,128)(2,1)S(1)}, u32[]{:S(2)}, u32[]{:S(2)}) collective-permute-start(bf16[16,2048]{1,0:T(8,128)(2,1)S(1)} %shard_map.90.refs_1_), channel_id=1, source_target_pairs={{0,8},{4,12},{8,0},{12,4},{1,9},{5,13},{9,1},{13,5},{2,10},{6,14},... | collective-permute-start | bytes 196616 | tf_op jit(solution)/shard_map/ppermute | solution.py:206
  41.4 5.3 %collective-permute-start.13 = (bf16[16,2048]{1,0:T(8,128)(2,1)S(1)}, bf16[16,2048]{1,0:T(8,128)(2,1)S(1)}, u32[]{:S(2)}, u32[]{:S(2)}) collective-permute-start(bf16[16,2048]{1,0:T(8,128)(2,1)S(1)} %shard_map.89.refs_0_), channel_id=1, source_target_pairs={{0,8},{4,12},{8,0},{12,4},{1,9},{5,13},{9,1},{13,5},{2,10},{6,14},... | collective-permute-start | bytes 196616 | tf_op jit(solution)/shard_map/ppermute | solution.py:206
  41.5 7.4 %collective-permute-start.12 = (bf16[16,2048]{1,0:T(8,128)(2,1)S(1)}, bf16[16,2048]{1,0:T(8,128)(2,1)S(1)}, u32[]{:S(2)}, u32[]{:S(2)}) collective-permute-start(bf16[16,2048]{1,0:T(8,128)(2,1)S(1)} %shard_map.90.refs_1_), channel_id=1, source_target_pairs={{0,4},{4,0},{8,12},{12,8},{1,5},{5,1},{9,13},{13,9},{2,6},{6,2},{1... | collective-permute-start | bytes 196616 | tf_op jit(solution)/shard_map/ppermute | solution.py:206
  43.4 5.5 %collective-permute-start.11 = (bf16[16,2048]{1,0:T(8,128)(2,1)S(1)}, bf16[16,2048]{1,0:T(8,128)(2,1)S(1)}, u32[]{:S(2)}, u32[]{:S(2)}) collective-permute-start(bf16[16,2048]{1,0:T(8,128)(2,1)S(1)} %shard_map.89.refs_0_), channel_id=1, source_target_pairs={{0,4},{4,0},{8,12},{12,8},{1,5},{5,1},{9,13},{13,9},{2,6},{6,2},{1... | collective-permute-start | bytes 196616 | tf_op jit(solution)/shard_map/ppermute | solution.py:206
  43.6 5.8 %collective-permute-start.16 = (bf16[16,2048]{1,0:T(8,128)(2,1)S(1)}, bf16[16,2048]{1,0:T(8,128)(2,1)S(1)}, u32[]{:S(2)}, u32[]{:S(2)}) collective-permute-start(bf16[16,2048]{1,0:T(8,128)(2,1)S(1)} %collective-permute-done.14.refs_5_), channel_id=1, source_target_pairs={{0,4},{4,0},{8,12},{12,8},{1,5},{5,1},{9,13},{13,9},{2,6},{6,2},{1... | collective-permute-start | bytes 196616 | tf_op jit(solution)/shard_map/ppermute | solution.py:206
  46.7 4.3 %collective-permute-start.15 = (bf16[16,2048]{1,0:T(8,128)(2,1)S(1)}, bf16[16,2048]{1,0:T(8,128)(2,1)S(1)}, u32[]{:S(2)}, u32[]{:S(2)}) collective-permute-start(bf16[16,2048]{1,0:T(8,128)(2,1)S(1)} %collective-permute-done.13.refs_4_), channel_id=1, source_target_pairs={{0,4},{4,0},{8,12},{12,8},{1,5},{5,1},{9,13},{13,9},{2,6},{6,2},{1... | collective-permute-start | bytes 196616 | tf_op jit(solution)/shard_map/ppermute | solution.py:206
  51.1 16.1 %copy-start = (bf16[32,4096]{1,0:T(8,128)(2,1)S(1)}, bf16[32,4096]{1,0:T(8,128)(2,1)}, u32[]{:S(2)}) copy-start(bf16[32,4096]{1,0:T(8,128)(2,1)} %hidden.1) | copy-start | bytes 786436
  52.6 1.6 %collective-permute-start.17 = (bf16[128,1024]{1,0:T(8,128)(2,1)S(1)}, bf16[128,1024]{1,0:T(8,128)(2,1)S(1)}, u32[]{:S(2)}, u32[]{:S(2)}) collective-permute-start(bf16[128,1024]{1,0:T(8,128)(2,1)S(1)} %get-tuple-element.40.given), channel_id=1, source_target_pairs={{0,1},{1,0},{2,3},{3,2},{4,5},{5,4},{6,7},{7,6},{8,9},{9,8},{10,11... | collective-permute-start | bytes 786440 | tf_op jit(solution)/shard_map/ppermute | solution.py:206
  54.3 8.2 %collective-permute-start.18 = (bf16[32,1024]{1,0:T(8,128)(2,1)S(1)}, bf16[32,1024]{1,0:T(8,128)(2,1)S(1)}, u32[]{:S(2)}, u32[]{:S(2)}) collective-permute-start(bf16[32,1024]{1,0:T(8,128)(2,1)S(1)} %get-tuple-element.41), channel_id=1, source_target_pairs={{0,0},{2,8},{4,4},{6,12},{8,2},{10,10},{12,6},{14,14},{1,1},{3,9},... | collective-permute-start | bytes 196616 | tf_op jit(solution)/shard_map/ppermute | solution.py:408
  54.9 7.5 %collective-permute-start.19 = (bf16[32,1024]{1,0:T(8,128)(2,1)S(1)}, bf16[32,1024]{1,0:T(8,128)(2,1)S(1)}, u32[]{:S(2)}, u32[]{:S(2)}) collective-permute-start(bf16[32,1024]{1,0:T(8,128)(2,1)S(1)} %get-tuple-element.42), channel_id=1, source_target_pairs={{0,4},{2,12},{4,0},{6,8},{8,6},{10,14},{12,2},{14,10},{1,5},{3,13}... | collective-permute-start | bytes 196616 | tf_op jit(solution)/shard_map/ppermute | solution.py:408
  57.0 8.5 %collective-permute-start.20 = (bf16[32,1024]{1,0:T(8,128)(2,1)S(1)}, bf16[32,1024]{1,0:T(8,128)(2,1)S(1)}, u32[]{:S(2)}, u32[]{:S(2)}) collective-permute-start(bf16[32,1024]{1,0:T(8,128)(2,1)S(1)} %get-tuple-element.43), channel_id=1, source_target_pairs={{0,8},{2,0},{4,12},{6,4},{8,10},{10,2},{12,14},{14,6},{1,9},{3,1},... | collective-permute-start | bytes 196616 | tf_op jit(solution)/shard_map/ppermute | solution.py:408
  61.1 6.1 %collective-permute-start.21 = (bf16[32,1024]{1,0:T(8,128)(2,1)S(1)}, bf16[32,1024]{1,0:T(8,128)(2,1)S(1)}, u32[]{:S(2)}, u32[]{:S(2)}) collective-permute-start(bf16[32,1024]{1,0:T(8,128)(2,1)S(1)} %get-tuple-element.44), channel_id=1, source_target_pairs={{0,12},{2,4},{4,8},{6,0},{8,14},{10,6},{12,10},{14,2},{1,13},{3,5}... | collective-permute-start | bytes 196616 | tf_op jit(solution)/shard_map/ppermute | solution.py:408
  67.8 1.4 %collective-permute-start.22 = (bf16[32,2048]{1,0:T(8,128)(2,1)S(1)}, bf16[32,2048]{1,0:T(8,128)(2,1)S(1)}, u32[]{:S(2)}, u32[]{:S(2)}) collective-permute-start(bf16[32,2048]{1,0:T(8,128)(2,1)S(1)} %get-tuple-element.46), channel_id=1, source_target_pairs={{0,1},{1,0},{2,3},{3,2},{4,5},{5,4},{6,7},{7,6},{8,9},{9,8},{10,11... | collective-permute-start | bytes 393224 | tf_op jit(solution)/shard_map/ppermute | solution.py:206

commit v5 on v4

--- a/solution.py
+++ b/solution.py
@@ -206,21 +206,6 @@
     return lax.ppermute(value, axis, pairs)
 
 
-def hold_kernel(value, token, out):
-    pass
-
-
-def held(value, token):
-    return pl.pallas_call(
-        hold_kernel,
-        out_shape=pltpu.VMEM(value.shape, value.dtype),
-        in_specs=[VMEM, HBM],
-        out_specs=VMEM,
-        input_output_aliases={0: 0},
-        compiler_params=pltpu.CompilerParams(vmem_limit_bytes=MIB),
-    )(in_vmem(value), token)
-
-
 def halves(place, weight, staged, row, target_row, size):
     width = staged[0].shape[1]
     copies = []
@@ -232,23 +217,36 @@
     return copies
 
 
-def run_copies(copies, sems):
+def started(copies, sems):
     copies = [
         pltpu.make_async_copy(source, target, sems.at[i])
         for i, (source, target) in enumerate(copies)
     ]
     for copy in copies:
         copy.start()
-    for copy in copies:
+    return copies
+
+
+def run_copies(copies, sems):
+    for copy in started(copies, sems):
         copy.wait()
 
 
-def stage_in_kernel(place, weight, *refs):
-    give_part, own_part, token, sems = refs[-4:]
-    token[...] = jnp.zeros(token.shape, token.dtype)
-    depth = own_part.shape[0]
-    first = pl.multiple_of(place[0] * depth, depth)
-    run_copies(halves(place, weight, (give_part, own_part), first, 0, depth), sems)
+def rows_of(place, weight, half, target, chunks=4):
+    depth, width = target.shape
+    size = depth // chunks
+    columns = pl.ds(pl.multiple_of(half * width, width), width)
+    return [
+        (
+            weight.at[pl.ds(pl.multiple_of(place[0] * depth + i * size, size), size), columns],
+            target.at[i * size : (i + 1) * size, :],
+        )
+        for i in range(chunks)
+    ]
+
+
+def stage_in_kernel(place, weight, gain, give_part, sems):
+    run_copies(rows_of(place, weight, 1 - place[0], give_part), sems)
 
 
 def stage_rest_kernel(
@@ -303,8 +301,10 @@
 
 
 def in_kernel(count, blocks, place, slots, *refs):
-    pieces_in, (gain, weight, give, permuted, scratch) = refs[:count], refs[count:]
+    pieces_in, refs = refs[:count], refs[count:]
+    gain, whole, weight, give, permuted, own_part, scratch, sems = refs
     side = place[0]
+    copies = started(rows_of(place, whole, side, own_part), sems)
     depth = pieces_in[0].shape[1]
     half = weight.shape[1]
     gains = gain[:, pl.ds(pl.multiple_of(side * depth, depth), depth)].astype(jnp.float32)
@@ -317,6 +317,8 @@
     permuted[...] = order
     give[:, half:] = jnp.dot(chosen, sums, preferred_element_type=jnp.float32).astype(jnp.bfloat16)
     dot_columns(order, weight, give)
+    for copy in copies:
+        copy.wait()
 
 
 def out_kernel(count, blocks, place, slots, *refs):
@@ -347,22 +349,29 @@
     dot_columns(permuted[...], weight, own)
 
 
-def project(kernel, place, slots, pieces_in, extra, weights, more, pairs):
+def project(kernel, place, slots, pieces_in, extra, weight, own_weight, more, pairs):
     count = lax.axis_size("col")
     parts = len(pieces_in)
     rows, depth = pieces_in[0].shape
     rows = rows * parts
-    half = weights[0].shape[1]
+    half = weight.shape[1]
     flops = 2 * rows * depth * half
-    give, permuted = call(
+    staged = own_weight is None
+    give, permuted, *rest = call(
         functools.partial(kernel, parts, count),
-        [struct((rows, half + more)), struct((rows, depth))],
-        [SMEM, VMEM] + [VMEM] * (parts + len(extra) + 1),
-        [VMEM, VMEM],
+        [struct((rows, half + more)), struct((rows, depth))]
+        + [pltpu.VMEM(weight.shape, weight.dtype)] * staged,
+        [SMEM, VMEM]
+        + [VMEM] * parts
+        + ([VMEM, HBM] if staged else [])
+        + [VMEM],
+        [VMEM] * (2 + staged),
         flops,
         depth * half * 2,
-        [pltpu.VMEM((rows, rows), jnp.float32)],
-    )(place, slots, *pieces_in, *extra, in_vmem(weights[0]))
+        [pltpu.VMEM((rows, rows), jnp.float32)] + [pltpu.SemaphoreType.DMA((4,))] * staged,
+    )(place, slots, *pieces_in, *extra, in_vmem(weight))
+    if staged:
+        (own_weight,) = rest
     received = moved(give, "side", 1)
     own = call(
         own_kernel,
@@ -371,7 +380,7 @@
         VMEM,
         flops,
         depth * half * 2,
-    )(permuted, in_vmem(weights[1]))
+    )(permuted, in_vmem(own_weight))
     return call(
         merge_kernel,
         [
@@ -384,7 +393,7 @@
     )(own, give, received)
 
 
-def gathered(parts, axis, token=None):
+def gathered(parts, axis):
     blocks = {0: parts}
     mask = lax.axis_size(axis) // 2
     while mask:
@@ -392,11 +401,6 @@
             known | mask: [moved(part, axis, mask) for part in block]
             for known, block in blocks.items()
         }
-        if token is not None and mask > 1:
-            blocks = {
-                known: [held(part, token) for part in block] if known else block
-                for known, block in blocks.items()
-            }
         mask //= 2
     return [part for i in sorted(blocks) for part in blocks[i]]
 
@@ -552,24 +556,22 @@
     rows, depth = hidden_in.shape
     half = depth // 2
     cache = key_cache.shape[1]
-    parts = 2
+    parts = 1
     piece = rows // parts
 
     own_part = lax.dynamic_slice_in_dim(hidden_in, side * half, half, 1)
     gain = norm_gain.reshape(1, depth)
     half_in, half_out = qkv_weight.shape[1] // 2, out_weight.shape[1] // 2
-    *weights_in, token = call(
+    weight_in = call(
         stage_in_kernel,
-        [pltpu.VMEM((half, half_in), jnp.bfloat16)] * 2 + [struct((8, 128), jnp.float32)],
+        pltpu.VMEM((half, half_in), jnp.bfloat16),
         [SMEM, HBM, HBM],
-        [VMEM] * 3,
+        VMEM,
         0,
-        half * half_in * 4,
-        [pltpu.SemaphoreType.DMA((2,))],
+        half * half_in * 2,
+        [pltpu.SemaphoreType.DMA((4,))],
     )(place, in_hbm(qkv_weight), gain)
-    blocks = gathered(
-        [own_part[i * piece : (i + 1) * piece] for i in range(parts)], "col", token
-    )
+    blocks = gathered([own_part], "col")
     *weights_out, key_part, value_part = call(
         stage_rest_kernel,
         [pltpu.VMEM((half, half_out), jnp.bfloat16)] * 2
@@ -582,7 +584,17 @@
     )(place, in_hbm(out_weight), in_hbm(key_cache), in_hbm(value_cache))
 
     products = spread(
-        project(in_kernel, place, slot_request, blocks, [gain], weights_in, HEAD_DIM, pairs)
+        project(
+            in_kernel,
+            place,
+            slot_request,
+            blocks,
+            [gain, in_hbm(qkv_weight)],
+            weight_in,
+            None,
+            HEAD_DIM,
+            pairs,
+        )
     )
 
     key_part, value_part = in_vmem(key_part), in_vmem(value_part)
@@ -602,7 +614,7 @@
 
     products = spread(
         project(
-            out_kernel, place, slot_request, gathered(attended, "col"), [], weights_out, 0, pairs
+            out_kernel, place, slot_request, gathered(attended, "col"), [], *weights_out, 0, pairs
         )
     )
     keep, send = call(

time: 71.1 us -> 73.1 us (1.028)
  waiting for transfers between devices: 16.5 us -> 25.2 us
  starting transfers between devices: 32.7 us -> 26.7 us
    ppermute x15 -> x9, starting transfers between devices: 18 us -> 9.12 us  [moved(): return lax.ppermute(value, axis, pairs)]
    ppermute x15 -> x9, waiting for transfers between devices: 10.5 us -> 19 us  [moved(): return lax.ppermute(value, axis, pairs)]
    ppermute x8, starting transfers between devices: 14.7 us -> 17.6 us  [spread(): lax.ppermute(products[j], ('col', 'row'), [(col * row_count + row, (row *...]
    pallas_call x2, Pallas kernels: 3.26 us -> 5.33 us  [project(): call(functools.partial(kernel, parts, count), [struct((rows, half + more)...]
    pallas_call x3 -> x1, Pallas kernels: 4.62 us -> 3.08 us  [paired_plan(): call(stage_in_kernel, pltpu.VMEM((half, half_in), jnp.bfloat16), [SMEM, H...]
    pallas_call x2 -> x1, Pallas kernels: 3.29 us -> 2.26 us  [paired_plan(): call(functools.partial(attend_all, col_count, first), struct((piece, half...]
    dynamic_slice x0 -> x1, local copies, waits for them, and re-layouts: none -> 0.91 us  [paired_plan(): own_part = lax.dynamic_slice_in_dim(hidden_in, side * half, half, 1)]
    slice x1 -> x0, local copies, waits for them, and re-layouts: 0.88 us -> none  [paired_plan(): own_part[i * piece:(i + 1) * piece]]
  transfers between devices with their start and end apart: 23 -> 17, of which waited for: 12 -> 10; matrix products, arithmetic and copies ran while one was open for 1% -> 1% of each run, Pallas kernels for 18% -> 13%
where the time goes in v5:
time: 73.1 us; the launch traced here: 72.8 us
  starting transfers between devices  26.7 us (37%)
  waiting for transfers between devices  25.2 us (34%)
  Pallas kernels  19.1 us (26%)
  local copies, waits for them, and re-layouts  1.63 us (2%)
    ppermute x9, waiting for transfers between devices, moved(): return lax.ppermute(value, axis, pairs)  19 us
    ppermute x8, starting transfers between devices, spread(): lax.ppermute(products[j], ('col', 'row'), [(col * row_count + row, (row *...  17.6 us
    ppermute x9, starting transfers between devices, moved(): return lax.ppermute(value, axis, pairs)  9.12 us
    ppermute x8, waiting for transfers between devices, spread(): lax.ppermute(products[j], ('col', 'row'), [(col * row_count + row, (row *...  6.22 us
    pallas_call x2, Pallas kernels, project(): call(functools.partial(kernel, parts, count), [struct((rows, half + more)...  5.33 us
    pallas_call x1, Pallas kernels, paired_plan(): call(stage_rest_kernel, [pltpu.VMEM((half, half_out), jnp.bfloat16)] * 2...  4.77 us
    pallas_call x1, Pallas kernels, paired_plan(): call(stage_in_kernel, pltpu.VMEM((half, half_in), jnp.bfloat16), [SMEM, H...  3.08 us
    pallas_call x1, Pallas kernels, paired_plan(): call(functools.partial(attend_all, col_count, first), struct((piece, half...  2.26 us
  transfers between devices with their start and end apart: 17, of which 10 were waited for; matrix products, arithmetic and copies ran while one was open for 1% of the time, Pallas kernels for 13%

profile of v5, /device:TPU:0, one launch (start us, length us, event | category | flops | bytes accessed | tf_op | source)
XLA Modules:
  0.0 72.8 jit_solution(1207838321900812632)
XLA Ops:
  0.0 0.9 %constant_dynamic-slice_fusion.refs_0_ = bf16[32,2048]{1,0:T(8,128)(2,1)S(1)} fusion(bf16[32,4096]{1,0:T(8,128)(2,1)} %hidden.1, s32[]{:T(128)S(6)} %select_n.3), kind=kLoop, calls=%fused_computation.1 | loop fusion | bytes 262148 | tf_op jit(solution)/shard_map/dynamic_slice | solution.py:562
  0.9 4.1 %collective-permute-start.1 = (bf16[32,2048]{1,0:T(8,128)(2,1)S(1)}, bf16[32,2048]{1,0:T(8,128)(2,1)S(1)}, u32[]{:S(2)}, u32[]{:S(2)}) collective-permute-start(bf16[32,2048]{1,0:T(8,128)(2,1)S(1)} %constant_dynamic-slice_fusion.refs_0_), channel_id=1, source_target_pairs={{0,8},{4,12},{8,0},{12,4},{1,9},{5,13},{9,1},{13,5},{2,10},{6,14},... | collective-permute-start | bytes 393224 | tf_op jit(solution)/shard_map/ppermute | solution.py:206
  5.0 1.6 %collective-permute-start = (bf16[32,2048]{1,0:T(8,128)(2,1)S(1)}, bf16[32,2048]{1,0:T(8,128)(2,1)S(1)}, u32[]{:S(2)}, u32[]{:S(2)}) collective-permute-start(bf16[32,2048]{1,0:T(8,128)(2,1)S(1)} %constant_dynamic-slice_fusion.refs_0_), channel_id=1, source_target_pairs={{0,4},{4,0},{8,12},{12,8},{1,5},{5,1},{9,13},{13,9},{2,6},{6,2},{1... | collective-permute-start | bytes 393224 | tf_op jit(solution)/shard_map/ppermute | solution.py:206
  6.6 4.8 %collective-permute-done.1.refs_2_ = bf16[32,2048]{1,0:T(8,128)(2,1)S(1)} collective-permute-done((bf16[32,2048]{1,0:T(8,128)(2,1)S(1)}, bf16[32,2048]{1,0:T(8,128)(2,1)S(1)}, u32[]{:S(2)}, u32[]{:S(2)}) %collective-permute-start.1) | collective-permute-done | bytes 131104 | tf_op jit(solution)/shard_map/ppermute | solution.py:206
  11.4 0.6 collective-permute-start.2
  12.0 0.7 reshape.3.gain.refs_4_
  12.8 0.1 pad_add_fusion.place
  12.8 3.1 %shard_map.82.refs_6_ = bf16[2048,1280]{1,0:T(8,128)(2,1)S(1)} custom-call(s32[3]{0:T(128)S(1)} %pad_add_fusion.place, bf16[4096,2560]{1,0:T(8,128)(2,1)} %refs_5_.1, bf16[1,4096]{1,0:T(2,128)(2,1)S(1)} %reshape.3.gain.refs_4_), custom_call_target="tpu_custom_call" | custom-call | bytes 5242880 | tf_op jit(solution)/shard_map/pallas_call | solution.py:565
  15.9 0.0 collective-permute-done.refs_1_
  15.9 0.5 collective-permute-done.2.refs_3_
  16.4 3.8 %shard_map.83 = (bf16[128,1408]{1,0:T(8,128)(2,1)S(1)}, bf16[128,2048]{1,0:T(8,128)(2,1)S(1)}, bf16[2048,1280]{1,0:T(8,128)(2,1)S(1)}) custom-call(s32[3]{0:T(128)S(1)} %pad_add_fusion.place, s32[128]{0:T(128)S(1)} %copy-done.1, bf16[32,2048]{1,0:T(8,128)(2,1)S(1)} %constant_dynamic-slice_fusion.refs_0_, bf16[32,2048]{1,0:T(8,128)(2,1)S(1)} %collective-permute-done.refs_1_, ...), custom_call_target="tpu_custom_call" | custom-call | flops 671088640 | bytes 5242880 | tf_op jit(solution)/shard_map/pallas_call | solution.py:360
  20.2 0.1 collective-permute-start.3
  20.3 0.9 %shard_map.84.own = f32[128,1280]{1,0:T(8,128)S(1)} custom-call(bf16[128,2048]{1,0:T(8,128)(2,1)S(1)} %get-tuple-element.24.permuted, bf16[2048,1280]{1,0:T(8,128)(2,1)S(1)} %get-tuple-element.25.weight), custom_call_target="tpu_custom_call" | custom-call | flops 671088640 | bytes 5242880 | tf_op jit(solution)/shard_map/pallas_call | solution.py:376
  21.2 0.8 %collective-permute-done.3.received = bf16[128,1408]{1,0:T(8,128)(2,1)S(1)} collective-permute-done((bf16[128,1408]{1,0:T(8,128)(2,1)S(1)}, bf16[128,1408]{1,0:T(8,128)(2,1)S(1)}, u32[]{:S(2)}, u32[]{:S(2)}) %collective-permute-start.3) | collective-permute-done | bytes 360480 | tf_op jit(solution)/shard_map/ppermute | solution.py:206
  22.0 0.1 shard_map.85
  22.0 0.7 collective-permute-start.4
  22.7 5.2 %collective-permute-start.6 = (bf16[32,1408]{1,0:T(8,128)(2,1)S(1)}, bf16[32,1408]{1,0:T(8,128)(2,1)S(1)}, u32[]{:S(2)}, u32[]{:S(2)}) collective-permute-start(bf16[32,1408]{1,0:T(8,128)(2,1)S(1)} %get-tuple-element.29), channel_id=1, source_target_pairs={{0,8},{2,0},{4,12},{6,4},{8,10},{10,2},{12,14},{14,6},{1,9},{3,1},... | collective-permute-start | bytes 270344 | tf_op jit(solution)/shard_map/ppermute | solution.py:412
  27.9 1.0 %collective-permute-start.5 = (bf16[32,1280]{1,0:T(8,128)(2,1)S(1)}, bf16[32,1280]{1,0:T(8,128)(2,1)S(1)}, u32[]{:S(2)}, u32[]{:S(2)}) collective-permute-start(bf16[32,1280]{1,0:T(8,128)(2,1)S(1)} %get-tuple-element.28), channel_id=1, source_target_pairs={{0,4},{2,12},{4,0},{6,8},{8,6},{10,14},{12,2},{14,10},{1,5},{3,13}... | collective-permute-start | bytes 245768 | tf_op jit(solution)/shard_map/ppermute | solution.py:412
  28.9 2.8 %collective-permute-start.7 = (bf16[32,1280]{1,0:T(8,128)(2,1)S(1)}, bf16[32,1280]{1,0:T(8,128)(2,1)S(1)}, u32[]{:S(2)}, u32[]{:S(2)}) collective-permute-start(bf16[32,1280]{1,0:T(8,128)(2,1)S(1)} %get-tuple-element.30), channel_id=1, source_target_pairs={{0,12},{2,4},{4,8},{6,0},{8,14},{10,6},{12,10},{14,2},{1,13},{3,5}... | collective-permute-start | bytes 245768 | tf_op jit(solution)/shard_map/ppermute | solution.py:412
  31.7 4.8 %shard_map.86 = (bf16[2048,1024]{1,0:T(8,128)(2,1)S(1)}, bf16[2048,1024]{1,0:T(8,128)(2,1)S(1)}, bf16[32,64,256]{2,1,0:T(8,128)(2,1)S(1)}, bf16[32,64,256]{2,1,0:T(8,128)(2,1)S(1)}) custom-call(s32[3]{0:T(128)S(1)} %pad_add_fusion.place, bf16[4096,2048]{1,0:T(8,128)(2,1)} %weight.3, bf16[32,64,512]{2,1,0:T(8,128)(2,1)} %keys.1, bf16[32,64,512]{2,1,0:T(8,128)(2,1)} %values.1), custom_call_target="tpu_custom_call" | custom-call | bytes 10485760 | tf_op jit(solution)/shard_map/pallas_call | solution.py:575
  36.5 0.0 collective-permute-done.5.refs_1_
  36.5 0.0 collective-permute-done.7.refs_3_
  36.5 0.0 collective-permute-done.4.refs_0_
  36.6 0.0 collective-permute-done.6.refs_2_
  36.6 2.3 %shard_map.87.refs_0_ = bf16[32,2048]{1,0:T(8,128)(2,1)S(1)} custom-call(s32[3]{0:T(128)S(1)} %pad_add_fusion.place, s32[32]{0:T(128)S(1)} %copy-done.2, bf16[32,1408]{1,0:T(8,128)(2,1)S(1)} %collective-permute-done.4.refs_0_, bf16[32,1280]{1,0:T(8,128)(2,1)S(1)} %collective-permute-done.5.refs_1_, bf16[32,1408]{1,0:T(8,128)(2,1)S(1)} %collective-permute-done.6.refs_2_, ...), custom_call_target="tpu_custom_call" | custom-call | flops 16777216 | tf_op jit(solution)/shard_map/pallas_call | solution.py:603
  38.8 2.3 %collective-permute-start.9 = (bf16[32,2048]{1,0:T(8,128)(2,1)S(1)}, bf16[32,2048]{1,0:T(8,128)(2,1)S(1)}, u32[]{:S(2)}, u32[]{:S(2)}) collective-permute-start(bf16[32,2048]{1,0:T(8,128)(2,1)S(1)} %shard_map.87.refs_0_), channel_id=1, source_target_pairs={{0,8},{4,12},{8,0},{12,4},{1,9},{5,13},{9,1},{13,5},{2,10},{6,14},... | collective-permute-start | bytes 393224 | tf_op jit(solution)/shard_map/ppermute | solution.py:206
  41.2 0.3 collective-permute-start.8
  41.4 5.4 %collective-permute-done.9.refs_2_ = bf16[32,2048]{1,0:T(8,128)(2,1)S(1)} collective-permute-done((bf16[32,2048]{1,0:T(8,128)(2,1)S(1)}, bf16[32,2048]{1,0:T(8,128)(2,1)S(1)}, u32[]{:S(2)}, u32[]{:S(2)}) %collective-permute-start.9) | collective-permute-done | bytes 131104 | tf_op jit(solution)/shard_map/ppermute | solution.py:206
  46.9 0.0 collective-permute-start.10
  46.9 2.1 %collective-permute-done.8.refs_1_ = bf16[32,2048]{1,0:T(8,128)(2,1)S(1)} collective-permute-done((bf16[32,2048]{1,0:T(8,128)(2,1)S(1)}, bf16[32,2048]{1,0:T(8,128)(2,1)S(1)}, u32[]{:S(2)}, u32[]{:S(2)}) %collective-permute-start.8) | collective-permute-done | bytes 131104 | tf_op jit(solution)/shard_map/ppermute | solution.py:206
  49.0 3.2 %collective-permute-done.10.refs_3_ = bf16[32,2048]{1,0:T(8,128)(2,1)S(1)} collective-permute-done((bf16[32,2048]{1,0:T(8,128)(2,1)S(1)}, bf16[32,2048]{1,0:T(8,128)(2,1)S(1)}, u32[]{:S(2)}, u32[]{:S(2)}) %collective-permute-start.10) | collective-permute-done | bytes 131104 | tf_op jit(solution)/shard_map/ppermute | solution.py:206
  52.2 1.5 %shard_map.88 = (bf16[128,1024]{1,0:T(8,128)(2,1)S(1)}, bf16[128,2048]{1,0:T(8,128)(2,1)S(1)}) custom-call(s32[3]{0:T(128)S(1)} %pad_add_fusion.place, s32[128]{0:T(128)S(1)} %copy-done.1, bf16[32,2048]{1,0:T(8,128)(2,1)S(1)} %shard_map.87.refs_0_, bf16[32,2048]{1,0:T(8,128)(2,1)S(1)} %collective-permute-done.8.refs_1_, ...), custom_call_target="tpu_custom_call" | custom-call | flops 536870912 | bytes 4194304 | tf_op jit(solution)/shard_map/pallas_call | solution.py:360
  53.8 0.1 collective-permute-start.11
  53.9 0.8 %shard_map.89.own = f32[128,1024]{1,0:T(8,128)S(1)} custom-call(bf16[128,2048]{1,0:T(8,128)(2,1)S(1)} %get-tuple-element.34.permuted, bf16[2048,1024]{1,0:T(8,128)(2,1)S(1)} %get-tuple-element.35.weight), custom_call_target="tpu_custom_call" | custom-call | flops 536870912 | bytes 4194304 | tf_op jit(solution)/shard_map/pallas_call | solution.py:376
  54.6 0.8 %collective-permute-done.11.received = bf16[128,1024]{1,0:T(8,128)(2,1)S(1)} collective-permute-done((bf16[128,1024]{1,0:T(8,128)(2,1)S(1)}, bf16[128,1024]{1,0:T(8,128)(2,1)S(1)}, u32[]{:S(2)}, u32[]{:S(2)}) %collective-permute-start.11) | collective-permute-done | bytes 262176 | tf_op jit(solution)/shard_map/ppermute | solution.py:206
  55.4 0.7 collective-permute-start.12
  56.1 0.4 collective-permute-start.13
  56.5 6.3 %collective-permute-start.14 = (bf16[32,1024]{1,0:T(8,128)(2,1)S(1)}, bf16[32,1024]{1,0:T(8,128)(2,1)S(1)}, u32[]{:S(2)}, u32[]{:S(2)}) collective-permute-start(bf16[32,1024]{1,0:T(8,128)(2,1)S(1)} %get-tuple-element.39), channel_id=1, source_target_pairs={{0,8},{2,0},{4,12},{6,4},{8,10},{10,2},{12,14},{14,6},{1,9},{3,1},... | collective-permute-start | bytes 196616 | tf_op jit(solution)/shard_map/ppermute | solution.py:412
  62.7 0.6 collective-permute-start.15
  63.3 0.0 collective-permute-done.12.refs_1_
  63.3 0.0 collective-permute-done.13.refs_2_
  63.3 1.3 %collective-permute-done.14.refs_3_ = bf16[32,1024]{1,0:T(8,128)(2,1)S(1)} collective-permute-done((bf16[32,1024]{1,0:T(8,128)(2,1)S(1)}, bf16[32,1024]{1,0:T(8,128)(2,1)S(1)}, u32[]{:S(2)}, u32[]{:S(2)}) %collective-permute-start.14) | collective-permute-done | bytes 65568 | tf_op jit(solution)/shard_map/ppermute | solution.py:412
  64.7 4.9 %collective-permute-done.15.refs_4_ = bf16[32,1024]{1,0:T(8,128)(2,1)S(1)} collective-permute-done((bf16[32,1024]{1,0:T(8,128)(2,1)S(1)}, bf16[32,1024]{1,0:T(8,128)(2,1)S(1)}, u32[]{:S(2)}, u32[]{:S(2)}) %collective-permute-start.15) | collective-permute-done | bytes 65568 | tf_op jit(solution)/shard_map/ppermute | solution.py:412
  69.5 0.0 copy-done
  69.5 0.6 shard_map.91
  70.2 0.1 collective-permute-start.16
  70.2 1.3 %collective-permute-done.16.received = bf16[32,2048]{1,0:T(8,128)(2,1)S(1)} collective-permute-done((bf16[32,2048]{1,0:T(8,128)(2,1)S(1)}, bf16[32,2048]{1,0:T(8,128)(2,1)S(1)}, u32[]{:S(2)}, u32[]{:S(2)}) %collective-permute-start.16) | collective-permute-done | bytes 131104 | tf_op jit(solution)/shard_map/ppermute | solution.py:206
  71.6 1.3 %shard_map.92 = bf16[1,32,4096]{2,1,0:T(8,128)(2,1)} custom-call(s32[3]{0:T(128)S(1)} %pad_add_fusion.place, bf16[32,2048]{1,0:T(8,128)(2,1)S(1)} %get-tuple-element.41.keep, bf16[32,2048]{1,0:T(8,128)(2,1)S(1)} %collective-permute-done.16.received), custom_call_target="tpu_custom_call" | custom-call | bytes 524288 | tf_op jit(solution)/shard_map/pallas_call | solution.py:628
  (6 shorter events, 0.1 us)
Async XLA Ops:
  0.9 10.5 %collective-permute-start.1 = (bf16[32,2048]{1,0:T(8,128)(2,1)S(1)}, bf16[32,2048]{1,0:T(8,128)(2,1)S(1)}, u32[]{:S(2)}, u32[]{:S(2)}) collective-permute-start(bf16[32,2048]{1,0:T(8,128)(2,1)S(1)} %constant_dynamic-slice_fusion.refs_0_), channel_id=1, source_target_pairs={{0,8},{4,12},{8,0},{12,4},{1,9},{5,13},{9,1},{13,5},{2,10},{6,14},... | collective-permute-start | bytes 393224 | tf_op jit(solution)/shard_map/ppermute | solution.py:206
  5.0 10.9 %collective-permute-start = (bf16[32,2048]{1,0:T(8,128)(2,1)S(1)}, bf16[32,2048]{1,0:T(8,128)(2,1)S(1)}, u32[]{:S(2)}, u32[]{:S(2)}) collective-permute-start(bf16[32,2048]{1,0:T(8,128)(2,1)S(1)} %constant_dynamic-slice_fusion.refs_0_), channel_id=1, source_target_pairs={{0,4},{4,0},{8,12},{12,8},{1,5},{5,1},{9,13},{13,9},{2,6},{6,2},{1... | collective-permute-start | bytes 393224 | tf_op jit(solution)/shard_map/ppermute | solution.py:206
  11.4 5.0 %collective-permute-start.2 = (bf16[32,2048]{1,0:T(8,128)(2,1)S(1)}, bf16[32,2048]{1,0:T(8,128)(2,1)S(1)}, u32[]{:S(2)}, u32[]{:S(2)}) collective-permute-start(bf16[32,2048]{1,0:T(8,128)(2,1)S(1)} %collective-permute-done.1.refs_2_), channel_id=1, source_target_pairs={{0,4},{4,0},{8,12},{12,8},{1,5},{5,1},{9,13},{13,9},{2,6},{6,2},{1... | collective-permute-start | bytes 393224 | tf_op jit(solution)/shard_map/ppermute | solution.py:206
  12.8 3.6 %copy-start.1 = (s32[128]{0:T(128)S(1)}, s32[128]{0:T(128)}, u32[]{:S(2)}) copy-start(s32[128]{0:T(128)} %slots.3) | copy-start | bytes 1540
  20.2 1.7 %collective-permute-start.3 = (bf16[128,1408]{1,0:T(8,128)(2,1)S(1)}, bf16[128,1408]{1,0:T(8,128)(2,1)S(1)}, u32[]{:S(2)}, u32[]{:S(2)}) collective-permute-start(bf16[128,1408]{1,0:T(8,128)(2,1)S(1)} %get-tuple-element.26.given), channel_id=1, source_target_pairs={{0,1},{1,0},{2,3},{3,2},{4,5},{5,4},{6,7},{7,6},{8,9},{9,8},{10,11... | collective-permute-start | bytes 1081352 | tf_op jit(solution)/shard_map/ppermute | solution.py:206
  22.0 14.5 %collective-permute-start.4 = (bf16[32,1408]{1,0:T(8,128)(2,1)S(1)}, bf16[32,1408]{1,0:T(8,128)(2,1)S(1)}, u32[]{:S(2)}, u32[]{:S(2)}) collective-permute-start(bf16[32,1408]{1,0:T(8,128)(2,1)S(1)} %get-tuple-element.27), channel_id=1, source_target_pairs={{0,0},{2,8},{4,4},{6,12},{8,2},{10,10},{12,6},{14,14},{1,1},{3,9},... | collective-permute-start | bytes 270344 | tf_op jit(solution)/shard_map/ppermute | solution.py:412
  22.7 13.9 %collective-permute-start.6 = (bf16[32,1408]{1,0:T(8,128)(2,1)S(1)}, bf16[32,1408]{1,0:T(8,128)(2,1)S(1)}, u32[]{:S(2)}, u32[]{:S(2)}) collective-permute-start(bf16[32,1408]{1,0:T(8,128)(2,1)S(1)} %get-tuple-element.29), channel_id=1, source_target_pairs={{0,8},{2,0},{4,12},{6,4},{8,10},{10,2},{12,14},{14,6},{1,9},{3,1},... | collective-permute-start | bytes 270344 | tf_op jit(solution)/shard_map/ppermute | solution.py:412
  27.9 8.6 %collective-permute-start.5 = (bf16[32,1280]{1,0:T(8,128)(2,1)S(1)}, bf16[32,1280]{1,0:T(8,128)(2,1)S(1)}, u32[]{:S(2)}, u32[]{:S(2)}) collective-permute-start(bf16[32,1280]{1,0:T(8,128)(2,1)S(1)} %get-tuple-element.28), channel_id=1, source_target_pairs={{0,4},{2,12},{4,0},{6,8},{8,6},{10,14},{12,2},{14,10},{1,5},{3,13}... | collective-permute-start | bytes 245768 | tf_op jit(solution)/shard_map/ppermute | solution.py:412
  28.9 7.7 %copy-start.2 = (s32[32]{0:T(128)S(1)}, s32[32]{0:T(128)}, u32[]{:S(2)}) copy-start(s32[32]{0:T(128)} %lengths.1) | copy-start | bytes 388
  28.9 7.6 %collective-permute-start.7 = (bf16[32,1280]{1,0:T(8,128)(2,1)S(1)}, bf16[32,1280]{1,0:T(8,128)(2,1)S(1)}, u32[]{:S(2)}, u32[]{:S(2)}) collective-permute-start(bf16[32,1280]{1,0:T(8,128)(2,1)S(1)} %get-tuple-element.30), channel_id=1, source_target_pairs={{0,12},{2,4},{4,8},{6,0},{8,14},{10,6},{12,10},{14,2},{1,13},{3,5}... | collective-permute-start | bytes 245768 | tf_op jit(solution)/shard_map/ppermute | solution.py:412
  38.8 8.1 %collective-permute-start.9 = (bf16[32,2048]{1,0:T(8,128)(2,1)S(1)}, bf16[32,2048]{1,0:T(8,128)(2,1)S(1)}, u32[]{:S(2)}, u32[]{:S(2)}) collective-permute-start(bf16[32,2048]{1,0:T(8,128)(2,1)S(1)} %shard_map.87.refs_0_), channel_id=1, source_target_pairs={{0,8},{4,12},{8,0},{12,4},{1,9},{5,13},{9,1},{13,5},{2,10},{6,14},... | collective-permute-start | bytes 393224 | tf_op jit(solution)/shard_map/ppermute | solution.py:206
  41.2 7.8 %collective-permute-start.8 = (bf16[32,2048]{1,0:T(8,128)(2,1)S(1)}, bf16[32,2048]{1,0:T(8,128)(2,1)S(1)}, u32[]{:S(2)}, u32[]{:S(2)}) collective-permute-start(bf16[32,2048]{1,0:T(8,128)(2,1)S(1)} %shard_map.87.refs_0_), channel_id=1, source_target_pairs={{0,4},{4,0},{8,12},{12,8},{1,5},{5,1},{9,13},{13,9},{2,6},{6,2},{1... | collective-permute-start | bytes 393224 | tf_op jit(solution)/shard_map/ppermute | solution.py:206
  46.9 5.4 %collective-permute-start.10 = (bf16[32,2048]{1,0:T(8,128)(2,1)S(1)}, bf16[32,2048]{1,0:T(8,128)(2,1)S(1)}, u32[]{:S(2)}, u32[]{:S(2)}) collective-permute-start(bf16[32,2048]{1,0:T(8,128)(2,1)S(1)} %collective-permute-done.9.refs_2_), channel_id=1, source_target_pairs={{0,4},{4,0},{8,12},{12,8},{1,5},{5,1},{9,13},{13,9},{2,6},{6,2},{1... | collective-permute-start | bytes 393224 | tf_op jit(solution)/shard_map/ppermute | solution.py:206
  52.2 17.3 %copy-start = (bf16[32,4096]{1,0:T(8,128)(2,1)S(1)}, bf16[32,4096]{1,0:T(8,128)(2,1)}, u32[]{:S(2)}) copy-start(bf16[32,4096]{1,0:T(8,128)(2,1)} %hidden.1) | copy-start | bytes 786436
  53.8 1.6 %collective-permute-start.11 = (bf16[128,1024]{1,0:T(8,128)(2,1)S(1)}, bf16[128,1024]{1,0:T(8,128)(2,1)S(1)}, u32[]{:S(2)}, u32[]{:S(2)}) collective-permute-start(bf16[128,1024]{1,0:T(8,128)(2,1)S(1)} %get-tuple-element.36.given), channel_id=1, source_target_pairs={{0,1},{1,0},{2,3},{3,2},{4,5},{5,4},{6,7},{7,6},{8,9},{9,8},{10,11... | collective-permute-start | bytes 786440 | tf_op jit(solution)/shard_map/ppermute | solution.py:206
  55.4 7.9 %collective-permute-start.12 = (bf16[32,1024]{1,0:T(8,128)(2,1)S(1)}, bf16[32,1024]{1,0:T(8,128)(2,1)S(1)}, u32[]{:S(2)}, u32[]{:S(2)}) collective-permute-start(bf16[32,1024]{1,0:T(8,128)(2,1)S(1)} %get-tuple-element.37), channel_id=1, source_target_pairs={{0,0},{2,8},{4,4},{6,12},{8,2},{10,10},{12,6},{14,14},{1,1},{3,9},... | collective-permute-start | bytes 196616 | tf_op jit(solution)/shard_map/ppermute | solution.py:412
  56.1 7.2 %collective-permute-start.13 = (bf16[32,1024]{1,0:T(8,128)(2,1)S(1)}, bf16[32,1024]{1,0:T(8,128)(2,1)S(1)}, u32[]{:S(2)}, u32[]{:S(2)}) collective-permute-start(bf16[32,1024]{1,0:T(8,128)(2,1)S(1)} %get-tuple-element.38), channel_id=1, source_target_pairs={{0,4},{2,12},{4,0},{6,8},{8,6},{10,14},{12,2},{14,10},{1,5},{3,13}... | collective-permute-start | bytes 196616 | tf_op jit(solution)/shard_map/ppermute | solution.py:412
  56.5 8.2 %collective-permute-start.14 = (bf16[32,1024]{1,0:T(8,128)(2,1)S(1)}, bf16[32,1024]{1,0:T(8,128)(2,1)S(1)}, u32[]{:S(2)}, u32[]{:S(2)}) collective-permute-start(bf16[32,1024]{1,0:T(8,128)(2,1)S(1)} %get-tuple-element.39), channel_id=1, source_target_pairs={{0,8},{2,0},{4,12},{6,4},{8,10},{10,2},{12,14},{14,6},{1,9},{3,1},... | collective-permute-start | bytes 196616 | tf_op jit(solution)/shard_map/ppermute | solution.py:412
  62.7 6.8 %collective-permute-start.15 = (bf16[32,1024]{1,0:T(8,128)(2,1)S(1)}, bf16[32,1024]{1,0:T(8,128)(2,1)S(1)}, u32[]{:S(2)}, u32[]{:S(2)}) collective-permute-start(bf16[32,1024]{1,0:T(8,128)(2,1)S(1)} %get-tuple-element.40), channel_id=1, source_target_pairs={{0,12},{2,4},{4,8},{6,0},{8,14},{10,6},{12,10},{14,2},{1,13},{3,5}... | collective-permute-start | bytes 196616 | tf_op jit(solution)/shard_map/ppermute | solution.py:412
  70.2 1.4 %collective-permute-start.16 = (bf16[32,2048]{1,0:T(8,128)(2,1)S(1)}, bf16[32,2048]{1,0:T(8,128)(2,1)S(1)}, u32[]{:S(2)}, u32[]{:S(2)}) collective-permute-start(bf16[32,2048]{1,0:T(8,128)(2,1)S(1)} %get-tuple-element.42), channel_id=1, source_target_pairs={{0,1},{1,0},{2,3},{3,2},{4,5},{5,4},{6,7},{7,6},{8,9},{9,8},{10,11... | collective-permute-start | bytes 393224 | tf_op jit(solution)/shard_map/ppermute | solution.py:206

commit v6 on v4

--- a/solution.py
+++ b/solution.py
@@ -206,32 +206,6 @@
     return lax.ppermute(value, axis, pairs)
 
 
-def hold_kernel(value, token, out):
-    pass
-
-
-def held(value, token):
-    return pl.pallas_call(
-        hold_kernel,
-        out_shape=pltpu.VMEM(value.shape, value.dtype),
-        in_specs=[VMEM, HBM],
-        out_specs=VMEM,
-        input_output_aliases={0: 0},
-        compiler_params=pltpu.CompilerParams(vmem_limit_bytes=MIB),
-    )(in_vmem(value), token)
-
-
-def halves(place, weight, staged, row, target_row, size):
-    width = staged[0].shape[1]
-    copies = []
-    for target, half in zip(staged, (1 - place[0], place[0])):
-        columns = pl.ds(pl.multiple_of(half * width, width), width)
-        copies.append(
-            (weight.at[pl.ds(row, size), columns], target.at[pl.ds(target_row, size), :])
-        )
-    return copies
-
-
 def run_copies(copies, sems):
     copies = [
         pltpu.make_async_copy(source, target, sems.at[i])
@@ -243,31 +217,41 @@
         copy.wait()
 
 
-def stage_in_kernel(place, weight, *refs):
-    give_part, own_part, token, sems = refs[-4:]
-    token[...] = jnp.zeros(token.shape, token.dtype)
-    depth = own_part.shape[0]
-    first = pl.multiple_of(place[0] * depth, depth)
-    run_copies(halves(place, weight, (give_part, own_part), first, 0, depth), sems)
-
-
-def stage_rest_kernel(
-    place, weight, keys, values, give_part, own_part, key_part, value_part, sems
-):
+def stage_in_kernel(place, weight, gain, give_part, own_part, sems):
+    depth, width = own_part.shape
+    rows = pl.ds(pl.multiple_of(place[0] * depth, depth), depth)
     copies = []
-    for j in range(own_part.shape[0] // OUT_WIDTH):
+    for target, half in ((give_part, 1 - place[0]), (own_part, place[0])):
+        columns = pl.ds(pl.multiple_of(half * width, width), width)
+        copies.append((weight.at[rows, columns], target))
+    run_copies(copies, sems)
+
+
+def stage_out_kernel(give, place, weight, *refs):
+    sems = refs[-1]
+    target = refs[2] if give else refs[1]
+    width = target.shape[1]
+    half = 1 - place[0] if give else place[0]
+    columns = pl.ds(pl.multiple_of(half * width, width), width)
+    copies = []
+    for j in range(target.shape[0] // OUT_WIDTH):
         head = 2 * j + place[0]
         row = pl.multiple_of(head * OUT_WIDTH, OUT_WIDTH)
-        lane = pl.multiple_of(head * HEAD_DIM, HEAD_DIM)
-        for source, target in ((keys, key_part), (values, value_part)):
-            copies.append(
-                (
-                    source.at[:, :, pl.ds(lane, HEAD_DIM)],
-                    target.at[:, :, pl.ds(j * HEAD_DIM, HEAD_DIM)],
+        if give:
+            keys, values, _, key_part, value_part, _ = refs
+            lane = pl.multiple_of(head * HEAD_DIM, HEAD_DIM)
+            for cache, part in ((keys, key_part), (values, value_part)):
+                copies.append(
+                    (
+                        cache.at[:, :, pl.ds(lane, HEAD_DIM)],
+                        part.at[:, :, pl.ds(j * HEAD_DIM, HEAD_DIM)],
+                    )
                 )
+        copies.append(
+            (
+                weight.at[pl.ds(row, OUT_WIDTH), columns],
+                target.at[pl.ds(j * OUT_WIDTH, OUT_WIDTH), :],
             )
-        copies += halves(
-            place, weight, (give_part, own_part), row, j * OUT_WIDTH, OUT_WIDTH
         )
     run_copies(copies, sems)
 
@@ -320,7 +304,7 @@
 
 
 def out_kernel(count, blocks, place, slots, *refs):
-    pieces_in, (weight, give, permuted, scratch) = refs[:count], refs[count:]
+    pieces_in, (_, weight, give, permuted, scratch) = refs[:count], refs[count:]
     values = jnp.concatenate([piece[...] for piece in pieces_in], axis=0)
     chosen = one_hot(slots, scratch, blocks, place[1], place[2]).T.astype(jnp.bfloat16)
     order = jnp.dot(chosen, values, preferred_element_type=jnp.float32).astype(jnp.bfloat16)
@@ -375,7 +359,8 @@
     return call(
         merge_kernel,
         [
-            struct((rows // count, half + (0 if i % pairs else more))) for i in range(count)
+            struct((rows // count, half + (more if i % pairs == pairs - 1 else 0)))
+            for i in range(count)
         ],
         [VMEM] * 3,
         [VMEM] * count,
@@ -384,7 +369,7 @@
     )(own, give, received)
 
 
-def gathered(parts, axis, token=None):
+def gathered(parts, axis):
     blocks = {0: parts}
     mask = lax.axis_size(axis) // 2
     while mask:
@@ -392,11 +377,6 @@
             known | mask: [moved(part, axis, mask) for part in block]
             for known, block in blocks.items()
         }
-        if token is not None and mask > 1:
-            blocks = {
-                known: [held(part, token) for part in block] if known else block
-                for known, block in blocks.items()
-            }
         mask //= 2
     return [part for i in sorted(blocks) for part in blocks[i]]
 
@@ -404,8 +384,9 @@
 def spread(products):
     col_count, row_count = lax.axis_size("col"), lax.axis_size("row")
     pairs = col_count // row_count
-    return [
-        lax.ppermute(
+    order = sorted(range(col_count), key=lambda j: (-(j % pairs), -j))
+    sent = {
+        j: lax.ppermute(
             products[j],
             ("col", "row"),
             [
@@ -417,19 +398,20 @@
                 for row in range(row_count)
             ],
         )
-        for j in range(col_count)
-    ]
+        for j in order
+    }
+    return [sent[j] for j in range(col_count)]
 
 
 def rotated(vector, cosine, sine):
     return vector * cosine + pltpu.roll(vector, HEAD_DIM // 2, 1) * sine
 
 
-def rope(lengths, first, rows):
+def rope(lengths, rows):
     slot = lax.broadcasted_iota(jnp.int32, (rows, HEAD_DIM), 0)
     length_of = jnp.zeros((rows, HEAD_DIM), jnp.int32)
     for i in range(rows):
-        length_of = jnp.where(slot == i, lengths[first + i], length_of)
+        length_of = jnp.where(slot == i, lengths[i], length_of)
     lane = lax.broadcasted_iota(jnp.int32, (rows, HEAD_DIM), 1)
     half = HEAD_DIM // 2
     step = lax.rem(lane, half).astype(jnp.float32)
@@ -438,20 +420,19 @@
     return jnp.cos(phases), jnp.where(lane < half, -sine, sine), length_of[:, :1]
 
 
-def attend_all(count, first, place, lengths, *refs):
-    blocks, (keys, values, out, scores_of, probs_of) = refs[:count], refs[count:]
+def attend_all(count, parts, place, lengths, *refs):
+    blocks, (keys, values), refs = refs[:count], refs[count : count + 2], refs[count + 2 :]
+    outs, (scores_of, probs_of) = refs[:parts], refs[parts:]
     pairs = keys.shape[2] // HEAD_DIM
-    cache = keys.shape[1]
-    rows = out.shape[0]
-    here = slice(first, first + rows)
+    rows, cache = keys.shape[:2]
     low = place[1] % pairs
     width = GROUP_WIDTH
-    squares = blocks[0][here, width:].astype(jnp.float32)
-    for i in range(pairs, count, pairs):
-        squares = squares + blocks[i][here, width:].astype(jnp.float32)
+    squares = blocks[pairs - 1][:, width:].astype(jnp.float32)
+    for i in range(2 * pairs - 1, count, pairs):
+        squares = squares + blocks[i][:, width:].astype(jnp.float32)
     scale = lax.rsqrt(jnp.sum(squares, axis=1, keepdims=True) / D + EPSILON)
     factor = HEAD_DIM ** (-0.5)
-    cosines, sines, length_of = rope(lengths, first, rows)
+    cosines, sines, length_of = rope(lengths, rows)
     lane = lax.broadcasted_iota(jnp.int32, (SLOTS, SLOTS * cache), 1)
     slot = lax.broadcasted_iota(jnp.int32, (SLOTS, SLOTS * cache), 0)
     position = lane - slot * cache
@@ -459,9 +440,9 @@
     filled = [(position >= 0) & (position < length_of[part]) for part in runs]
     own, new_values, own_probs = [], [], []
     for pair in range(pairs):
-        total = blocks[pair][here, :width].astype(jnp.float32)
+        total = blocks[pair][:, :width].astype(jnp.float32)
         for i in range(pair + pairs, count, pairs):
-            total = total + blocks[i][here, :width].astype(jnp.float32)
+            total = total + blocks[i][:, :width].astype(jnp.float32)
         total = (total * scale).astype(jnp.bfloat16).astype(jnp.float32)
         heads = [total[:, h * HEAD_DIM : (h + 1) * HEAD_DIM] for h in range(GROUP + 2)]
         queries = [
@@ -474,7 +455,7 @@
         lanes = pl.ds(pl.multiple_of((low ^ pair) * HEAD_DIM, HEAD_DIM), HEAD_DIM)
         for run, part in enumerate(runs):
             query = jnp.concatenate([head[part] for head in queries], axis=0)
-            key = keys[first + part.start : first + part.stop, :, lanes].reshape(SLOTS * cache, HEAD_DIM)
+            key = keys[part, :, lanes].reshape(SLOTS * cache, HEAD_DIM)
             scores_of[pair, run] = lax.dot_general(
                 query.astype(jnp.bfloat16),
                 key,
@@ -499,16 +480,20 @@
         lanes = pl.ds(pl.multiple_of((low ^ pair) * HEAD_DIM, HEAD_DIM), HEAD_DIM)
         results = []
         for run, part in enumerate(runs):
-            value = values[first + part.start : first + part.stop, :, lanes].reshape(SLOTS * cache, HEAD_DIM)
+            value = values[part, :, lanes].reshape(SLOTS * cache, HEAD_DIM)
             mixed = jnp.dot(probs_of[pair, run], value, preferred_element_type=jnp.float32)
             own_prob = own_probs[pair * len(runs) + run]
             results.append(
                 mixed.reshape(GROUP, SLOTS, HEAD_DIM) + own_prob * new_values[pair][part][None]
             )
         for head in range(GROUP):
-            joined = jnp.concatenate([result[head] for result in results], axis=0)
             at = pl.multiple_of((low ^ pair) * OUT_WIDTH + head * HEAD_DIM, HEAD_DIM)
-            out[:, pl.ds(at, HEAD_DIM)] = joined.astype(jnp.bfloat16)
+            size = len(results) // parts
+            for i, out in enumerate(outs):
+                joined = jnp.concatenate(
+                    [result[head] for result in results[i * size : (i + 1) * size]], axis=0
+                )
+                out[:, pl.ds(at, HEAD_DIM)] = joined.astype(jnp.bfloat16)
 
 
 def sum_kernel(count, parts, place, hidden, *refs):
@@ -558,27 +543,27 @@
     own_part = lax.dynamic_slice_in_dim(hidden_in, side * half, half, 1)
     gain = norm_gain.reshape(1, depth)
     half_in, half_out = qkv_weight.shape[1] // 2, out_weight.shape[1] // 2
-    *weights_in, token = call(
+    weights_in = call(
         stage_in_kernel,
-        [pltpu.VMEM((half, half_in), jnp.bfloat16)] * 2 + [struct((8, 128), jnp.float32)],
+        [pltpu.VMEM((half, half_in), jnp.bfloat16)] * 2,
         [SMEM, HBM, HBM],
-        [VMEM] * 3,
+        [VMEM] * 2,
         0,
         half * half_in * 4,
         [pltpu.SemaphoreType.DMA((2,))],
     )(place, in_hbm(qkv_weight), gain)
     blocks = gathered(
-        [own_part[i * piece : (i + 1) * piece] for i in range(parts)], "col", token
-    )
-    *weights_out, key_part, value_part = call(
-        stage_rest_kernel,
-        [pltpu.VMEM((half, half_out), jnp.bfloat16)] * 2
+        [own_part[i * piece : (i + 1) * piece] for i in range(parts)], "col"
+    )
+    out_give, key_part, value_part = call(
+        functools.partial(stage_out_kernel, True),
+        [pltpu.VMEM((half, half_out), jnp.bfloat16)]
         + [pltpu.VMEM((rows, cache, pairs * HEAD_DIM), jnp.bfloat16)] * 2,
         [SMEM, HBM, HBM, HBM],
-        [VMEM] * 4,
+        [VMEM] * 3,
         0,
-        half * half_out * 4 + 4 * rows * cache * pairs * HEAD_DIM,
-        [pltpu.SemaphoreType.DMA((4 * pairs,))],
+        half * half_out * 2 + 4 * rows * cache * pairs * HEAD_DIM,
+        [pltpu.SemaphoreType.DMA((3 * pairs,))],
     )(place, in_hbm(out_weight), in_hbm(key_cache), in_hbm(value_cache))
 
     products = spread(
@@ -586,23 +571,36 @@
     )
 
     key_part, value_part = in_vmem(key_part), in_vmem(value_part)
-    runs = (pairs, piece // SLOTS, GROUP * SLOTS, SLOTS * cache)
-    attended = [
-        call(
-            functools.partial(attend_all, col_count, first),
-            struct((piece, half)),
-            [SMEM, SMEM] + [VMEM] * (col_count + 2),
-            VMEM,
-            4 * piece * half * cache,
-            0,
-            [pltpu.VMEM(runs, jnp.float32), pltpu.VMEM(runs, jnp.bfloat16)],
-        )(place, cache_lengths, *products, key_part, value_part)
-        for first in range(0, rows, piece)
-    ]
-
+    runs = (pairs, rows // SLOTS, GROUP * SLOTS, SLOTS * cache)
+    attended = call(
+        functools.partial(attend_all, col_count, parts),
+        [struct((piece, half))] * parts,
+        [SMEM, SMEM] + [VMEM] * (col_count + 2),
+        [VMEM] * parts,
+        4 * rows * half * cache,
+        0,
+        [pltpu.VMEM(runs, jnp.float32), pltpu.VMEM(runs, jnp.bfloat16)],
+    )(place, cache_lengths, *products, key_part, value_part)
+
+    out_own = call(
+        functools.partial(stage_out_kernel, False),
+        pltpu.VMEM((half, half_out), jnp.bfloat16),
+        [SMEM, HBM, HBM],
+        VMEM,
+        0,
+        half * half_out * 2,
+        [pltpu.SemaphoreType.DMA((pairs,))],
+    )(place, in_hbm(out_weight), attended[-1])
     products = spread(
         project(
-            out_kernel, place, slot_request, gathered(attended, "col"), [], weights_out, 0, pairs
+            out_kernel,
+            place,
+            slot_request,
+            gathered(attended, "col"),
+            [in_vmem(out_own)],
+            [out_give, out_own],
+            0,
+            pairs,
         )
     )
     keep, send = call(

time: 71.1 us -> 70.8 us (level)
  waiting for transfers between devices: 16.5 us -> 13.9 us
  starting transfers between devices: 32.7 us -> 34.6 us
    ppermute x8, starting transfers between devices: 14.7 us -> 19.2 us  [spread(): lax.ppermute(products[j], ('col', 'row'), [(col * row_count + row, (row *...]
    ppermute x15, waiting for transfers between devices: 10.5 us -> 7.91 us  [moved(): return lax.ppermute(value, axis, pairs)]
    ppermute x15, starting transfers between devices: 18 us -> 15.5 us  [moved(): return lax.ppermute(value, axis, pairs)]
    pallas_call x8 -> x6, Pallas kernels: 12.8 us -> 13.3 us  [the longest x1 4.62 us: paired_plan(): call(stage_in_kernel, [pltpu.VMEM((half, half_in), jnp.bfloat16)] * 2, [S...]
  transfers between devices with their start and end apart: 23 -> 23, of which waited for: 12 -> 10; matrix products, arithmetic and copies ran while one was open for 1% -> 1% of each run, Pallas kernels for 18% -> 18%
where the time goes in v6:
time: 70.8 us; the launch traced here: 70.6 us
  starting transfers between devices  34.6 us (49%)
  Pallas kernels  20.1 us (28%)
  waiting for transfers between devices  13.9 us (20%)
  local copies, waits for them, and re-layouts  1.6 us (2%)
    ppermute x8, starting transfers between devices, spread(): lax.ppermute(products[j], ('col', 'row'), [(col * row_count + row, (row *...  19.2 us
    ppermute x15, starting transfers between devices, moved(): return lax.ppermute(value, axis, pairs)  15.5 us
    ppermute x15, waiting for transfers between devices, moved(): return lax.ppermute(value, axis, pairs)  7.91 us
    ppermute x8, waiting for transfers between devices, spread(): lax.ppermute(products[j], ('col', 'row'), [(col * row_count + row, (row *...  6 us
    pallas_call x1, Pallas kernels, paired_plan(): call(stage_in_kernel, [pltpu.VMEM((half, half_in), jnp.bfloat16)] * 2, [S...  4.62 us
    pallas_call x1, Pallas kernels, paired_plan(): call(functools.partial(stage_out_kernel, True), [pltpu.VMEM((half, half_o...  3.54 us
    pallas_call x2, Pallas kernels, project(): call(functools.partial(kernel, parts, count), [struct((rows, half + more)...  3.26 us
    pallas_call x1, Pallas kernels, paired_plan(): call(functools.partial(stage_out_kernel, False), pltpu.VMEM((half, half_o...  2.78 us
  transfers between devices with their start and end apart: 23, of which 10 were waited for; matrix products, arithmetic and copies ran while one was open for 1% of the time, Pallas kernels for 18%

profile of v6, /device:TPU:0, one launch (start us, length us, event | category | flops | bytes accessed | tf_op | source)
XLA Modules:
  0.0 70.6 jit_solution(16779781288129467340)
XLA Ops:
  0.0 0.9 %fusion = (bf16[16,2048]{1,0:T(8,128)(2,1)S(1)}, bf16[16,2048]{1,0:T(8,128)(2,1)S(1)}) fusion(bf16[32,4096]{1,0:T(8,128)(2,1)} %hidden.1, s32[]{:T(128)S(6)} %add.10, s32[]{:T(128)S(6)} %select_n.3), kind=kLoop, calls=%fused_computation.2 | loop fusion | bytes 262152 | tf_op jit(solution)/shard_map/slice | solution.py:556
  0.9 4.1 %collective-permute-start.2 = (bf16[16,2048]{1,0:T(8,128)(2,1)S(1)}, bf16[16,2048]{1,0:T(8,128)(2,1)S(1)}, u32[]{:S(2)}, u32[]{:S(2)}) collective-permute-start(bf16[16,2048]{1,0:T(8,128)(2,1)S(1)} %get-tuple-element.48.refs_0_), channel_id=1, source_target_pairs={{0,8},{4,12},{8,0},{12,4},{1,9},{5,13},{9,1},{13,5},{2,10},{6,14},... | collective-permute-start | bytes 196616 | tf_op jit(solution)/shard_map/ppermute | solution.py:206
  5.0 0.1 collective-permute-start.3
  5.1 1.8 %collective-permute-start = (bf16[16,2048]{1,0:T(8,128)(2,1)S(1)}, bf16[16,2048]{1,0:T(8,128)(2,1)S(1)}, u32[]{:S(2)}, u32[]{:S(2)}) collective-permute-start(bf16[16,2048]{1,0:T(8,128)(2,1)S(1)} %get-tuple-element.48.refs_0_), channel_id=1, source_target_pairs={{0,4},{4,0},{8,12},{12,8},{1,5},{5,1},{9,13},{13,9},{2,6},{6,2},{1... | collective-permute-start | bytes 196616 | tf_op jit(solution)/shard_map/ppermute | solution.py:206
  6.9 0.2 collective-permute-start.1
  7.1 0.7 %reshape.3.gain.refs_8_ = bf16[1,4096]{1,0:T(2,128)(2,1)S(1)} reshape(bf16[4096]{0:T(1024)(128)(2,1)} %param.9) | data formatting | bytes 16384 | tf_op jit(solution)/shard_map/reshape | solution.py:544
  7.8 0.9 %collective-permute-done.2.refs_4_ = bf16[16,2048]{1,0:T(8,128)(2,1)S(1)} collective-permute-done((bf16[16,2048]{1,0:T(8,128)(2,1)S(1)}, bf16[16,2048]{1,0:T(8,128)(2,1)S(1)}, u32[]{:S(2)}, u32[]{:S(2)}) %collective-permute-start.2) | collective-permute-done | bytes 65568 | tf_op jit(solution)/shard_map/ppermute | solution.py:206
  8.7 1.9 %collective-permute-start.4 = (bf16[16,2048]{1,0:T(8,128)(2,1)S(1)}, bf16[16,2048]{1,0:T(8,128)(2,1)S(1)}, u32[]{:S(2)}, u32[]{:S(2)}) collective-permute-start(bf16[16,2048]{1,0:T(8,128)(2,1)S(1)} %collective-permute-done.2.refs_4_), channel_id=1, source_target_pairs={{0,4},{4,0},{8,12},{12,8},{1,5},{5,1},{9,13},{13,9},{2,6},{6,2},{1... | collective-permute-start | bytes 196616 | tf_op jit(solution)/shard_map/ppermute | solution.py:206
  10.6 0.4 collective-permute-done.3.refs_5_
  11.1 1.3 %collective-permute-start.5 = (bf16[16,2048]{1,0:T(8,128)(2,1)S(1)}, bf16[16,2048]{1,0:T(8,128)(2,1)S(1)}, u32[]{:S(2)}, u32[]{:S(2)}) collective-permute-start(bf16[16,2048]{1,0:T(8,128)(2,1)S(1)} %collective-permute-done.3.refs_5_), channel_id=1, source_target_pairs={{0,4},{4,0},{8,12},{12,8},{1,5},{5,1},{9,13},{13,9},{2,6},{6,2},{1... | collective-permute-start | bytes 196616 | tf_op jit(solution)/shard_map/ppermute | solution.py:206
  12.4 0.1 pad_add_fusion.place
  12.5 4.6 %shard_map.82 = (bf16[2048,1280]{1,0:T(8,128)(2,1)S(1)}, bf16[2048,1280]{1,0:T(8,128)(2,1)S(1)}) custom-call(s32[3]{0:T(128)S(1)} %pad_add_fusion.place, bf16[4096,2560]{1,0:T(8,128)(2,1)} %weight.3, bf16[1,4096]{1,0:T(2,128)(2,1)S(1)} %reshape.3.gain.refs_8_), custom_call_target="tpu_custom_call" | custom-call | bytes 10485760 | tf_op jit(solution)/shard_map/pallas_call | solution.py:546
  17.1 0.0 collective-permute-done.1.refs_3_
  17.1 1.7 %shard_map.83 = (bf16[128,1408]{1,0:T(8,128)(2,1)S(1)}, bf16[128,2048]{1,0:T(8,128)(2,1)S(1)}) custom-call(s32[3]{0:T(128)S(1)} %pad_add_fusion.place, s32[128]{0:T(128)S(1)} %copy-done.1, bf16[16,2048]{1,0:T(8,128)(2,1)S(1)} %get-tuple-element.48.refs_0_, bf16[16,2048]{1,0:T(8,128)(2,1)S(1)} %get-tuple-element.47.refs_1_, ...), custom_call_target="tpu_custom_call" | custom-call | flops 671088640 | bytes 5242880 | tf_op jit(solution)/shard_map/pallas_call | solution.py:341
  18.9 0.1 collective-permute-start.6
  19.0 0.9 %shard_map.84.own = f32[128,1280]{1,0:T(8,128)S(1)} custom-call(bf16[128,2048]{1,0:T(8,128)(2,1)S(1)} %get-tuple-element.27.permuted, bf16[2048,1280]{1,0:T(8,128)(2,1)S(1)} %get-tuple-element.28.weight), custom_call_target="tpu_custom_call" | custom-call | flops 671088640 | bytes 5242880 | tf_op jit(solution)/shard_map/pallas_call | solution.py:351
  19.8 0.8 %collective-permute-done.6.received = bf16[128,1408]{1,0:T(8,128)(2,1)S(1)} collective-permute-done((bf16[128,1408]{1,0:T(8,128)(2,1)S(1)}, bf16[128,1408]{1,0:T(8,128)(2,1)S(1)}, u32[]{:S(2)}, u32[]{:S(2)}) %collective-permute-start.6) | collective-permute-done | bytes 360480 | tf_op jit(solution)/shard_map/ppermute | solution.py:206
  20.6 0.1 shard_map.85
  20.7 3.3 %collective-permute-start.10 = (bf16[32,1408]{1,0:T(8,128)(2,1)S(1)}, bf16[32,1408]{1,0:T(8,128)(2,1)S(1)}, u32[]{:S(2)}, u32[]{:S(2)}) collective-permute-start(bf16[32,1408]{1,0:T(8,128)(2,1)S(1)} %get-tuple-element.33), channel_id=1, source_target_pairs={{0,12},{2,4},{4,8},{6,0},{8,14},{10,6},{12,10},{14,2},{1,13},{3,5}... | collective-permute-start | bytes 270344 | tf_op jit(solution)/shard_map/ppermute | solution.py:389
  24.0 0.4 collective-permute-start.8
  24.4 0.7 collective-permute-start.7
  25.1 0.0 copy-start.2
  25.1 6.9 %collective-permute-start.9 = (bf16[32,1280]{1,0:T(8,128)(2,1)S(1)}, bf16[32,1280]{1,0:T(8,128)(2,1)S(1)}, u32[]{:S(2)}, u32[]{:S(2)}) collective-permute-start(bf16[32,1280]{1,0:T(8,128)(2,1)S(1)} %get-tuple-element.32), channel_id=1, source_target_pairs={{0,8},{2,0},{4,12},{6,4},{8,10},{10,2},{12,14},{14,6},{1,9},{3,1},... | collective-permute-start | bytes 245768 | tf_op jit(solution)/shard_map/ppermute | solution.py:389
  32.0 3.5 %shard_map.86 = (bf16[2048,1024]{1,0:T(8,128)(2,1)S(1)}, bf16[32,64,256]{2,1,0:T(8,128)(2,1)S(1)}, bf16[32,64,256]{2,1,0:T(8,128)(2,1)S(1)}) custom-call(s32[3]{0:T(128)S(1)} %pad_add_fusion.place, bf16[4096,2048]{1,0:T(8,128)(2,1)} %weight.5, bf16[32,64,512]{2,1,0:T(8,128)(2,1)} %refs_0_.1, bf16[32,64,512]{2,1,0:T(8,128)(2,1)} %refs_1_.1), custom_call_target="tpu_custom_call" | custom-call | bytes 6291456 | tf_op jit(solution)/shard_map/pallas_call | solution.py:558
  35.6 2.3 %shard_map.87 = (bf16[16,2048]{1,0:T(8,128)(2,1)S(1)}, bf16[16,2048]{1,0:T(8,128)(2,1)S(1)}) custom-call(s32[3]{0:T(128)S(1)} %pad_add_fusion.place, s32[32]{0:T(128)S(1)} %copy-done.2, bf16[32,1280]{1,0:T(8,128)(2,1)S(1)} %collective-permute-done.7.refs_0_, bf16[32,1408]{1,0:T(8,128)(2,1)S(1)} %collective-permute-done.8.refs_1_, ...), custom_call_target="tpu_custom_call" | custom-call | flops 16777216 | tf_op jit(solution)/shard_map/pallas_call | solution.py:575
  37.9 1.9 %collective-permute-start.13 = (bf16[16,2048]{1,0:T(8,128)(2,1)S(1)}, bf16[16,2048]{1,0:T(8,128)(2,1)S(1)}, u32[]{:S(2)}, u32[]{:S(2)}) collective-permute-start(bf16[16,2048]{1,0:T(8,128)(2,1)S(1)} %get-tuple-element.36.refs_0_), channel_id=1, source_target_pairs={{0,8},{4,12},{8,0},{12,4},{1,9},{5,13},{9,1},{13,5},{2,10},{6,14},... | collective-permute-start | bytes 196616 | tf_op jit(solution)/shard_map/ppermute | solution.py:206
  39.8 1.1 %collective-permute-start.14 = (bf16[16,2048]{1,0:T(8,128)(2,1)S(1)}, bf16[16,2048]{1,0:T(8,128)(2,1)S(1)}, u32[]{:S(2)}, u32[]{:S(2)}) collective-permute-start(bf16[16,2048]{1,0:T(8,128)(2,1)S(1)} %get-tuple-element.37.refs_0_.refs_1_), channel_id=1, source_target_pairs={{0,8},{4,12},{8,0},{12,4},{1,9},{5,13},{9,1},{13,5},{2,10},{6,14},... | collective-permute-start | bytes 196616 | tf_op jit(solution)/shard_map/ppermute | solution.py:206
  40.9 2.0 %collective-permute-start.12 = (bf16[16,2048]{1,0:T(8,128)(2,1)S(1)}, bf16[16,2048]{1,0:T(8,128)(2,1)S(1)}, u32[]{:S(2)}, u32[]{:S(2)}) collective-permute-start(bf16[16,2048]{1,0:T(8,128)(2,1)S(1)} %get-tuple-element.37.refs_0_.refs_1_), channel_id=1, source_target_pairs={{0,4},{4,0},{8,12},{12,8},{1,5},{5,1},{9,13},{13,9},{2,6},{6,2},{1... | collective-permute-start | bytes 196616 | tf_op jit(solution)/shard_map/ppermute | solution.py:206
  42.9 1.8 %collective-permute-done.13.refs_4_ = bf16[16,2048]{1,0:T(8,128)(2,1)S(1)} collective-permute-done((bf16[16,2048]{1,0:T(8,128)(2,1)S(1)}, bf16[16,2048]{1,0:T(8,128)(2,1)S(1)}, u32[]{:S(2)}, u32[]{:S(2)}) %collective-permute-start.13) | collective-permute-done | bytes 65568 | tf_op jit(solution)/shard_map/ppermute | solution.py:206
  44.8 1.2 %collective-permute-done.14.refs_5_ = bf16[16,2048]{1,0:T(8,128)(2,1)S(1)} collective-permute-done((bf16[16,2048]{1,0:T(8,128)(2,1)S(1)}, bf16[16,2048]{1,0:T(8,128)(2,1)S(1)}, u32[]{:S(2)}, u32[]{:S(2)}) %collective-permute-start.14) | collective-permute-done | bytes 65568 | tf_op jit(solution)/shard_map/ppermute | solution.py:206
  46.0 0.8 %collective-permute-start.16 = (bf16[16,2048]{1,0:T(8,128)(2,1)S(1)}, bf16[16,2048]{1,0:T(8,128)(2,1)S(1)}, u32[]{:S(2)}, u32[]{:S(2)}) collective-permute-start(bf16[16,2048]{1,0:T(8,128)(2,1)S(1)} %collective-permute-done.14.refs_5_), channel_id=1, source_target_pairs={{0,4},{4,0},{8,12},{12,8},{1,5},{5,1},{9,13},{13,9},{2,6},{6,2},{1... | collective-permute-start | bytes 196616 | tf_op jit(solution)/shard_map/ppermute | solution.py:206
  46.8 2.8 %shard_map.88.refs_8_.weight = bf16[2048,1024]{1,0:T(8,128)(2,1)S(1)} custom-call(s32[3]{0:T(128)S(1)} %pad_add_fusion.place, bf16[4096,2048]{1,0:T(8,128)(2,1)} %weight.5, bf16[16,2048]{1,0:T(8,128)(2,1)S(1)} %get-tuple-element.37.refs_0_.refs_1_), custom_call_target="tpu_custom_call" | custom-call | bytes 4194304 | tf_op jit(solution)/shard_map/pallas_call | solution.py:585
  49.6 0.6 collective-permute-done.16.refs_7_
  50.2 1.5 %shard_map.89 = (bf16[128,1024]{1,0:T(8,128)(2,1)S(1)}, bf16[128,2048]{1,0:T(8,128)(2,1)S(1)}) custom-call(s32[3]{0:T(128)S(1)} %pad_add_fusion.place, s32[128]{0:T(128)S(1)} %copy-done.1, bf16[16,2048]{1,0:T(8,128)(2,1)S(1)} %get-tuple-element.36.refs_0_, bf16[16,2048]{1,0:T(8,128)(2,1)S(1)} %get-tuple-element.37.refs_0_.refs_1_, ...), custom_call_target="tpu_custom_call" | custom-call | flops 536870912 | bytes 4194304 | tf_op jit(solution)/shard_map/pallas_call | solution.py:341
  51.8 0.0 copy-start
  51.8 0.1 collective-permute-start.17
  51.9 0.7 %shard_map.90.own = f32[128,1024]{1,0:T(8,128)S(1)} custom-call(bf16[128,2048]{1,0:T(8,128)(2,1)S(1)} %get-tuple-element.39.permuted, bf16[2048,1024]{1,0:T(8,128)(2,1)S(1)} %shard_map.88.refs_8_.weight), custom_call_target="tpu_custom_call" | custom-call | flops 536870912 | bytes 4194304 | tf_op jit(solution)/shard_map/pallas_call | solution.py:351
  52.6 0.8 %collective-permute-done.17.received = bf16[128,1024]{1,0:T(8,128)(2,1)S(1)} collective-permute-done((bf16[128,1024]{1,0:T(8,128)(2,1)S(1)}, bf16[128,1024]{1,0:T(8,128)(2,1)S(1)}, u32[]{:S(2)}, u32[]{:S(2)}) %collective-permute-start.17) | collective-permute-done | bytes 262176 | tf_op jit(solution)/shard_map/ppermute | solution.py:206
  53.4 0.7 collective-permute-start.18
  54.1 0.9 %collective-permute-start.19 = (bf16[32,1024]{1,0:T(8,128)(2,1)S(1)}, bf16[32,1024]{1,0:T(8,128)(2,1)S(1)}, u32[]{:S(2)}, u32[]{:S(2)}) collective-permute-start(bf16[32,1024]{1,0:T(8,128)(2,1)S(1)} %get-tuple-element.42), channel_id=1, source_target_pairs={{0,4},{2,12},{4,0},{6,8},{8,6},{10,14},{12,2},{14,10},{1,5},{3,13}... | collective-permute-start | bytes 196616 | tf_op jit(solution)/shard_map/ppermute | solution.py:389
  55.0 5.3 %collective-permute-start.20 = (bf16[32,1024]{1,0:T(8,128)(2,1)S(1)}, bf16[32,1024]{1,0:T(8,128)(2,1)S(1)}, u32[]{:S(2)}, u32[]{:S(2)}) collective-permute-start(bf16[32,1024]{1,0:T(8,128)(2,1)S(1)} %get-tuple-element.43), channel_id=1, source_target_pairs={{0,8},{2,0},{4,12},{6,4},{8,10},{10,2},{12,14},{14,6},{1,9},{3,1},... | collective-permute-start | bytes 196616 | tf_op jit(solution)/shard_map/ppermute | solution.py:389
  60.3 1.0 %collective-permute-start.21 = (bf16[32,1024]{1,0:T(8,128)(2,1)S(1)}, bf16[32,1024]{1,0:T(8,128)(2,1)S(1)}, u32[]{:S(2)}, u32[]{:S(2)}) collective-permute-start(bf16[32,1024]{1,0:T(8,128)(2,1)S(1)} %get-tuple-element.44), channel_id=1, source_target_pairs={{0,12},{2,4},{4,8},{6,0},{8,14},{10,6},{12,10},{14,2},{1,13},{3,5}... | collective-permute-start | bytes 196616 | tf_op jit(solution)/shard_map/ppermute | solution.py:389
  61.3 1.1 %collective-permute-done.20.refs_4_ = bf16[32,1024]{1,0:T(8,128)(2,1)S(1)} collective-permute-done((bf16[32,1024]{1,0:T(8,128)(2,1)S(1)}, bf16[32,1024]{1,0:T(8,128)(2,1)S(1)}, u32[]{:S(2)}, u32[]{:S(2)}) %collective-permute-start.20) | collective-permute-done | bytes 65568 | tf_op jit(solution)/shard_map/ppermute | solution.py:389
  62.4 4.9 %collective-permute-done.21.refs_5_ = bf16[32,1024]{1,0:T(8,128)(2,1)S(1)} collective-permute-done((bf16[32,1024]{1,0:T(8,128)(2,1)S(1)}, bf16[32,1024]{1,0:T(8,128)(2,1)S(1)}, u32[]{:S(2)}, u32[]{:S(2)}) %collective-permute-start.21) | collective-permute-done | bytes 65568 | tf_op jit(solution)/shard_map/ppermute | solution.py:389
  67.3 0.6 shard_map.92
  67.9 0.1 collective-permute-start.22
  68.0 1.3 %collective-permute-done.22.received = bf16[32,2048]{1,0:T(8,128)(2,1)S(1)} collective-permute-done((bf16[32,2048]{1,0:T(8,128)(2,1)S(1)}, bf16[32,2048]{1,0:T(8,128)(2,1)S(1)}, u32[]{:S(2)}, u32[]{:S(2)}) %collective-permute-start.22) | collective-permute-done | bytes 131104 | tf_op jit(solution)/shard_map/ppermute | solution.py:206
  69.3 1.3 %shard_map.93 = bf16[1,32,4096]{2,1,0:T(8,128)(2,1)} custom-call(s32[3]{0:T(128)S(1)} %pad_add_fusion.place, bf16[32,2048]{1,0:T(8,128)(2,1)S(1)} %get-tuple-element.45.keep, bf16[32,2048]{1,0:T(8,128)(2,1)S(1)} %collective-permute-done.22.received), custom_call_target="tpu_custom_call" | custom-call | bytes 524288 | tf_op jit(solution)/shard_map/pallas_call | solution.py:614
  (19 shorter events, 0.1 us)
Async XLA Ops:
  0.9 7.9 %collective-permute-start.2 = (bf16[16,2048]{1,0:T(8,128)(2,1)S(1)}, bf16[16,2048]{1,0:T(8,128)(2,1)S(1)}, u32[]{:S(2)}, u32[]{:S(2)}) collective-permute-start(bf16[16,2048]{1,0:T(8,128)(2,1)S(1)} %get-tuple-element.48.refs_0_), channel_id=1, source_target_pairs={{0,8},{4,12},{8,0},{12,4},{1,9},{5,13},{9,1},{13,5},{2,10},{6,14},... | collective-permute-start | bytes 196616 | tf_op jit(solution)/shard_map/ppermute | solution.py:206
  5.0 6.1 %collective-permute-start.3 = (bf16[16,2048]{1,0:T(8,128)(2,1)S(1)}, bf16[16,2048]{1,0:T(8,128)(2,1)S(1)}, u32[]{:S(2)}, u32[]{:S(2)}) collective-permute-start(bf16[16,2048]{1,0:T(8,128)(2,1)S(1)} %get-tuple-element.47.refs_1_), channel_id=1, source_target_pairs={{0,8},{4,12},{8,0},{12,4},{1,9},{5,13},{9,1},{13,5},{2,10},{6,14},... | collective-permute-start | bytes 196616 | tf_op jit(solution)/shard_map/ppermute | solution.py:206
  5.1 12.0 %collective-permute-start = (bf16[16,2048]{1,0:T(8,128)(2,1)S(1)}, bf16[16,2048]{1,0:T(8,128)(2,1)S(1)}, u32[]{:S(2)}, u32[]{:S(2)}) collective-permute-start(bf16[16,2048]{1,0:T(8,128)(2,1)S(1)} %get-tuple-element.48.refs_0_), channel_id=1, source_target_pairs={{0,4},{4,0},{8,12},{12,8},{1,5},{5,1},{9,13},{13,9},{2,6},{6,2},{1... | collective-permute-start | bytes 196616 | tf_op jit(solution)/shard_map/ppermute | solution.py:206
  6.9 10.2 %collective-permute-start.1 = (bf16[16,2048]{1,0:T(8,128)(2,1)S(1)}, bf16[16,2048]{1,0:T(8,128)(2,1)S(1)}, u32[]{:S(2)}, u32[]{:S(2)}) collective-permute-start(bf16[16,2048]{1,0:T(8,128)(2,1)S(1)} %get-tuple-element.47.refs_1_), channel_id=1, source_target_pairs={{0,4},{4,0},{8,12},{12,8},{1,5},{5,1},{9,13},{13,9},{2,6},{6,2},{1... | collective-permute-start | bytes 196616 | tf_op jit(solution)/shard_map/ppermute | solution.py:206
  8.7 8.4 %collective-permute-start.4 = (bf16[16,2048]{1,0:T(8,128)(2,1)S(1)}, bf16[16,2048]{1,0:T(8,128)(2,1)S(1)}, u32[]{:S(2)}, u32[]{:S(2)}) collective-permute-start(bf16[16,2048]{1,0:T(8,128)(2,1)S(1)} %collective-permute-done.2.refs_4_), channel_id=1, source_target_pairs={{0,4},{4,0},{8,12},{12,8},{1,5},{5,1},{9,13},{13,9},{2,6},{6,2},{1... | collective-permute-start | bytes 196616 | tf_op jit(solution)/shard_map/ppermute | solution.py:206
  11.1 6.0 %collective-permute-start.5 = (bf16[16,2048]{1,0:T(8,128)(2,1)S(1)}, bf16[16,2048]{1,0:T(8,128)(2,1)S(1)}, u32[]{:S(2)}, u32[]{:S(2)}) collective-permute-start(bf16[16,2048]{1,0:T(8,128)(2,1)S(1)} %collective-permute-done.3.refs_5_), channel_id=1, source_target_pairs={{0,4},{4,0},{8,12},{12,8},{1,5},{5,1},{9,13},{13,9},{2,6},{6,2},{1... | collective-permute-start | bytes 196616 | tf_op jit(solution)/shard_map/ppermute | solution.py:206
  12.5 4.7 %copy-start.1 = (s32[128]{0:T(128)S(1)}, s32[128]{0:T(128)}, u32[]{:S(2)}) copy-start(s32[128]{0:T(128)} %slots.3) | copy-start | bytes 1540
  18.9 1.7 %collective-permute-start.6 = (bf16[128,1408]{1,0:T(8,128)(2,1)S(1)}, bf16[128,1408]{1,0:T(8,128)(2,1)S(1)}, u32[]{:S(2)}, u32[]{:S(2)}) collective-permute-start(bf16[128,1408]{1,0:T(8,128)(2,1)S(1)} %get-tuple-element.29.given), channel_id=1, source_target_pairs={{0,1},{1,0},{2,3},{3,2},{4,5},{5,4},{6,7},{7,6},{8,9},{9,8},{10,11... | collective-permute-start | bytes 1081352 | tf_op jit(solution)/shard_map/ppermute | solution.py:206
  20.7 14.9 %collective-permute-start.10 = (bf16[32,1408]{1,0:T(8,128)(2,1)S(1)}, bf16[32,1408]{1,0:T(8,128)(2,1)S(1)}, u32[]{:S(2)}, u32[]{:S(2)}) collective-permute-start(bf16[32,1408]{1,0:T(8,128)(2,1)S(1)} %get-tuple-element.33), channel_id=1, source_target_pairs={{0,12},{2,4},{4,8},{6,0},{8,14},{10,6},{12,10},{14,2},{1,13},{3,5}... | collective-permute-start | bytes 270344 | tf_op jit(solution)/shard_map/ppermute | solution.py:389
  24.0 11.6 %collective-permute-start.8 = (bf16[32,1408]{1,0:T(8,128)(2,1)S(1)}, bf16[32,1408]{1,0:T(8,128)(2,1)S(1)}, u32[]{:S(2)}, u32[]{:S(2)}) collective-permute-start(bf16[32,1408]{1,0:T(8,128)(2,1)S(1)} %get-tuple-element.31), channel_id=1, source_target_pairs={{0,4},{2,12},{4,0},{6,8},{8,6},{10,14},{12,2},{14,10},{1,5},{3,13}... | collective-permute-start | bytes 270344 | tf_op jit(solution)/shard_map/ppermute | solution.py:389
  24.4 11.2 %collective-permute-start.7 = (bf16[32,1280]{1,0:T(8,128)(2,1)S(1)}, bf16[32,1280]{1,0:T(8,128)(2,1)S(1)}, u32[]{:S(2)}, u32[]{:S(2)}) collective-permute-start(bf16[32,1280]{1,0:T(8,128)(2,1)S(1)} %get-tuple-element.30), channel_id=1, source_target_pairs={{0,0},{2,8},{4,4},{6,12},{8,2},{10,10},{12,6},{14,14},{1,1},{3,9},... | collective-permute-start | bytes 245768 | tf_op jit(solution)/shard_map/ppermute | solution.py:389
  25.1 10.6 %copy-start.2 = (s32[32]{0:T(128)S(1)}, s32[32]{0:T(128)}, u32[]{:S(2)}) copy-start(s32[32]{0:T(128)} %lengths.1) | copy-start | bytes 388
  25.1 10.5 %collective-permute-start.9 = (bf16[32,1280]{1,0:T(8,128)(2,1)S(1)}, bf16[32,1280]{1,0:T(8,128)(2,1)S(1)}, u32[]{:S(2)}, u32[]{:S(2)}) collective-permute-start(bf16[32,1280]{1,0:T(8,128)(2,1)S(1)} %get-tuple-element.32), channel_id=1, source_target_pairs={{0,8},{2,0},{4,12},{6,4},{8,10},{10,2},{12,14},{14,6},{1,9},{3,1},... | collective-permute-start | bytes 245768 | tf_op jit(solution)/shard_map/ppermute | solution.py:389
  37.9 6.8 %collective-permute-start.13 = (bf16[16,2048]{1,0:T(8,128)(2,1)S(1)}, bf16[16,2048]{1,0:T(8,128)(2,1)S(1)}, u32[]{:S(2)}, u32[]{:S(2)}) collective-permute-start(bf16[16,2048]{1,0:T(8,128)(2,1)S(1)} %get-tuple-element.36.refs_0_), channel_id=1, source_target_pairs={{0,8},{4,12},{8,0},{12,4},{1,9},{5,13},{9,1},{13,5},{2,10},{6,14},... | collective-permute-start | bytes 196616 | tf_op jit(solution)/shard_map/ppermute | solution.py:206
  39.8 6.2 %collective-permute-start.14 = (bf16[16,2048]{1,0:T(8,128)(2,1)S(1)}, bf16[16,2048]{1,0:T(8,128)(2,1)S(1)}, u32[]{:S(2)}, u32[]{:S(2)}) collective-permute-start(bf16[16,2048]{1,0:T(8,128)(2,1)S(1)} %get-tuple-element.37.refs_0_.refs_1_), channel_id=1, source_target_pairs={{0,8},{4,12},{8,0},{12,4},{1,9},{5,13},{9,1},{13,5},{2,10},{6,14},... | collective-permute-start | bytes 196616 | tf_op jit(solution)/shard_map/ppermute | solution.py:206
  40.9 8.7 %collective-permute-start.11 = (bf16[16,2048]{1,0:T(8,128)(2,1)S(1)}, bf16[16,2048]{1,0:T(8,128)(2,1)S(1)}, u32[]{:S(2)}, u32[]{:S(2)}) collective-permute-start(bf16[16,2048]{1,0:T(8,128)(2,1)S(1)} %get-tuple-element.36.refs_0_), channel_id=1, source_target_pairs={{0,4},{4,0},{8,12},{12,8},{1,5},{5,1},{9,13},{13,9},{2,6},{6,2},{1... | collective-permute-start | bytes 196616 | tf_op jit(solution)/shard_map/ppermute | solution.py:206
  40.9 8.7 %collective-permute-start.12 = (bf16[16,2048]{1,0:T(8,128)(2,1)S(1)}, bf16[16,2048]{1,0:T(8,128)(2,1)S(1)}, u32[]{:S(2)}, u32[]{:S(2)}) collective-permute-start(bf16[16,2048]{1,0:T(8,128)(2,1)S(1)} %get-tuple-element.37.refs_0_.refs_1_), channel_id=1, source_target_pairs={{0,4},{4,0},{8,12},{12,8},{1,5},{5,1},{9,13},{13,9},{2,6},{6,2},{1... | collective-permute-start | bytes 196616 | tf_op jit(solution)/shard_map/ppermute | solution.py:206
  44.8 4.8 %collective-permute-start.15 = (bf16[16,2048]{1,0:T(8,128)(2,1)S(1)}, bf16[16,2048]{1,0:T(8,128)(2,1)S(1)}, u32[]{:S(2)}, u32[]{:S(2)}) collective-permute-start(bf16[16,2048]{1,0:T(8,128)(2,1)S(1)} %collective-permute-done.13.refs_4_), channel_id=1, source_target_pairs={{0,4},{4,0},{8,12},{12,8},{1,5},{5,1},{9,13},{13,9},{2,6},{6,2},{1... | collective-permute-start | bytes 196616 | tf_op jit(solution)/shard_map/ppermute | solution.py:206
  46.0 4.3 %collective-permute-start.16 = (bf16[16,2048]{1,0:T(8,128)(2,1)S(1)}, bf16[16,2048]{1,0:T(8,128)(2,1)S(1)}, u32[]{:S(2)}, u32[]{:S(2)}) collective-permute-start(bf16[16,2048]{1,0:T(8,128)(2,1)S(1)} %collective-permute-done.14.refs_5_), channel_id=1, source_target_pairs={{0,4},{4,0},{8,12},{12,8},{1,5},{5,1},{9,13},{13,9},{2,6},{6,2},{1... | collective-permute-start | bytes 196616 | tf_op jit(solution)/shard_map/ppermute | solution.py:206
  51.8 15.5 %copy-start = (bf16[32,4096]{1,0:T(8,128)(2,1)S(1)}, bf16[32,4096]{1,0:T(8,128)(2,1)}, u32[]{:S(2)}) copy-start(bf16[32,4096]{1,0:T(8,128)(2,1)} %hidden.1) | copy-start | bytes 786436
  51.8 1.6 %collective-permute-start.17 = (bf16[128,1024]{1,0:T(8,128)(2,1)S(1)}, bf16[128,1024]{1,0:T(8,128)(2,1)S(1)}, u32[]{:S(2)}, u32[]{:S(2)}) collective-permute-start(bf16[128,1024]{1,0:T(8,128)(2,1)S(1)} %get-tuple-element.40.given), channel_id=1, source_target_pairs={{0,1},{1,0},{2,3},{3,2},{4,5},{5,4},{6,7},{7,6},{8,9},{9,8},{10,11... | collective-permute-start | bytes 786440 | tf_op jit(solution)/shard_map/ppermute | solution.py:206
  53.4 7.9 %collective-permute-start.18 = (bf16[32,1024]{1,0:T(8,128)(2,1)S(1)}, bf16[32,1024]{1,0:T(8,128)(2,1)S(1)}, u32[]{:S(2)}, u32[]{:S(2)}) collective-permute-start(bf16[32,1024]{1,0:T(8,128)(2,1)S(1)} %get-tuple-element.41), channel_id=1, source_target_pairs={{0,0},{2,8},{4,4},{6,12},{8,2},{10,10},{12,6},{14,14},{1,1},{3,9},... | collective-permute-start | bytes 196616 | tf_op jit(solution)/shard_map/ppermute | solution.py:389
  54.1 7.2 %collective-permute-start.19 = (bf16[32,1024]{1,0:T(8,128)(2,1)S(1)}, bf16[32,1024]{1,0:T(8,128)(2,1)S(1)}, u32[]{:S(2)}, u32[]{:S(2)}) collective-permute-start(bf16[32,1024]{1,0:T(8,128)(2,1)S(1)} %get-tuple-element.42), channel_id=1, source_target_pairs={{0,4},{2,12},{4,0},{6,8},{8,6},{10,14},{12,2},{14,10},{1,5},{3,13}... | collective-permute-start | bytes 196616 | tf_op jit(solution)/shard_map/ppermute | solution.py:389
  55.0 7.4 %collective-permute-start.20 = (bf16[32,1024]{1,0:T(8,128)(2,1)S(1)}, bf16[32,1024]{1,0:T(8,128)(2,1)S(1)}, u32[]{:S(2)}, u32[]{:S(2)}) collective-permute-start(bf16[32,1024]{1,0:T(8,128)(2,1)S(1)} %get-tuple-element.43), channel_id=1, source_target_pairs={{0,8},{2,0},{4,12},{6,4},{8,10},{10,2},{12,14},{14,6},{1,9},{3,1},... | collective-permute-start | bytes 196616 | tf_op jit(solution)/shard_map/ppermute | solution.py:389
  60.3 7.0 %collective-permute-start.21 = (bf16[32,1024]{1,0:T(8,128)(2,1)S(1)}, bf16[32,1024]{1,0:T(8,128)(2,1)S(1)}, u32[]{:S(2)}, u32[]{:S(2)}) collective-permute-start(bf16[32,1024]{1,0:T(8,128)(2,1)S(1)} %get-tuple-element.44), channel_id=1, source_target_pairs={{0,12},{2,4},{4,8},{6,0},{8,14},{10,6},{12,10},{14,2},{1,13},{3,5}... | collective-permute-start | bytes 196616 | tf_op jit(solution)/shard_map/ppermute | solution.py:389
  67.9 1.4 %collective-permute-start.22 = (bf16[32,2048]{1,0:T(8,128)(2,1)S(1)}, bf16[32,2048]{1,0:T(8,128)(2,1)S(1)}, u32[]{:S(2)}, u32[]{:S(2)}) collective-permute-start(bf16[32,2048]{1,0:T(8,128)(2,1)S(1)} %get-tuple-element.46), channel_id=1, source_target_pairs={{0,1},{1,0},{2,3},{3,2},{4,5},{5,4},{6,7},{7,6},{8,9},{9,8},{10,11... | collective-permute-start | bytes 393224 | tf_op jit(solution)/shard_map/ppermute | solution.py:206

commit v7 on v6

--- a/solution.py
+++ b/solution.py
@@ -227,17 +227,16 @@
     run_copies(copies, sems)
 
 
-def stage_out_kernel(give, place, weight, *refs):
+def stage_out_kernel(first, place, weight, *refs):
     sems = refs[-1]
-    target = refs[2] if give else refs[1]
+    target = refs[2] if first else refs[1]
     width = target.shape[1]
-    half = 1 - place[0] if give else place[0]
-    columns = pl.ds(pl.multiple_of(half * width, width), width)
+    columns = pl.ds(0 if first else width, width)
     copies = []
     for j in range(target.shape[0] // OUT_WIDTH):
         head = 2 * j + place[0]
         row = pl.multiple_of(head * OUT_WIDTH, OUT_WIDTH)
-        if give:
+        if first:
             keys, values, _, key_part, value_part, _ = refs
             lane = pl.multiple_of(head * HEAD_DIM, HEAD_DIM)
             for cache, part in ((keys, key_part), (values, value_part)):
@@ -304,12 +303,21 @@
 
 
 def out_kernel(count, blocks, place, slots, *refs):
-    pieces_in, (_, weight, give, permuted, scratch) = refs[:count], refs[count:]
+    pieces_in, (first, second, give, own, scratch) = refs[:count], refs[count:]
+    half = first.shape[1]
     values = jnp.concatenate([piece[...] for piece in pieces_in], axis=0)
-    chosen = one_hot(slots, scratch, blocks, place[1], place[2]).T.astype(jnp.bfloat16)
+    chosen = one_hot(slots, scratch, blocks, place[1], place[1]).T.astype(jnp.bfloat16)
     order = jnp.dot(chosen, values, preferred_element_type=jnp.float32).astype(jnp.bfloat16)
-    permuted[...] = order
-    dot_columns(order, weight, give)
+    dot_columns(order, first, own.at[:, :half])
+    dot_columns(order, second, own.at[:, half:])
+    give[...] = own[...].astype(give.dtype)
+
+
+def sum_kernel(own, received, *outs):
+    rows = outs[0].shape[0]
+    for i, out in enumerate(outs):
+        part = slice(i * rows, (i + 1) * rows)
+        out[...] = (own[part, :] + received[part, :].astype(jnp.float32)).astype(out.dtype)
 
 
 def merge_kernel(own, given, received, *outs):
@@ -334,8 +342,8 @@
 def project(kernel, place, slots, pieces_in, extra, weights, more, pairs):
     count = lax.axis_size("col")
     parts = len(pieces_in)
-    rows, depth = pieces_in[0].shape
-    rows = rows * parts
+    depth = pieces_in[0].shape[1]
+    rows = sum(part.shape[0] for part in pieces_in)
     half = weights[0].shape[1]
     flops = 2 * rows * depth * half
     give, permuted = call(
@@ -369,15 +377,17 @@
     )(own, give, received)
 
 
-def gathered(parts, axis):
+def gathered(whole, parts, axis):
     blocks = {0: parts}
     mask = lax.axis_size(axis) // 2
     while mask:
-        blocks |= {
-            known | mask: [moved(part, axis, mask) for part in block]
-            for known, block in blocks.items()
-        }
+        arrived = {}
+        for known, block in blocks.items():
+            sent = [whole] if mask == 1 and known == 0 else block
+            arrived[known | mask] = [moved(part, axis, mask) for part in sent]
+        blocks |= arrived
         mask //= 2
+    blocks[0] = [whole]
     return [part for i in sorted(blocks) for part in blocks[i]]
 
 
@@ -422,7 +432,7 @@
 
 def attend_all(count, parts, place, lengths, *refs):
     blocks, (keys, values), refs = refs[:count], refs[count : count + 2], refs[count + 2 :]
-    outs, (scores_of, probs_of) = refs[:parts], refs[parts:]
+    whole, outs, (scores_of, probs_of) = refs[0], refs[1 : parts + 1], refs[parts + 1 :]
     pairs = keys.shape[2] // HEAD_DIM
     rows, cache = keys.shape[:2]
     low = place[1] % pairs
@@ -493,37 +503,48 @@
                 joined = jnp.concatenate(
                     [result[head] for result in results[i * size : (i + 1) * size]], axis=0
                 )
-                out[:, pl.ds(at, HEAD_DIM)] = joined.astype(jnp.bfloat16)
-
-
-def sum_kernel(count, parts, place, hidden, *refs):
-    attended, blocks, (keep, send) = refs[:parts], refs[parts : parts + count], refs[parts + count :]
-    rows, width = blocks[0].shape
-    pairs = keep.shape[1] // width
-    side = place[0]
+                joined = joined.astype(jnp.bfloat16)
+                out[:, pl.ds(at, HEAD_DIM)] = joined
+                run = slice(i * joined.shape[0], (i + 1) * joined.shape[0])
+                whole[run, pl.ds(at, HEAD_DIM)] = joined
+
+
+def choose_kernel(count, other, place, *refs):
+    blocks, out = refs[:count], refs[count]
+    pairs = out.shape[0]
+    wanted = place[3] ^ other
+    for chunk in range(count // pairs):
+
+        @pl.when(wanted == chunk)
+        def _():
+            for pair in range(pairs):
+                out[pair] = blocks[chunk * pairs + pair][...]
+
+
+def finish_kernel(count, others, place, hidden, attended, given, *refs):
+    blocks, arrived, out = refs[:count], refs[count : count + others], refs[-1]
+    pairs, _, width = arrived[0].shape
     low = place[1] % pairs
-    for pair in range(pairs):
-        column = low ^ pair
-        total = blocks[pair][...].astype(jnp.float32)
-        for i in range(pair + pairs, count, pairs):
-            total = total + blocks[i][...].astype(jnp.float32)
-        at = pl.ds(pl.multiple_of((2 * column + side) * width, width), width)
-        hidden_out = (hidden[:, at].astype(jnp.float32) + total).astype(jnp.bfloat16)
-        at = pl.ds(pl.multiple_of(column * width, width), width)
-        attention = jnp.concatenate([part[:, at] for part in attended], axis=0)
-        keep[:, at] = jnp.where(side == 0, hidden_out, attention)
-        send[:, at] = jnp.where(side == 0, attention, hidden_out)
-
-
-def join_kernel(place, keep, received, out):
-    side = place[0]
-    width = OUT_WIDTH
-    for j in range(keep.shape[1] // width):
-        part = slice(j * width, (j + 1) * width)
-        out[0, :, pl.ds(pl.multiple_of((2 * j + side) * width, width), width)] = keep[:, part]
-        out[0, :, pl.ds(pl.multiple_of((2 * j + 1 - side) * width, width), width)] = received[
-            :, part
-        ]
+
+    @pl.when(place[0] == 0)
+    def _():
+        for pair in range(pairs):
+            total = jnp.zeros(arrived[0].shape[1:], jnp.float32)
+            for chunk in range(count // pairs):
+                part = blocks[chunk * pairs + pair][...].astype(jnp.float32)
+                total = total + jnp.where(place[3] == chunk, part, 0.0)
+            for ref in arrived:
+                total = total + ref[pair].astype(jnp.float32)
+            at = pl.ds(pl.multiple_of((low ^ pair) * width, width), width)
+            out[0, :, at] = (hidden[:, at].astype(jnp.float32) + total).astype(jnp.bfloat16)
+
+    @pl.when(place[0] != 0)
+    def _():
+        size = OUT_WIDTH
+        for j in range(attended.shape[1] // size):
+            part = slice(j * size, (j + 1) * size)
+            out[0, :, 2 * j * size : (2 * j + 1) * size] = given[:, part]
+            out[0, :, (2 * j + 1) * size : (2 * j + 2) * size] = attended[:, part]
 
 
 def paired_plan(
@@ -533,7 +554,8 @@
     pairs = col_count // row_count
     side, col, row = (lax.axis_index(name) for name in ("side", "col", "row"))
     run = row * pairs + lax.rem(col, pairs)
-    place = jnp.stack([side, col, run]).astype(jnp.int32)
+    base = lax.div(col, pairs) ^ row
+    place = jnp.stack([side, col, run, base]).astype(jnp.int32)
     rows, depth = hidden_in.shape
     half = depth // 2
     cache = key_cache.shape[1]
@@ -553,9 +575,9 @@
         [pltpu.SemaphoreType.DMA((2,))],
     )(place, in_hbm(qkv_weight), gain)
     blocks = gathered(
-        [own_part[i * piece : (i + 1) * piece] for i in range(parts)], "col"
-    )
-    out_give, key_part, value_part = call(
+        own_part, [own_part[i * piece : (i + 1) * piece] for i in range(parts)], "col"
+    )
+    out_first, key_part, value_part = call(
         functools.partial(stage_out_kernel, True),
         [pltpu.VMEM((half, half_out), jnp.bfloat16)]
         + [pltpu.VMEM((rows, cache, pairs * HEAD_DIM), jnp.bfloat16)] * 2,
@@ -572,17 +594,17 @@
 
     key_part, value_part = in_vmem(key_part), in_vmem(value_part)
     runs = (pairs, rows // SLOTS, GROUP * SLOTS, SLOTS * cache)
-    attended = call(
+    attended, *attended_parts = call(
         functools.partial(attend_all, col_count, parts),
-        [struct((piece, half))] * parts,
+        [struct((rows, half))] + [struct((piece, half))] * parts,
         [SMEM, SMEM] + [VMEM] * (col_count + 2),
-        [VMEM] * parts,
+        [VMEM] * (parts + 1),
         4 * rows * half * cache,
         0,
         [pltpu.VMEM(runs, jnp.float32), pltpu.VMEM(runs, jnp.bfloat16)],
     )(place, cache_lengths, *products, key_part, value_part)
 
-    out_own = call(
+    out_second = call(
         functools.partial(stage_out_kernel, False),
         pltpu.VMEM((half, half_out), jnp.bfloat16),
         [SMEM, HBM, HBM],
@@ -590,35 +612,57 @@
         0,
         half * half_out * 2,
         [pltpu.SemaphoreType.DMA((pairs,))],
-    )(place, in_hbm(out_weight), attended[-1])
-    products = spread(
-        project(
-            out_kernel,
-            place,
-            slot_request,
-            gathered(attended, "col"),
-            [in_vmem(out_own)],
-            [out_give, out_own],
-            0,
-            pairs,
+    )(place, in_hbm(out_weight), attended)
+    given = lax.ppermute(attended, "side", [(0, 1)])
+    pieces_in = gathered(attended, attended_parts, "col")
+    total_rows = rows * col_count
+    give, own = call(
+        functools.partial(out_kernel, len(pieces_in), col_count),
+        [struct((total_rows, 2 * half_out)), struct((total_rows, 2 * half_out), jnp.float32)],
+        [SMEM] + [VMEM] * (len(pieces_in) + 3),
+        [VMEM] * 2,
+        4 * total_rows * half * half_out,
+        half * half_out * 4,
+        [pltpu.VMEM((total_rows, total_rows), jnp.float32)],
+    )(place, slot_request, *pieces_in, in_vmem(out_first), in_vmem(out_second))
+    received = lax.ppermute(give, "side", [(1, 0)])
+    products = call(
+        sum_kernel,
+        [struct((rows, 2 * half_out))] * col_count,
+        [VMEM] * 2,
+        [VMEM] * col_count,
+        2 * total_rows * half_out,
+        total_rows * half_out * 16,
+    )(own, received)
+    products = [products[0]] + [
+        lax.ppermute(
+            products[mask], ("col", "side"), [(2 * c, 2 * (c ^ mask)) for c in range(col_count)]
         )
-    )
-    keep, send = call(
-        functools.partial(sum_kernel, col_count, parts),
-        [struct((rows, half)), struct((rows, half))],
-        [SMEM] + [VMEM] * (1 + parts + col_count),
-        [VMEM, VMEM],
+        for mask in range(1, col_count)
+    ]
+    arrived = [
+        lax.ppermute(
+            call(
+                functools.partial(choose_kernel, col_count, mask),
+                struct((pairs, rows, 2 * half_out)),
+                [SMEM] + [VMEM] * col_count,
+                VMEM,
+                0,
+                pairs * rows * half_out * 8,
+            )(place, *products),
+            ("row", "side"),
+            [(2 * r, 2 * (r ^ mask)) for r in range(row_count)],
+        )
+        for mask in range(1, row_count)
+    ]
+    return call(
+        functools.partial(finish_kernel, col_count, row_count - 1),
+        struct((1, rows, depth)),
+        [SMEM] + [VMEM] * (3 + col_count + row_count - 1),
+        VMEM,
         rows * depth * 4,
         rows * depth * 8,
-    )(place, hidden_in, *attended, *products)
-    return call(
-        join_kernel,
-        struct((1, rows, depth)),
-        [SMEM, VMEM, VMEM],
-        VMEM,
-        0,
-        rows * depth * 4,
-    )(place, keep, moved(send, "side", 1))
+    )(place, hidden_in, attended, given, *products, *arrived)
 
 
 def per_device(*args):
@@ -628,6 +672,7 @@
         lax.axis_size("side") == 2
         and qkv_weight.shape[1] == 2 * GROUP_WIDTH
         and col_count % row_count == 0
+        and row_count > 1
         and col_count & (col_count - 1) == 0
         and hidden_in.shape[0] % 32 == 0
         and key_cache.shape[1] % 16 == 0

time: 70.8 us -> 80 us (1.13)
  starting transfers between devices: 34.6 us -> 40.6 us
  waiting for transfers between devices: 13.9 us -> 16.1 us
  local copies, waits for them, and re-layouts: 1.6 us -> 2.52 us
    ppermute x0 -> x6, starting transfers between devices: none -> 16.5 us  [the longest x3 10.1 us: paired_plan(): lax.ppermute(products[mask], ('col', 'side'), [(2 * c, 2 * (c ^ mask)) fo...]
    ppermute x0 -> x6, waiting for transfers between devices: none -> 10.8 us  [the longest x3 5.18 us: paired_plan(): lax.ppermute(products[mask], ('col', 'side'), [(2 * c, 2 * (c ^ mask)) fo...]
    ppermute x8 -> x4, starting transfers between devices: 19.2 us -> 9.06 us  [spread(): lax.ppermute(products[j], ('col', 'row'), [(col * row_count + row, (row *...]
    ppermute x8 -> x4, waiting for transfers between devices: 6 us -> 0.01 us  [spread(): lax.ppermute(products[j], ('col', 'row'), [(col * row_count + row, (row *...]
    ppermute x15 -> x11, waiting for transfers between devices: 7.91 us -> 5.26 us  [moved(): return lax.ppermute(value, axis, pairs)]
    pallas_call x3 -> x5, Pallas kernels: 4.15 us -> 6.45 us  [the longest x1 2.27 us: paired_plan(): call(functools.partial(attend_all, col_count, parts), [struct((rows, half...]
    pallas_call x2 -> x1, Pallas kernels: 3.26 us -> 1.73 us  [project(): call(functools.partial(kernel, parts, count), [struct((rows, half + more)...]
    dynamic_slice x0 -> x1, local copies, waits for them, and re-layouts: none -> 0.91 us  [paired_plan(): own_part = lax.dynamic_slice_in_dim(hidden_in, side * half, half, 1)]
  transfers between devices with their start and end apart: 23 -> 21, of which waited for: 10 -> 10; matrix products, arithmetic and copies ran while one was open for 1% -> 2% of each run, Pallas kernels for 18% -> 15%
where the time goes in v7:
time: 80 us; the launch traced here: 79.6 us
  starting transfers between devices  40.6 us (51%)
  Pallas kernels  20.1 us (25%)
  waiting for transfers between devices  16.1 us (20%)
  local copies, waits for them, and re-layouts  2.52 us (3%)
    ppermute x11, starting transfers between devices, moved(): return lax.ppermute(value, axis, pairs)  15 us
    ppermute x3, starting transfers between devices, paired_plan(): lax.ppermute(products[mask], ('col', 'side'), [(2 * c, 2 * (c ^ mask)) fo...  10.1 us
    ppermute x4, starting transfers between devices, spread(): lax.ppermute(products[j], ('col', 'row'), [(col * row_count + row, (row *...  9.06 us
    ppermute x11, waiting for transfers between devices, moved(): return lax.ppermute(value, axis, pairs)  5.26 us
    ppermute x3, waiting for transfers between devices, paired_plan(): lax.ppermute(products[mask], ('col', 'side'), [(2 * c, 2 * (c ^ mask)) fo...  5.18 us
    pallas_call x1, Pallas kernels, paired_plan(): call(stage_in_kernel, [pltpu.VMEM((half, half_in), jnp.bfloat16)] * 2, [S...  4.62 us
    ppermute x1, starting transfers between devices, paired_plan(): lax.ppermute(call(functools.partial(choose_kernel, col_count, mask), stru...  3.8 us
    pallas_call x1, Pallas kernels, paired_plan(): call(functools.partial(stage_out_kernel, True), [pltpu.VMEM((half, half_o...  3.54 us
  transfers between devices with their start and end apart: 21, of which 10 were waited for; matrix products, arithmetic and copies ran while one was open for 2% of the time, Pallas kernels for 15%

profile of v7, /device:TPU:0, one launch (start us, length us, event | category | flops | bytes accessed | tf_op | source)
XLA Modules:
  0.0 79.6 jit_solution(17170131594355162006)
XLA Ops:
  0.0 0.9 %fusion = (bf16[16,2048]{1,0:T(8,128)(2,1)S(1)}, bf16[16,2048]{1,0:T(8,128)(2,1)S(1)}) fusion(bf16[32,4096]{1,0:T(8,128)(2,1)} %hidden.1, s32[]{:T(128)S(6)} %add.11, s32[]{:T(128)S(6)} %select_n.3), kind=kLoop, calls=%fused_computation.3 | loop fusion | bytes 262152 | tf_op jit(solution)/shard_map/slice | solution.py:578
  0.9 4.1 %collective-permute-start.1 = (bf16[16,2048]{1,0:T(8,128)(2,1)S(1)}, bf16[16,2048]{1,0:T(8,128)(2,1)S(1)}, u32[]{:S(2)}, u32[]{:S(2)}) collective-permute-start(bf16[16,2048]{1,0:T(8,128)(2,1)S(1)} %get-tuple-element.46), channel_id=1, source_target_pairs={{0,8},{4,12},{8,0},{12,4},{1,9},{5,13},{9,1},{13,5},{2,10},{6,14},... | collective-permute-start | bytes 196616 | tf_op jit(solution)/shard_map/ppermute | solution.py:206
  5.0 0.1 collective-permute-start.2
  5.1 0.9 %constant_dynamic-slice_fusion.1.refs_0_ = bf16[32,2048]{1,0:T(8,128)(2,1)S(1)} fusion(bf16[32,4096]{1,0:T(8,128)(2,1)} %hidden.1, s32[]{:T(128)S(6)} %select_n.3), kind=kLoop, calls=%fused_computation.2 | loop fusion | bytes 262148 | tf_op jit(solution)/shard_map/dynamic_slice | solution.py:565
  6.0 1.9 %collective-permute-start = (bf16[32,2048]{1,0:T(8,128)(2,1)S(1)}, bf16[32,2048]{1,0:T(8,128)(2,1)S(1)}, u32[]{:S(2)}, u32[]{:S(2)}) collective-permute-start(bf16[32,2048]{1,0:T(8,128)(2,1)S(1)} %constant_dynamic-slice_fusion.1.refs_0_), channel_id=1, source_target_pairs={{0,4},{4,0},{8,12},{12,8},{1,5},{5,1},{9,13},{13,9},{2,6},{6,2},{1... | collective-permute-start | bytes 393224 | tf_op jit(solution)/shard_map/ppermute | solution.py:206
  7.9 0.7 reshape.3.gain.refs_6_
  8.6 0.1 collective-permute-done.1.refs_2_
  8.7 2.0 %collective-permute-start.3 = (bf16[16,2048]{1,0:T(8,128)(2,1)S(1)}, bf16[16,2048]{1,0:T(8,128)(2,1)S(1)}, u32[]{:S(2)}, u32[]{:S(2)}) collective-permute-start(bf16[16,2048]{1,0:T(8,128)(2,1)S(1)} %collective-permute-done.1.refs_2_), channel_id=1, source_target_pairs={{0,4},{4,0},{8,12},{12,8},{1,5},{5,1},{9,13},{13,9},{2,6},{6,2},{1... | collective-permute-start | bytes 196616 | tf_op jit(solution)/shard_map/ppermute | solution.py:206
  10.7 0.3 collective-permute-done.2.refs_3_
  11.0 1.4 %collective-permute-start.4 = (bf16[16,2048]{1,0:T(8,128)(2,1)S(1)}, bf16[16,2048]{1,0:T(8,128)(2,1)S(1)}, u32[]{:S(2)}, u32[]{:S(2)}) collective-permute-start(bf16[16,2048]{1,0:T(8,128)(2,1)S(1)} %collective-permute-done.2.refs_3_), channel_id=1, source_target_pairs={{0,4},{4,0},{8,12},{12,8},{1,5},{5,1},{9,13},{13,9},{2,6},{6,2},{1... | collective-permute-start | bytes 196616 | tf_op jit(solution)/shard_map/ppermute | solution.py:206
  12.4 0.1 pad_add_fusion.place
  12.5 4.6 %shard_map.82 = (bf16[2048,1280]{1,0:T(8,128)(2,1)S(1)}, bf16[2048,1280]{1,0:T(8,128)(2,1)S(1)}) custom-call(s32[4]{0:T(128)S(1)} %pad_add_fusion.place, bf16[4096,2560]{1,0:T(8,128)(2,1)} %weight.3, bf16[1,4096]{1,0:T(2,128)(2,1)S(1)} %reshape.3.gain.refs_6_), custom_call_target="tpu_custom_call" | custom-call | bytes 10485760 | tf_op jit(solution)/shard_map/pallas_call | solution.py:568
  17.1 0.0 collective-permute-done.3.refs_4_
  17.2 1.7 %shard_map.83 = (bf16[128,1408]{1,0:T(8,128)(2,1)S(1)}, bf16[128,2048]{1,0:T(8,128)(2,1)S(1)}) custom-call(s32[4]{0:T(128)S(1)} %pad_add_fusion.place, s32[128]{0:T(128)S(1)} %copy-done.1, bf16[32,2048]{1,0:T(8,128)(2,1)S(1)} %constant_dynamic-slice_fusion.1.refs_0_, bf16[32,2048]{1,0:T(8,128)(2,1)S(1)} %collective-permute-done.refs_1_, ...), custom_call_target="tpu_custom_call" | custom-call | flops 671088640 | bytes 5242880 | tf_op jit(solution)/shard_map/pallas_call | solution.py:349
  18.9 0.1 collective-permute-start.5
  19.0 0.9 %shard_map.84.own = f32[128,1280]{1,0:T(8,128)S(1)} custom-call(bf16[128,2048]{1,0:T(8,128)(2,1)S(1)} %get-tuple-element.26.permuted, bf16[2048,1280]{1,0:T(8,128)(2,1)S(1)} %get-tuple-element.27.weight), custom_call_target="tpu_custom_call" | custom-call | flops 671088640 | bytes 5242880 | tf_op jit(solution)/shard_map/pallas_call | solution.py:359
  19.9 0.8 collective-permute-done.5.received
  20.7 0.1 shard_map.85
  20.7 0.7 collective-permute-start.7
  21.4 4.1 %collective-permute-start.9 = (bf16[32,1408]{1,0:T(8,128)(2,1)S(1)}, bf16[32,1408]{1,0:T(8,128)(2,1)S(1)}, u32[]{:S(2)}, u32[]{:S(2)}) collective-permute-start(bf16[32,1408]{1,0:T(8,128)(2,1)S(1)} %get-tuple-element.32), channel_id=1, source_target_pairs={{0,12},{2,4},{4,8},{6,0},{8,14},{10,6},{12,10},{14,2},{1,13},{3,5}... | collective-permute-start | bytes 270344 | tf_op jit(solution)/shard_map/ppermute | solution.py:399
  25.5 0.7 collective-permute-start.6
  26.2 0.0 copy-start.2
  26.2 3.6 %collective-permute-start.8 = (bf16[32,1280]{1,0:T(8,128)(2,1)S(1)}, bf16[32,1280]{1,0:T(8,128)(2,1)S(1)}, u32[]{:S(2)}, u32[]{:S(2)}) collective-permute-start(bf16[32,1280]{1,0:T(8,128)(2,1)S(1)} %get-tuple-element.31), channel_id=1, source_target_pairs={{0,8},{2,0},{4,12},{6,4},{8,10},{10,2},{12,14},{14,6},{1,9},{3,1},... | collective-permute-start | bytes 245768 | tf_op jit(solution)/shard_map/ppermute | solution.py:399
  29.8 3.5 %shard_map.86 = (bf16[2048,1024]{1,0:T(8,128)(2,1)S(1)}, bf16[32,64,256]{2,1,0:T(8,128)(2,1)S(1)}, bf16[32,64,256]{2,1,0:T(8,128)(2,1)S(1)}) custom-call(s32[4]{0:T(128)S(1)} %pad_add_fusion.place, bf16[4096,2048]{1,0:T(8,128)(2,1)} %weight.5, bf16[32,64,512]{2,1,0:T(8,128)(2,1)} %refs_0_.1, bf16[32,64,512]{2,1,0:T(8,128)(2,1)} %refs_1_.1), custom_call_target="tpu_custom_call" | custom-call | bytes 6291456 | tf_op jit(solution)/shard_map/pallas_call | solution.py:580
  33.4 2.3 %shard_map.87 = (bf16[32,2048]{1,0:T(8,128)(2,1)S(1)}, bf16[16,2048]{1,0:T(8,128)(2,1)S(1)}, bf16[16,2048]{1,0:T(8,128)(2,1)S(1)}) custom-call(s32[4]{0:T(128)S(1)} %pad_add_fusion.place, s32[32]{0:T(128)S(1)} %copy-done.2, bf16[32,1280]{1,0:T(8,128)(2,1)S(1)} %collective-permute-done.6.refs_0_, bf16[32,1408]{1,0:T(8,128)(2,1)S(1)} %collective-permute-done.7.refs_1_, ...), custom_call_target="tpu_custom_call" | custom-call | flops 16777216 | tf_op jit(solution)/shard_map/pallas_call | solution.py:597
  35.7 1.9 %collective-permute-start.12 = (bf16[16,2048]{1,0:T(8,128)(2,1)S(1)}, bf16[16,2048]{1,0:T(8,128)(2,1)S(1)}, u32[]{:S(2)}, u32[]{:S(2)}) collective-permute-start(bf16[16,2048]{1,0:T(8,128)(2,1)S(1)} %get-tuple-element.36), channel_id=1, source_target_pairs={{0,8},{4,12},{8,0},{12,4},{1,9},{5,13},{9,1},{13,5},{2,10},{6,14},... | collective-permute-start | bytes 196616 | tf_op jit(solution)/shard_map/ppermute | solution.py:206
  37.6 1.1 %collective-permute-start.13 = (bf16[16,2048]{1,0:T(8,128)(2,1)S(1)}, bf16[16,2048]{1,0:T(8,128)(2,1)S(1)}, u32[]{:S(2)}, u32[]{:S(2)}) collective-permute-start(bf16[16,2048]{1,0:T(8,128)(2,1)S(1)} %get-tuple-element.37), channel_id=1, source_target_pairs={{0,8},{4,12},{8,0},{12,4},{1,9},{5,13},{9,1},{13,5},{2,10},{6,14},... | collective-permute-start | bytes 196616 | tf_op jit(solution)/shard_map/ppermute | solution.py:206
  38.7 0.7 collective-permute-start.11
  39.4 3.3 %collective-permute-done.12.refs_2_ = bf16[16,2048]{1,0:T(8,128)(2,1)S(1)} collective-permute-done((bf16[16,2048]{1,0:T(8,128)(2,1)S(1)}, bf16[16,2048]{1,0:T(8,128)(2,1)S(1)}, u32[]{:S(2)}, u32[]{:S(2)}) %collective-permute-start.12) | collective-permute-done | bytes 65568 | tf_op jit(solution)/shard_map/ppermute | solution.py:206
  42.7 0.7 collective-permute-done.13.refs_3_
  43.4 1.8 %collective-permute-start.15 = (bf16[16,2048]{1,0:T(8,128)(2,1)S(1)}, bf16[16,2048]{1,0:T(8,128)(2,1)S(1)}, u32[]{:S(2)}, u32[]{:S(2)}) collective-permute-start(bf16[16,2048]{1,0:T(8,128)(2,1)S(1)} %collective-permute-done.13.refs_3_), channel_id=1, source_target_pairs={{0,4},{4,0},{8,12},{12,8},{1,5},{5,1},{9,13},{13,9},{2,6},{6,2},{1... | collective-permute-start | bytes 196616 | tf_op jit(solution)/shard_map/ppermute | solution.py:206
  45.2 2.8 %shard_map.88.refs_7_ = bf16[2048,1024]{1,0:T(8,128)(2,1)S(1)} custom-call(s32[4]{0:T(128)S(1)} %pad_add_fusion.place, bf16[4096,2048]{1,0:T(8,128)(2,1)} %weight.5, bf16[32,2048]{1,0:T(8,128)(2,1)S(1)} %get-tuple-element.35.refs_0_.attended), custom_call_target="tpu_custom_call" | custom-call | bytes 4194304 | tf_op jit(solution)/shard_map/pallas_call | solution.py:607
  48.0 0.0 copy-start
  48.0 2.1 %shard_map.89 = (bf16[128,2048]{1,0:T(8,128)(2,1)S(1)}, f32[128,2048]{1,0:T(8,128)S(1)}) custom-call(s32[4]{0:T(128)S(1)} %pad_add_fusion.place, s32[128]{0:T(128)S(1)} %copy-done.1, bf16[32,2048]{1,0:T(8,128)(2,1)S(1)} %get-tuple-element.35.refs_0_.attended, bf16[32,2048]{1,0:T(8,128)(2,1)S(1)} %collective-permute-done.11.refs_1_, ...), custom_call_target="tpu_custom_call" | custom-call | flops 1073741824 | bytes 8388608 | tf_op jit(solution)/shard_map/pallas_call | solution.py:619
  50.1 1.3 %collective-permute-start.16 = (bf16[128,2048]{1,0:T(8,128)(2,1)S(1)}, bf16[128,2048]{1,0:T(8,128)(2,1)S(1)}, u32[]{:S(2)}, u32[]{:S(2)}) collective-permute-start(bf16[128,2048]{1,0:T(8,128)(2,1)S(1)} %get-tuple-element.40), channel_id=1, source_target_pairs={{1,0},{3,2},{5,4},{7,6},{9,8},{11,10},{13,12},{15,14},{17,16},{19,... | collective-permute-start | bytes 1572872 | tf_op jit(solution)/shard_map/ppermute | solution.py:628
  51.4 2.5 %collective-permute-done.16.received = bf16[128,2048]{1,0:T(8,128)(2,1)S(1)} collective-permute-done((bf16[128,2048]{1,0:T(8,128)(2,1)S(1)}, bf16[128,2048]{1,0:T(8,128)(2,1)S(1)}, u32[]{:S(2)}, u32[]{:S(2)}) %collective-permute-start.16) | collective-permute-done | bytes 524320 | tf_op jit(solution)/shard_map/ppermute | solution.py:628
  53.9 0.1 shard_map.90
  54.0 3.3 %collective-permute-start.17 = (bf16[32,2048]{1,0:T(8,128)(2,1)S(1)}, bf16[32,2048]{1,0:T(8,128)(2,1)S(1)}, u32[]{:S(2)}, u32[]{:S(2)}) collective-permute-start(bf16[32,2048]{1,0:T(8,128)(2,1)S(1)} %get-tuple-element.42), channel_id=1, source_target_pairs={{0,4},{4,0},{8,12},{12,8},{2,6},{6,2},{10,14},{14,10},{16,20},{20,... | collective-permute-start | bytes 393224 | tf_op jit(solution)/shard_map/ppermute | solution.py:638
  57.4 3.2 %collective-permute-start.18 = (bf16[32,2048]{1,0:T(8,128)(2,1)S(1)}, bf16[32,2048]{1,0:T(8,128)(2,1)S(1)}, u32[]{:S(2)}, u32[]{:S(2)}) collective-permute-start(bf16[32,2048]{1,0:T(8,128)(2,1)S(1)} %get-tuple-element.43), channel_id=1, source_target_pairs={{0,8},{4,12},{8,0},{12,4},{2,10},{6,14},{10,2},{14,6},{16,24},{20,... | collective-permute-start | bytes 393224 | tf_op jit(solution)/shard_map/ppermute | solution.py:638
  60.6 3.6 %collective-permute-start.19 = (bf16[32,2048]{1,0:T(8,128)(2,1)S(1)}, bf16[32,2048]{1,0:T(8,128)(2,1)S(1)}, u32[]{:S(2)}, u32[]{:S(2)}) collective-permute-start(bf16[32,2048]{1,0:T(8,128)(2,1)S(1)} %get-tuple-element.44), channel_id=1, source_target_pairs={{0,12},{4,8},{8,4},{12,0},{2,14},{6,10},{10,6},{14,2},{16,28},{20,... | collective-permute-start | bytes 393224 | tf_op jit(solution)/shard_map/ppermute | solution.py:638
  64.2 2.4 %collective-permute-done.18.refs_2_ = bf16[32,2048]{1,0:T(8,128)(2,1)S(1)} collective-permute-done((bf16[32,2048]{1,0:T(8,128)(2,1)S(1)}, bf16[32,2048]{1,0:T(8,128)(2,1)S(1)}, u32[]{:S(2)}, u32[]{:S(2)}) %collective-permute-start.18) | collective-permute-done | bytes 131104 | tf_op jit(solution)/shard_map/ppermute | solution.py:638
  66.5 2.8 %collective-permute-done.19.refs_3_ = bf16[32,2048]{1,0:T(8,128)(2,1)S(1)} collective-permute-done((bf16[32,2048]{1,0:T(8,128)(2,1)S(1)}, bf16[32,2048]{1,0:T(8,128)(2,1)S(1)}, u32[]{:S(2)}, u32[]{:S(2)}) %collective-permute-start.19) | collective-permute-done | bytes 131104 | tf_op jit(solution)/shard_map/ppermute | solution.py:638
  69.3 0.6 shard_map.91
  69.9 3.8 %collective-permute-start.20 = (bf16[2,32,2048]{2,1,0:T(8,128)(2,1)S(1)}, bf16[2,32,2048]{2,1,0:T(8,128)(2,1)S(1)}, u32[]{:S(2)}, u32[]{:S(2)}) collective-permute-start(bf16[2,32,2048]{2,1,0:T(8,128)(2,1)S(1)} %shard_map.91), channel_id=1, source_target_pairs={{0,2},{2,0},{4,6},{6,4},{8,10},{10,8},{12,14},{14,12},{16,18},{18,... | collective-permute-start | bytes 786440 | tf_op jit(solution)/shard_map/ppermute | solution.py:644
  73.7 1.3 %collective-permute-start.10 = (bf16[32,2048]{1,0:T(8,128)(2,1)S(1)}, bf16[32,2048]{1,0:T(8,128)(2,1)S(1)}, u32[]{:S(2)}, u32[]{:S(2)}) collective-permute-start(bf16[32,2048]{1,0:T(8,128)(2,1)S(1)} %get-tuple-element.35.refs_0_.attended), channel_id=1, source_target_pairs={{0,1},{2,3},{4,5},{6,7},{8,9},{10,11},{12,13},{14,15},{16,17},{18,... | collective-permute-start | bytes 393224 | tf_op jit(solution)/shard_map/ppermute | solution.py:616
  75.0 1.0 %collective-permute-done.10.given = bf16[32,2048]{1,0:T(8,128)(2,1)S(1)} collective-permute-done((bf16[32,2048]{1,0:T(8,128)(2,1)S(1)}, bf16[32,2048]{1,0:T(8,128)(2,1)S(1)}, u32[]{:S(2)}, u32[]{:S(2)}) %collective-permute-start.10) | collective-permute-done | bytes 131104 | tf_op jit(solution)/shard_map/ppermute | solution.py:616
  76.0 2.2 %collective-permute-done.20.refs_4_ = bf16[2,32,2048]{2,1,0:T(8,128)(2,1)S(1)} collective-permute-done((bf16[2,32,2048]{2,1,0:T(8,128)(2,1)S(1)}, bf16[2,32,2048]{2,1,0:T(8,128)(2,1)S(1)}, u32[]{:S(2)}, u32[]{:S(2)}) %collective-permute-start.20) | collective-permute-done | bytes 262176 | tf_op jit(solution)/shard_map/ppermute | solution.py:644
  78.2 1.4 %shard_map.92 = bf16[1,32,4096]{2,1,0:T(8,128)(2,1)} custom-call(s32[4]{0:T(128)S(1)} %pad_add_fusion.place, bf16[32,4096]{1,0:T(8,128)(2,1)S(1)} %copy-done, bf16[32,2048]{1,0:T(8,128)(2,1)S(1)} %get-tuple-element.35.refs_0_.attended, bf16[32,2048]{1,0:T(8,128)(2,1)S(1)} %collective-permute-done.10.given, bf16[32,2048]{1,0:T(8,128)(2,1)S(1)} %get-tuple-element.41.refs_0_, ...), custom_call_target="tpu_custom_call" | custom-call | flops 524288 | bytes 1048576 | tf_op jit(solution)/shard_map/pallas_call | solution.py:658
  (15 shorter events, 0.0 us)
Async XLA Ops:
  0.9 7.9 %collective-permute-start.1 = (bf16[16,2048]{1,0:T(8,128)(2,1)S(1)}, bf16[16,2048]{1,0:T(8,128)(2,1)S(1)}, u32[]{:S(2)}, u32[]{:S(2)}) collective-permute-start(bf16[16,2048]{1,0:T(8,128)(2,1)S(1)} %get-tuple-element.46), channel_id=1, source_target_pairs={{0,8},{4,12},{8,0},{12,4},{1,9},{5,13},{9,1},{13,5},{2,10},{6,14},... | collective-permute-start | bytes 196616 | tf_op jit(solution)/shard_map/ppermute | solution.py:206
  5.0 6.0 %collective-permute-start.2 = (bf16[16,2048]{1,0:T(8,128)(2,1)S(1)}, bf16[16,2048]{1,0:T(8,128)(2,1)S(1)}, u32[]{:S(2)}, u32[]{:S(2)}) collective-permute-start(bf16[16,2048]{1,0:T(8,128)(2,1)S(1)} %get-tuple-element.45), channel_id=1, source_target_pairs={{0,8},{4,12},{8,0},{12,4},{1,9},{5,13},{9,1},{13,5},{2,10},{6,14},... | collective-permute-start | bytes 196616 | tf_op jit(solution)/shard_map/ppermute | solution.py:206
  6.0 11.2 %collective-permute-start = (bf16[32,2048]{1,0:T(8,128)(2,1)S(1)}, bf16[32,2048]{1,0:T(8,128)(2,1)S(1)}, u32[]{:S(2)}, u32[]{:S(2)}) collective-permute-start(bf16[32,2048]{1,0:T(8,128)(2,1)S(1)} %constant_dynamic-slice_fusion.1.refs_0_), channel_id=1, source_target_pairs={{0,4},{4,0},{8,12},{12,8},{1,5},{5,1},{9,13},{13,9},{2,6},{6,2},{1... | collective-permute-start | bytes 393224 | tf_op jit(solution)/shard_map/ppermute | solution.py:206
  8.7 8.4 %collective-permute-start.3 = (bf16[16,2048]{1,0:T(8,128)(2,1)S(1)}, bf16[16,2048]{1,0:T(8,128)(2,1)S(1)}, u32[]{:S(2)}, u32[]{:S(2)}) collective-permute-start(bf16[16,2048]{1,0:T(8,128)(2,1)S(1)} %collective-permute-done.1.refs_2_), channel_id=1, source_target_pairs={{0,4},{4,0},{8,12},{12,8},{1,5},{5,1},{9,13},{13,9},{2,6},{6,2},{1... | collective-permute-start | bytes 196616 | tf_op jit(solution)/shard_map/ppermute | solution.py:206
  11.0 6.1 %collective-permute-start.4 = (bf16[16,2048]{1,0:T(8,128)(2,1)S(1)}, bf16[16,2048]{1,0:T(8,128)(2,1)S(1)}, u32[]{:S(2)}, u32[]{:S(2)}) collective-permute-start(bf16[16,2048]{1,0:T(8,128)(2,1)S(1)} %collective-permute-done.2.refs_3_), channel_id=1, source_target_pairs={{0,4},{4,0},{8,12},{12,8},{1,5},{5,1},{9,13},{13,9},{2,6},{6,2},{1... | collective-permute-start | bytes 196616 | tf_op jit(solution)/shard_map/ppermute | solution.py:206
  12.5 4.7 %copy-start.1 = (s32[128]{0:T(128)S(1)}, s32[128]{0:T(128)}, u32[]{:S(2)}) copy-start(s32[128]{0:T(128)} %slots.3) | copy-start | bytes 1540
  18.9 1.7 %collective-permute-start.5 = (bf16[128,1408]{1,0:T(8,128)(2,1)S(1)}, bf16[128,1408]{1,0:T(8,128)(2,1)S(1)}, u32[]{:S(2)}, u32[]{:S(2)}) collective-permute-start(bf16[128,1408]{1,0:T(8,128)(2,1)S(1)} %get-tuple-element.28.given), channel_id=1, source_target_pairs={{0,1},{1,0},{2,3},{3,2},{4,5},{5,4},{6,7},{7,6},{8,9},{9,8},{10,11... | collective-permute-start | bytes 1081352 | tf_op jit(solution)/shard_map/ppermute | solution.py:206
  20.7 12.7 %collective-permute-start.7 = (bf16[32,1408]{1,0:T(8,128)(2,1)S(1)}, bf16[32,1408]{1,0:T(8,128)(2,1)S(1)}, u32[]{:S(2)}, u32[]{:S(2)}) collective-permute-start(bf16[32,1408]{1,0:T(8,128)(2,1)S(1)} %get-tuple-element.30), channel_id=1, source_target_pairs={{0,4},{2,12},{4,0},{6,8},{8,6},{10,14},{12,2},{14,10},{1,5},{3,13}... | collective-permute-start | bytes 270344 | tf_op jit(solution)/shard_map/ppermute | solution.py:399
  21.4 12.0 %collective-permute-start.9 = (bf16[32,1408]{1,0:T(8,128)(2,1)S(1)}, bf16[32,1408]{1,0:T(8,128)(2,1)S(1)}, u32[]{:S(2)}, u32[]{:S(2)}) collective-permute-start(bf16[32,1408]{1,0:T(8,128)(2,1)S(1)} %get-tuple-element.32), channel_id=1, source_target_pairs={{0,12},{2,4},{4,8},{6,0},{8,14},{10,6},{12,10},{14,2},{1,13},{3,5}... | collective-permute-start | bytes 270344 | tf_op jit(solution)/shard_map/ppermute | solution.py:399
  25.5 7.8 %collective-permute-start.6 = (bf16[32,1280]{1,0:T(8,128)(2,1)S(1)}, bf16[32,1280]{1,0:T(8,128)(2,1)S(1)}, u32[]{:S(2)}, u32[]{:S(2)}) collective-permute-start(bf16[32,1280]{1,0:T(8,128)(2,1)S(1)} %get-tuple-element.29), channel_id=1, source_target_pairs={{0,0},{2,8},{4,4},{6,12},{8,2},{10,10},{12,6},{14,14},{1,1},{3,9},... | collective-permute-start | bytes 245768 | tf_op jit(solution)/shard_map/ppermute | solution.py:399
  26.2 7.2 %copy-start.2 = (s32[32]{0:T(128)S(1)}, s32[32]{0:T(128)}, u32[]{:S(2)}) copy-start(s32[32]{0:T(128)} %lengths.1) | copy-start | bytes 388
  26.2 7.2 %collective-permute-start.8 = (bf16[32,1280]{1,0:T(8,128)(2,1)S(1)}, bf16[32,1280]{1,0:T(8,128)(2,1)S(1)}, u32[]{:S(2)}, u32[]{:S(2)}) collective-permute-start(bf16[32,1280]{1,0:T(8,128)(2,1)S(1)} %get-tuple-element.31), channel_id=1, source_target_pairs={{0,8},{2,0},{4,12},{6,4},{8,10},{10,2},{12,14},{14,6},{1,9},{3,1},... | collective-permute-start | bytes 245768 | tf_op jit(solution)/shard_map/ppermute | solution.py:399
  35.7 7.0 %collective-permute-start.12 = (bf16[16,2048]{1,0:T(8,128)(2,1)S(1)}, bf16[16,2048]{1,0:T(8,128)(2,1)S(1)}, u32[]{:S(2)}, u32[]{:S(2)}) collective-permute-start(bf16[16,2048]{1,0:T(8,128)(2,1)S(1)} %get-tuple-element.36), channel_id=1, source_target_pairs={{0,8},{4,12},{8,0},{12,4},{1,9},{5,13},{9,1},{13,5},{2,10},{6,14},... | collective-permute-start | bytes 196616 | tf_op jit(solution)/shard_map/ppermute | solution.py:206
  37.6 5.8 %collective-permute-start.13 = (bf16[16,2048]{1,0:T(8,128)(2,1)S(1)}, bf16[16,2048]{1,0:T(8,128)(2,1)S(1)}, u32[]{:S(2)}, u32[]{:S(2)}) collective-permute-start(bf16[16,2048]{1,0:T(8,128)(2,1)S(1)} %get-tuple-element.37), channel_id=1, source_target_pairs={{0,8},{4,12},{8,0},{12,4},{1,9},{5,13},{9,1},{13,5},{2,10},{6,14},... | collective-permute-start | bytes 196616 | tf_op jit(solution)/shard_map/ppermute | solution.py:206
  38.7 9.3 %collective-permute-start.11 = (bf16[32,2048]{1,0:T(8,128)(2,1)S(1)}, bf16[32,2048]{1,0:T(8,128)(2,1)S(1)}, u32[]{:S(2)}, u32[]{:S(2)}) collective-permute-start(bf16[32,2048]{1,0:T(8,128)(2,1)S(1)} %get-tuple-element.35.refs_0_.attended), channel_id=1, source_target_pairs={{0,4},{4,0},{8,12},{12,8},{1,5},{5,1},{9,13},{13,9},{2,6},{6,2},{1... | collective-permute-start | bytes 393224 | tf_op jit(solution)/shard_map/ppermute | solution.py:206
  42.7 5.3 %collective-permute-start.14 = (bf16[16,2048]{1,0:T(8,128)(2,1)S(1)}, bf16[16,2048]{1,0:T(8,128)(2,1)S(1)}, u32[]{:S(2)}, u32[]{:S(2)}) collective-permute-start(bf16[16,2048]{1,0:T(8,128)(2,1)S(1)} %collective-permute-done.12.refs_2_), channel_id=1, source_target_pairs={{0,4},{4,0},{8,12},{12,8},{1,5},{5,1},{9,13},{13,9},{2,6},{6,2},{1... | collective-permute-start | bytes 196616 | tf_op jit(solution)/shard_map/ppermute | solution.py:206
  43.4 4.6 %collective-permute-start.15 = (bf16[16,2048]{1,0:T(8,128)(2,1)S(1)}, bf16[16,2048]{1,0:T(8,128)(2,1)S(1)}, u32[]{:S(2)}, u32[]{:S(2)}) collective-permute-start(bf16[16,2048]{1,0:T(8,128)(2,1)S(1)} %collective-permute-done.13.refs_3_), channel_id=1, source_target_pairs={{0,4},{4,0},{8,12},{12,8},{1,5},{5,1},{9,13},{13,9},{2,6},{6,2},{1... | collective-permute-start | bytes 196616 | tf_op jit(solution)/shard_map/ppermute | solution.py:206
  48.0 30.2 %copy-start = (bf16[32,4096]{1,0:T(8,128)(2,1)S(1)}, bf16[32,4096]{1,0:T(8,128)(2,1)}, u32[]{:S(2)}) copy-start(bf16[32,4096]{1,0:T(8,128)(2,1)} %hidden.1) | copy-start | bytes 786436
  50.1 3.8 %collective-permute-start.16 = (bf16[128,2048]{1,0:T(8,128)(2,1)S(1)}, bf16[128,2048]{1,0:T(8,128)(2,1)S(1)}, u32[]{:S(2)}, u32[]{:S(2)}) collective-permute-start(bf16[128,2048]{1,0:T(8,128)(2,1)S(1)} %get-tuple-element.40), channel_id=1, source_target_pairs={{1,0},{3,2},{5,4},{7,6},{9,8},{11,10},{13,12},{15,14},{17,16},{19,... | collective-permute-start | bytes 1572872 | tf_op jit(solution)/shard_map/ppermute | solution.py:628
  54.0 10.1 %collective-permute-start.17 = (bf16[32,2048]{1,0:T(8,128)(2,1)S(1)}, bf16[32,2048]{1,0:T(8,128)(2,1)S(1)}, u32[]{:S(2)}, u32[]{:S(2)}) collective-permute-start(bf16[32,2048]{1,0:T(8,128)(2,1)S(1)} %get-tuple-element.42), channel_id=1, source_target_pairs={{0,4},{4,0},{8,12},{12,8},{2,6},{6,2},{10,14},{14,10},{16,20},{20,... | collective-permute-start | bytes 393224 | tf_op jit(solution)/shard_map/ppermute | solution.py:638
  57.4 9.2 %collective-permute-start.18 = (bf16[32,2048]{1,0:T(8,128)(2,1)S(1)}, bf16[32,2048]{1,0:T(8,128)(2,1)S(1)}, u32[]{:S(2)}, u32[]{:S(2)}) collective-permute-start(bf16[32,2048]{1,0:T(8,128)(2,1)S(1)} %get-tuple-element.43), channel_id=1, source_target_pairs={{0,8},{4,12},{8,0},{12,4},{2,10},{6,14},{10,2},{14,6},{16,24},{20,... | collective-permute-start | bytes 393224 | tf_op jit(solution)/shard_map/ppermute | solution.py:638
  60.6 8.8 %collective-permute-start.19 = (bf16[32,2048]{1,0:T(8,128)(2,1)S(1)}, bf16[32,2048]{1,0:T(8,128)(2,1)S(1)}, u32[]{:S(2)}, u32[]{:S(2)}) collective-permute-start(bf16[32,2048]{1,0:T(8,128)(2,1)S(1)} %get-tuple-element.44), channel_id=1, source_target_pairs={{0,12},{4,8},{8,4},{12,0},{2,14},{6,10},{10,6},{14,2},{16,28},{20,... | collective-permute-start | bytes 393224 | tf_op jit(solution)/shard_map/ppermute | solution.py:638
  69.9 8.3 %collective-permute-start.20 = (bf16[2,32,2048]{2,1,0:T(8,128)(2,1)S(1)}, bf16[2,32,2048]{2,1,0:T(8,128)(2,1)S(1)}, u32[]{:S(2)}, u32[]{:S(2)}) collective-permute-start(bf16[2,32,2048]{2,1,0:T(8,128)(2,1)S(1)} %shard_map.91), channel_id=1, source_target_pairs={{0,2},{2,0},{4,6},{6,4},{8,10},{10,8},{12,14},{14,12},{16,18},{18,... | collective-permute-start | bytes 786440 | tf_op jit(solution)/shard_map/ppermute | solution.py:644
  73.7 2.3 %collective-permute-start.10 = (bf16[32,2048]{1,0:T(8,128)(2,1)S(1)}, bf16[32,2048]{1,0:T(8,128)(2,1)S(1)}, u32[]{:S(2)}, u32[]{:S(2)}) collective-permute-start(bf16[32,2048]{1,0:T(8,128)(2,1)S(1)} %get-tuple-element.35.refs_0_.attended), channel_id=1, source_target_pairs={{0,1},{2,3},{4,5},{6,7},{8,9},{10,11},{12,13},{14,15},{16,17},{18,... | collective-permute-start | bytes 393224 | tf_op jit(solution)/shard_map/ppermute | solution.py:616

commit v8 on v6

--- a/solution.py
+++ b/solution.py
@@ -294,7 +294,7 @@
     gains = gain[:, pl.ds(pl.multiple_of(side * depth, depth), depth)].astype(jnp.float32)
     values = jnp.concatenate([piece[...].astype(jnp.float32) for piece in pieces_in], axis=0)
     sums = pieces(jnp.sum(values * values, axis=1, keepdims=True))
-    chosen = one_hot(slots, scratch, blocks, place[2], place[1]).astype(jnp.bfloat16)
+    chosen = one_hot(slots, scratch, blocks, place[1], place[1]).astype(jnp.bfloat16)
     order = jnp.dot(
         chosen, (values * gains).astype(jnp.bfloat16), preferred_element_type=jnp.float32
     ).astype(jnp.bfloat16)
@@ -306,36 +306,34 @@
 def out_kernel(count, blocks, place, slots, *refs):
     pieces_in, (_, weight, give, permuted, scratch) = refs[:count], refs[count:]
     values = jnp.concatenate([piece[...] for piece in pieces_in], axis=0)
-    chosen = one_hot(slots, scratch, blocks, place[1], place[2]).T.astype(jnp.bfloat16)
+    chosen = one_hot(slots, scratch, blocks, place[1], place[1]).T.astype(jnp.bfloat16)
     order = jnp.dot(chosen, values, preferred_element_type=jnp.float32).astype(jnp.bfloat16)
     permuted[...] = order
     dot_columns(order, weight, give)
 
 
-def merge_kernel(own, given, received, *outs):
+def merge_kernel(count, own, given, received, *outs):
     rows = outs[0].shape[0]
     half = own.shape[1]
     more = given.shape[1] - half
-    for i, out in enumerate(outs):
+    for i, out in enumerate(outs[:count]):
         part = slice(i * rows, (i + 1) * rows)
         total = own[part, :] + received[part, :half].astype(jnp.float32)
-        out[:, :half] = total.astype(jnp.bfloat16)
-        if out.shape[1] > half:
-            out[:, half:] = jnp.concatenate(
-                [given[part, half : half + more // 2], received[part, half : half + more // 2]],
-                axis=1,
-            )
+        out[...] = total.astype(jnp.bfloat16)
+    for out in outs[count:]:
+        lanes = slice(half, half + more // 2)
+        out[...] = jnp.concatenate([given[:rows, lanes], received[:rows, lanes]], axis=1)
 
 
 def own_kernel(permuted, weight, own):
     dot_columns(permuted[...], weight, own)
 
 
-def project(kernel, place, slots, pieces_in, extra, weights, more, pairs):
+def project(kernel, place, slots, pieces_in, extra, weights, more):
     count = lax.axis_size("col")
     parts = len(pieces_in)
-    rows, depth = pieces_in[0].shape
-    rows = rows * parts
+    depth = pieces_in[0].shape[1]
+    rows = sum(part.shape[0] for part in pieces_in)
     half = weights[0].shape[1]
     flops = 2 * rows * depth * half
     give, permuted = call(
@@ -356,51 +354,89 @@
         flops,
         depth * half * 2,
     )(permuted, in_vmem(weights[1]))
-    return call(
-        merge_kernel,
-        [
-            struct((rows // count, half + (more if i % pairs == pairs - 1 else 0)))
-            for i in range(count)
-        ],
+    outs = [struct((rows // count, half))] * count
+    if more:
+        outs = outs + [struct((rows // count, more))]
+    merged = call(
+        functools.partial(merge_kernel, count),
+        outs,
         [VMEM] * 3,
-        [VMEM] * count,
+        [VMEM] * len(outs),
         rows * half,
         rows * half * 8,
     )(own, give, received)
-
-
-def gathered(parts, axis):
+    return merged[:count], merged[count:]
+
+
+def gathered(whole, parts, axis):
     blocks = {0: parts}
     mask = lax.axis_size(axis) // 2
     while mask:
-        blocks |= {
-            known | mask: [moved(part, axis, mask) for part in block]
-            for known, block in blocks.items()
-        }
+        arrived = {}
+        for known, block in blocks.items():
+            sent = [whole] if mask == 1 and known == 0 else block
+            arrived[known | mask] = [moved(part, axis, mask) for part in sent]
+        blocks |= arrived
         mask //= 2
+    blocks[0] = [whole]
     return [part for i in sorted(blocks) for part in blocks[i]]
 
 
 def spread(products):
-    col_count, row_count = lax.axis_size("col"), lax.axis_size("row")
-    pairs = col_count // row_count
-    order = sorted(range(col_count), key=lambda j: (-(j % pairs), -j))
-    sent = {
-        j: lax.ppermute(
-            products[j],
-            ("col", "row"),
-            [
-                (
-                    col * row_count + row,
-                    ((row * pairs + col % pairs) ^ j) * row_count + col // pairs,
-                )
-                for col in range(col_count)
-                for row in range(row_count)
-            ],
+    return [products[0]] + [
+        moved(products[mask], "col", mask) for mask in range(1, len(products))
+    ]
+
+
+def choose_kernel(count, other, place, *refs):
+    blocks, sums, out = refs[:count], refs[count:-1], refs[-1]
+    pairs = out.shape[0]
+    width = blocks[0].shape[1]
+    wanted = place[2] ^ other
+    for chunk in range(count // pairs):
+
+        @pl.when(wanted == chunk)
+        def _():
+            for pair in range(pairs):
+                out[pair, :, :width] = blocks[chunk * pairs + pair][...]
+
+    for ref in sums:
+        for pair in range(pairs):
+            out[pair, :, width:] = ref[...]
+
+
+def exchanged(place, blocks, sums):
+    row_count = lax.axis_size("row")
+    pairs = len(blocks) // row_count
+    rows, width = blocks[0].shape
+    width = width + sum(part.shape[1] for part in sums)
+    return [
+        moved(
+            call(
+                functools.partial(choose_kernel, len(blocks), mask),
+                struct((pairs, rows, width)),
+                [SMEM] + [VMEM] * (len(blocks) + len(sums)),
+                VMEM,
+                0,
+                pairs * rows * width * 4,
+            )(place, *blocks, *sums),
+            "row",
+            mask,
         )
-        for j in order
-    }
-    return [sent[j] for j in range(col_count)]
+        for mask in range(1, row_count)
+    ]
+
+
+def total_of(place, blocks, arrived, pair):
+    pairs, _, width = arrived[0].shape
+    width = min(width, blocks[0].shape[1])
+    total = jnp.zeros(blocks[0].shape, jnp.float32)
+    for chunk in range(len(blocks) // pairs):
+        part = blocks[chunk * pairs + pair][...].astype(jnp.float32)
+        total = total + jnp.where(place[2] == chunk, part, 0.0)
+    for ref in arrived:
+        total = total + ref[pair, :, :width].astype(jnp.float32)
+    return total
 
 
 def rotated(vector, cosine, sine):
@@ -420,16 +456,17 @@
     return jnp.cos(phases), jnp.where(lane < half, -sine, sine), length_of[:, :1]
 
 
-def attend_all(count, parts, place, lengths, *refs):
-    blocks, (keys, values), refs = refs[:count], refs[count : count + 2], refs[count + 2 :]
+def attend_all(count, others, parts, place, lengths, *refs):
+    blocks, own_sums, arrived = refs[:count], refs[count], refs[count + 1 : count + 1 + others]
+    keys, values, whole, *refs = refs[count + 1 + others :]
     outs, (scores_of, probs_of) = refs[:parts], refs[parts:]
     pairs = keys.shape[2] // HEAD_DIM
     rows, cache = keys.shape[:2]
     low = place[1] % pairs
     width = GROUP_WIDTH
-    squares = blocks[pairs - 1][:, width:].astype(jnp.float32)
-    for i in range(2 * pairs - 1, count, pairs):
-        squares = squares + blocks[i][:, width:].astype(jnp.float32)
+    squares = own_sums[...].astype(jnp.float32)
+    for ref in arrived:
+        squares = squares + ref[0, :, width:].astype(jnp.float32)
     scale = lax.rsqrt(jnp.sum(squares, axis=1, keepdims=True) / D + EPSILON)
     factor = HEAD_DIM ** (-0.5)
     cosines, sines, length_of = rope(lengths, rows)
@@ -440,9 +477,7 @@
     filled = [(position >= 0) & (position < length_of[part]) for part in runs]
     own, new_values, own_probs = [], [], []
     for pair in range(pairs):
-        total = blocks[pair][:, :width].astype(jnp.float32)
-        for i in range(pair + pairs, count, pairs):
-            total = total + blocks[i][:, :width].astype(jnp.float32)
+        total = total_of(place, blocks, arrived, pair)
         total = (total * scale).astype(jnp.bfloat16).astype(jnp.float32)
         heads = [total[:, h * HEAD_DIM : (h + 1) * HEAD_DIM] for h in range(GROUP + 2)]
         queries = [
@@ -493,24 +528,24 @@
                 joined = jnp.concatenate(
                     [result[head] for result in results[i * size : (i + 1) * size]], axis=0
                 )
-                out[:, pl.ds(at, HEAD_DIM)] = joined.astype(jnp.bfloat16)
-
-
-def sum_kernel(count, parts, place, hidden, *refs):
-    attended, blocks, (keep, send) = refs[:parts], refs[parts : parts + count], refs[parts + count :]
-    rows, width = blocks[0].shape
-    pairs = keep.shape[1] // width
+                joined = joined.astype(jnp.bfloat16)
+                out[:, pl.ds(at, HEAD_DIM)] = joined
+                run = slice(i * joined.shape[0], (i + 1) * joined.shape[0])
+                whole[run, pl.ds(at, HEAD_DIM)] = joined
+
+
+def sum_kernel(count, others, place, hidden, attended, *refs):
+    blocks, arrived, (keep, send) = refs[:count], refs[count : count + others], refs[-2:]
+    pairs, _, width = arrived[0].shape
     side = place[0]
     low = place[1] % pairs
     for pair in range(pairs):
         column = low ^ pair
-        total = blocks[pair][...].astype(jnp.float32)
-        for i in range(pair + pairs, count, pairs):
-            total = total + blocks[i][...].astype(jnp.float32)
+        total = total_of(place, blocks, arrived, pair)
         at = pl.ds(pl.multiple_of((2 * column + side) * width, width), width)
         hidden_out = (hidden[:, at].astype(jnp.float32) + total).astype(jnp.bfloat16)
         at = pl.ds(pl.multiple_of(column * width, width), width)
-        attention = jnp.concatenate([part[:, at] for part in attended], axis=0)
+        attention = attended[:, at]
         keep[:, at] = jnp.where(side == 0, hidden_out, attention)
         send[:, at] = jnp.where(side == 0, attention, hidden_out)
 
@@ -532,8 +567,8 @@
     col_count, row_count = lax.axis_size("col"), lax.axis_size("row")
     pairs = col_count // row_count
     side, col, row = (lax.axis_index(name) for name in ("side", "col", "row"))
-    run = row * pairs + lax.rem(col, pairs)
-    place = jnp.stack([side, col, run]).astype(jnp.int32)
+    base = lax.div(col, pairs) ^ row
+    place = jnp.stack([side, col, base]).astype(jnp.int32)
     rows, depth = hidden_in.shape
     half = depth // 2
     cache = key_cache.shape[1]
@@ -553,7 +588,7 @@
         [pltpu.SemaphoreType.DMA((2,))],
     )(place, in_hbm(qkv_weight), gain)
     blocks = gathered(
-        [own_part[i * piece : (i + 1) * piece] for i in range(parts)], "col"
+        own_part, [own_part[i * piece : (i + 1) * piece] for i in range(parts)], "col"
     )
     out_give, key_part, value_part = call(
         functools.partial(stage_out_kernel, True),
@@ -566,21 +601,23 @@
         [pltpu.SemaphoreType.DMA((3 * pairs,))],
     )(place, in_hbm(out_weight), in_hbm(key_cache), in_hbm(value_cache))
 
-    products = spread(
-        project(in_kernel, place, slot_request, blocks, [gain], weights_in, HEAD_DIM, pairs)
-    )
+    products, sums = project(
+        in_kernel, place, slot_request, blocks, [gain], weights_in, HEAD_DIM
+    )
+    products = spread(products)
+    arrived = exchanged(place, products, sums)
 
     key_part, value_part = in_vmem(key_part), in_vmem(value_part)
     runs = (pairs, rows // SLOTS, GROUP * SLOTS, SLOTS * cache)
-    attended = call(
-        functools.partial(attend_all, col_count, parts),
-        [struct((piece, half))] * parts,
-        [SMEM, SMEM] + [VMEM] * (col_count + 2),
-        [VMEM] * parts,
+    attended, *attended_parts = call(
+        functools.partial(attend_all, col_count, row_count - 1, parts),
+        [struct((rows, half))] + [struct((piece, half))] * parts,
+        [SMEM, SMEM] + [VMEM] * (col_count + row_count + 2),
+        [VMEM] * (parts + 1),
         4 * rows * half * cache,
         0,
         [pltpu.VMEM(runs, jnp.float32), pltpu.VMEM(runs, jnp.bfloat16)],
-    )(place, cache_lengths, *products, key_part, value_part)
+    )(place, cache_lengths, *products, *sums, *arrived, key_part, value_part)
 
     out_own = call(
         functools.partial(stage_out_kernel, False),
@@ -590,27 +627,26 @@
         0,
         half * half_out * 2,
         [pltpu.SemaphoreType.DMA((pairs,))],
-    )(place, in_hbm(out_weight), attended[-1])
-    products = spread(
-        project(
-            out_kernel,
-            place,
-            slot_request,
-            gathered(attended, "col"),
-            [in_vmem(out_own)],
-            [out_give, out_own],
-            0,
-            pairs,
-        )
-    )
+    )(place, in_hbm(out_weight), attended)
+    products, _ = project(
+        out_kernel,
+        place,
+        slot_request,
+        gathered(attended, attended_parts, "col"),
+        [in_vmem(out_own)],
+        [out_give, out_own],
+        0,
+    )
+    products = spread(products)
+    arrived = exchanged(place, products, [])
     keep, send = call(
-        functools.partial(sum_kernel, col_count, parts),
+        functools.partial(sum_kernel, col_count, row_count - 1),
         [struct((rows, half)), struct((rows, half))],
-        [SMEM] + [VMEM] * (1 + parts + col_count),
+        [SMEM] + [VMEM] * (2 + col_count + row_count - 1),
         [VMEM, VMEM],
         rows * depth * 4,
         rows * depth * 8,
-    )(place, hidden_in, *attended, *products)
+    )(place, hidden_in, attended, *products, *arrived)
     return call(
         join_kernel,
         struct((1, rows, depth)),
@@ -628,6 +664,7 @@
         lax.axis_size("side") == 2
         and qkv_weight.shape[1] == 2 * GROUP_WIDTH
         and col_count % row_count == 0
+        and row_count > 1
         and col_count & (col_count - 1) == 0
         and hidden_in.shape[0] % 32 == 0
         and key_cache.shape[1] % 16 == 0

time: 70.8 us -> 76.4 us (1.079)
  waiting for transfers between devices: 13.9 us -> 22.5 us
  starting transfers between devices: 34.6 us -> 29.6 us
  Pallas kernels: 20.1 us -> 21.3 us
  local copies, waits for them, and re-layouts: 1.6 us -> 2.52 us
    ppermute x8 -> x0, starting transfers between devices: 19.2 us -> none  [spread(): lax.ppermute(products[j], ('col', 'row'), [(col * row_count + row, (row *...]
    ppermute x15 -> x21, waiting for transfers between devices: 7.91 us -> 22.5 us  [moved(): return lax.ppermute(value, axis, pairs)]
    ppermute x15 -> x21, starting transfers between devices: 15.5 us -> 29.6 us  [moved(): return lax.ppermute(value, axis, pairs)]
    ppermute x8 -> x0, waiting for transfers between devices: 6 us -> none  [spread(): lax.ppermute(products[j], ('col', 'row'), [(col * row_count + row, (row *...]
    pallas_call x4 -> x6, Pallas kernels: 3.01 us -> 4.2 us  [the longest x1 2.3 us: paired_plan(): call(functools.partial(attend_all, col_count, row_count - 1, parts), [str...]
    dynamic_slice x0 -> x1, local copies, waits for them, and re-layouts: none -> 0.91 us  [paired_plan(): own_part = lax.dynamic_slice_in_dim(hidden_in, side * half, half, 1)]
  transfers between devices with their start and end apart: 23 -> 21, of which waited for: 10 -> 12; matrix products, arithmetic and copies ran while one was open for 1% -> 2% of each run, Pallas kernels for 18% -> 16%
where the time goes in v8:
time: 76.4 us; the launch traced here: 76.2 us
  starting transfers between devices  29.6 us (39%)
  waiting for transfers between devices  22.5 us (29%)
  Pallas kernels  21.3 us (28%)
  local copies, waits for them, and re-layouts  2.52 us (3%)
    ppermute x21, starting transfers between devices, moved(): return lax.ppermute(value, axis, pairs)  29.6 us
    ppermute x21, waiting for transfers between devices, moved(): return lax.ppermute(value, axis, pairs)  22.5 us
    pallas_call x1, Pallas kernels, paired_plan(): call(stage_in_kernel, [pltpu.VMEM((half, half_in), jnp.bfloat16)] * 2, [S...  4.62 us
    pallas_call x1, Pallas kernels, paired_plan(): call(functools.partial(stage_out_kernel, True), [pltpu.VMEM((half, half_o...  3.54 us
    pallas_call x2, Pallas kernels, project(): call(functools.partial(kernel, parts, count), [struct((rows, half + more)...  3.26 us
    pallas_call x1, Pallas kernels, paired_plan(): call(functools.partial(stage_out_kernel, False), pltpu.VMEM((half, half_o...  2.78 us
    pallas_call x1, Pallas kernels, paired_plan(): call(functools.partial(attend_all, col_count, row_count - 1, parts), [str...  2.3 us
    pallas_call x2, Pallas kernels, project(): call(own_kernel, struct((rows, half), jnp.float32), [VMEM, VMEM], VMEM, f...  1.6 us
  transfers between devices with their start and end apart: 21, of which 12 were waited for; matrix products, arithmetic and copies ran while one was open for 2% of the time, Pallas kernels for 16%

profile of v8, /device:TPU:0, one launch (start us, length us, event | category | flops | bytes accessed | tf_op | source)
XLA Modules:
  0.0 76.2 jit_solution(10648591389025965794)
XLA Ops:
  0.0 0.9 %fusion = (bf16[16,2048]{1,0:T(8,128)(2,1)S(1)}, bf16[16,2048]{1,0:T(8,128)(2,1)S(1)}) fusion(bf16[32,4096]{1,0:T(8,128)(2,1)} %hidden.1, s32[]{:T(128)S(6)} %add.6, s32[]{:T(128)S(6)} %select_n.3), kind=kLoop, calls=%fused_computation.3 | loop fusion | bytes 262152 | tf_op jit(solution)/shard_map/slice | solution.py:591
  0.9 4.1 %collective-permute-start.1 = (bf16[16,2048]{1,0:T(8,128)(2,1)S(1)}, bf16[16,2048]{1,0:T(8,128)(2,1)S(1)}, u32[]{:S(2)}, u32[]{:S(2)}) collective-permute-start(bf16[16,2048]{1,0:T(8,128)(2,1)S(1)} %get-tuple-element.52), channel_id=1, source_target_pairs={{0,8},{4,12},{8,0},{12,4},{1,9},{5,13},{9,1},{13,5},{2,10},{6,14},... | collective-permute-start | bytes 196616 | tf_op jit(solution)/shard_map/ppermute | solution.py:206
  5.0 0.1 collective-permute-start.2
  5.1 0.9 %constant_dynamic-slice_fusion.1.refs_0_ = bf16[32,2048]{1,0:T(8,128)(2,1)S(1)} fusion(bf16[32,4096]{1,0:T(8,128)(2,1)} %hidden.1, s32[]{:T(128)S(6)} %select_n.3), kind=kLoop, calls=%fused_computation.2 | loop fusion | bytes 262148 | tf_op jit(solution)/shard_map/dynamic_slice | solution.py:578
  6.0 1.9 %collective-permute-start = (bf16[32,2048]{1,0:T(8,128)(2,1)S(1)}, bf16[32,2048]{1,0:T(8,128)(2,1)S(1)}, u32[]{:S(2)}, u32[]{:S(2)}) collective-permute-start(bf16[32,2048]{1,0:T(8,128)(2,1)S(1)} %constant_dynamic-slice_fusion.1.refs_0_), channel_id=1, source_target_pairs={{0,4},{4,0},{8,12},{12,8},{1,5},{5,1},{9,13},{13,9},{2,6},{6,2},{1... | collective-permute-start | bytes 393224 | tf_op jit(solution)/shard_map/ppermute | solution.py:206
  7.9 0.7 reshape.3.gain.refs_6_
  8.6 0.1 collective-permute-done.1.refs_2_
  8.7 2.0 %collective-permute-start.3 = (bf16[16,2048]{1,0:T(8,128)(2,1)S(1)}, bf16[16,2048]{1,0:T(8,128)(2,1)S(1)}, u32[]{:S(2)}, u32[]{:S(2)}) collective-permute-start(bf16[16,2048]{1,0:T(8,128)(2,1)S(1)} %collective-permute-done.1.refs_2_), channel_id=1, source_target_pairs={{0,4},{4,0},{8,12},{12,8},{1,5},{5,1},{9,13},{13,9},{2,6},{6,2},{1... | collective-permute-start | bytes 196616 | tf_op jit(solution)/shard_map/ppermute | solution.py:206
  10.7 0.3 collective-permute-done.2.refs_3_
  11.0 1.4 %collective-permute-start.4 = (bf16[16,2048]{1,0:T(8,128)(2,1)S(1)}, bf16[16,2048]{1,0:T(8,128)(2,1)S(1)}, u32[]{:S(2)}, u32[]{:S(2)}) collective-permute-start(bf16[16,2048]{1,0:T(8,128)(2,1)S(1)} %collective-permute-done.2.refs_3_), channel_id=1, source_target_pairs={{0,4},{4,0},{8,12},{12,8},{1,5},{5,1},{9,13},{13,9},{2,6},{6,2},{1... | collective-permute-start | bytes 196616 | tf_op jit(solution)/shard_map/ppermute | solution.py:206
  12.4 0.1 pad_add_fusion.place
  12.5 4.6 %shard_map.82 = (bf16[2048,1280]{1,0:T(8,128)(2,1)S(1)}, bf16[2048,1280]{1,0:T(8,128)(2,1)S(1)}) custom-call(s32[3]{0:T(128)S(1)} %pad_add_fusion.place, bf16[4096,2560]{1,0:T(8,128)(2,1)} %weight.3, bf16[1,4096]{1,0:T(2,128)(2,1)S(1)} %reshape.3.gain.refs_6_), custom_call_target="tpu_custom_call" | custom-call | bytes 10485760 | tf_op jit(solution)/shard_map/pallas_call | solution.py:581
  17.2 1.7 %shard_map.83 = (bf16[128,1408]{1,0:T(8,128)(2,1)S(1)}, bf16[128,2048]{1,0:T(8,128)(2,1)S(1)}) custom-call(s32[3]{0:T(128)S(1)} %pad_add_fusion.place, s32[128]{0:T(128)S(1)} %copy-done.1, bf16[32,2048]{1,0:T(8,128)(2,1)S(1)} %constant_dynamic-slice_fusion.1.refs_0_, bf16[32,2048]{1,0:T(8,128)(2,1)S(1)} %collective-permute-done.refs_1_, ...), custom_call_target="tpu_custom_call" | custom-call | flops 671088640 | bytes 5242880 | tf_op jit(solution)/shard_map/pallas_call | solution.py:339
  18.9 0.1 collective-permute-start.5
  19.0 0.9 %shard_map.84.own = f32[128,1280]{1,0:T(8,128)S(1)} custom-call(bf16[128,2048]{1,0:T(8,128)(2,1)S(1)} %get-tuple-element.29.permuted, bf16[2048,1280]{1,0:T(8,128)(2,1)S(1)} %get-tuple-element.30.weight), custom_call_target="tpu_custom_call" | custom-call | flops 671088640 | bytes 5242880 | tf_op jit(solution)/shard_map/pallas_call | solution.py:349
  19.9 0.8 %collective-permute-done.5.received = bf16[128,1408]{1,0:T(8,128)(2,1)S(1)} collective-permute-done((bf16[128,1408]{1,0:T(8,128)(2,1)S(1)}, bf16[128,1408]{1,0:T(8,128)(2,1)S(1)}, u32[]{:S(2)}, u32[]{:S(2)}) %collective-permute-start.5) | collective-permute-done | bytes 360480 | tf_op jit(solution)/shard_map/ppermute | solution.py:206
  20.7 0.1 shard_map.85
  20.7 0.7 collective-permute-start.6
  21.4 3.2 %collective-permute-start.7 = (bf16[32,1280]{1,0:T(8,128)(2,1)S(1)}, bf16[32,1280]{1,0:T(8,128)(2,1)S(1)}, u32[]{:S(2)}, u32[]{:S(2)}) collective-permute-start(bf16[32,1280]{1,0:T(8,128)(2,1)S(1)} %get-tuple-element.34), channel_id=1, source_target_pairs={{0,8},{4,12},{8,0},{12,4},{1,9},{5,13},{9,1},{13,5},{2,10},{6,14},... | collective-permute-start | bytes 245768 | tf_op jit(solution)/shard_map/ppermute | solution.py:206
  24.6 0.7 collective-permute-start.8
  25.3 1.9 %collective-permute-done.7.refs_2_ = bf16[32,1280]{1,0:T(8,128)(2,1)S(1)} collective-permute-done((bf16[32,1280]{1,0:T(8,128)(2,1)S(1)}, bf16[32,1280]{1,0:T(8,128)(2,1)S(1)}, u32[]{:S(2)}, u32[]{:S(2)}) %collective-permute-start.7) | collective-permute-done | bytes 81952 | tf_op jit(solution)/shard_map/ppermute | solution.py:206
  27.2 4.2 %collective-permute-done.8.refs_3_ = bf16[32,1280]{1,0:T(8,128)(2,1)S(1)} collective-permute-done((bf16[32,1280]{1,0:T(8,128)(2,1)S(1)}, bf16[32,1280]{1,0:T(8,128)(2,1)S(1)}, u32[]{:S(2)}, u32[]{:S(2)}) %collective-permute-start.8) | collective-permute-done | bytes 81952 | tf_op jit(solution)/shard_map/ppermute | solution.py:206
  31.4 0.6 shard_map.86
  32.0 1.6 %collective-permute-start.9 = (bf16[2,32,1408]{2,1,0:T(8,128)(2,1)S(1)}, bf16[2,32,1408]{2,1,0:T(8,128)(2,1)S(1)}, u32[]{:S(2)}, u32[]{:S(2)}) collective-permute-start(bf16[2,32,1408]{2,1,0:T(8,128)(2,1)S(1)} %shard_map.86), channel_id=1, source_target_pairs={{0,2},{2,0},{1,3},{3,1},{4,6},{6,4},{5,7},{7,5},{8,10},{10,8},{9,1... | collective-permute-start | bytes 540680 | tf_op jit(solution)/shard_map/ppermute | solution.py:206
  33.5 3.5 %shard_map.87 = (bf16[2048,1024]{1,0:T(8,128)(2,1)S(1)}, bf16[32,64,256]{2,1,0:T(8,128)(2,1)S(1)}, bf16[32,64,256]{2,1,0:T(8,128)(2,1)S(1)}) custom-call(s32[3]{0:T(128)S(1)} %pad_add_fusion.place, bf16[4096,2048]{1,0:T(8,128)(2,1)} %weight.5, bf16[32,64,512]{2,1,0:T(8,128)(2,1)} %refs_0_.1, bf16[32,64,512]{2,1,0:T(8,128)(2,1)} %refs_1_.1), custom_call_target="tpu_custom_call" | custom-call | bytes 6291456 | tf_op jit(solution)/shard_map/pallas_call | solution.py:593
  37.1 0.7 collective-permute-done.9.refs_5_
  37.8 2.3 %shard_map.88 = (bf16[32,2048]{1,0:T(8,128)(2,1)S(1)}, bf16[16,2048]{1,0:T(8,128)(2,1)S(1)}, bf16[16,2048]{1,0:T(8,128)(2,1)S(1)}) custom-call(s32[3]{0:T(128)S(1)} %pad_add_fusion.place, s32[32]{0:T(128)S(1)} %copy-done.2, bf16[32,1280]{1,0:T(8,128)(2,1)S(1)} %get-tuple-element.32.refs_0_, bf16[32,1280]{1,0:T(8,128)(2,1)S(1)} %collective-permute-done.6.refs_1_, ...), custom_call_target="tpu_custom_call" | custom-call | flops 16777216 | tf_op jit(solution)/shard_map/pallas_call | solution.py:612
  40.1 4.1 %collective-permute-start.11 = (bf16[16,2048]{1,0:T(8,128)(2,1)S(1)}, bf16[16,2048]{1,0:T(8,128)(2,1)S(1)}, u32[]{:S(2)}, u32[]{:S(2)}) collective-permute-start(bf16[16,2048]{1,0:T(8,128)(2,1)S(1)} %get-tuple-element.40), channel_id=1, source_target_pairs={{0,8},{4,12},{8,0},{12,4},{1,9},{5,13},{9,1},{13,5},{2,10},{6,14},... | collective-permute-start | bytes 196616 | tf_op jit(solution)/shard_map/ppermute | solution.py:206
  44.1 1.0 %collective-permute-start.12 = (bf16[16,2048]{1,0:T(8,128)(2,1)S(1)}, bf16[16,2048]{1,0:T(8,128)(2,1)S(1)}, u32[]{:S(2)}, u32[]{:S(2)}) collective-permute-start(bf16[16,2048]{1,0:T(8,128)(2,1)S(1)} %get-tuple-element.41), channel_id=1, source_target_pairs={{0,8},{4,12},{8,0},{12,4},{1,9},{5,13},{9,1},{13,5},{2,10},{6,14},... | collective-permute-start | bytes 196616 | tf_op jit(solution)/shard_map/ppermute | solution.py:206
  45.1 1.9 %collective-permute-done.11.refs_2_ = bf16[16,2048]{1,0:T(8,128)(2,1)S(1)} collective-permute-done((bf16[16,2048]{1,0:T(8,128)(2,1)S(1)}, bf16[16,2048]{1,0:T(8,128)(2,1)S(1)}, u32[]{:S(2)}, u32[]{:S(2)}) %collective-permute-start.11) | collective-permute-done | bytes 65568 | tf_op jit(solution)/shard_map/ppermute | solution.py:206
  47.1 0.8 %collective-permute-start.13 = (bf16[16,2048]{1,0:T(8,128)(2,1)S(1)}, bf16[16,2048]{1,0:T(8,128)(2,1)S(1)}, u32[]{:S(2)}, u32[]{:S(2)}) collective-permute-start(bf16[16,2048]{1,0:T(8,128)(2,1)S(1)} %collective-permute-done.11.refs_2_), channel_id=1, source_target_pairs={{0,4},{4,0},{8,12},{12,8},{1,5},{5,1},{9,13},{13,9},{2,6},{6,2},{1... | collective-permute-start | bytes 196616 | tf_op jit(solution)/shard_map/ppermute | solution.py:206
  47.9 1.7 %collective-permute-done.12.refs_3_ = bf16[16,2048]{1,0:T(8,128)(2,1)S(1)} collective-permute-done((bf16[16,2048]{1,0:T(8,128)(2,1)S(1)}, bf16[16,2048]{1,0:T(8,128)(2,1)S(1)}, u32[]{:S(2)}, u32[]{:S(2)}) %collective-permute-start.12) | collective-permute-done | bytes 65568 | tf_op jit(solution)/shard_map/ppermute | solution.py:206
  49.6 1.8 %collective-permute-start.14 = (bf16[16,2048]{1,0:T(8,128)(2,1)S(1)}, bf16[16,2048]{1,0:T(8,128)(2,1)S(1)}, u32[]{:S(2)}, u32[]{:S(2)}) collective-permute-start(bf16[16,2048]{1,0:T(8,128)(2,1)S(1)} %collective-permute-done.12.refs_3_), channel_id=1, source_target_pairs={{0,4},{4,0},{8,12},{12,8},{1,5},{5,1},{9,13},{13,9},{2,6},{6,2},{1... | collective-permute-start | bytes 196616 | tf_op jit(solution)/shard_map/ppermute | solution.py:206
  51.4 2.8 %shard_map.89.refs_6_.weight = bf16[2048,1024]{1,0:T(8,128)(2,1)S(1)} custom-call(s32[3]{0:T(128)S(1)} %pad_add_fusion.place, bf16[4096,2048]{1,0:T(8,128)(2,1)} %weight.5, bf16[32,2048]{1,0:T(8,128)(2,1)S(1)} %get-tuple-element.39.refs_0_.attended), custom_call_target="tpu_custom_call" | custom-call | bytes 4194304 | tf_op jit(solution)/shard_map/pallas_call | solution.py:622
  54.2 1.5 %shard_map.90 = (bf16[128,1024]{1,0:T(8,128)(2,1)S(1)}, bf16[128,2048]{1,0:T(8,128)(2,1)S(1)}) custom-call(s32[3]{0:T(128)S(1)} %pad_add_fusion.place, s32[128]{0:T(128)S(1)} %copy-done.1, bf16[32,2048]{1,0:T(8,128)(2,1)S(1)} %get-tuple-element.39.refs_0_.attended, bf16[32,2048]{1,0:T(8,128)(2,1)S(1)} %collective-permute-done.10.refs_1_, ...), custom_call_target="tpu_custom_call" | custom-call | flops 536870912 | bytes 4194304 | tf_op jit(solution)/shard_map/pallas_call | solution.py:339
  55.8 0.1 collective-permute-start.15
  55.9 0.7 shard_map.91.own
  56.6 0.8 %collective-permute-done.15.received = bf16[128,1024]{1,0:T(8,128)(2,1)S(1)} collective-permute-done((bf16[128,1024]{1,0:T(8,128)(2,1)S(1)}, bf16[128,1024]{1,0:T(8,128)(2,1)S(1)}, u32[]{:S(2)}, u32[]{:S(2)}) %collective-permute-start.15) | collective-permute-done | bytes 262176 | tf_op jit(solution)/shard_map/ppermute | solution.py:206
  57.4 1.5 %collective-permute-start.16 = (bf16[32,1024]{1,0:T(8,128)(2,1)S(1)}, bf16[32,1024]{1,0:T(8,128)(2,1)S(1)}, u32[]{:S(2)}, u32[]{:S(2)}) collective-permute-start(bf16[32,1024]{1,0:T(8,128)(2,1)S(1)} %get-tuple-element.46), channel_id=1, source_target_pairs={{0,4},{4,0},{8,12},{12,8},{1,5},{5,1},{9,13},{13,9},{2,6},{6,2},{1... | collective-permute-start | bytes 196616 | tf_op jit(solution)/shard_map/ppermute | solution.py:206
  58.9 2.1 %collective-permute-start.17 = (bf16[32,1024]{1,0:T(8,128)(2,1)S(1)}, bf16[32,1024]{1,0:T(8,128)(2,1)S(1)}, u32[]{:S(2)}, u32[]{:S(2)}) collective-permute-start(bf16[32,1024]{1,0:T(8,128)(2,1)S(1)} %get-tuple-element.47), channel_id=1, source_target_pairs={{0,8},{4,12},{8,0},{12,4},{1,9},{5,13},{9,1},{13,5},{2,10},{6,14},... | collective-permute-start | bytes 196616 | tf_op jit(solution)/shard_map/ppermute | solution.py:206
  61.1 0.9 %collective-permute-start.18 = (bf16[32,1024]{1,0:T(8,128)(2,1)S(1)}, bf16[32,1024]{1,0:T(8,128)(2,1)S(1)}, u32[]{:S(2)}, u32[]{:S(2)}) collective-permute-start(bf16[32,1024]{1,0:T(8,128)(2,1)S(1)} %get-tuple-element.48), channel_id=1, source_target_pairs={{0,12},{4,8},{8,4},{12,0},{1,13},{5,9},{9,5},{13,1},{2,14},{6,10},... | collective-permute-start | bytes 196616 | tf_op jit(solution)/shard_map/ppermute | solution.py:206
  62.0 5.3 %collective-permute-done.17.refs_2_ = bf16[32,1024]{1,0:T(8,128)(2,1)S(1)} collective-permute-done((bf16[32,1024]{1,0:T(8,128)(2,1)S(1)}, bf16[32,1024]{1,0:T(8,128)(2,1)S(1)}, u32[]{:S(2)}, u32[]{:S(2)}) %collective-permute-start.17) | collective-permute-done | bytes 65568 | tf_op jit(solution)/shard_map/ppermute | solution.py:206
  67.2 0.6 shard_map.93
  67.8 1.6 %collective-permute-start.19 = (bf16[2,32,1024]{2,1,0:T(8,128)(2,1)S(1)}, bf16[2,32,1024]{2,1,0:T(8,128)(2,1)S(1)}, u32[]{:S(2)}, u32[]{:S(2)}) collective-permute-start(bf16[2,32,1024]{2,1,0:T(8,128)(2,1)S(1)} %shard_map.93), channel_id=1, source_target_pairs={{0,2},{2,0},{1,3},{3,1},{4,6},{6,4},{5,7},{7,5},{8,10},{10,8},{9,1... | collective-permute-start | bytes 393224 | tf_op jit(solution)/shard_map/ppermute | solution.py:206
  69.4 3.5 %collective-permute-done.19.refs_4_ = bf16[2,32,1024]{2,1,0:T(8,128)(2,1)S(1)} collective-permute-done((bf16[2,32,1024]{2,1,0:T(8,128)(2,1)S(1)}, bf16[2,32,1024]{2,1,0:T(8,128)(2,1)S(1)}, u32[]{:S(2)}, u32[]{:S(2)}) %collective-permute-start.19) | collective-permute-done | bytes 131104 | tf_op jit(solution)/shard_map/ppermute | solution.py:206
  72.8 0.7 shard_map.94
  73.6 1.3 %collective-permute-done.20.received = bf16[32,2048]{1,0:T(8,128)(2,1)S(1)} collective-permute-done((bf16[32,2048]{1,0:T(8,128)(2,1)S(1)}, bf16[32,2048]{1,0:T(8,128)(2,1)S(1)}, u32[]{:S(2)}, u32[]{:S(2)}) %collective-permute-start.20) | collective-permute-done | bytes 131104 | tf_op jit(solution)/shard_map/ppermute | solution.py:206
  74.9 1.3 %shard_map.95 = bf16[1,32,4096]{2,1,0:T(8,128)(2,1)} custom-call(s32[3]{0:T(128)S(1)} %pad_add_fusion.place, bf16[32,2048]{1,0:T(8,128)(2,1)S(1)} %get-tuple-element.49.keep, bf16[32,2048]{1,0:T(8,128)(2,1)S(1)} %collective-permute-done.20.received), custom_call_target="tpu_custom_call" | custom-call | bytes 524288 | tf_op jit(solution)/shard_map/pallas_call | solution.py:650
  (18 shorter events, 0.2 us)
Async XLA Ops:
  0.9 7.9 %collective-permute-start.1 = (bf16[16,2048]{1,0:T(8,128)(2,1)S(1)}, bf16[16,2048]{1,0:T(8,128)(2,1)S(1)}, u32[]{:S(2)}, u32[]{:S(2)}) collective-permute-start(bf16[16,2048]{1,0:T(8,128)(2,1)S(1)} %get-tuple-element.52), channel_id=1, source_target_pairs={{0,8},{4,12},{8,0},{12,4},{1,9},{5,13},{9,1},{13,5},{2,10},{6,14},... | collective-permute-start | bytes 196616 | tf_op jit(solution)/shard_map/ppermute | solution.py:206
  5.0 6.0 %collective-permute-start.2 = (bf16[16,2048]{1,0:T(8,128)(2,1)S(1)}, bf16[16,2048]{1,0:T(8,128)(2,1)S(1)}, u32[]{:S(2)}, u32[]{:S(2)}) collective-permute-start(bf16[16,2048]{1,0:T(8,128)(2,1)S(1)} %get-tuple-element.51), channel_id=1, source_target_pairs={{0,8},{4,12},{8,0},{12,4},{1,9},{5,13},{9,1},{13,5},{2,10},{6,14},... | collective-permute-start | bytes 196616 | tf_op jit(solution)/shard_map/ppermute | solution.py:206
  6.0 11.2 %collective-permute-start = (bf16[32,2048]{1,0:T(8,128)(2,1)S(1)}, bf16[32,2048]{1,0:T(8,128)(2,1)S(1)}, u32[]{:S(2)}, u32[]{:S(2)}) collective-permute-start(bf16[32,2048]{1,0:T(8,128)(2,1)S(1)} %constant_dynamic-slice_fusion.1.refs_0_), channel_id=1, source_target_pairs={{0,4},{4,0},{8,12},{12,8},{1,5},{5,1},{9,13},{13,9},{2,6},{6,2},{1... | collective-permute-start | bytes 393224 | tf_op jit(solution)/shard_map/ppermute | solution.py:206
  8.7 8.4 %collective-permute-start.3 = (bf16[16,2048]{1,0:T(8,128)(2,1)S(1)}, bf16[16,2048]{1,0:T(8,128)(2,1)S(1)}, u32[]{:S(2)}, u32[]{:S(2)}) collective-permute-start(bf16[16,2048]{1,0:T(8,128)(2,1)S(1)} %collective-permute-done.1.refs_2_), channel_id=1, source_target_pairs={{0,4},{4,0},{8,12},{12,8},{1,5},{5,1},{9,13},{13,9},{2,6},{6,2},{1... | collective-permute-start | bytes 196616 | tf_op jit(solution)/shard_map/ppermute | solution.py:206
  11.0 6.1 %collective-permute-start.4 = (bf16[16,2048]{1,0:T(8,128)(2,1)S(1)}, bf16[16,2048]{1,0:T(8,128)(2,1)S(1)}, u32[]{:S(2)}, u32[]{:S(2)}) collective-permute-start(bf16[16,2048]{1,0:T(8,128)(2,1)S(1)} %collective-permute-done.2.refs_3_), channel_id=1, source_target_pairs={{0,4},{4,0},{8,12},{12,8},{1,5},{5,1},{9,13},{13,9},{2,6},{6,2},{1... | collective-permute-start | bytes 196616 | tf_op jit(solution)/shard_map/ppermute | solution.py:206
  12.5 4.7 %copy-start.1 = (s32[128]{0:T(128)S(1)}, s32[128]{0:T(128)}, u32[]{:S(2)}) copy-start(s32[128]{0:T(128)} %slots.3) | copy-start | bytes 1540
  18.9 1.7 %collective-permute-start.5 = (bf16[128,1408]{1,0:T(8,128)(2,1)S(1)}, bf16[128,1408]{1,0:T(8,128)(2,1)S(1)}, u32[]{:S(2)}, u32[]{:S(2)}) collective-permute-start(bf16[128,1408]{1,0:T(8,128)(2,1)S(1)} %get-tuple-element.31.given), channel_id=1, source_target_pairs={{0,1},{1,0},{2,3},{3,2},{4,5},{5,4},{6,7},{7,6},{8,9},{9,8},{10,11... | collective-permute-start | bytes 1081352 | tf_op jit(solution)/shard_map/ppermute | solution.py:206
  20.7 4.6 %collective-permute-start.6 = (bf16[32,1280]{1,0:T(8,128)(2,1)S(1)}, bf16[32,1280]{1,0:T(8,128)(2,1)S(1)}, u32[]{:S(2)}, u32[]{:S(2)}) collective-permute-start(bf16[32,1280]{1,0:T(8,128)(2,1)S(1)} %get-tuple-element.33), channel_id=1, source_target_pairs={{0,4},{4,0},{8,12},{12,8},{1,5},{5,1},{9,13},{13,9},{2,6},{6,2},{1... | collective-permute-start | bytes 245768 | tf_op jit(solution)/shard_map/ppermute | solution.py:206
  21.4 5.8 %collective-permute-start.7 = (bf16[32,1280]{1,0:T(8,128)(2,1)S(1)}, bf16[32,1280]{1,0:T(8,128)(2,1)S(1)}, u32[]{:S(2)}, u32[]{:S(2)}) collective-permute-start(bf16[32,1280]{1,0:T(8,128)(2,1)S(1)} %get-tuple-element.34), channel_id=1, source_target_pairs={{0,8},{4,12},{8,0},{12,4},{1,9},{5,13},{9,1},{13,5},{2,10},{6,14},... | collective-permute-start | bytes 245768 | tf_op jit(solution)/shard_map/ppermute | solution.py:206
  24.6 6.8 %collective-permute-start.8 = (bf16[32,1280]{1,0:T(8,128)(2,1)S(1)}, bf16[32,1280]{1,0:T(8,128)(2,1)S(1)}, u32[]{:S(2)}, u32[]{:S(2)}) collective-permute-start(bf16[32,1280]{1,0:T(8,128)(2,1)S(1)} %get-tuple-element.35), channel_id=1, source_target_pairs={{0,12},{4,8},{8,4},{12,0},{1,13},{5,9},{9,5},{13,1},{2,14},{6,10},... | collective-permute-start | bytes 245768 | tf_op jit(solution)/shard_map/ppermute | solution.py:206
  32.0 5.8 %copy-start.2 = (s32[32]{0:T(128)S(1)}, s32[32]{0:T(128)}, u32[]{:S(2)}) copy-start(s32[32]{0:T(128)} %lengths.1) | copy-start | bytes 388
  32.0 5.8 %collective-permute-start.9 = (bf16[2,32,1408]{2,1,0:T(8,128)(2,1)S(1)}, bf16[2,32,1408]{2,1,0:T(8,128)(2,1)S(1)}, u32[]{:S(2)}, u32[]{:S(2)}) collective-permute-start(bf16[2,32,1408]{2,1,0:T(8,128)(2,1)S(1)} %shard_map.86), channel_id=1, source_target_pairs={{0,2},{2,0},{1,3},{3,1},{4,6},{6,4},{5,7},{7,5},{8,10},{10,8},{9,1... | collective-permute-start | bytes 540680 | tf_op jit(solution)/shard_map/ppermute | solution.py:206
  40.1 7.0 %collective-permute-start.11 = (bf16[16,2048]{1,0:T(8,128)(2,1)S(1)}, bf16[16,2048]{1,0:T(8,128)(2,1)S(1)}, u32[]{:S(2)}, u32[]{:S(2)}) collective-permute-start(bf16[16,2048]{1,0:T(8,128)(2,1)S(1)} %get-tuple-element.40), channel_id=1, source_target_pairs={{0,8},{4,12},{8,0},{12,4},{1,9},{5,13},{9,1},{13,5},{2,10},{6,14},... | collective-permute-start | bytes 196616 | tf_op jit(solution)/shard_map/ppermute | solution.py:206
  44.1 10.1 %collective-permute-start.10 = (bf16[32,2048]{1,0:T(8,128)(2,1)S(1)}, bf16[32,2048]{1,0:T(8,128)(2,1)S(1)}, u32[]{:S(2)}, u32[]{:S(2)}) collective-permute-start(bf16[32,2048]{1,0:T(8,128)(2,1)S(1)} %get-tuple-element.39.refs_0_.attended), channel_id=1, source_target_pairs={{0,4},{4,0},{8,12},{12,8},{1,5},{5,1},{9,13},{13,9},{2,6},{6,2},{1... | collective-permute-start | bytes 393224 | tf_op jit(solution)/shard_map/ppermute | solution.py:206
  44.1 5.5 %collective-permute-start.12 = (bf16[16,2048]{1,0:T(8,128)(2,1)S(1)}, bf16[16,2048]{1,0:T(8,128)(2,1)S(1)}, u32[]{:S(2)}, u32[]{:S(2)}) collective-permute-start(bf16[16,2048]{1,0:T(8,128)(2,1)S(1)} %get-tuple-element.41), channel_id=1, source_target_pairs={{0,8},{4,12},{8,0},{12,4},{1,9},{5,13},{9,1},{13,5},{2,10},{6,14},... | collective-permute-start | bytes 196616 | tf_op jit(solution)/shard_map/ppermute | solution.py:206
  47.1 7.2 %collective-permute-start.13 = (bf16[16,2048]{1,0:T(8,128)(2,1)S(1)}, bf16[16,2048]{1,0:T(8,128)(2,1)S(1)}, u32[]{:S(2)}, u32[]{:S(2)}) collective-permute-start(bf16[16,2048]{1,0:T(8,128)(2,1)S(1)} %collective-permute-done.11.refs_2_), channel_id=1, source_target_pairs={{0,4},{4,0},{8,12},{12,8},{1,5},{5,1},{9,13},{13,9},{2,6},{6,2},{1... | collective-permute-start | bytes 196616 | tf_op jit(solution)/shard_map/ppermute | solution.py:206
  49.6 4.6 %collective-permute-start.14 = (bf16[16,2048]{1,0:T(8,128)(2,1)S(1)}, bf16[16,2048]{1,0:T(8,128)(2,1)S(1)}, u32[]{:S(2)}, u32[]{:S(2)}) collective-permute-start(bf16[16,2048]{1,0:T(8,128)(2,1)S(1)} %collective-permute-done.12.refs_3_), channel_id=1, source_target_pairs={{0,4},{4,0},{8,12},{12,8},{1,5},{5,1},{9,13},{13,9},{2,6},{6,2},{1... | collective-permute-start | bytes 196616 | tf_op jit(solution)/shard_map/ppermute | solution.py:206
  55.8 17.1 %copy-start = (bf16[32,4096]{1,0:T(8,128)(2,1)S(1)}, bf16[32,4096]{1,0:T(8,128)(2,1)}, u32[]{:S(2)}) copy-start(bf16[32,4096]{1,0:T(8,128)(2,1)} %hidden.1) | copy-start | bytes 786436
  55.8 1.6 %collective-permute-start.15 = (bf16[128,1024]{1,0:T(8,128)(2,1)S(1)}, bf16[128,1024]{1,0:T(8,128)(2,1)S(1)}, u32[]{:S(2)}, u32[]{:S(2)}) collective-permute-start(bf16[128,1024]{1,0:T(8,128)(2,1)S(1)} %get-tuple-element.44.given), channel_id=1, source_target_pairs={{0,1},{1,0},{2,3},{3,2},{4,5},{5,4},{6,7},{7,6},{8,9},{9,8},{10,11... | collective-permute-start | bytes 786440 | tf_op jit(solution)/shard_map/ppermute | solution.py:206
  57.4 4.5 %collective-permute-start.16 = (bf16[32,1024]{1,0:T(8,128)(2,1)S(1)}, bf16[32,1024]{1,0:T(8,128)(2,1)S(1)}, u32[]{:S(2)}, u32[]{:S(2)}) collective-permute-start(bf16[32,1024]{1,0:T(8,128)(2,1)S(1)} %get-tuple-element.46), channel_id=1, source_target_pairs={{0,4},{4,0},{8,12},{12,8},{1,5},{5,1},{9,13},{13,9},{2,6},{6,2},{1... | collective-permute-start | bytes 196616 | tf_op jit(solution)/shard_map/ppermute | solution.py:206
  58.9 8.3 %collective-permute-start.17 = (bf16[32,1024]{1,0:T(8,128)(2,1)S(1)}, bf16[32,1024]{1,0:T(8,128)(2,1)S(1)}, u32[]{:S(2)}, u32[]{:S(2)}) collective-permute-start(bf16[32,1024]{1,0:T(8,128)(2,1)S(1)} %get-tuple-element.47), channel_id=1, source_target_pairs={{0,8},{4,12},{8,0},{12,4},{1,9},{5,13},{9,1},{13,5},{2,10},{6,14},... | collective-permute-start | bytes 196616 | tf_op jit(solution)/shard_map/ppermute | solution.py:206
  61.1 6.2 %collective-permute-start.18 = (bf16[32,1024]{1,0:T(8,128)(2,1)S(1)}, bf16[32,1024]{1,0:T(8,128)(2,1)S(1)}, u32[]{:S(2)}, u32[]{:S(2)}) collective-permute-start(bf16[32,1024]{1,0:T(8,128)(2,1)S(1)} %get-tuple-element.48), channel_id=1, source_target_pairs={{0,12},{4,8},{8,4},{12,0},{1,13},{5,9},{9,5},{13,1},{2,14},{6,10},... | collective-permute-start | bytes 196616 | tf_op jit(solution)/shard_map/ppermute | solution.py:206
  67.8 5.0 %collective-permute-start.19 = (bf16[2,32,1024]{2,1,0:T(8,128)(2,1)S(1)}, bf16[2,32,1024]{2,1,0:T(8,128)(2,1)S(1)}, u32[]{:S(2)}, u32[]{:S(2)}) collective-permute-start(bf16[2,32,1024]{2,1,0:T(8,128)(2,1)S(1)} %shard_map.93), channel_id=1, source_target_pairs={{0,2},{2,0},{1,3},{3,1},{4,6},{6,4},{5,7},{7,5},{8,10},{10,8},{9,1... | collective-permute-start | bytes 393224 | tf_op jit(solution)/shard_map/ppermute | solution.py:206
  73.5 1.4 %collective-permute-start.20 = (bf16[32,2048]{1,0:T(8,128)(2,1)S(1)}, bf16[32,2048]{1,0:T(8,128)(2,1)S(1)}, u32[]{:S(2)}, u32[]{:S(2)}) collective-permute-start(bf16[32,2048]{1,0:T(8,128)(2,1)S(1)} %get-tuple-element.50), channel_id=1, source_target_pairs={{0,1},{1,0},{2,3},{3,2},{4,5},{5,4},{6,7},{7,6},{8,9},{9,8},{10,11... | collective-permute-start | bytes 393224 | tf_op jit(solution)/shard_map/ppermute | solution.py:206

commit v9 on v6

--- a/solution.py
+++ b/solution.py
@@ -206,54 +206,98 @@
     return lax.ppermute(value, axis, pairs)
 
 
-def run_copies(copies, sems):
+def started(copies, sems):
     copies = [
         pltpu.make_async_copy(source, target, sems.at[i])
         for i, (source, target) in enumerate(copies)
     ]
     for copy in copies:
         copy.start()
+    return copies
+
+
+def run_copies(copies, sems):
+    for copy in started(copies, sems):
+        copy.wait()
+
+
+def position():
+    col = lax.axis_index("col")
+    pairs = lax.axis_size("col") // lax.axis_size("row")
+    return lax.axis_index("side"), col, lax.axis_index("row") * pairs + lax.rem(col, pairs)
+
+
+def rows_copy(weight, target, half):
+    depth, width = target.shape
+    rows = pl.ds(pl.multiple_of(lax.axis_index("side") * depth, depth), depth)
+    columns = pl.ds(pl.multiple_of(half * width, width), width)
+    return weight.at[rows, columns], target
+
+
+def stage_give_kernel(blocks, weight, slots, gain, give_part, chosen, scratch, sems):
+    side, col, run = position()
+    copies = started([rows_copy(weight, give_part, 1 - side)], sems)
+    chosen[...] = one_hot(slots, scratch, blocks, run, col).astype(jnp.bfloat16)
     for copy in copies:
         copy.wait()
 
 
-def stage_in_kernel(place, weight, gain, give_part, own_part, sems):
-    depth, width = own_part.shape
-    rows = pl.ds(pl.multiple_of(place[0] * depth, depth), depth)
-    copies = []
-    for target, half in ((give_part, 1 - place[0]), (own_part, place[0])):
-        columns = pl.ds(pl.multiple_of(half * width, width), width)
-        copies.append((weight.at[rows, columns], target))
-    run_copies(copies, sems)
-
-
-def stage_out_kernel(give, place, weight, *refs):
-    sems = refs[-1]
-    target = refs[2] if give else refs[1]
+def stage_own_kernel(weight, own_part, sems):
+    run_copies([rows_copy(weight, own_part, lax.axis_index("side"))], sems)
+
+
+def head_copies(weight, target, half):
     width = target.shape[1]
-    half = 1 - place[0] if give else place[0]
     columns = pl.ds(pl.multiple_of(half * width, width), width)
     copies = []
     for j in range(target.shape[0] // OUT_WIDTH):
-        head = 2 * j + place[0]
-        row = pl.multiple_of(head * OUT_WIDTH, OUT_WIDTH)
-        if give:
-            keys, values, _, key_part, value_part, _ = refs
-            lane = pl.multiple_of(head * HEAD_DIM, HEAD_DIM)
-            for cache, part in ((keys, key_part), (values, value_part)):
-                copies.append(
-                    (
-                        cache.at[:, :, pl.ds(lane, HEAD_DIM)],
-                        part.at[:, :, pl.ds(j * HEAD_DIM, HEAD_DIM)],
-                    )
-                )
+        row = pl.multiple_of((2 * j + lax.axis_index("side")) * OUT_WIDTH, OUT_WIDTH)
         copies.append(
             (
                 weight.at[pl.ds(row, OUT_WIDTH), columns],
                 target.at[pl.ds(j * OUT_WIDTH, OUT_WIDTH), :],
             )
         )
-    run_copies(copies, sems)
+    return copies
+
+
+def stage_rest_kernel(blocks, lengths, weight, keys, values, slots, *refs):
+    target, key_part, value_part, cosine, sine, length_of, chosen, scratch, sems = refs
+    side, col, run = position()
+    copies = []
+    for j in range(key_part.shape[2] // HEAD_DIM):
+        lane = pl.multiple_of((2 * j + side) * HEAD_DIM, HEAD_DIM)
+        for cache, part in ((keys, key_part), (values, value_part)):
+            copies.append(
+                (
+                    cache.at[:, :, pl.ds(lane, HEAD_DIM)],
+                    part.at[:, :, pl.ds(j * HEAD_DIM, HEAD_DIM)],
+                )
+            )
+    copies = started(copies + head_copies(weight, target, 1 - side), sems)
+    cosine[...], sine[...], length_of[...] = rope(lengths, cosine.shape[0])
+    chosen[...] = one_hot(slots, scratch, blocks, col, run).T.astype(jnp.bfloat16)
+    for copy in copies:
+        copy.wait()
+
+
+def stage_last_kernel(weight, attended, target, sems):
+    run_copies(head_copies(weight, target, lax.axis_index("side")), sems)
+
+
+def hold_kernel(value, token, out):
+    pass
+
+
+def held(value, token):
+    return pl.pallas_call(
+        hold_kernel,
+        out_shape=pltpu.VMEM(value.shape, value.dtype),
+        in_specs=[VMEM, HBM],
+        out_specs=VMEM,
+        input_output_aliases={0: 0},
+        compiler_params=pltpu.CompilerParams(vmem_limit_bytes=MIB),
+    )(in_vmem(value), token)
 
 
 def one_hot(slots, scratch, blocks, slot_base, request_base):
@@ -286,28 +330,27 @@
         out[:, part] = product.astype(out.dtype)
 
 
-def in_kernel(count, blocks, place, slots, *refs):
-    pieces_in, (gain, weight, give, permuted, scratch) = refs[:count], refs[count:]
-    side = place[0]
+def in_kernel(count, chosen, *refs):
+    pieces_in, (_, gain, weight, give, permuted) = refs[:count], refs[count:]
     depth = pieces_in[0].shape[1]
     half = weight.shape[1]
-    gains = gain[:, pl.ds(pl.multiple_of(side * depth, depth), depth)].astype(jnp.float32)
+    first = pl.multiple_of(lax.axis_index("side") * depth, depth)
+    gains = gain[:, pl.ds(first, depth)].astype(jnp.float32)
     values = jnp.concatenate([piece[...].astype(jnp.float32) for piece in pieces_in], axis=0)
     sums = pieces(jnp.sum(values * values, axis=1, keepdims=True))
-    chosen = one_hot(slots, scratch, blocks, place[2], place[1]).astype(jnp.bfloat16)
     order = jnp.dot(
-        chosen, (values * gains).astype(jnp.bfloat16), preferred_element_type=jnp.float32
+        chosen[...], (values * gains).astype(jnp.bfloat16), preferred_element_type=jnp.float32
     ).astype(jnp.bfloat16)
     permuted[...] = order
-    give[:, half:] = jnp.dot(chosen, sums, preferred_element_type=jnp.float32).astype(jnp.bfloat16)
+    own_sums = jnp.dot(chosen[...], sums, preferred_element_type=jnp.float32)
+    give[:, half:] = own_sums.astype(jnp.bfloat16)
     dot_columns(order, weight, give)
 
 
-def out_kernel(count, blocks, place, slots, *refs):
-    pieces_in, (_, weight, give, permuted, scratch) = refs[:count], refs[count:]
+def out_kernel(count, chosen, *refs):
+    pieces_in, (_, weight, give, permuted) = refs[:count], refs[count:]
     values = jnp.concatenate([piece[...] for piece in pieces_in], axis=0)
-    chosen = one_hot(slots, scratch, blocks, place[1], place[2]).T.astype(jnp.bfloat16)
-    order = jnp.dot(chosen, values, preferred_element_type=jnp.float32).astype(jnp.bfloat16)
+    order = jnp.dot(chosen[...], values, preferred_element_type=jnp.float32).astype(jnp.bfloat16)
     permuted[...] = order
     dot_columns(order, weight, give)
 
@@ -331,7 +374,7 @@
     dot_columns(permuted[...], weight, own)
 
 
-def project(kernel, place, slots, pieces_in, extra, weights, more, pairs):
+def project(kernel, chosen, pieces_in, extra, weights, more, pairs):
     count = lax.axis_size("col")
     parts = len(pieces_in)
     rows, depth = pieces_in[0].shape
@@ -339,14 +382,13 @@
     half = weights[0].shape[1]
     flops = 2 * rows * depth * half
     give, permuted = call(
-        functools.partial(kernel, parts, count),
+        functools.partial(kernel, parts),
         [struct((rows, half + more)), struct((rows, depth))],
-        [SMEM, VMEM] + [VMEM] * (parts + len(extra) + 1),
+        [VMEM] * (parts + len(extra) + 3),
         [VMEM, VMEM],
         flops,
         depth * half * 2,
-        [pltpu.VMEM((rows, rows), jnp.float32)],
-    )(place, slots, *pieces_in, *extra, in_vmem(weights[0]))
+    )(chosen, *pieces_in, in_vmem(weights[1]), *extra, in_vmem(weights[0]))
     received = moved(give, "side", 1)
     own = call(
         own_kernel,
@@ -369,7 +411,7 @@
     )(own, give, received)
 
 
-def gathered(parts, axis):
+def gathered(parts, axis, token=None):
     blocks = {0: parts}
     mask = lax.axis_size(axis) // 2
     while mask:
@@ -378,6 +420,11 @@
             for known, block in blocks.items()
         }
         mask //= 2
+        if mask and token is not None:
+            blocks = {
+                known: [held(part, token) for part in block] if known else block
+                for known, block in blocks.items()
+            }
     return [part for i in sorted(blocks) for part in blocks[i]]
 
 
@@ -417,22 +464,22 @@
     step = lax.rem(lane, half).astype(jnp.float32)
     phases = length_of.astype(jnp.float32) * jnp.exp(-math.log(THETA) * step / half)
     sine = jnp.sin(phases)
-    return jnp.cos(phases), jnp.where(lane < half, -sine, sine), length_of[:, :1]
-
-
-def attend_all(count, parts, place, lengths, *refs):
+    return jnp.cos(phases), jnp.where(lane < half, -sine, sine), length_of
+
+
+def attend_all(count, parts, cosine, sine, lengths, *refs):
     blocks, (keys, values), refs = refs[:count], refs[count : count + 2], refs[count + 2 :]
     outs, (scores_of, probs_of) = refs[:parts], refs[parts:]
     pairs = keys.shape[2] // HEAD_DIM
     rows, cache = keys.shape[:2]
-    low = place[1] % pairs
+    low = lax.rem(lax.axis_index("col"), pairs)
     width = GROUP_WIDTH
     squares = blocks[pairs - 1][:, width:].astype(jnp.float32)
     for i in range(2 * pairs - 1, count, pairs):
         squares = squares + blocks[i][:, width:].astype(jnp.float32)
     scale = lax.rsqrt(jnp.sum(squares, axis=1, keepdims=True) / D + EPSILON)
     factor = HEAD_DIM ** (-0.5)
-    cosines, sines, length_of = rope(lengths, rows)
+    cosines, sines, length_of = cosine[...], sine[...], lengths[:, :1]
     lane = lax.broadcasted_iota(jnp.int32, (SLOTS, SLOTS * cache), 1)
     slot = lax.broadcasted_iota(jnp.int32, (SLOTS, SLOTS * cache), 0)
     position = lane - slot * cache
@@ -496,12 +543,12 @@
                 out[:, pl.ds(at, HEAD_DIM)] = joined.astype(jnp.bfloat16)
 
 
-def sum_kernel(count, parts, place, hidden, *refs):
+def sum_kernel(count, parts, hidden, *refs):
     attended, blocks, (keep, send) = refs[:parts], refs[parts : parts + count], refs[parts + count :]
     rows, width = blocks[0].shape
     pairs = keep.shape[1] // width
-    side = place[0]
-    low = place[1] % pairs
+    side = lax.axis_index("side")
+    low = lax.rem(lax.axis_index("col"), pairs)
     for pair in range(pairs):
         column = low ^ pair
         total = blocks[pair][...].astype(jnp.float32)
@@ -515,15 +562,16 @@
         send[:, at] = jnp.where(side == 0, attention, hidden_out)
 
 
-def join_kernel(place, keep, received, out):
-    side = place[0]
+def join_kernel(keep, received, out, sems):
+    side = lax.axis_index("side")
     width = OUT_WIDTH
+    copies = []
     for j in range(keep.shape[1] // width):
         part = slice(j * width, (j + 1) * width)
-        out[0, :, pl.ds(pl.multiple_of((2 * j + side) * width, width), width)] = keep[:, part]
-        out[0, :, pl.ds(pl.multiple_of((2 * j + 1 - side) * width, width), width)] = received[
-            :, part
-        ]
+        for ref, core in ((keep, side), (received, 1 - side)):
+            at = pl.ds(pl.multiple_of((2 * j + core) * width, width), width)
+            copies.append((ref.at[:, part], out.at[0, :, at]))
+    run_copies(copies, sems)
 
 
 def paired_plan(
@@ -531,9 +579,7 @@
 ):
     col_count, row_count = lax.axis_size("col"), lax.axis_size("row")
     pairs = col_count // row_count
-    side, col, row = (lax.axis_index(name) for name in ("side", "col", "row"))
-    run = row * pairs + lax.rem(col, pairs)
-    place = jnp.stack([side, col, run]).astype(jnp.int32)
+    side = lax.axis_index("side")
     rows, depth = hidden_in.shape
     half = depth // 2
     cache = key_cache.shape[1]
@@ -543,82 +589,87 @@
     own_part = lax.dynamic_slice_in_dim(hidden_in, side * half, half, 1)
     gain = norm_gain.reshape(1, depth)
     half_in, half_out = qkv_weight.shape[1] // 2, out_weight.shape[1] // 2
-    weights_in = call(
-        stage_in_kernel,
-        [pltpu.VMEM((half, half_in), jnp.bfloat16)] * 2,
-        [SMEM, HBM, HBM],
+    total = rows * col_count
+    square = (total, total)
+    give_in, chosen_in = call(
+        functools.partial(stage_give_kernel, col_count),
+        [pltpu.VMEM((half, half_in), jnp.bfloat16), struct(square)],
+        [HBM, VMEM, HBM],
         [VMEM] * 2,
         0,
-        half * half_in * 4,
-        [pltpu.SemaphoreType.DMA((2,))],
-    )(place, in_hbm(qkv_weight), gain)
+        half * half_in * 2,
+        [pltpu.VMEM(square, jnp.float32), pltpu.SemaphoreType.DMA((1,))],
+    )(in_hbm(qkv_weight), slot_request, gain)
+    own_in = call(
+        stage_own_kernel,
+        pltpu.VMEM((half, half_in), jnp.bfloat16),
+        [HBM],
+        VMEM,
+        0,
+        half * half_in * 2,
+        [pltpu.SemaphoreType.DMA((1,))],
+    )(in_hbm(qkv_weight))
     blocks = gathered(
-        [own_part[i * piece : (i + 1) * piece] for i in range(parts)], "col"
-    )
-    out_give, key_part, value_part = call(
-        functools.partial(stage_out_kernel, True),
+        [own_part[i * piece : (i + 1) * piece] for i in range(parts)], "col", chosen_in
+    )
+    products = spread(
+        project(in_kernel, chosen_in, blocks, [gain], [give_in, own_in], HEAD_DIM, pairs)
+    )
+
+    table = struct((rows, HEAD_DIM), jnp.float32)
+    give_out, key_part, value_part, *tables, chosen_out = call(
+        functools.partial(stage_rest_kernel, col_count),
         [pltpu.VMEM((half, half_out), jnp.bfloat16)]
-        + [pltpu.VMEM((rows, cache, pairs * HEAD_DIM), jnp.bfloat16)] * 2,
-        [SMEM, HBM, HBM, HBM],
-        [VMEM] * 3,
+        + [pltpu.VMEM((rows, cache, pairs * HEAD_DIM), jnp.bfloat16)] * 2
+        + [table, table, struct((rows, HEAD_DIM), jnp.int32), struct(square)],
+        [SMEM, HBM, HBM, HBM, VMEM],
+        [VMEM] * 7,
         0,
         half * half_out * 2 + 4 * rows * cache * pairs * HEAD_DIM,
-        [pltpu.SemaphoreType.DMA((3 * pairs,))],
-    )(place, in_hbm(out_weight), in_hbm(key_cache), in_hbm(value_cache))
-
-    products = spread(
-        project(in_kernel, place, slot_request, blocks, [gain], weights_in, HEAD_DIM, pairs)
-    )
-
-    key_part, value_part = in_vmem(key_part), in_vmem(value_part)
+        [pltpu.VMEM(square, jnp.float32), pltpu.SemaphoreType.DMA((3 * pairs,))],
+    )(cache_lengths, in_hbm(out_weight), in_hbm(key_cache), in_hbm(value_cache), slot_request)
     runs = (pairs, rows // SLOTS, GROUP * SLOTS, SLOTS * cache)
     attended = call(
         functools.partial(attend_all, col_count, parts),
         [struct((piece, half))] * parts,
-        [SMEM, SMEM] + [VMEM] * (col_count + 2),
+        [VMEM] * (col_count + 5),
         [VMEM] * parts,
         4 * rows * half * cache,
         0,
         [pltpu.VMEM(runs, jnp.float32), pltpu.VMEM(runs, jnp.bfloat16)],
-    )(place, cache_lengths, *products, key_part, value_part)
-
-    out_own = call(
-        functools.partial(stage_out_kernel, False),
+    )(*tables, *products, in_vmem(key_part), in_vmem(value_part))
+
+    own_out = call(
+        stage_last_kernel,
         pltpu.VMEM((half, half_out), jnp.bfloat16),
-        [SMEM, HBM, HBM],
+        [HBM, HBM],
         VMEM,
         0,
         half * half_out * 2,
         [pltpu.SemaphoreType.DMA((pairs,))],
-    )(place, in_hbm(out_weight), attended[-1])
+    )(in_hbm(out_weight), attended[-1])
     products = spread(
         project(
-            out_kernel,
-            place,
-            slot_request,
-            gathered(attended, "col"),
-            [in_vmem(out_own)],
-            [out_give, out_own],
-            0,
-            pairs,
+            out_kernel, chosen_out, gathered(attended, "col"), [], [give_out, own_out], 0, pairs
         )
     )
     keep, send = call(
         functools.partial(sum_kernel, col_count, parts),
         [struct((rows, half)), struct((rows, half))],
-        [SMEM] + [VMEM] * (1 + parts + col_count),
+        [VMEM] * (1 + parts + col_count),
         [VMEM, VMEM],
         rows * depth * 4,
         rows * depth * 8,
-    )(place, hidden_in, *attended, *products)
+    )(hidden_in, *attended, *products)
     return call(
         join_kernel,
         struct((1, rows, depth)),
-        [SMEM, VMEM, VMEM],
-        VMEM,
+        [VMEM, VMEM],
+        HBM,
         0,
         rows * depth * 4,
-    )(place, keep, moved(send, "side", 1))
+        [pltpu.SemaphoreType.DMA((2 * pairs,))],
+    )(keep, moved(send, "side", 1))
 
 
 def per_device(*args):

time: 70.8 us -> 64.6 us (0.912)
  starting transfers between devices: 34.6 us -> 31.4 us
  Pallas kernels: 20.1 us -> 17.1 us
    ppermute x8, starting transfers between devices: 19.2 us -> 16.7 us  [spread(): lax.ppermute(products[j], ('col', 'row'), [(col * row_count + row, (row *...]
    pallas_call x6 -> x9, Pallas kernels: 15.5 us -> 13.6 us  [the longest x1 3.71 us: paired_plan(): call(functools.partial(stage_rest_kernel, col_count), [pltpu.VMEM((half,...]
    ppermute x8, waiting for transfers between devices: 6 us -> 5.07 us  [spread(): lax.ppermute(products[j], ('col', 'row'), [(col * row_count + row, (row *...]
    ppermute x15, starting transfers between devices: 15.5 us -> 14.7 us  [moved(): return lax.ppermute(value, axis, pairs)]
  transfers between devices with their start and end apart: 23 -> 23, of which waited for: 10 -> 9; matrix products, arithmetic and copies ran while one was open for 1% -> 1% of each run, Pallas kernels for 18% -> 19%
where the time goes in v9:
time: 64.6 us; the launch traced here: 64.2 us
  starting transfers between devices  31.4 us (49%)
  Pallas kernels  17.1 us (26%)
  waiting for transfers between devices  13.3 us (21%)
  local copies, waits for them, and re-layouts  2.26 us (3%)
    ppermute x8, starting transfers between devices, spread(): lax.ppermute(products[j], ('col', 'row'), [(col * row_count + row, (row *...  16.7 us
    ppermute x15, starting transfers between devices, moved(): return lax.ppermute(value, axis, pairs)  14.7 us
    ppermute x15, waiting for transfers between devices, moved(): return lax.ppermute(value, axis, pairs)  8.23 us
    ppermute x8, waiting for transfers between devices, spread(): lax.ppermute(products[j], ('col', 'row'), [(col * row_count + row, (row *...  5.07 us
    pallas_call x1, Pallas kernels, paired_plan(): call(functools.partial(stage_rest_kernel, col_count), [pltpu.VMEM((half,...  3.71 us
    pallas_call x1, Pallas kernels, paired_plan(): call(functools.partial(stage_give_kernel, col_count), [pltpu.VMEM((half,...  2.5 us
    pallas_call x1, Pallas kernels, paired_plan(): call(stage_own_kernel, pltpu.VMEM((half, half_in), jnp.bfloat16), [HBM],...  2.49 us
    pallas_call x1, Pallas kernels, paired_plan(): call(stage_last_kernel, pltpu.VMEM((half, half_out), jnp.bfloat16), [HBM,...  2.24 us
  transfers between devices with their start and end apart: 23, of which 9 were waited for; matrix products, arithmetic and copies ran while one was open for 1% of the time, Pallas kernels for 19%

profile of v9, /device:TPU:0, one launch (start us, length us, event | category | flops | bytes accessed | tf_op | source)
XLA Modules:
  0.0 64.2 jit_solution(10613401064301646486)
XLA Ops:
  0.0 0.9 %fusion = (bf16[16,2048]{1,0:T(8,128)(2,1)S(1)}, bf16[16,2048]{1,0:T(8,128)(2,1)S(1)}) fusion(bf16[32,4096]{1,0:T(8,128)(2,1)} %hidden.1, s32[]{:T(128)S(6)} %add.4, s32[]{:T(128)S(6)} %select_n.3), kind=kLoop, calls=%fused_computation.1 | loop fusion | bytes 262152 | tf_op jit(solution)/shard_map/slice | solution.py:613
  0.9 4.1 %collective-permute-start.2 = (bf16[16,2048]{1,0:T(8,128)(2,1)S(1)}, bf16[16,2048]{1,0:T(8,128)(2,1)S(1)}, u32[]{:S(2)}, u32[]{:S(2)}) collective-permute-start(bf16[16,2048]{1,0:T(8,128)(2,1)S(1)} %get-tuple-element.56.refs_0_), channel_id=1, source_target_pairs={{0,8},{4,12},{8,0},{12,4},{1,9},{5,13},{9,1},{13,5},{2,10},{6,14},... | collective-permute-start | bytes 196616 | tf_op jit(solution)/shard_map/ppermute | solution.py:206
  5.0 0.1 collective-permute-start.3
  5.1 1.8 %collective-permute-start.1 = (bf16[16,2048]{1,0:T(8,128)(2,1)S(1)}, bf16[16,2048]{1,0:T(8,128)(2,1)S(1)}, u32[]{:S(2)}, u32[]{:S(2)}) collective-permute-start(bf16[16,2048]{1,0:T(8,128)(2,1)S(1)} %get-tuple-element.55.refs_1_), channel_id=1, source_target_pairs={{0,4},{4,0},{8,12},{12,8},{1,5},{5,1},{9,13},{13,9},{2,6},{6,2},{1... | collective-permute-start | bytes 196616 | tf_op jit(solution)/shard_map/ppermute | solution.py:206
  6.9 0.2 collective-permute-start
  7.1 0.7 %reshape.3.gain.refs_9_ = bf16[1,4096]{1,0:T(2,128)(2,1)S(1)} reshape(bf16[4096]{0:T(1024)(128)(2,1)} %param.9) | data formatting | bytes 16384 | tf_op jit(solution)/shard_map/reshape | solution.py:590
  7.8 0.6 %copy-done.1 = s32[128]{0:T(128)S(1)} copy-done((s32[128]{0:T(128)S(1)}, s32[128]{0:T(128)}, u32[]{:S(2)}) %copy-start.1) | copy-done | bytes 536
  8.5 2.5 %shard_map.83 = (bf16[2048,1280]{1,0:T(8,128)(2,1)S(1)}, bf16[128,128]{1,0:T(8,128)(2,1)S(1)}) custom-call(bf16[4096,2560]{1,0:T(8,128)(2,1)} %weight.6, s32[128]{0:T(128)S(1)} %copy-done.1, bf16[1,4096]{1,0:T(2,128)(2,1)S(1)} %reshape.3.gain.refs_9_), custom_call_target="tpu_custom_call" | custom-call | bytes 5242880 | tf_op jit(solution)/shard_map/pallas_call | solution.py:594
  11.0 1.9 %collective-permute-start.4 = (bf16[16,2048]{1,0:T(8,128)(2,1)S(1)}, bf16[16,2048]{1,0:T(8,128)(2,1)S(1)}, u32[]{:S(2)}, u32[]{:S(2)}) collective-permute-start(bf16[16,2048]{1,0:T(8,128)(2,1)S(1)} %shard_map.84.refs_4_), channel_id=1, source_target_pairs={{0,4},{4,0},{8,12},{12,8},{1,5},{5,1},{9,13},{13,9},{2,6},{6,2},{1... | collective-permute-start | bytes 196616 | tf_op jit(solution)/shard_map/ppermute | solution.py:206
  12.9 0.2 collective-permute-start.5
  13.1 2.5 %shard_map.86.refs_8_.weight = bf16[2048,1280]{1,0:T(8,128)(2,1)S(1)} custom-call(bf16[4096,2560]{1,0:T(8,128)(2,1)} %weight.6), custom_call_target="tpu_custom_call" | custom-call | bytes 5242880 | tf_op jit(solution)/shard_map/pallas_call | solution.py:603
  15.6 1.5 %collective-permute-done.5.refs_7_ = bf16[16,2048]{1,0:T(8,128)(2,1)S(1)} collective-permute-done((bf16[16,2048]{1,0:T(8,128)(2,1)S(1)}, bf16[16,2048]{1,0:T(8,128)(2,1)S(1)}, u32[]{:S(2)}, u32[]{:S(2)}) %collective-permute-start.5) | collective-permute-done | bytes 65568 | tf_op jit(solution)/shard_map/ppermute | solution.py:206
  17.2 1.1 %shard_map.87 = (bf16[128,1408]{1,0:T(8,128)(2,1)S(1)}, bf16[128,2048]{1,0:T(8,128)(2,1)S(1)}) custom-call(bf16[128,128]{1,0:T(8,128)(2,1)S(1)} %get-tuple-element.33.token.chosen, bf16[16,2048]{1,0:T(8,128)(2,1)S(1)} %get-tuple-element.56.refs_0_, bf16[16,2048]{1,0:T(8,128)(2,1)S(1)} %get-tuple-element.55.refs_1_, ...), custom_call_target="tpu_custom_call" | custom-call | flops 671088640 | bytes 5242880 | tf_op jit(solution)/shard_map/pallas_call | solution.py:384
  18.2 0.0 copy-start.2
  18.3 0.0 copy-start.3
  18.3 0.1 collective-permute-start.6
  18.4 0.8 %shard_map.88.own = f32[128,1280]{1,0:T(8,128)S(1)} custom-call(bf16[128,2048]{1,0:T(8,128)(2,1)S(1)} %get-tuple-element.35.permuted, bf16[2048,1280]{1,0:T(8,128)(2,1)S(1)} %shard_map.86.refs_8_.weight), custom_call_target="tpu_custom_call" | custom-call | flops 671088640 | bytes 5242880 | tf_op jit(solution)/shard_map/pallas_call | solution.py:393
  19.2 0.8 %collective-permute-done.6.received = bf16[128,1408]{1,0:T(8,128)(2,1)S(1)} collective-permute-done((bf16[128,1408]{1,0:T(8,128)(2,1)S(1)}, bf16[128,1408]{1,0:T(8,128)(2,1)S(1)}, u32[]{:S(2)}, u32[]{:S(2)}) %collective-permute-start.6) | collective-permute-done | bytes 360480 | tf_op jit(solution)/shard_map/ppermute | solution.py:206
  20.0 0.1 shard_map.89
  20.1 0.8 %collective-permute-start.8 = (bf16[32,1408]{1,0:T(8,128)(2,1)S(1)}, bf16[32,1408]{1,0:T(8,128)(2,1)S(1)}, u32[]{:S(2)}, u32[]{:S(2)}) collective-permute-start(bf16[32,1408]{1,0:T(8,128)(2,1)S(1)} %get-tuple-element.38), channel_id=1, source_target_pairs={{0,4},{2,12},{4,0},{6,8},{8,6},{10,14},{12,2},{14,10},{1,5},{3,13}... | collective-permute-start | bytes 270344 | tf_op jit(solution)/shard_map/ppermute | solution.py:436
  20.8 4.1 %collective-permute-start.10 = (bf16[32,1408]{1,0:T(8,128)(2,1)S(1)}, bf16[32,1408]{1,0:T(8,128)(2,1)S(1)}, u32[]{:S(2)}, u32[]{:S(2)}) collective-permute-start(bf16[32,1408]{1,0:T(8,128)(2,1)S(1)} %get-tuple-element.40), channel_id=1, source_target_pairs={{0,12},{2,4},{4,8},{6,0},{8,14},{10,6},{12,10},{14,2},{1,13},{3,5}... | collective-permute-start | bytes 270344 | tf_op jit(solution)/shard_map/ppermute | solution.py:436
  24.9 0.7 %collective-permute-start.7 = (bf16[32,1280]{1,0:T(8,128)(2,1)S(1)}, bf16[32,1280]{1,0:T(8,128)(2,1)S(1)}, u32[]{:S(2)}, u32[]{:S(2)}) collective-permute-start(bf16[32,1280]{1,0:T(8,128)(2,1)S(1)} %get-tuple-element.37), channel_id=1, source_target_pairs={{0,0},{2,8},{4,4},{6,12},{8,2},{10,10},{12,6},{14,14},{1,1},{3,9},... | collective-permute-start | bytes 245768 | tf_op jit(solution)/shard_map/ppermute | solution.py:436
  25.6 3.1 %collective-permute-start.9 = (bf16[32,1280]{1,0:T(8,128)(2,1)S(1)}, bf16[32,1280]{1,0:T(8,128)(2,1)S(1)}, u32[]{:S(2)}, u32[]{:S(2)}) collective-permute-start(bf16[32,1280]{1,0:T(8,128)(2,1)S(1)} %get-tuple-element.39), channel_id=1, source_target_pairs={{0,8},{2,0},{4,12},{6,4},{8,10},{10,2},{12,14},{14,6},{1,9},{3,1},... | collective-permute-start | bytes 245768 | tf_op jit(solution)/shard_map/ppermute | solution.py:436
  28.7 3.7 %shard_map.82 = (bf16[2048,1024]{1,0:T(8,128)(2,1)S(1)}, bf16[32,64,256]{2,1,0:T(8,128)(2,1)S(1)}, bf16[32,64,256]{2,1,0:T(8,128)(2,1)S(1)}, f32[32,128]{1,0:T(8...) custom-call(s32[32]{0:T(128)S(1)} %copy-done.3, bf16[4096,2048]{1,0:T(8,128)(2,1)} %weight.7, ...), custom_call_target="tpu_custom_call" | custom-call | bytes 6291456 | tf_op jit(solution)/shard_map/pallas_call | solution.py:620
  32.4 1.7 %shard_map.90 = (bf16[16,2048]{1,0:T(8,128)(2,1)S(1)}, bf16[16,2048]{1,0:T(8,128)(2,1)S(1)}) custom-call(f32[32,128]{1,0:T(8,128)S(1)} %get-tuple-element.30.cosine, f32[32,128]{1,0:T(8,128)S(1)} %get-tuple-element.31.sine, s32[32,128]{1,0:T(8,128)S(1)} %get-tuple-element.32.lengths, bf16[32,1280]{1,0:T(8,128)(2,1)S(1)} %collective-permute-done.7.refs_0_, ...), custom_call_target="tpu_custom_call" | custom-call | flops 16777216 | tf_op jit(solution)/shard_map/pallas_call | solution.py:632
  34.1 1.7 %collective-permute-start.13 = (bf16[16,2048]{1,0:T(8,128)(2,1)S(1)}, bf16[16,2048]{1,0:T(8,128)(2,1)S(1)}, u32[]{:S(2)}, u32[]{:S(2)}) collective-permute-start(bf16[16,2048]{1,0:T(8,128)(2,1)S(1)} %get-tuple-element.43.refs_0_), channel_id=1, source_target_pairs={{0,8},{4,12},{8,0},{12,4},{1,9},{5,13},{9,1},{13,5},{2,10},{6,14},... | collective-permute-start | bytes 196616 | tf_op jit(solution)/shard_map/ppermute | solution.py:206
  35.9 1.2 %collective-permute-start.14 = (bf16[16,2048]{1,0:T(8,128)(2,1)S(1)}, bf16[16,2048]{1,0:T(8,128)(2,1)S(1)}, u32[]{:S(2)}, u32[]{:S(2)}) collective-permute-start(bf16[16,2048]{1,0:T(8,128)(2,1)S(1)} %get-tuple-element.44.attended.refs_1_), channel_id=1, source_target_pairs={{0,8},{4,12},{8,0},{12,4},{1,9},{5,13},{9,1},{13,5},{2,10},{6,14},... | collective-permute-start | bytes 196616 | tf_op jit(solution)/shard_map/ppermute | solution.py:206
  37.1 0.6 collective-permute-start.11
  37.7 1.5 %collective-permute-start.12 = (bf16[16,2048]{1,0:T(8,128)(2,1)S(1)}, bf16[16,2048]{1,0:T(8,128)(2,1)S(1)}, u32[]{:S(2)}, u32[]{:S(2)}) collective-permute-start(bf16[16,2048]{1,0:T(8,128)(2,1)S(1)} %get-tuple-element.44.attended.refs_1_), channel_id=1, source_target_pairs={{0,4},{4,0},{8,12},{12,8},{1,5},{5,1},{9,13},{13,9},{2,6},{6,2},{1... | collective-permute-start | bytes 196616 | tf_op jit(solution)/shard_map/ppermute | solution.py:206
  39.1 2.0 %collective-permute-done.13.refs_4_ = bf16[16,2048]{1,0:T(8,128)(2,1)S(1)} collective-permute-done((bf16[16,2048]{1,0:T(8,128)(2,1)S(1)}, bf16[16,2048]{1,0:T(8,128)(2,1)S(1)}, u32[]{:S(2)}, u32[]{:S(2)}) %collective-permute-start.13) | collective-permute-done | bytes 65568 | tf_op jit(solution)/shard_map/ppermute | solution.py:206
  41.2 0.9 %collective-permute-done.14.refs_5_ = bf16[16,2048]{1,0:T(8,128)(2,1)S(1)} collective-permute-done((bf16[16,2048]{1,0:T(8,128)(2,1)S(1)}, bf16[16,2048]{1,0:T(8,128)(2,1)S(1)}, u32[]{:S(2)}, u32[]{:S(2)}) %collective-permute-start.14) | collective-permute-done | bytes 65568 | tf_op jit(solution)/shard_map/ppermute | solution.py:206
  42.0 1.2 %collective-permute-start.16 = (bf16[16,2048]{1,0:T(8,128)(2,1)S(1)}, bf16[16,2048]{1,0:T(8,128)(2,1)S(1)}, u32[]{:S(2)}, u32[]{:S(2)}) collective-permute-start(bf16[16,2048]{1,0:T(8,128)(2,1)S(1)} %collective-permute-done.14.refs_5_), channel_id=1, source_target_pairs={{0,4},{4,0},{8,12},{12,8},{1,5},{5,1},{9,13},{13,9},{2,6},{6,2},{1... | collective-permute-start | bytes 196616 | tf_op jit(solution)/shard_map/ppermute | solution.py:206
  43.2 2.2 %shard_map.91.refs_8_.weight = bf16[2048,1024]{1,0:T(8,128)(2,1)S(1)} custom-call(bf16[4096,2048]{1,0:T(8,128)(2,1)} %weight.7, bf16[16,2048]{1,0:T(8,128)(2,1)S(1)} %get-tuple-element.44.attended.refs_1_), custom_call_target="tpu_custom_call" | custom-call | bytes 4194304 | tf_op jit(solution)/shard_map/pallas_call | solution.py:642
  45.5 0.8 %collective-permute-done.16.refs_7_ = bf16[16,2048]{1,0:T(8,128)(2,1)S(1)} collective-permute-done((bf16[16,2048]{1,0:T(8,128)(2,1)S(1)}, bf16[16,2048]{1,0:T(8,128)(2,1)S(1)}, u32[]{:S(2)}, u32[]{:S(2)}) %collective-permute-start.16) | collective-permute-done | bytes 65568 | tf_op jit(solution)/shard_map/ppermute | solution.py:206
  46.3 0.8 %shard_map.92 = (bf16[128,1024]{1,0:T(8,128)(2,1)S(1)}, bf16[128,2048]{1,0:T(8,128)(2,1)S(1)}) custom-call(bf16[128,128]{1,0:T(8,128)(2,1)S(1)} %get-tuple-element.45.chosen, bf16[16,2048]{1,0:T(8,128)(2,1)S(1)} %get-tuple-element.43.refs_0_, bf16[16,2048]{1,0:T(8,128)(2,1)S(1)} %get-tuple-element.44.attended.refs_1_, ...), custom_call_target="tpu_custom_call" | custom-call | flops 536870912 | bytes 4194304 | tf_op jit(solution)/shard_map/pallas_call | solution.py:384
  47.2 0.1 collective-permute-start.17
  47.2 0.7 %shard_map.93.own = f32[128,1024]{1,0:T(8,128)S(1)} custom-call(bf16[128,2048]{1,0:T(8,128)(2,1)S(1)} %get-tuple-element.47.permuted, bf16[2048,1024]{1,0:T(8,128)(2,1)S(1)} %shard_map.91.refs_8_.weight), custom_call_target="tpu_custom_call" | custom-call | flops 536870912 | bytes 4194304 | tf_op jit(solution)/shard_map/pallas_call | solution.py:393
  48.0 0.8 %collective-permute-done.17.received = bf16[128,1024]{1,0:T(8,128)(2,1)S(1)} collective-permute-done((bf16[128,1024]{1,0:T(8,128)(2,1)S(1)}, bf16[128,1024]{1,0:T(8,128)(2,1)S(1)}, u32[]{:S(2)}, u32[]{:S(2)}) %collective-permute-start.17) | collective-permute-done | bytes 262176 | tf_op jit(solution)/shard_map/ppermute | solution.py:206
  48.8 0.7 %collective-permute-start.18 = (bf16[32,1024]{1,0:T(8,128)(2,1)S(1)}, bf16[32,1024]{1,0:T(8,128)(2,1)S(1)}, u32[]{:S(2)}, u32[]{:S(2)}) collective-permute-start(bf16[32,1024]{1,0:T(8,128)(2,1)S(1)} %get-tuple-element.49), channel_id=1, source_target_pairs={{0,0},{2,8},{4,4},{6,12},{8,2},{10,10},{12,6},{14,14},{1,1},{3,9},... | collective-permute-start | bytes 196616 | tf_op jit(solution)/shard_map/ppermute | solution.py:436
  49.5 1.2 %collective-permute-start.19 = (bf16[32,1024]{1,0:T(8,128)(2,1)S(1)}, bf16[32,1024]{1,0:T(8,128)(2,1)S(1)}, u32[]{:S(2)}, u32[]{:S(2)}) collective-permute-start(bf16[32,1024]{1,0:T(8,128)(2,1)S(1)} %get-tuple-element.50), channel_id=1, source_target_pairs={{0,4},{2,12},{4,0},{6,8},{8,6},{10,14},{12,2},{14,10},{1,5},{3,13}... | collective-permute-start | bytes 196616 | tf_op jit(solution)/shard_map/ppermute | solution.py:436
  50.7 5.2 %collective-permute-start.20 = (bf16[32,1024]{1,0:T(8,128)(2,1)S(1)}, bf16[32,1024]{1,0:T(8,128)(2,1)S(1)}, u32[]{:S(2)}, u32[]{:S(2)}) collective-permute-start(bf16[32,1024]{1,0:T(8,128)(2,1)S(1)} %get-tuple-element.51), channel_id=1, source_target_pairs={{0,8},{2,0},{4,12},{6,4},{8,10},{10,2},{12,14},{14,6},{1,9},{3,1},... | collective-permute-start | bytes 196616 | tf_op jit(solution)/shard_map/ppermute | solution.py:436
  55.9 1.0 %collective-permute-start.21 = (bf16[32,1024]{1,0:T(8,128)(2,1)S(1)}, bf16[32,1024]{1,0:T(8,128)(2,1)S(1)}, u32[]{:S(2)}, u32[]{:S(2)}) collective-permute-start(bf16[32,1024]{1,0:T(8,128)(2,1)S(1)} %get-tuple-element.52), channel_id=1, source_target_pairs={{0,12},{2,4},{4,8},{6,0},{8,14},{10,6},{12,10},{14,2},{1,13},{3,5}... | collective-permute-start | bytes 196616 | tf_op jit(solution)/shard_map/ppermute | solution.py:436
  57.0 3.1 %collective-permute-done.20.refs_4_ = bf16[32,1024]{1,0:T(8,128)(2,1)S(1)} collective-permute-done((bf16[32,1024]{1,0:T(8,128)(2,1)S(1)}, bf16[32,1024]{1,0:T(8,128)(2,1)S(1)}, u32[]{:S(2)}, u32[]{:S(2)}) %collective-permute-start.20) | collective-permute-done | bytes 65568 | tf_op jit(solution)/shard_map/ppermute | solution.py:436
  60.0 2.0 %collective-permute-done.21.refs_5_ = bf16[32,1024]{1,0:T(8,128)(2,1)S(1)} collective-permute-done((bf16[32,1024]{1,0:T(8,128)(2,1)S(1)}, bf16[32,1024]{1,0:T(8,128)(2,1)S(1)}, u32[]{:S(2)}, u32[]{:S(2)}) %collective-permute-start.21) | collective-permute-done | bytes 65568 | tf_op jit(solution)/shard_map/ppermute | solution.py:436
  62.0 0.1 shard_map.95
  62.1 0.1 collective-permute-start.22
  62.2 1.3 %collective-permute-done.22.received = bf16[32,2048]{1,0:T(8,128)(2,1)S(1)} collective-permute-done((bf16[32,2048]{1,0:T(8,128)(2,1)S(1)}, bf16[32,2048]{1,0:T(8,128)(2,1)S(1)}, u32[]{:S(2)}, u32[]{:S(2)}) %collective-permute-start.22) | collective-permute-done | bytes 131104 | tf_op jit(solution)/shard_map/ppermute | solution.py:206
  63.5 0.7 %shard_map.96 = bf16[1,32,4096]{2,1,0:T(8,128)(2,1)} custom-call(bf16[32,2048]{1,0:T(8,128)(2,1)S(1)} %get-tuple-element.53.keep, bf16[32,2048]{1,0:T(8,128)(2,1)S(1)} %collective-permute-done.22.received), custom_call_target="tpu_custom_call" | custom-call | bytes 524288 | tf_op jit(solution)/shard_map/pallas_call | solution.py:664
  (23 shorter events, 0.1 us)
Async XLA Ops:
  0.9 10.1 %collective-permute-start.2 = (bf16[16,2048]{1,0:T(8,128)(2,1)S(1)}, bf16[16,2048]{1,0:T(8,128)(2,1)S(1)}, u32[]{:S(2)}, u32[]{:S(2)}) collective-permute-start(bf16[16,2048]{1,0:T(8,128)(2,1)S(1)} %get-tuple-element.56.refs_0_), channel_id=1, source_target_pairs={{0,8},{4,12},{8,0},{12,4},{1,9},{5,13},{9,1},{13,5},{2,10},{6,14},... | collective-permute-start | bytes 196616 | tf_op jit(solution)/shard_map/ppermute | solution.py:206
  5.0 7.9 %collective-permute-start.3 = (bf16[16,2048]{1,0:T(8,128)(2,1)S(1)}, bf16[16,2048]{1,0:T(8,128)(2,1)S(1)}, u32[]{:S(2)}, u32[]{:S(2)}) collective-permute-start(bf16[16,2048]{1,0:T(8,128)(2,1)S(1)} %get-tuple-element.55.refs_1_), channel_id=1, source_target_pairs={{0,8},{4,12},{8,0},{12,4},{1,9},{5,13},{9,1},{13,5},{2,10},{6,14},... | collective-permute-start | bytes 196616 | tf_op jit(solution)/shard_map/ppermute | solution.py:206
  5.1 10.5 %collective-permute-start.1 = (bf16[16,2048]{1,0:T(8,128)(2,1)S(1)}, bf16[16,2048]{1,0:T(8,128)(2,1)S(1)}, u32[]{:S(2)}, u32[]{:S(2)}) collective-permute-start(bf16[16,2048]{1,0:T(8,128)(2,1)S(1)} %get-tuple-element.55.refs_1_), channel_id=1, source_target_pairs={{0,4},{4,0},{8,12},{12,8},{1,5},{5,1},{9,13},{13,9},{2,6},{6,2},{1... | collective-permute-start | bytes 196616 | tf_op jit(solution)/shard_map/ppermute | solution.py:206
  6.9 8.7 %collective-permute-start = (bf16[16,2048]{1,0:T(8,128)(2,1)S(1)}, bf16[16,2048]{1,0:T(8,128)(2,1)S(1)}, u32[]{:S(2)}, u32[]{:S(2)}) collective-permute-start(bf16[16,2048]{1,0:T(8,128)(2,1)S(1)} %get-tuple-element.56.refs_0_), channel_id=1, source_target_pairs={{0,4},{4,0},{8,12},{12,8},{1,5},{5,1},{9,13},{13,9},{2,6},{6,2},{1... | collective-permute-start | bytes 196616 | tf_op jit(solution)/shard_map/ppermute | solution.py:206
  7.8 0.7 %copy-start.1 = (s32[128]{0:T(128)S(1)}, s32[128]{0:T(128)}, u32[]{:S(2)}) copy-start(s32[128]{0:T(128)} %slots.3) | copy-start | bytes 1540
  11.0 4.6 %collective-permute-start.4 = (bf16[16,2048]{1,0:T(8,128)(2,1)S(1)}, bf16[16,2048]{1,0:T(8,128)(2,1)S(1)}, u32[]{:S(2)}, u32[]{:S(2)}) collective-permute-start(bf16[16,2048]{1,0:T(8,128)(2,1)S(1)} %shard_map.84.refs_4_), channel_id=1, source_target_pairs={{0,4},{4,0},{8,12},{12,8},{1,5},{5,1},{9,13},{13,9},{2,6},{6,2},{1... | collective-permute-start | bytes 196616 | tf_op jit(solution)/shard_map/ppermute | solution.py:206
  12.9 4.3 %collective-permute-start.5 = (bf16[16,2048]{1,0:T(8,128)(2,1)S(1)}, bf16[16,2048]{1,0:T(8,128)(2,1)S(1)}, u32[]{:S(2)}, u32[]{:S(2)}) collective-permute-start(bf16[16,2048]{1,0:T(8,128)(2,1)S(1)} %shard_map.85.refs_5_), channel_id=1, source_target_pairs={{0,4},{4,0},{8,12},{12,8},{1,5},{5,1},{9,13},{13,9},{2,6},{6,2},{1... | collective-permute-start | bytes 196616 | tf_op jit(solution)/shard_map/ppermute | solution.py:206
  18.2 10.4 %copy-start.2 = (s32[128]{0:T(128)S(1)}, s32[128]{0:T(128)}, u32[]{:S(2)}) copy-start(s32[128]{0:T(128)} %slots.3) | copy-start | bytes 1540
  18.3 10.4 %copy-start.3 = (s32[32]{0:T(128)S(1)}, s32[32]{0:T(128)}, u32[]{:S(2)}) copy-start(s32[32]{0:T(128)} %lengths.1) | copy-start | bytes 388
  18.3 1.7 %collective-permute-start.6 = (bf16[128,1408]{1,0:T(8,128)(2,1)S(1)}, bf16[128,1408]{1,0:T(8,128)(2,1)S(1)}, u32[]{:S(2)}, u32[]{:S(2)}) collective-permute-start(bf16[128,1408]{1,0:T(8,128)(2,1)S(1)} %get-tuple-element.36.given), channel_id=1, source_target_pairs={{0,1},{1,0},{2,3},{3,2},{4,5},{5,4},{6,7},{7,6},{8,9},{9,8},{10,11... | collective-permute-start | bytes 1081352 | tf_op jit(solution)/shard_map/ppermute | solution.py:206
  20.1 12.3 %collective-permute-start.8 = (bf16[32,1408]{1,0:T(8,128)(2,1)S(1)}, bf16[32,1408]{1,0:T(8,128)(2,1)S(1)}, u32[]{:S(2)}, u32[]{:S(2)}) collective-permute-start(bf16[32,1408]{1,0:T(8,128)(2,1)S(1)} %get-tuple-element.38), channel_id=1, source_target_pairs={{0,4},{2,12},{4,0},{6,8},{8,6},{10,14},{12,2},{14,10},{1,5},{3,13}... | collective-permute-start | bytes 270344 | tf_op jit(solution)/shard_map/ppermute | solution.py:436
  20.8 11.6 %collective-permute-start.10 = (bf16[32,1408]{1,0:T(8,128)(2,1)S(1)}, bf16[32,1408]{1,0:T(8,128)(2,1)S(1)}, u32[]{:S(2)}, u32[]{:S(2)}) collective-permute-start(bf16[32,1408]{1,0:T(8,128)(2,1)S(1)} %get-tuple-element.40), channel_id=1, source_target_pairs={{0,12},{2,4},{4,8},{6,0},{8,14},{10,6},{12,10},{14,2},{1,13},{3,5}... | collective-permute-start | bytes 270344 | tf_op jit(solution)/shard_map/ppermute | solution.py:436
  24.9 7.5 %collective-permute-start.7 = (bf16[32,1280]{1,0:T(8,128)(2,1)S(1)}, bf16[32,1280]{1,0:T(8,128)(2,1)S(1)}, u32[]{:S(2)}, u32[]{:S(2)}) collective-permute-start(bf16[32,1280]{1,0:T(8,128)(2,1)S(1)} %get-tuple-element.37), channel_id=1, source_target_pairs={{0,0},{2,8},{4,4},{6,12},{8,2},{10,10},{12,6},{14,14},{1,1},{3,9},... | collective-permute-start | bytes 245768 | tf_op jit(solution)/shard_map/ppermute | solution.py:436
  25.6 6.8 %collective-permute-start.9 = (bf16[32,1280]{1,0:T(8,128)(2,1)S(1)}, bf16[32,1280]{1,0:T(8,128)(2,1)S(1)}, u32[]{:S(2)}, u32[]{:S(2)}) collective-permute-start(bf16[32,1280]{1,0:T(8,128)(2,1)S(1)} %get-tuple-element.39), channel_id=1, source_target_pairs={{0,8},{2,0},{4,12},{6,4},{8,10},{10,2},{12,14},{14,6},{1,9},{3,1},... | collective-permute-start | bytes 245768 | tf_op jit(solution)/shard_map/ppermute | solution.py:436
  34.1 7.0 %collective-permute-start.13 = (bf16[16,2048]{1,0:T(8,128)(2,1)S(1)}, bf16[16,2048]{1,0:T(8,128)(2,1)S(1)}, u32[]{:S(2)}, u32[]{:S(2)}) collective-permute-start(bf16[16,2048]{1,0:T(8,128)(2,1)S(1)} %get-tuple-element.43.refs_0_), channel_id=1, source_target_pairs={{0,8},{4,12},{8,0},{12,4},{1,9},{5,13},{9,1},{13,5},{2,10},{6,14},... | collective-permute-start | bytes 196616 | tf_op jit(solution)/shard_map/ppermute | solution.py:206
  35.9 6.2 %collective-permute-start.14 = (bf16[16,2048]{1,0:T(8,128)(2,1)S(1)}, bf16[16,2048]{1,0:T(8,128)(2,1)S(1)}, u32[]{:S(2)}, u32[]{:S(2)}) collective-permute-start(bf16[16,2048]{1,0:T(8,128)(2,1)S(1)} %get-tuple-element.44.attended.refs_1_), channel_id=1, source_target_pairs={{0,8},{4,12},{8,0},{12,4},{1,9},{5,13},{9,1},{13,5},{2,10},{6,14},... | collective-permute-start | bytes 196616 | tf_op jit(solution)/shard_map/ppermute | solution.py:206
  37.1 8.3 %collective-permute-start.11 = (bf16[16,2048]{1,0:T(8,128)(2,1)S(1)}, bf16[16,2048]{1,0:T(8,128)(2,1)S(1)}, u32[]{:S(2)}, u32[]{:S(2)}) collective-permute-start(bf16[16,2048]{1,0:T(8,128)(2,1)S(1)} %get-tuple-element.43.refs_0_), channel_id=1, source_target_pairs={{0,4},{4,0},{8,12},{12,8},{1,5},{5,1},{9,13},{13,9},{2,6},{6,2},{1... | collective-permute-start | bytes 196616 | tf_op jit(solution)/shard_map/ppermute | solution.py:206
  37.7 7.8 %collective-permute-start.12 = (bf16[16,2048]{1,0:T(8,128)(2,1)S(1)}, bf16[16,2048]{1,0:T(8,128)(2,1)S(1)}, u32[]{:S(2)}, u32[]{:S(2)}) collective-permute-start(bf16[16,2048]{1,0:T(8,128)(2,1)S(1)} %get-tuple-element.44.attended.refs_1_), channel_id=1, source_target_pairs={{0,4},{4,0},{8,12},{12,8},{1,5},{5,1},{9,13},{13,9},{2,6},{6,2},{1... | collective-permute-start | bytes 196616 | tf_op jit(solution)/shard_map/ppermute | solution.py:206
  41.2 4.3 %collective-permute-start.15 = (bf16[16,2048]{1,0:T(8,128)(2,1)S(1)}, bf16[16,2048]{1,0:T(8,128)(2,1)S(1)}, u32[]{:S(2)}, u32[]{:S(2)}) collective-permute-start(bf16[16,2048]{1,0:T(8,128)(2,1)S(1)} %collective-permute-done.13.refs_4_), channel_id=1, source_target_pairs={{0,4},{4,0},{8,12},{12,8},{1,5},{5,1},{9,13},{13,9},{2,6},{6,2},{1... | collective-permute-start | bytes 196616 | tf_op jit(solution)/shard_map/ppermute | solution.py:206
  42.0 4.3 %collective-permute-start.16 = (bf16[16,2048]{1,0:T(8,128)(2,1)S(1)}, bf16[16,2048]{1,0:T(8,128)(2,1)S(1)}, u32[]{:S(2)}, u32[]{:S(2)}) collective-permute-start(bf16[16,2048]{1,0:T(8,128)(2,1)S(1)} %collective-permute-done.14.refs_5_), channel_id=1, source_target_pairs={{0,4},{4,0},{8,12},{12,8},{1,5},{5,1},{9,13},{13,9},{2,6},{6,2},{1... | collective-permute-start | bytes 196616 | tf_op jit(solution)/shard_map/ppermute | solution.py:206
  47.2 14.9 %copy-start = (bf16[32,4096]{1,0:T(8,128)(2,1)S(1)}, bf16[32,4096]{1,0:T(8,128)(2,1)}, u32[]{:S(2)}) copy-start(bf16[32,4096]{1,0:T(8,128)(2,1)} %hidden.1) | copy-start | bytes 786436
  47.2 1.6 %collective-permute-start.17 = (bf16[128,1024]{1,0:T(8,128)(2,1)S(1)}, bf16[128,1024]{1,0:T(8,128)(2,1)S(1)}, u32[]{:S(2)}, u32[]{:S(2)}) collective-permute-start(bf16[128,1024]{1,0:T(8,128)(2,1)S(1)} %get-tuple-element.48.given), channel_id=1, source_target_pairs={{0,1},{1,0},{2,3},{3,2},{4,5},{5,4},{6,7},{7,6},{8,9},{9,8},{10,11... | collective-permute-start | bytes 786440 | tf_op jit(solution)/shard_map/ppermute | solution.py:206
  48.8 8.1 %collective-permute-start.18 = (bf16[32,1024]{1,0:T(8,128)(2,1)S(1)}, bf16[32,1024]{1,0:T(8,128)(2,1)S(1)}, u32[]{:S(2)}, u32[]{:S(2)}) collective-permute-start(bf16[32,1024]{1,0:T(8,128)(2,1)S(1)} %get-tuple-element.49), channel_id=1, source_target_pairs={{0,0},{2,8},{4,4},{6,12},{8,2},{10,10},{12,6},{14,14},{1,1},{3,9},... | collective-permute-start | bytes 196616 | tf_op jit(solution)/shard_map/ppermute | solution.py:436
  49.5 7.5 %collective-permute-start.19 = (bf16[32,1024]{1,0:T(8,128)(2,1)S(1)}, bf16[32,1024]{1,0:T(8,128)(2,1)S(1)}, u32[]{:S(2)}, u32[]{:S(2)}) collective-permute-start(bf16[32,1024]{1,0:T(8,128)(2,1)S(1)} %get-tuple-element.50), channel_id=1, source_target_pairs={{0,4},{2,12},{4,0},{6,8},{8,6},{10,14},{12,2},{14,10},{1,5},{3,13}... | collective-permute-start | bytes 196616 | tf_op jit(solution)/shard_map/ppermute | solution.py:436
  50.7 9.3 %collective-permute-start.20 = (bf16[32,1024]{1,0:T(8,128)(2,1)S(1)}, bf16[32,1024]{1,0:T(8,128)(2,1)S(1)}, u32[]{:S(2)}, u32[]{:S(2)}) collective-permute-start(bf16[32,1024]{1,0:T(8,128)(2,1)S(1)} %get-tuple-element.51), channel_id=1, source_target_pairs={{0,8},{2,0},{4,12},{6,4},{8,10},{10,2},{12,14},{14,6},{1,9},{3,1},... | collective-permute-start | bytes 196616 | tf_op jit(solution)/shard_map/ppermute | solution.py:436
  55.9 6.1 %collective-permute-start.21 = (bf16[32,1024]{1,0:T(8,128)(2,1)S(1)}, bf16[32,1024]{1,0:T(8,128)(2,1)S(1)}, u32[]{:S(2)}, u32[]{:S(2)}) collective-permute-start(bf16[32,1024]{1,0:T(8,128)(2,1)S(1)} %get-tuple-element.52), channel_id=1, source_target_pairs={{0,12},{2,4},{4,8},{6,0},{8,14},{10,6},{12,10},{14,2},{1,13},{3,5}... | collective-permute-start | bytes 196616 | tf_op jit(solution)/shard_map/ppermute | solution.py:436
  62.1 1.4 %collective-permute-start.22 = (bf16[32,2048]{1,0:T(8,128)(2,1)S(1)}, bf16[32,2048]{1,0:T(8,128)(2,1)S(1)}, u32[]{:S(2)}, u32[]{:S(2)}) collective-permute-start(bf16[32,2048]{1,0:T(8,128)(2,1)S(1)} %get-tuple-element.54), channel_id=1, source_target_pairs={{0,1},{1,0},{2,3},{3,2},{4,5},{5,4},{6,7},{7,6},{8,9},{9,8},{10,11... | collective-permute-start | bytes 393224 | tf_op jit(solution)/shard_map/ppermute | solution.py:206

commit v10 on v9

--- a/solution.py
+++ b/solution.py
@@ -234,16 +234,20 @@
     return weight.at[rows, columns], target
 
 
-def stage_give_kernel(blocks, weight, slots, gain, give_part, chosen, scratch, sems):
+def stage_in_kernel(blocks, weight, slots, give_part, own_part, chosen, scratch, slot_part, sems):
     side, col, run = position()
-    copies = started([rows_copy(weight, give_part, 1 - side)], sems)
-    chosen[...] = one_hot(slots, scratch, blocks, run, col).astype(jnp.bfloat16)
+    slots_copy, *copies = started(
+        [
+            (slots, slot_part),
+            rows_copy(weight, give_part, 1 - side),
+            rows_copy(weight, own_part, side),
+        ],
+        sems,
+    )
+    slots_copy.wait()
+    chosen[...] = one_hot(slot_part, scratch, blocks, run, col).astype(jnp.bfloat16)
     for copy in copies:
         copy.wait()
-
-
-def stage_own_kernel(weight, own_part, sems):
-    run_copies([rows_copy(weight, own_part, lax.axis_index("side"))], sems)
 
 
 def head_copies(weight, target, half):
@@ -261,8 +265,8 @@
     return copies
 
 
-def stage_rest_kernel(blocks, lengths, weight, keys, values, slots, *refs):
-    target, key_part, value_part, cosine, sine, length_of, chosen, scratch, sems = refs
+def stage_cache_kernel(blocks, lengths, keys, values, slots, *refs):
+    key_part, value_part, cosine, sine, length_of, chosen, scratch, sems = refs
     side, col, run = position()
     copies = []
     for j in range(key_part.shape[2] // HEAD_DIM):
@@ -274,30 +278,17 @@
                     part.at[:, :, pl.ds(j * HEAD_DIM, HEAD_DIM)],
                 )
             )
-    copies = started(copies + head_copies(weight, target, 1 - side), sems)
+    copies = started(copies, sems)
     cosine[...], sine[...], length_of[...] = rope(lengths, cosine.shape[0])
     chosen[...] = one_hot(slots, scratch, blocks, col, run).T.astype(jnp.bfloat16)
     for copy in copies:
         copy.wait()
 
 
-def stage_last_kernel(weight, attended, target, sems):
-    run_copies(head_copies(weight, target, lax.axis_index("side")), sems)
-
-
-def hold_kernel(value, token, out):
-    pass
-
-
-def held(value, token):
-    return pl.pallas_call(
-        hold_kernel,
-        out_shape=pltpu.VMEM(value.shape, value.dtype),
-        in_specs=[VMEM, HBM],
-        out_specs=VMEM,
-        input_output_aliases={0: 0},
-        compiler_params=pltpu.CompilerParams(vmem_limit_bytes=MIB),
-    )(in_vmem(value), token)
+def stage_out_kernel(weight, attended, give_part, own_part, sems):
+    side = lax.axis_index("side")
+    copies = head_copies(weight, give_part, 1 - side) + head_copies(weight, own_part, side)
+    run_copies(copies, sems)
 
 
 def one_hot(slots, scratch, blocks, slot_base, request_base):
@@ -334,12 +325,20 @@
     pieces_in, (_, gain, weight, give, permuted) = refs[:count], refs[count:]
     depth = pieces_in[0].shape[1]
     half = weight.shape[1]
-    first = pl.multiple_of(lax.axis_index("side") * depth, depth)
-    gains = gain[:, pl.ds(first, depth)].astype(jnp.float32)
+    runs = depth // HEAD_DIM
+    first = pl.multiple_of(lax.axis_index("side") * runs, runs)
+    gains = gain[pl.ds(first, runs), :].astype(jnp.float32)
     values = jnp.concatenate([piece[...].astype(jnp.float32) for piece in pieces_in], axis=0)
+    scaled = jnp.concatenate(
+        [
+            values[:, i * HEAD_DIM : (i + 1) * HEAD_DIM] * gains[i : i + 1, :]
+            for i in range(runs)
+        ],
+        axis=1,
+    )
     sums = pieces(jnp.sum(values * values, axis=1, keepdims=True))
     order = jnp.dot(
-        chosen[...], (values * gains).astype(jnp.bfloat16), preferred_element_type=jnp.float32
+        chosen[...], scaled.astype(jnp.bfloat16), preferred_element_type=jnp.float32
     ).astype(jnp.bfloat16)
     permuted[...] = order
     own_sums = jnp.dot(chosen[...], sums, preferred_element_type=jnp.float32)
@@ -353,6 +352,14 @@
     order = jnp.dot(chosen[...], values, preferred_element_type=jnp.float32).astype(jnp.bfloat16)
     permuted[...] = order
     dot_columns(order, weight, give)
+
+
+def carries(entry, pairs):
+    return entry % pairs == (0 if entry // pairs % 2 else pairs - 1)
+
+
+def arrival_order(count, pairs):
+    return sorted(range(count), key=lambda i: (i == 0, not carries(i, pairs), i % pairs, -i))
 
 
 def merge_kernel(own, given, received, *outs):
@@ -401,8 +408,7 @@
     return call(
         merge_kernel,
         [
-            struct((rows // count, half + (more if i % pairs == pairs - 1 else 0)))
-            for i in range(count)
+            struct((rows // count, half + (more if carries(i, pairs) else 0))) for i in range(count)
         ],
         [VMEM] * 3,
         [VMEM] * count,
@@ -411,7 +417,7 @@
     )(own, give, received)
 
 
-def gathered(parts, axis, token=None):
+def gathered(parts, axis):
     blocks = {0: parts}
     mask = lax.axis_size(axis) // 2
     while mask:
@@ -420,18 +426,16 @@
             for known, block in blocks.items()
         }
         mask //= 2
-        if mask and token is not None:
-            blocks = {
-                known: [held(part, token) for part in block] if known else block
-                for known, block in blocks.items()
-            }
     return [part for i in sorted(blocks) for part in blocks[i]]
+
+
+def in_place(blocks, pairs):
+    return [blocks[arrival_order(len(blocks), pairs).index(i)] for i in range(len(blocks))]
 
 
 def spread(products):
     col_count, row_count = lax.axis_size("col"), lax.axis_size("row")
     pairs = col_count // row_count
-    order = sorted(range(col_count), key=lambda j: (-(j % pairs), -j))
     sent = {
         j: lax.ppermute(
             products[j],
@@ -445,9 +449,9 @@
                 for row in range(row_count)
             ],
         )
-        for j in order
+        for j in range(col_count)
     }
-    return [sent[j] for j in range(col_count)]
+    return [sent[j] for j in arrival_order(col_count, pairs)]
 
 
 def rotated(vector, cosine, sine):
@@ -469,14 +473,15 @@
 
 def attend_all(count, parts, cosine, sine, lengths, *refs):
     blocks, (keys, values), refs = refs[:count], refs[count : count + 2], refs[count + 2 :]
+    blocks = in_place(blocks, keys.shape[2] // HEAD_DIM)
     outs, (scores_of, probs_of) = refs[:parts], refs[parts:]
     pairs = keys.shape[2] // HEAD_DIM
     rows, cache = keys.shape[:2]
     low = lax.rem(lax.axis_index("col"), pairs)
     width = GROUP_WIDTH
-    squares = blocks[pairs - 1][:, width:].astype(jnp.float32)
-    for i in range(2 * pairs - 1, count, pairs):
-        squares = squares + blocks[i][:, width:].astype(jnp.float32)
+    squares = sum(
+        blocks[i][:, width:].astype(jnp.float32) for i in range(count) if carries(i, pairs)
+    )
     scale = lax.rsqrt(jnp.sum(squares, axis=1, keepdims=True) / D + EPSILON)
     factor = HEAD_DIM ** (-0.5)
     cosines, sines, length_of = cosine[...], sine[...], lengths[:, :1]
@@ -547,6 +552,7 @@
     attended, blocks, (keep, send) = refs[:parts], refs[parts : parts + count], refs[parts + count :]
     rows, width = blocks[0].shape
     pairs = keep.shape[1] // width
+    blocks = in_place(blocks, pairs)
     side = lax.axis_index("side")
     low = lax.rem(lax.axis_index("col"), pairs)
     for pair in range(pairs):
@@ -587,47 +593,41 @@
     piece = rows // parts
 
     own_part = lax.dynamic_slice_in_dim(hidden_in, side * half, half, 1)
-    gain = norm_gain.reshape(1, depth)
+    gain = norm_gain.reshape(depth // HEAD_DIM, HEAD_DIM)
     half_in, half_out = qkv_weight.shape[1] // 2, out_weight.shape[1] // 2
     total = rows * col_count
     square = (total, total)
-    give_in, chosen_in = call(
-        functools.partial(stage_give_kernel, col_count),
-        [pltpu.VMEM((half, half_in), jnp.bfloat16), struct(square)],
-        [HBM, VMEM, HBM],
-        [VMEM] * 2,
+    give_in, own_in, chosen_in = call(
+        functools.partial(stage_in_kernel, col_count),
+        [pltpu.VMEM((half, half_in), jnp.bfloat16)] * 2 + [struct(square)],
+        [HBM, HBM],
+        [VMEM] * 3,
         0,
-        half * half_in * 2,
-        [pltpu.VMEM(square, jnp.float32), pltpu.SemaphoreType.DMA((1,))],
-    )(in_hbm(qkv_weight), slot_request, gain)
-    own_in = call(
-        stage_own_kernel,
-        pltpu.VMEM((half, half_in), jnp.bfloat16),
-        [HBM],
-        VMEM,
-        0,
-        half * half_in * 2,
-        [pltpu.SemaphoreType.DMA((1,))],
-    )(in_hbm(qkv_weight))
+        half * half_in * 4,
+        [
+            pltpu.VMEM(square, jnp.float32),
+            pltpu.VMEM((total,), jnp.int32),
+            pltpu.SemaphoreType.DMA((3,)),
+        ],
+    )(in_hbm(qkv_weight), in_hbm(slot_request))
     blocks = gathered(
-        [own_part[i * piece : (i + 1) * piece] for i in range(parts)], "col", chosen_in
+        [own_part[i * piece : (i + 1) * piece] for i in range(parts)], "col"
     )
     products = spread(
         project(in_kernel, chosen_in, blocks, [gain], [give_in, own_in], HEAD_DIM, pairs)
     )
 
     table = struct((rows, HEAD_DIM), jnp.float32)
-    give_out, key_part, value_part, *tables, chosen_out = call(
-        functools.partial(stage_rest_kernel, col_count),
-        [pltpu.VMEM((half, half_out), jnp.bfloat16)]
-        + [pltpu.VMEM((rows, cache, pairs * HEAD_DIM), jnp.bfloat16)] * 2
+    key_part, value_part, *tables, chosen_out = call(
+        functools.partial(stage_cache_kernel, col_count),
+        [pltpu.VMEM((rows, cache, pairs * HEAD_DIM), jnp.bfloat16)] * 2
         + [table, table, struct((rows, HEAD_DIM), jnp.int32), struct(square)],
-        [SMEM, HBM, HBM, HBM, VMEM],
-        [VMEM] * 7,
+        [SMEM, HBM, HBM, VMEM],
+        [VMEM] * 6,
         0,
-        half * half_out * 2 + 4 * rows * cache * pairs * HEAD_DIM,
-        [pltpu.VMEM(square, jnp.float32), pltpu.SemaphoreType.DMA((3 * pairs,))],
-    )(cache_lengths, in_hbm(out_weight), in_hbm(key_cache), in_hbm(value_cache), slot_request)
+        4 * rows * cache * pairs * HEAD_DIM,
+        [pltpu.VMEM(square, jnp.float32), pltpu.SemaphoreType.DMA((2 * pairs,))],
+    )(cache_lengths, in_hbm(key_cache), in_hbm(value_cache), slot_request)
     runs = (pairs, rows // SLOTS, GROUP * SLOTS, SLOTS * cache)
     attended = call(
         functools.partial(attend_all, col_count, parts),
@@ -639,14 +639,14 @@
         [pltpu.VMEM(runs, jnp.float32), pltpu.VMEM(runs, jnp.bfloat16)],
     )(*tables, *products, in_vmem(key_part), in_vmem(value_part))
 
-    own_out = call(
-        stage_last_kernel,
-        pltpu.VMEM((half, half_out), jnp.bfloat16),
+    give_out, own_out = call(
+        stage_out_kernel,
+        [pltpu.VMEM((half, half_out), jnp.bfloat16)] * 2,
         [HBM, HBM],
-        VMEM,
+        [VMEM] * 2,
         0,
-        half * half_out * 2,
-        [pltpu.SemaphoreType.DMA((pairs,))],
+        half * half_out * 4,
+        [pltpu.SemaphoreType.DMA((2 * pairs,))],
     )(in_hbm(out_weight), attended[-1])
     products = spread(
         project(

time: 64.6 us -> 64.3 us (level)
  the two profiles are of different devices: /device:TPU:0 before, /device:TPU:3 now
where the time goes in v10:
time: 64.3 us; the launch traced here: 64.1 us
  starting transfers between devices  29.9 us (47%)
  waiting for transfers between devices  17 us (26%)
  Pallas kernels  16 us (25%)
  local copies, waits for them, and re-layouts  0.9 us (1%)
    ppermute x15, starting transfers between devices, moved(): return lax.ppermute(value, axis, pairs)  17.1 us
    ppermute x8, starting transfers between devices, spread(): lax.ppermute(products[j], ('col', 'row'), [(col * row_count + row, (row *...  12.9 us
    ppermute x8, waiting for transfers between devices, spread(): lax.ppermute(products[j], ('col', 'row'), [(col * row_count + row, (row *...  9.51 us
    ppermute x15, waiting for transfers between devices, moved(): return lax.ppermute(value, axis, pairs)  7.45 us
    pallas_call x1, Pallas kernels, paired_plan(): call(functools.partial(stage_in_kernel, col_count), [pltpu.VMEM((half, ha...  4.09 us
    pallas_call x1, Pallas kernels, paired_plan(): call(stage_out_kernel, [pltpu.VMEM((half, half_out), jnp.bfloat16)] * 2,...  3.5 us
    pallas_call x1, Pallas kernels, paired_plan(): call(functools.partial(stage_cache_kernel, col_count), [pltpu.VMEM((rows,...  2.31 us
    pallas_call x2, Pallas kernels, project(): call(functools.partial(kernel, parts), [struct((rows, half + more)), stru...  1.91 us
  transfers between devices with their start and end apart: 23, of which 13 were waited for; matrix products, arithmetic and copies ran while one was open for 0% of the time, Pallas kernels for 18%

profile of v10, /device:TPU:3, one launch (start us, length us, event | category | flops | bytes accessed | tf_op | source)
XLA Modules:
  0.0 64.1 jit_solution(11959603992002102866)
XLA Ops:
  0.0 0.9 %fusion = (bf16[16,2048]{1,0:T(8,128)(2,1)S(1)}, bf16[16,2048]{1,0:T(8,128)(2,1)S(1)}) fusion(bf16[32,4096]{1,0:T(8,128)(2,1)} %hidden.1, s32[]{:T(128)S(6)} %add.4, s32[]{:T(128)S(6)} %select_n.3), kind=kLoop, calls=%fused_computation.1 | loop fusion | bytes 262152 | tf_op jit(solution)/shard_map/slice | solution.py:614
  0.9 2.4 %collective-permute-start.2 = (bf16[16,2048]{1,0:T(8,128)(2,1)S(1)}, bf16[16,2048]{1,0:T(8,128)(2,1)S(1)}, u32[]{:S(2)}, u32[]{:S(2)}) collective-permute-start(bf16[16,2048]{1,0:T(8,128)(2,1)S(1)} %get-tuple-element.60.refs_0_), channel_id=1, source_target_pairs={{0,8},{4,12},{8,0},{12,4},{1,9},{5,13},{9,1},{13,5},{2,10},{6,14},... | collective-permute-start | bytes 196616 | tf_op jit(solution)/shard_map/ppermute | solution.py:206
  3.3 0.1 collective-permute-start.3
  3.3 1.3 %collective-permute-start = (bf16[16,2048]{1,0:T(8,128)(2,1)S(1)}, bf16[16,2048]{1,0:T(8,128)(2,1)S(1)}, u32[]{:S(2)}, u32[]{:S(2)}) collective-permute-start(bf16[16,2048]{1,0:T(8,128)(2,1)S(1)} %get-tuple-element.60.refs_0_), channel_id=1, source_target_pairs={{0,4},{4,0},{8,12},{12,8},{1,5},{5,1},{9,13},{13,9},{2,6},{6,2},{1... | collective-permute-start | bytes 196616 | tf_op jit(solution)/shard_map/ppermute | solution.py:206
  4.6 0.2 collective-permute-start.1
  4.8 0.1 collective-permute-done.2.refs_4_
  5.0 3.8 %collective-permute-start.4 = (bf16[16,2048]{1,0:T(8,128)(2,1)S(1)}, bf16[16,2048]{1,0:T(8,128)(2,1)S(1)}, u32[]{:S(2)}, u32[]{:S(2)}) collective-permute-start(bf16[16,2048]{1,0:T(8,128)(2,1)S(1)} %collective-permute-done.2.refs_4_), channel_id=1, source_target_pairs={{0,4},{4,0},{8,12},{12,8},{1,5},{5,1},{9,13},{13,9},{2,6},{6,2},{1... | collective-permute-start | bytes 196616 | tf_op jit(solution)/shard_map/ppermute | solution.py:206
  8.7 1.0 %collective-permute-done.3.refs_5_ = bf16[16,2048]{1,0:T(8,128)(2,1)S(1)} collective-permute-done((bf16[16,2048]{1,0:T(8,128)(2,1)S(1)}, bf16[16,2048]{1,0:T(8,128)(2,1)S(1)}, u32[]{:S(2)}, u32[]{:S(2)}) %collective-permute-start.3) | collective-permute-done | bytes 65568 | tf_op jit(solution)/shard_map/ppermute | solution.py:206
  9.7 0.8 %collective-permute-start.5 = (bf16[16,2048]{1,0:T(8,128)(2,1)S(1)}, bf16[16,2048]{1,0:T(8,128)(2,1)S(1)}, u32[]{:S(2)}, u32[]{:S(2)}) collective-permute-start(bf16[16,2048]{1,0:T(8,128)(2,1)S(1)} %collective-permute-done.3.refs_5_), channel_id=1, source_target_pairs={{0,4},{4,0},{8,12},{12,8},{1,5},{5,1},{9,13},{13,9},{2,6},{6,2},{1... | collective-permute-start | bytes 196616 | tf_op jit(solution)/shard_map/ppermute | solution.py:206
  10.5 4.1 %shard_map.83 = (bf16[2048,1280]{1,0:T(8,128)(2,1)S(1)}, bf16[2048,1280]{1,0:T(8,128)(2,1)S(1)}, bf16[128,128]{1,0:T(8,128)(2,1)S(1)}) custom-call(bf16[4096,2560]{1,0:T(8,128)(2,1)} %weight.2, s32[128]{0:T(128)} %slots.3), custom_call_target="tpu_custom_call" | custom-call | bytes 10485760 | tf_op jit(solution)/shard_map/pallas_call | solution.py:600
  14.7 1.1 %shard_map.84 = (bf16[128,1408]{1,0:T(8,128)(2,1)S(1)}, bf16[128,2048]{1,0:T(8,128)(2,1)S(1)}) custom-call(bf16[128,128]{1,0:T(8,128)(2,1)S(1)} %get-tuple-element.35.chosen, bf16[16,2048]{1,0:T(8,128)(2,1)S(1)} %get-tuple-element.60.refs_0_, bf16[16,2048]{1,0:T(8,128)(2,1)S(1)} %get-tuple-element.59.refs_1_, ...), custom_call_target="tpu_custom_call" | custom-call | flops 671088640 | bytes 5242880 | tf_op jit(solution)/shard_map/pallas_call | solution.py:391
  15.8 0.0 copy-start.2
  15.8 0.0 copy-start.3
  15.8 1.2 %collective-permute-start.6 = (bf16[128,1408]{1,0:T(8,128)(2,1)S(1)}, bf16[128,1408]{1,0:T(8,128)(2,1)S(1)}, u32[]{:S(2)}, u32[]{:S(2)}) collective-permute-start(bf16[128,1408]{1,0:T(8,128)(2,1)S(1)} %get-tuple-element.39.given), channel_id=1, source_target_pairs={{0,1},{1,0},{2,3},{3,2},{4,5},{5,4},{6,7},{7,6},{8,9},{9,8},{10,11... | collective-permute-start | bytes 1081352 | tf_op jit(solution)/shard_map/ppermute | solution.py:206
  16.9 0.9 %shard_map.85.own = f32[128,1280]{1,0:T(8,128)S(1)} custom-call(bf16[128,2048]{1,0:T(8,128)(2,1)S(1)} %get-tuple-element.38.permuted, bf16[2048,1280]{1,0:T(8,128)(2,1)S(1)} %get-tuple-element.36.refs_8_.weight), custom_call_target="tpu_custom_call" | custom-call | flops 671088640 | bytes 5242880 | tf_op jit(solution)/shard_map/pallas_call | solution.py:400
  17.8 0.4 collective-permute-done.6.received
  18.2 0.1 shard_map.86
  18.3 0.3 collective-permute-start.7
  18.6 3.9 %collective-permute-start.8 = (bf16[32,1408]{1,0:T(8,128)(2,1)S(1)}, bf16[32,1408]{1,0:T(8,128)(2,1)S(1)}, u32[]{:S(2)}, u32[]{:S(2)}) collective-permute-start(bf16[32,1408]{1,0:T(8,128)(2,1)S(1)} %get-tuple-element.41), channel_id=1, source_target_pairs={{0,4},{2,12},{4,0},{6,8},{8,6},{10,14},{12,2},{14,10},{1,5},{3,13}... | collective-permute-start | bytes 270344 | tf_op jit(solution)/shard_map/ppermute | solution.py:440
  22.5 1.9 %collective-permute-start.10 = (bf16[32,1280]{1,0:T(8,128)(2,1)S(1)}, bf16[32,1280]{1,0:T(8,128)(2,1)S(1)}, u32[]{:S(2)}, u32[]{:S(2)}) collective-permute-start(bf16[32,1280]{1,0:T(8,128)(2,1)S(1)} %get-tuple-element.43), channel_id=1, source_target_pairs={{0,0},{2,8},{4,4},{6,12},{8,2},{10,10},{12,6},{14,14},{1,1},{3,9},... | collective-permute-start | bytes 245768 | tf_op jit(solution)/shard_map/ppermute | solution.py:440
  24.4 0.1 collective-permute-start.9
  24.5 2.3 %shard_map.82 = (bf16[32,64,256]{2,1,0:T(8,128)(2,1)S(1)}, bf16[32,64,256]{2,1,0:T(8,128)(2,1)S(1)}, f32[32,128]{1,0:T(8,128)S(1)}, f32[32,128]{1,0:T(8,128)S(1)...) custom-call(s32[32]{0:T(128)S(1)} %copy-done.3, bf16[32,64,512]{2,1,0:T(8,128)(2,1)} %keys.1, ...), custom_call_target="tpu_custom_call" | custom-call | bytes 2097152 | tf_op jit(solution)/shard_map/pallas_call | solution.py:621
  26.9 4.8 %collective-permute-done.10.refs_3_ = bf16[32,1280]{1,0:T(8,128)(2,1)S(1)} collective-permute-done((bf16[32,1280]{1,0:T(8,128)(2,1)S(1)}, bf16[32,1280]{1,0:T(8,128)(2,1)S(1)}, u32[]{:S(2)}, u32[]{:S(2)}) %collective-permute-start.10) | collective-permute-done | bytes 81952 | tf_op jit(solution)/shard_map/ppermute | solution.py:440
  31.6 1.7 %shard_map.87 = (bf16[16,2048]{1,0:T(8,128)(2,1)S(1)}, bf16[16,2048]{1,0:T(8,128)(2,1)S(1)}) custom-call(f32[32,128]{1,0:T(8,128)S(1)} %get-tuple-element.32.cosine, f32[32,128]{1,0:T(8,128)S(1)} %get-tuple-element.33.sine, s32[32,128]{1,0:T(8,128)S(1)} %get-tuple-element.34.lengths, bf16[32,1408]{1,0:T(8,128)(2,1)S(1)} %collective-permute-done.7.refs_0_, ...), custom_call_target="tpu_custom_call" | custom-call | flops 16777216 | tf_op jit(solution)/shard_map/pallas_call | solution.py:632
  33.3 0.1 collective-permute-start.13
  33.4 2.4 %collective-permute-start.14 = (bf16[16,2048]{1,0:T(8,128)(2,1)S(1)}, bf16[16,2048]{1,0:T(8,128)(2,1)S(1)}, u32[]{:S(2)}, u32[]{:S(2)}) collective-permute-start(bf16[16,2048]{1,0:T(8,128)(2,1)S(1)} %get-tuple-element.47.attended.refs_1_), channel_id=1, source_target_pairs={{0,8},{4,12},{8,0},{12,4},{1,9},{5,13},{9,1},{13,5},{2,10},{6,14},... | collective-permute-start | bytes 196616 | tf_op jit(solution)/shard_map/ppermute | solution.py:206
  35.8 1.5 %collective-permute-start.12 = (bf16[16,2048]{1,0:T(8,128)(2,1)S(1)}, bf16[16,2048]{1,0:T(8,128)(2,1)S(1)}, u32[]{:S(2)}, u32[]{:S(2)}) collective-permute-start(bf16[16,2048]{1,0:T(8,128)(2,1)S(1)} %get-tuple-element.47.attended.refs_1_), channel_id=1, source_target_pairs={{0,4},{4,0},{8,12},{12,8},{1,5},{5,1},{9,13},{13,9},{2,6},{6,2},{1... | collective-permute-start | bytes 196616 | tf_op jit(solution)/shard_map/ppermute | solution.py:206
  37.2 0.2 collective-permute-done.13.refs_4_
  37.4 2.0 %collective-permute-done.14.refs_5_ = bf16[16,2048]{1,0:T(8,128)(2,1)S(1)} collective-permute-done((bf16[16,2048]{1,0:T(8,128)(2,1)S(1)}, bf16[16,2048]{1,0:T(8,128)(2,1)S(1)}, u32[]{:S(2)}, u32[]{:S(2)}) %collective-permute-start.14) | collective-permute-done | bytes 65568 | tf_op jit(solution)/shard_map/ppermute | solution.py:206
  39.4 3.5 %shard_map.88 = (bf16[2048,1024]{1,0:T(8,128)(2,1)S(1)}, bf16[2048,1024]{1,0:T(8,128)(2,1)S(1)}) custom-call(bf16[4096,2048]{1,0:T(8,128)(2,1)} %weight.3, bf16[16,2048]{1,0:T(8,128)(2,1)S(1)} %get-tuple-element.47.attended.refs_1_), custom_call_target="tpu_custom_call" | custom-call | bytes 8388608 | tf_op jit(solution)/shard_map/pallas_call | solution.py:642
  42.9 0.9 %collective-permute-done.15.refs_6_ = bf16[16,2048]{1,0:T(8,128)(2,1)S(1)} collective-permute-done((bf16[16,2048]{1,0:T(8,128)(2,1)S(1)}, bf16[16,2048]{1,0:T(8,128)(2,1)S(1)}, u32[]{:S(2)}, u32[]{:S(2)}) %collective-permute-start.15) | collective-permute-done | bytes 65568 | tf_op jit(solution)/shard_map/ppermute | solution.py:206
  43.8 1.4 %collective-permute-done.16.refs_7_ = bf16[16,2048]{1,0:T(8,128)(2,1)S(1)} collective-permute-done((bf16[16,2048]{1,0:T(8,128)(2,1)S(1)}, bf16[16,2048]{1,0:T(8,128)(2,1)S(1)}, u32[]{:S(2)}, u32[]{:S(2)}) %collective-permute-start.16) | collective-permute-done | bytes 65568 | tf_op jit(solution)/shard_map/ppermute | solution.py:206
  45.2 0.8 %shard_map.89 = (bf16[128,1024]{1,0:T(8,128)(2,1)S(1)}, bf16[128,2048]{1,0:T(8,128)(2,1)S(1)}) custom-call(bf16[128,128]{1,0:T(8,128)(2,1)S(1)} %get-tuple-element.48.chosen, bf16[16,2048]{1,0:T(8,128)(2,1)S(1)} %get-tuple-element.46.refs_0_, bf16[16,2048]{1,0:T(8,128)(2,1)S(1)} %get-tuple-element.47.attended.refs_1_, ...), custom_call_target="tpu_custom_call" | custom-call | flops 536870912 | bytes 4194304 | tf_op jit(solution)/shard_map/pallas_call | solution.py:391
  46.1 0.0 copy-start
  46.1 1.1 %collective-permute-start.17 = (bf16[128,1024]{1,0:T(8,128)(2,1)S(1)}, bf16[128,1024]{1,0:T(8,128)(2,1)S(1)}, u32[]{:S(2)}, u32[]{:S(2)}) collective-permute-start(bf16[128,1024]{1,0:T(8,128)(2,1)S(1)} %get-tuple-element.52.given), channel_id=1, source_target_pairs={{0,1},{1,0},{2,3},{3,2},{4,5},{5,4},{6,7},{7,6},{8,9},{9,8},{10,11... | collective-permute-start | bytes 786440 | tf_op jit(solution)/shard_map/ppermute | solution.py:206
  47.2 0.7 %shard_map.90.own = f32[128,1024]{1,0:T(8,128)S(1)} custom-call(bf16[128,2048]{1,0:T(8,128)(2,1)S(1)} %get-tuple-element.51.permuted, bf16[2048,1024]{1,0:T(8,128)(2,1)S(1)} %get-tuple-element.49.refs_8_.weight), custom_call_target="tpu_custom_call" | custom-call | flops 536870912 | bytes 4194304 | tf_op jit(solution)/shard_map/pallas_call | solution.py:400
  47.9 0.4 collective-permute-done.17.received
  48.4 1.0 %collective-permute-start.18 = (bf16[32,1024]{1,0:T(8,128)(2,1)S(1)}, bf16[32,1024]{1,0:T(8,128)(2,1)S(1)}, u32[]{:S(2)}, u32[]{:S(2)}) collective-permute-start(bf16[32,1024]{1,0:T(8,128)(2,1)S(1)} %get-tuple-element.53), channel_id=1, source_target_pairs={{0,8},{2,0},{4,12},{6,4},{8,10},{10,2},{12,14},{14,6},{1,9},{3,1},... | collective-permute-start | bytes 196616 | tf_op jit(solution)/shard_map/ppermute | solution.py:440
  49.4 2.0 %collective-permute-start.19 = (bf16[32,1024]{1,0:T(8,128)(2,1)S(1)}, bf16[32,1024]{1,0:T(8,128)(2,1)S(1)}, u32[]{:S(2)}, u32[]{:S(2)}) collective-permute-start(bf16[32,1024]{1,0:T(8,128)(2,1)S(1)} %get-tuple-element.54), channel_id=1, source_target_pairs={{0,4},{2,12},{4,0},{6,8},{8,6},{10,14},{12,2},{14,10},{1,5},{3,13}... | collective-permute-start | bytes 196616 | tf_op jit(solution)/shard_map/ppermute | solution.py:440
  51.4 0.9 %collective-permute-start.20 = (bf16[32,1024]{1,0:T(8,128)(2,1)S(1)}, bf16[32,1024]{1,0:T(8,128)(2,1)S(1)}, u32[]{:S(2)}, u32[]{:S(2)}) collective-permute-start(bf16[32,1024]{1,0:T(8,128)(2,1)S(1)} %get-tuple-element.55), channel_id=1, source_target_pairs={{0,12},{2,4},{4,8},{6,0},{8,14},{10,6},{12,10},{14,2},{1,13},{3,5}... | collective-permute-start | bytes 196616 | tf_op jit(solution)/shard_map/ppermute | solution.py:440
  52.3 2.7 %collective-permute-start.21 = (bf16[32,1024]{1,0:T(8,128)(2,1)S(1)}, bf16[32,1024]{1,0:T(8,128)(2,1)S(1)}, u32[]{:S(2)}, u32[]{:S(2)}) collective-permute-start(bf16[32,1024]{1,0:T(8,128)(2,1)S(1)} %get-tuple-element.56), channel_id=1, source_target_pairs={{0,0},{2,8},{4,4},{6,12},{8,2},{10,10},{12,6},{14,14},{1,1},{3,9},... | collective-permute-start | bytes 196616 | tf_op jit(solution)/shard_map/ppermute | solution.py:440
  55.1 0.3 collective-permute-done.19.refs_3_
  55.4 1.3 %collective-permute-done.20.refs_4_ = bf16[32,1024]{1,0:T(8,128)(2,1)S(1)} collective-permute-done((bf16[32,1024]{1,0:T(8,128)(2,1)S(1)}, bf16[32,1024]{1,0:T(8,128)(2,1)S(1)}, u32[]{:S(2)}, u32[]{:S(2)}) %collective-permute-start.20) | collective-permute-done | bytes 65568 | tf_op jit(solution)/shard_map/ppermute | solution.py:440
  56.6 3.2 %collective-permute-done.21.refs_5_ = bf16[32,1024]{1,0:T(8,128)(2,1)S(1)} collective-permute-done((bf16[32,1024]{1,0:T(8,128)(2,1)S(1)}, bf16[32,1024]{1,0:T(8,128)(2,1)S(1)}, u32[]{:S(2)}, u32[]{:S(2)}) %collective-permute-start.21) | collective-permute-done | bytes 65568 | tf_op jit(solution)/shard_map/ppermute | solution.py:440
  59.8 0.1 shard_map.92
  59.9 2.4 %collective-permute-start.22 = (bf16[32,2048]{1,0:T(8,128)(2,1)S(1)}, bf16[32,2048]{1,0:T(8,128)(2,1)S(1)}, u32[]{:S(2)}, u32[]{:S(2)}) collective-permute-start(bf16[32,2048]{1,0:T(8,128)(2,1)S(1)} %get-tuple-element.58), channel_id=1, source_target_pairs={{0,1},{1,0},{2,3},{3,2},{4,5},{5,4},{6,7},{7,6},{8,9},{9,8},{10,11... | collective-permute-start | bytes 393224 | tf_op jit(solution)/shard_map/ppermute | solution.py:206
  62.3 1.0 %collective-permute-done.22.received = bf16[32,2048]{1,0:T(8,128)(2,1)S(1)} collective-permute-done((bf16[32,2048]{1,0:T(8,128)(2,1)S(1)}, bf16[32,2048]{1,0:T(8,128)(2,1)S(1)}, u32[]{:S(2)}, u32[]{:S(2)}) %collective-permute-start.22) | collective-permute-done | bytes 131104 | tf_op jit(solution)/shard_map/ppermute | solution.py:206
  63.3 0.7 %shard_map.93 = bf16[1,32,4096]{2,1,0:T(8,128)(2,1)} custom-call(bf16[32,2048]{1,0:T(8,128)(2,1)S(1)} %get-tuple-element.57.keep, bf16[32,2048]{1,0:T(8,128)(2,1)S(1)} %collective-permute-done.22.received), custom_call_target="tpu_custom_call" | custom-call | bytes 524288 | tf_op jit(solution)/shard_map/pallas_call | solution.py:664
  (19 shorter events, 0.1 us)
Async XLA Ops:
  0.9 4.1 %collective-permute-start.2 = (bf16[16,2048]{1,0:T(8,128)(2,1)S(1)}, bf16[16,2048]{1,0:T(8,128)(2,1)S(1)}, u32[]{:S(2)}, u32[]{:S(2)}) collective-permute-start(bf16[16,2048]{1,0:T(8,128)(2,1)S(1)} %get-tuple-element.60.refs_0_), channel_id=1, source_target_pairs={{0,8},{4,12},{8,0},{12,4},{1,9},{5,13},{9,1},{13,5},{2,10},{6,14},... | collective-permute-start | bytes 196616 | tf_op jit(solution)/shard_map/ppermute | solution.py:206
  3.3 11.4 %copy-start.1 = (bf16[4096]{0:T(1024)(128)(2,1)S(1)}, bf16[4096]{0:T(1024)(128)(2,1)}, u32[]{:S(2)}) copy-start(bf16[4096]{0:T(1024)(128)(2,1)} %param.9) | copy-start | bytes 24580
  3.3 6.4 %collective-permute-start.3 = (bf16[16,2048]{1,0:T(8,128)(2,1)S(1)}, bf16[16,2048]{1,0:T(8,128)(2,1)S(1)}, u32[]{:S(2)}, u32[]{:S(2)}) collective-permute-start(bf16[16,2048]{1,0:T(8,128)(2,1)S(1)} %get-tuple-element.59.refs_1_), channel_id=1, source_target_pairs={{0,8},{4,12},{8,0},{12,4},{1,9},{5,13},{9,1},{13,5},{2,10},{6,14},... | collective-permute-start | bytes 196616 | tf_op jit(solution)/shard_map/ppermute | solution.py:206
  3.3 11.3 %collective-permute-start = (bf16[16,2048]{1,0:T(8,128)(2,1)S(1)}, bf16[16,2048]{1,0:T(8,128)(2,1)S(1)}, u32[]{:S(2)}, u32[]{:S(2)}) collective-permute-start(bf16[16,2048]{1,0:T(8,128)(2,1)S(1)} %get-tuple-element.60.refs_0_), channel_id=1, source_target_pairs={{0,4},{4,0},{8,12},{12,8},{1,5},{5,1},{9,13},{13,9},{2,6},{6,2},{1... | collective-permute-start | bytes 196616 | tf_op jit(solution)/shard_map/ppermute | solution.py:206
  4.6 10.0 %collective-permute-start.1 = (bf16[16,2048]{1,0:T(8,128)(2,1)S(1)}, bf16[16,2048]{1,0:T(8,128)(2,1)S(1)}, u32[]{:S(2)}, u32[]{:S(2)}) collective-permute-start(bf16[16,2048]{1,0:T(8,128)(2,1)S(1)} %get-tuple-element.59.refs_1_), channel_id=1, source_target_pairs={{0,4},{4,0},{8,12},{12,8},{1,5},{5,1},{9,13},{13,9},{2,6},{6,2},{1... | collective-permute-start | bytes 196616 | tf_op jit(solution)/shard_map/ppermute | solution.py:206
  5.0 9.7 %collective-permute-start.4 = (bf16[16,2048]{1,0:T(8,128)(2,1)S(1)}, bf16[16,2048]{1,0:T(8,128)(2,1)S(1)}, u32[]{:S(2)}, u32[]{:S(2)}) collective-permute-start(bf16[16,2048]{1,0:T(8,128)(2,1)S(1)} %collective-permute-done.2.refs_4_), channel_id=1, source_target_pairs={{0,4},{4,0},{8,12},{12,8},{1,5},{5,1},{9,13},{13,9},{2,6},{6,2},{1... | collective-permute-start | bytes 196616 | tf_op jit(solution)/shard_map/ppermute | solution.py:206
  9.7 5.0 %collective-permute-start.5 = (bf16[16,2048]{1,0:T(8,128)(2,1)S(1)}, bf16[16,2048]{1,0:T(8,128)(2,1)S(1)}, u32[]{:S(2)}, u32[]{:S(2)}) collective-permute-start(bf16[16,2048]{1,0:T(8,128)(2,1)S(1)} %collective-permute-done.3.refs_5_), channel_id=1, source_target_pairs={{0,4},{4,0},{8,12},{12,8},{1,5},{5,1},{9,13},{13,9},{2,6},{6,2},{1... | collective-permute-start | bytes 196616 | tf_op jit(solution)/shard_map/ppermute | solution.py:206
  15.8 8.8 %copy-start.2 = (s32[128]{0:T(128)S(1)}, s32[128]{0:T(128)}, u32[]{:S(2)}) copy-start(s32[128]{0:T(128)} %slots.3) | copy-start | bytes 1540
  15.8 8.8 %copy-start.3 = (s32[32]{0:T(128)S(1)}, s32[32]{0:T(128)}, u32[]{:S(2)}) copy-start(s32[32]{0:T(128)} %lengths.1) | copy-start | bytes 388
  15.8 2.5 %collective-permute-start.6 = (bf16[128,1408]{1,0:T(8,128)(2,1)S(1)}, bf16[128,1408]{1,0:T(8,128)(2,1)S(1)}, u32[]{:S(2)}, u32[]{:S(2)}) collective-permute-start(bf16[128,1408]{1,0:T(8,128)(2,1)S(1)} %get-tuple-element.39.given), channel_id=1, source_target_pairs={{0,1},{1,0},{2,3},{3,2},{4,5},{5,4},{6,7},{7,6},{8,9},{9,8},{10,11... | collective-permute-start | bytes 1081352 | tf_op jit(solution)/shard_map/ppermute | solution.py:206
  18.3 13.3 %collective-permute-start.7 = (bf16[32,1408]{1,0:T(8,128)(2,1)S(1)}, bf16[32,1408]{1,0:T(8,128)(2,1)S(1)}, u32[]{:S(2)}, u32[]{:S(2)}) collective-permute-start(bf16[32,1408]{1,0:T(8,128)(2,1)S(1)} %get-tuple-element.40), channel_id=1, source_target_pairs={{0,8},{2,0},{4,12},{6,4},{8,10},{10,2},{12,14},{14,6},{1,9},{3,1},... | collective-permute-start | bytes 270344 | tf_op jit(solution)/shard_map/ppermute | solution.py:440
  18.6 13.0 %collective-permute-start.8 = (bf16[32,1408]{1,0:T(8,128)(2,1)S(1)}, bf16[32,1408]{1,0:T(8,128)(2,1)S(1)}, u32[]{:S(2)}, u32[]{:S(2)}) collective-permute-start(bf16[32,1408]{1,0:T(8,128)(2,1)S(1)} %get-tuple-element.41), channel_id=1, source_target_pairs={{0,4},{2,12},{4,0},{6,8},{8,6},{10,14},{12,2},{14,10},{1,5},{3,13}... | collective-permute-start | bytes 270344 | tf_op jit(solution)/shard_map/ppermute | solution.py:440
  22.5 9.1 %collective-permute-start.10 = (bf16[32,1280]{1,0:T(8,128)(2,1)S(1)}, bf16[32,1280]{1,0:T(8,128)(2,1)S(1)}, u32[]{:S(2)}, u32[]{:S(2)}) collective-permute-start(bf16[32,1280]{1,0:T(8,128)(2,1)S(1)} %get-tuple-element.43), channel_id=1, source_target_pairs={{0,0},{2,8},{4,4},{6,12},{8,2},{10,10},{12,6},{14,14},{1,1},{3,9},... | collective-permute-start | bytes 245768 | tf_op jit(solution)/shard_map/ppermute | solution.py:440
  24.4 7.2 %collective-permute-start.9 = (bf16[32,1280]{1,0:T(8,128)(2,1)S(1)}, bf16[32,1280]{1,0:T(8,128)(2,1)S(1)}, u32[]{:S(2)}, u32[]{:S(2)}) collective-permute-start(bf16[32,1280]{1,0:T(8,128)(2,1)S(1)} %get-tuple-element.42), channel_id=1, source_target_pairs={{0,12},{2,4},{4,8},{6,0},{8,14},{10,6},{12,10},{14,2},{1,13},{3,5}... | collective-permute-start | bytes 245768 | tf_op jit(solution)/shard_map/ppermute | solution.py:440
  33.3 4.1 %collective-permute-start.13 = (bf16[16,2048]{1,0:T(8,128)(2,1)S(1)}, bf16[16,2048]{1,0:T(8,128)(2,1)S(1)}, u32[]{:S(2)}, u32[]{:S(2)}) collective-permute-start(bf16[16,2048]{1,0:T(8,128)(2,1)S(1)} %get-tuple-element.46.refs_0_), channel_id=1, source_target_pairs={{0,8},{4,12},{8,0},{12,4},{1,9},{5,13},{9,1},{13,5},{2,10},{6,14},... | collective-permute-start | bytes 196616 | tf_op jit(solution)/shard_map/ppermute | solution.py:206
  33.4 6.0 %collective-permute-start.14 = (bf16[16,2048]{1,0:T(8,128)(2,1)S(1)}, bf16[16,2048]{1,0:T(8,128)(2,1)S(1)}, u32[]{:S(2)}, u32[]{:S(2)}) collective-permute-start(bf16[16,2048]{1,0:T(8,128)(2,1)S(1)} %get-tuple-element.47.attended.refs_1_), channel_id=1, source_target_pairs={{0,8},{4,12},{8,0},{12,4},{1,9},{5,13},{9,1},{13,5},{2,10},{6,14},... | collective-permute-start | bytes 196616 | tf_op jit(solution)/shard_map/ppermute | solution.py:206
  35.8 7.1 %collective-permute-start.11 = (bf16[16,2048]{1,0:T(8,128)(2,1)S(1)}, bf16[16,2048]{1,0:T(8,128)(2,1)S(1)}, u32[]{:S(2)}, u32[]{:S(2)}) collective-permute-start(bf16[16,2048]{1,0:T(8,128)(2,1)S(1)} %get-tuple-element.46.refs_0_), channel_id=1, source_target_pairs={{0,4},{4,0},{8,12},{12,8},{1,5},{5,1},{9,13},{13,9},{2,6},{6,2},{1... | collective-permute-start | bytes 196616 | tf_op jit(solution)/shard_map/ppermute | solution.py:206
  35.8 7.1 %collective-permute-start.12 = (bf16[16,2048]{1,0:T(8,128)(2,1)S(1)}, bf16[16,2048]{1,0:T(8,128)(2,1)S(1)}, u32[]{:S(2)}, u32[]{:S(2)}) collective-permute-start(bf16[16,2048]{1,0:T(8,128)(2,1)S(1)} %get-tuple-element.47.attended.refs_1_), channel_id=1, source_target_pairs={{0,4},{4,0},{8,12},{12,8},{1,5},{5,1},{9,13},{13,9},{2,6},{6,2},{1... | collective-permute-start | bytes 196616 | tf_op jit(solution)/shard_map/ppermute | solution.py:206
  37.4 6.4 %collective-permute-start.15 = (bf16[16,2048]{1,0:T(8,128)(2,1)S(1)}, bf16[16,2048]{1,0:T(8,128)(2,1)S(1)}, u32[]{:S(2)}, u32[]{:S(2)}) collective-permute-start(bf16[16,2048]{1,0:T(8,128)(2,1)S(1)} %collective-permute-done.13.refs_4_), channel_id=1, source_target_pairs={{0,4},{4,0},{8,12},{12,8},{1,5},{5,1},{9,13},{13,9},{2,6},{6,2},{1... | collective-permute-start | bytes 196616 | tf_op jit(solution)/shard_map/ppermute | solution.py:206
  39.4 5.8 %collective-permute-start.16 = (bf16[16,2048]{1,0:T(8,128)(2,1)S(1)}, bf16[16,2048]{1,0:T(8,128)(2,1)S(1)}, u32[]{:S(2)}, u32[]{:S(2)}) collective-permute-start(bf16[16,2048]{1,0:T(8,128)(2,1)S(1)} %collective-permute-done.14.refs_5_), channel_id=1, source_target_pairs={{0,4},{4,0},{8,12},{12,8},{1,5},{5,1},{9,13},{13,9},{2,6},{6,2},{1... | collective-permute-start | bytes 196616 | tf_op jit(solution)/shard_map/ppermute | solution.py:206
  46.1 13.8 %copy-start = (bf16[32,4096]{1,0:T(8,128)(2,1)S(1)}, bf16[32,4096]{1,0:T(8,128)(2,1)}, u32[]{:S(2)}) copy-start(bf16[32,4096]{1,0:T(8,128)(2,1)} %hidden.1) | copy-start | bytes 786436
  46.1 2.3 %collective-permute-start.17 = (bf16[128,1024]{1,0:T(8,128)(2,1)S(1)}, bf16[128,1024]{1,0:T(8,128)(2,1)S(1)}, u32[]{:S(2)}, u32[]{:S(2)}) collective-permute-start(bf16[128,1024]{1,0:T(8,128)(2,1)S(1)} %get-tuple-element.52.given), channel_id=1, source_target_pairs={{0,1},{1,0},{2,3},{3,2},{4,5},{5,4},{6,7},{7,6},{8,9},{9,8},{10,11... | collective-permute-start | bytes 786440 | tf_op jit(solution)/shard_map/ppermute | solution.py:206
  48.4 6.7 %collective-permute-start.18 = (bf16[32,1024]{1,0:T(8,128)(2,1)S(1)}, bf16[32,1024]{1,0:T(8,128)(2,1)S(1)}, u32[]{:S(2)}, u32[]{:S(2)}) collective-permute-start(bf16[32,1024]{1,0:T(8,128)(2,1)S(1)} %get-tuple-element.53), channel_id=1, source_target_pairs={{0,8},{2,0},{4,12},{6,4},{8,10},{10,2},{12,14},{14,6},{1,9},{3,1},... | collective-permute-start | bytes 196616 | tf_op jit(solution)/shard_map/ppermute | solution.py:440
  49.4 6.0 %collective-permute-start.19 = (bf16[32,1024]{1,0:T(8,128)(2,1)S(1)}, bf16[32,1024]{1,0:T(8,128)(2,1)S(1)}, u32[]{:S(2)}, u32[]{:S(2)}) collective-permute-start(bf16[32,1024]{1,0:T(8,128)(2,1)S(1)} %get-tuple-element.54), channel_id=1, source_target_pairs={{0,4},{2,12},{4,0},{6,8},{8,6},{10,14},{12,2},{14,10},{1,5},{3,13}... | collective-permute-start | bytes 196616 | tf_op jit(solution)/shard_map/ppermute | solution.py:440
  51.4 5.2 %collective-permute-start.20 = (bf16[32,1024]{1,0:T(8,128)(2,1)S(1)}, bf16[32,1024]{1,0:T(8,128)(2,1)S(1)}, u32[]{:S(2)}, u32[]{:S(2)}) collective-permute-start(bf16[32,1024]{1,0:T(8,128)(2,1)S(1)} %get-tuple-element.55), channel_id=1, source_target_pairs={{0,12},{2,4},{4,8},{6,0},{8,14},{10,6},{12,10},{14,2},{1,13},{3,5}... | collective-permute-start | bytes 196616 | tf_op jit(solution)/shard_map/ppermute | solution.py:440
  52.3 7.5 %collective-permute-start.21 = (bf16[32,1024]{1,0:T(8,128)(2,1)S(1)}, bf16[32,1024]{1,0:T(8,128)(2,1)S(1)}, u32[]{:S(2)}, u32[]{:S(2)}) collective-permute-start(bf16[32,1024]{1,0:T(8,128)(2,1)S(1)} %get-tuple-element.56), channel_id=1, source_target_pairs={{0,0},{2,8},{4,4},{6,12},{8,2},{10,10},{12,6},{14,14},{1,1},{3,9},... | collective-permute-start | bytes 196616 | tf_op jit(solution)/shard_map/ppermute | solution.py:440
  59.9 3.4 %collective-permute-start.22 = (bf16[32,2048]{1,0:T(8,128)(2,1)S(1)}, bf16[32,2048]{1,0:T(8,128)(2,1)S(1)}, u32[]{:S(2)}, u32[]{:S(2)}) collective-permute-start(bf16[32,2048]{1,0:T(8,128)(2,1)S(1)} %get-tuple-element.58), channel_id=1, source_target_pairs={{0,1},{1,0},{2,3},{3,2},{4,5},{5,4},{6,7},{7,6},{8,9},{9,8},{10,11... | collective-permute-start | bytes 393224 | tf_op jit(solution)/shard_map/ppermute | solution.py:206

commit v11 on v10

--- a/solution.py
+++ b/solution.py
@@ -285,10 +285,8 @@
         copy.wait()
 
 
-def stage_out_kernel(weight, attended, give_part, own_part, sems):
-    side = lax.axis_index("side")
-    copies = head_copies(weight, give_part, 1 - side) + head_copies(weight, own_part, side)
-    run_copies(copies, sems)
+def stage_out_kernel(weight, attended, own_part, sems):
+    run_copies(head_copies(weight, own_part, lax.axis_index("side")), sems)
 
 
 def one_hot(slots, scratch, blocks, slot_base, request_base):
@@ -354,12 +352,16 @@
     dot_columns(order, weight, give)
 
 
-def carries(entry, pairs):
-    return entry % pairs == (0 if entry // pairs % 2 else pairs - 1)
+def carries(entry):
+    return entry > 0
+
+
+def sums_entry(run, pairs):
+    return run * pairs + (pairs - 1 if run == 0 else 0)
 
 
 def arrival_order(count, pairs):
-    return sorted(range(count), key=lambda i: (i == 0, not carries(i, pairs), i % pairs, -i))
+    return sorted(range(count), key=lambda i: (i == 0, i % pairs, -i))
 
 
 def merge_kernel(own, given, received, *outs):
@@ -408,7 +410,7 @@
     return call(
         merge_kernel,
         [
-            struct((rows // count, half + (more if carries(i, pairs) else 0))) for i in range(count)
+            struct((rows // count, half + (more if carries(i) else 0))) for i in range(count)
         ],
         [VMEM] * 3,
         [VMEM] * count,
@@ -472,15 +474,17 @@
 
 
 def attend_all(count, parts, cosine, sine, lengths, *refs):
-    blocks, (keys, values), refs = refs[:count], refs[count : count + 2], refs[count + 2 :]
+    blocks, (keys, values, weight), refs = refs[:count], refs[count : count + 3], refs[count + 3 :]
     blocks = in_place(blocks, keys.shape[2] // HEAD_DIM)
-    outs, (scores_of, probs_of) = refs[:parts], refs[parts:]
+    outs, (give_part, scores_of, probs_of, sems) = refs[:parts], refs[parts:]
+    copies = started(head_copies(weight, give_part, 1 - lax.axis_index("side")), sems)
     pairs = keys.shape[2] // HEAD_DIM
     rows, cache = keys.shape[:2]
     low = lax.rem(lax.axis_index("col"), pairs)
     width = GROUP_WIDTH
     squares = sum(
-        blocks[i][:, width:].astype(jnp.float32) for i in range(count) if carries(i, pairs)
+        blocks[sums_entry(run, pairs)][:, width:].astype(jnp.float32)
+        for run in range(count // pairs)
     )
     scale = lax.rsqrt(jnp.sum(squares, axis=1, keepdims=True) / D + EPSILON)
     factor = HEAD_DIM ** (-0.5)
@@ -546,6 +550,8 @@
                     [result[head] for result in results[i * size : (i + 1) * size]], axis=0
                 )
                 out[:, pl.ds(at, HEAD_DIM)] = joined.astype(jnp.bfloat16)
+    for copy in copies:
+        copy.wait()
 
 
 def sum_kernel(count, parts, hidden, *refs):
@@ -629,24 +635,28 @@
         [pltpu.VMEM(square, jnp.float32), pltpu.SemaphoreType.DMA((2 * pairs,))],
     )(cache_lengths, in_hbm(key_cache), in_hbm(value_cache), slot_request)
     runs = (pairs, rows // SLOTS, GROUP * SLOTS, SLOTS * cache)
-    attended = call(
+    *attended, give_out = call(
         functools.partial(attend_all, col_count, parts),
-        [struct((piece, half))] * parts,
-        [VMEM] * (col_count + 5),
-        [VMEM] * parts,
+        [struct((piece, half))] * parts + [pltpu.VMEM((half, half_out), jnp.bfloat16)],
+        [VMEM] * (col_count + 5) + [HBM],
+        [VMEM] * (parts + 1),
         4 * rows * half * cache,
+        half * half_out * 2,
+        [
+            pltpu.VMEM(runs, jnp.float32),
+            pltpu.VMEM(runs, jnp.bfloat16),
+            pltpu.SemaphoreType.DMA((pairs,)),
+        ],
+    )(*tables, *products, in_vmem(key_part), in_vmem(value_part), in_hbm(out_weight))
+
+    own_out = call(
+        stage_out_kernel,
+        pltpu.VMEM((half, half_out), jnp.bfloat16),
+        [HBM, HBM],
+        VMEM,
         0,
-        [pltpu.VMEM(runs, jnp.float32), pltpu.VMEM(runs, jnp.bfloat16)],
-    )(*tables, *products, in_vmem(key_part), in_vmem(value_part))
-
-    give_out, own_out = call(
-        stage_out_kernel,
-        [pltpu.VMEM((half, half_out), jnp.bfloat16)] * 2,
-        [HBM, HBM],
-        [VMEM] * 2,
-        0,
-        half * half_out * 4,
-        [pltpu.SemaphoreType.DMA((2 * pairs,))],
+        half * half_out * 2,
+        [pltpu.SemaphoreType.DMA((pairs,))],
     )(in_hbm(out_weight), attended[-1])
     products = spread(
         project(
@@ -679,6 +689,7 @@
         lax.axis_size("side") == 2
         and qkv_weight.shape[1] == 2 * GROUP_WIDTH
         and col_count % row_count == 0
+        and col_count > row_count
         and col_count & (col_count - 1) == 0
         and hidden_in.shape[0] % 32 == 0
         and key_cache.shape[1] % 16 == 0

time: 64.3 us -> 68.6 us (1.067)
  waiting for transfers between devices: 17 us -> 19.4 us
  Pallas kernels: 16 us -> 17 us
  starting transfers between devices: 29.9 us -> 30.9 us
    ppermute x15, waiting for transfers between devices: 7.45 us -> 10 us  [moved(): return lax.ppermute(value, axis, pairs)]
    pallas_call x1, Pallas kernels: 1.71 us -> 3.89 us  [paired_plan(): call(functools.partial(attend_all, col_count, parts), [struct((piece, hal...]
    ppermute x8, starting transfers between devices: 12.9 us -> 14.7 us  [spread(): lax.ppermute(products[j], ('col', 'row'), [(col * row_count + row, (row *...]
    pallas_call x3, Pallas kernels: 3.62 us -> 2.36 us  [the longest x1 2.24 us: paired_plan(): call(stage_out_kernel, pltpu.VMEM((half, half_out), jnp.bfloat16), [HBM,...]
    ppermute x15, starting transfers between devices: 17.1 us -> 16.2 us  [moved(): return lax.ppermute(value, axis, pairs)]
  transfers between devices with their start and end apart: 23 -> 23, of which waited for: 13 -> 14; matrix products, arithmetic and copies ran while one was open for 0% -> 0% of each run, Pallas kernels for 18% -> 15%
where the time goes in v11:
time: 68.6 us; the launch traced here: 68.3 us
  starting transfers between devices  30.9 us (45%)
  waiting for transfers between devices  19.4 us (28%)
  Pallas kernels  17 us (25%)
  local copies, waits for them, and re-layouts  0.9 us (1%)
    ppermute x15, starting transfers between devices, moved(): return lax.ppermute(value, axis, pairs)  16.2 us
    ppermute x8, starting transfers between devices, spread(): lax.ppermute(products[j], ('col', 'row'), [(col * row_count + row, (row *...  14.7 us
    ppermute x15, waiting for transfers between devices, moved(): return lax.ppermute(value, axis, pairs)  10 us
    ppermute x8, waiting for transfers between devices, spread(): lax.ppermute(products[j], ('col', 'row'), [(col * row_count + row, (row *...  9.36 us
    pallas_call x1, Pallas kernels, paired_plan(): call(functools.partial(stage_in_kernel, col_count), [pltpu.VMEM((half, ha...  4.09 us
    pallas_call x1, Pallas kernels, paired_plan(): call(functools.partial(attend_all, col_count, parts), [struct((piece, hal...  3.89 us
    pallas_call x1, Pallas kernels, paired_plan(): call(functools.partial(stage_cache_kernel, col_count), [pltpu.VMEM((rows,...  2.31 us
    pallas_call x1, Pallas kernels, paired_plan(): call(stage_out_kernel, pltpu.VMEM((half, half_out), jnp.bfloat16), [HBM,...  2.24 us
  transfers between devices with their start and end apart: 23, of which 14 were waited for; matrix products, arithmetic and copies ran while one was open for 0% of the time, Pallas kernels for 15%

profile of v11, /device:TPU:3, one launch (start us, length us, event | category | flops | bytes accessed | tf_op | source)
XLA Modules:
  0.0 68.3 jit_solution(12532053179759831544)
XLA Ops:
  0.0 0.9 %fusion = (bf16[16,2048]{1,0:T(8,128)(2,1)S(1)}, bf16[16,2048]{1,0:T(8,128)(2,1)S(1)}) fusion(bf16[32,4096]{1,0:T(8,128)(2,1)} %hidden.1, s32[]{:T(128)S(6)} %add.4, s32[]{:T(128)S(6)} %select_n.3), kind=kLoop, calls=%fused_computation.1 | loop fusion | bytes 262152 | tf_op jit(solution)/shard_map/slice | solution.py:620
  0.9 2.4 %collective-permute-start.2 = (bf16[16,2048]{1,0:T(8,128)(2,1)S(1)}, bf16[16,2048]{1,0:T(8,128)(2,1)S(1)}, u32[]{:S(2)}, u32[]{:S(2)}) collective-permute-start(bf16[16,2048]{1,0:T(8,128)(2,1)S(1)} %get-tuple-element.58.refs_0_), channel_id=1, source_target_pairs={{0,8},{4,12},{8,0},{12,4},{1,9},{5,13},{9,1},{13,5},{2,10},{6,14},... | collective-permute-start | bytes 196616 | tf_op jit(solution)/shard_map/ppermute | solution.py:206
  3.3 0.1 collective-permute-start.3
  3.3 1.3 %collective-permute-start = (bf16[16,2048]{1,0:T(8,128)(2,1)S(1)}, bf16[16,2048]{1,0:T(8,128)(2,1)S(1)}, u32[]{:S(2)}, u32[]{:S(2)}) collective-permute-start(bf16[16,2048]{1,0:T(8,128)(2,1)S(1)} %get-tuple-element.58.refs_0_), channel_id=1, source_target_pairs={{0,4},{4,0},{8,12},{12,8},{1,5},{5,1},{9,13},{13,9},{2,6},{6,2},{1... | collective-permute-start | bytes 196616 | tf_op jit(solution)/shard_map/ppermute | solution.py:206
  4.6 0.2 collective-permute-start.1
  4.8 0.1 collective-permute-done.2.refs_4_
  5.0 3.8 %collective-permute-start.4 = (bf16[16,2048]{1,0:T(8,128)(2,1)S(1)}, bf16[16,2048]{1,0:T(8,128)(2,1)S(1)}, u32[]{:S(2)}, u32[]{:S(2)}) collective-permute-start(bf16[16,2048]{1,0:T(8,128)(2,1)S(1)} %collective-permute-done.2.refs_4_), channel_id=1, source_target_pairs={{0,4},{4,0},{8,12},{12,8},{1,5},{5,1},{9,13},{13,9},{2,6},{6,2},{1... | collective-permute-start | bytes 196616 | tf_op jit(solution)/shard_map/ppermute | solution.py:206
  8.7 1.0 %collective-permute-done.3.refs_5_ = bf16[16,2048]{1,0:T(8,128)(2,1)S(1)} collective-permute-done((bf16[16,2048]{1,0:T(8,128)(2,1)S(1)}, bf16[16,2048]{1,0:T(8,128)(2,1)S(1)}, u32[]{:S(2)}, u32[]{:S(2)}) %collective-permute-start.3) | collective-permute-done | bytes 65568 | tf_op jit(solution)/shard_map/ppermute | solution.py:206
  9.7 0.8 %collective-permute-start.5 = (bf16[16,2048]{1,0:T(8,128)(2,1)S(1)}, bf16[16,2048]{1,0:T(8,128)(2,1)S(1)}, u32[]{:S(2)}, u32[]{:S(2)}) collective-permute-start(bf16[16,2048]{1,0:T(8,128)(2,1)S(1)} %collective-permute-done.3.refs_5_), channel_id=1, source_target_pairs={{0,4},{4,0},{8,12},{12,8},{1,5},{5,1},{9,13},{13,9},{2,6},{6,2},{1... | collective-permute-start | bytes 196616 | tf_op jit(solution)/shard_map/ppermute | solution.py:206
  10.5 4.1 %shard_map.83 = (bf16[2048,1280]{1,0:T(8,128)(2,1)S(1)}, bf16[2048,1280]{1,0:T(8,128)(2,1)S(1)}, bf16[128,128]{1,0:T(8,128)(2,1)S(1)}) custom-call(bf16[4096,2560]{1,0:T(8,128)(2,1)} %weight.2, s32[128]{0:T(128)} %slots.3), custom_call_target="tpu_custom_call" | custom-call | bytes 10485760 | tf_op jit(solution)/shard_map/pallas_call | solution.py:606
  14.7 1.1 %shard_map.84 = (bf16[128,1408]{1,0:T(8,128)(2,1)S(1)}, bf16[128,2048]{1,0:T(8,128)(2,1)S(1)}) custom-call(bf16[128,128]{1,0:T(8,128)(2,1)S(1)} %get-tuple-element.34.chosen, bf16[16,2048]{1,0:T(8,128)(2,1)S(1)} %get-tuple-element.58.refs_0_, bf16[16,2048]{1,0:T(8,128)(2,1)S(1)} %get-tuple-element.57.refs_1_, ...), custom_call_target="tpu_custom_call" | custom-call | flops 671088640 | bytes 5242880 | tf_op jit(solution)/shard_map/pallas_call | solution.py:393
  15.8 0.0 copy-start.2
  15.8 1.2 %collective-permute-start.6 = (bf16[128,1408]{1,0:T(8,128)(2,1)S(1)}, bf16[128,1408]{1,0:T(8,128)(2,1)S(1)}, u32[]{:S(2)}, u32[]{:S(2)}) collective-permute-start(bf16[128,1408]{1,0:T(8,128)(2,1)S(1)} %get-tuple-element.38.given), channel_id=1, source_target_pairs={{0,1},{1,0},{2,3},{3,2},{4,5},{5,4},{6,7},{7,6},{8,9},{9,8},{10,11... | collective-permute-start | bytes 1081352 | tf_op jit(solution)/shard_map/ppermute | solution.py:206
  16.9 0.9 %shard_map.85.own = f32[128,1280]{1,0:T(8,128)S(1)} custom-call(bf16[128,2048]{1,0:T(8,128)(2,1)S(1)} %get-tuple-element.37.permuted, bf16[2048,1280]{1,0:T(8,128)(2,1)S(1)} %get-tuple-element.35.refs_8_.weight), custom_call_target="tpu_custom_call" | custom-call | flops 671088640 | bytes 5242880 | tf_op jit(solution)/shard_map/pallas_call | solution.py:402
  17.8 0.4 collective-permute-done.6.received
  18.2 0.1 shard_map.86
  18.3 0.3 collective-permute-start.7
  18.6 3.0 %collective-permute-start.8 = (bf16[32,1408]{1,0:T(8,128)(2,1)S(1)}, bf16[32,1408]{1,0:T(8,128)(2,1)S(1)}, u32[]{:S(2)}, u32[]{:S(2)}) collective-permute-start(bf16[32,1408]{1,0:T(8,128)(2,1)S(1)} %get-tuple-element.40), channel_id=1, source_target_pairs={{0,12},{2,4},{4,8},{6,0},{8,14},{10,6},{12,10},{14,2},{1,13},{3,5}... | collective-permute-start | bytes 270344 | tf_op jit(solution)/shard_map/ppermute | solution.py:442
  21.6 1.7 %collective-permute-start.9 = (bf16[32,1408]{1,0:T(8,128)(2,1)S(1)}, bf16[32,1408]{1,0:T(8,128)(2,1)S(1)}, u32[]{:S(2)}, u32[]{:S(2)}) collective-permute-start(bf16[32,1408]{1,0:T(8,128)(2,1)S(1)} %get-tuple-element.41), channel_id=1, source_target_pairs={{0,4},{2,12},{4,0},{6,8},{8,6},{10,14},{12,2},{14,10},{1,5},{3,13}... | collective-permute-start | bytes 270344 | tf_op jit(solution)/shard_map/ppermute | solution.py:442
  23.3 3.3 %collective-permute-start.10 = (bf16[32,1280]{1,0:T(8,128)(2,1)S(1)}, bf16[32,1280]{1,0:T(8,128)(2,1)S(1)}, u32[]{:S(2)}, u32[]{:S(2)}) collective-permute-start(bf16[32,1280]{1,0:T(8,128)(2,1)S(1)} %get-tuple-element.42), channel_id=1, source_target_pairs={{0,0},{2,8},{4,4},{6,12},{8,2},{10,10},{12,6},{14,14},{1,1},{3,9},... | collective-permute-start | bytes 245768 | tf_op jit(solution)/shard_map/ppermute | solution.py:442
  26.6 2.3 %shard_map.82 = (bf16[32,64,256]{2,1,0:T(8,128)(2,1)S(1)}, bf16[32,64,256]{2,1,0:T(8,128)(2,1)S(1)}, f32[32,128]{1,0:T(8,128)S(1)}, f32[32,128]{1,0:T(8,128)S(1)...) custom-call(s32[32]{0:T(128)S(1)} %copy-done.3, bf16[32,64,512]{2,1,0:T(8,128)(2,1)} %keys.1, ...), custom_call_target="tpu_custom_call" | custom-call | bytes 2097152 | tf_op jit(solution)/shard_map/pallas_call | solution.py:627
  29.0 4.0 %collective-permute-done.10.refs_3_ = bf16[32,1280]{1,0:T(8,128)(2,1)S(1)} collective-permute-done((bf16[32,1280]{1,0:T(8,128)(2,1)S(1)}, bf16[32,1280]{1,0:T(8,128)(2,1)S(1)}, u32[]{:S(2)}, u32[]{:S(2)}) %collective-permute-start.10) | collective-permute-done | bytes 81952 | tf_op jit(solution)/shard_map/ppermute | solution.py:442
  33.0 3.9 %shard_map.87 = (bf16[16,2048]{1,0:T(8,128)(2,1)S(1)}, bf16[16,2048]{1,0:T(8,128)(2,1)S(1)}, bf16[2048,1024]{1,0:T(8,128)(2,1)S(1)}) custom-call(f32[32,128]{1,0:T(8,128)S(1)} %get-tuple-element.31.cosine, f32[32,128]{1,0:T(8,128)S(1)} %get-tuple-element.32.sine, s32[32,128]{1,0:T(8,128)S(1)} %get-tuple-element.33.lengths, ...), custom_call_target="tpu_custom_call" | custom-call | flops 16777216 | bytes 4194304 | tf_op jit(solution)/shard_map/pallas_call | solution.py:638
  36.9 0.1 collective-permute-start.13
  36.9 2.4 %collective-permute-start.14 = (bf16[16,2048]{1,0:T(8,128)(2,1)S(1)}, bf16[16,2048]{1,0:T(8,128)(2,1)S(1)}, u32[]{:S(2)}, u32[]{:S(2)}) collective-permute-start(bf16[16,2048]{1,0:T(8,128)(2,1)S(1)} %get-tuple-element.46.attended.refs_1_), channel_id=1, source_target_pairs={{0,8},{4,12},{8,0},{12,4},{1,9},{5,13},{9,1},{13,5},{2,10},{6,14},... | collective-permute-start | bytes 196616 | tf_op jit(solution)/shard_map/ppermute | solution.py:206
  39.3 1.5 %collective-permute-start.12 = (bf16[16,2048]{1,0:T(8,128)(2,1)S(1)}, bf16[16,2048]{1,0:T(8,128)(2,1)S(1)}, u32[]{:S(2)}, u32[]{:S(2)}) collective-permute-start(bf16[16,2048]{1,0:T(8,128)(2,1)S(1)} %get-tuple-element.46.attended.refs_1_), channel_id=1, source_target_pairs={{0,4},{4,0},{8,12},{12,8},{1,5},{5,1},{9,13},{13,9},{2,6},{6,2},{1... | collective-permute-start | bytes 196616 | tf_op jit(solution)/shard_map/ppermute | solution.py:206
  40.8 2.5 %collective-permute-done.13.refs_4_ = bf16[16,2048]{1,0:T(8,128)(2,1)S(1)} collective-permute-done((bf16[16,2048]{1,0:T(8,128)(2,1)S(1)}, bf16[16,2048]{1,0:T(8,128)(2,1)S(1)}, u32[]{:S(2)}, u32[]{:S(2)}) %collective-permute-start.13) | collective-permute-done | bytes 65568 | tf_op jit(solution)/shard_map/ppermute | solution.py:206
  43.3 1.4 %collective-permute-done.14.refs_5_ = bf16[16,2048]{1,0:T(8,128)(2,1)S(1)} collective-permute-done((bf16[16,2048]{1,0:T(8,128)(2,1)S(1)}, bf16[16,2048]{1,0:T(8,128)(2,1)S(1)}, u32[]{:S(2)}, u32[]{:S(2)}) %collective-permute-start.14) | collective-permute-done | bytes 65568 | tf_op jit(solution)/shard_map/ppermute | solution.py:206
  44.7 0.1 collective-permute-start.16
  44.7 2.2 %shard_map.88.refs_8_.weight = bf16[2048,1024]{1,0:T(8,128)(2,1)S(1)} custom-call(bf16[4096,2048]{1,0:T(8,128)(2,1)} %weight.3, bf16[16,2048]{1,0:T(8,128)(2,1)S(1)} %get-tuple-element.46.attended.refs_1_), custom_call_target="tpu_custom_call" | custom-call | bytes 4194304 | tf_op jit(solution)/shard_map/pallas_call | solution.py:652
  47.0 0.3 collective-permute-done.12.refs_3_
  47.3 1.4 %collective-permute-done.15.refs_6_ = bf16[16,2048]{1,0:T(8,128)(2,1)S(1)} collective-permute-done((bf16[16,2048]{1,0:T(8,128)(2,1)S(1)}, bf16[16,2048]{1,0:T(8,128)(2,1)S(1)}, u32[]{:S(2)}, u32[]{:S(2)}) %collective-permute-start.15) | collective-permute-done | bytes 65568 | tf_op jit(solution)/shard_map/ppermute | solution.py:206
  48.7 1.4 %collective-permute-done.16.refs_7_ = bf16[16,2048]{1,0:T(8,128)(2,1)S(1)} collective-permute-done((bf16[16,2048]{1,0:T(8,128)(2,1)S(1)}, bf16[16,2048]{1,0:T(8,128)(2,1)S(1)}, u32[]{:S(2)}, u32[]{:S(2)}) %collective-permute-start.16) | collective-permute-done | bytes 65568 | tf_op jit(solution)/shard_map/ppermute | solution.py:206
  50.1 0.8 %shard_map.89 = (bf16[128,1024]{1,0:T(8,128)(2,1)S(1)}, bf16[128,2048]{1,0:T(8,128)(2,1)S(1)}) custom-call(bf16[128,128]{1,0:T(8,128)(2,1)S(1)} %get-tuple-element.47.chosen, bf16[16,2048]{1,0:T(8,128)(2,1)S(1)} %get-tuple-element.45.refs_0_, bf16[16,2048]{1,0:T(8,128)(2,1)S(1)} %get-tuple-element.46.attended.refs_1_, ...), custom_call_target="tpu_custom_call" | custom-call | flops 536870912 | bytes 4194304 | tf_op jit(solution)/shard_map/pallas_call | solution.py:393
  51.0 0.6 collective-permute-start.17
  51.6 0.7 %shard_map.90.own = f32[128,1024]{1,0:T(8,128)S(1)} custom-call(bf16[128,2048]{1,0:T(8,128)(2,1)S(1)} %get-tuple-element.49.permuted, bf16[2048,1024]{1,0:T(8,128)(2,1)S(1)} %shard_map.88.refs_8_.weight), custom_call_target="tpu_custom_call" | custom-call | flops 536870912 | bytes 4194304 | tf_op jit(solution)/shard_map/pallas_call | solution.py:402
  52.3 0.4 collective-permute-done.17.received
  52.8 0.1 collective-permute-start.18
  52.9 0.6 collective-permute-start.19
  53.5 3.8 %collective-permute-start.20 = (bf16[32,1024]{1,0:T(8,128)(2,1)S(1)}, bf16[32,1024]{1,0:T(8,128)(2,1)S(1)}, u32[]{:S(2)}, u32[]{:S(2)}) collective-permute-start(bf16[32,1024]{1,0:T(8,128)(2,1)S(1)} %get-tuple-element.53), channel_id=1, source_target_pairs={{0,4},{2,12},{4,0},{6,8},{8,6},{10,14},{12,2},{14,10},{1,5},{3,13}... | collective-permute-start | bytes 196616 | tf_op jit(solution)/shard_map/ppermute | solution.py:442
  57.3 1.9 %collective-permute-start.21 = (bf16[32,1024]{1,0:T(8,128)(2,1)S(1)}, bf16[32,1024]{1,0:T(8,128)(2,1)S(1)}, u32[]{:S(2)}, u32[]{:S(2)}) collective-permute-start(bf16[32,1024]{1,0:T(8,128)(2,1)S(1)} %get-tuple-element.54), channel_id=1, source_target_pairs={{0,0},{2,8},{4,4},{6,12},{8,2},{10,10},{12,6},{14,14},{1,1},{3,9},... | collective-permute-start | bytes 196616 | tf_op jit(solution)/shard_map/ppermute | solution.py:442
  59.2 0.4 collective-permute-done.18.refs_2_
  59.6 0.3 collective-permute-done.20.refs_4_
  60.0 4.7 %collective-permute-done.21.refs_5_ = bf16[32,1024]{1,0:T(8,128)(2,1)S(1)} collective-permute-done((bf16[32,1024]{1,0:T(8,128)(2,1)S(1)}, bf16[32,1024]{1,0:T(8,128)(2,1)S(1)}, u32[]{:S(2)}, u32[]{:S(2)}) %collective-permute-start.21) | collective-permute-done | bytes 65568 | tf_op jit(solution)/shard_map/ppermute | solution.py:442
  64.6 0.1 shard_map.92
  64.7 1.9 %collective-permute-start.22 = (bf16[32,2048]{1,0:T(8,128)(2,1)S(1)}, bf16[32,2048]{1,0:T(8,128)(2,1)S(1)}, u32[]{:S(2)}, u32[]{:S(2)}) collective-permute-start(bf16[32,2048]{1,0:T(8,128)(2,1)S(1)} %get-tuple-element.56), channel_id=1, source_target_pairs={{0,1},{1,0},{2,3},{3,2},{4,5},{5,4},{6,7},{7,6},{8,9},{9,8},{10,11... | collective-permute-start | bytes 393224 | tf_op jit(solution)/shard_map/ppermute | solution.py:206
  66.6 1.0 %collective-permute-done.22.received = bf16[32,2048]{1,0:T(8,128)(2,1)S(1)} collective-permute-done((bf16[32,2048]{1,0:T(8,128)(2,1)S(1)}, bf16[32,2048]{1,0:T(8,128)(2,1)S(1)}, u32[]{:S(2)}, u32[]{:S(2)}) %collective-permute-start.22) | collective-permute-done | bytes 131104 | tf_op jit(solution)/shard_map/ppermute | solution.py:206
  67.6 0.7 %shard_map.93 = bf16[1,32,4096]{2,1,0:T(8,128)(2,1)} custom-call(bf16[32,2048]{1,0:T(8,128)(2,1)S(1)} %get-tuple-element.55.keep, bf16[32,2048]{1,0:T(8,128)(2,1)S(1)} %collective-permute-done.22.received), custom_call_target="tpu_custom_call" | custom-call | bytes 524288 | tf_op jit(solution)/shard_map/pallas_call | solution.py:674
  (19 shorter events, 0.1 us)
Async XLA Ops:
  0.9 4.1 %collective-permute-start.2 = (bf16[16,2048]{1,0:T(8,128)(2,1)S(1)}, bf16[16,2048]{1,0:T(8,128)(2,1)S(1)}, u32[]{:S(2)}, u32[]{:S(2)}) collective-permute-start(bf16[16,2048]{1,0:T(8,128)(2,1)S(1)} %get-tuple-element.58.refs_0_), channel_id=1, source_target_pairs={{0,8},{4,12},{8,0},{12,4},{1,9},{5,13},{9,1},{13,5},{2,10},{6,14},... | collective-permute-start | bytes 196616 | tf_op jit(solution)/shard_map/ppermute | solution.py:206
  3.3 11.4 %copy-start.1 = (bf16[4096]{0:T(1024)(128)(2,1)S(1)}, bf16[4096]{0:T(1024)(128)(2,1)}, u32[]{:S(2)}) copy-start(bf16[4096]{0:T(1024)(128)(2,1)} %param.9) | copy-start | bytes 24580
  3.3 6.4 %collective-permute-start.3 = (bf16[16,2048]{1,0:T(8,128)(2,1)S(1)}, bf16[16,2048]{1,0:T(8,128)(2,1)S(1)}, u32[]{:S(2)}, u32[]{:S(2)}) collective-permute-start(bf16[16,2048]{1,0:T(8,128)(2,1)S(1)} %get-tuple-element.57.refs_1_), channel_id=1, source_target_pairs={{0,8},{4,12},{8,0},{12,4},{1,9},{5,13},{9,1},{13,5},{2,10},{6,14},... | collective-permute-start | bytes 196616 | tf_op jit(solution)/shard_map/ppermute | solution.py:206
  3.3 11.3 %collective-permute-start = (bf16[16,2048]{1,0:T(8,128)(2,1)S(1)}, bf16[16,2048]{1,0:T(8,128)(2,1)S(1)}, u32[]{:S(2)}, u32[]{:S(2)}) collective-permute-start(bf16[16,2048]{1,0:T(8,128)(2,1)S(1)} %get-tuple-element.58.refs_0_), channel_id=1, source_target_pairs={{0,4},{4,0},{8,12},{12,8},{1,5},{5,1},{9,13},{13,9},{2,6},{6,2},{1... | collective-permute-start | bytes 196616 | tf_op jit(solution)/shard_map/ppermute | solution.py:206
  4.6 10.0 %collective-permute-start.1 = (bf16[16,2048]{1,0:T(8,128)(2,1)S(1)}, bf16[16,2048]{1,0:T(8,128)(2,1)S(1)}, u32[]{:S(2)}, u32[]{:S(2)}) collective-permute-start(bf16[16,2048]{1,0:T(8,128)(2,1)S(1)} %get-tuple-element.57.refs_1_), channel_id=1, source_target_pairs={{0,4},{4,0},{8,12},{12,8},{1,5},{5,1},{9,13},{13,9},{2,6},{6,2},{1... | collective-permute-start | bytes 196616 | tf_op jit(solution)/shard_map/ppermute | solution.py:206
  5.0 9.7 %collective-permute-start.4 = (bf16[16,2048]{1,0:T(8,128)(2,1)S(1)}, bf16[16,2048]{1,0:T(8,128)(2,1)S(1)}, u32[]{:S(2)}, u32[]{:S(2)}) collective-permute-start(bf16[16,2048]{1,0:T(8,128)(2,1)S(1)} %collective-permute-done.2.refs_4_), channel_id=1, source_target_pairs={{0,4},{4,0},{8,12},{12,8},{1,5},{5,1},{9,13},{13,9},{2,6},{6,2},{1... | collective-permute-start | bytes 196616 | tf_op jit(solution)/shard_map/ppermute | solution.py:206
  9.7 5.0 %collective-permute-start.5 = (bf16[16,2048]{1,0:T(8,128)(2,1)S(1)}, bf16[16,2048]{1,0:T(8,128)(2,1)S(1)}, u32[]{:S(2)}, u32[]{:S(2)}) collective-permute-start(bf16[16,2048]{1,0:T(8,128)(2,1)S(1)} %collective-permute-done.3.refs_5_), channel_id=1, source_target_pairs={{0,4},{4,0},{8,12},{12,8},{1,5},{5,1},{9,13},{13,9},{2,6},{6,2},{1... | collective-permute-start | bytes 196616 | tf_op jit(solution)/shard_map/ppermute | solution.py:206
  15.8 10.9 %copy-start.2 = (s32[128]{0:T(128)S(1)}, s32[128]{0:T(128)}, u32[]{:S(2)}) copy-start(s32[128]{0:T(128)} %slots.3) | copy-start | bytes 1540
  15.8 10.9 %copy-start.3 = (s32[32]{0:T(128)S(1)}, s32[32]{0:T(128)}, u32[]{:S(2)}) copy-start(s32[32]{0:T(128)} %lengths.1) | copy-start | bytes 388
  15.8 2.5 %collective-permute-start.6 = (bf16[128,1408]{1,0:T(8,128)(2,1)S(1)}, bf16[128,1408]{1,0:T(8,128)(2,1)S(1)}, u32[]{:S(2)}, u32[]{:S(2)}) collective-permute-start(bf16[128,1408]{1,0:T(8,128)(2,1)S(1)} %get-tuple-element.38.given), channel_id=1, source_target_pairs={{0,1},{1,0},{2,3},{3,2},{4,5},{5,4},{6,7},{7,6},{8,9},{9,8},{10,11... | collective-permute-start | bytes 1081352 | tf_op jit(solution)/shard_map/ppermute | solution.py:206
  18.3 14.6 %collective-permute-start.7 = (bf16[32,1408]{1,0:T(8,128)(2,1)S(1)}, bf16[32,1408]{1,0:T(8,128)(2,1)S(1)}, u32[]{:S(2)}, u32[]{:S(2)}) collective-permute-start(bf16[32,1408]{1,0:T(8,128)(2,1)S(1)} %get-tuple-element.39), channel_id=1, source_target_pairs={{0,8},{2,0},{4,12},{6,4},{8,10},{10,2},{12,14},{14,6},{1,9},{3,1},... | collective-permute-start | bytes 270344 | tf_op jit(solution)/shard_map/ppermute | solution.py:442
  18.6 14.3 %collective-permute-start.8 = (bf16[32,1408]{1,0:T(8,128)(2,1)S(1)}, bf16[32,1408]{1,0:T(8,128)(2,1)S(1)}, u32[]{:S(2)}, u32[]{:S(2)}) collective-permute-start(bf16[32,1408]{1,0:T(8,128)(2,1)S(1)} %get-tuple-element.40), channel_id=1, source_target_pairs={{0,12},{2,4},{4,8},{6,0},{8,14},{10,6},{12,10},{14,2},{1,13},{3,5}... | collective-permute-start | bytes 270344 | tf_op jit(solution)/shard_map/ppermute | solution.py:442
  21.6 11.4 %collective-permute-start.9 = (bf16[32,1408]{1,0:T(8,128)(2,1)S(1)}, bf16[32,1408]{1,0:T(8,128)(2,1)S(1)}, u32[]{:S(2)}, u32[]{:S(2)}) collective-permute-start(bf16[32,1408]{1,0:T(8,128)(2,1)S(1)} %get-tuple-element.41), channel_id=1, source_target_pairs={{0,4},{2,12},{4,0},{6,8},{8,6},{10,14},{12,2},{14,10},{1,5},{3,13}... | collective-permute-start | bytes 270344 | tf_op jit(solution)/shard_map/ppermute | solution.py:442
  23.3 9.6 %collective-permute-start.10 = (bf16[32,1280]{1,0:T(8,128)(2,1)S(1)}, bf16[32,1280]{1,0:T(8,128)(2,1)S(1)}, u32[]{:S(2)}, u32[]{:S(2)}) collective-permute-start(bf16[32,1280]{1,0:T(8,128)(2,1)S(1)} %get-tuple-element.42), channel_id=1, source_target_pairs={{0,0},{2,8},{4,4},{6,12},{8,2},{10,10},{12,6},{14,14},{1,1},{3,9},... | collective-permute-start | bytes 245768 | tf_op jit(solution)/shard_map/ppermute | solution.py:442
  36.9 6.4 %collective-permute-start.13 = (bf16[16,2048]{1,0:T(8,128)(2,1)S(1)}, bf16[16,2048]{1,0:T(8,128)(2,1)S(1)}, u32[]{:S(2)}, u32[]{:S(2)}) collective-permute-start(bf16[16,2048]{1,0:T(8,128)(2,1)S(1)} %get-tuple-element.45.refs_0_), channel_id=1, source_target_pairs={{0,8},{4,12},{8,0},{12,4},{1,9},{5,13},{9,1},{13,5},{2,10},{6,14},... | collective-permute-start | bytes 196616 | tf_op jit(solution)/shard_map/ppermute | solution.py:206
  36.9 7.7 %collective-permute-start.14 = (bf16[16,2048]{1,0:T(8,128)(2,1)S(1)}, bf16[16,2048]{1,0:T(8,128)(2,1)S(1)}, u32[]{:S(2)}, u32[]{:S(2)}) collective-permute-start(bf16[16,2048]{1,0:T(8,128)(2,1)S(1)} %get-tuple-element.46.attended.refs_1_), channel_id=1, source_target_pairs={{0,8},{4,12},{8,0},{12,4},{1,9},{5,13},{9,1},{13,5},{2,10},{6,14},... | collective-permute-start | bytes 196616 | tf_op jit(solution)/shard_map/ppermute | solution.py:206
  39.3 7.7 %collective-permute-start.11 = (bf16[16,2048]{1,0:T(8,128)(2,1)S(1)}, bf16[16,2048]{1,0:T(8,128)(2,1)S(1)}, u32[]{:S(2)}, u32[]{:S(2)}) collective-permute-start(bf16[16,2048]{1,0:T(8,128)(2,1)S(1)} %get-tuple-element.45.refs_0_), channel_id=1, source_target_pairs={{0,4},{4,0},{8,12},{12,8},{1,5},{5,1},{9,13},{13,9},{2,6},{6,2},{1... | collective-permute-start | bytes 196616 | tf_op jit(solution)/shard_map/ppermute | solution.py:206
  39.3 8.0 %collective-permute-start.12 = (bf16[16,2048]{1,0:T(8,128)(2,1)S(1)}, bf16[16,2048]{1,0:T(8,128)(2,1)S(1)}, u32[]{:S(2)}, u32[]{:S(2)}) collective-permute-start(bf16[16,2048]{1,0:T(8,128)(2,1)S(1)} %get-tuple-element.46.attended.refs_1_), channel_id=1, source_target_pairs={{0,4},{4,0},{8,12},{12,8},{1,5},{5,1},{9,13},{13,9},{2,6},{6,2},{1... | collective-permute-start | bytes 196616 | tf_op jit(solution)/shard_map/ppermute | solution.py:206
  43.3 5.4 %collective-permute-start.15 = (bf16[16,2048]{1,0:T(8,128)(2,1)S(1)}, bf16[16,2048]{1,0:T(8,128)(2,1)S(1)}, u32[]{:S(2)}, u32[]{:S(2)}) collective-permute-start(bf16[16,2048]{1,0:T(8,128)(2,1)S(1)} %collective-permute-done.13.refs_4_), channel_id=1, source_target_pairs={{0,4},{4,0},{8,12},{12,8},{1,5},{5,1},{9,13},{13,9},{2,6},{6,2},{1... | collective-permute-start | bytes 196616 | tf_op jit(solution)/shard_map/ppermute | solution.py:206
  44.7 5.4 %collective-permute-start.16 = (bf16[16,2048]{1,0:T(8,128)(2,1)S(1)}, bf16[16,2048]{1,0:T(8,128)(2,1)S(1)}, u32[]{:S(2)}, u32[]{:S(2)}) collective-permute-start(bf16[16,2048]{1,0:T(8,128)(2,1)S(1)} %collective-permute-done.14.refs_5_), channel_id=1, source_target_pairs={{0,4},{4,0},{8,12},{12,8},{1,5},{5,1},{9,13},{13,9},{2,6},{6,2},{1... | collective-permute-start | bytes 196616 | tf_op jit(solution)/shard_map/ppermute | solution.py:206
  50.9 13.7 %copy-start = (bf16[32,4096]{1,0:T(8,128)(2,1)S(1)}, bf16[32,4096]{1,0:T(8,128)(2,1)}, u32[]{:S(2)}) copy-start(bf16[32,4096]{1,0:T(8,128)(2,1)} %hidden.1) | copy-start | bytes 786436
  51.0 1.8 %collective-permute-start.17 = (bf16[128,1024]{1,0:T(8,128)(2,1)S(1)}, bf16[128,1024]{1,0:T(8,128)(2,1)S(1)}, u32[]{:S(2)}, u32[]{:S(2)}) collective-permute-start(bf16[128,1024]{1,0:T(8,128)(2,1)S(1)} %get-tuple-element.50.given), channel_id=1, source_target_pairs={{0,1},{1,0},{2,3},{3,2},{4,5},{5,4},{6,7},{7,6},{8,9},{9,8},{10,11... | collective-permute-start | bytes 786440 | tf_op jit(solution)/shard_map/ppermute | solution.py:206
  52.8 6.8 %collective-permute-start.18 = (bf16[32,1024]{1,0:T(8,128)(2,1)S(1)}, bf16[32,1024]{1,0:T(8,128)(2,1)S(1)}, u32[]{:S(2)}, u32[]{:S(2)}) collective-permute-start(bf16[32,1024]{1,0:T(8,128)(2,1)S(1)} %get-tuple-element.51), channel_id=1, source_target_pairs={{0,8},{2,0},{4,12},{6,4},{8,10},{10,2},{12,14},{14,6},{1,9},{3,1},... | collective-permute-start | bytes 196616 | tf_op jit(solution)/shard_map/ppermute | solution.py:442
  52.9 6.7 %collective-permute-start.19 = (bf16[32,1024]{1,0:T(8,128)(2,1)S(1)}, bf16[32,1024]{1,0:T(8,128)(2,1)S(1)}, u32[]{:S(2)}, u32[]{:S(2)}) collective-permute-start(bf16[32,1024]{1,0:T(8,128)(2,1)S(1)} %get-tuple-element.52), channel_id=1, source_target_pairs={{0,12},{2,4},{4,8},{6,0},{8,14},{10,6},{12,10},{14,2},{1,13},{3,5}... | collective-permute-start | bytes 196616 | tf_op jit(solution)/shard_map/ppermute | solution.py:442
  53.5 6.4 %collective-permute-start.20 = (bf16[32,1024]{1,0:T(8,128)(2,1)S(1)}, bf16[32,1024]{1,0:T(8,128)(2,1)S(1)}, u32[]{:S(2)}, u32[]{:S(2)}) collective-permute-start(bf16[32,1024]{1,0:T(8,128)(2,1)S(1)} %get-tuple-element.53), channel_id=1, source_target_pairs={{0,4},{2,12},{4,0},{6,8},{8,6},{10,14},{12,2},{14,10},{1,5},{3,13}... | collective-permute-start | bytes 196616 | tf_op jit(solution)/shard_map/ppermute | solution.py:442
  57.3 7.3 %collective-permute-start.21 = (bf16[32,1024]{1,0:T(8,128)(2,1)S(1)}, bf16[32,1024]{1,0:T(8,128)(2,1)S(1)}, u32[]{:S(2)}, u32[]{:S(2)}) collective-permute-start(bf16[32,1024]{1,0:T(8,128)(2,1)S(1)} %get-tuple-element.54), channel_id=1, source_target_pairs={{0,0},{2,8},{4,4},{6,12},{8,2},{10,10},{12,6},{14,14},{1,1},{3,9},... | collective-permute-start | bytes 196616 | tf_op jit(solution)/shard_map/ppermute | solution.py:442
  64.7 2.9 %collective-permute-start.22 = (bf16[32,2048]{1,0:T(8,128)(2,1)S(1)}, bf16[32,2048]{1,0:T(8,128)(2,1)S(1)}, u32[]{:S(2)}, u32[]{:S(2)}) collective-permute-start(bf16[32,2048]{1,0:T(8,128)(2,1)S(1)} %get-tuple-element.56), channel_id=1, source_target_pairs={{0,1},{1,0},{2,3},{3,2},{4,5},{5,4},{6,7},{7,6},{8,9},{9,8},{10,11... | collective-permute-start | bytes 393224 | tf_op jit(solution)/shard_map/ppermute | solution.py:206

commit v12 on v11

--- a/solution.py
+++ b/solution.py
@@ -265,8 +265,8 @@
     return copies
 
 
-def stage_cache_kernel(blocks, lengths, keys, values, slots, *refs):
-    key_part, value_part, cosine, sine, length_of, chosen, scratch, sems = refs
+def stage_rest_kernel(blocks, lengths, weight, keys, values, slots, *refs):
+    target, key_part, value_part, cosine, sine, length_of, chosen, scratch, sems = refs
     side, col, run = position()
     copies = []
     for j in range(key_part.shape[2] // HEAD_DIM):
@@ -278,7 +278,7 @@
                     part.at[:, :, pl.ds(j * HEAD_DIM, HEAD_DIM)],
                 )
             )
-    copies = started(copies, sems)
+    copies = started(copies + head_copies(weight, target, 1 - side), sems)
     cosine[...], sine[...], length_of[...] = rope(lengths, cosine.shape[0])
     chosen[...] = one_hot(slots, scratch, blocks, col, run).T.astype(jnp.bfloat16)
     for copy in copies:
@@ -474,10 +474,9 @@
 
 
 def attend_all(count, parts, cosine, sine, lengths, *refs):
-    blocks, (keys, values, weight), refs = refs[:count], refs[count : count + 3], refs[count + 3 :]
+    blocks, (keys, values), refs = refs[:count], refs[count : count + 2], refs[count + 2 :]
     blocks = in_place(blocks, keys.shape[2] // HEAD_DIM)
-    outs, (give_part, scores_of, probs_of, sems) = refs[:parts], refs[parts:]
-    copies = started(head_copies(weight, give_part, 1 - lax.axis_index("side")), sems)
+    outs, (scores_of, probs_of) = refs[:parts], refs[parts:]
     pairs = keys.shape[2] // HEAD_DIM
     rows, cache = keys.shape[:2]
     low = lax.rem(lax.axis_index("col"), pairs)
@@ -550,8 +549,6 @@
                     [result[head] for result in results[i * size : (i + 1) * size]], axis=0
                 )
                 out[:, pl.ds(at, HEAD_DIM)] = joined.astype(jnp.bfloat16)
-    for copy in copies:
-        copy.wait()
 
 
 def sum_kernel(count, parts, hidden, *refs):
@@ -624,30 +621,27 @@
     )
 
     table = struct((rows, HEAD_DIM), jnp.float32)
-    key_part, value_part, *tables, chosen_out = call(
-        functools.partial(stage_cache_kernel, col_count),
-        [pltpu.VMEM((rows, cache, pairs * HEAD_DIM), jnp.bfloat16)] * 2
+    give_out, key_part, value_part, *tables, chosen_out = call(
+        functools.partial(stage_rest_kernel, col_count),
+        [pltpu.VMEM((half, half_out), jnp.bfloat16)]
+        + [pltpu.VMEM((rows, cache, pairs * HEAD_DIM), jnp.bfloat16)] * 2
         + [table, table, struct((rows, HEAD_DIM), jnp.int32), struct(square)],
-        [SMEM, HBM, HBM, VMEM],
-        [VMEM] * 6,
+        [SMEM, HBM, HBM, HBM, VMEM],
+        [VMEM] * 7,
         0,
-        4 * rows * cache * pairs * HEAD_DIM,
-        [pltpu.VMEM(square, jnp.float32), pltpu.SemaphoreType.DMA((2 * pairs,))],
-    )(cache_lengths, in_hbm(key_cache), in_hbm(value_cache), slot_request)
+        half * half_out * 2 + 4 * rows * cache * pairs * HEAD_DIM,
+        [pltpu.VMEM(square, jnp.float32), pltpu.SemaphoreType.DMA((3 * pairs,))],
+    )(cache_lengths, in_hbm(out_weight), in_hbm(key_cache), in_hbm(value_cache), slot_request)
     runs = (pairs, rows // SLOTS, GROUP * SLOTS, SLOTS * cache)
-    *attended, give_out = call(
+    attended = call(
         functools.partial(attend_all, col_count, parts),
-        [struct((piece, half))] * parts + [pltpu.VMEM((half, half_out), jnp.bfloat16)],
-        [VMEM] * (col_count + 5) + [HBM],
-        [VMEM] * (parts + 1),
+        [struct((piece, half))] * parts,
+        [VMEM] * (col_count + 5),
+        [VMEM] * parts,
         4 * rows * half * cache,
-        half * half_out * 2,
-        [
-            pltpu.VMEM(runs, jnp.float32),
-            pltpu.VMEM(runs, jnp.bfloat16),
-            pltpu.SemaphoreType.DMA((pairs,)),
-        ],
-    )(*tables, *products, in_vmem(key_part), in_vmem(value_part), in_hbm(out_weight))
+        0,
+        [pltpu.VMEM(runs, jnp.float32), pltpu.VMEM(runs, jnp.bfloat16)],
+    )(*tables, *products, in_vmem(key_part), in_vmem(value_part))
 
     own_out = call(
         stage_out_kernel,

time: 68.6 us -> 65.9 us (0.961)
  waiting for transfers between devices: 19.4 us -> 16.6 us
  starting transfers between devices: 30.9 us -> 31.8 us
  Pallas kernels: 17 us -> 16.2 us
    pallas_call x1, Pallas kernels: 3.89 us -> 1.73 us  [paired_plan(): call(functools.partial(attend_all, col_count, parts), [struct((piece, hal...]
    ppermute x8, waiting for transfers between devices: 9.36 us -> 7.48 us  [spread(): lax.ppermute(products[j], ('col', 'row'), [(col * row_count + row, (row *...]
    pallas_call x1, Pallas kernels: 2.31 us -> 3.71 us  [paired_plan(): call(functools.partial(stage_rest_kernel, col_count), [pltpu.VMEM((half,...]
    ppermute x15, starting transfers between devices: 16.2 us -> 17.1 us  [moved(): return lax.ppermute(value, axis, pairs)]
    ppermute x15, waiting for transfers between devices: 10 us -> 9.16 us  [moved(): return lax.ppermute(value, axis, pairs)]
  transfers between devices with their start and end apart: 23 -> 23, of which waited for: 14 -> 12; matrix products, arithmetic and copies ran while one was open for 0% -> 0% of each run, Pallas kernels for 15% -> 18%
where the time goes in v12:
time: 65.9 us; the launch traced here: 65.7 us
  starting transfers between devices  31.8 us (48%)
  waiting for transfers between devices  16.6 us (25%)
  Pallas kernels  16.2 us (25%)
  local copies, waits for them, and re-layouts  0.9 us (1%)
    ppermute x15, starting transfers between devices, moved(): return lax.ppermute(value, axis, pairs)  17.1 us
    ppermute x8, starting transfers between devices, spread(): lax.ppermute(products[j], ('col', 'row'), [(col * row_count + row, (row *...  14.7 us
    ppermute x15, waiting for transfers between devices, moved(): return lax.ppermute(value, axis, pairs)  9.16 us
    ppermute x8, waiting for transfers between devices, spread(): lax.ppermute(products[j], ('col', 'row'), [(col * row_count + row, (row *...  7.48 us
    pallas_call x1, Pallas kernels, paired_plan(): call(functools.partial(stage_in_kernel, col_count), [pltpu.VMEM((half, ha...  4.09 us
    pallas_call x1, Pallas kernels, paired_plan(): call(functools.partial(stage_rest_kernel, col_count), [pltpu.VMEM((half,...  3.71 us
    pallas_call x1, Pallas kernels, paired_plan(): call(stage_out_kernel, pltpu.VMEM((half, half_out), jnp.bfloat16), [HBM,...  2.24 us
    pallas_call x2, Pallas kernels, project(): call(functools.partial(kernel, parts), [struct((rows, half + more)), stru...  1.91 us
  transfers between devices with their start and end apart: 23, of which 12 were waited for; matrix products, arithmetic and copies ran while one was open for 0% of the time, Pallas kernels for 18%

profile of v12, /device:TPU:3, one launch (start us, length us, event | category | flops | bytes accessed | tf_op | source)
XLA Modules:
  0.0 65.7 jit_solution(4720578996177617781)
XLA Ops:
  0.0 0.9 %fusion = (bf16[16,2048]{1,0:T(8,128)(2,1)S(1)}, bf16[16,2048]{1,0:T(8,128)(2,1)S(1)}) fusion(bf16[32,4096]{1,0:T(8,128)(2,1)} %hidden.1, s32[]{:T(128)S(6)} %add.4, s32[]{:T(128)S(6)} %select_n.3), kind=kLoop, calls=%fused_computation.1 | loop fusion | bytes 262152 | tf_op jit(solution)/shard_map/slice | solution.py:617
  0.9 2.4 %collective-permute-start.2 = (bf16[16,2048]{1,0:T(8,128)(2,1)S(1)}, bf16[16,2048]{1,0:T(8,128)(2,1)S(1)}, u32[]{:S(2)}, u32[]{:S(2)}) collective-permute-start(bf16[16,2048]{1,0:T(8,128)(2,1)S(1)} %get-tuple-element.58.refs_0_), channel_id=1, source_target_pairs={{0,8},{4,12},{8,0},{12,4},{1,9},{5,13},{9,1},{13,5},{2,10},{6,14},... | collective-permute-start | bytes 196616 | tf_op jit(solution)/shard_map/ppermute | solution.py:206
  3.3 0.1 collective-permute-start.3
  3.3 1.3 %collective-permute-start = (bf16[16,2048]{1,0:T(8,128)(2,1)S(1)}, bf16[16,2048]{1,0:T(8,128)(2,1)S(1)}, u32[]{:S(2)}, u32[]{:S(2)}) collective-permute-start(bf16[16,2048]{1,0:T(8,128)(2,1)S(1)} %get-tuple-element.58.refs_0_), channel_id=1, source_target_pairs={{0,4},{4,0},{8,12},{12,8},{1,5},{5,1},{9,13},{13,9},{2,6},{6,2},{1... | collective-permute-start | bytes 196616 | tf_op jit(solution)/shard_map/ppermute | solution.py:206
  4.6 0.2 collective-permute-start.1
  4.8 0.1 collective-permute-done.2.refs_4_
  5.0 3.8 %collective-permute-start.4 = (bf16[16,2048]{1,0:T(8,128)(2,1)S(1)}, bf16[16,2048]{1,0:T(8,128)(2,1)S(1)}, u32[]{:S(2)}, u32[]{:S(2)}) collective-permute-start(bf16[16,2048]{1,0:T(8,128)(2,1)S(1)} %collective-permute-done.2.refs_4_), channel_id=1, source_target_pairs={{0,4},{4,0},{8,12},{12,8},{1,5},{5,1},{9,13},{13,9},{2,6},{6,2},{1... | collective-permute-start | bytes 196616 | tf_op jit(solution)/shard_map/ppermute | solution.py:206
  8.7 1.0 %collective-permute-done.3.refs_5_ = bf16[16,2048]{1,0:T(8,128)(2,1)S(1)} collective-permute-done((bf16[16,2048]{1,0:T(8,128)(2,1)S(1)}, bf16[16,2048]{1,0:T(8,128)(2,1)S(1)}, u32[]{:S(2)}, u32[]{:S(2)}) %collective-permute-start.3) | collective-permute-done | bytes 65568 | tf_op jit(solution)/shard_map/ppermute | solution.py:206
  9.7 0.8 %collective-permute-start.5 = (bf16[16,2048]{1,0:T(8,128)(2,1)S(1)}, bf16[16,2048]{1,0:T(8,128)(2,1)S(1)}, u32[]{:S(2)}, u32[]{:S(2)}) collective-permute-start(bf16[16,2048]{1,0:T(8,128)(2,1)S(1)} %collective-permute-done.3.refs_5_), channel_id=1, source_target_pairs={{0,4},{4,0},{8,12},{12,8},{1,5},{5,1},{9,13},{13,9},{2,6},{6,2},{1... | collective-permute-start | bytes 196616 | tf_op jit(solution)/shard_map/ppermute | solution.py:206
  10.5 4.1 %shard_map.83 = (bf16[2048,1280]{1,0:T(8,128)(2,1)S(1)}, bf16[2048,1280]{1,0:T(8,128)(2,1)S(1)}, bf16[128,128]{1,0:T(8,128)(2,1)S(1)}) custom-call(bf16[4096,2560]{1,0:T(8,128)(2,1)} %weight.4, s32[128]{0:T(128)} %slots.3), custom_call_target="tpu_custom_call" | custom-call | bytes 10485760 | tf_op jit(solution)/shard_map/pallas_call | solution.py:603
  14.6 0.0 collective-permute-done.refs_2_
  14.7 1.1 %shard_map.84 = (bf16[128,1408]{1,0:T(8,128)(2,1)S(1)}, bf16[128,2048]{1,0:T(8,128)(2,1)S(1)}) custom-call(bf16[128,128]{1,0:T(8,128)(2,1)S(1)} %get-tuple-element.34.chosen, bf16[16,2048]{1,0:T(8,128)(2,1)S(1)} %get-tuple-element.58.refs_0_, bf16[16,2048]{1,0:T(8,128)(2,1)S(1)} %get-tuple-element.57.refs_1_, ...), custom_call_target="tpu_custom_call" | custom-call | flops 671088640 | bytes 5242880 | tf_op jit(solution)/shard_map/pallas_call | solution.py:393
  15.8 0.0 copy-start.2
  15.8 0.0 copy-start.3
  15.8 1.2 %collective-permute-start.6 = (bf16[128,1408]{1,0:T(8,128)(2,1)S(1)}, bf16[128,1408]{1,0:T(8,128)(2,1)S(1)}, u32[]{:S(2)}, u32[]{:S(2)}) collective-permute-start(bf16[128,1408]{1,0:T(8,128)(2,1)S(1)} %get-tuple-element.38.given), channel_id=1, source_target_pairs={{0,1},{1,0},{2,3},{3,2},{4,5},{5,4},{6,7},{7,6},{8,9},{9,8},{10,11... | collective-permute-start | bytes 1081352 | tf_op jit(solution)/shard_map/ppermute | solution.py:206
  16.9 0.9 %shard_map.85.own = f32[128,1280]{1,0:T(8,128)S(1)} custom-call(bf16[128,2048]{1,0:T(8,128)(2,1)S(1)} %get-tuple-element.37.permuted, bf16[2048,1280]{1,0:T(8,128)(2,1)S(1)} %get-tuple-element.35.refs_8_.weight), custom_call_target="tpu_custom_call" | custom-call | flops 671088640 | bytes 5242880 | tf_op jit(solution)/shard_map/pallas_call | solution.py:402
  17.8 0.4 collective-permute-done.6.received
  18.2 0.1 shard_map.86
  18.3 0.3 collective-permute-start.7
  18.6 3.0 %collective-permute-start.8 = (bf16[32,1408]{1,0:T(8,128)(2,1)S(1)}, bf16[32,1408]{1,0:T(8,128)(2,1)S(1)}, u32[]{:S(2)}, u32[]{:S(2)}) collective-permute-start(bf16[32,1408]{1,0:T(8,128)(2,1)S(1)} %get-tuple-element.40), channel_id=1, source_target_pairs={{0,12},{2,4},{4,8},{6,0},{8,14},{10,6},{12,10},{14,2},{1,13},{3,5}... | collective-permute-start | bytes 270344 | tf_op jit(solution)/shard_map/ppermute | solution.py:442
  21.6 1.7 %collective-permute-start.9 = (bf16[32,1408]{1,0:T(8,128)(2,1)S(1)}, bf16[32,1408]{1,0:T(8,128)(2,1)S(1)}, u32[]{:S(2)}, u32[]{:S(2)}) collective-permute-start(bf16[32,1408]{1,0:T(8,128)(2,1)S(1)} %get-tuple-element.41), channel_id=1, source_target_pairs={{0,4},{2,12},{4,0},{6,8},{8,6},{10,14},{12,2},{14,10},{1,5},{3,13}... | collective-permute-start | bytes 270344 | tf_op jit(solution)/shard_map/ppermute | solution.py:442
  23.3 3.3 %collective-permute-start.10 = (bf16[32,1280]{1,0:T(8,128)(2,1)S(1)}, bf16[32,1280]{1,0:T(8,128)(2,1)S(1)}, u32[]{:S(2)}, u32[]{:S(2)}) collective-permute-start(bf16[32,1280]{1,0:T(8,128)(2,1)S(1)} %get-tuple-element.42), channel_id=1, source_target_pairs={{0,0},{2,8},{4,4},{6,12},{8,2},{10,10},{12,6},{14,14},{1,1},{3,9},... | collective-permute-start | bytes 245768 | tf_op jit(solution)/shard_map/ppermute | solution.py:442
  26.6 3.7 %shard_map.82 = (bf16[2048,1024]{1,0:T(8,128)(2,1)S(1)}, bf16[32,64,256]{2,1,0:T(8,128)(2,1)S(1)}, bf16[32,64,256]{2,1,0:T(8,128)(2,1)S(1)}, f32[32,128]{1,0:T(8...) custom-call(s32[32]{0:T(128)S(1)} %copy-done.3, bf16[4096,2048]{1,0:T(8,128)(2,1)} %weight.5, ...), custom_call_target="tpu_custom_call" | custom-call | bytes 6291456 | tf_op jit(solution)/shard_map/pallas_call | solution.py:624
  30.4 2.6 %collective-permute-done.10.refs_3_ = bf16[32,1280]{1,0:T(8,128)(2,1)S(1)} collective-permute-done((bf16[32,1280]{1,0:T(8,128)(2,1)S(1)}, bf16[32,1280]{1,0:T(8,128)(2,1)S(1)}, u32[]{:S(2)}, u32[]{:S(2)}) %collective-permute-start.10) | collective-permute-done | bytes 81952 | tf_op jit(solution)/shard_map/ppermute | solution.py:442
  33.0 1.7 %shard_map.87 = (bf16[16,2048]{1,0:T(8,128)(2,1)S(1)}, bf16[16,2048]{1,0:T(8,128)(2,1)S(1)}) custom-call(f32[32,128]{1,0:T(8,128)S(1)} %get-tuple-element.31.cosine, f32[32,128]{1,0:T(8,128)S(1)} %get-tuple-element.32.sine, s32[32,128]{1,0:T(8,128)S(1)} %get-tuple-element.33.lengths, bf16[32,1408]{1,0:T(8,128)(2,1)S(1)} %collective-permute-done.7.refs_0_, ...), custom_call_target="tpu_custom_call" | custom-call | flops 16777216 | tf_op jit(solution)/shard_map/pallas_call | solution.py:636
  34.7 0.1 collective-permute-start.13
  34.8 2.4 %collective-permute-start.14 = (bf16[16,2048]{1,0:T(8,128)(2,1)S(1)}, bf16[16,2048]{1,0:T(8,128)(2,1)S(1)}, u32[]{:S(2)}, u32[]{:S(2)}) collective-permute-start(bf16[16,2048]{1,0:T(8,128)(2,1)S(1)} %get-tuple-element.46.attended.refs_1_), channel_id=1, source_target_pairs={{0,8},{4,12},{8,0},{12,4},{1,9},{5,13},{9,1},{13,5},{2,10},{6,14},... | collective-permute-start | bytes 196616 | tf_op jit(solution)/shard_map/ppermute | solution.py:206
  37.1 1.5 %collective-permute-start.12 = (bf16[16,2048]{1,0:T(8,128)(2,1)S(1)}, bf16[16,2048]{1,0:T(8,128)(2,1)S(1)}, u32[]{:S(2)}, u32[]{:S(2)}) collective-permute-start(bf16[16,2048]{1,0:T(8,128)(2,1)S(1)} %get-tuple-element.46.attended.refs_1_), channel_id=1, source_target_pairs={{0,4},{4,0},{8,12},{12,8},{1,5},{5,1},{9,13},{13,9},{2,6},{6,2},{1... | collective-permute-start | bytes 196616 | tf_op jit(solution)/shard_map/ppermute | solution.py:206
  38.6 1.7 %collective-permute-done.13.refs_4_ = bf16[16,2048]{1,0:T(8,128)(2,1)S(1)} collective-permute-done((bf16[16,2048]{1,0:T(8,128)(2,1)S(1)}, bf16[16,2048]{1,0:T(8,128)(2,1)S(1)}, u32[]{:S(2)}, u32[]{:S(2)}) %collective-permute-start.13) | collective-permute-done | bytes 65568 | tf_op jit(solution)/shard_map/ppermute | solution.py:206
  40.3 1.7 %collective-permute-done.14.refs_5_ = bf16[16,2048]{1,0:T(8,128)(2,1)S(1)} collective-permute-done((bf16[16,2048]{1,0:T(8,128)(2,1)S(1)}, bf16[16,2048]{1,0:T(8,128)(2,1)S(1)}, u32[]{:S(2)}, u32[]{:S(2)}) %collective-permute-start.14) | collective-permute-done | bytes 65568 | tf_op jit(solution)/shard_map/ppermute | solution.py:206
  42.0 2.2 %shard_map.88.refs_8_.weight = bf16[2048,1024]{1,0:T(8,128)(2,1)S(1)} custom-call(bf16[4096,2048]{1,0:T(8,128)(2,1)} %weight.5, bf16[16,2048]{1,0:T(8,128)(2,1)S(1)} %get-tuple-element.46.attended.refs_1_), custom_call_target="tpu_custom_call" | custom-call | bytes 4194304 | tf_op jit(solution)/shard_map/pallas_call | solution.py:646
  44.3 1.3 %collective-permute-done.15.refs_6_ = bf16[16,2048]{1,0:T(8,128)(2,1)S(1)} collective-permute-done((bf16[16,2048]{1,0:T(8,128)(2,1)S(1)}, bf16[16,2048]{1,0:T(8,128)(2,1)S(1)}, u32[]{:S(2)}, u32[]{:S(2)}) %collective-permute-start.15) | collective-permute-done | bytes 65568 | tf_op jit(solution)/shard_map/ppermute | solution.py:206
  45.6 1.4 %collective-permute-done.16.refs_7_ = bf16[16,2048]{1,0:T(8,128)(2,1)S(1)} collective-permute-done((bf16[16,2048]{1,0:T(8,128)(2,1)S(1)}, bf16[16,2048]{1,0:T(8,128)(2,1)S(1)}, u32[]{:S(2)}, u32[]{:S(2)}) %collective-permute-start.16) | collective-permute-done | bytes 65568 | tf_op jit(solution)/shard_map/ppermute | solution.py:206
  47.0 0.8 %shard_map.89 = (bf16[128,1024]{1,0:T(8,128)(2,1)S(1)}, bf16[128,2048]{1,0:T(8,128)(2,1)S(1)}) custom-call(bf16[128,128]{1,0:T(8,128)(2,1)S(1)} %get-tuple-element.47.chosen, bf16[16,2048]{1,0:T(8,128)(2,1)S(1)} %get-tuple-element.45.refs_0_, bf16[16,2048]{1,0:T(8,128)(2,1)S(1)} %get-tuple-element.46.attended.refs_1_, ...), custom_call_target="tpu_custom_call" | custom-call | flops 536870912 | bytes 4194304 | tf_op jit(solution)/shard_map/pallas_call | solution.py:393
  47.9 0.0 copy-start
  47.9 1.1 %collective-permute-start.17 = (bf16[128,1024]{1,0:T(8,128)(2,1)S(1)}, bf16[128,1024]{1,0:T(8,128)(2,1)S(1)}, u32[]{:S(2)}, u32[]{:S(2)}) collective-permute-start(bf16[128,1024]{1,0:T(8,128)(2,1)S(1)} %get-tuple-element.50.given), channel_id=1, source_target_pairs={{0,1},{1,0},{2,3},{3,2},{4,5},{5,4},{6,7},{7,6},{8,9},{9,8},{10,11... | collective-permute-start | bytes 786440 | tf_op jit(solution)/shard_map/ppermute | solution.py:206
  49.0 0.7 %shard_map.90.own = f32[128,1024]{1,0:T(8,128)S(1)} custom-call(bf16[128,2048]{1,0:T(8,128)(2,1)S(1)} %get-tuple-element.49.permuted, bf16[2048,1024]{1,0:T(8,128)(2,1)S(1)} %shard_map.88.refs_8_.weight), custom_call_target="tpu_custom_call" | custom-call | flops 536870912 | bytes 4194304 | tf_op jit(solution)/shard_map/pallas_call | solution.py:402
  49.7 0.4 collective-permute-done.17.received
  50.2 0.1 collective-permute-start.18
  50.3 1.1 %collective-permute-start.19 = (bf16[32,1024]{1,0:T(8,128)(2,1)S(1)}, bf16[32,1024]{1,0:T(8,128)(2,1)S(1)}, u32[]{:S(2)}, u32[]{:S(2)}) collective-permute-start(bf16[32,1024]{1,0:T(8,128)(2,1)S(1)} %get-tuple-element.52), channel_id=1, source_target_pairs={{0,12},{2,4},{4,8},{6,0},{8,14},{10,6},{12,10},{14,2},{1,13},{3,5}... | collective-permute-start | bytes 196616 | tf_op jit(solution)/shard_map/ppermute | solution.py:442
  51.4 3.3 %collective-permute-start.20 = (bf16[32,1024]{1,0:T(8,128)(2,1)S(1)}, bf16[32,1024]{1,0:T(8,128)(2,1)S(1)}, u32[]{:S(2)}, u32[]{:S(2)}) collective-permute-start(bf16[32,1024]{1,0:T(8,128)(2,1)S(1)} %get-tuple-element.53), channel_id=1, source_target_pairs={{0,4},{2,12},{4,0},{6,8},{8,6},{10,14},{12,2},{14,10},{1,5},{3,13}... | collective-permute-start | bytes 196616 | tf_op jit(solution)/shard_map/ppermute | solution.py:442
  54.7 1.9 %collective-permute-start.21 = (bf16[32,1024]{1,0:T(8,128)(2,1)S(1)}, bf16[32,1024]{1,0:T(8,128)(2,1)S(1)}, u32[]{:S(2)}, u32[]{:S(2)}) collective-permute-start(bf16[32,1024]{1,0:T(8,128)(2,1)S(1)} %get-tuple-element.54), channel_id=1, source_target_pairs={{0,0},{2,8},{4,4},{6,12},{8,2},{10,10},{12,6},{14,14},{1,1},{3,9},... | collective-permute-start | bytes 196616 | tf_op jit(solution)/shard_map/ppermute | solution.py:442
  56.6 1.3 %collective-permute-done.18.refs_2_ = bf16[32,1024]{1,0:T(8,128)(2,1)S(1)} collective-permute-done((bf16[32,1024]{1,0:T(8,128)(2,1)S(1)}, bf16[32,1024]{1,0:T(8,128)(2,1)S(1)}, u32[]{:S(2)}, u32[]{:S(2)}) %collective-permute-start.18) | collective-permute-done | bytes 65568 | tf_op jit(solution)/shard_map/ppermute | solution.py:442
  57.9 3.6 %collective-permute-done.21.refs_5_ = bf16[32,1024]{1,0:T(8,128)(2,1)S(1)} collective-permute-done((bf16[32,1024]{1,0:T(8,128)(2,1)S(1)}, bf16[32,1024]{1,0:T(8,128)(2,1)S(1)}, u32[]{:S(2)}, u32[]{:S(2)}) %collective-permute-start.21) | collective-permute-done | bytes 65568 | tf_op jit(solution)/shard_map/ppermute | solution.py:442
  61.5 0.1 shard_map.92
  61.6 2.4 %collective-permute-start.22 = (bf16[32,2048]{1,0:T(8,128)(2,1)S(1)}, bf16[32,2048]{1,0:T(8,128)(2,1)S(1)}, u32[]{:S(2)}, u32[]{:S(2)}) collective-permute-start(bf16[32,2048]{1,0:T(8,128)(2,1)S(1)} %get-tuple-element.56), channel_id=1, source_target_pairs={{0,1},{1,0},{2,3},{3,2},{4,5},{5,4},{6,7},{7,6},{8,9},{9,8},{10,11... | collective-permute-start | bytes 393224 | tf_op jit(solution)/shard_map/ppermute | solution.py:206
  64.0 1.0 %collective-permute-done.22.received = bf16[32,2048]{1,0:T(8,128)(2,1)S(1)} collective-permute-done((bf16[32,2048]{1,0:T(8,128)(2,1)S(1)}, bf16[32,2048]{1,0:T(8,128)(2,1)S(1)}, u32[]{:S(2)}, u32[]{:S(2)}) %collective-permute-start.22) | collective-permute-done | bytes 131104 | tf_op jit(solution)/shard_map/ppermute | solution.py:206
  65.0 0.7 %shard_map.93 = bf16[1,32,4096]{2,1,0:T(8,128)(2,1)} custom-call(bf16[32,2048]{1,0:T(8,128)(2,1)S(1)} %get-tuple-element.55.keep, bf16[32,2048]{1,0:T(8,128)(2,1)S(1)} %collective-permute-done.22.received), custom_call_target="tpu_custom_call" | custom-call | bytes 524288 | tf_op jit(solution)/shard_map/pallas_call | solution.py:668
  (19 shorter events, 0.1 us)
Async XLA Ops:
  0.9 4.1 %collective-permute-start.2 = (bf16[16,2048]{1,0:T(8,128)(2,1)S(1)}, bf16[16,2048]{1,0:T(8,128)(2,1)S(1)}, u32[]{:S(2)}, u32[]{:S(2)}) collective-permute-start(bf16[16,2048]{1,0:T(8,128)(2,1)S(1)} %get-tuple-element.58.refs_0_), channel_id=1, source_target_pairs={{0,8},{4,12},{8,0},{12,4},{1,9},{5,13},{9,1},{13,5},{2,10},{6,14},... | collective-permute-start | bytes 196616 | tf_op jit(solution)/shard_map/ppermute | solution.py:206
  3.3 11.4 %copy-start.1 = (bf16[4096]{0:T(1024)(128)(2,1)S(1)}, bf16[4096]{0:T(1024)(128)(2,1)}, u32[]{:S(2)}) copy-start(bf16[4096]{0:T(1024)(128)(2,1)} %param.9) | copy-start | bytes 24580
  3.3 6.4 %collective-permute-start.3 = (bf16[16,2048]{1,0:T(8,128)(2,1)S(1)}, bf16[16,2048]{1,0:T(8,128)(2,1)S(1)}, u32[]{:S(2)}, u32[]{:S(2)}) collective-permute-start(bf16[16,2048]{1,0:T(8,128)(2,1)S(1)} %get-tuple-element.57.refs_1_), channel_id=1, source_target_pairs={{0,8},{4,12},{8,0},{12,4},{1,9},{5,13},{9,1},{13,5},{2,10},{6,14},... | collective-permute-start | bytes 196616 | tf_op jit(solution)/shard_map/ppermute | solution.py:206
  3.3 11.3 %collective-permute-start = (bf16[16,2048]{1,0:T(8,128)(2,1)S(1)}, bf16[16,2048]{1,0:T(8,128)(2,1)S(1)}, u32[]{:S(2)}, u32[]{:S(2)}) collective-permute-start(bf16[16,2048]{1,0:T(8,128)(2,1)S(1)} %get-tuple-element.58.refs_0_), channel_id=1, source_target_pairs={{0,4},{4,0},{8,12},{12,8},{1,5},{5,1},{9,13},{13,9},{2,6},{6,2},{1... | collective-permute-start | bytes 196616 | tf_op jit(solution)/shard_map/ppermute | solution.py:206
  4.6 10.0 %collective-permute-start.1 = (bf16[16,2048]{1,0:T(8,128)(2,1)S(1)}, bf16[16,2048]{1,0:T(8,128)(2,1)S(1)}, u32[]{:S(2)}, u32[]{:S(2)}) collective-permute-start(bf16[16,2048]{1,0:T(8,128)(2,1)S(1)} %get-tuple-element.57.refs_1_), channel_id=1, source_target_pairs={{0,4},{4,0},{8,12},{12,8},{1,5},{5,1},{9,13},{13,9},{2,6},{6,2},{1... | collective-permute-start | bytes 196616 | tf_op jit(solution)/shard_map/ppermute | solution.py:206
  5.0 9.7 %collective-permute-start.4 = (bf16[16,2048]{1,0:T(8,128)(2,1)S(1)}, bf16[16,2048]{1,0:T(8,128)(2,1)S(1)}, u32[]{:S(2)}, u32[]{:S(2)}) collective-permute-start(bf16[16,2048]{1,0:T(8,128)(2,1)S(1)} %collective-permute-done.2.refs_4_), channel_id=1, source_target_pairs={{0,4},{4,0},{8,12},{12,8},{1,5},{5,1},{9,13},{13,9},{2,6},{6,2},{1... | collective-permute-start | bytes 196616 | tf_op jit(solution)/shard_map/ppermute | solution.py:206
  9.7 5.0 %collective-permute-start.5 = (bf16[16,2048]{1,0:T(8,128)(2,1)S(1)}, bf16[16,2048]{1,0:T(8,128)(2,1)S(1)}, u32[]{:S(2)}, u32[]{:S(2)}) collective-permute-start(bf16[16,2048]{1,0:T(8,128)(2,1)S(1)} %collective-permute-done.3.refs_5_), channel_id=1, source_target_pairs={{0,4},{4,0},{8,12},{12,8},{1,5},{5,1},{9,13},{13,9},{2,6},{6,2},{1... | collective-permute-start | bytes 196616 | tf_op jit(solution)/shard_map/ppermute | solution.py:206
  15.8 10.9 %copy-start.2 = (s32[128]{0:T(128)S(1)}, s32[128]{0:T(128)}, u32[]{:S(2)}) copy-start(s32[128]{0:T(128)} %slots.3) | copy-start | bytes 1540
  15.8 10.9 %copy-start.3 = (s32[32]{0:T(128)S(1)}, s32[32]{0:T(128)}, u32[]{:S(2)}) copy-start(s32[32]{0:T(128)} %lengths.1) | copy-start | bytes 388
  15.8 2.5 %collective-permute-start.6 = (bf16[128,1408]{1,0:T(8,128)(2,1)S(1)}, bf16[128,1408]{1,0:T(8,128)(2,1)S(1)}, u32[]{:S(2)}, u32[]{:S(2)}) collective-permute-start(bf16[128,1408]{1,0:T(8,128)(2,1)S(1)} %get-tuple-element.38.given), channel_id=1, source_target_pairs={{0,1},{1,0},{2,3},{3,2},{4,5},{5,4},{6,7},{7,6},{8,9},{9,8},{10,11... | collective-permute-start | bytes 1081352 | tf_op jit(solution)/shard_map/ppermute | solution.py:206
  18.3 14.6 %collective-permute-start.7 = (bf16[32,1408]{1,0:T(8,128)(2,1)S(1)}, bf16[32,1408]{1,0:T(8,128)(2,1)S(1)}, u32[]{:S(2)}, u32[]{:S(2)}) collective-permute-start(bf16[32,1408]{1,0:T(8,128)(2,1)S(1)} %get-tuple-element.39), channel_id=1, source_target_pairs={{0,8},{2,0},{4,12},{6,4},{8,10},{10,2},{12,14},{14,6},{1,9},{3,1},... | collective-permute-start | bytes 270344 | tf_op jit(solution)/shard_map/ppermute | solution.py:442
  18.6 14.3 %collective-permute-start.8 = (bf16[32,1408]{1,0:T(8,128)(2,1)S(1)}, bf16[32,1408]{1,0:T(8,128)(2,1)S(1)}, u32[]{:S(2)}, u32[]{:S(2)}) collective-permute-start(bf16[32,1408]{1,0:T(8,128)(2,1)S(1)} %get-tuple-element.40), channel_id=1, source_target_pairs={{0,12},{2,4},{4,8},{6,0},{8,14},{10,6},{12,10},{14,2},{1,13},{3,5}... | collective-permute-start | bytes 270344 | tf_op jit(solution)/shard_map/ppermute | solution.py:442
  21.6 11.4 %collective-permute-start.9 = (bf16[32,1408]{1,0:T(8,128)(2,1)S(1)}, bf16[32,1408]{1,0:T(8,128)(2,1)S(1)}, u32[]{:S(2)}, u32[]{:S(2)}) collective-permute-start(bf16[32,1408]{1,0:T(8,128)(2,1)S(1)} %get-tuple-element.41), channel_id=1, source_target_pairs={{0,4},{2,12},{4,0},{6,8},{8,6},{10,14},{12,2},{14,10},{1,5},{3,13}... | collective-permute-start | bytes 270344 | tf_op jit(solution)/shard_map/ppermute | solution.py:442
  23.3 9.6 %collective-permute-start.10 = (bf16[32,1280]{1,0:T(8,128)(2,1)S(1)}, bf16[32,1280]{1,0:T(8,128)(2,1)S(1)}, u32[]{:S(2)}, u32[]{:S(2)}) collective-permute-start(bf16[32,1280]{1,0:T(8,128)(2,1)S(1)} %get-tuple-element.42), channel_id=1, source_target_pairs={{0,0},{2,8},{4,4},{6,12},{8,2},{10,10},{12,6},{14,14},{1,1},{3,9},... | collective-permute-start | bytes 245768 | tf_op jit(solution)/shard_map/ppermute | solution.py:442
  34.7 5.6 %collective-permute-start.13 = (bf16[16,2048]{1,0:T(8,128)(2,1)S(1)}, bf16[16,2048]{1,0:T(8,128)(2,1)S(1)}, u32[]{:S(2)}, u32[]{:S(2)}) collective-permute-start(bf16[16,2048]{1,0:T(8,128)(2,1)S(1)} %get-tuple-element.45.refs_0_), channel_id=1, source_target_pairs={{0,8},{4,12},{8,0},{12,4},{1,9},{5,13},{9,1},{13,5},{2,10},{6,14},... | collective-permute-start | bytes 196616 | tf_op jit(solution)/shard_map/ppermute | solution.py:206
  34.8 7.3 %collective-permute-start.14 = (bf16[16,2048]{1,0:T(8,128)(2,1)S(1)}, bf16[16,2048]{1,0:T(8,128)(2,1)S(1)}, u32[]{:S(2)}, u32[]{:S(2)}) collective-permute-start(bf16[16,2048]{1,0:T(8,128)(2,1)S(1)} %get-tuple-element.46.attended.refs_1_), channel_id=1, source_target_pairs={{0,8},{4,12},{8,0},{12,4},{1,9},{5,13},{9,1},{13,5},{2,10},{6,14},... | collective-permute-start | bytes 196616 | tf_op jit(solution)/shard_map/ppermute | solution.py:206
  37.1 7.2 %collective-permute-start.11 = (bf16[16,2048]{1,0:T(8,128)(2,1)S(1)}, bf16[16,2048]{1,0:T(8,128)(2,1)S(1)}, u32[]{:S(2)}, u32[]{:S(2)}) collective-permute-start(bf16[16,2048]{1,0:T(8,128)(2,1)S(1)} %get-tuple-element.45.refs_0_), channel_id=1, source_target_pairs={{0,4},{4,0},{8,12},{12,8},{1,5},{5,1},{9,13},{13,9},{2,6},{6,2},{1... | collective-permute-start | bytes 196616 | tf_op jit(solution)/shard_map/ppermute | solution.py:206
  37.1 7.2 %collective-permute-start.12 = (bf16[16,2048]{1,0:T(8,128)(2,1)S(1)}, bf16[16,2048]{1,0:T(8,128)(2,1)S(1)}, u32[]{:S(2)}, u32[]{:S(2)}) collective-permute-start(bf16[16,2048]{1,0:T(8,128)(2,1)S(1)} %get-tuple-element.46.attended.refs_1_), channel_id=1, source_target_pairs={{0,4},{4,0},{8,12},{12,8},{1,5},{5,1},{9,13},{13,9},{2,6},{6,2},{1... | collective-permute-start | bytes 196616 | tf_op jit(solution)/shard_map/ppermute | solution.py:206
  40.3 5.3 %collective-permute-start.15 = (bf16[16,2048]{1,0:T(8,128)(2,1)S(1)}, bf16[16,2048]{1,0:T(8,128)(2,1)S(1)}, u32[]{:S(2)}, u32[]{:S(2)}) collective-permute-start(bf16[16,2048]{1,0:T(8,128)(2,1)S(1)} %collective-permute-done.13.refs_4_), channel_id=1, source_target_pairs={{0,4},{4,0},{8,12},{12,8},{1,5},{5,1},{9,13},{13,9},{2,6},{6,2},{1... | collective-permute-start | bytes 196616 | tf_op jit(solution)/shard_map/ppermute | solution.py:206
  42.0 5.0 %collective-permute-start.16 = (bf16[16,2048]{1,0:T(8,128)(2,1)S(1)}, bf16[16,2048]{1,0:T(8,128)(2,1)S(1)}, u32[]{:S(2)}, u32[]{:S(2)}) collective-permute-start(bf16[16,2048]{1,0:T(8,128)(2,1)S(1)} %collective-permute-done.14.refs_5_), channel_id=1, source_target_pairs={{0,4},{4,0},{8,12},{12,8},{1,5},{5,1},{9,13},{13,9},{2,6},{6,2},{1... | collective-permute-start | bytes 196616 | tf_op jit(solution)/shard_map/ppermute | solution.py:206
  47.9 13.7 %copy-start = (bf16[32,4096]{1,0:T(8,128)(2,1)S(1)}, bf16[32,4096]{1,0:T(8,128)(2,1)}, u32[]{:S(2)}) copy-start(bf16[32,4096]{1,0:T(8,128)(2,1)} %hidden.1) | copy-start | bytes 786436
  47.9 2.3 %collective-permute-start.17 = (bf16[128,1024]{1,0:T(8,128)(2,1)S(1)}, bf16[128,1024]{1,0:T(8,128)(2,1)S(1)}, u32[]{:S(2)}, u32[]{:S(2)}) collective-permute-start(bf16[128,1024]{1,0:T(8,128)(2,1)S(1)} %get-tuple-element.50.given), channel_id=1, source_target_pairs={{0,1},{1,0},{2,3},{3,2},{4,5},{5,4},{6,7},{7,6},{8,9},{9,8},{10,11... | collective-permute-start | bytes 786440 | tf_op jit(solution)/shard_map/ppermute | solution.py:206
  50.2 7.7 %collective-permute-start.18 = (bf16[32,1024]{1,0:T(8,128)(2,1)S(1)}, bf16[32,1024]{1,0:T(8,128)(2,1)S(1)}, u32[]{:S(2)}, u32[]{:S(2)}) collective-permute-start(bf16[32,1024]{1,0:T(8,128)(2,1)S(1)} %get-tuple-element.51), channel_id=1, source_target_pairs={{0,8},{2,0},{4,12},{6,4},{8,10},{10,2},{12,14},{14,6},{1,9},{3,1},... | collective-permute-start | bytes 196616 | tf_op jit(solution)/shard_map/ppermute | solution.py:442
  50.3 7.6 %collective-permute-start.19 = (bf16[32,1024]{1,0:T(8,128)(2,1)S(1)}, bf16[32,1024]{1,0:T(8,128)(2,1)S(1)}, u32[]{:S(2)}, u32[]{:S(2)}) collective-permute-start(bf16[32,1024]{1,0:T(8,128)(2,1)S(1)} %get-tuple-element.52), channel_id=1, source_target_pairs={{0,12},{2,4},{4,8},{6,0},{8,14},{10,6},{12,10},{14,2},{1,13},{3,5}... | collective-permute-start | bytes 196616 | tf_op jit(solution)/shard_map/ppermute | solution.py:442
  51.4 6.5 %collective-permute-start.20 = (bf16[32,1024]{1,0:T(8,128)(2,1)S(1)}, bf16[32,1024]{1,0:T(8,128)(2,1)S(1)}, u32[]{:S(2)}, u32[]{:S(2)}) collective-permute-start(bf16[32,1024]{1,0:T(8,128)(2,1)S(1)} %get-tuple-element.53), channel_id=1, source_target_pairs={{0,4},{2,12},{4,0},{6,8},{8,6},{10,14},{12,2},{14,10},{1,5},{3,13}... | collective-permute-start | bytes 196616 | tf_op jit(solution)/shard_map/ppermute | solution.py:442
  54.7 6.8 %collective-permute-start.21 = (bf16[32,1024]{1,0:T(8,128)(2,1)S(1)}, bf16[32,1024]{1,0:T(8,128)(2,1)S(1)}, u32[]{:S(2)}, u32[]{:S(2)}) collective-permute-start(bf16[32,1024]{1,0:T(8,128)(2,1)S(1)} %get-tuple-element.54), channel_id=1, source_target_pairs={{0,0},{2,8},{4,4},{6,12},{8,2},{10,10},{12,6},{14,14},{1,1},{3,9},... | collective-permute-start | bytes 196616 | tf_op jit(solution)/shard_map/ppermute | solution.py:442
  61.6 3.4 %collective-permute-start.22 = (bf16[32,2048]{1,0:T(8,128)(2,1)S(1)}, bf16[32,2048]{1,0:T(8,128)(2,1)S(1)}, u32[]{:S(2)}, u32[]{:S(2)}) collective-permute-start(bf16[32,2048]{1,0:T(8,128)(2,1)S(1)} %get-tuple-element.56), channel_id=1, source_target_pairs={{0,1},{1,0},{2,3},{3,2},{4,5},{5,4},{6,7},{7,6},{8,9},{9,8},{10,11... | collective-permute-start | bytes 393224 | tf_op jit(solution)/shard_map/ppermute | solution.py:206

commit v13 on v12

--- a/solution.py
+++ b/solution.py
@@ -438,22 +438,35 @@
 def spread(products):
     col_count, row_count = lax.axis_size("col"), lax.axis_size("row")
     pairs = col_count // row_count
+    def target(col, row, j):
+        if j == 0 and row_count == 2:
+            return (col ^ pairs) * row_count + (row ^ 1)
+        return ((row * pairs + col % pairs) ^ j) * row_count + col // pairs
+
     sent = {
         j: lax.ppermute(
             products[j],
             ("col", "row"),
             [
-                (
-                    col * row_count + row,
-                    ((row * pairs + col % pairs) ^ j) * row_count + col // pairs,
-                )
+                (col * row_count + row, target(col, row, j))
                 for col in range(col_count)
                 for row in range(row_count)
             ],
         )
         for j in range(col_count)
     }
-    return [sent[j] for j in arrival_order(col_count, pairs)]
+    return [sent[j] for j in arrival_order(col_count, pairs)] + [products[0]]
+
+
+def total_of(blocks, own, pairs, entry, width):
+    first = blocks[entry][:, :width]
+    if entry == 0:
+        keeps = lax.axis_index("row") == lax.div(lax.axis_index("col"), pairs)
+        first = jnp.where(keeps, own[...], first)
+    total = first.astype(jnp.float32)
+    for i in range(entry + pairs, len(blocks), pairs):
+        total = total + blocks[i][:, :width].astype(jnp.float32)
+    return total
 
 
 def rotated(vector, cosine, sine):
@@ -474,7 +487,7 @@
 
 
 def attend_all(count, parts, cosine, sine, lengths, *refs):
-    blocks, (keys, values), refs = refs[:count], refs[count : count + 2], refs[count + 2 :]
+    blocks, (own_block, keys, values), refs = refs[:count], refs[count : count + 3], refs[count + 3 :]
     blocks = in_place(blocks, keys.shape[2] // HEAD_DIM)
     outs, (scores_of, probs_of) = refs[:parts], refs[parts:]
     pairs = keys.shape[2] // HEAD_DIM
@@ -495,9 +508,7 @@
     filled = [(position >= 0) & (position < length_of[part]) for part in runs]
     own, new_values, own_probs = [], [], []
     for pair in range(pairs):
-        total = blocks[pair][:, :width].astype(jnp.float32)
-        for i in range(pair + pairs, count, pairs):
-            total = total + blocks[i][:, :width].astype(jnp.float32)
+        total = total_of(blocks, own_block, pairs, pair, width)
         total = (total * scale).astype(jnp.bfloat16).astype(jnp.float32)
         heads = [total[:, h * HEAD_DIM : (h + 1) * HEAD_DIM] for h in range(GROUP + 2)]
         queries = [
@@ -552,7 +563,7 @@
 
 
 def sum_kernel(count, parts, hidden, *refs):
-    attended, blocks, (keep, send) = refs[:parts], refs[parts : parts + count], refs[parts + count :]
+    attended, blocks, (own_block, keep, send) = refs[:parts], refs[parts:-3], refs[-3:]
     rows, width = blocks[0].shape
     pairs = keep.shape[1] // width
     blocks = in_place(blocks, pairs)
@@ -560,9 +571,7 @@
     low = lax.rem(lax.axis_index("col"), pairs)
     for pair in range(pairs):
         column = low ^ pair
-        total = blocks[pair][...].astype(jnp.float32)
-        for i in range(pair + pairs, count, pairs):
-            total = total + blocks[i][...].astype(jnp.float32)
+        total = total_of(blocks, own_block, pairs, pair, width)
         at = pl.ds(pl.multiple_of((2 * column + side) * width, width), width)
         hidden_out = (hidden[:, at].astype(jnp.float32) + total).astype(jnp.bfloat16)
         at = pl.ds(pl.multiple_of(column * width, width), width)
@@ -636,7 +645,7 @@
     attended = call(
         functools.partial(attend_all, col_count, parts),
         [struct((piece, half))] * parts,
-        [VMEM] * (col_count + 5),
+        [VMEM] * (col_count + 6),
         [VMEM] * parts,
         4 * rows * half * cache,
         0,
@@ -660,7 +669,7 @@
     keep, send = call(
         functools.partial(sum_kernel, col_count, parts),
         [struct((rows, half)), struct((rows, half))],
-        [VMEM] * (1 + parts + col_count),
+        [VMEM] * (2 + parts + col_count),
         [VMEM, VMEM],
         rows * depth * 4,
         rows * depth * 8,

time: 65.9 us -> 66.2 us (level)
  the two profiles are of different devices: /device:TPU:3 before, /device:TPU:0 now
where the time goes in v13:
time: 66.2 us; the launch traced here: 66 us
  starting transfers between devices  27.2 us (41%)
  waiting for transfers between devices  21.5 us (32%)
  Pallas kernels  16.2 us (24%)
  local copies, waits for them, and re-layouts  0.9 us (1%)
    ppermute x15, starting transfers between devices, moved(): return lax.ppermute(value, axis, pairs)  15.4 us
    ppermute x8, starting transfers between devices, spread(): lax.ppermute(products[j], ('col', 'row'), [(col * row_count + row, target...  11.8 us
    ppermute x8, waiting for transfers between devices, spread(): lax.ppermute(products[j], ('col', 'row'), [(col * row_count + row, target...  11.8 us
    ppermute x15, waiting for transfers between devices, moved(): return lax.ppermute(value, axis, pairs)  9.75 us
    pallas_call x1, Pallas kernels, paired_plan(): call(functools.partial(stage_in_kernel, col_count), [pltpu.VMEM((half, ha...  4.09 us
    pallas_call x1, Pallas kernels, paired_plan(): call(functools.partial(stage_rest_kernel, col_count), [pltpu.VMEM((half,...  3.71 us
    pallas_call x1, Pallas kernels, paired_plan(): call(stage_out_kernel, pltpu.VMEM((half, half_out), jnp.bfloat16), [HBM,...  2.24 us
    pallas_call x2, Pallas kernels, project(): call(functools.partial(kernel, parts), [struct((rows, half + more)), stru...  1.91 us
  transfers between devices with their start and end apart: 23, of which 12 were waited for; matrix products, arithmetic and copies ran while one was open for 0% of the time, Pallas kernels for 18%

profile of v13, /device:TPU:0, one launch (start us, length us, event | category | flops | bytes accessed | tf_op | source)
XLA Modules:
  0.0 66.0 jit_solution(9793768662320633036)
XLA Ops:
  0.0 0.9 %fusion = (bf16[16,2048]{1,0:T(8,128)(2,1)S(1)}, bf16[16,2048]{1,0:T(8,128)(2,1)S(1)}) fusion(bf16[32,4096]{1,0:T(8,128)(2,1)} %hidden.1, s32[]{:T(128)S(6)} %add.4, s32[]{:T(128)S(6)} %select_n.3), kind=kLoop, calls=%fused_computation.1 | loop fusion | bytes 262152 | tf_op jit(solution)/shard_map/slice | solution.py:626
  0.9 4.1 %collective-permute-start.2 = (bf16[16,2048]{1,0:T(8,128)(2,1)S(1)}, bf16[16,2048]{1,0:T(8,128)(2,1)S(1)}, u32[]{:S(2)}, u32[]{:S(2)}) collective-permute-start(bf16[16,2048]{1,0:T(8,128)(2,1)S(1)} %get-tuple-element.58.refs_0_), channel_id=1, source_target_pairs={{0,8},{4,12},{8,0},{12,4},{1,9},{5,13},{9,1},{13,5},{2,10},{6,14},... | collective-permute-start | bytes 196616 | tf_op jit(solution)/shard_map/ppermute | solution.py:206
  5.0 0.1 collective-permute-start.3
  5.1 1.8 %collective-permute-start = (bf16[16,2048]{1,0:T(8,128)(2,1)S(1)}, bf16[16,2048]{1,0:T(8,128)(2,1)S(1)}, u32[]{:S(2)}, u32[]{:S(2)}) collective-permute-start(bf16[16,2048]{1,0:T(8,128)(2,1)S(1)} %get-tuple-element.58.refs_0_), channel_id=1, source_target_pairs={{0,4},{4,0},{8,12},{12,8},{1,5},{5,1},{9,13},{13,9},{2,6},{6,2},{1... | collective-permute-start | bytes 196616 | tf_op jit(solution)/shard_map/ppermute | solution.py:206
  6.9 0.2 collective-permute-start.1
  7.1 1.6 %collective-permute-done.2.refs_4_ = bf16[16,2048]{1,0:T(8,128)(2,1)S(1)} collective-permute-done((bf16[16,2048]{1,0:T(8,128)(2,1)S(1)}, bf16[16,2048]{1,0:T(8,128)(2,1)S(1)}, u32[]{:S(2)}, u32[]{:S(2)}) %collective-permute-start.2) | collective-permute-done | bytes 65568 | tf_op jit(solution)/shard_map/ppermute | solution.py:206
  8.7 1.9 %collective-permute-start.4 = (bf16[16,2048]{1,0:T(8,128)(2,1)S(1)}, bf16[16,2048]{1,0:T(8,128)(2,1)S(1)}, u32[]{:S(2)}, u32[]{:S(2)}) collective-permute-start(bf16[16,2048]{1,0:T(8,128)(2,1)S(1)} %collective-permute-done.2.refs_4_), channel_id=1, source_target_pairs={{0,4},{4,0},{8,12},{12,8},{1,5},{5,1},{9,13},{13,9},{2,6},{6,2},{1... | collective-permute-start | bytes 196616 | tf_op jit(solution)/shard_map/ppermute | solution.py:206
  10.6 0.4 collective-permute-done.3.refs_5_
  11.1 1.3 %collective-permute-start.5 = (bf16[16,2048]{1,0:T(8,128)(2,1)S(1)}, bf16[16,2048]{1,0:T(8,128)(2,1)S(1)}, u32[]{:S(2)}, u32[]{:S(2)}) collective-permute-start(bf16[16,2048]{1,0:T(8,128)(2,1)S(1)} %collective-permute-done.3.refs_5_), channel_id=1, source_target_pairs={{0,4},{4,0},{8,12},{12,8},{1,5},{5,1},{9,13},{13,9},{2,6},{6,2},{1... | collective-permute-start | bytes 196616 | tf_op jit(solution)/shard_map/ppermute | solution.py:206
  12.4 4.1 %shard_map.83 = (bf16[2048,1280]{1,0:T(8,128)(2,1)S(1)}, bf16[2048,1280]{1,0:T(8,128)(2,1)S(1)}, bf16[128,128]{1,0:T(8,128)(2,1)S(1)}) custom-call(bf16[4096,2560]{1,0:T(8,128)(2,1)} %weight.4, s32[128]{0:T(128)} %slots.3), custom_call_target="tpu_custom_call" | custom-call | bytes 10485760 | tf_op jit(solution)/shard_map/pallas_call | solution.py:612
  16.5 0.0 collective-permute-done.refs_2_
  16.5 1.1 %shard_map.84 = (bf16[128,1408]{1,0:T(8,128)(2,1)S(1)}, bf16[128,2048]{1,0:T(8,128)(2,1)S(1)}) custom-call(bf16[128,128]{1,0:T(8,128)(2,1)S(1)} %get-tuple-element.34.chosen, bf16[16,2048]{1,0:T(8,128)(2,1)S(1)} %get-tuple-element.58.refs_0_, bf16[16,2048]{1,0:T(8,128)(2,1)S(1)} %get-tuple-element.57.refs_1_, ...), custom_call_target="tpu_custom_call" | custom-call | flops 671088640 | bytes 5242880 | tf_op jit(solution)/shard_map/pallas_call | solution.py:393
  17.6 0.0 copy-start.2
  17.6 0.0 copy-start.3
  17.6 0.1 collective-permute-start.6
  17.7 0.9 %shard_map.85.own = f32[128,1280]{1,0:T(8,128)S(1)} custom-call(bf16[128,2048]{1,0:T(8,128)(2,1)S(1)} %get-tuple-element.37.permuted, bf16[2048,1280]{1,0:T(8,128)(2,1)S(1)} %get-tuple-element.35.refs_8_.weight), custom_call_target="tpu_custom_call" | custom-call | flops 671088640 | bytes 5242880 | tf_op jit(solution)/shard_map/pallas_call | solution.py:402
  18.6 0.8 %collective-permute-done.6.received = bf16[128,1408]{1,0:T(8,128)(2,1)S(1)} collective-permute-done((bf16[128,1408]{1,0:T(8,128)(2,1)S(1)}, bf16[128,1408]{1,0:T(8,128)(2,1)S(1)}, u32[]{:S(2)}, u32[]{:S(2)}) %collective-permute-start.6) | collective-permute-done | bytes 360480 | tf_op jit(solution)/shard_map/ppermute | solution.py:206
  19.4 0.1 shard_map.86
  19.5 3.2 %collective-permute-start.7 = (bf16[32,1408]{1,0:T(8,128)(2,1)S(1)}, bf16[32,1408]{1,0:T(8,128)(2,1)S(1)}, u32[]{:S(2)}, u32[]{:S(2)}) collective-permute-start(bf16[32,1408]{1,0:T(8,128)(2,1)S(1)} %get-tuple-element.39), channel_id=1, source_target_pairs={{0,8},{2,0},{4,12},{6,4},{8,10},{10,2},{12,14},{14,6},{1,9},{3,1},... | collective-permute-start | bytes 270344 | tf_op jit(solution)/shard_map/ppermute | solution.py:447
  22.6 1.6 %collective-permute-start.8 = (bf16[32,1408]{1,0:T(8,128)(2,1)S(1)}, bf16[32,1408]{1,0:T(8,128)(2,1)S(1)}, u32[]{:S(2)}, u32[]{:S(2)}) collective-permute-start(bf16[32,1408]{1,0:T(8,128)(2,1)S(1)} %get-tuple-element.40), channel_id=1, source_target_pairs={{0,12},{2,4},{4,8},{6,0},{8,14},{10,6},{12,10},{14,2},{1,13},{3,5}... | collective-permute-start | bytes 270344 | tf_op jit(solution)/shard_map/ppermute | solution.py:447
  24.3 0.4 collective-permute-start.9
  24.7 0.7 %collective-permute-start.10 = (bf16[32,1280]{1,0:T(8,128)(2,1)S(1)}, bf16[32,1280]{1,0:T(8,128)(2,1)S(1)}, u32[]{:S(2)}, u32[]{:S(2)}) collective-permute-start(bf16[32,1280]{1,0:T(8,128)(2,1)S(1)} %get-tuple-element.42.refs_4_), channel_id=1, source_target_pairs={{0,10},{2,8},{4,14},{6,12},{8,2},{10,0},{12,6},{14,4},{1,11},{3,9}... | collective-permute-start | bytes 245768 | tf_op jit(solution)/shard_map/ppermute | solution.py:447
  25.4 3.7 %shard_map.82 = (bf16[2048,1024]{1,0:T(8,128)(2,1)S(1)}, bf16[32,64,256]{2,1,0:T(8,128)(2,1)S(1)}, bf16[32,64,256]{2,1,0:T(8,128)(2,1)S(1)}, f32[32,128]{1,0:T(8...) custom-call(s32[32]{0:T(128)S(1)} %copy-done.3, bf16[4096,2048]{1,0:T(8,128)(2,1)} %weight.5, ...), custom_call_target="tpu_custom_call" | custom-call | bytes 6291456 | tf_op jit(solution)/shard_map/pallas_call | solution.py:633
  29.1 6.7 %collective-permute-done.10.refs_3_ = bf16[32,1280]{1,0:T(8,128)(2,1)S(1)} collective-permute-done((bf16[32,1280]{1,0:T(8,128)(2,1)S(1)}, bf16[32,1280]{1,0:T(8,128)(2,1)S(1)}, u32[]{:S(2)}, u32[]{:S(2)}) %collective-permute-start.10) | collective-permute-done | bytes 81952 | tf_op jit(solution)/shard_map/ppermute | solution.py:447
  35.8 1.7 %shard_map.87 = (bf16[16,2048]{1,0:T(8,128)(2,1)S(1)}, bf16[16,2048]{1,0:T(8,128)(2,1)S(1)}) custom-call(f32[32,128]{1,0:T(8,128)S(1)} %get-tuple-element.31.cosine, f32[32,128]{1,0:T(8,128)S(1)} %get-tuple-element.32.sine, s32[32,128]{1,0:T(8,128)S(1)} %get-tuple-element.33.lengths, bf16[32,1408]{1,0:T(8,128)(2,1)S(1)} %collective-permute-done.7.refs_0_, ...), custom_call_target="tpu_custom_call" | custom-call | flops 16777216 | tf_op jit(solution)/shard_map/pallas_call | solution.py:645
  37.6 0.1 collective-permute-start.13
  37.6 2.9 %collective-permute-start.14 = (bf16[16,2048]{1,0:T(8,128)(2,1)S(1)}, bf16[16,2048]{1,0:T(8,128)(2,1)S(1)}, u32[]{:S(2)}, u32[]{:S(2)}) collective-permute-start(bf16[16,2048]{1,0:T(8,128)(2,1)S(1)} %get-tuple-element.46.attended.refs_1_), channel_id=1, source_target_pairs={{0,8},{4,12},{8,0},{12,4},{1,9},{5,13},{9,1},{13,5},{2,10},{6,14},... | collective-permute-start | bytes 196616 | tf_op jit(solution)/shard_map/ppermute | solution.py:206
  40.6 2.0 %collective-permute-start.12 = (bf16[16,2048]{1,0:T(8,128)(2,1)S(1)}, bf16[16,2048]{1,0:T(8,128)(2,1)S(1)}, u32[]{:S(2)}, u32[]{:S(2)}) collective-permute-start(bf16[16,2048]{1,0:T(8,128)(2,1)S(1)} %get-tuple-element.46.attended.refs_1_), channel_id=1, source_target_pairs={{0,4},{4,0},{8,12},{12,8},{1,5},{5,1},{9,13},{13,9},{2,6},{6,2},{1... | collective-permute-start | bytes 196616 | tf_op jit(solution)/shard_map/ppermute | solution.py:206
  42.6 1.6 %collective-permute-done.13.refs_4_ = bf16[16,2048]{1,0:T(8,128)(2,1)S(1)} collective-permute-done((bf16[16,2048]{1,0:T(8,128)(2,1)S(1)}, bf16[16,2048]{1,0:T(8,128)(2,1)S(1)}, u32[]{:S(2)}, u32[]{:S(2)}) %collective-permute-start.13) | collective-permute-done | bytes 65568 | tf_op jit(solution)/shard_map/ppermute | solution.py:206
  44.2 1.3 %collective-permute-done.14.refs_5_ = bf16[16,2048]{1,0:T(8,128)(2,1)S(1)} collective-permute-done((bf16[16,2048]{1,0:T(8,128)(2,1)S(1)}, bf16[16,2048]{1,0:T(8,128)(2,1)S(1)}, u32[]{:S(2)}, u32[]{:S(2)}) %collective-permute-start.14) | collective-permute-done | bytes 65568 | tf_op jit(solution)/shard_map/ppermute | solution.py:206
  45.5 0.7 %collective-permute-start.16 = (bf16[16,2048]{1,0:T(8,128)(2,1)S(1)}, bf16[16,2048]{1,0:T(8,128)(2,1)S(1)}, u32[]{:S(2)}, u32[]{:S(2)}) collective-permute-start(bf16[16,2048]{1,0:T(8,128)(2,1)S(1)} %collective-permute-done.14.refs_5_), channel_id=1, source_target_pairs={{0,4},{4,0},{8,12},{12,8},{1,5},{5,1},{9,13},{13,9},{2,6},{6,2},{1... | collective-permute-start | bytes 196616 | tf_op jit(solution)/shard_map/ppermute | solution.py:206
  46.2 2.2 %shard_map.88.refs_8_.weight = bf16[2048,1024]{1,0:T(8,128)(2,1)S(1)} custom-call(bf16[4096,2048]{1,0:T(8,128)(2,1)} %weight.5, bf16[16,2048]{1,0:T(8,128)(2,1)S(1)} %get-tuple-element.46.attended.refs_1_), custom_call_target="tpu_custom_call" | custom-call | bytes 4194304 | tf_op jit(solution)/shard_map/pallas_call | solution.py:655
  48.5 1.1 %collective-permute-done.15.refs_6_ = bf16[16,2048]{1,0:T(8,128)(2,1)S(1)} collective-permute-done((bf16[16,2048]{1,0:T(8,128)(2,1)S(1)}, bf16[16,2048]{1,0:T(8,128)(2,1)S(1)}, u32[]{:S(2)}, u32[]{:S(2)}) %collective-permute-start.15) | collective-permute-done | bytes 65568 | tf_op jit(solution)/shard_map/ppermute | solution.py:206
  49.6 0.7 %collective-permute-done.16.refs_7_ = bf16[16,2048]{1,0:T(8,128)(2,1)S(1)} collective-permute-done((bf16[16,2048]{1,0:T(8,128)(2,1)S(1)}, bf16[16,2048]{1,0:T(8,128)(2,1)S(1)}, u32[]{:S(2)}, u32[]{:S(2)}) %collective-permute-start.16) | collective-permute-done | bytes 65568 | tf_op jit(solution)/shard_map/ppermute | solution.py:206
  50.4 0.8 %shard_map.89 = (bf16[128,1024]{1,0:T(8,128)(2,1)S(1)}, bf16[128,2048]{1,0:T(8,128)(2,1)S(1)}) custom-call(bf16[128,128]{1,0:T(8,128)(2,1)S(1)} %get-tuple-element.47.chosen, bf16[16,2048]{1,0:T(8,128)(2,1)S(1)} %get-tuple-element.45.refs_0_, bf16[16,2048]{1,0:T(8,128)(2,1)S(1)} %get-tuple-element.46.attended.refs_1_, ...), custom_call_target="tpu_custom_call" | custom-call | flops 536870912 | bytes 4194304 | tf_op jit(solution)/shard_map/pallas_call | solution.py:393
  51.2 0.0 copy-start
  51.2 0.1 collective-permute-start.17
  51.3 0.7 %shard_map.90.own = f32[128,1024]{1,0:T(8,128)S(1)} custom-call(bf16[128,2048]{1,0:T(8,128)(2,1)S(1)} %get-tuple-element.49.permuted, bf16[2048,1024]{1,0:T(8,128)(2,1)S(1)} %shard_map.88.refs_8_.weight), custom_call_target="tpu_custom_call" | custom-call | flops 536870912 | bytes 4194304 | tf_op jit(solution)/shard_map/pallas_call | solution.py:402
  52.0 0.8 %collective-permute-done.17.received = bf16[128,1024]{1,0:T(8,128)(2,1)S(1)} collective-permute-done((bf16[128,1024]{1,0:T(8,128)(2,1)S(1)}, bf16[128,1024]{1,0:T(8,128)(2,1)S(1)}, u32[]{:S(2)}, u32[]{:S(2)}) %collective-permute-start.17) | collective-permute-done | bytes 262176 | tf_op jit(solution)/shard_map/ppermute | solution.py:206
  52.9 0.3 collective-permute-start.18
  53.2 2.4 %collective-permute-start.19 = (bf16[32,1024]{1,0:T(8,128)(2,1)S(1)}, bf16[32,1024]{1,0:T(8,128)(2,1)S(1)}, u32[]{:S(2)}, u32[]{:S(2)}) collective-permute-start(bf16[32,1024]{1,0:T(8,128)(2,1)S(1)} %get-tuple-element.52), channel_id=1, source_target_pairs={{0,12},{2,4},{4,8},{6,0},{8,14},{10,6},{12,10},{14,2},{1,13},{3,5}... | collective-permute-start | bytes 196616 | tf_op jit(solution)/shard_map/ppermute | solution.py:447
  55.6 3.1 %collective-permute-start.21 = (bf16[32,1024]{1,0:T(8,128)(2,1)S(1)}, bf16[32,1024]{1,0:T(8,128)(2,1)S(1)}, u32[]{:S(2)}, u32[]{:S(2)}) collective-permute-start(bf16[32,1024]{1,0:T(8,128)(2,1)S(1)} %get-tuple-element.54.refs_6_), channel_id=1, source_target_pairs={{0,10},{2,8},{4,14},{6,12},{8,2},{10,0},{12,6},{14,4},{1,11},{3,9}... | collective-permute-start | bytes 196616 | tf_op jit(solution)/shard_map/ppermute | solution.py:447
  58.8 1.9 %collective-permute-done.20.refs_4_ = bf16[32,1024]{1,0:T(8,128)(2,1)S(1)} collective-permute-done((bf16[32,1024]{1,0:T(8,128)(2,1)S(1)}, bf16[32,1024]{1,0:T(8,128)(2,1)S(1)}, u32[]{:S(2)}, u32[]{:S(2)}) %collective-permute-start.20) | collective-permute-done | bytes 65568 | tf_op jit(solution)/shard_map/ppermute | solution.py:447
  60.6 3.2 %collective-permute-done.21.refs_5_ = bf16[32,1024]{1,0:T(8,128)(2,1)S(1)} collective-permute-done((bf16[32,1024]{1,0:T(8,128)(2,1)S(1)}, bf16[32,1024]{1,0:T(8,128)(2,1)S(1)}, u32[]{:S(2)}, u32[]{:S(2)}) %collective-permute-start.21) | collective-permute-done | bytes 65568 | tf_op jit(solution)/shard_map/ppermute | solution.py:447
  63.8 0.1 shard_map.92
  63.9 0.1 collective-permute-start.22
  64.0 1.3 %collective-permute-done.22.received = bf16[32,2048]{1,0:T(8,128)(2,1)S(1)} collective-permute-done((bf16[32,2048]{1,0:T(8,128)(2,1)S(1)}, bf16[32,2048]{1,0:T(8,128)(2,1)S(1)}, u32[]{:S(2)}, u32[]{:S(2)}) %collective-permute-start.22) | collective-permute-done | bytes 131104 | tf_op jit(solution)/shard_map/ppermute | solution.py:206
  65.3 0.7 %shard_map.93 = bf16[1,32,4096]{2,1,0:T(8,128)(2,1)} custom-call(bf16[32,2048]{1,0:T(8,128)(2,1)S(1)} %get-tuple-element.55.keep, bf16[32,2048]{1,0:T(8,128)(2,1)S(1)} %collective-permute-done.22.received), custom_call_target="tpu_custom_call" | custom-call | bytes 524288 | tf_op jit(solution)/shard_map/pallas_call | solution.py:677
  (19 shorter events, 0.1 us)
Async XLA Ops:
  0.9 7.9 %collective-permute-start.2 = (bf16[16,2048]{1,0:T(8,128)(2,1)S(1)}, bf16[16,2048]{1,0:T(8,128)(2,1)S(1)}, u32[]{:S(2)}, u32[]{:S(2)}) collective-permute-start(bf16[16,2048]{1,0:T(8,128)(2,1)S(1)} %get-tuple-element.58.refs_0_), channel_id=1, source_target_pairs={{0,8},{4,12},{8,0},{12,4},{1,9},{5,13},{9,1},{13,5},{2,10},{6,14},... | collective-permute-start | bytes 196616 | tf_op jit(solution)/shard_map/ppermute | solution.py:206
  5.0 11.5 %copy-start.1 = (bf16[4096]{0:T(1024)(128)(2,1)S(1)}, bf16[4096]{0:T(1024)(128)(2,1)}, u32[]{:S(2)}) copy-start(bf16[4096]{0:T(1024)(128)(2,1)} %param.9) | copy-start | bytes 24580
  5.0 6.1 %collective-permute-start.3 = (bf16[16,2048]{1,0:T(8,128)(2,1)S(1)}, bf16[16,2048]{1,0:T(8,128)(2,1)S(1)}, u32[]{:S(2)}, u32[]{:S(2)}) collective-permute-start(bf16[16,2048]{1,0:T(8,128)(2,1)S(1)} %get-tuple-element.57.refs_1_), channel_id=1, source_target_pairs={{0,8},{4,12},{8,0},{12,4},{1,9},{5,13},{9,1},{13,5},{2,10},{6,14},... | collective-permute-start | bytes 196616 | tf_op jit(solution)/shard_map/ppermute | solution.py:206
  5.1 11.4 %collective-permute-start = (bf16[16,2048]{1,0:T(8,128)(2,1)S(1)}, bf16[16,2048]{1,0:T(8,128)(2,1)S(1)}, u32[]{:S(2)}, u32[]{:S(2)}) collective-permute-start(bf16[16,2048]{1,0:T(8,128)(2,1)S(1)} %get-tuple-element.58.refs_0_), channel_id=1, source_target_pairs={{0,4},{4,0},{8,12},{12,8},{1,5},{5,1},{9,13},{13,9},{2,6},{6,2},{1... | collective-permute-start | bytes 196616 | tf_op jit(solution)/shard_map/ppermute | solution.py:206
  6.9 9.6 %collective-permute-start.1 = (bf16[16,2048]{1,0:T(8,128)(2,1)S(1)}, bf16[16,2048]{1,0:T(8,128)(2,1)S(1)}, u32[]{:S(2)}, u32[]{:S(2)}) collective-permute-start(bf16[16,2048]{1,0:T(8,128)(2,1)S(1)} %get-tuple-element.57.refs_1_), channel_id=1, source_target_pairs={{0,4},{4,0},{8,12},{12,8},{1,5},{5,1},{9,13},{13,9},{2,6},{6,2},{1... | collective-permute-start | bytes 196616 | tf_op jit(solution)/shard_map/ppermute | solution.py:206
  8.7 7.8 %collective-permute-start.4 = (bf16[16,2048]{1,0:T(8,128)(2,1)S(1)}, bf16[16,2048]{1,0:T(8,128)(2,1)S(1)}, u32[]{:S(2)}, u32[]{:S(2)}) collective-permute-start(bf16[16,2048]{1,0:T(8,128)(2,1)S(1)} %collective-permute-done.2.refs_4_), channel_id=1, source_target_pairs={{0,4},{4,0},{8,12},{12,8},{1,5},{5,1},{9,13},{13,9},{2,6},{6,2},{1... | collective-permute-start | bytes 196616 | tf_op jit(solution)/shard_map/ppermute | solution.py:206
  11.1 5.4 %collective-permute-start.5 = (bf16[16,2048]{1,0:T(8,128)(2,1)S(1)}, bf16[16,2048]{1,0:T(8,128)(2,1)S(1)}, u32[]{:S(2)}, u32[]{:S(2)}) collective-permute-start(bf16[16,2048]{1,0:T(8,128)(2,1)S(1)} %collective-permute-done.3.refs_5_), channel_id=1, source_target_pairs={{0,4},{4,0},{8,12},{12,8},{1,5},{5,1},{9,13},{13,9},{2,6},{6,2},{1... | collective-permute-start | bytes 196616 | tf_op jit(solution)/shard_map/ppermute | solution.py:206
  17.6 7.7 %copy-start.2 = (s32[128]{0:T(128)S(1)}, s32[128]{0:T(128)}, u32[]{:S(2)}) copy-start(s32[128]{0:T(128)} %slots.3) | copy-start | bytes 1540
  17.6 7.7 %copy-start.3 = (s32[32]{0:T(128)S(1)}, s32[32]{0:T(128)}, u32[]{:S(2)}) copy-start(s32[32]{0:T(128)} %lengths.1) | copy-start | bytes 388
  17.6 1.7 %collective-permute-start.6 = (bf16[128,1408]{1,0:T(8,128)(2,1)S(1)}, bf16[128,1408]{1,0:T(8,128)(2,1)S(1)}, u32[]{:S(2)}, u32[]{:S(2)}) collective-permute-start(bf16[128,1408]{1,0:T(8,128)(2,1)S(1)} %get-tuple-element.38.given), channel_id=1, source_target_pairs={{0,1},{1,0},{2,3},{3,2},{4,5},{5,4},{6,7},{7,6},{8,9},{9,8},{10,11... | collective-permute-start | bytes 1081352 | tf_op jit(solution)/shard_map/ppermute | solution.py:206
  19.5 16.4 %collective-permute-start.7 = (bf16[32,1408]{1,0:T(8,128)(2,1)S(1)}, bf16[32,1408]{1,0:T(8,128)(2,1)S(1)}, u32[]{:S(2)}, u32[]{:S(2)}) collective-permute-start(bf16[32,1408]{1,0:T(8,128)(2,1)S(1)} %get-tuple-element.39), channel_id=1, source_target_pairs={{0,8},{2,0},{4,12},{6,4},{8,10},{10,2},{12,14},{14,6},{1,9},{3,1},... | collective-permute-start | bytes 270344 | tf_op jit(solution)/shard_map/ppermute | solution.py:447
  22.6 13.2 %collective-permute-start.8 = (bf16[32,1408]{1,0:T(8,128)(2,1)S(1)}, bf16[32,1408]{1,0:T(8,128)(2,1)S(1)}, u32[]{:S(2)}, u32[]{:S(2)}) collective-permute-start(bf16[32,1408]{1,0:T(8,128)(2,1)S(1)} %get-tuple-element.40), channel_id=1, source_target_pairs={{0,12},{2,4},{4,8},{6,0},{8,14},{10,6},{12,10},{14,2},{1,13},{3,5}... | collective-permute-start | bytes 270344 | tf_op jit(solution)/shard_map/ppermute | solution.py:447
  24.3 11.6 %collective-permute-start.9 = (bf16[32,1408]{1,0:T(8,128)(2,1)S(1)}, bf16[32,1408]{1,0:T(8,128)(2,1)S(1)}, u32[]{:S(2)}, u32[]{:S(2)}) collective-permute-start(bf16[32,1408]{1,0:T(8,128)(2,1)S(1)} %get-tuple-element.41), channel_id=1, source_target_pairs={{0,4},{2,12},{4,0},{6,8},{8,6},{10,14},{12,2},{14,10},{1,5},{3,13}... | collective-permute-start | bytes 270344 | tf_op jit(solution)/shard_map/ppermute | solution.py:447
  24.7 11.1 %collective-permute-start.10 = (bf16[32,1280]{1,0:T(8,128)(2,1)S(1)}, bf16[32,1280]{1,0:T(8,128)(2,1)S(1)}, u32[]{:S(2)}, u32[]{:S(2)}) collective-permute-start(bf16[32,1280]{1,0:T(8,128)(2,1)S(1)} %get-tuple-element.42.refs_4_), channel_id=1, source_target_pairs={{0,10},{2,8},{4,14},{6,12},{8,2},{10,0},{12,6},{14,4},{1,11},{3,9}... | collective-permute-start | bytes 245768 | tf_op jit(solution)/shard_map/ppermute | solution.py:447
  37.6 6.7 %collective-permute-start.13 = (bf16[16,2048]{1,0:T(8,128)(2,1)S(1)}, bf16[16,2048]{1,0:T(8,128)(2,1)S(1)}, u32[]{:S(2)}, u32[]{:S(2)}) collective-permute-start(bf16[16,2048]{1,0:T(8,128)(2,1)S(1)} %get-tuple-element.45.refs_0_), channel_id=1, source_target_pairs={{0,8},{4,12},{8,0},{12,4},{1,9},{5,13},{9,1},{13,5},{2,10},{6,14},... | collective-permute-start | bytes 196616 | tf_op jit(solution)/shard_map/ppermute | solution.py:206
  37.6 7.9 %collective-permute-start.14 = (bf16[16,2048]{1,0:T(8,128)(2,1)S(1)}, bf16[16,2048]{1,0:T(8,128)(2,1)S(1)}, u32[]{:S(2)}, u32[]{:S(2)}) collective-permute-start(bf16[16,2048]{1,0:T(8,128)(2,1)S(1)} %get-tuple-element.46.attended.refs_1_), channel_id=1, source_target_pairs={{0,8},{4,12},{8,0},{12,4},{1,9},{5,13},{9,1},{13,5},{2,10},{6,14},... | collective-permute-start | bytes 196616 | tf_op jit(solution)/shard_map/ppermute | solution.py:206
  40.5 7.9 %collective-permute-start.11 = (bf16[16,2048]{1,0:T(8,128)(2,1)S(1)}, bf16[16,2048]{1,0:T(8,128)(2,1)S(1)}, u32[]{:S(2)}, u32[]{:S(2)}) collective-permute-start(bf16[16,2048]{1,0:T(8,128)(2,1)S(1)} %get-tuple-element.45.refs_0_), channel_id=1, source_target_pairs={{0,4},{4,0},{8,12},{12,8},{1,5},{5,1},{9,13},{13,9},{2,6},{6,2},{1... | collective-permute-start | bytes 196616 | tf_op jit(solution)/shard_map/ppermute | solution.py:206
  40.6 8.0 %collective-permute-start.12 = (bf16[16,2048]{1,0:T(8,128)(2,1)S(1)}, bf16[16,2048]{1,0:T(8,128)(2,1)S(1)}, u32[]{:S(2)}, u32[]{:S(2)}) collective-permute-start(bf16[16,2048]{1,0:T(8,128)(2,1)S(1)} %get-tuple-element.46.attended.refs_1_), channel_id=1, source_target_pairs={{0,4},{4,0},{8,12},{12,8},{1,5},{5,1},{9,13},{13,9},{2,6},{6,2},{1... | collective-permute-start | bytes 196616 | tf_op jit(solution)/shard_map/ppermute | solution.py:206
  44.2 5.4 %collective-permute-start.15 = (bf16[16,2048]{1,0:T(8,128)(2,1)S(1)}, bf16[16,2048]{1,0:T(8,128)(2,1)S(1)}, u32[]{:S(2)}, u32[]{:S(2)}) collective-permute-start(bf16[16,2048]{1,0:T(8,128)(2,1)S(1)} %collective-permute-done.13.refs_4_), channel_id=1, source_target_pairs={{0,4},{4,0},{8,12},{12,8},{1,5},{5,1},{9,13},{13,9},{2,6},{6,2},{1... | collective-permute-start | bytes 196616 | tf_op jit(solution)/shard_map/ppermute | solution.py:206
  45.5 4.9 %collective-permute-start.16 = (bf16[16,2048]{1,0:T(8,128)(2,1)S(1)}, bf16[16,2048]{1,0:T(8,128)(2,1)S(1)}, u32[]{:S(2)}, u32[]{:S(2)}) collective-permute-start(bf16[16,2048]{1,0:T(8,128)(2,1)S(1)} %collective-permute-done.14.refs_5_), channel_id=1, source_target_pairs={{0,4},{4,0},{8,12},{12,8},{1,5},{5,1},{9,13},{13,9},{2,6},{6,2},{1... | collective-permute-start | bytes 196616 | tf_op jit(solution)/shard_map/ppermute | solution.py:206
  51.2 12.6 %copy-start = (bf16[32,4096]{1,0:T(8,128)(2,1)S(1)}, bf16[32,4096]{1,0:T(8,128)(2,1)}, u32[]{:S(2)}) copy-start(bf16[32,4096]{1,0:T(8,128)(2,1)} %hidden.1) | copy-start | bytes 786436
  51.2 1.6 %collective-permute-start.17 = (bf16[128,1024]{1,0:T(8,128)(2,1)S(1)}, bf16[128,1024]{1,0:T(8,128)(2,1)S(1)}, u32[]{:S(2)}, u32[]{:S(2)}) collective-permute-start(bf16[128,1024]{1,0:T(8,128)(2,1)S(1)} %get-tuple-element.50.given), channel_id=1, source_target_pairs={{0,1},{1,0},{2,3},{3,2},{4,5},{5,4},{6,7},{7,6},{8,9},{9,8},{10,11... | collective-permute-start | bytes 786440 | tf_op jit(solution)/shard_map/ppermute | solution.py:206
  52.9 5.9 %collective-permute-start.18 = (bf16[32,1024]{1,0:T(8,128)(2,1)S(1)}, bf16[32,1024]{1,0:T(8,128)(2,1)S(1)}, u32[]{:S(2)}, u32[]{:S(2)}) collective-permute-start(bf16[32,1024]{1,0:T(8,128)(2,1)S(1)} %get-tuple-element.51), channel_id=1, source_target_pairs={{0,8},{2,0},{4,12},{6,4},{8,10},{10,2},{12,14},{14,6},{1,9},{3,1},... | collective-permute-start | bytes 196616 | tf_op jit(solution)/shard_map/ppermute | solution.py:447
  53.2 5.6 %collective-permute-start.19 = (bf16[32,1024]{1,0:T(8,128)(2,1)S(1)}, bf16[32,1024]{1,0:T(8,128)(2,1)S(1)}, u32[]{:S(2)}, u32[]{:S(2)}) collective-permute-start(bf16[32,1024]{1,0:T(8,128)(2,1)S(1)} %get-tuple-element.52), channel_id=1, source_target_pairs={{0,12},{2,4},{4,8},{6,0},{8,14},{10,6},{12,10},{14,2},{1,13},{3,5}... | collective-permute-start | bytes 196616 | tf_op jit(solution)/shard_map/ppermute | solution.py:447
  55.6 5.0 %collective-permute-start.20 = (bf16[32,1024]{1,0:T(8,128)(2,1)S(1)}, bf16[32,1024]{1,0:T(8,128)(2,1)S(1)}, u32[]{:S(2)}, u32[]{:S(2)}) collective-permute-start(bf16[32,1024]{1,0:T(8,128)(2,1)S(1)} %get-tuple-element.53), channel_id=1, source_target_pairs={{0,4},{2,12},{4,0},{6,8},{8,6},{10,14},{12,2},{14,10},{1,5},{3,13}... | collective-permute-start | bytes 196616 | tf_op jit(solution)/shard_map/ppermute | solution.py:447
  55.6 8.2 %collective-permute-start.21 = (bf16[32,1024]{1,0:T(8,128)(2,1)S(1)}, bf16[32,1024]{1,0:T(8,128)(2,1)S(1)}, u32[]{:S(2)}, u32[]{:S(2)}) collective-permute-start(bf16[32,1024]{1,0:T(8,128)(2,1)S(1)} %get-tuple-element.54.refs_6_), channel_id=1, source_target_pairs={{0,10},{2,8},{4,14},{6,12},{8,2},{10,0},{12,6},{14,4},{1,11},{3,9}... | collective-permute-start | bytes 196616 | tf_op jit(solution)/shard_map/ppermute | solution.py:447
  63.9 1.4 %collective-permute-start.22 = (bf16[32,2048]{1,0:T(8,128)(2,1)S(1)}, bf16[32,2048]{1,0:T(8,128)(2,1)S(1)}, u32[]{:S(2)}, u32[]{:S(2)}) collective-permute-start(bf16[32,2048]{1,0:T(8,128)(2,1)S(1)} %get-tuple-element.56), channel_id=1, source_target_pairs={{0,1},{1,0},{2,3},{3,2},{4,5},{5,4},{6,7},{7,6},{8,9},{9,8},{10,11... | collective-permute-start | bytes 393224 | tf_op jit(solution)/shard_map/ppermute | solution.py:206

commit v14 on v13

--- a/solution.py
+++ b/solution.py
@@ -438,17 +438,21 @@
 def spread(products):
     col_count, row_count = lax.axis_size("col"), lax.axis_size("row")
     pairs = col_count // row_count
-    def target(col, row, j):
-        if j == 0 and row_count == 2:
-            return (col ^ pairs) * row_count + (row ^ 1)
-        return ((row * pairs + col % pairs) ^ j) * row_count + col // pairs
+    groups = lax.axis_size("groups")
+
+    def target(group, col, row, j):
+        if j == 0 and col // pairs == row:
+            group = (group + 1) % groups
+        col, row = (row * pairs + col % pairs) ^ j, col // pairs
+        return (group * col_count + col) * row_count + row
 
     sent = {
         j: lax.ppermute(
             products[j],
-            ("col", "row"),
+            ("groups", "col", "row"),
             [
-                (col * row_count + row, target(col, row, j))
+                ((group * col_count + col) * row_count + row, target(group, col, row, j))
+                for group in range(groups)
                 for col in range(col_count)
                 for row in range(row_count)
             ],

time: 66.2 us -> 64.6 us (0.976)
  the two profiles are of different devices: /device:TPU:0 before, /device:TPU:3 now
where the time goes in v14:
time: 64.6 us; the launch traced here: 64.4 us
  starting transfers between devices  28.2 us (44%)
  waiting for transfers between devices  18.9 us (29%)
  Pallas kernels  16.2 us (25%)
  local copies, waits for them, and re-layouts  0.9 us (1%)
    ppermute x15, starting transfers between devices, moved(): return lax.ppermute(value, axis, pairs)  16.8 us
    ppermute x8, waiting for transfers between devices, spread(): lax.ppermute(products[j], ('groups', 'col', 'row'), [((group * col_count...  11.9 us
    ppermute x8, starting transfers between devices, spread(): lax.ppermute(products[j], ('groups', 'col', 'row'), [((group * col_count...  11.4 us
    ppermute x15, waiting for transfers between devices, moved(): return lax.ppermute(value, axis, pairs)  7.08 us
    pallas_call x1, Pallas kernels, paired_plan(): call(functools.partial(stage_in_kernel, col_count), [pltpu.VMEM((half, ha...  4.09 us
    pallas_call x1, Pallas kernels, paired_plan(): call(functools.partial(stage_rest_kernel, col_count), [pltpu.VMEM((half,...  3.71 us
    pallas_call x1, Pallas kernels, paired_plan(): call(stage_out_kernel, pltpu.VMEM((half, half_out), jnp.bfloat16), [HBM,...  2.24 us
    pallas_call x2, Pallas kernels, project(): call(functools.partial(kernel, parts), [struct((rows, half + more)), stru...  1.91 us
  transfers between devices with their start and end apart: 23, of which 13 were waited for; matrix products, arithmetic and copies ran while one was open for 0% of the time, Pallas kernels for 18%

profile of v14, /device:TPU:3, one launch (start us, length us, event | category | flops | bytes accessed | tf_op | source)
XLA Modules:
  0.0 64.4 jit_solution(15950874138003134762)
XLA Ops:
  0.0 0.9 %fusion = (bf16[16,2048]{1,0:T(8,128)(2,1)S(1)}, bf16[16,2048]{1,0:T(8,128)(2,1)S(1)}) fusion(bf16[32,4096]{1,0:T(8,128)(2,1)} %hidden.1, s32[]{:T(128)S(6)} %add.4, s32[]{:T(128)S(6)} %select_n.3), kind=kLoop, calls=%fused_computation.1 | loop fusion | bytes 262152 | tf_op jit(solution)/shard_map/slice | solution.py:630
  0.9 2.4 %collective-permute-start.2 = (bf16[16,2048]{1,0:T(8,128)(2,1)S(1)}, bf16[16,2048]{1,0:T(8,128)(2,1)S(1)}, u32[]{:S(2)}, u32[]{:S(2)}) collective-permute-start(bf16[16,2048]{1,0:T(8,128)(2,1)S(1)} %get-tuple-element.58.refs_0_), channel_id=1, source_target_pairs={{0,8},{4,12},{8,0},{12,4},{1,9},{5,13},{9,1},{13,5},{2,10},{6,14},... | collective-permute-start | bytes 196616 | tf_op jit(solution)/shard_map/ppermute | solution.py:206
  3.3 0.1 collective-permute-start.3
  3.3 1.3 %collective-permute-start = (bf16[16,2048]{1,0:T(8,128)(2,1)S(1)}, bf16[16,2048]{1,0:T(8,128)(2,1)S(1)}, u32[]{:S(2)}, u32[]{:S(2)}) collective-permute-start(bf16[16,2048]{1,0:T(8,128)(2,1)S(1)} %get-tuple-element.58.refs_0_), channel_id=1, source_target_pairs={{0,4},{4,0},{8,12},{12,8},{1,5},{5,1},{9,13},{13,9},{2,6},{6,2},{1... | collective-permute-start | bytes 196616 | tf_op jit(solution)/shard_map/ppermute | solution.py:206
  4.6 0.2 collective-permute-start.1
  4.8 0.1 collective-permute-done.2.refs_4_
  5.0 3.8 %collective-permute-start.4 = (bf16[16,2048]{1,0:T(8,128)(2,1)S(1)}, bf16[16,2048]{1,0:T(8,128)(2,1)S(1)}, u32[]{:S(2)}, u32[]{:S(2)}) collective-permute-start(bf16[16,2048]{1,0:T(8,128)(2,1)S(1)} %collective-permute-done.2.refs_4_), channel_id=1, source_target_pairs={{0,4},{4,0},{8,12},{12,8},{1,5},{5,1},{9,13},{13,9},{2,6},{6,2},{1... | collective-permute-start | bytes 196616 | tf_op jit(solution)/shard_map/ppermute | solution.py:206
  8.7 1.0 %collective-permute-done.3.refs_5_ = bf16[16,2048]{1,0:T(8,128)(2,1)S(1)} collective-permute-done((bf16[16,2048]{1,0:T(8,128)(2,1)S(1)}, bf16[16,2048]{1,0:T(8,128)(2,1)S(1)}, u32[]{:S(2)}, u32[]{:S(2)}) %collective-permute-start.3) | collective-permute-done | bytes 65568 | tf_op jit(solution)/shard_map/ppermute | solution.py:206
  9.7 0.8 %collective-permute-start.5 = (bf16[16,2048]{1,0:T(8,128)(2,1)S(1)}, bf16[16,2048]{1,0:T(8,128)(2,1)S(1)}, u32[]{:S(2)}, u32[]{:S(2)}) collective-permute-start(bf16[16,2048]{1,0:T(8,128)(2,1)S(1)} %collective-permute-done.3.refs_5_), channel_id=1, source_target_pairs={{0,4},{4,0},{8,12},{12,8},{1,5},{5,1},{9,13},{13,9},{2,6},{6,2},{1... | collective-permute-start | bytes 196616 | tf_op jit(solution)/shard_map/ppermute | solution.py:206
  10.5 4.1 %shard_map.83 = (bf16[2048,1280]{1,0:T(8,128)(2,1)S(1)}, bf16[2048,1280]{1,0:T(8,128)(2,1)S(1)}, bf16[128,128]{1,0:T(8,128)(2,1)S(1)}) custom-call(bf16[4096,2560]{1,0:T(8,128)(2,1)} %weight.4, s32[128]{0:T(128)} %slots.3), custom_call_target="tpu_custom_call" | custom-call | bytes 10485760 | tf_op jit(solution)/shard_map/pallas_call | solution.py:616
  14.7 1.1 %shard_map.84 = (bf16[128,1408]{1,0:T(8,128)(2,1)S(1)}, bf16[128,2048]{1,0:T(8,128)(2,1)S(1)}) custom-call(bf16[128,128]{1,0:T(8,128)(2,1)S(1)} %get-tuple-element.34.chosen, bf16[16,2048]{1,0:T(8,128)(2,1)S(1)} %get-tuple-element.58.refs_0_, bf16[16,2048]{1,0:T(8,128)(2,1)S(1)} %get-tuple-element.57.refs_1_, ...), custom_call_target="tpu_custom_call" | custom-call | flops 671088640 | bytes 5242880 | tf_op jit(solution)/shard_map/pallas_call | solution.py:393
  15.8 0.0 copy-start.2
  15.8 1.2 %collective-permute-start.6 = (bf16[128,1408]{1,0:T(8,128)(2,1)S(1)}, bf16[128,1408]{1,0:T(8,128)(2,1)S(1)}, u32[]{:S(2)}, u32[]{:S(2)}) collective-permute-start(bf16[128,1408]{1,0:T(8,128)(2,1)S(1)} %get-tuple-element.38.given), channel_id=1, source_target_pairs={{0,1},{1,0},{2,3},{3,2},{4,5},{5,4},{6,7},{7,6},{8,9},{9,8},{10,11... | collective-permute-start | bytes 1081352 | tf_op jit(solution)/shard_map/ppermute | solution.py:206
  16.9 0.9 %shard_map.85.own = f32[128,1280]{1,0:T(8,128)S(1)} custom-call(bf16[128,2048]{1,0:T(8,128)(2,1)S(1)} %get-tuple-element.37.permuted, bf16[2048,1280]{1,0:T(8,128)(2,1)S(1)} %get-tuple-element.35.refs_8_.weight), custom_call_target="tpu_custom_call" | custom-call | flops 671088640 | bytes 5242880 | tf_op jit(solution)/shard_map/pallas_call | solution.py:402
  17.8 0.4 collective-permute-done.6.received
  18.2 0.1 shard_map.86
  18.3 0.3 collective-permute-start.7
  18.6 3.0 %collective-permute-start.8 = (bf16[32,1408]{1,0:T(8,128)(2,1)S(1)}, bf16[32,1408]{1,0:T(8,128)(2,1)S(1)}, u32[]{:S(2)}, u32[]{:S(2)}) collective-permute-start(bf16[32,1408]{1,0:T(8,128)(2,1)S(1)} %get-tuple-element.40), channel_id=1, source_target_pairs={{0,12},{2,4},{4,8},{6,0},{8,14},{10,6},{12,10},{14,2},{16,28},{18,... | collective-permute-start | bytes 270344 | tf_op jit(solution)/shard_map/ppermute | solution.py:450
  21.6 1.7 %collective-permute-start.9 = (bf16[32,1408]{1,0:T(8,128)(2,1)S(1)}, bf16[32,1408]{1,0:T(8,128)(2,1)S(1)}, u32[]{:S(2)}, u32[]{:S(2)}) collective-permute-start(bf16[32,1408]{1,0:T(8,128)(2,1)S(1)} %get-tuple-element.41), channel_id=1, source_target_pairs={{0,4},{2,12},{4,0},{6,8},{8,6},{10,14},{12,2},{14,10},{16,20},{18,... | collective-permute-start | bytes 270344 | tf_op jit(solution)/shard_map/ppermute | solution.py:450
  23.3 1.4 %collective-permute-start.10 = (bf16[32,1280]{1,0:T(8,128)(2,1)S(1)}, bf16[32,1280]{1,0:T(8,128)(2,1)S(1)}, u32[]{:S(2)}, u32[]{:S(2)}) collective-permute-start(bf16[32,1280]{1,0:T(8,128)(2,1)S(1)} %get-tuple-element.42.refs_4_), channel_id=1, source_target_pairs={{0,16},{2,8},{4,20},{6,12},{8,2},{10,26},{12,6},{14,30},{16,0},{18... | collective-permute-start | bytes 245768 | tf_op jit(solution)/shard_map/ppermute | solution.py:450
  24.7 3.7 %shard_map.82 = (bf16[2048,1024]{1,0:T(8,128)(2,1)S(1)}, bf16[32,64,256]{2,1,0:T(8,128)(2,1)S(1)}, bf16[32,64,256]{2,1,0:T(8,128)(2,1)S(1)}, f32[32,128]{1,0:T(8...) custom-call(s32[32]{0:T(128)S(1)} %copy-done.3, bf16[4096,2048]{1,0:T(8,128)(2,1)} %weight.5, ...), custom_call_target="tpu_custom_call" | custom-call | bytes 6291456 | tf_op jit(solution)/shard_map/pallas_call | solution.py:637
  28.4 3.8 %collective-permute-done.10.refs_3_ = bf16[32,1280]{1,0:T(8,128)(2,1)S(1)} collective-permute-done((bf16[32,1280]{1,0:T(8,128)(2,1)S(1)}, bf16[32,1280]{1,0:T(8,128)(2,1)S(1)}, u32[]{:S(2)}, u32[]{:S(2)}) %collective-permute-start.10) | collective-permute-done | bytes 81952 | tf_op jit(solution)/shard_map/ppermute | solution.py:450
  32.2 1.7 %shard_map.87 = (bf16[16,2048]{1,0:T(8,128)(2,1)S(1)}, bf16[16,2048]{1,0:T(8,128)(2,1)S(1)}) custom-call(f32[32,128]{1,0:T(8,128)S(1)} %get-tuple-element.31.cosine, f32[32,128]{1,0:T(8,128)S(1)} %get-tuple-element.32.sine, s32[32,128]{1,0:T(8,128)S(1)} %get-tuple-element.33.lengths, bf16[32,1408]{1,0:T(8,128)(2,1)S(1)} %collective-permute-done.7.refs_0_, ...), custom_call_target="tpu_custom_call" | custom-call | flops 16777216 | tf_op jit(solution)/shard_map/pallas_call | solution.py:649
  33.9 0.1 collective-permute-start.13
  34.0 2.4 %collective-permute-start.14 = (bf16[16,2048]{1,0:T(8,128)(2,1)S(1)}, bf16[16,2048]{1,0:T(8,128)(2,1)S(1)}, u32[]{:S(2)}, u32[]{:S(2)}) collective-permute-start(bf16[16,2048]{1,0:T(8,128)(2,1)S(1)} %get-tuple-element.46.attended.refs_1_), channel_id=1, source_target_pairs={{0,8},{4,12},{8,0},{12,4},{1,9},{5,13},{9,1},{13,5},{2,10},{6,14},... | collective-permute-start | bytes 196616 | tf_op jit(solution)/shard_map/ppermute | solution.py:206
  36.4 1.5 %collective-permute-start.12 = (bf16[16,2048]{1,0:T(8,128)(2,1)S(1)}, bf16[16,2048]{1,0:T(8,128)(2,1)S(1)}, u32[]{:S(2)}, u32[]{:S(2)}) collective-permute-start(bf16[16,2048]{1,0:T(8,128)(2,1)S(1)} %get-tuple-element.46.attended.refs_1_), channel_id=1, source_target_pairs={{0,4},{4,0},{8,12},{12,8},{1,5},{5,1},{9,13},{13,9},{2,6},{6,2},{1... | collective-permute-start | bytes 196616 | tf_op jit(solution)/shard_map/ppermute | solution.py:206
  37.8 0.2 collective-permute-done.13.refs_4_
  38.0 1.0 %collective-permute-done.14.refs_5_ = bf16[16,2048]{1,0:T(8,128)(2,1)S(1)} collective-permute-done((bf16[16,2048]{1,0:T(8,128)(2,1)S(1)}, bf16[16,2048]{1,0:T(8,128)(2,1)S(1)}, u32[]{:S(2)}, u32[]{:S(2)}) %collective-permute-start.14) | collective-permute-done | bytes 65568 | tf_op jit(solution)/shard_map/ppermute | solution.py:206
  39.0 0.5 collective-permute-start.16
  39.5 2.2 %shard_map.88.refs_8_.weight = bf16[2048,1024]{1,0:T(8,128)(2,1)S(1)} custom-call(bf16[4096,2048]{1,0:T(8,128)(2,1)} %weight.5, bf16[16,2048]{1,0:T(8,128)(2,1)S(1)} %get-tuple-element.46.attended.refs_1_), custom_call_target="tpu_custom_call" | custom-call | bytes 4194304 | tf_op jit(solution)/shard_map/pallas_call | solution.py:659
  41.8 1.5 %collective-permute-done.15.refs_6_ = bf16[16,2048]{1,0:T(8,128)(2,1)S(1)} collective-permute-done((bf16[16,2048]{1,0:T(8,128)(2,1)S(1)}, bf16[16,2048]{1,0:T(8,128)(2,1)S(1)}, u32[]{:S(2)}, u32[]{:S(2)}) %collective-permute-start.15) | collective-permute-done | bytes 65568 | tf_op jit(solution)/shard_map/ppermute | solution.py:206
  43.3 1.4 %collective-permute-done.16.refs_7_ = bf16[16,2048]{1,0:T(8,128)(2,1)S(1)} collective-permute-done((bf16[16,2048]{1,0:T(8,128)(2,1)S(1)}, bf16[16,2048]{1,0:T(8,128)(2,1)S(1)}, u32[]{:S(2)}, u32[]{:S(2)}) %collective-permute-start.16) | collective-permute-done | bytes 65568 | tf_op jit(solution)/shard_map/ppermute | solution.py:206
  44.7 0.8 %shard_map.89 = (bf16[128,1024]{1,0:T(8,128)(2,1)S(1)}, bf16[128,2048]{1,0:T(8,128)(2,1)S(1)}) custom-call(bf16[128,128]{1,0:T(8,128)(2,1)S(1)} %get-tuple-element.47.chosen, bf16[16,2048]{1,0:T(8,128)(2,1)S(1)} %get-tuple-element.45.refs_0_, bf16[16,2048]{1,0:T(8,128)(2,1)S(1)} %get-tuple-element.46.attended.refs_1_, ...), custom_call_target="tpu_custom_call" | custom-call | flops 536870912 | bytes 4194304 | tf_op jit(solution)/shard_map/pallas_call | solution.py:393
  45.5 0.0 copy-start
  45.5 2.2 %collective-permute-start.17 = (bf16[128,1024]{1,0:T(8,128)(2,1)S(1)}, bf16[128,1024]{1,0:T(8,128)(2,1)S(1)}, u32[]{:S(2)}, u32[]{:S(2)}) collective-permute-start(bf16[128,1024]{1,0:T(8,128)(2,1)S(1)} %get-tuple-element.50.given), channel_id=1, source_target_pairs={{0,1},{1,0},{2,3},{3,2},{4,5},{5,4},{6,7},{7,6},{8,9},{9,8},{10,11... | collective-permute-start | bytes 786440 | tf_op jit(solution)/shard_map/ppermute | solution.py:206
  47.7 0.7 %shard_map.90.own = f32[128,1024]{1,0:T(8,128)S(1)} custom-call(bf16[128,2048]{1,0:T(8,128)(2,1)S(1)} %get-tuple-element.49.permuted, bf16[2048,1024]{1,0:T(8,128)(2,1)S(1)} %shard_map.88.refs_8_.weight), custom_call_target="tpu_custom_call" | custom-call | flops 536870912 | bytes 4194304 | tf_op jit(solution)/shard_map/pallas_call | solution.py:402
  48.4 0.4 collective-permute-done.17.received
  48.9 0.1 collective-permute-start.18
  49.0 3.6 %collective-permute-start.19 = (bf16[32,1024]{1,0:T(8,128)(2,1)S(1)}, bf16[32,1024]{1,0:T(8,128)(2,1)S(1)}, u32[]{:S(2)}, u32[]{:S(2)}) collective-permute-start(bf16[32,1024]{1,0:T(8,128)(2,1)S(1)} %get-tuple-element.52), channel_id=1, source_target_pairs={{0,12},{2,4},{4,8},{6,0},{8,14},{10,6},{12,10},{14,2},{16,28},{18,... | collective-permute-start | bytes 196616 | tf_op jit(solution)/shard_map/ppermute | solution.py:450
  52.5 0.9 %collective-permute-start.20 = (bf16[32,1024]{1,0:T(8,128)(2,1)S(1)}, bf16[32,1024]{1,0:T(8,128)(2,1)S(1)}, u32[]{:S(2)}, u32[]{:S(2)}) collective-permute-start(bf16[32,1024]{1,0:T(8,128)(2,1)S(1)} %get-tuple-element.53), channel_id=1, source_target_pairs={{0,4},{2,12},{4,0},{6,8},{8,6},{10,14},{12,2},{14,10},{16,20},{18,... | collective-permute-start | bytes 196616 | tf_op jit(solution)/shard_map/ppermute | solution.py:450
  53.4 0.5 collective-permute-start.21
  53.9 2.0 %collective-permute-done.18.refs_2_ = bf16[32,1024]{1,0:T(8,128)(2,1)S(1)} collective-permute-done((bf16[32,1024]{1,0:T(8,128)(2,1)S(1)}, bf16[32,1024]{1,0:T(8,128)(2,1)S(1)}, u32[]{:S(2)}, u32[]{:S(2)}) %collective-permute-start.18) | collective-permute-done | bytes 65568 | tf_op jit(solution)/shard_map/ppermute | solution.py:450
  55.9 2.6 %collective-permute-done.20.refs_4_ = bf16[32,1024]{1,0:T(8,128)(2,1)S(1)} collective-permute-done((bf16[32,1024]{1,0:T(8,128)(2,1)S(1)}, bf16[32,1024]{1,0:T(8,128)(2,1)S(1)}, u32[]{:S(2)}, u32[]{:S(2)}) %collective-permute-start.20) | collective-permute-done | bytes 65568 | tf_op jit(solution)/shard_map/ppermute | solution.py:450
  58.5 3.5 %collective-permute-done.21.refs_5_ = bf16[32,1024]{1,0:T(8,128)(2,1)S(1)} collective-permute-done((bf16[32,1024]{1,0:T(8,128)(2,1)S(1)}, bf16[32,1024]{1,0:T(8,128)(2,1)S(1)}, u32[]{:S(2)}, u32[]{:S(2)}) %collective-permute-start.21) | collective-permute-done | bytes 65568 | tf_op jit(solution)/shard_map/ppermute | solution.py:450
  62.0 0.1 shard_map.92
  62.1 0.6 collective-permute-start.22
  62.7 1.0 %collective-permute-done.22.received = bf16[32,2048]{1,0:T(8,128)(2,1)S(1)} collective-permute-done((bf16[32,2048]{1,0:T(8,128)(2,1)S(1)}, bf16[32,2048]{1,0:T(8,128)(2,1)S(1)}, u32[]{:S(2)}, u32[]{:S(2)}) %collective-permute-start.22) | collective-permute-done | bytes 131104 | tf_op jit(solution)/shard_map/ppermute | solution.py:206
  63.7 0.7 %shard_map.93 = bf16[1,32,4096]{2,1,0:T(8,128)(2,1)} custom-call(bf16[32,2048]{1,0:T(8,128)(2,1)S(1)} %get-tuple-element.55.keep, bf16[32,2048]{1,0:T(8,128)(2,1)S(1)} %collective-permute-done.22.received), custom_call_target="tpu_custom_call" | custom-call | bytes 524288 | tf_op jit(solution)/shard_map/pallas_call | solution.py:681
  (19 shorter events, 0.1 us)
Async XLA Ops:
  0.9 4.1 %collective-permute-start.2 = (bf16[16,2048]{1,0:T(8,128)(2,1)S(1)}, bf16[16,2048]{1,0:T(8,128)(2,1)S(1)}, u32[]{:S(2)}, u32[]{:S(2)}) collective-permute-start(bf16[16,2048]{1,0:T(8,128)(2,1)S(1)} %get-tuple-element.58.refs_0_), channel_id=1, source_target_pairs={{0,8},{4,12},{8,0},{12,4},{1,9},{5,13},{9,1},{13,5},{2,10},{6,14},... | collective-permute-start | bytes 196616 | tf_op jit(solution)/shard_map/ppermute | solution.py:206
  3.3 11.4 %copy-start.1 = (bf16[4096]{0:T(1024)(128)(2,1)S(1)}, bf16[4096]{0:T(1024)(128)(2,1)}, u32[]{:S(2)}) copy-start(bf16[4096]{0:T(1024)(128)(2,1)} %param.9) | copy-start | bytes 24580
  3.3 6.4 %collective-permute-start.3 = (bf16[16,2048]{1,0:T(8,128)(2,1)S(1)}, bf16[16,2048]{1,0:T(8,128)(2,1)S(1)}, u32[]{:S(2)}, u32[]{:S(2)}) collective-permute-start(bf16[16,2048]{1,0:T(8,128)(2,1)S(1)} %get-tuple-element.57.refs_1_), channel_id=1, source_target_pairs={{0,8},{4,12},{8,0},{12,4},{1,9},{5,13},{9,1},{13,5},{2,10},{6,14},... | collective-permute-start | bytes 196616 | tf_op jit(solution)/shard_map/ppermute | solution.py:206
  3.3 11.3 %collective-permute-start = (bf16[16,2048]{1,0:T(8,128)(2,1)S(1)}, bf16[16,2048]{1,0:T(8,128)(2,1)S(1)}, u32[]{:S(2)}, u32[]{:S(2)}) collective-permute-start(bf16[16,2048]{1,0:T(8,128)(2,1)S(1)} %get-tuple-element.58.refs_0_), channel_id=1, source_target_pairs={{0,4},{4,0},{8,12},{12,8},{1,5},{5,1},{9,13},{13,9},{2,6},{6,2},{1... | collective-permute-start | bytes 196616 | tf_op jit(solution)/shard_map/ppermute | solution.py:206
  4.6 10.0 %collective-permute-start.1 = (bf16[16,2048]{1,0:T(8,128)(2,1)S(1)}, bf16[16,2048]{1,0:T(8,128)(2,1)S(1)}, u32[]{:S(2)}, u32[]{:S(2)}) collective-permute-start(bf16[16,2048]{1,0:T(8,128)(2,1)S(1)} %get-tuple-element.57.refs_1_), channel_id=1, source_target_pairs={{0,4},{4,0},{8,12},{12,8},{1,5},{5,1},{9,13},{13,9},{2,6},{6,2},{1... | collective-permute-start | bytes 196616 | tf_op jit(solution)/shard_map/ppermute | solution.py:206
  5.0 9.7 %collective-permute-start.4 = (bf16[16,2048]{1,0:T(8,128)(2,1)S(1)}, bf16[16,2048]{1,0:T(8,128)(2,1)S(1)}, u32[]{:S(2)}, u32[]{:S(2)}) collective-permute-start(bf16[16,2048]{1,0:T(8,128)(2,1)S(1)} %collective-permute-done.2.refs_4_), channel_id=1, source_target_pairs={{0,4},{4,0},{8,12},{12,8},{1,5},{5,1},{9,13},{13,9},{2,6},{6,2},{1... | collective-permute-start | bytes 196616 | tf_op jit(solution)/shard_map/ppermute | solution.py:206
  9.7 5.0 %collective-permute-start.5 = (bf16[16,2048]{1,0:T(8,128)(2,1)S(1)}, bf16[16,2048]{1,0:T(8,128)(2,1)S(1)}, u32[]{:S(2)}, u32[]{:S(2)}) collective-permute-start(bf16[16,2048]{1,0:T(8,128)(2,1)S(1)} %collective-permute-done.3.refs_5_), channel_id=1, source_target_pairs={{0,4},{4,0},{8,12},{12,8},{1,5},{5,1},{9,13},{13,9},{2,6},{6,2},{1... | collective-permute-start | bytes 196616 | tf_op jit(solution)/shard_map/ppermute | solution.py:206
  15.8 9.0 %copy-start.2 = (s32[128]{0:T(128)S(1)}, s32[128]{0:T(128)}, u32[]{:S(2)}) copy-start(s32[128]{0:T(128)} %slots.3) | copy-start | bytes 1540
  15.8 9.0 %copy-start.3 = (s32[32]{0:T(128)S(1)}, s32[32]{0:T(128)}, u32[]{:S(2)}) copy-start(s32[32]{0:T(128)} %lengths.1) | copy-start | bytes 388
  15.8 2.5 %collective-permute-start.6 = (bf16[128,1408]{1,0:T(8,128)(2,1)S(1)}, bf16[128,1408]{1,0:T(8,128)(2,1)S(1)}, u32[]{:S(2)}, u32[]{:S(2)}) collective-permute-start(bf16[128,1408]{1,0:T(8,128)(2,1)S(1)} %get-tuple-element.38.given), channel_id=1, source_target_pairs={{0,1},{1,0},{2,3},{3,2},{4,5},{5,4},{6,7},{7,6},{8,9},{9,8},{10,11... | collective-permute-start | bytes 1081352 | tf_op jit(solution)/shard_map/ppermute | solution.py:206
  18.3 13.9 %collective-permute-start.7 = (bf16[32,1408]{1,0:T(8,128)(2,1)S(1)}, bf16[32,1408]{1,0:T(8,128)(2,1)S(1)}, u32[]{:S(2)}, u32[]{:S(2)}) collective-permute-start(bf16[32,1408]{1,0:T(8,128)(2,1)S(1)} %get-tuple-element.39), channel_id=1, source_target_pairs={{0,8},{2,0},{4,12},{6,4},{8,10},{10,2},{12,14},{14,6},{16,24},{18,... | collective-permute-start | bytes 270344 | tf_op jit(solution)/shard_map/ppermute | solution.py:450
  18.6 13.6 %collective-permute-start.8 = (bf16[32,1408]{1,0:T(8,128)(2,1)S(1)}, bf16[32,1408]{1,0:T(8,128)(2,1)S(1)}, u32[]{:S(2)}, u32[]{:S(2)}) collective-permute-start(bf16[32,1408]{1,0:T(8,128)(2,1)S(1)} %get-tuple-element.40), channel_id=1, source_target_pairs={{0,12},{2,4},{4,8},{6,0},{8,14},{10,6},{12,10},{14,2},{16,28},{18,... | collective-permute-start | bytes 270344 | tf_op jit(solution)/shard_map/ppermute | solution.py:450
  21.6 10.6 %collective-permute-start.9 = (bf16[32,1408]{1,0:T(8,128)(2,1)S(1)}, bf16[32,1408]{1,0:T(8,128)(2,1)S(1)}, u32[]{:S(2)}, u32[]{:S(2)}) collective-permute-start(bf16[32,1408]{1,0:T(8,128)(2,1)S(1)} %get-tuple-element.41), channel_id=1, source_target_pairs={{0,4},{2,12},{4,0},{6,8},{8,6},{10,14},{12,2},{14,10},{16,20},{18,... | collective-permute-start | bytes 270344 | tf_op jit(solution)/shard_map/ppermute | solution.py:450
  23.3 8.9 %collective-permute-start.10 = (bf16[32,1280]{1,0:T(8,128)(2,1)S(1)}, bf16[32,1280]{1,0:T(8,128)(2,1)S(1)}, u32[]{:S(2)}, u32[]{:S(2)}) collective-permute-start(bf16[32,1280]{1,0:T(8,128)(2,1)S(1)} %get-tuple-element.42.refs_4_), channel_id=1, source_target_pairs={{0,16},{2,8},{4,20},{6,12},{8,2},{10,26},{12,6},{14,30},{16,0},{18... | collective-permute-start | bytes 245768 | tf_op jit(solution)/shard_map/ppermute | solution.py:450
  33.9 4.1 %collective-permute-start.13 = (bf16[16,2048]{1,0:T(8,128)(2,1)S(1)}, bf16[16,2048]{1,0:T(8,128)(2,1)S(1)}, u32[]{:S(2)}, u32[]{:S(2)}) collective-permute-start(bf16[16,2048]{1,0:T(8,128)(2,1)S(1)} %get-tuple-element.45.refs_0_), channel_id=1, source_target_pairs={{0,8},{4,12},{8,0},{12,4},{1,9},{5,13},{9,1},{13,5},{2,10},{6,14},... | collective-permute-start | bytes 196616 | tf_op jit(solution)/shard_map/ppermute | solution.py:206
  34.0 5.0 %collective-permute-start.14 = (bf16[16,2048]{1,0:T(8,128)(2,1)S(1)}, bf16[16,2048]{1,0:T(8,128)(2,1)S(1)}, u32[]{:S(2)}, u32[]{:S(2)}) collective-permute-start(bf16[16,2048]{1,0:T(8,128)(2,1)S(1)} %get-tuple-element.46.attended.refs_1_), channel_id=1, source_target_pairs={{0,8},{4,12},{8,0},{12,4},{1,9},{5,13},{9,1},{13,5},{2,10},{6,14},... | collective-permute-start | bytes 196616 | tf_op jit(solution)/shard_map/ppermute | solution.py:206
  36.4 5.4 %collective-permute-start.11 = (bf16[16,2048]{1,0:T(8,128)(2,1)S(1)}, bf16[16,2048]{1,0:T(8,128)(2,1)S(1)}, u32[]{:S(2)}, u32[]{:S(2)}) collective-permute-start(bf16[16,2048]{1,0:T(8,128)(2,1)S(1)} %get-tuple-element.45.refs_0_), channel_id=1, source_target_pairs={{0,4},{4,0},{8,12},{12,8},{1,5},{5,1},{9,13},{13,9},{2,6},{6,2},{1... | collective-permute-start | bytes 196616 | tf_op jit(solution)/shard_map/ppermute | solution.py:206
  36.4 5.4 %collective-permute-start.12 = (bf16[16,2048]{1,0:T(8,128)(2,1)S(1)}, bf16[16,2048]{1,0:T(8,128)(2,1)S(1)}, u32[]{:S(2)}, u32[]{:S(2)}) collective-permute-start(bf16[16,2048]{1,0:T(8,128)(2,1)S(1)} %get-tuple-element.46.attended.refs_1_), channel_id=1, source_target_pairs={{0,4},{4,0},{8,12},{12,8},{1,5},{5,1},{9,13},{13,9},{2,6},{6,2},{1... | collective-permute-start | bytes 196616 | tf_op jit(solution)/shard_map/ppermute | solution.py:206
  38.0 5.2 %collective-permute-start.15 = (bf16[16,2048]{1,0:T(8,128)(2,1)S(1)}, bf16[16,2048]{1,0:T(8,128)(2,1)S(1)}, u32[]{:S(2)}, u32[]{:S(2)}) collective-permute-start(bf16[16,2048]{1,0:T(8,128)(2,1)S(1)} %collective-permute-done.13.refs_4_), channel_id=1, source_target_pairs={{0,4},{4,0},{8,12},{12,8},{1,5},{5,1},{9,13},{13,9},{2,6},{6,2},{1... | collective-permute-start | bytes 196616 | tf_op jit(solution)/shard_map/ppermute | solution.py:206
  39.0 5.6 %collective-permute-start.16 = (bf16[16,2048]{1,0:T(8,128)(2,1)S(1)}, bf16[16,2048]{1,0:T(8,128)(2,1)S(1)}, u32[]{:S(2)}, u32[]{:S(2)}) collective-permute-start(bf16[16,2048]{1,0:T(8,128)(2,1)S(1)} %collective-permute-done.14.refs_5_), channel_id=1, source_target_pairs={{0,4},{4,0},{8,12},{12,8},{1,5},{5,1},{9,13},{13,9},{2,6},{6,2},{1... | collective-permute-start | bytes 196616 | tf_op jit(solution)/shard_map/ppermute | solution.py:206
  45.5 16.5 %copy-start = (bf16[32,4096]{1,0:T(8,128)(2,1)S(1)}, bf16[32,4096]{1,0:T(8,128)(2,1)}, u32[]{:S(2)}) copy-start(bf16[32,4096]{1,0:T(8,128)(2,1)} %hidden.1) | copy-start | bytes 786436
  45.5 3.3 %collective-permute-start.17 = (bf16[128,1024]{1,0:T(8,128)(2,1)S(1)}, bf16[128,1024]{1,0:T(8,128)(2,1)S(1)}, u32[]{:S(2)}, u32[]{:S(2)}) collective-permute-start(bf16[128,1024]{1,0:T(8,128)(2,1)S(1)} %get-tuple-element.50.given), channel_id=1, source_target_pairs={{0,1},{1,0},{2,3},{3,2},{4,5},{5,4},{6,7},{7,6},{8,9},{9,8},{10,11... | collective-permute-start | bytes 786440 | tf_op jit(solution)/shard_map/ppermute | solution.py:206
  48.9 7.0 %collective-permute-start.18 = (bf16[32,1024]{1,0:T(8,128)(2,1)S(1)}, bf16[32,1024]{1,0:T(8,128)(2,1)S(1)}, u32[]{:S(2)}, u32[]{:S(2)}) collective-permute-start(bf16[32,1024]{1,0:T(8,128)(2,1)S(1)} %get-tuple-element.51), channel_id=1, source_target_pairs={{0,8},{2,0},{4,12},{6,4},{8,10},{10,2},{12,14},{14,6},{16,24},{18,... | collective-permute-start | bytes 196616 | tf_op jit(solution)/shard_map/ppermute | solution.py:450
  49.0 6.9 %collective-permute-start.19 = (bf16[32,1024]{1,0:T(8,128)(2,1)S(1)}, bf16[32,1024]{1,0:T(8,128)(2,1)S(1)}, u32[]{:S(2)}, u32[]{:S(2)}) collective-permute-start(bf16[32,1024]{1,0:T(8,128)(2,1)S(1)} %get-tuple-element.52), channel_id=1, source_target_pairs={{0,12},{2,4},{4,8},{6,0},{8,14},{10,6},{12,10},{14,2},{16,28},{18,... | collective-permute-start | bytes 196616 | tf_op jit(solution)/shard_map/ppermute | solution.py:450
  52.5 5.9 %collective-permute-start.20 = (bf16[32,1024]{1,0:T(8,128)(2,1)S(1)}, bf16[32,1024]{1,0:T(8,128)(2,1)S(1)}, u32[]{:S(2)}, u32[]{:S(2)}) collective-permute-start(bf16[32,1024]{1,0:T(8,128)(2,1)S(1)} %get-tuple-element.53), channel_id=1, source_target_pairs={{0,4},{2,12},{4,0},{6,8},{8,6},{10,14},{12,2},{14,10},{16,20},{18,... | collective-permute-start | bytes 196616 | tf_op jit(solution)/shard_map/ppermute | solution.py:450
  53.4 8.6 %collective-permute-start.21 = (bf16[32,1024]{1,0:T(8,128)(2,1)S(1)}, bf16[32,1024]{1,0:T(8,128)(2,1)S(1)}, u32[]{:S(2)}, u32[]{:S(2)}) collective-permute-start(bf16[32,1024]{1,0:T(8,128)(2,1)S(1)} %get-tuple-element.54.refs_6_), channel_id=1, source_target_pairs={{0,16},{2,8},{4,20},{6,12},{8,2},{10,26},{12,6},{14,30},{16,0},{18... | collective-permute-start | bytes 196616 | tf_op jit(solution)/shard_map/ppermute | solution.py:450
  62.1 1.6 %collective-permute-start.22 = (bf16[32,2048]{1,0:T(8,128)(2,1)S(1)}, bf16[32,2048]{1,0:T(8,128)(2,1)S(1)}, u32[]{:S(2)}, u32[]{:S(2)}) collective-permute-start(bf16[32,2048]{1,0:T(8,128)(2,1)S(1)} %get-tuple-element.56), channel_id=1, source_target_pairs={{0,1},{1,0},{2,3},{3,2},{4,5},{5,4},{6,7},{7,6},{8,9},{9,8},{10,11... | collective-permute-start | bytes 393224 | tf_op jit(solution)/shard_map/ppermute | solution.py:206

commit v15 on v12

--- a/solution.py
+++ b/solution.py
@@ -222,9 +222,12 @@
 
 
 def position():
-    col = lax.axis_index("col")
+    return lax.axis_index("side"), lax.axis_index("col")
+
+
+def run_base():
     pairs = lax.axis_size("col") // lax.axis_size("row")
-    return lax.axis_index("side"), col, lax.axis_index("row") * pairs + lax.rem(col, pairs)
+    return lax.div(lax.axis_index("col"), pairs) ^ lax.axis_index("row")
 
 
 def rows_copy(weight, target, half):
@@ -235,7 +238,7 @@
 
 
 def stage_in_kernel(blocks, weight, slots, give_part, own_part, chosen, scratch, slot_part, sems):
-    side, col, run = position()
+    side, col = position()
     slots_copy, *copies = started(
         [
             (slots, slot_part),
@@ -245,7 +248,7 @@
         sems,
     )
     slots_copy.wait()
-    chosen[...] = one_hot(slot_part, scratch, blocks, run, col).astype(jnp.bfloat16)
+    chosen[...] = one_hot(slot_part, scratch, blocks, col, col).astype(jnp.bfloat16)
     for copy in copies:
         copy.wait()
 
@@ -267,7 +270,7 @@
 
 def stage_rest_kernel(blocks, lengths, weight, keys, values, slots, *refs):
     target, key_part, value_part, cosine, sine, length_of, chosen, scratch, sems = refs
-    side, col, run = position()
+    side, col = position()
     copies = []
     for j in range(key_part.shape[2] // HEAD_DIM):
         lane = pl.multiple_of((2 * j + side) * HEAD_DIM, HEAD_DIM)
@@ -280,7 +283,7 @@
             )
     copies = started(copies + head_copies(weight, target, 1 - side), sems)
     cosine[...], sine[...], length_of[...] = rope(lengths, cosine.shape[0])
-    chosen[...] = one_hot(slots, scratch, blocks, col, run).T.astype(jnp.bfloat16)
+    chosen[...] = one_hot(slots, scratch, blocks, col, col).T.astype(jnp.bfloat16)
     for copy in copies:
         copy.wait()
 
@@ -352,38 +355,24 @@
     dot_columns(order, weight, give)
 
 
-def carries(entry):
-    return entry > 0
-
-
-def sums_entry(run, pairs):
-    return run * pairs + (pairs - 1 if run == 0 else 0)
-
-
-def arrival_order(count, pairs):
-    return sorted(range(count), key=lambda i: (i == 0, i % pairs, -i))
-
-
-def merge_kernel(own, given, received, *outs):
+def merge_kernel(count, own, given, received, *outs):
     rows = outs[0].shape[0]
     half = own.shape[1]
     more = given.shape[1] - half
-    for i, out in enumerate(outs):
+    for i, out in enumerate(outs[:count]):
         part = slice(i * rows, (i + 1) * rows)
         total = own[part, :] + received[part, :half].astype(jnp.float32)
-        out[:, :half] = total.astype(jnp.bfloat16)
-        if out.shape[1] > half:
-            out[:, half:] = jnp.concatenate(
-                [given[part, half : half + more // 2], received[part, half : half + more // 2]],
-                axis=1,
-            )
+        out[...] = total.astype(jnp.bfloat16)
+    for out in outs[count:]:
+        lanes = slice(half, half + more // 2)
+        out[...] = jnp.concatenate([given[:rows, lanes], received[:rows, lanes]], axis=1)
 
 
 def own_kernel(permuted, weight, own):
     dot_columns(permuted[...], weight, own)
 
 
-def project(kernel, chosen, pieces_in, extra, weights, more, pairs):
+def project(kernel, chosen, pieces_in, extra, weights, more):
     count = lax.axis_size("col")
     parts = len(pieces_in)
     rows, depth = pieces_in[0].shape
@@ -407,16 +396,18 @@
         flops,
         depth * half * 2,
     )(permuted, in_vmem(weights[1]))
-    return call(
-        merge_kernel,
-        [
-            struct((rows // count, half + (more if carries(i) else 0))) for i in range(count)
-        ],
+    outs = [struct((rows // count, half))] * count
+    if more:
+        outs = outs + [struct((rows // count, more))]
+    merged = call(
+        functools.partial(merge_kernel, count),
+        outs,
         [VMEM] * 3,
-        [VMEM] * count,
+        [VMEM] * len(outs),
         rows * half,
         rows * half * 8,
     )(own, give, received)
+    return merged[:count], merged[count:]
 
 
 def gathered(parts, axis):
@@ -431,29 +422,54 @@
     return [part for i in sorted(blocks) for part in blocks[i]]
 
 
-def in_place(blocks, pairs):
-    return [blocks[arrival_order(len(blocks), pairs).index(i)] for i in range(len(blocks))]
-
-
-def spread(products):
+def choose_kernel(count, other, *refs):
+    blocks, sums, out = refs[:count], refs[count:-1], refs[-1]
+    width = blocks[0].shape[1]
+    wanted = run_base() ^ other
+    chosen = blocks[0][...]
+    for run, block in enumerate(blocks[1:], 1):
+        chosen = jnp.where(wanted == run, block[...], chosen)
+    out[:, :width] = chosen
+    for ref in sums:
+        out[:, width:] = ref[...]
+
+
+def spread(products, sums):
     col_count, row_count = lax.axis_size("col"), lax.axis_size("row")
     pairs = col_count // row_count
-    sent = {
-        j: lax.ppermute(
-            products[j],
-            ("col", "row"),
-            [
-                (
-                    col * row_count + row,
-                    ((row * pairs + col % pairs) ^ j) * row_count + col // pairs,
-                )
-                for col in range(col_count)
-                for row in range(row_count)
-            ],
-        )
-        for j in range(col_count)
-    }
-    return [sent[j] for j in arrival_order(col_count, pairs)]
+    blocks = {0: products[0]}
+    for mask in [*range(pairs, col_count), *range(1, pairs)]:
+        blocks[mask] = moved(products[mask], "col", mask)
+    arrived = []
+    for pair in range(pairs):
+        runs = [blocks[run * pairs + pair] for run in range(row_count)]
+        beside = sums if pair == 0 else []
+        width = sum(part.shape[1] for part in [runs[0], *beside])
+        for mask in range(1, row_count):
+            chosen = call(
+                functools.partial(choose_kernel, row_count, mask),
+                struct((runs[0].shape[0], width)),
+                [VMEM] * (row_count + len(beside)),
+                VMEM,
+                0,
+                width * runs[0].shape[0] * 4,
+            )(*runs, *beside)
+            arrived.append(moved(chosen, "row", mask))
+    return [blocks[i] for i in range(col_count)] + arrived
+
+
+def total_of(blocks, arrived, pair):
+    others = lax.axis_size("row") - 1
+    pairs = len(blocks) // (others + 1)
+    rows, width = blocks[0].shape
+    base = run_base()
+    kept = blocks[pair][...]
+    for run in range(1, others + 1):
+        kept = jnp.where(base == run, blocks[run * pairs + pair][...], kept)
+    total = kept.astype(jnp.float32)
+    for ref in arrived[pair * others : (pair + 1) * others]:
+        total = total + ref[:, :width].astype(jnp.float32)
+    return total
 
 
 def rotated(vector, cosine, sine):
@@ -474,17 +490,18 @@
 
 
 def attend_all(count, parts, cosine, sine, lengths, *refs):
-    blocks, (keys, values), refs = refs[:count], refs[count : count + 2], refs[count + 2 :]
-    blocks = in_place(blocks, keys.shape[2] // HEAD_DIM)
+    others = lax.axis_size("row") - 1
+    pairs = count // (others + 1)
+    blocks, refs = refs[:count], refs[count:]
+    arrived, refs = refs[: pairs * others], refs[pairs * others :]
+    (sums, keys, values), refs = refs[:3], refs[3:]
     outs, (scores_of, probs_of) = refs[:parts], refs[parts:]
-    pairs = keys.shape[2] // HEAD_DIM
     rows, cache = keys.shape[:2]
     low = lax.rem(lax.axis_index("col"), pairs)
     width = GROUP_WIDTH
-    squares = sum(
-        blocks[sums_entry(run, pairs)][:, width:].astype(jnp.float32)
-        for run in range(count // pairs)
-    )
+    squares = sums[...].astype(jnp.float32)
+    for ref in arrived[:others]:
+        squares = squares + ref[:, width:].astype(jnp.float32)
     scale = lax.rsqrt(jnp.sum(squares, axis=1, keepdims=True) / D + EPSILON)
     factor = HEAD_DIM ** (-0.5)
     cosines, sines, length_of = cosine[...], sine[...], lengths[:, :1]
@@ -495,9 +512,7 @@
     filled = [(position >= 0) & (position < length_of[part]) for part in runs]
     own, new_values, own_probs = [], [], []
     for pair in range(pairs):
-        total = blocks[pair][:, :width].astype(jnp.float32)
-        for i in range(pair + pairs, count, pairs):
-            total = total + blocks[i][:, :width].astype(jnp.float32)
+        total = total_of(blocks, arrived, pair)
         total = (total * scale).astype(jnp.bfloat16).astype(jnp.float32)
         heads = [total[:, h * HEAD_DIM : (h + 1) * HEAD_DIM] for h in range(GROUP + 2)]
         queries = [
@@ -552,17 +567,15 @@
 
 
 def sum_kernel(count, parts, hidden, *refs):
-    attended, blocks, (keep, send) = refs[:parts], refs[parts : parts + count], refs[parts + count :]
+    attended, blocks, arrived = refs[:parts], refs[parts : parts + count], refs[parts + count : -2]
+    keep, send = refs[-2:]
     rows, width = blocks[0].shape
     pairs = keep.shape[1] // width
-    blocks = in_place(blocks, pairs)
     side = lax.axis_index("side")
     low = lax.rem(lax.axis_index("col"), pairs)
     for pair in range(pairs):
         column = low ^ pair
-        total = blocks[pair][...].astype(jnp.float32)
-        for i in range(pair + pairs, count, pairs):
-            total = total + blocks[i][...].astype(jnp.float32)
+        total = total_of(blocks, arrived, pair)
         at = pl.ds(pl.multiple_of((2 * column + side) * width, width), width)
         hidden_out = (hidden[:, at].astype(jnp.float32) + total).astype(jnp.bfloat16)
         at = pl.ds(pl.multiple_of(column * width, width), width)
@@ -616,9 +629,8 @@
     blocks = gathered(
         [own_part[i * piece : (i + 1) * piece] for i in range(parts)], "col"
     )
-    products = spread(
-        project(in_kernel, chosen_in, blocks, [gain], [give_in, own_in], HEAD_DIM, pairs)
-    )
+    products, sums = project(in_kernel, chosen_in, blocks, [gain], [give_in, own_in], HEAD_DIM)
+    products = spread(products, sums)
 
     table = struct((rows, HEAD_DIM), jnp.float32)
     give_out, key_part, value_part, *tables, chosen_out = call(
@@ -636,12 +648,12 @@
     attended = call(
         functools.partial(attend_all, col_count, parts),
         [struct((piece, half))] * parts,
-        [VMEM] * (col_count + 5),
+        [VMEM] * (len(products) + 6),
         [VMEM] * parts,
         4 * rows * half * cache,
         0,
         [pltpu.VMEM(runs, jnp.float32), pltpu.VMEM(runs, jnp.bfloat16)],
-    )(*tables, *products, in_vmem(key_part), in_vmem(value_part))
+    )(*tables, *products, *sums, in_vmem(key_part), in_vmem(value_part))
 
     own_out = call(
         stage_out_kernel,
@@ -652,15 +664,14 @@
         half * half_out * 2,
         [pltpu.SemaphoreType.DMA((pairs,))],
     )(in_hbm(out_weight), attended[-1])
-    products = spread(
-        project(
-            out_kernel, chosen_out, gathered(attended, "col"), [], [give_out, own_out], 0, pairs
-        )
-    )
+    products, _ = project(
+        out_kernel, chosen_out, gathered(attended, "col"), [], [give_out, own_out], 0
+    )
+    products = spread(products, [])
     keep, send = call(
         functools.partial(sum_kernel, col_count, parts),
         [struct((rows, half)), struct((rows, half))],
-        [VMEM] * (1 + parts + col_count),
+        [VMEM] * (1 + parts + len(products)),
         [VMEM, VMEM],
         rows * depth * 4,
         rows * depth * 8,

time: 65.9 us -> 69.1 us (1.049)
  the two profiles are of different devices: /device:TPU:3 before, /device:TPU:0 now
where the time goes in v15:
time: 69.1 us; the launch traced here: 68.9 us
  starting transfers between devices  28.7 us (42%)
  waiting for transfers between devices  22.8 us (33%)
  Pallas kernels  16.3 us (24%)
  local copies, waits for them, and re-layouts  0.9 us (1%)
    ppermute x25, starting transfers between devices, moved(): return lax.ppermute(value, axis, pairs)  28.7 us
    ppermute x25, waiting for transfers between devices, moved(): return lax.ppermute(value, axis, pairs)  22.8 us
    pallas_call x1, Pallas kernels, paired_plan(): call(functools.partial(stage_in_kernel, col_count), [pltpu.VMEM((half, ha...  4.09 us
    pallas_call x1, Pallas kernels, paired_plan(): call(functools.partial(stage_rest_kernel, col_count), [pltpu.VMEM((half,...  3.71 us
    pallas_call x1, Pallas kernels, paired_plan(): call(stage_out_kernel, pltpu.VMEM((half, half_out), jnp.bfloat16), [HBM,...  2.24 us
    pallas_call x2, Pallas kernels, project(): call(functools.partial(kernel, parts), [struct((rows, half + more)), stru...  1.91 us
    pallas_call x1, Pallas kernels, paired_plan(): call(functools.partial(attend_all, col_count, parts), [struct((piece, hal...  1.71 us
    pallas_call x2, Pallas kernels, project(): call(own_kernel, struct((rows, half), jnp.float32), [VMEM, VMEM], VMEM, f...  1.58 us
  transfers between devices with their start and end apart: 25, of which 15 were waited for; matrix products, arithmetic and copies ran while one was open for 0% of the time, Pallas kernels for 17%

profile of v15, /device:TPU:0, one launch (start us, length us, event | category | flops | bytes accessed | tf_op | source)
XLA Modules:
  0.0 68.9 jit_solution(4359981406010479183)
XLA Ops:
  0.0 0.9 %fusion = (bf16[16,2048]{1,0:T(8,128)(2,1)S(1)}, bf16[16,2048]{1,0:T(8,128)(2,1)S(1)}) fusion(bf16[32,4096]{1,0:T(8,128)(2,1)} %hidden.1, s32[]{:T(128)S(6)} %add.4, s32[]{:T(128)S(6)} %select_n.3), kind=kLoop, calls=%fused_computation.1 | loop fusion | bytes 262152 | tf_op jit(solution)/shard_map/slice | solution.py:630
  0.9 4.1 %collective-permute-start.2 = (bf16[16,2048]{1,0:T(8,128)(2,1)S(1)}, bf16[16,2048]{1,0:T(8,128)(2,1)S(1)}, u32[]{:S(2)}, u32[]{:S(2)}) collective-permute-start(bf16[16,2048]{1,0:T(8,128)(2,1)S(1)} %get-tuple-element.60.refs_0_), channel_id=1, source_target_pairs={{0,8},{4,12},{8,0},{12,4},{1,9},{5,13},{9,1},{13,5},{2,10},{6,14},... | collective-permute-start | bytes 196616 | tf_op jit(solution)/shard_map/ppermute | solution.py:206
  5.0 0.1 collective-permute-start.3
  5.1 1.8 %collective-permute-start = (bf16[16,2048]{1,0:T(8,128)(2,1)S(1)}, bf16[16,2048]{1,0:T(8,128)(2,1)S(1)}, u32[]{:S(2)}, u32[]{:S(2)}) collective-permute-start(bf16[16,2048]{1,0:T(8,128)(2,1)S(1)} %get-tuple-element.60.refs_0_), channel_id=1, source_target_pairs={{0,4},{4,0},{8,12},{12,8},{1,5},{5,1},{9,13},{13,9},{2,6},{6,2},{1... | collective-permute-start | bytes 196616 | tf_op jit(solution)/shard_map/ppermute | solution.py:206
  6.9 0.2 collective-permute-start.1
  7.1 1.6 %collective-permute-done.2.refs_4_ = bf16[16,2048]{1,0:T(8,128)(2,1)S(1)} collective-permute-done((bf16[16,2048]{1,0:T(8,128)(2,1)S(1)}, bf16[16,2048]{1,0:T(8,128)(2,1)S(1)}, u32[]{:S(2)}, u32[]{:S(2)}) %collective-permute-start.2) | collective-permute-done | bytes 65568 | tf_op jit(solution)/shard_map/ppermute | solution.py:206
  8.7 1.9 %collective-permute-start.4 = (bf16[16,2048]{1,0:T(8,128)(2,1)S(1)}, bf16[16,2048]{1,0:T(8,128)(2,1)S(1)}, u32[]{:S(2)}, u32[]{:S(2)}) collective-permute-start(bf16[16,2048]{1,0:T(8,128)(2,1)S(1)} %collective-permute-done.2.refs_4_), channel_id=1, source_target_pairs={{0,4},{4,0},{8,12},{12,8},{1,5},{5,1},{9,13},{13,9},{2,6},{6,2},{1... | collective-permute-start | bytes 196616 | tf_op jit(solution)/shard_map/ppermute | solution.py:206
  10.6 0.4 collective-permute-done.3.refs_5_
  11.1 1.3 %collective-permute-start.5 = (bf16[16,2048]{1,0:T(8,128)(2,1)S(1)}, bf16[16,2048]{1,0:T(8,128)(2,1)S(1)}, u32[]{:S(2)}, u32[]{:S(2)}) collective-permute-start(bf16[16,2048]{1,0:T(8,128)(2,1)S(1)} %collective-permute-done.3.refs_5_), channel_id=1, source_target_pairs={{0,4},{4,0},{8,12},{12,8},{1,5},{5,1},{9,13},{13,9},{2,6},{6,2},{1... | collective-permute-start | bytes 196616 | tf_op jit(solution)/shard_map/ppermute | solution.py:206
  12.4 4.1 %shard_map.83 = (bf16[2048,1280]{1,0:T(8,128)(2,1)S(1)}, bf16[2048,1280]{1,0:T(8,128)(2,1)S(1)}, bf16[128,128]{1,0:T(8,128)(2,1)S(1)}) custom-call(bf16[4096,2560]{1,0:T(8,128)(2,1)} %weight.4, s32[128]{0:T(128)} %slots.3), custom_call_target="tpu_custom_call" | custom-call | bytes 10485760 | tf_op jit(solution)/shard_map/pallas_call | solution.py:616
  16.5 1.1 %shard_map.84 = (bf16[128,1408]{1,0:T(8,128)(2,1)S(1)}, bf16[128,2048]{1,0:T(8,128)(2,1)S(1)}) custom-call(bf16[128,128]{1,0:T(8,128)(2,1)S(1)} %get-tuple-element.35.chosen, bf16[16,2048]{1,0:T(8,128)(2,1)S(1)} %get-tuple-element.60.refs_0_, bf16[16,2048]{1,0:T(8,128)(2,1)S(1)} %get-tuple-element.59.refs_1_, ...), custom_call_target="tpu_custom_call" | custom-call | flops 671088640 | bytes 5242880 | tf_op jit(solution)/shard_map/pallas_call | solution.py:382
  17.7 0.9 %shard_map.85.own = f32[128,1280]{1,0:T(8,128)S(1)} custom-call(bf16[128,2048]{1,0:T(8,128)(2,1)S(1)} %get-tuple-element.38.permuted, bf16[2048,1280]{1,0:T(8,128)(2,1)S(1)} %get-tuple-element.36.refs_8_.weight), custom_call_target="tpu_custom_call" | custom-call | flops 671088640 | bytes 5242880 | tf_op jit(solution)/shard_map/pallas_call | solution.py:391
  18.6 0.8 %collective-permute-done.6.received = bf16[128,1408]{1,0:T(8,128)(2,1)S(1)} collective-permute-done((bf16[128,1408]{1,0:T(8,128)(2,1)S(1)}, bf16[128,1408]{1,0:T(8,128)(2,1)S(1)}, u32[]{:S(2)}, u32[]{:S(2)}) %collective-permute-start.6) | collective-permute-done | bytes 360480 | tf_op jit(solution)/shard_map/ppermute | solution.py:206
  19.4 0.1 shard_map.86
  19.5 3.2 %collective-permute-start.8 = (bf16[32,1280]{1,0:T(8,128)(2,1)S(1)}, bf16[32,1280]{1,0:T(8,128)(2,1)S(1)}, u32[]{:S(2)}, u32[]{:S(2)}) collective-permute-start(bf16[32,1280]{1,0:T(8,128)(2,1)S(1)} %get-tuple-element.42), channel_id=1, source_target_pairs={{0,8},{4,12},{8,0},{12,4},{1,9},{5,13},{9,1},{13,5},{2,10},{6,14},... | collective-permute-start | bytes 245768 | tf_op jit(solution)/shard_map/ppermute | solution.py:206
  22.6 0.7 %collective-permute-start.7 = (bf16[32,1280]{1,0:T(8,128)(2,1)S(1)}, bf16[32,1280]{1,0:T(8,128)(2,1)S(1)}, u32[]{:S(2)}, u32[]{:S(2)}) collective-permute-start(bf16[32,1280]{1,0:T(8,128)(2,1)S(1)} %get-tuple-element.41), channel_id=1, source_target_pairs={{0,4},{4,0},{8,12},{12,8},{1,5},{5,1},{9,13},{13,9},{2,6},{6,2},{1... | collective-permute-start | bytes 245768 | tf_op jit(solution)/shard_map/ppermute | solution.py:206
  23.4 0.8 %collective-permute-start.9 = (bf16[32,1280]{1,0:T(8,128)(2,1)S(1)}, bf16[32,1280]{1,0:T(8,128)(2,1)S(1)}, u32[]{:S(2)}, u32[]{:S(2)}) collective-permute-start(bf16[32,1280]{1,0:T(8,128)(2,1)S(1)} %get-tuple-element.43), channel_id=1, source_target_pairs={{0,12},{4,8},{8,4},{12,0},{1,13},{5,9},{9,5},{13,1},{2,14},{6,10},... | collective-permute-start | bytes 245768 | tf_op jit(solution)/shard_map/ppermute | solution.py:206
  24.2 3.2 %collective-permute-done.8.refs_1_.refs_2_ = bf16[32,1280]{1,0:T(8,128)(2,1)S(1)} collective-permute-done((bf16[32,1280]{1,0:T(8,128)(2,1)S(1)}, bf16[32,1280]{1,0:T(8,128)(2,1)S(1)}, u32[]{:S(2)}, u32[]{:S(2)}) %collective-permute-start.8) | collective-permute-done | bytes 81952 | tf_op jit(solution)/shard_map/ppermute | solution.py:206
  27.4 1.6 %collective-permute-start.10 = (bf16[32,1408]{1,0:T(8,128)(2,1)S(1)}, bf16[32,1408]{1,0:T(8,128)(2,1)S(1)}, u32[]{:S(2)}, u32[]{:S(2)}) collective-permute-start(bf16[32,1408]{1,0:T(8,128)(2,1)S(1)} %shard_map.87), channel_id=1, source_target_pairs={{0,2},{2,0},{1,3},{3,1},{4,6},{6,4},{5,7},{7,5},{8,10},{10,8},{9,1... | collective-permute-start | bytes 270344 | tf_op jit(solution)/shard_map/ppermute | solution.py:206
  29.0 1.1 %collective-permute-done.7.refs_0_.refs_1_ = bf16[32,1280]{1,0:T(8,128)(2,1)S(1)} collective-permute-done((bf16[32,1280]{1,0:T(8,128)(2,1)S(1)}, bf16[32,1280]{1,0:T(8,128)(2,1)S(1)}, u32[]{:S(2)}, u32[]{:S(2)}) %collective-permute-start.7) | collective-permute-done | bytes 81952 | tf_op jit(solution)/shard_map/ppermute | solution.py:206
  30.1 1.5 %collective-permute-start.11 = (bf16[32,1280]{1,0:T(8,128)(2,1)S(1)}, bf16[32,1280]{1,0:T(8,128)(2,1)S(1)}, u32[]{:S(2)}, u32[]{:S(2)}) collective-permute-start(bf16[32,1280]{1,0:T(8,128)(2,1)S(1)} %shard_map.88), channel_id=1, source_target_pairs={{0,2},{2,0},{1,3},{3,1},{4,6},{6,4},{5,7},{7,5},{8,10},{10,8},{9,1... | collective-permute-start | bytes 245768 | tf_op jit(solution)/shard_map/ppermute | solution.py:206
  31.6 3.7 %shard_map.82 = (bf16[2048,1024]{1,0:T(8,128)(2,1)S(1)}, bf16[32,64,256]{2,1,0:T(8,128)(2,1)S(1)}, bf16[32,64,256]{2,1,0:T(8,128)(2,1)S(1)}, f32[32,128]{1,0:T(8...) custom-call(s32[32]{0:T(128)S(1)} %copy-done.3, bf16[4096,2048]{1,0:T(8,128)(2,1)} %weight.5, ...), custom_call_target="tpu_custom_call" | custom-call | bytes 6291456 | tf_op jit(solution)/shard_map/pallas_call | solution.py:636
  35.4 1.7 %shard_map.89 = (bf16[16,2048]{1,0:T(8,128)(2,1)S(1)}, bf16[16,2048]{1,0:T(8,128)(2,1)S(1)}) custom-call(f32[32,128]{1,0:T(8,128)S(1)} %get-tuple-element.32.cosine, f32[32,128]{1,0:T(8,128)S(1)} %get-tuple-element.33.sine, s32[32,128]{1,0:T(8,128)S(1)} %get-tuple-element.34.lengths, bf16[32,1280]{1,0:T(8,128)(2,1)S(1)} %get-tuple-element.40.refs_0_, ...), custom_call_target="tpu_custom_call" | custom-call | flops 16777216 | tf_op jit(solution)/shard_map/pallas_call | solution.py:648
  37.1 2.5 %collective-permute-start.14 = (bf16[16,2048]{1,0:T(8,128)(2,1)S(1)}, bf16[16,2048]{1,0:T(8,128)(2,1)S(1)}, u32[]{:S(2)}, u32[]{:S(2)}) collective-permute-start(bf16[16,2048]{1,0:T(8,128)(2,1)S(1)} %get-tuple-element.47.refs_0_), channel_id=1, source_target_pairs={{0,8},{4,12},{8,0},{12,4},{1,9},{5,13},{9,1},{13,5},{2,10},{6,14},... | collective-permute-start | bytes 196616 | tf_op jit(solution)/shard_map/ppermute | solution.py:206
  39.6 0.4 collective-permute-start.15
  40.1 1.2 %collective-permute-start.12 = (bf16[16,2048]{1,0:T(8,128)(2,1)S(1)}, bf16[16,2048]{1,0:T(8,128)(2,1)S(1)}, u32[]{:S(2)}, u32[]{:S(2)}) collective-permute-start(bf16[16,2048]{1,0:T(8,128)(2,1)S(1)} %get-tuple-element.47.refs_0_), channel_id=1, source_target_pairs={{0,4},{4,0},{8,12},{12,8},{1,5},{5,1},{9,13},{13,9},{2,6},{6,2},{1... | collective-permute-start | bytes 196616 | tf_op jit(solution)/shard_map/ppermute | solution.py:206
  41.2 0.9 %collective-permute-start.13 = (bf16[16,2048]{1,0:T(8,128)(2,1)S(1)}, bf16[16,2048]{1,0:T(8,128)(2,1)S(1)}, u32[]{:S(2)}, u32[]{:S(2)}) collective-permute-start(bf16[16,2048]{1,0:T(8,128)(2,1)S(1)} %get-tuple-element.48.attended.refs_1_), channel_id=1, source_target_pairs={{0,4},{4,0},{8,12},{12,8},{1,5},{5,1},{9,13},{13,9},{2,6},{6,2},{1... | collective-permute-start | bytes 196616 | tf_op jit(solution)/shard_map/ppermute | solution.py:206
  42.1 2.2 %collective-permute-done.14.refs_4_ = bf16[16,2048]{1,0:T(8,128)(2,1)S(1)} collective-permute-done((bf16[16,2048]{1,0:T(8,128)(2,1)S(1)}, bf16[16,2048]{1,0:T(8,128)(2,1)S(1)}, u32[]{:S(2)}, u32[]{:S(2)}) %collective-permute-start.14) | collective-permute-done | bytes 65568 | tf_op jit(solution)/shard_map/ppermute | solution.py:206
  44.3 1.2 %collective-permute-done.15.refs_5_ = bf16[16,2048]{1,0:T(8,128)(2,1)S(1)} collective-permute-done((bf16[16,2048]{1,0:T(8,128)(2,1)S(1)}, bf16[16,2048]{1,0:T(8,128)(2,1)S(1)}, u32[]{:S(2)}, u32[]{:S(2)}) %collective-permute-start.15) | collective-permute-done | bytes 65568 | tf_op jit(solution)/shard_map/ppermute | solution.py:206
  45.5 1.2 %collective-permute-start.17 = (bf16[16,2048]{1,0:T(8,128)(2,1)S(1)}, bf16[16,2048]{1,0:T(8,128)(2,1)S(1)}, u32[]{:S(2)}, u32[]{:S(2)}) collective-permute-start(bf16[16,2048]{1,0:T(8,128)(2,1)S(1)} %collective-permute-done.15.refs_5_), channel_id=1, source_target_pairs={{0,4},{4,0},{8,12},{12,8},{1,5},{5,1},{9,13},{13,9},{2,6},{6,2},{1... | collective-permute-start | bytes 196616 | tf_op jit(solution)/shard_map/ppermute | solution.py:206
  46.7 2.2 %shard_map.90.refs_8_.weight = bf16[2048,1024]{1,0:T(8,128)(2,1)S(1)} custom-call(bf16[4096,2048]{1,0:T(8,128)(2,1)} %weight.5, bf16[16,2048]{1,0:T(8,128)(2,1)S(1)} %get-tuple-element.48.attended.refs_1_), custom_call_target="tpu_custom_call" | custom-call | bytes 4194304 | tf_op jit(solution)/shard_map/pallas_call | solution.py:658
  49.0 0.8 %collective-permute-done.17.refs_7_ = bf16[16,2048]{1,0:T(8,128)(2,1)S(1)} collective-permute-done((bf16[16,2048]{1,0:T(8,128)(2,1)S(1)}, bf16[16,2048]{1,0:T(8,128)(2,1)S(1)}, u32[]{:S(2)}, u32[]{:S(2)}) %collective-permute-start.17) | collective-permute-done | bytes 65568 | tf_op jit(solution)/shard_map/ppermute | solution.py:206
  49.8 0.8 %shard_map.91 = (bf16[128,1024]{1,0:T(8,128)(2,1)S(1)}, bf16[128,2048]{1,0:T(8,128)(2,1)S(1)}) custom-call(bf16[128,128]{1,0:T(8,128)(2,1)S(1)} %get-tuple-element.49.chosen, bf16[16,2048]{1,0:T(8,128)(2,1)S(1)} %get-tuple-element.47.refs_0_, bf16[16,2048]{1,0:T(8,128)(2,1)S(1)} %get-tuple-element.48.attended.refs_1_, ...), custom_call_target="tpu_custom_call" | custom-call | flops 536870912 | bytes 4194304 | tf_op jit(solution)/shard_map/pallas_call | solution.py:382
  50.7 0.7 %shard_map.92.own = f32[128,1024]{1,0:T(8,128)S(1)} custom-call(bf16[128,2048]{1,0:T(8,128)(2,1)S(1)} %get-tuple-element.51.permuted, bf16[2048,1024]{1,0:T(8,128)(2,1)S(1)} %shard_map.90.refs_8_.weight), custom_call_target="tpu_custom_call" | custom-call | flops 536870912 | bytes 4194304 | tf_op jit(solution)/shard_map/pallas_call | solution.py:391
  51.4 0.8 %collective-permute-done.18.received = bf16[128,1024]{1,0:T(8,128)(2,1)S(1)} collective-permute-done((bf16[128,1024]{1,0:T(8,128)(2,1)S(1)}, bf16[128,1024]{1,0:T(8,128)(2,1)S(1)}, u32[]{:S(2)}, u32[]{:S(2)}) %collective-permute-start.18) | collective-permute-done | bytes 262176 | tf_op jit(solution)/shard_map/ppermute | solution.py:206
  52.3 1.3 %collective-permute-start.19 = (bf16[32,1024]{1,0:T(8,128)(2,1)S(1)}, bf16[32,1024]{1,0:T(8,128)(2,1)S(1)}, u32[]{:S(2)}, u32[]{:S(2)}) collective-permute-start(bf16[32,1024]{1,0:T(8,128)(2,1)S(1)} %get-tuple-element.54), channel_id=1, source_target_pairs={{0,4},{4,0},{8,12},{12,8},{1,5},{5,1},{9,13},{13,9},{2,6},{6,2},{1... | collective-permute-start | bytes 196616 | tf_op jit(solution)/shard_map/ppermute | solution.py:206
  53.6 2.1 %collective-permute-start.21 = (bf16[32,1024]{1,0:T(8,128)(2,1)S(1)}, bf16[32,1024]{1,0:T(8,128)(2,1)S(1)}, u32[]{:S(2)}, u32[]{:S(2)}) collective-permute-start(bf16[32,1024]{1,0:T(8,128)(2,1)S(1)} %get-tuple-element.56), channel_id=1, source_target_pairs={{0,12},{4,8},{8,4},{12,0},{1,13},{5,9},{9,5},{13,1},{2,14},{6,10},... | collective-permute-start | bytes 196616 | tf_op jit(solution)/shard_map/ppermute | solution.py:206
  55.7 0.1 collective-permute-start.20
  55.8 0.8 %collective-permute-done.19.refs_0_.refs_3_ = bf16[32,1024]{1,0:T(8,128)(2,1)S(1)} collective-permute-done((bf16[32,1024]{1,0:T(8,128)(2,1)S(1)}, bf16[32,1024]{1,0:T(8,128)(2,1)S(1)}, u32[]{:S(2)}, u32[]{:S(2)}) %collective-permute-start.19) | collective-permute-done | bytes 65568 | tf_op jit(solution)/shard_map/ppermute | solution.py:206
  56.6 3.5 %collective-permute-done.21.refs_1_.refs_5_ = bf16[32,1024]{1,0:T(8,128)(2,1)S(1)} collective-permute-done((bf16[32,1024]{1,0:T(8,128)(2,1)S(1)}, bf16[32,1024]{1,0:T(8,128)(2,1)S(1)}, u32[]{:S(2)}, u32[]{:S(2)}) %collective-permute-start.21) | collective-permute-done | bytes 65568 | tf_op jit(solution)/shard_map/ppermute | solution.py:206
  60.1 0.8 %collective-permute-start.23 = (bf16[32,1024]{1,0:T(8,128)(2,1)S(1)}, bf16[32,1024]{1,0:T(8,128)(2,1)S(1)}, u32[]{:S(2)}, u32[]{:S(2)}) collective-permute-start(bf16[32,1024]{1,0:T(8,128)(2,1)S(1)} %shard_map.95), channel_id=1, source_target_pairs={{0,2},{2,0},{1,3},{3,1},{4,6},{6,4},{5,7},{7,5},{8,10},{10,8},{9,1... | collective-permute-start | bytes 196616 | tf_op jit(solution)/shard_map/ppermute | solution.py:206
  61.0 1.3 %collective-permute-done.20.refs_1_.refs_4_ = bf16[32,1024]{1,0:T(8,128)(2,1)S(1)} collective-permute-done((bf16[32,1024]{1,0:T(8,128)(2,1)S(1)}, bf16[32,1024]{1,0:T(8,128)(2,1)S(1)}, u32[]{:S(2)}, u32[]{:S(2)}) %collective-permute-start.20) | collective-permute-done | bytes 65568 | tf_op jit(solution)/shard_map/ppermute | solution.py:206
  62.3 0.7 collective-permute-start.22
  63.0 1.5 %collective-permute-done.23.refs_7_ = bf16[32,1024]{1,0:T(8,128)(2,1)S(1)} collective-permute-done((bf16[32,1024]{1,0:T(8,128)(2,1)S(1)}, bf16[32,1024]{1,0:T(8,128)(2,1)S(1)}, u32[]{:S(2)}, u32[]{:S(2)}) %collective-permute-start.23) | collective-permute-done | bytes 65568 | tf_op jit(solution)/shard_map/ppermute | solution.py:206
  64.4 2.2 %collective-permute-done.22.refs_6_ = bf16[32,1024]{1,0:T(8,128)(2,1)S(1)} collective-permute-done((bf16[32,1024]{1,0:T(8,128)(2,1)S(1)}, bf16[32,1024]{1,0:T(8,128)(2,1)S(1)}, u32[]{:S(2)}, u32[]{:S(2)}) %collective-permute-start.22) | collective-permute-done | bytes 65568 | tf_op jit(solution)/shard_map/ppermute | solution.py:206
  66.6 0.1 shard_map.96
  66.8 1.3 %collective-permute-done.24.received = bf16[32,2048]{1,0:T(8,128)(2,1)S(1)} collective-permute-done((bf16[32,2048]{1,0:T(8,128)(2,1)S(1)}, bf16[32,2048]{1,0:T(8,128)(2,1)S(1)}, u32[]{:S(2)}, u32[]{:S(2)}) %collective-permute-start.24) | collective-permute-done | bytes 131104 | tf_op jit(solution)/shard_map/ppermute | solution.py:206
  68.2 0.7 %shard_map.97 = bf16[1,32,4096]{2,1,0:T(8,128)(2,1)} custom-call(bf16[32,2048]{1,0:T(8,128)(2,1)S(1)} %get-tuple-element.57.keep, bf16[32,2048]{1,0:T(8,128)(2,1)S(1)} %collective-permute-done.24.received), custom_call_target="tpu_custom_call" | custom-call | bytes 524288 | tf_op jit(solution)/shard_map/pallas_call | solution.py:679
  (27 shorter events, 0.4 us)
Async XLA Ops:
  0.9 7.9 %collective-permute-start.2 = (bf16[16,2048]{1,0:T(8,128)(2,1)S(1)}, bf16[16,2048]{1,0:T(8,128)(2,1)S(1)}, u32[]{:S(2)}, u32[]{:S(2)}) collective-permute-start(bf16[16,2048]{1,0:T(8,128)(2,1)S(1)} %get-tuple-element.60.refs_0_), channel_id=1, source_target_pairs={{0,8},{4,12},{8,0},{12,4},{1,9},{5,13},{9,1},{13,5},{2,10},{6,14},... | collective-permute-start | bytes 196616 | tf_op jit(solution)/shard_map/ppermute | solution.py:206
  5.0 11.5 %copy-start.1 = (bf16[4096]{0:T(1024)(128)(2,1)S(1)}, bf16[4096]{0:T(1024)(128)(2,1)}, u32[]{:S(2)}) copy-start(bf16[4096]{0:T(1024)(128)(2,1)} %param.9) | copy-start | bytes 24580
  5.0 6.1 %collective-permute-start.3 = (bf16[16,2048]{1,0:T(8,128)(2,1)S(1)}, bf16[16,2048]{1,0:T(8,128)(2,1)S(1)}, u32[]{:S(2)}, u32[]{:S(2)}) collective-permute-start(bf16[16,2048]{1,0:T(8,128)(2,1)S(1)} %get-tuple-element.59.refs_1_), channel_id=1, source_target_pairs={{0,8},{4,12},{8,0},{12,4},{1,9},{5,13},{9,1},{13,5},{2,10},{6,14},... | collective-permute-start | bytes 196616 | tf_op jit(solution)/shard_map/ppermute | solution.py:206
  5.1 11.4 %collective-permute-start = (bf16[16,2048]{1,0:T(8,128)(2,1)S(1)}, bf16[16,2048]{1,0:T(8,128)(2,1)S(1)}, u32[]{:S(2)}, u32[]{:S(2)}) collective-permute-start(bf16[16,2048]{1,0:T(8,128)(2,1)S(1)} %get-tuple-element.60.refs_0_), channel_id=1, source_target_pairs={{0,4},{4,0},{8,12},{12,8},{1,5},{5,1},{9,13},{13,9},{2,6},{6,2},{1... | collective-permute-start | bytes 196616 | tf_op jit(solution)/shard_map/ppermute | solution.py:206
  6.9 9.6 %collective-permute-start.1 = (bf16[16,2048]{1,0:T(8,128)(2,1)S(1)}, bf16[16,2048]{1,0:T(8,128)(2,1)S(1)}, u32[]{:S(2)}, u32[]{:S(2)}) collective-permute-start(bf16[16,2048]{1,0:T(8,128)(2,1)S(1)} %get-tuple-element.59.refs_1_), channel_id=1, source_target_pairs={{0,4},{4,0},{8,12},{12,8},{1,5},{5,1},{9,13},{13,9},{2,6},{6,2},{1... | collective-permute-start | bytes 196616 | tf_op jit(solution)/shard_map/ppermute | solution.py:206
  8.7 7.8 %collective-permute-start.4 = (bf16[16,2048]{1,0:T(8,128)(2,1)S(1)}, bf16[16,2048]{1,0:T(8,128)(2,1)S(1)}, u32[]{:S(2)}, u32[]{:S(2)}) collective-permute-start(bf16[16,2048]{1,0:T(8,128)(2,1)S(1)} %collective-permute-done.2.refs_4_), channel_id=1, source_target_pairs={{0,4},{4,0},{8,12},{12,8},{1,5},{5,1},{9,13},{13,9},{2,6},{6,2},{1... | collective-permute-start | bytes 196616 | tf_op jit(solution)/shard_map/ppermute | solution.py:206
  11.1 5.4 %collective-permute-start.5 = (bf16[16,2048]{1,0:T(8,128)(2,1)S(1)}, bf16[16,2048]{1,0:T(8,128)(2,1)S(1)}, u32[]{:S(2)}, u32[]{:S(2)}) collective-permute-start(bf16[16,2048]{1,0:T(8,128)(2,1)S(1)} %collective-permute-done.3.refs_5_), channel_id=1, source_target_pairs={{0,4},{4,0},{8,12},{12,8},{1,5},{5,1},{9,13},{13,9},{2,6},{6,2},{1... | collective-permute-start | bytes 196616 | tf_op jit(solution)/shard_map/ppermute | solution.py:206
  17.6 14.0 %copy-start.2 = (s32[128]{0:T(128)S(1)}, s32[128]{0:T(128)}, u32[]{:S(2)}) copy-start(s32[128]{0:T(128)} %slots.3) | copy-start | bytes 1540
  17.6 14.0 %copy-start.3 = (s32[32]{0:T(128)S(1)}, s32[32]{0:T(128)}, u32[]{:S(2)}) copy-start(s32[32]{0:T(128)} %lengths.1) | copy-start | bytes 388
  17.6 1.7 %collective-permute-start.6 = (bf16[128,1408]{1,0:T(8,128)(2,1)S(1)}, bf16[128,1408]{1,0:T(8,128)(2,1)S(1)}, u32[]{:S(2)}, u32[]{:S(2)}) collective-permute-start(bf16[128,1408]{1,0:T(8,128)(2,1)S(1)} %get-tuple-element.39.given), channel_id=1, source_target_pairs={{0,1},{1,0},{2,3},{3,2},{4,5},{5,4},{6,7},{7,6},{8,9},{9,8},{10,11... | collective-permute-start | bytes 1081352 | tf_op jit(solution)/shard_map/ppermute | solution.py:206
  19.5 7.9 %collective-permute-start.8 = (bf16[32,1280]{1,0:T(8,128)(2,1)S(1)}, bf16[32,1280]{1,0:T(8,128)(2,1)S(1)}, u32[]{:S(2)}, u32[]{:S(2)}) collective-permute-start(bf16[32,1280]{1,0:T(8,128)(2,1)S(1)} %get-tuple-element.42), channel_id=1, source_target_pairs={{0,8},{4,12},{8,0},{12,4},{1,9},{5,13},{9,1},{13,5},{2,10},{6,14},... | collective-permute-start | bytes 245768 | tf_op jit(solution)/shard_map/ppermute | solution.py:206
  22.6 7.5 %collective-permute-start.7 = (bf16[32,1280]{1,0:T(8,128)(2,1)S(1)}, bf16[32,1280]{1,0:T(8,128)(2,1)S(1)}, u32[]{:S(2)}, u32[]{:S(2)}) collective-permute-start(bf16[32,1280]{1,0:T(8,128)(2,1)S(1)} %get-tuple-element.41), channel_id=1, source_target_pairs={{0,4},{4,0},{8,12},{12,8},{1,5},{5,1},{9,13},{13,9},{2,6},{6,2},{1... | collective-permute-start | bytes 245768 | tf_op jit(solution)/shard_map/ppermute | solution.py:206
  23.4 6.8 %collective-permute-start.9 = (bf16[32,1280]{1,0:T(8,128)(2,1)S(1)}, bf16[32,1280]{1,0:T(8,128)(2,1)S(1)}, u32[]{:S(2)}, u32[]{:S(2)}) collective-permute-start(bf16[32,1280]{1,0:T(8,128)(2,1)S(1)} %get-tuple-element.43), channel_id=1, source_target_pairs={{0,12},{4,8},{8,4},{12,0},{1,13},{5,9},{9,5},{13,1},{2,14},{6,10},... | collective-permute-start | bytes 245768 | tf_op jit(solution)/shard_map/ppermute | solution.py:206
  27.4 8.0 %collective-permute-start.10 = (bf16[32,1408]{1,0:T(8,128)(2,1)S(1)}, bf16[32,1408]{1,0:T(8,128)(2,1)S(1)}, u32[]{:S(2)}, u32[]{:S(2)}) collective-permute-start(bf16[32,1408]{1,0:T(8,128)(2,1)S(1)} %shard_map.87), channel_id=1, source_target_pairs={{0,2},{2,0},{1,3},{3,1},{4,6},{6,4},{5,7},{7,5},{8,10},{10,8},{9,1... | collective-permute-start | bytes 270344 | tf_op jit(solution)/shard_map/ppermute | solution.py:206
  30.1 5.2 %collective-permute-start.11 = (bf16[32,1280]{1,0:T(8,128)(2,1)S(1)}, bf16[32,1280]{1,0:T(8,128)(2,1)S(1)}, u32[]{:S(2)}, u32[]{:S(2)}) collective-permute-start(bf16[32,1280]{1,0:T(8,128)(2,1)S(1)} %shard_map.88), channel_id=1, source_target_pairs={{0,2},{2,0},{1,3},{3,1},{4,6},{6,4},{5,7},{7,5},{8,10},{10,8},{9,1... | collective-permute-start | bytes 245768 | tf_op jit(solution)/shard_map/ppermute | solution.py:206
  37.1 7.2 %collective-permute-start.14 = (bf16[16,2048]{1,0:T(8,128)(2,1)S(1)}, bf16[16,2048]{1,0:T(8,128)(2,1)S(1)}, u32[]{:S(2)}, u32[]{:S(2)}) collective-permute-start(bf16[16,2048]{1,0:T(8,128)(2,1)S(1)} %get-tuple-element.47.refs_0_), channel_id=1, source_target_pairs={{0,8},{4,12},{8,0},{12,4},{1,9},{5,13},{9,1},{13,5},{2,10},{6,14},... | collective-permute-start | bytes 196616 | tf_op jit(solution)/shard_map/ppermute | solution.py:206
  39.6 5.9 %collective-permute-start.15 = (bf16[16,2048]{1,0:T(8,128)(2,1)S(1)}, bf16[16,2048]{1,0:T(8,128)(2,1)S(1)}, u32[]{:S(2)}, u32[]{:S(2)}) collective-permute-start(bf16[16,2048]{1,0:T(8,128)(2,1)S(1)} %get-tuple-element.48.attended.refs_1_), channel_id=1, source_target_pairs={{0,8},{4,12},{8,0},{12,4},{1,9},{5,13},{9,1},{13,5},{2,10},{6,14},... | collective-permute-start | bytes 196616 | tf_op jit(solution)/shard_map/ppermute | solution.py:206
  40.1 8.9 %collective-permute-start.12 = (bf16[16,2048]{1,0:T(8,128)(2,1)S(1)}, bf16[16,2048]{1,0:T(8,128)(2,1)S(1)}, u32[]{:S(2)}, u32[]{:S(2)}) collective-permute-start(bf16[16,2048]{1,0:T(8,128)(2,1)S(1)} %get-tuple-element.47.refs_0_), channel_id=1, source_target_pairs={{0,4},{4,0},{8,12},{12,8},{1,5},{5,1},{9,13},{13,9},{2,6},{6,2},{1... | collective-permute-start | bytes 196616 | tf_op jit(solution)/shard_map/ppermute | solution.py:206
  41.2 7.8 %collective-permute-start.13 = (bf16[16,2048]{1,0:T(8,128)(2,1)S(1)}, bf16[16,2048]{1,0:T(8,128)(2,1)S(1)}, u32[]{:S(2)}, u32[]{:S(2)}) collective-permute-start(bf16[16,2048]{1,0:T(8,128)(2,1)S(1)} %get-tuple-element.48.attended.refs_1_), channel_id=1, source_target_pairs={{0,4},{4,0},{8,12},{12,8},{1,5},{5,1},{9,13},{13,9},{2,6},{6,2},{1... | collective-permute-start | bytes 196616 | tf_op jit(solution)/shard_map/ppermute | solution.py:206
  44.3 4.7 %collective-permute-start.16 = (bf16[16,2048]{1,0:T(8,128)(2,1)S(1)}, bf16[16,2048]{1,0:T(8,128)(2,1)S(1)}, u32[]{:S(2)}, u32[]{:S(2)}) collective-permute-start(bf16[16,2048]{1,0:T(8,128)(2,1)S(1)} %collective-permute-done.14.refs_4_), channel_id=1, source_target_pairs={{0,4},{4,0},{8,12},{12,8},{1,5},{5,1},{9,13},{13,9},{2,6},{6,2},{1... | collective-permute-start | bytes 196616 | tf_op jit(solution)/shard_map/ppermute | solution.py:206
  45.5 4.3 %collective-permute-start.17 = (bf16[16,2048]{1,0:T(8,128)(2,1)S(1)}, bf16[16,2048]{1,0:T(8,128)(2,1)S(1)}, u32[]{:S(2)}, u32[]{:S(2)}) collective-permute-start(bf16[16,2048]{1,0:T(8,128)(2,1)S(1)} %collective-permute-done.15.refs_5_), channel_id=1, source_target_pairs={{0,4},{4,0},{8,12},{12,8},{1,5},{5,1},{9,13},{13,9},{2,6},{6,2},{1... | collective-permute-start | bytes 196616 | tf_op jit(solution)/shard_map/ppermute | solution.py:206
  50.6 16.0 %copy-start = (bf16[32,4096]{1,0:T(8,128)(2,1)S(1)}, bf16[32,4096]{1,0:T(8,128)(2,1)}, u32[]{:S(2)}) copy-start(bf16[32,4096]{1,0:T(8,128)(2,1)} %hidden.1) | copy-start | bytes 786436
  50.6 1.6 %collective-permute-start.18 = (bf16[128,1024]{1,0:T(8,128)(2,1)S(1)}, bf16[128,1024]{1,0:T(8,128)(2,1)S(1)}, u32[]{:S(2)}, u32[]{:S(2)}) collective-permute-start(bf16[128,1024]{1,0:T(8,128)(2,1)S(1)} %get-tuple-element.52.given), channel_id=1, source_target_pairs={{0,1},{1,0},{2,3},{3,2},{4,5},{5,4},{6,7},{7,6},{8,9},{9,8},{10,11... | collective-permute-start | bytes 786440 | tf_op jit(solution)/shard_map/ppermute | solution.py:206
  52.3 4.3 %collective-permute-start.19 = (bf16[32,1024]{1,0:T(8,128)(2,1)S(1)}, bf16[32,1024]{1,0:T(8,128)(2,1)S(1)}, u32[]{:S(2)}, u32[]{:S(2)}) collective-permute-start(bf16[32,1024]{1,0:T(8,128)(2,1)S(1)} %get-tuple-element.54), channel_id=1, source_target_pairs={{0,4},{4,0},{8,12},{12,8},{1,5},{5,1},{9,13},{13,9},{2,6},{6,2},{1... | collective-permute-start | bytes 196616 | tf_op jit(solution)/shard_map/ppermute | solution.py:206
  53.6 6.5 %collective-permute-start.21 = (bf16[32,1024]{1,0:T(8,128)(2,1)S(1)}, bf16[32,1024]{1,0:T(8,128)(2,1)S(1)}, u32[]{:S(2)}, u32[]{:S(2)}) collective-permute-start(bf16[32,1024]{1,0:T(8,128)(2,1)S(1)} %get-tuple-element.56), channel_id=1, source_target_pairs={{0,12},{4,8},{8,4},{12,0},{1,13},{5,9},{9,5},{13,1},{2,14},{6,10},... | collective-permute-start | bytes 196616 | tf_op jit(solution)/shard_map/ppermute | solution.py:206
  55.7 6.6 %collective-permute-start.20 = (bf16[32,1024]{1,0:T(8,128)(2,1)S(1)}, bf16[32,1024]{1,0:T(8,128)(2,1)S(1)}, u32[]{:S(2)}, u32[]{:S(2)}) collective-permute-start(bf16[32,1024]{1,0:T(8,128)(2,1)S(1)} %get-tuple-element.55), channel_id=1, source_target_pairs={{0,8},{4,12},{8,0},{12,4},{1,9},{5,13},{9,1},{13,5},{2,10},{6,14},... | collective-permute-start | bytes 196616 | tf_op jit(solution)/shard_map/ppermute | solution.py:206
  60.1 4.3 %collective-permute-start.23 = (bf16[32,1024]{1,0:T(8,128)(2,1)S(1)}, bf16[32,1024]{1,0:T(8,128)(2,1)S(1)}, u32[]{:S(2)}, u32[]{:S(2)}) collective-permute-start(bf16[32,1024]{1,0:T(8,128)(2,1)S(1)} %shard_map.95), channel_id=1, source_target_pairs={{0,2},{2,0},{1,3},{3,1},{4,6},{6,4},{5,7},{7,5},{8,10},{10,8},{9,1... | collective-permute-start | bytes 196616 | tf_op jit(solution)/shard_map/ppermute | solution.py:206
  62.3 4.3 %collective-permute-start.22 = (bf16[32,1024]{1,0:T(8,128)(2,1)S(1)}, bf16[32,1024]{1,0:T(8,128)(2,1)S(1)}, u32[]{:S(2)}, u32[]{:S(2)}) collective-permute-start(bf16[32,1024]{1,0:T(8,128)(2,1)S(1)} %shard_map.94), channel_id=1, source_target_pairs={{0,2},{2,0},{1,3},{3,1},{4,6},{6,4},{5,7},{7,5},{8,10},{10,8},{9,1... | collective-permute-start | bytes 196616 | tf_op jit(solution)/shard_map/ppermute | solution.py:206
  66.7 1.4 %collective-permute-start.24 = (bf16[32,2048]{1,0:T(8,128)(2,1)S(1)}, bf16[32,2048]{1,0:T(8,128)(2,1)S(1)}, u32[]{:S(2)}, u32[]{:S(2)}) collective-permute-start(bf16[32,2048]{1,0:T(8,128)(2,1)S(1)} %get-tuple-element.58), channel_id=1, source_target_pairs={{0,1},{1,0},{2,3},{3,2},{4,5},{5,4},{6,7},{7,6},{8,9},{9,8},{10,11... | collective-permute-start | bytes 393224 | tf_op jit(solution)/shard_map/ppermute | solution.py:206

commit v16 on v15

--- a/solution.py
+++ b/solution.py
@@ -225,11 +225,6 @@
     return lax.axis_index("side"), lax.axis_index("col")
 
 
-def run_base():
-    pairs = lax.axis_size("col") // lax.axis_size("row")
-    return lax.div(lax.axis_index("col"), pairs) ^ lax.axis_index("row")
-
-
 def rows_copy(weight, target, half):
     depth, width = target.shape
     rows = pl.ds(pl.multiple_of(lax.axis_index("side") * depth, depth), depth)
@@ -355,17 +350,37 @@
     dot_columns(order, weight, give)
 
 
+def at_home():
+    pairs = lax.axis_size("col") // lax.axis_size("row")
+    return lax.axis_index("row") == lax.div(lax.axis_index("col"), pairs)
+
+
 def merge_kernel(count, own, given, received, *outs):
     rows = outs[0].shape[0]
     half = own.shape[1]
     more = given.shape[1] - half
-    for i, out in enumerate(outs[:count]):
-        part = slice(i * rows, (i + 1) * rows)
+    pairs = count // 2
+
+    def write(out, first):
+        first = first if isinstance(first, int) else pl.multiple_of(first, rows)
+        part = pl.ds(first, rows)
         total = own[part, :] + received[part, :half].astype(jnp.float32)
-        out[...] = total.astype(jnp.bfloat16)
+        out[:, :half] = total.astype(jnp.bfloat16)
+        if out.shape[1] > half:
+            out[:, half:] = squares(part)
+
+    def squares(part):
+        lanes = slice(half, half + more // 2)
+        return jnp.concatenate([given[part, lanes], received[part, lanes]], axis=1)
+
+    write(outs[0], 0)
+    write(outs[1], pairs * rows)
+    home = at_home()
+    for pair in range(1, pairs):
+        write(outs[2 * pair], jnp.where(home, pairs + pair, pair) * rows)
+        write(outs[2 * pair + 1], jnp.where(home, pair, pairs + pair) * rows)
     for out in outs[count:]:
-        lanes = slice(half, half + more // 2)
-        out[...] = jnp.concatenate([given[:rows, lanes], received[:rows, lanes]], axis=1)
+        out[...] = squares(pl.ds(0, rows))
 
 
 def own_kernel(permuted, weight, own):
@@ -396,7 +411,7 @@
         flops,
         depth * half * 2,
     )(permuted, in_vmem(weights[1]))
-    outs = [struct((rows // count, half))] * count
+    outs = [struct((rows // count, half + (more if i > 1 else 0))) for i in range(count)]
     if more:
         outs = outs + [struct((rows // count, more))]
     merged = call(
@@ -422,54 +437,44 @@
     return [part for i in sorted(blocks) for part in blocks[i]]
 
 
-def choose_kernel(count, other, *refs):
-    blocks, sums, out = refs[:count], refs[count:-1], refs[-1]
-    width = blocks[0].shape[1]
-    wanted = run_base() ^ other
-    chosen = blocks[0][...]
-    for run, block in enumerate(blocks[1:], 1):
-        chosen = jnp.where(wanted == run, block[...], chosen)
-    out[:, :width] = chosen
-    for ref in sums:
-        out[:, width:] = ref[...]
-
-
-def spread(products, sums):
-    col_count, row_count = lax.axis_size("col"), lax.axis_size("row")
-    pairs = col_count // row_count
-    blocks = {0: products[0]}
-    for mask in [*range(pairs, col_count), *range(1, pairs)]:
-        blocks[mask] = moved(products[mask], "col", mask)
-    arrived = []
-    for pair in range(pairs):
-        runs = [blocks[run * pairs + pair] for run in range(row_count)]
-        beside = sums if pair == 0 else []
-        width = sum(part.shape[1] for part in [runs[0], *beside])
-        for mask in range(1, row_count):
-            chosen = call(
-                functools.partial(choose_kernel, row_count, mask),
-                struct((runs[0].shape[0], width)),
-                [VMEM] * (row_count + len(beside)),
-                VMEM,
-                0,
-                width * runs[0].shape[0] * 4,
-            )(*runs, *beside)
-            arrived.append(moved(chosen, "row", mask))
-    return [blocks[i] for i in range(col_count)] + arrived
-
-
-def total_of(blocks, arrived, pair):
-    others = lax.axis_size("row") - 1
-    pairs = len(blocks) // (others + 1)
-    rows, width = blocks[0].shape
-    base = run_base()
-    kept = blocks[pair][...]
-    for run in range(1, others + 1):
-        kept = jnp.where(base == run, blocks[run * pairs + pair][...], kept)
-    total = kept.astype(jnp.float32)
-    for ref in arrived[pair * others : (pair + 1) * others]:
-        total = total + ref[:, :width].astype(jnp.float32)
-    return total
+def choose_kernel(own, passed, out):
+    out[...] = jnp.where(at_home(), passed[...], own[...])
+
+
+def direct(value, far, pair):
+    pairs = lax.axis_size("col") // 2
+    moves = []
+    for col in range(2 * pairs):
+        for row in range(2):
+            home = row == col // pairs
+            target = col ^ pair ^ (pairs if home == far else 0)
+            moves.append((2 * col + row, 2 * target + (row if home else 1 - row)))
+    return lax.ppermute(value, ("col", "row"), moves)
+
+
+def spread(products):
+    own, passed, *rest = products
+    pairs = len(products) // 2
+    passed = moved(passed, "col", pairs)
+    blocks = []
+    for pair in range(1, pairs):
+        blocks += [
+            direct(rest[2 * pair - 2], True, pair),
+            direct(rest[2 * pair - 1], False, pair),
+        ]
+    crossing = call(
+        choose_kernel, struct(own.shape), [VMEM] * 2, VMEM, 0, own.size * 4
+    )(own, passed)
+    return [passed, *blocks, own, moved(crossing, "row", 1)]
+
+
+def total_of(blocks, pair, width):
+    if pair > 0:
+        first, second = blocks[2 * pair - 1][:, :width], blocks[2 * pair][:, :width]
+    else:
+        passed, own, crossed = blocks[0], blocks[-2], blocks[-1]
+        first, second = jnp.where(at_home(), own[...], passed[...]), crossed[...]
+    return first.astype(jnp.float32) + second.astype(jnp.float32)
 
 
 def rotated(vector, cosine, sine):
@@ -490,18 +495,14 @@
 
 
 def attend_all(count, parts, cosine, sine, lengths, *refs):
-    others = lax.axis_size("row") - 1
-    pairs = count // (others + 1)
-    blocks, refs = refs[:count], refs[count:]
-    arrived, refs = refs[: pairs * others], refs[pairs * others :]
-    (sums, keys, values), refs = refs[:3], refs[3:]
+    pairs = (count - 1) // 2
+    blocks, (sums, keys, values), refs = refs[:count], refs[count : count + 3], refs[count + 3 :]
     outs, (scores_of, probs_of) = refs[:parts], refs[parts:]
     rows, cache = keys.shape[:2]
     low = lax.rem(lax.axis_index("col"), pairs)
     width = GROUP_WIDTH
-    squares = sums[...].astype(jnp.float32)
-    for ref in arrived[:others]:
-        squares = squares + ref[:, width:].astype(jnp.float32)
+    other_sums = jnp.where(at_home(), blocks[1][:, width:], blocks[2][:, width:])
+    squares = sums[...].astype(jnp.float32) + other_sums.astype(jnp.float32)
     scale = lax.rsqrt(jnp.sum(squares, axis=1, keepdims=True) / D + EPSILON)
     factor = HEAD_DIM ** (-0.5)
     cosines, sines, length_of = cosine[...], sine[...], lengths[:, :1]
@@ -512,7 +513,7 @@
     filled = [(position >= 0) & (position < length_of[part]) for part in runs]
     own, new_values, own_probs = [], [], []
     for pair in range(pairs):
-        total = total_of(blocks, arrived, pair)
+        total = total_of(blocks, pair, width)
         total = (total * scale).astype(jnp.bfloat16).astype(jnp.float32)
         heads = [total[:, h * HEAD_DIM : (h + 1) * HEAD_DIM] for h in range(GROUP + 2)]
         queries = [
@@ -567,15 +568,14 @@
 
 
 def sum_kernel(count, parts, hidden, *refs):
-    attended, blocks, arrived = refs[:parts], refs[parts : parts + count], refs[parts + count : -2]
-    keep, send = refs[-2:]
+    attended, blocks, (keep, send) = refs[:parts], refs[parts : parts + count], refs[-2:]
     rows, width = blocks[0].shape
     pairs = keep.shape[1] // width
     side = lax.axis_index("side")
     low = lax.rem(lax.axis_index("col"), pairs)
     for pair in range(pairs):
         column = low ^ pair
-        total = total_of(blocks, arrived, pair)
+        total = total_of(blocks, pair, width)
         at = pl.ds(pl.multiple_of((2 * column + side) * width, width), width)
         hidden_out = (hidden[:, at].astype(jnp.float32) + total).astype(jnp.bfloat16)
         at = pl.ds(pl.multiple_of(column * width, width), width)
@@ -630,7 +630,7 @@
         [own_part[i * piece : (i + 1) * piece] for i in range(parts)], "col"
     )
     products, sums = project(in_kernel, chosen_in, blocks, [gain], [give_in, own_in], HEAD_DIM)
-    products = spread(products, sums)
+    products = spread(products)
 
     table = struct((rows, HEAD_DIM), jnp.float32)
     give_out, key_part, value_part, *tables, chosen_out = call(
@@ -646,7 +646,7 @@
     )(cache_lengths, in_hbm(out_weight), in_hbm(key_cache), in_hbm(value_cache), slot_request)
     runs = (pairs, rows // SLOTS, GROUP * SLOTS, SLOTS * cache)
     attended = call(
-        functools.partial(attend_all, col_count, parts),
+        functools.partial(attend_all, len(products), parts),
         [struct((piece, half))] * parts,
         [VMEM] * (len(products) + 6),
         [VMEM] * parts,
@@ -667,9 +667,9 @@
     products, _ = project(
         out_kernel, chosen_out, gathered(attended, "col"), [], [give_out, own_out], 0
     )
-    products = spread(products, [])
+    products = spread(products)
     keep, send = call(
-        functools.partial(sum_kernel, col_count, parts),
+        functools.partial(sum_kernel, len(products), parts),
         [struct((rows, half)), struct((rows, half))],
         [VMEM] * (1 + parts + len(products)),
         [VMEM, VMEM],
@@ -693,7 +693,7 @@
     fits = (
         lax.axis_size("side") == 2
         and qkv_weight.shape[1] == 2 * GROUP_WIDTH
-        and col_count % row_count == 0
+        and row_count == 2
         and col_count > row_count
         and col_count & (col_count - 1) == 0
         and hidden_in.shape[0] % 32 == 0

time: 69.1 us -> 62.9 us (0.910)
  waiting for transfers between devices: 22.8 us -> 13.8 us
  starting transfers between devices: 28.7 us -> 31.5 us
    ppermute x25 -> x19, waiting for transfers between devices: 22.8 us -> 11.5 us  [moved(): return lax.ppermute(value, axis, pairs)]
    ppermute x0 -> x4, starting transfers between devices: none -> 3.66 us  [direct(): return lax.ppermute(value, ('col', 'row'), moves)]
    ppermute x0 -> x4, waiting for transfers between devices: none -> 2.24 us  [direct(): return lax.ppermute(value, ('col', 'row'), moves)]
    ppermute x25 -> x19, starting transfers between devices: 28.7 us -> 27.9 us  [moved(): return lax.ppermute(value, axis, pairs)]
    pallas_call x6 -> x4, Pallas kernels: 1.87 us -> 1.91 us  [the longest x1 1.79 us: paired_plan(): call(functools.partial(attend_all, len(products), parts), [struct((piece,...]
  transfers between devices with their start and end apart: 25 -> 23, of which waited for: 15 -> 10; matrix products, arithmetic and copies ran while one was open for 0% -> 0% of each run, Pallas kernels for 17% -> 19%
where the time goes in v16:
time: 62.9 us; the launch traced here: 62.8 us
  starting transfers between devices  31.5 us (50%)
  Pallas kernels  16.3 us (26%)
  waiting for transfers between devices  13.8 us (22%)
  local copies, waits for them, and re-layouts  0.9 us (1%)
    ppermute x19, starting transfers between devices, moved(): return lax.ppermute(value, axis, pairs)  27.9 us
    ppermute x19, waiting for transfers between devices, moved(): return lax.ppermute(value, axis, pairs)  11.5 us
    pallas_call x1, Pallas kernels, paired_plan(): call(functools.partial(stage_in_kernel, col_count), [pltpu.VMEM((half, ha...  4.09 us
    pallas_call x1, Pallas kernels, paired_plan(): call(functools.partial(stage_rest_kernel, col_count), [pltpu.VMEM((half,...  3.71 us
    ppermute x4, starting transfers between devices, direct(): return lax.ppermute(value, ('col', 'row'), moves)  3.66 us
    pallas_call x1, Pallas kernels, paired_plan(): call(stage_out_kernel, pltpu.VMEM((half, half_out), jnp.bfloat16), [HBM,...  2.24 us
    ppermute x4, waiting for transfers between devices, direct(): return lax.ppermute(value, ('col', 'row'), moves)  2.24 us
    pallas_call x2, Pallas kernels, project(): call(functools.partial(kernel, parts), [struct((rows, half + more)), stru...  1.92 us
  transfers between devices with their start and end apart: 23, of which 10 were waited for; matrix products, arithmetic and copies ran while one was open for 0% of the time, Pallas kernels for 19%

profile of v16, /device:TPU:0, one launch (start us, length us, event | category | flops | bytes accessed | tf_op | source)
XLA Modules:
  0.0 62.8 jit_solution(2614614206920067891)
XLA Ops:
  0.0 0.9 %fusion = (bf16[16,2048]{1,0:T(8,128)(2,1)S(1)}, bf16[16,2048]{1,0:T(8,128)(2,1)S(1)}) fusion(bf16[32,4096]{1,0:T(8,128)(2,1)} %hidden.1, s32[]{:T(128)S(6)} %add.4, s32[]{:T(128)S(6)} %select_n.3), kind=kLoop, calls=%fused_computation.1 | loop fusion | bytes 262152 | tf_op jit(solution)/shard_map/slice | solution.py:630
  0.9 4.1 %collective-permute-start.2 = (bf16[16,2048]{1,0:T(8,128)(2,1)S(1)}, bf16[16,2048]{1,0:T(8,128)(2,1)S(1)}, u32[]{:S(2)}, u32[]{:S(2)}) collective-permute-start(bf16[16,2048]{1,0:T(8,128)(2,1)S(1)} %get-tuple-element.60.refs_0_), channel_id=1, source_target_pairs={{0,8},{4,12},{8,0},{12,4},{1,9},{5,13},{9,1},{13,5},{2,10},{6,14},... | collective-permute-start | bytes 196616 | tf_op jit(solution)/shard_map/ppermute | solution.py:206
  5.0 0.1 collective-permute-start.3
  5.1 1.8 %collective-permute-start = (bf16[16,2048]{1,0:T(8,128)(2,1)S(1)}, bf16[16,2048]{1,0:T(8,128)(2,1)S(1)}, u32[]{:S(2)}, u32[]{:S(2)}) collective-permute-start(bf16[16,2048]{1,0:T(8,128)(2,1)S(1)} %get-tuple-element.60.refs_0_), channel_id=1, source_target_pairs={{0,4},{4,0},{8,12},{12,8},{1,5},{5,1},{9,13},{13,9},{2,6},{6,2},{1... | collective-permute-start | bytes 196616 | tf_op jit(solution)/shard_map/ppermute | solution.py:206
  6.9 0.2 collective-permute-start.1
  7.1 1.6 %collective-permute-done.2.refs_4_ = bf16[16,2048]{1,0:T(8,128)(2,1)S(1)} collective-permute-done((bf16[16,2048]{1,0:T(8,128)(2,1)S(1)}, bf16[16,2048]{1,0:T(8,128)(2,1)S(1)}, u32[]{:S(2)}, u32[]{:S(2)}) %collective-permute-start.2) | collective-permute-done | bytes 65568 | tf_op jit(solution)/shard_map/ppermute | solution.py:206
  8.7 1.9 %collective-permute-start.4 = (bf16[16,2048]{1,0:T(8,128)(2,1)S(1)}, bf16[16,2048]{1,0:T(8,128)(2,1)S(1)}, u32[]{:S(2)}, u32[]{:S(2)}) collective-permute-start(bf16[16,2048]{1,0:T(8,128)(2,1)S(1)} %collective-permute-done.2.refs_4_), channel_id=1, source_target_pairs={{0,4},{4,0},{8,12},{12,8},{1,5},{5,1},{9,13},{13,9},{2,6},{6,2},{1... | collective-permute-start | bytes 196616 | tf_op jit(solution)/shard_map/ppermute | solution.py:206
  10.6 0.4 collective-permute-done.3.refs_5_
  11.1 1.3 %collective-permute-start.5 = (bf16[16,2048]{1,0:T(8,128)(2,1)S(1)}, bf16[16,2048]{1,0:T(8,128)(2,1)S(1)}, u32[]{:S(2)}, u32[]{:S(2)}) collective-permute-start(bf16[16,2048]{1,0:T(8,128)(2,1)S(1)} %collective-permute-done.3.refs_5_), channel_id=1, source_target_pairs={{0,4},{4,0},{8,12},{12,8},{1,5},{5,1},{9,13},{13,9},{2,6},{6,2},{1... | collective-permute-start | bytes 196616 | tf_op jit(solution)/shard_map/ppermute | solution.py:206
  12.4 4.1 %shard_map.83 = (bf16[2048,1280]{1,0:T(8,128)(2,1)S(1)}, bf16[2048,1280]{1,0:T(8,128)(2,1)S(1)}, bf16[128,128]{1,0:T(8,128)(2,1)S(1)}) custom-call(bf16[4096,2560]{1,0:T(8,128)(2,1)} %weight.4, s32[128]{0:T(128)} %slots.3), custom_call_target="tpu_custom_call" | custom-call | bytes 10485760 | tf_op jit(solution)/shard_map/pallas_call | solution.py:616
  16.5 1.1 %shard_map.84 = (bf16[128,1408]{1,0:T(8,128)(2,1)S(1)}, bf16[128,2048]{1,0:T(8,128)(2,1)S(1)}) custom-call(bf16[128,128]{1,0:T(8,128)(2,1)S(1)} %get-tuple-element.35.chosen, bf16[16,2048]{1,0:T(8,128)(2,1)S(1)} %get-tuple-element.60.refs_0_, bf16[16,2048]{1,0:T(8,128)(2,1)S(1)} %get-tuple-element.59.refs_1_, ...), custom_call_target="tpu_custom_call" | custom-call | flops 671088640 | bytes 5242880 | tf_op jit(solution)/shard_map/pallas_call | solution.py:397
  17.6 0.0 copy-start.2
  17.6 0.0 copy-start.3
  17.6 0.1 collective-permute-start.6
  17.7 0.9 %shard_map.85.own = f32[128,1280]{1,0:T(8,128)S(1)} custom-call(bf16[128,2048]{1,0:T(8,128)(2,1)S(1)} %get-tuple-element.38.permuted, bf16[2048,1280]{1,0:T(8,128)(2,1)S(1)} %get-tuple-element.36.refs_8_.weight), custom_call_target="tpu_custom_call" | custom-call | flops 671088640 | bytes 5242880 | tf_op jit(solution)/shard_map/pallas_call | solution.py:406
  18.6 0.8 %collective-permute-done.6.received = bf16[128,1408]{1,0:T(8,128)(2,1)S(1)} collective-permute-done((bf16[128,1408]{1,0:T(8,128)(2,1)S(1)}, bf16[128,1408]{1,0:T(8,128)(2,1)S(1)}, u32[]{:S(2)}, u32[]{:S(2)}) %collective-permute-start.6) | collective-permute-done | bytes 360480 | tf_op jit(solution)/shard_map/ppermute | solution.py:206
  19.4 0.1 shard_map.86
  19.5 3.2 %collective-permute-start.7 = (bf16[32,1280]{1,0:T(8,128)(2,1)S(1)}, bf16[32,1280]{1,0:T(8,128)(2,1)S(1)}, u32[]{:S(2)}, u32[]{:S(2)}) collective-permute-start(bf16[32,1280]{1,0:T(8,128)(2,1)S(1)} %get-tuple-element.40), channel_id=1, source_target_pairs={{0,8},{4,12},{8,0},{12,4},{1,9},{5,13},{9,1},{13,5},{2,10},{6,14},... | collective-permute-start | bytes 245768 | tf_op jit(solution)/shard_map/ppermute | solution.py:206
  22.7 0.2 collective-permute-start.8
  22.9 0.5 collective-permute-start.9
  23.4 3.9 %collective-permute-done.7.passed.refs_0_ = bf16[32,1280]{1,0:T(8,128)(2,1)S(1)} collective-permute-done((bf16[32,1280]{1,0:T(8,128)(2,1)S(1)}, bf16[32,1280]{1,0:T(8,128)(2,1)S(1)}, u32[]{:S(2)}, u32[]{:S(2)}) %collective-permute-start.7) | collective-permute-done | bytes 81952 | tf_op jit(solution)/shard_map/ppermute | solution.py:206
  27.3 3.1 %collective-permute-start.10 = (bf16[32,1280]{1,0:T(8,128)(2,1)S(1)}, bf16[32,1280]{1,0:T(8,128)(2,1)S(1)}, u32[]{:S(2)}, u32[]{:S(2)}) collective-permute-start(bf16[32,1280]{1,0:T(8,128)(2,1)S(1)} %shard_map.87), channel_id=1, source_target_pairs={{0,2},{2,0},{1,3},{3,1},{4,6},{6,4},{5,7},{7,5},{8,10},{10,8},{9,1... | collective-permute-start | bytes 245768 | tf_op jit(solution)/shard_map/ppermute | solution.py:206
  30.4 3.7 %shard_map.82 = (bf16[2048,1024]{1,0:T(8,128)(2,1)S(1)}, bf16[32,64,256]{2,1,0:T(8,128)(2,1)S(1)}, bf16[32,64,256]{2,1,0:T(8,128)(2,1)S(1)}, f32[32,128]{1,0:T(8...) custom-call(s32[32]{0:T(128)S(1)} %copy-done.3, bf16[4096,2048]{1,0:T(8,128)(2,1)} %weight.5, ...), custom_call_target="tpu_custom_call" | custom-call | bytes 6291456 | tf_op jit(solution)/shard_map/pallas_call | solution.py:636
  34.1 1.8 %shard_map.88 = (bf16[16,2048]{1,0:T(8,128)(2,1)S(1)}, bf16[16,2048]{1,0:T(8,128)(2,1)S(1)}) custom-call(f32[32,128]{1,0:T(8,128)S(1)} %get-tuple-element.32.cosine, f32[32,128]{1,0:T(8,128)S(1)} %get-tuple-element.33.sine, s32[32,128]{1,0:T(8,128)S(1)} %get-tuple-element.34.lengths, bf16[32,1280]{1,0:T(8,128)(2,1)S(1)} %collective-permute-done.7.passed.refs_0_, ...), custom_call_target="tpu_custom_call" | custom-call | flops 16777216 | tf_op jit(solution)/shard_map/pallas_call | solution.py:648
  35.9 0.4 collective-permute-start.13
  36.3 2.6 %collective-permute-start.14 = (bf16[16,2048]{1,0:T(8,128)(2,1)S(1)}, bf16[16,2048]{1,0:T(8,128)(2,1)S(1)}, u32[]{:S(2)}, u32[]{:S(2)}) collective-permute-start(bf16[16,2048]{1,0:T(8,128)(2,1)S(1)} %get-tuple-element.48.attended.refs_1_), channel_id=1, source_target_pairs={{0,8},{4,12},{8,0},{12,4},{1,9},{5,13},{9,1},{13,5},{2,10},{6,14},... | collective-permute-start | bytes 196616 | tf_op jit(solution)/shard_map/ppermute | solution.py:206
  38.9 0.8 %collective-permute-start.11 = (bf16[16,2048]{1,0:T(8,128)(2,1)S(1)}, bf16[16,2048]{1,0:T(8,128)(2,1)S(1)}, u32[]{:S(2)}, u32[]{:S(2)}) collective-permute-start(bf16[16,2048]{1,0:T(8,128)(2,1)S(1)} %get-tuple-element.47.refs_0_), channel_id=1, source_target_pairs={{0,4},{4,0},{8,12},{12,8},{1,5},{5,1},{9,13},{13,9},{2,6},{6,2},{1... | collective-permute-start | bytes 196616 | tf_op jit(solution)/shard_map/ppermute | solution.py:206
  39.7 1.2 %collective-permute-start.12 = (bf16[16,2048]{1,0:T(8,128)(2,1)S(1)}, bf16[16,2048]{1,0:T(8,128)(2,1)S(1)}, u32[]{:S(2)}, u32[]{:S(2)}) collective-permute-start(bf16[16,2048]{1,0:T(8,128)(2,1)S(1)} %get-tuple-element.48.attended.refs_1_), channel_id=1, source_target_pairs={{0,4},{4,0},{8,12},{12,8},{1,5},{5,1},{9,13},{13,9},{2,6},{6,2},{1... | collective-permute-start | bytes 196616 | tf_op jit(solution)/shard_map/ppermute | solution.py:206
  40.9 0.8 %collective-permute-done.13.refs_4_ = bf16[16,2048]{1,0:T(8,128)(2,1)S(1)} collective-permute-done((bf16[16,2048]{1,0:T(8,128)(2,1)S(1)}, bf16[16,2048]{1,0:T(8,128)(2,1)S(1)}, u32[]{:S(2)}, u32[]{:S(2)}) %collective-permute-start.13) | collective-permute-done | bytes 65568 | tf_op jit(solution)/shard_map/ppermute | solution.py:206
  41.7 0.9 %collective-permute-start.15 = (bf16[16,2048]{1,0:T(8,128)(2,1)S(1)}, bf16[16,2048]{1,0:T(8,128)(2,1)S(1)}, u32[]{:S(2)}, u32[]{:S(2)}) collective-permute-start(bf16[16,2048]{1,0:T(8,128)(2,1)S(1)} %collective-permute-done.13.refs_4_), channel_id=1, source_target_pairs={{0,4},{4,0},{8,12},{12,8},{1,5},{5,1},{9,13},{13,9},{2,6},{6,2},{1... | collective-permute-start | bytes 196616 | tf_op jit(solution)/shard_map/ppermute | solution.py:206
  42.6 0.0 collective-permute-done.14.refs_5_
  42.6 2.8 %collective-permute-start.16 = (bf16[16,2048]{1,0:T(8,128)(2,1)S(1)}, bf16[16,2048]{1,0:T(8,128)(2,1)S(1)}, u32[]{:S(2)}, u32[]{:S(2)}) collective-permute-start(bf16[16,2048]{1,0:T(8,128)(2,1)S(1)} %collective-permute-done.14.refs_5_), channel_id=1, source_target_pairs={{0,4},{4,0},{8,12},{12,8},{1,5},{5,1},{9,13},{13,9},{2,6},{6,2},{1... | collective-permute-start | bytes 196616 | tf_op jit(solution)/shard_map/ppermute | solution.py:206
  45.5 2.2 %shard_map.89.refs_8_.weight = bf16[2048,1024]{1,0:T(8,128)(2,1)S(1)} custom-call(bf16[4096,2048]{1,0:T(8,128)(2,1)} %weight.5, bf16[16,2048]{1,0:T(8,128)(2,1)S(1)} %get-tuple-element.48.attended.refs_1_), custom_call_target="tpu_custom_call" | custom-call | bytes 4194304 | tf_op jit(solution)/shard_map/pallas_call | solution.py:658
  47.7 0.8 %shard_map.90 = (bf16[128,1024]{1,0:T(8,128)(2,1)S(1)}, bf16[128,2048]{1,0:T(8,128)(2,1)S(1)}) custom-call(bf16[128,128]{1,0:T(8,128)(2,1)S(1)} %get-tuple-element.49.chosen, bf16[16,2048]{1,0:T(8,128)(2,1)S(1)} %get-tuple-element.47.refs_0_, bf16[16,2048]{1,0:T(8,128)(2,1)S(1)} %get-tuple-element.48.attended.refs_1_, ...), custom_call_target="tpu_custom_call" | custom-call | flops 536870912 | bytes 4194304 | tf_op jit(solution)/shard_map/pallas_call | solution.py:397
  48.6 0.0 copy-start
  48.6 0.1 collective-permute-start.17
  48.7 0.7 %shard_map.91.own = f32[128,1024]{1,0:T(8,128)S(1)} custom-call(bf16[128,2048]{1,0:T(8,128)(2,1)S(1)} %get-tuple-element.51.permuted, bf16[2048,1024]{1,0:T(8,128)(2,1)S(1)} %shard_map.89.refs_8_.weight), custom_call_target="tpu_custom_call" | custom-call | flops 536870912 | bytes 4194304 | tf_op jit(solution)/shard_map/pallas_call | solution.py:406
  49.4 0.8 %collective-permute-done.17.received = bf16[128,1024]{1,0:T(8,128)(2,1)S(1)} collective-permute-done((bf16[128,1024]{1,0:T(8,128)(2,1)S(1)}, bf16[128,1024]{1,0:T(8,128)(2,1)S(1)}, u32[]{:S(2)}, u32[]{:S(2)}) %collective-permute-start.17) | collective-permute-done | bytes 262176 | tf_op jit(solution)/shard_map/ppermute | solution.py:206
  50.3 1.5 %collective-permute-start.18 = (bf16[32,1024]{1,0:T(8,128)(2,1)S(1)}, bf16[32,1024]{1,0:T(8,128)(2,1)S(1)}, u32[]{:S(2)}, u32[]{:S(2)}) collective-permute-start(bf16[32,1024]{1,0:T(8,128)(2,1)S(1)} %get-tuple-element.53), channel_id=1, source_target_pairs={{0,8},{4,12},{8,0},{12,4},{1,9},{5,13},{9,1},{13,5},{2,10},{6,14},... | collective-permute-start | bytes 196616 | tf_op jit(solution)/shard_map/ppermute | solution.py:206
  51.7 2.9 %collective-permute-start.19 = (bf16[32,1024]{1,0:T(8,128)(2,1)S(1)}, bf16[32,1024]{1,0:T(8,128)(2,1)S(1)}, u32[]{:S(2)}, u32[]{:S(2)}) collective-permute-start(bf16[32,1024]{1,0:T(8,128)(2,1)S(1)} %get-tuple-element.54), channel_id=1, source_target_pairs={{0,12},{2,4},{4,8},{6,0},{8,14},{10,6},{12,10},{14,2},{1,13},{3,5}... | collective-permute-start | bytes 196616 | tf_op jit(solution)/shard_map/ppermute | solution.py:452
  54.7 1.5 %collective-permute-done.18.passed.refs_2_ = bf16[32,1024]{1,0:T(8,128)(2,1)S(1)} collective-permute-done((bf16[32,1024]{1,0:T(8,128)(2,1)S(1)}, bf16[32,1024]{1,0:T(8,128)(2,1)S(1)}, u32[]{:S(2)}, u32[]{:S(2)}) %collective-permute-start.18) | collective-permute-done | bytes 65568 | tf_op jit(solution)/shard_map/ppermute | solution.py:206
  56.2 1.8 %collective-permute-start.21 = (bf16[32,1024]{1,0:T(8,128)(2,1)S(1)}, bf16[32,1024]{1,0:T(8,128)(2,1)S(1)}, u32[]{:S(2)}, u32[]{:S(2)}) collective-permute-start(bf16[32,1024]{1,0:T(8,128)(2,1)S(1)} %shard_map.93), channel_id=1, source_target_pairs={{0,2},{2,0},{1,3},{3,1},{4,6},{6,4},{5,7},{7,5},{8,10},{10,8},{9,1... | collective-permute-start | bytes 196616 | tf_op jit(solution)/shard_map/ppermute | solution.py:206
  58.0 2.2 %collective-permute-done.20.refs_4_ = bf16[32,1024]{1,0:T(8,128)(2,1)S(1)} collective-permute-done((bf16[32,1024]{1,0:T(8,128)(2,1)S(1)}, bf16[32,1024]{1,0:T(8,128)(2,1)S(1)}, u32[]{:S(2)}, u32[]{:S(2)}) %collective-permute-start.20) | collective-permute-done | bytes 65568 | tf_op jit(solution)/shard_map/ppermute | solution.py:452
  60.2 0.3 collective-permute-done.21.refs_6_
  60.5 0.1 shard_map.94
  60.6 0.1 collective-permute-start.22
  60.7 1.3 %collective-permute-done.22.received = bf16[32,2048]{1,0:T(8,128)(2,1)S(1)} collective-permute-done((bf16[32,2048]{1,0:T(8,128)(2,1)S(1)}, bf16[32,2048]{1,0:T(8,128)(2,1)S(1)}, u32[]{:S(2)}, u32[]{:S(2)}) %collective-permute-start.22) | collective-permute-done | bytes 131104 | tf_op jit(solution)/shard_map/ppermute | solution.py:206
  62.0 0.7 %shard_map.95 = bf16[1,32,4096]{2,1,0:T(8,128)(2,1)} custom-call(bf16[32,2048]{1,0:T(8,128)(2,1)S(1)} %get-tuple-element.57.keep, bf16[32,2048]{1,0:T(8,128)(2,1)S(1)} %collective-permute-done.22.received), custom_call_target="tpu_custom_call" | custom-call | bytes 524288 | tf_op jit(solution)/shard_map/pallas_call | solution.py:679
  (21 shorter events, 0.1 us)
Async XLA Ops:
  0.9 7.9 %collective-permute-start.2 = (bf16[16,2048]{1,0:T(8,128)(2,1)S(1)}, bf16[16,2048]{1,0:T(8,128)(2,1)S(1)}, u32[]{:S(2)}, u32[]{:S(2)}) collective-permute-start(bf16[16,2048]{1,0:T(8,128)(2,1)S(1)} %get-tuple-element.60.refs_0_), channel_id=1, source_target_pairs={{0,8},{4,12},{8,0},{12,4},{1,9},{5,13},{9,1},{13,5},{2,10},{6,14},... | collective-permute-start | bytes 196616 | tf_op jit(solution)/shard_map/ppermute | solution.py:206
  5.0 11.5 %copy-start.1 = (bf16[4096]{0:T(1024)(128)(2,1)S(1)}, bf16[4096]{0:T(1024)(128)(2,1)}, u32[]{:S(2)}) copy-start(bf16[4096]{0:T(1024)(128)(2,1)} %param.9) | copy-start | bytes 24580
  5.0 6.1 %collective-permute-start.3 = (bf16[16,2048]{1,0:T(8,128)(2,1)S(1)}, bf16[16,2048]{1,0:T(8,128)(2,1)S(1)}, u32[]{:S(2)}, u32[]{:S(2)}) collective-permute-start(bf16[16,2048]{1,0:T(8,128)(2,1)S(1)} %get-tuple-element.59.refs_1_), channel_id=1, source_target_pairs={{0,8},{4,12},{8,0},{12,4},{1,9},{5,13},{9,1},{13,5},{2,10},{6,14},... | collective-permute-start | bytes 196616 | tf_op jit(solution)/shard_map/ppermute | solution.py:206
  5.1 11.4 %collective-permute-start = (bf16[16,2048]{1,0:T(8,128)(2,1)S(1)}, bf16[16,2048]{1,0:T(8,128)(2,1)S(1)}, u32[]{:S(2)}, u32[]{:S(2)}) collective-permute-start(bf16[16,2048]{1,0:T(8,128)(2,1)S(1)} %get-tuple-element.60.refs_0_), channel_id=1, source_target_pairs={{0,4},{4,0},{8,12},{12,8},{1,5},{5,1},{9,13},{13,9},{2,6},{6,2},{1... | collective-permute-start | bytes 196616 | tf_op jit(solution)/shard_map/ppermute | solution.py:206
  6.9 9.6 %collective-permute-start.1 = (bf16[16,2048]{1,0:T(8,128)(2,1)S(1)}, bf16[16,2048]{1,0:T(8,128)(2,1)S(1)}, u32[]{:S(2)}, u32[]{:S(2)}) collective-permute-start(bf16[16,2048]{1,0:T(8,128)(2,1)S(1)} %get-tuple-element.59.refs_1_), channel_id=1, source_target_pairs={{0,4},{4,0},{8,12},{12,8},{1,5},{5,1},{9,13},{13,9},{2,6},{6,2},{1... | collective-permute-start | bytes 196616 | tf_op jit(solution)/shard_map/ppermute | solution.py:206
  8.7 7.8 %collective-permute-start.4 = (bf16[16,2048]{1,0:T(8,128)(2,1)S(1)}, bf16[16,2048]{1,0:T(8,128)(2,1)S(1)}, u32[]{:S(2)}, u32[]{:S(2)}) collective-permute-start(bf16[16,2048]{1,0:T(8,128)(2,1)S(1)} %collective-permute-done.2.refs_4_), channel_id=1, source_target_pairs={{0,4},{4,0},{8,12},{12,8},{1,5},{5,1},{9,13},{13,9},{2,6},{6,2},{1... | collective-permute-start | bytes 196616 | tf_op jit(solution)/shard_map/ppermute | solution.py:206
  11.1 5.4 %collective-permute-start.5 = (bf16[16,2048]{1,0:T(8,128)(2,1)S(1)}, bf16[16,2048]{1,0:T(8,128)(2,1)S(1)}, u32[]{:S(2)}, u32[]{:S(2)}) collective-permute-start(bf16[16,2048]{1,0:T(8,128)(2,1)S(1)} %collective-permute-done.3.refs_5_), channel_id=1, source_target_pairs={{0,4},{4,0},{8,12},{12,8},{1,5},{5,1},{9,13},{13,9},{2,6},{6,2},{1... | collective-permute-start | bytes 196616 | tf_op jit(solution)/shard_map/ppermute | solution.py:206
  17.6 12.8 %copy-start.2 = (s32[128]{0:T(128)S(1)}, s32[128]{0:T(128)}, u32[]{:S(2)}) copy-start(s32[128]{0:T(128)} %slots.3) | copy-start | bytes 1540
  17.6 12.7 %copy-start.3 = (s32[32]{0:T(128)S(1)}, s32[32]{0:T(128)}, u32[]{:S(2)}) copy-start(s32[32]{0:T(128)} %lengths.1) | copy-start | bytes 388
  17.6 1.7 %collective-permute-start.6 = (bf16[128,1408]{1,0:T(8,128)(2,1)S(1)}, bf16[128,1408]{1,0:T(8,128)(2,1)S(1)}, u32[]{:S(2)}, u32[]{:S(2)}) collective-permute-start(bf16[128,1408]{1,0:T(8,128)(2,1)S(1)} %get-tuple-element.39.given), channel_id=1, source_target_pairs={{0,1},{1,0},{2,3},{3,2},{4,5},{5,4},{6,7},{7,6},{8,9},{9,8},{10,11... | collective-permute-start | bytes 1081352 | tf_op jit(solution)/shard_map/ppermute | solution.py:206
  19.5 7.8 %collective-permute-start.7 = (bf16[32,1280]{1,0:T(8,128)(2,1)S(1)}, bf16[32,1280]{1,0:T(8,128)(2,1)S(1)}, u32[]{:S(2)}, u32[]{:S(2)}) collective-permute-start(bf16[32,1280]{1,0:T(8,128)(2,1)S(1)} %get-tuple-element.40), channel_id=1, source_target_pairs={{0,8},{4,12},{8,0},{12,4},{1,9},{5,13},{9,1},{13,5},{2,10},{6,14},... | collective-permute-start | bytes 245768 | tf_op jit(solution)/shard_map/ppermute | solution.py:206
  22.7 11.4 %collective-permute-start.8 = (bf16[32,1408]{1,0:T(8,128)(2,1)S(1)}, bf16[32,1408]{1,0:T(8,128)(2,1)S(1)}, u32[]{:S(2)}, u32[]{:S(2)}) collective-permute-start(bf16[32,1408]{1,0:T(8,128)(2,1)S(1)} %get-tuple-element.41), channel_id=1, source_target_pairs={{0,12},{2,4},{4,8},{6,0},{8,14},{10,6},{12,10},{14,2},{1,13},{3,5}... | collective-permute-start | bytes 270344 | tf_op jit(solution)/shard_map/ppermute | solution.py:452
  22.9 11.2 %collective-permute-start.9 = (bf16[32,1408]{1,0:T(8,128)(2,1)S(1)}, bf16[32,1408]{1,0:T(8,128)(2,1)S(1)}, u32[]{:S(2)}, u32[]{:S(2)}) collective-permute-start(bf16[32,1408]{1,0:T(8,128)(2,1)S(1)} %get-tuple-element.42), channel_id=1, source_target_pairs={{0,4},{2,12},{4,0},{6,8},{8,6},{10,14},{12,2},{14,10},{1,5},{3,13}... | collective-permute-start | bytes 270344 | tf_op jit(solution)/shard_map/ppermute | solution.py:452
  27.3 6.8 %collective-permute-start.10 = (bf16[32,1280]{1,0:T(8,128)(2,1)S(1)}, bf16[32,1280]{1,0:T(8,128)(2,1)S(1)}, u32[]{:S(2)}, u32[]{:S(2)}) collective-permute-start(bf16[32,1280]{1,0:T(8,128)(2,1)S(1)} %shard_map.87), channel_id=1, source_target_pairs={{0,2},{2,0},{1,3},{3,1},{4,6},{6,4},{5,7},{7,5},{8,10},{10,8},{9,1... | collective-permute-start | bytes 245768 | tf_op jit(solution)/shard_map/ppermute | solution.py:206
  35.9 5.8 %collective-permute-start.13 = (bf16[16,2048]{1,0:T(8,128)(2,1)S(1)}, bf16[16,2048]{1,0:T(8,128)(2,1)S(1)}, u32[]{:S(2)}, u32[]{:S(2)}) collective-permute-start(bf16[16,2048]{1,0:T(8,128)(2,1)S(1)} %get-tuple-element.47.refs_0_), channel_id=1, source_target_pairs={{0,8},{4,12},{8,0},{12,4},{1,9},{5,13},{9,1},{13,5},{2,10},{6,14},... | collective-permute-start | bytes 196616 | tf_op jit(solution)/shard_map/ppermute | solution.py:206
  36.3 6.3 %collective-permute-start.14 = (bf16[16,2048]{1,0:T(8,128)(2,1)S(1)}, bf16[16,2048]{1,0:T(8,128)(2,1)S(1)}, u32[]{:S(2)}, u32[]{:S(2)}) collective-permute-start(bf16[16,2048]{1,0:T(8,128)(2,1)S(1)} %get-tuple-element.48.attended.refs_1_), channel_id=1, source_target_pairs={{0,8},{4,12},{8,0},{12,4},{1,9},{5,13},{9,1},{13,5},{2,10},{6,14},... | collective-permute-start | bytes 196616 | tf_op jit(solution)/shard_map/ppermute | solution.py:206
  38.9 8.8 %collective-permute-start.11 = (bf16[16,2048]{1,0:T(8,128)(2,1)S(1)}, bf16[16,2048]{1,0:T(8,128)(2,1)S(1)}, u32[]{:S(2)}, u32[]{:S(2)}) collective-permute-start(bf16[16,2048]{1,0:T(8,128)(2,1)S(1)} %get-tuple-element.47.refs_0_), channel_id=1, source_target_pairs={{0,4},{4,0},{8,12},{12,8},{1,5},{5,1},{9,13},{13,9},{2,6},{6,2},{1... | collective-permute-start | bytes 196616 | tf_op jit(solution)/shard_map/ppermute | solution.py:206
  39.7 8.0 %collective-permute-start.12 = (bf16[16,2048]{1,0:T(8,128)(2,1)S(1)}, bf16[16,2048]{1,0:T(8,128)(2,1)S(1)}, u32[]{:S(2)}, u32[]{:S(2)}) collective-permute-start(bf16[16,2048]{1,0:T(8,128)(2,1)S(1)} %get-tuple-element.48.attended.refs_1_), channel_id=1, source_target_pairs={{0,4},{4,0},{8,12},{12,8},{1,5},{5,1},{9,13},{13,9},{2,6},{6,2},{1... | collective-permute-start | bytes 196616 | tf_op jit(solution)/shard_map/ppermute | solution.py:206
  41.7 6.0 %collective-permute-start.15 = (bf16[16,2048]{1,0:T(8,128)(2,1)S(1)}, bf16[16,2048]{1,0:T(8,128)(2,1)S(1)}, u32[]{:S(2)}, u32[]{:S(2)}) collective-permute-start(bf16[16,2048]{1,0:T(8,128)(2,1)S(1)} %collective-permute-done.13.refs_4_), channel_id=1, source_target_pairs={{0,4},{4,0},{8,12},{12,8},{1,5},{5,1},{9,13},{13,9},{2,6},{6,2},{1... | collective-permute-start | bytes 196616 | tf_op jit(solution)/shard_map/ppermute | solution.py:206
  42.6 5.1 %collective-permute-start.16 = (bf16[16,2048]{1,0:T(8,128)(2,1)S(1)}, bf16[16,2048]{1,0:T(8,128)(2,1)S(1)}, u32[]{:S(2)}, u32[]{:S(2)}) collective-permute-start(bf16[16,2048]{1,0:T(8,128)(2,1)S(1)} %collective-permute-done.14.refs_5_), channel_id=1, source_target_pairs={{0,4},{4,0},{8,12},{12,8},{1,5},{5,1},{9,13},{13,9},{2,6},{6,2},{1... | collective-permute-start | bytes 196616 | tf_op jit(solution)/shard_map/ppermute | solution.py:206
  48.6 11.9 %copy-start = (bf16[32,4096]{1,0:T(8,128)(2,1)S(1)}, bf16[32,4096]{1,0:T(8,128)(2,1)}, u32[]{:S(2)}) copy-start(bf16[32,4096]{1,0:T(8,128)(2,1)} %hidden.1) | copy-start | bytes 786436
  48.6 1.6 %collective-permute-start.17 = (bf16[128,1024]{1,0:T(8,128)(2,1)S(1)}, bf16[128,1024]{1,0:T(8,128)(2,1)S(1)}, u32[]{:S(2)}, u32[]{:S(2)}) collective-permute-start(bf16[128,1024]{1,0:T(8,128)(2,1)S(1)} %get-tuple-element.52.given), channel_id=1, source_target_pairs={{0,1},{1,0},{2,3},{3,2},{4,5},{5,4},{6,7},{7,6},{8,9},{9,8},{10,11... | collective-permute-start | bytes 786440 | tf_op jit(solution)/shard_map/ppermute | solution.py:206
  50.3 5.9 %collective-permute-start.18 = (bf16[32,1024]{1,0:T(8,128)(2,1)S(1)}, bf16[32,1024]{1,0:T(8,128)(2,1)S(1)}, u32[]{:S(2)}, u32[]{:S(2)}) collective-permute-start(bf16[32,1024]{1,0:T(8,128)(2,1)S(1)} %get-tuple-element.53), channel_id=1, source_target_pairs={{0,8},{4,12},{8,0},{12,4},{1,9},{5,13},{9,1},{13,5},{2,10},{6,14},... | collective-permute-start | bytes 196616 | tf_op jit(solution)/shard_map/ppermute | solution.py:206
  51.7 6.3 %collective-permute-start.19 = (bf16[32,1024]{1,0:T(8,128)(2,1)S(1)}, bf16[32,1024]{1,0:T(8,128)(2,1)S(1)}, u32[]{:S(2)}, u32[]{:S(2)}) collective-permute-start(bf16[32,1024]{1,0:T(8,128)(2,1)S(1)} %get-tuple-element.54), channel_id=1, source_target_pairs={{0,12},{2,4},{4,8},{6,0},{8,14},{10,6},{12,10},{14,2},{1,13},{3,5}... | collective-permute-start | bytes 196616 | tf_op jit(solution)/shard_map/ppermute | solution.py:452
  54.7 5.5 %collective-permute-start.20 = (bf16[32,1024]{1,0:T(8,128)(2,1)S(1)}, bf16[32,1024]{1,0:T(8,128)(2,1)S(1)}, u32[]{:S(2)}, u32[]{:S(2)}) collective-permute-start(bf16[32,1024]{1,0:T(8,128)(2,1)S(1)} %get-tuple-element.55), channel_id=1, source_target_pairs={{0,4},{2,12},{4,0},{6,8},{8,6},{10,14},{12,2},{14,10},{1,5},{3,13}... | collective-permute-start | bytes 196616 | tf_op jit(solution)/shard_map/ppermute | solution.py:452
  56.2 4.3 %collective-permute-start.21 = (bf16[32,1024]{1,0:T(8,128)(2,1)S(1)}, bf16[32,1024]{1,0:T(8,128)(2,1)S(1)}, u32[]{:S(2)}, u32[]{:S(2)}) collective-permute-start(bf16[32,1024]{1,0:T(8,128)(2,1)S(1)} %shard_map.93), channel_id=1, source_target_pairs={{0,2},{2,0},{1,3},{3,1},{4,6},{6,4},{5,7},{7,5},{8,10},{10,8},{9,1... | collective-permute-start | bytes 196616 | tf_op jit(solution)/shard_map/ppermute | solution.py:206
  60.6 1.4 %collective-permute-start.22 = (bf16[32,2048]{1,0:T(8,128)(2,1)S(1)}, bf16[32,2048]{1,0:T(8,128)(2,1)S(1)}, u32[]{:S(2)}, u32[]{:S(2)}) collective-permute-start(bf16[32,2048]{1,0:T(8,128)(2,1)S(1)} %get-tuple-element.58), channel_id=1, source_target_pairs={{0,1},{1,0},{2,3},{3,2},{4,5},{5,4},{6,7},{7,6},{8,9},{9,8},{10,11... | collective-permute-start | bytes 393224 | tf_op jit(solution)/shard_map/ppermute | solution.py:206

commit v17 on v16

--- a/solution.py
+++ b/solution.py
@@ -263,8 +263,8 @@
     return copies
 
 
-def stage_rest_kernel(blocks, lengths, weight, keys, values, slots, *refs):
-    target, key_part, value_part, cosine, sine, length_of, chosen, scratch, sems = refs
+def stage_cache_kernel(blocks, lengths, keys, values, slots, *refs):
+    key_part, value_part, cosine, sine, length_of, chosen, scratch, sems = refs
     side, col = position()
     copies = []
     for j in range(key_part.shape[2] // HEAD_DIM):
@@ -276,11 +276,15 @@
                     part.at[:, :, pl.ds(j * HEAD_DIM, HEAD_DIM)],
                 )
             )
-    copies = started(copies + head_copies(weight, target, 1 - side), sems)
+    copies = started(copies, sems)
     cosine[...], sine[...], length_of[...] = rope(lengths, cosine.shape[0])
     chosen[...] = one_hot(slots, scratch, blocks, col, col).T.astype(jnp.bfloat16)
     for copy in copies:
         copy.wait()
+
+
+def stage_give_kernel(weight, give_part, sems):
+    run_copies(head_copies(weight, give_part, 1 - lax.axis_index("side")), sems)
 
 
 def stage_out_kernel(weight, attended, own_part, sems):
@@ -390,8 +394,8 @@
 def project(kernel, chosen, pieces_in, extra, weights, more):
     count = lax.axis_size("col")
     parts = len(pieces_in)
-    rows, depth = pieces_in[0].shape
-    rows = rows * parts
+    depth = pieces_in[0].shape[1]
+    rows = sum(part.shape[0] for part in pieces_in)
     half = weights[0].shape[1]
     flops = 2 * rows * depth * half
     give, permuted = call(
@@ -425,19 +429,25 @@
     return merged[:count], merged[count:]
 
 
-def gathered(parts, axis):
+def gathered(parts, axis, whole=None):
     blocks = {0: parts}
     mask = lax.axis_size(axis) // 2
     while mask:
         blocks |= {
-            known | mask: [moved(part, axis, mask) for part in block]
+            known | mask: [
+                moved(part, axis, mask)
+                for part in ([whole] if mask == 1 and known == 0 and whole is not None else block)
+            ]
             for known, block in blocks.items()
         }
         mask //= 2
+    if whole is not None:
+        blocks[0] = [whole]
     return [part for i in sorted(blocks) for part in blocks[i]]
 
 
-def choose_kernel(own, passed, out):
+def choose_kernel(own, passed, *refs):
+    out = refs[-1]
     out[...] = jnp.where(at_home(), passed[...], own[...])
 
 
@@ -452,7 +462,7 @@
     return lax.ppermute(value, ("col", "row"), moves)
 
 
-def spread(products):
+def spread(products, ready):
     own, passed, *rest = products
     pairs = len(products) // 2
     passed = moved(passed, "col", pairs)
@@ -463,8 +473,13 @@
             direct(rest[2 * pair - 1], False, pair),
         ]
     crossing = call(
-        choose_kernel, struct(own.shape), [VMEM] * 2, VMEM, 0, own.size * 4
-    )(own, passed)
+        choose_kernel,
+        struct(own.shape),
+        [VMEM] * 2 + [HBM] * len(ready),
+        VMEM,
+        0,
+        own.size * 4,
+    )(own, passed, *ready)
     return [passed, *blocks, own, moved(crossing, "row", 1)]
 
 
@@ -494,10 +509,10 @@
     return jnp.cos(phases), jnp.where(lane < half, -sine, sine), length_of
 
 
-def attend_all(count, parts, cosine, sine, lengths, *refs):
+def attend_all(count, parts, ready, cosine, sine, lengths, *refs):
     pairs = (count - 1) // 2
     blocks, (sums, keys, values), refs = refs[:count], refs[count : count + 3], refs[count + 3 :]
-    outs, (scores_of, probs_of) = refs[:parts], refs[parts:]
+    whole, outs, (scores_of, probs_of) = refs[0], refs[1 : parts + 1], refs[parts + 1 :]
     rows, cache = keys.shape[:2]
     low = lax.rem(lax.axis_index("col"), pairs)
     width = GROUP_WIDTH
@@ -564,11 +579,14 @@
                 joined = jnp.concatenate(
                     [result[head] for result in results[i * size : (i + 1) * size]], axis=0
                 )
-                out[:, pl.ds(at, HEAD_DIM)] = joined.astype(jnp.bfloat16)
-
-
-def sum_kernel(count, parts, hidden, *refs):
-    attended, blocks, (keep, send) = refs[:parts], refs[parts : parts + count], refs[-2:]
+                joined = joined.astype(jnp.bfloat16)
+                out[:, pl.ds(at, HEAD_DIM)] = joined
+                run = slice(i * joined.shape[0], (i + 1) * joined.shape[0])
+                whole[run, pl.ds(at, HEAD_DIM)] = joined
+
+
+def sum_kernel(count, hidden, attended, *refs):
+    blocks, (keep, send) = refs[:count], refs[count:]
     rows, width = blocks[0].shape
     pairs = keep.shape[1] // width
     side = lax.axis_index("side")
@@ -579,7 +597,7 @@
         at = pl.ds(pl.multiple_of((2 * column + side) * width, width), width)
         hidden_out = (hidden[:, at].astype(jnp.float32) + total).astype(jnp.bfloat16)
         at = pl.ds(pl.multiple_of(column * width, width), width)
-        attention = jnp.concatenate([part[:, at] for part in attended], axis=0)
+        attention = attended[:, at]
         keep[:, at] = jnp.where(side == 0, hidden_out, attention)
         send[:, at] = jnp.where(side == 0, attention, hidden_out)
 
@@ -629,31 +647,39 @@
     blocks = gathered(
         [own_part[i * piece : (i + 1) * piece] for i in range(parts)], "col"
     )
+    table = struct((rows, HEAD_DIM), jnp.float32)
+    key_part, value_part, *tables, chosen_out = call(
+        functools.partial(stage_cache_kernel, col_count),
+        [pltpu.VMEM((rows, cache, pairs * HEAD_DIM), jnp.bfloat16)] * 2
+        + [table, table, struct((rows, HEAD_DIM), jnp.int32), struct(square)],
+        [SMEM, HBM, HBM, VMEM],
+        [VMEM] * 6,
+        0,
+        4 * rows * cache * pairs * HEAD_DIM,
+        [pltpu.VMEM(square, jnp.float32), pltpu.SemaphoreType.DMA((2 * pairs,))],
+    )(cache_lengths, in_hbm(key_cache), in_hbm(value_cache), slot_request)
     products, sums = project(in_kernel, chosen_in, blocks, [gain], [give_in, own_in], HEAD_DIM)
-    products = spread(products)
-
-    table = struct((rows, HEAD_DIM), jnp.float32)
-    give_out, key_part, value_part, *tables, chosen_out = call(
-        functools.partial(stage_rest_kernel, col_count),
-        [pltpu.VMEM((half, half_out), jnp.bfloat16)]
-        + [pltpu.VMEM((rows, cache, pairs * HEAD_DIM), jnp.bfloat16)] * 2
-        + [table, table, struct((rows, HEAD_DIM), jnp.int32), struct(square)],
-        [SMEM, HBM, HBM, HBM, VMEM],
-        [VMEM] * 7,
+    products = spread(products, [chosen_out])
+
+    give_out = call(
+        stage_give_kernel,
+        pltpu.VMEM((half, half_out), jnp.bfloat16),
+        [HBM],
+        VMEM,
         0,
-        half * half_out * 2 + 4 * rows * cache * pairs * HEAD_DIM,
-        [pltpu.VMEM(square, jnp.float32), pltpu.SemaphoreType.DMA((3 * pairs,))],
-    )(cache_lengths, in_hbm(out_weight), in_hbm(key_cache), in_hbm(value_cache), slot_request)
+        half * half_out * 2,
+        [pltpu.SemaphoreType.DMA((pairs,))],
+    )(in_hbm(out_weight))
     runs = (pairs, rows // SLOTS, GROUP * SLOTS, SLOTS * cache)
-    attended = call(
+    attended, *attended_parts = call(
         functools.partial(attend_all, len(products), parts),
-        [struct((piece, half))] * parts,
-        [VMEM] * (len(products) + 6),
-        [VMEM] * parts,
+        [struct((rows, half))] + [struct((piece, half))] * parts,
+        [HBM] + [VMEM] * (len(products) + 6),
+        [VMEM] * (parts + 1),
         4 * rows * half * cache,
         0,
         [pltpu.VMEM(runs, jnp.float32), pltpu.VMEM(runs, jnp.bfloat16)],
-    )(*tables, *products, *sums, in_vmem(key_part), in_vmem(value_part))
+    )(give_out, *tables, *products, *sums, in_vmem(key_part), in_vmem(value_part))
 
     own_out = call(
         stage_out_kernel,
@@ -663,19 +689,19 @@
         0,
         half * half_out * 2,
         [pltpu.SemaphoreType.DMA((pairs,))],
-    )(in_hbm(out_weight), attended[-1])
+    )(in_hbm(out_weight), attended)
     products, _ = project(
-        out_kernel, chosen_out, gathered(attended, "col"), [], [give_out, own_out], 0
-    )
-    products = spread(products)
+        out_kernel, chosen_out, gathered(attended_parts, "col", attended), [], [give_out, own_out], 0
+    )
+    products = spread(products, [])
     keep, send = call(
-        functools.partial(sum_kernel, len(products), parts),
+        functools.partial(sum_kernel, len(products)),
         [struct((rows, half)), struct((rows, half))],
-        [VMEM] * (1 + parts + len(products)),
+        [VMEM] * (2 + len(products)),
         [VMEM, VMEM],
         rows * depth * 4,
         rows * depth * 8,
-    )(hidden_in, *attended, *products)
+    )(hidden_in, attended, *products)
     return call(
         join_kernel,
         struct((1, rows, depth)),

time: 62.9 us -> 63.2 us (level)
  waiting for transfers between devices: 13.8 us -> 11.5 us
  starting transfers between devices: 31.5 us -> 33.3 us
  Pallas kernels: 16.3 us -> 17.1 us
    ppermute x19 -> x18, starting transfers between devices: 27.9 us -> 30.3 us  [moved(): return lax.ppermute(value, axis, pairs)]
    ppermute x19 -> x18, waiting for transfers between devices: 11.5 us -> 9.85 us  [moved(): return lax.ppermute(value, axis, pairs)]
    pallas_call x5 -> x6, Pallas kernels: 5.62 us -> 6.4 us  [the longest x1 2.26 us: paired_plan(): call(functools.partial(stage_cache_kernel, col_count), [pltpu.VMEM((rows,...]
    ppermute x4, starting transfers between devices: 3.66 us -> 2.97 us  [direct(): return lax.ppermute(value, ('col', 'row'), moves)]
  transfers between devices with their start and end apart: 23 -> 22, of which waited for: 10 -> 12; matrix products, arithmetic and copies ran while one was open for 0% -> 0% of each run, Pallas kernels for 19% -> 20%
where the time goes in v17:
time: 63.2 us; the launch traced here: 63 us
  starting transfers between devices  33.3 us (53%)
  Pallas kernels  17.1 us (27%)
  waiting for transfers between devices  11.5 us (18%)
  local copies, waits for them, and re-layouts  0.9 us (1%)
    ppermute x18, starting transfers between devices, moved(): return lax.ppermute(value, axis, pairs)  30.3 us
    ppermute x18, waiting for transfers between devices, moved(): return lax.ppermute(value, axis, pairs)  9.85 us
    pallas_call x1, Pallas kernels, paired_plan(): call(functools.partial(stage_in_kernel, col_count), [pltpu.VMEM((half, ha...  4.09 us
    ppermute x4, starting transfers between devices, direct(): return lax.ppermute(value, ('col', 'row'), moves)  2.97 us
    pallas_call x1, Pallas kernels, paired_plan(): call(functools.partial(stage_cache_kernel, col_count), [pltpu.VMEM((rows,...  2.26 us
    pallas_call x1, Pallas kernels, paired_plan(): call(stage_give_kernel, pltpu.VMEM((half, half_out), jnp.bfloat16), [HBM]...  2.24 us
    pallas_call x1, Pallas kernels, paired_plan(): call(stage_out_kernel, pltpu.VMEM((half, half_out), jnp.bfloat16), [HBM,...  2.24 us
    pallas_call x2, Pallas kernels, project(): call(functools.partial(kernel, parts), [struct((rows, half + more)), stru...  1.92 us
  transfers between devices with their start and end apart: 22, of which 12 were waited for; matrix products, arithmetic and copies ran while one was open for 0% of the time, Pallas kernels for 20%

profile of v17, /device:TPU:0, one launch (start us, length us, event | category | flops | bytes accessed | tf_op | source)
XLA Modules:
  0.0 63.0 jit_solution(5105783762989451712)
XLA Ops:
  0.0 0.9 %fusion = (bf16[16,2048]{1,0:T(8,128)(2,1)S(1)}, bf16[16,2048]{1,0:T(8,128)(2,1)S(1)}) fusion(bf16[32,4096]{1,0:T(8,128)(2,1)} %hidden.1, s32[]{:T(128)S(6)} %add.4, s32[]{:T(128)S(6)} %select_n.3), kind=kLoop, calls=%fused_computation.1 | loop fusion | bytes 262152 | tf_op jit(solution)/shard_map/slice | solution.py:648
  0.9 4.1 %collective-permute-start.2 = (bf16[16,2048]{1,0:T(8,128)(2,1)S(1)}, bf16[16,2048]{1,0:T(8,128)(2,1)S(1)}, u32[]{:S(2)}, u32[]{:S(2)}) collective-permute-start(bf16[16,2048]{1,0:T(8,128)(2,1)S(1)} %get-tuple-element.60.refs_0_), channel_id=1, source_target_pairs={{0,8},{4,12},{8,0},{12,4},{1,9},{5,13},{9,1},{13,5},{2,10},{6,14},... | collective-permute-start | bytes 196616 | tf_op jit(solution)/shard_map/ppermute | solution.py:206
  5.0 0.1 collective-permute-start.3
  5.1 1.8 %collective-permute-start = (bf16[16,2048]{1,0:T(8,128)(2,1)S(1)}, bf16[16,2048]{1,0:T(8,128)(2,1)S(1)}, u32[]{:S(2)}, u32[]{:S(2)}) collective-permute-start(bf16[16,2048]{1,0:T(8,128)(2,1)S(1)} %get-tuple-element.60.refs_0_), channel_id=1, source_target_pairs={{0,4},{4,0},{8,12},{12,8},{1,5},{5,1},{9,13},{13,9},{2,6},{6,2},{1... | collective-permute-start | bytes 196616 | tf_op jit(solution)/shard_map/ppermute | solution.py:206
  6.9 0.2 collective-permute-start.1
  7.1 1.6 %collective-permute-done.2.refs_4_ = bf16[16,2048]{1,0:T(8,128)(2,1)S(1)} collective-permute-done((bf16[16,2048]{1,0:T(8,128)(2,1)S(1)}, bf16[16,2048]{1,0:T(8,128)(2,1)S(1)}, u32[]{:S(2)}, u32[]{:S(2)}) %collective-permute-start.2) | collective-permute-done | bytes 65568 | tf_op jit(solution)/shard_map/ppermute | solution.py:206
  8.7 1.9 %collective-permute-start.4 = (bf16[16,2048]{1,0:T(8,128)(2,1)S(1)}, bf16[16,2048]{1,0:T(8,128)(2,1)S(1)}, u32[]{:S(2)}, u32[]{:S(2)}) collective-permute-start(bf16[16,2048]{1,0:T(8,128)(2,1)S(1)} %collective-permute-done.2.refs_4_), channel_id=1, source_target_pairs={{0,4},{4,0},{8,12},{12,8},{1,5},{5,1},{9,13},{13,9},{2,6},{6,2},{1... | collective-permute-start | bytes 196616 | tf_op jit(solution)/shard_map/ppermute | solution.py:206
  10.6 0.4 collective-permute-done.3.refs_5_
  11.1 1.3 %collective-permute-start.5 = (bf16[16,2048]{1,0:T(8,128)(2,1)S(1)}, bf16[16,2048]{1,0:T(8,128)(2,1)S(1)}, u32[]{:S(2)}, u32[]{:S(2)}) collective-permute-start(bf16[16,2048]{1,0:T(8,128)(2,1)S(1)} %collective-permute-done.3.refs_5_), channel_id=1, source_target_pairs={{0,4},{4,0},{8,12},{12,8},{1,5},{5,1},{9,13},{13,9},{2,6},{6,2},{1... | collective-permute-start | bytes 196616 | tf_op jit(solution)/shard_map/ppermute | solution.py:206
  12.4 4.1 %shard_map.84 = (bf16[2048,1280]{1,0:T(8,128)(2,1)S(1)}, bf16[2048,1280]{1,0:T(8,128)(2,1)S(1)}, bf16[128,128]{1,0:T(8,128)(2,1)S(1)}) custom-call(bf16[4096,2560]{1,0:T(8,128)(2,1)} %weight.4, s32[128]{0:T(128)} %slots.3), custom_call_target="tpu_custom_call" | custom-call | bytes 10485760 | tf_op jit(solution)/shard_map/pallas_call | solution.py:634
  16.5 1.1 %shard_map.85 = (bf16[128,1408]{1,0:T(8,128)(2,1)S(1)}, bf16[128,2048]{1,0:T(8,128)(2,1)S(1)}) custom-call(bf16[128,128]{1,0:T(8,128)(2,1)S(1)} %get-tuple-element.35.chosen, bf16[16,2048]{1,0:T(8,128)(2,1)S(1)} %get-tuple-element.60.refs_0_, bf16[16,2048]{1,0:T(8,128)(2,1)S(1)} %get-tuple-element.59.refs_1_, ...), custom_call_target="tpu_custom_call" | custom-call | flops 671088640 | bytes 5242880 | tf_op jit(solution)/shard_map/pallas_call | solution.py:401
  17.6 0.0 copy-start.2
  17.6 0.1 collective-permute-start.6
  17.7 0.9 %shard_map.86.own = f32[128,1280]{1,0:T(8,128)S(1)} custom-call(bf16[128,2048]{1,0:T(8,128)(2,1)S(1)} %get-tuple-element.38.permuted, bf16[2048,1280]{1,0:T(8,128)(2,1)S(1)} %get-tuple-element.36.refs_8_.weight), custom_call_target="tpu_custom_call" | custom-call | flops 671088640 | bytes 5242880 | tf_op jit(solution)/shard_map/pallas_call | solution.py:410
  18.6 0.8 %collective-permute-done.6.received = bf16[128,1408]{1,0:T(8,128)(2,1)S(1)} collective-permute-done((bf16[128,1408]{1,0:T(8,128)(2,1)S(1)}, bf16[128,1408]{1,0:T(8,128)(2,1)S(1)}, u32[]{:S(2)}, u32[]{:S(2)}) %collective-permute-start.6) | collective-permute-done | bytes 360480 | tf_op jit(solution)/shard_map/ppermute | solution.py:206
  19.4 0.1 shard_map.87
  19.5 3.2 %collective-permute-start.7 = (bf16[32,1280]{1,0:T(8,128)(2,1)S(1)}, bf16[32,1280]{1,0:T(8,128)(2,1)S(1)}, u32[]{:S(2)}, u32[]{:S(2)}) collective-permute-start(bf16[32,1280]{1,0:T(8,128)(2,1)S(1)} %get-tuple-element.40), channel_id=1, source_target_pairs={{0,8},{4,12},{8,0},{12,4},{1,9},{5,13},{9,1},{13,5},{2,10},{6,14},... | collective-permute-start | bytes 245768 | tf_op jit(solution)/shard_map/ppermute | solution.py:206
  22.7 0.2 collective-permute-start.8
  22.9 0.5 collective-permute-start.9
  23.4 2.3 %shard_map.83 = (bf16[32,64,256]{2,1,0:T(8,128)(2,1)S(1)}, bf16[32,64,256]{2,1,0:T(8,128)(2,1)S(1)}, f32[32,128]{1,0:T(8,128)S(1)}, f32[32,128]{1,0:T(8,128)S(1)...) custom-call(s32[32]{0:T(128)S(1)} %copy-done.3, bf16[32,64,512]{2,1,0:T(8,128)(2,1)} %keys.1, ...), custom_call_target="tpu_custom_call" | custom-call | bytes 2097152 | tf_op jit(solution)/shard_map/pallas_call | solution.py:651
  25.6 1.6 %collective-permute-done.7.passed.refs_0_ = bf16[32,1280]{1,0:T(8,128)(2,1)S(1)} collective-permute-done((bf16[32,1280]{1,0:T(8,128)(2,1)S(1)}, bf16[32,1280]{1,0:T(8,128)(2,1)S(1)}, u32[]{:S(2)}, u32[]{:S(2)}) %collective-permute-start.7) | collective-permute-done | bytes 81952 | tf_op jit(solution)/shard_map/ppermute | solution.py:206
  27.3 3.1 %collective-permute-start.10 = (bf16[32,1280]{1,0:T(8,128)(2,1)S(1)}, bf16[32,1280]{1,0:T(8,128)(2,1)S(1)}, u32[]{:S(2)}, u32[]{:S(2)}) collective-permute-start(bf16[32,1280]{1,0:T(8,128)(2,1)S(1)} %shard_map.88), channel_id=1, source_target_pairs={{0,2},{2,0},{1,3},{3,1},{4,6},{6,4},{5,7},{7,5},{8,10},{10,8},{9,1... | collective-permute-start | bytes 245768 | tf_op jit(solution)/shard_map/ppermute | solution.py:206
  30.4 2.2 %shard_map.82.ready.refs_7_ = bf16[2048,1024]{1,0:T(8,128)(2,1)S(1)} custom-call(bf16[4096,2048]{1,0:T(8,128)(2,1)} %weight.5), custom_call_target="tpu_custom_call" | custom-call | bytes 4194304 | tf_op jit(solution)/shard_map/pallas_call | solution.py:664
  32.6 0.2 collective-permute-done.10.refs_4_
  32.8 1.8 %shard_map.89 = (bf16[32,2048]{1,0:T(8,128)(2,1)S(1)}, bf16[16,2048]{1,0:T(8,128)(2,1)S(1)}, bf16[16,2048]{1,0:T(8,128)(2,1)S(1)}) custom-call(bf16[2048,1024]{1,0:T(8,128)(2,1)S(1)} %shard_map.82.ready.refs_7_, f32[32,128]{1,0:T(8,128)S(1)} %get-tuple-element.32.cosine, f32[32,128]{1,0:T(8,128)S(1)} %get-tuple-element.33.sine, ...), custom_call_target="tpu_custom_call" | custom-call | flops 16777216 | tf_op jit(solution)/shard_map/pallas_call | solution.py:674
  34.6 2.0 %collective-permute-start.12 = (bf16[16,2048]{1,0:T(8,128)(2,1)S(1)}, bf16[16,2048]{1,0:T(8,128)(2,1)S(1)}, u32[]{:S(2)}, u32[]{:S(2)}) collective-permute-start(bf16[16,2048]{1,0:T(8,128)(2,1)S(1)} %get-tuple-element.49), channel_id=1, source_target_pairs={{0,8},{4,12},{8,0},{12,4},{1,9},{5,13},{9,1},{13,5},{2,10},{6,14},... | collective-permute-start | bytes 196616 | tf_op jit(solution)/shard_map/ppermute | solution.py:206
  36.6 1.0 %collective-permute-start.13 = (bf16[16,2048]{1,0:T(8,128)(2,1)S(1)}, bf16[16,2048]{1,0:T(8,128)(2,1)S(1)}, u32[]{:S(2)}, u32[]{:S(2)}) collective-permute-start(bf16[16,2048]{1,0:T(8,128)(2,1)S(1)} %get-tuple-element.50), channel_id=1, source_target_pairs={{0,8},{4,12},{8,0},{12,4},{1,9},{5,13},{9,1},{13,5},{2,10},{6,14},... | collective-permute-start | bytes 196616 | tf_op jit(solution)/shard_map/ppermute | solution.py:206
  37.6 2.1 %collective-permute-start.11 = (bf16[32,2048]{1,0:T(8,128)(2,1)S(1)}, bf16[32,2048]{1,0:T(8,128)(2,1)S(1)}, u32[]{:S(2)}, u32[]{:S(2)}) collective-permute-start(bf16[32,2048]{1,0:T(8,128)(2,1)S(1)} %get-tuple-element.48.attended.refs_0_), channel_id=1, source_target_pairs={{0,4},{4,0},{8,12},{12,8},{1,5},{5,1},{9,13},{13,9},{2,6},{6,2},{1... | collective-permute-start | bytes 393224 | tf_op jit(solution)/shard_map/ppermute | solution.py:206
  39.7 0.9 %collective-permute-done.12.refs_2_ = bf16[16,2048]{1,0:T(8,128)(2,1)S(1)} collective-permute-done((bf16[16,2048]{1,0:T(8,128)(2,1)S(1)}, bf16[16,2048]{1,0:T(8,128)(2,1)S(1)}, u32[]{:S(2)}, u32[]{:S(2)}) %collective-permute-start.12) | collective-permute-done | bytes 65568 | tf_op jit(solution)/shard_map/ppermute | solution.py:206
  40.6 1.9 %collective-permute-start.14 = (bf16[16,2048]{1,0:T(8,128)(2,1)S(1)}, bf16[16,2048]{1,0:T(8,128)(2,1)S(1)}, u32[]{:S(2)}, u32[]{:S(2)}) collective-permute-start(bf16[16,2048]{1,0:T(8,128)(2,1)S(1)} %collective-permute-done.12.refs_2_), channel_id=1, source_target_pairs={{0,4},{4,0},{8,12},{12,8},{1,5},{5,1},{9,13},{13,9},{2,6},{6,2},{1... | collective-permute-start | bytes 196616 | tf_op jit(solution)/shard_map/ppermute | solution.py:206
  42.6 2.8 %collective-permute-start.15 = (bf16[16,2048]{1,0:T(8,128)(2,1)S(1)}, bf16[16,2048]{1,0:T(8,128)(2,1)S(1)}, u32[]{:S(2)}, u32[]{:S(2)}) collective-permute-start(bf16[16,2048]{1,0:T(8,128)(2,1)S(1)} %collective-permute-done.13.refs_3_), channel_id=1, source_target_pairs={{0,4},{4,0},{8,12},{12,8},{1,5},{5,1},{9,13},{13,9},{2,6},{6,2},{1... | collective-permute-start | bytes 196616 | tf_op jit(solution)/shard_map/ppermute | solution.py:206
  45.3 2.2 %shard_map.90.refs_6_.weight = bf16[2048,1024]{1,0:T(8,128)(2,1)S(1)} custom-call(bf16[4096,2048]{1,0:T(8,128)(2,1)} %weight.5, bf16[32,2048]{1,0:T(8,128)(2,1)S(1)} %get-tuple-element.48.attended.refs_0_), custom_call_target="tpu_custom_call" | custom-call | bytes 4194304 | tf_op jit(solution)/shard_map/pallas_call | solution.py:684
  47.6 0.8 %shard_map.91 = (bf16[128,1024]{1,0:T(8,128)(2,1)S(1)}, bf16[128,2048]{1,0:T(8,128)(2,1)S(1)}) custom-call(bf16[128,128]{1,0:T(8,128)(2,1)S(1)} %get-tuple-element.44.refs_0_.chosen, bf16[32,2048]{1,0:T(8,128)(2,1)S(1)} %get-tuple-element.48.attended.refs_0_, bf16[32,2048]{1,0:T(8,128)(2,1)S(1)} %collective-permute-done.11.refs_1_, ...), custom_call_target="tpu_custom_call" | custom-call | flops 536870912 | bytes 4194304 | tf_op jit(solution)/shard_map/pallas_call | solution.py:401
  48.5 0.0 copy-start
  48.5 0.1 collective-permute-start.16
  48.5 0.7 %shard_map.92.own = f32[128,1024]{1,0:T(8,128)S(1)} custom-call(bf16[128,2048]{1,0:T(8,128)(2,1)S(1)} %get-tuple-element.51.permuted, bf16[2048,1024]{1,0:T(8,128)(2,1)S(1)} %shard_map.90.refs_6_.weight), custom_call_target="tpu_custom_call" | custom-call | flops 536870912 | bytes 4194304 | tf_op jit(solution)/shard_map/pallas_call | solution.py:410
  49.3 0.8 %collective-permute-done.16.received = bf16[128,1024]{1,0:T(8,128)(2,1)S(1)} collective-permute-done((bf16[128,1024]{1,0:T(8,128)(2,1)S(1)}, bf16[128,1024]{1,0:T(8,128)(2,1)S(1)}, u32[]{:S(2)}, u32[]{:S(2)}) %collective-permute-start.16) | collective-permute-done | bytes 262176 | tf_op jit(solution)/shard_map/ppermute | solution.py:206
  50.1 2.2 %collective-permute-start.17 = (bf16[32,1024]{1,0:T(8,128)(2,1)S(1)}, bf16[32,1024]{1,0:T(8,128)(2,1)S(1)}, u32[]{:S(2)}, u32[]{:S(2)}) collective-permute-start(bf16[32,1024]{1,0:T(8,128)(2,1)S(1)} %get-tuple-element.53), channel_id=1, source_target_pairs={{0,8},{4,12},{8,0},{12,4},{1,9},{5,13},{9,1},{13,5},{2,10},{6,14},... | collective-permute-start | bytes 196616 | tf_op jit(solution)/shard_map/ppermute | solution.py:206
  52.3 2.2 %collective-permute-start.18 = (bf16[32,1024]{1,0:T(8,128)(2,1)S(1)}, bf16[32,1024]{1,0:T(8,128)(2,1)S(1)}, u32[]{:S(2)}, u32[]{:S(2)}) collective-permute-start(bf16[32,1024]{1,0:T(8,128)(2,1)S(1)} %get-tuple-element.54), channel_id=1, source_target_pairs={{0,12},{2,4},{4,8},{6,0},{8,14},{10,6},{12,10},{14,2},{1,13},{3,5}... | collective-permute-start | bytes 196616 | tf_op jit(solution)/shard_map/ppermute | solution.py:462
  54.5 1.5 %collective-permute-done.17.passed.refs_0_ = bf16[32,1024]{1,0:T(8,128)(2,1)S(1)} collective-permute-done((bf16[32,1024]{1,0:T(8,128)(2,1)S(1)}, bf16[32,1024]{1,0:T(8,128)(2,1)S(1)}, u32[]{:S(2)}, u32[]{:S(2)}) %collective-permute-start.17) | collective-permute-done | bytes 65568 | tf_op jit(solution)/shard_map/ppermute | solution.py:206
  56.1 2.4 %collective-permute-start.20 = (bf16[32,1024]{1,0:T(8,128)(2,1)S(1)}, bf16[32,1024]{1,0:T(8,128)(2,1)S(1)}, u32[]{:S(2)}, u32[]{:S(2)}) collective-permute-start(bf16[32,1024]{1,0:T(8,128)(2,1)S(1)} %shard_map.94), channel_id=1, source_target_pairs={{0,2},{2,0},{1,3},{3,1},{4,6},{6,4},{5,7},{7,5},{8,10},{10,8},{9,1... | collective-permute-start | bytes 196616 | tf_op jit(solution)/shard_map/ppermute | solution.py:206
  58.5 0.2 collective-permute-done.18.refs_1_
  58.7 1.4 %collective-permute-done.19.refs_2_ = bf16[32,1024]{1,0:T(8,128)(2,1)S(1)} collective-permute-done((bf16[32,1024]{1,0:T(8,128)(2,1)S(1)}, bf16[32,1024]{1,0:T(8,128)(2,1)S(1)}, u32[]{:S(2)}, u32[]{:S(2)}) %collective-permute-start.19) | collective-permute-done | bytes 65568 | tf_op jit(solution)/shard_map/ppermute | solution.py:462
  60.1 0.6 %collective-permute-done.20.refs_4_ = bf16[32,1024]{1,0:T(8,128)(2,1)S(1)} collective-permute-done((bf16[32,1024]{1,0:T(8,128)(2,1)S(1)}, bf16[32,1024]{1,0:T(8,128)(2,1)S(1)}, u32[]{:S(2)}, u32[]{:S(2)}) %collective-permute-start.20) | collective-permute-done | bytes 65568 | tf_op jit(solution)/shard_map/ppermute | solution.py:206
  60.8 0.1 shard_map.95
  60.9 0.1 collective-permute-start.21
  60.9 1.3 %collective-permute-done.21.received = bf16[32,2048]{1,0:T(8,128)(2,1)S(1)} collective-permute-done((bf16[32,2048]{1,0:T(8,128)(2,1)S(1)}, bf16[32,2048]{1,0:T(8,128)(2,1)S(1)}, u32[]{:S(2)}, u32[]{:S(2)}) %collective-permute-start.21) | collective-permute-done | bytes 131104 | tf_op jit(solution)/shard_map/ppermute | solution.py:206
  62.3 0.7 %shard_map.96 = bf16[1,32,4096]{2,1,0:T(8,128)(2,1)} custom-call(bf16[32,2048]{1,0:T(8,128)(2,1)S(1)} %get-tuple-element.57.keep, bf16[32,2048]{1,0:T(8,128)(2,1)S(1)} %collective-permute-done.21.received), custom_call_target="tpu_custom_call" | custom-call | bytes 524288 | tf_op jit(solution)/shard_map/pallas_call | solution.py:705
  (20 shorter events, 0.1 us)
Async XLA Ops:
  0.9 7.9 %collective-permute-start.2 = (bf16[16,2048]{1,0:T(8,128)(2,1)S(1)}, bf16[16,2048]{1,0:T(8,128)(2,1)S(1)}, u32[]{:S(2)}, u32[]{:S(2)}) collective-permute-start(bf16[16,2048]{1,0:T(8,128)(2,1)S(1)} %get-tuple-element.60.refs_0_), channel_id=1, source_target_pairs={{0,8},{4,12},{8,0},{12,4},{1,9},{5,13},{9,1},{13,5},{2,10},{6,14},... | collective-permute-start | bytes 196616 | tf_op jit(solution)/shard_map/ppermute | solution.py:206
  5.0 11.5 %copy-start.1 = (bf16[4096]{0:T(1024)(128)(2,1)S(1)}, bf16[4096]{0:T(1024)(128)(2,1)}, u32[]{:S(2)}) copy-start(bf16[4096]{0:T(1024)(128)(2,1)} %param.9) | copy-start | bytes 24580
  5.0 6.1 %collective-permute-start.3 = (bf16[16,2048]{1,0:T(8,128)(2,1)S(1)}, bf16[16,2048]{1,0:T(8,128)(2,1)S(1)}, u32[]{:S(2)}, u32[]{:S(2)}) collective-permute-start(bf16[16,2048]{1,0:T(8,128)(2,1)S(1)} %get-tuple-element.59.refs_1_), channel_id=1, source_target_pairs={{0,8},{4,12},{8,0},{12,4},{1,9},{5,13},{9,1},{13,5},{2,10},{6,14},... | collective-permute-start | bytes 196616 | tf_op jit(solution)/shard_map/ppermute | solution.py:206
  5.1 11.4 %collective-permute-start = (bf16[16,2048]{1,0:T(8,128)(2,1)S(1)}, bf16[16,2048]{1,0:T(8,128)(2,1)S(1)}, u32[]{:S(2)}, u32[]{:S(2)}) collective-permute-start(bf16[16,2048]{1,0:T(8,128)(2,1)S(1)} %get-tuple-element.60.refs_0_), channel_id=1, source_target_pairs={{0,4},{4,0},{8,12},{12,8},{1,5},{5,1},{9,13},{13,9},{2,6},{6,2},{1... | collective-permute-start | bytes 196616 | tf_op jit(solution)/shard_map/ppermute | solution.py:206
  6.9 9.6 %collective-permute-start.1 = (bf16[16,2048]{1,0:T(8,128)(2,1)S(1)}, bf16[16,2048]{1,0:T(8,128)(2,1)S(1)}, u32[]{:S(2)}, u32[]{:S(2)}) collective-permute-start(bf16[16,2048]{1,0:T(8,128)(2,1)S(1)} %get-tuple-element.59.refs_1_), channel_id=1, source_target_pairs={{0,4},{4,0},{8,12},{12,8},{1,5},{5,1},{9,13},{13,9},{2,6},{6,2},{1... | collective-permute-start | bytes 196616 | tf_op jit(solution)/shard_map/ppermute | solution.py:206
  8.7 7.8 %collective-permute-start.4 = (bf16[16,2048]{1,0:T(8,128)(2,1)S(1)}, bf16[16,2048]{1,0:T(8,128)(2,1)S(1)}, u32[]{:S(2)}, u32[]{:S(2)}) collective-permute-start(bf16[16,2048]{1,0:T(8,128)(2,1)S(1)} %collective-permute-done.2.refs_4_), channel_id=1, source_target_pairs={{0,4},{4,0},{8,12},{12,8},{1,5},{5,1},{9,13},{13,9},{2,6},{6,2},{1... | collective-permute-start | bytes 196616 | tf_op jit(solution)/shard_map/ppermute | solution.py:206
  11.1 5.4 %collective-permute-start.5 = (bf16[16,2048]{1,0:T(8,128)(2,1)S(1)}, bf16[16,2048]{1,0:T(8,128)(2,1)S(1)}, u32[]{:S(2)}, u32[]{:S(2)}) collective-permute-start(bf16[16,2048]{1,0:T(8,128)(2,1)S(1)} %collective-permute-done.3.refs_5_), channel_id=1, source_target_pairs={{0,4},{4,0},{8,12},{12,8},{1,5},{5,1},{9,13},{13,9},{2,6},{6,2},{1... | collective-permute-start | bytes 196616 | tf_op jit(solution)/shard_map/ppermute | solution.py:206
  17.6 5.8 %copy-start.2 = (s32[128]{0:T(128)S(1)}, s32[128]{0:T(128)}, u32[]{:S(2)}) copy-start(s32[128]{0:T(128)} %slots.3) | copy-start | bytes 1540
  17.6 5.7 %copy-start.3 = (s32[32]{0:T(128)S(1)}, s32[32]{0:T(128)}, u32[]{:S(2)}) copy-start(s32[32]{0:T(128)} %lengths.1) | copy-start | bytes 388
  17.6 1.7 %collective-permute-start.6 = (bf16[128,1408]{1,0:T(8,128)(2,1)S(1)}, bf16[128,1408]{1,0:T(8,128)(2,1)S(1)}, u32[]{:S(2)}, u32[]{:S(2)}) collective-permute-start(bf16[128,1408]{1,0:T(8,128)(2,1)S(1)} %get-tuple-element.39.given), channel_id=1, source_target_pairs={{0,1},{1,0},{2,3},{3,2},{4,5},{5,4},{6,7},{7,6},{8,9},{9,8},{10,11... | collective-permute-start | bytes 1081352 | tf_op jit(solution)/shard_map/ppermute | solution.py:206
  19.5 7.8 %collective-permute-start.7 = (bf16[32,1280]{1,0:T(8,128)(2,1)S(1)}, bf16[32,1280]{1,0:T(8,128)(2,1)S(1)}, u32[]{:S(2)}, u32[]{:S(2)}) collective-permute-start(bf16[32,1280]{1,0:T(8,128)(2,1)S(1)} %get-tuple-element.40), channel_id=1, source_target_pairs={{0,8},{4,12},{8,0},{12,4},{1,9},{5,13},{9,1},{13,5},{2,10},{6,14},... | collective-permute-start | bytes 245768 | tf_op jit(solution)/shard_map/ppermute | solution.py:206
  22.7 10.0 %collective-permute-start.8 = (bf16[32,1408]{1,0:T(8,128)(2,1)S(1)}, bf16[32,1408]{1,0:T(8,128)(2,1)S(1)}, u32[]{:S(2)}, u32[]{:S(2)}) collective-permute-start(bf16[32,1408]{1,0:T(8,128)(2,1)S(1)} %get-tuple-element.41), channel_id=1, source_target_pairs={{0,12},{2,4},{4,8},{6,0},{8,14},{10,6},{12,10},{14,2},{1,13},{3,5}... | collective-permute-start | bytes 270344 | tf_op jit(solution)/shard_map/ppermute | solution.py:462
  22.9 9.8 %collective-permute-start.9 = (bf16[32,1408]{1,0:T(8,128)(2,1)S(1)}, bf16[32,1408]{1,0:T(8,128)(2,1)S(1)}, u32[]{:S(2)}, u32[]{:S(2)}) collective-permute-start(bf16[32,1408]{1,0:T(8,128)(2,1)S(1)} %get-tuple-element.42), channel_id=1, source_target_pairs={{0,4},{2,12},{4,0},{6,8},{8,6},{10,14},{12,2},{14,10},{1,5},{3,13}... | collective-permute-start | bytes 270344 | tf_op jit(solution)/shard_map/ppermute | solution.py:462
  27.3 5.5 %collective-permute-start.10 = (bf16[32,1280]{1,0:T(8,128)(2,1)S(1)}, bf16[32,1280]{1,0:T(8,128)(2,1)S(1)}, u32[]{:S(2)}, u32[]{:S(2)}) collective-permute-start(bf16[32,1280]{1,0:T(8,128)(2,1)S(1)} %shard_map.88), channel_id=1, source_target_pairs={{0,2},{2,0},{1,3},{3,1},{4,6},{6,4},{5,7},{7,5},{8,10},{10,8},{9,1... | collective-permute-start | bytes 245768 | tf_op jit(solution)/shard_map/ppermute | solution.py:206
  34.6 6.0 %collective-permute-start.12 = (bf16[16,2048]{1,0:T(8,128)(2,1)S(1)}, bf16[16,2048]{1,0:T(8,128)(2,1)S(1)}, u32[]{:S(2)}, u32[]{:S(2)}) collective-permute-start(bf16[16,2048]{1,0:T(8,128)(2,1)S(1)} %get-tuple-element.49), channel_id=1, source_target_pairs={{0,8},{4,12},{8,0},{12,4},{1,9},{5,13},{9,1},{13,5},{2,10},{6,14},... | collective-permute-start | bytes 196616 | tf_op jit(solution)/shard_map/ppermute | solution.py:206
  36.6 6.0 %collective-permute-start.13 = (bf16[16,2048]{1,0:T(8,128)(2,1)S(1)}, bf16[16,2048]{1,0:T(8,128)(2,1)S(1)}, u32[]{:S(2)}, u32[]{:S(2)}) collective-permute-start(bf16[16,2048]{1,0:T(8,128)(2,1)S(1)} %get-tuple-element.50), channel_id=1, source_target_pairs={{0,8},{4,12},{8,0},{12,4},{1,9},{5,13},{9,1},{13,5},{2,10},{6,14},... | collective-permute-start | bytes 196616 | tf_op jit(solution)/shard_map/ppermute | solution.py:206
  37.6 10.0 %collective-permute-start.11 = (bf16[32,2048]{1,0:T(8,128)(2,1)S(1)}, bf16[32,2048]{1,0:T(8,128)(2,1)S(1)}, u32[]{:S(2)}, u32[]{:S(2)}) collective-permute-start(bf16[32,2048]{1,0:T(8,128)(2,1)S(1)} %get-tuple-element.48.attended.refs_0_), channel_id=1, source_target_pairs={{0,4},{4,0},{8,12},{12,8},{1,5},{5,1},{9,13},{13,9},{2,6},{6,2},{1... | collective-permute-start | bytes 393224 | tf_op jit(solution)/shard_map/ppermute | solution.py:206
  40.6 7.0 %collective-permute-start.14 = (bf16[16,2048]{1,0:T(8,128)(2,1)S(1)}, bf16[16,2048]{1,0:T(8,128)(2,1)S(1)}, u32[]{:S(2)}, u32[]{:S(2)}) collective-permute-start(bf16[16,2048]{1,0:T(8,128)(2,1)S(1)} %collective-permute-done.12.refs_2_), channel_id=1, source_target_pairs={{0,4},{4,0},{8,12},{12,8},{1,5},{5,1},{9,13},{13,9},{2,6},{6,2},{1... | collective-permute-start | bytes 196616 | tf_op jit(solution)/shard_map/ppermute | solution.py:206
  42.6 5.0 %collective-permute-start.15 = (bf16[16,2048]{1,0:T(8,128)(2,1)S(1)}, bf16[16,2048]{1,0:T(8,128)(2,1)S(1)}, u32[]{:S(2)}, u32[]{:S(2)}) collective-permute-start(bf16[16,2048]{1,0:T(8,128)(2,1)S(1)} %collective-permute-done.13.refs_3_), channel_id=1, source_target_pairs={{0,4},{4,0},{8,12},{12,8},{1,5},{5,1},{9,13},{13,9},{2,6},{6,2},{1... | collective-permute-start | bytes 196616 | tf_op jit(solution)/shard_map/ppermute | solution.py:206
  48.5 12.3 %copy-start = (bf16[32,4096]{1,0:T(8,128)(2,1)S(1)}, bf16[32,4096]{1,0:T(8,128)(2,1)}, u32[]{:S(2)}) copy-start(bf16[32,4096]{1,0:T(8,128)(2,1)} %hidden.1) | copy-start | bytes 786436
  48.5 1.6 %collective-permute-start.16 = (bf16[128,1024]{1,0:T(8,128)(2,1)S(1)}, bf16[128,1024]{1,0:T(8,128)(2,1)S(1)}, u32[]{:S(2)}, u32[]{:S(2)}) collective-permute-start(bf16[128,1024]{1,0:T(8,128)(2,1)S(1)} %get-tuple-element.52.given), channel_id=1, source_target_pairs={{0,1},{1,0},{2,3},{3,2},{4,5},{5,4},{6,7},{7,6},{8,9},{9,8},{10,11... | collective-permute-start | bytes 786440 | tf_op jit(solution)/shard_map/ppermute | solution.py:206
  50.1 5.9 %collective-permute-start.17 = (bf16[32,1024]{1,0:T(8,128)(2,1)S(1)}, bf16[32,1024]{1,0:T(8,128)(2,1)S(1)}, u32[]{:S(2)}, u32[]{:S(2)}) collective-permute-start(bf16[32,1024]{1,0:T(8,128)(2,1)S(1)} %get-tuple-element.53), channel_id=1, source_target_pairs={{0,8},{4,12},{8,0},{12,4},{1,9},{5,13},{9,1},{13,5},{2,10},{6,14},... | collective-permute-start | bytes 196616 | tf_op jit(solution)/shard_map/ppermute | solution.py:206
  52.3 6.4 %collective-permute-start.18 = (bf16[32,1024]{1,0:T(8,128)(2,1)S(1)}, bf16[32,1024]{1,0:T(8,128)(2,1)S(1)}, u32[]{:S(2)}, u32[]{:S(2)}) collective-permute-start(bf16[32,1024]{1,0:T(8,128)(2,1)S(1)} %get-tuple-element.54), channel_id=1, source_target_pairs={{0,12},{2,4},{4,8},{6,0},{8,14},{10,6},{12,10},{14,2},{1,13},{3,5}... | collective-permute-start | bytes 196616 | tf_op jit(solution)/shard_map/ppermute | solution.py:462
  54.5 5.6 %collective-permute-start.19 = (bf16[32,1024]{1,0:T(8,128)(2,1)S(1)}, bf16[32,1024]{1,0:T(8,128)(2,1)S(1)}, u32[]{:S(2)}, u32[]{:S(2)}) collective-permute-start(bf16[32,1024]{1,0:T(8,128)(2,1)S(1)} %get-tuple-element.55), channel_id=1, source_target_pairs={{0,4},{2,12},{4,0},{6,8},{8,6},{10,14},{12,2},{14,10},{1,5},{3,13}... | collective-permute-start | bytes 196616 | tf_op jit(solution)/shard_map/ppermute | solution.py:462
  56.1 4.7 %collective-permute-start.20 = (bf16[32,1024]{1,0:T(8,128)(2,1)S(1)}, bf16[32,1024]{1,0:T(8,128)(2,1)S(1)}, u32[]{:S(2)}, u32[]{:S(2)}) collective-permute-start(bf16[32,1024]{1,0:T(8,128)(2,1)S(1)} %shard_map.94), channel_id=1, source_target_pairs={{0,2},{2,0},{1,3},{3,1},{4,6},{6,4},{5,7},{7,5},{8,10},{10,8},{9,1... | collective-permute-start | bytes 196616 | tf_op jit(solution)/shard_map/ppermute | solution.py:206
  60.9 1.4 %collective-permute-start.21 = (bf16[32,2048]{1,0:T(8,128)(2,1)S(1)}, bf16[32,2048]{1,0:T(8,128)(2,1)S(1)}, u32[]{:S(2)}, u32[]{:S(2)}) collective-permute-start(bf16[32,2048]{1,0:T(8,128)(2,1)S(1)} %get-tuple-element.58), channel_id=1, source_target_pairs={{0,1},{1,0},{2,3},{3,2},{4,5},{5,4},{6,7},{7,6},{8,9},{9,8},{10,11... | collective-permute-start | bytes 393224 | tf_op jit(solution)/shard_map/ppermute | solution.py:206

commit v18 on v17

--- a/solution.py
+++ b/solution.py
@@ -263,8 +263,8 @@
     return copies
 
 
-def stage_cache_kernel(blocks, lengths, keys, values, slots, *refs):
-    key_part, value_part, cosine, sine, length_of, chosen, scratch, sems = refs
+def stage_rest_kernel(blocks, lengths, weight, keys, values, slots, *refs):
+    target, key_part, value_part, cosine, sine, length_of, chosen, scratch, sems = refs
     side, col = position()
     copies = []
     for j in range(key_part.shape[2] // HEAD_DIM):
@@ -276,15 +276,11 @@
                     part.at[:, :, pl.ds(j * HEAD_DIM, HEAD_DIM)],
                 )
             )
-    copies = started(copies, sems)
+    copies = started(copies + head_copies(weight, target, 1 - side), sems)
     cosine[...], sine[...], length_of[...] = rope(lengths, cosine.shape[0])
     chosen[...] = one_hot(slots, scratch, blocks, col, col).T.astype(jnp.bfloat16)
     for copy in copies:
         copy.wait()
-
-
-def stage_give_kernel(weight, give_part, sems):
-    run_copies(head_copies(weight, give_part, 1 - lax.axis_index("side")), sems)
 
 
 def stage_out_kernel(weight, attended, own_part, sems):
@@ -369,13 +365,7 @@
         first = first if isinstance(first, int) else pl.multiple_of(first, rows)
         part = pl.ds(first, rows)
         total = own[part, :] + received[part, :half].astype(jnp.float32)
-        out[:, :half] = total.astype(jnp.bfloat16)
-        if out.shape[1] > half:
-            out[:, half:] = squares(part)
-
-    def squares(part):
-        lanes = slice(half, half + more // 2)
-        return jnp.concatenate([given[part, lanes], received[part, lanes]], axis=1)
+        out[...] = total.astype(jnp.bfloat16)
 
     write(outs[0], 0)
     write(outs[1], pairs * rows)
@@ -384,7 +374,8 @@
         write(outs[2 * pair], jnp.where(home, pairs + pair, pair) * rows)
         write(outs[2 * pair + 1], jnp.where(home, pair, pairs + pair) * rows)
     for out in outs[count:]:
-        out[...] = squares(pl.ds(0, rows))
+        lanes = slice(half, half + more // 2)
+        out[...] = jnp.concatenate([given[:rows, lanes], received[:rows, lanes]], axis=1)
 
 
 def own_kernel(permuted, weight, own):
@@ -415,7 +406,7 @@
         flops,
         depth * half * 2,
     )(permuted, in_vmem(weights[1]))
-    outs = [struct((rows // count, half + (more if i > 1 else 0))) for i in range(count)]
+    outs = [struct((rows // count, half))] * count
     if more:
         outs = outs + [struct((rows // count, more))]
     merged = call(
@@ -483,9 +474,9 @@
     return [passed, *blocks, own, moved(crossing, "row", 1)]
 
 
-def total_of(blocks, pair, width):
+def total_of(blocks, pair):
     if pair > 0:
-        first, second = blocks[2 * pair - 1][:, :width], blocks[2 * pair][:, :width]
+        first, second = blocks[2 * pair - 1][...], blocks[2 * pair][...]
     else:
         passed, own, crossed = blocks[0], blocks[-2], blocks[-1]
         first, second = jnp.where(at_home(), own[...], passed[...]), crossed[...]
@@ -509,15 +500,15 @@
     return jnp.cos(phases), jnp.where(lane < half, -sine, sine), length_of
 
 
-def attend_all(count, parts, ready, cosine, sine, lengths, *refs):
+def attend_all(count, parts, cosine, sine, lengths, *refs):
     pairs = (count - 1) // 2
-    blocks, (sums, keys, values), refs = refs[:count], refs[count : count + 3], refs[count + 3 :]
+    blocks, (sums, other_sums, keys, values) = refs[:count], refs[count : count + 4]
+    refs = refs[count + 4 :]
     whole, outs, (scores_of, probs_of) = refs[0], refs[1 : parts + 1], refs[parts + 1 :]
     rows, cache = keys.shape[:2]
     low = lax.rem(lax.axis_index("col"), pairs)
     width = GROUP_WIDTH
-    other_sums = jnp.where(at_home(), blocks[1][:, width:], blocks[2][:, width:])
-    squares = sums[...].astype(jnp.float32) + other_sums.astype(jnp.float32)
+    squares = sums[...].astype(jnp.float32) + other_sums[...].astype(jnp.float32)
     scale = lax.rsqrt(jnp.sum(squares, axis=1, keepdims=True) / D + EPSILON)
     factor = HEAD_DIM ** (-0.5)
     cosines, sines, length_of = cosine[...], sine[...], lengths[:, :1]
@@ -528,7 +519,7 @@
     filled = [(position >= 0) & (position < length_of[part]) for part in runs]
     own, new_values, own_probs = [], [], []
     for pair in range(pairs):
-        total = total_of(blocks, pair, width)
+        total = total_of(blocks, pair)
         total = (total * scale).astype(jnp.bfloat16).astype(jnp.float32)
         heads = [total[:, h * HEAD_DIM : (h + 1) * HEAD_DIM] for h in range(GROUP + 2)]
         queries = [
@@ -593,7 +584,7 @@
     low = lax.rem(lax.axis_index("col"), pairs)
     for pair in range(pairs):
         column = low ^ pair
-        total = total_of(blocks, pair, width)
+        total = total_of(blocks, pair)
         at = pl.ds(pl.multiple_of((2 * column + side) * width, width), width)
         hidden_out = (hidden[:, at].astype(jnp.float32) + total).astype(jnp.bfloat16)
         at = pl.ds(pl.multiple_of(column * width, width), width)
@@ -648,38 +639,38 @@
         [own_part[i * piece : (i + 1) * piece] for i in range(parts)], "col"
     )
     table = struct((rows, HEAD_DIM), jnp.float32)
-    key_part, value_part, *tables, chosen_out = call(
-        functools.partial(stage_cache_kernel, col_count),
-        [pltpu.VMEM((rows, cache, pairs * HEAD_DIM), jnp.bfloat16)] * 2
+    give_out, key_part, value_part, *tables, chosen_out = call(
+        functools.partial(stage_rest_kernel, col_count),
+        [pltpu.VMEM((half, half_out), jnp.bfloat16)]
+        + [pltpu.VMEM((rows, cache, pairs * HEAD_DIM), jnp.bfloat16)] * 2
         + [table, table, struct((rows, HEAD_DIM), jnp.int32), struct(square)],
-        [SMEM, HBM, HBM, VMEM],
-        [VMEM] * 6,
+        [SMEM, HBM, HBM, HBM, VMEM],
+        [VMEM] * 7,
         0,
-        4 * rows * cache * pairs * HEAD_DIM,
-        [pltpu.VMEM(square, jnp.float32), pltpu.SemaphoreType.DMA((2 * pairs,))],
-    )(cache_lengths, in_hbm(key_cache), in_hbm(value_cache), slot_request)
+        half * half_out * 2 + 4 * rows * cache * pairs * HEAD_DIM,
+        [pltpu.VMEM(square, jnp.float32), pltpu.SemaphoreType.DMA((3 * pairs,))],
+    )(cache_lengths, in_hbm(out_weight), in_hbm(key_cache), in_hbm(value_cache), slot_request)
     products, sums = project(in_kernel, chosen_in, blocks, [gain], [give_in, own_in], HEAD_DIM)
-    products = spread(products, [chosen_out])
-
-    give_out = call(
-        stage_give_kernel,
-        pltpu.VMEM((half, half_out), jnp.bfloat16),
-        [HBM],
-        VMEM,
-        0,
-        half * half_out * 2,
-        [pltpu.SemaphoreType.DMA((pairs,))],
-    )(in_hbm(out_weight))
+    other_sums = moved(sums[0], "row", 1)
+    products = spread(products, [other_sums])
+
     runs = (pairs, rows // SLOTS, GROUP * SLOTS, SLOTS * cache)
     attended, *attended_parts = call(
         functools.partial(attend_all, len(products), parts),
         [struct((rows, half))] + [struct((piece, half))] * parts,
-        [HBM] + [VMEM] * (len(products) + 6),
+        [VMEM] * (len(products) + 7),
         [VMEM] * (parts + 1),
         4 * rows * half * cache,
         0,
         [pltpu.VMEM(runs, jnp.float32), pltpu.VMEM(runs, jnp.bfloat16)],
-    )(give_out, *tables, *products, *sums, in_vmem(key_part), in_vmem(value_part))
+    )(
+        *tables,
+        *products,
+        *sums,
+        other_sums,
+        in_vmem(key_part),
+        in_vmem(value_part),
+    )
 
     own_out = call(
         stage_out_kernel,

time: 63.2 us -> 62.6 us (level)
  waiting for transfers between devices: 11.5 us -> 13.2 us
  starting transfers between devices: 33.3 us -> 32 us
  Pallas kernels: 17.1 us -> 16.2 us
    ppermute x18 -> x19, starting transfers between devices: 30.3 us -> 28.4 us  [moved(): return lax.ppermute(value, axis, pairs)]
    ppermute x18 -> x19, waiting for transfers between devices: 9.85 us -> 10.7 us  [moved(): return lax.ppermute(value, axis, pairs)]
    ppermute x4, waiting for transfers between devices: 1.61 us -> 2.44 us  [direct(): return lax.ppermute(value, ('col', 'row'), moves)]
    pallas_call x2 -> x1, Pallas kernels: 4.49 us -> 3.71 us  [paired_plan(): call(functools.partial(stage_rest_kernel, col_count), [pltpu.VMEM((half,...]
  transfers between devices with their start and end apart: 22 -> 23, of which waited for: 12 -> 11; matrix products, arithmetic and copies ran while one was open for 0% -> 0% of each run, Pallas kernels for 20% -> 19%
where the time goes in v18:
time: 62.6 us; the launch traced here: 62.5 us
  starting transfers between devices  32 us (51%)
  Pallas kernels  16.2 us (26%)
  waiting for transfers between devices  13.2 us (21%)
  local copies, waits for them, and re-layouts  0.9 us (1%)
    ppermute x19, starting transfers between devices, moved(): return lax.ppermute(value, axis, pairs)  28.4 us
    ppermute x19, waiting for transfers between devices, moved(): return lax.ppermute(value, axis, pairs)  10.7 us
    pallas_call x1, Pallas kernels, paired_plan(): call(functools.partial(stage_in_kernel, col_count), [pltpu.VMEM((half, ha...  4.09 us
    pallas_call x1, Pallas kernels, paired_plan(): call(functools.partial(stage_rest_kernel, col_count), [pltpu.VMEM((half,...  3.71 us
    ppermute x4, starting transfers between devices, direct(): return lax.ppermute(value, ('col', 'row'), moves)  3.53 us
    ppermute x4, waiting for transfers between devices, direct(): return lax.ppermute(value, ('col', 'row'), moves)  2.44 us
    pallas_call x1, Pallas kernels, paired_plan(): call(stage_out_kernel, pltpu.VMEM((half, half_out), jnp.bfloat16), [HBM,...  2.24 us
    pallas_call x2, Pallas kernels, project(): call(functools.partial(kernel, parts), [struct((rows, half + more)), stru...  1.91 us
  transfers between devices with their start and end apart: 23, of which 11 were waited for; matrix products, arithmetic and copies ran while one was open for 0% of the time, Pallas kernels for 19%

profile of v18, /device:TPU:0, one launch (start us, length us, event | category | flops | bytes accessed | tf_op | source)
XLA Modules:
  0.0 62.5 jit_solution(6850923060566647571)
XLA Ops:
  0.0 0.9 %fusion = (bf16[16,2048]{1,0:T(8,128)(2,1)S(1)}, bf16[16,2048]{1,0:T(8,128)(2,1)S(1)}) fusion(bf16[32,4096]{1,0:T(8,128)(2,1)} %hidden.1, s32[]{:T(128)S(6)} %add.4, s32[]{:T(128)S(6)} %select_n.3), kind=kLoop, calls=%fused_computation.1 | loop fusion | bytes 262152 | tf_op jit(solution)/shard_map/slice | solution.py:639
  0.9 4.1 %collective-permute-start.2 = (bf16[16,2048]{1,0:T(8,128)(2,1)S(1)}, bf16[16,2048]{1,0:T(8,128)(2,1)S(1)}, u32[]{:S(2)}, u32[]{:S(2)}) collective-permute-start(bf16[16,2048]{1,0:T(8,128)(2,1)S(1)} %get-tuple-element.62.refs_0_), channel_id=1, source_target_pairs={{0,8},{4,12},{8,0},{12,4},{1,9},{5,13},{9,1},{13,5},{2,10},{6,14},... | collective-permute-start | bytes 196616 | tf_op jit(solution)/shard_map/ppermute | solution.py:206
  5.0 0.1 collective-permute-start.3
  5.1 1.8 %collective-permute-start = (bf16[16,2048]{1,0:T(8,128)(2,1)S(1)}, bf16[16,2048]{1,0:T(8,128)(2,1)S(1)}, u32[]{:S(2)}, u32[]{:S(2)}) collective-permute-start(bf16[16,2048]{1,0:T(8,128)(2,1)S(1)} %get-tuple-element.62.refs_0_), channel_id=1, source_target_pairs={{0,4},{4,0},{8,12},{12,8},{1,5},{5,1},{9,13},{13,9},{2,6},{6,2},{1... | collective-permute-start | bytes 196616 | tf_op jit(solution)/shard_map/ppermute | solution.py:206
  6.9 0.2 collective-permute-start.1
  7.1 1.6 %collective-permute-done.2.refs_4_ = bf16[16,2048]{1,0:T(8,128)(2,1)S(1)} collective-permute-done((bf16[16,2048]{1,0:T(8,128)(2,1)S(1)}, bf16[16,2048]{1,0:T(8,128)(2,1)S(1)}, u32[]{:S(2)}, u32[]{:S(2)}) %collective-permute-start.2) | collective-permute-done | bytes 65568 | tf_op jit(solution)/shard_map/ppermute | solution.py:206
  8.7 1.9 %collective-permute-start.4 = (bf16[16,2048]{1,0:T(8,128)(2,1)S(1)}, bf16[16,2048]{1,0:T(8,128)(2,1)S(1)}, u32[]{:S(2)}, u32[]{:S(2)}) collective-permute-start(bf16[16,2048]{1,0:T(8,128)(2,1)S(1)} %collective-permute-done.2.refs_4_), channel_id=1, source_target_pairs={{0,4},{4,0},{8,12},{12,8},{1,5},{5,1},{9,13},{13,9},{2,6},{6,2},{1... | collective-permute-start | bytes 196616 | tf_op jit(solution)/shard_map/ppermute | solution.py:206
  10.6 0.4 collective-permute-done.3.refs_5_
  11.1 1.3 %collective-permute-start.5 = (bf16[16,2048]{1,0:T(8,128)(2,1)S(1)}, bf16[16,2048]{1,0:T(8,128)(2,1)S(1)}, u32[]{:S(2)}, u32[]{:S(2)}) collective-permute-start(bf16[16,2048]{1,0:T(8,128)(2,1)S(1)} %collective-permute-done.3.refs_5_), channel_id=1, source_target_pairs={{0,4},{4,0},{8,12},{12,8},{1,5},{5,1},{9,13},{13,9},{2,6},{6,2},{1... | collective-permute-start | bytes 196616 | tf_op jit(solution)/shard_map/ppermute | solution.py:206
  12.4 4.1 %shard_map.83 = (bf16[2048,1280]{1,0:T(8,128)(2,1)S(1)}, bf16[2048,1280]{1,0:T(8,128)(2,1)S(1)}, bf16[128,128]{1,0:T(8,128)(2,1)S(1)}) custom-call(bf16[4096,2560]{1,0:T(8,128)(2,1)} %weight.4, s32[128]{0:T(128)} %slots.3), custom_call_target="tpu_custom_call" | custom-call | bytes 10485760 | tf_op jit(solution)/shard_map/pallas_call | solution.py:625
  16.5 1.1 %shard_map.84 = (bf16[128,1408]{1,0:T(8,128)(2,1)S(1)}, bf16[128,2048]{1,0:T(8,128)(2,1)S(1)}) custom-call(bf16[128,128]{1,0:T(8,128)(2,1)S(1)} %get-tuple-element.36.chosen, bf16[16,2048]{1,0:T(8,128)(2,1)S(1)} %get-tuple-element.62.refs_0_, bf16[16,2048]{1,0:T(8,128)(2,1)S(1)} %get-tuple-element.61.refs_1_, ...), custom_call_target="tpu_custom_call" | custom-call | flops 671088640 | bytes 5242880 | tf_op jit(solution)/shard_map/pallas_call | solution.py:392
  17.6 0.0 copy-start.2
  17.6 0.0 copy-start.3
  17.6 0.1 collective-permute-start.6
  17.7 0.9 %shard_map.85.own = f32[128,1280]{1,0:T(8,128)S(1)} custom-call(bf16[128,2048]{1,0:T(8,128)(2,1)S(1)} %get-tuple-element.39.permuted, bf16[2048,1280]{1,0:T(8,128)(2,1)S(1)} %get-tuple-element.37.refs_8_.weight), custom_call_target="tpu_custom_call" | custom-call | flops 671088640 | bytes 5242880 | tf_op jit(solution)/shard_map/pallas_call | solution.py:401
  18.6 0.8 %collective-permute-done.6.received = bf16[128,1408]{1,0:T(8,128)(2,1)S(1)} collective-permute-done((bf16[128,1408]{1,0:T(8,128)(2,1)S(1)}, bf16[128,1408]{1,0:T(8,128)(2,1)S(1)}, u32[]{:S(2)}, u32[]{:S(2)}) %collective-permute-start.6) | collective-permute-done | bytes 360480 | tf_op jit(solution)/shard_map/ppermute | solution.py:206
  19.4 0.1 shard_map.86
  19.5 3.2 %collective-permute-start.7 = (bf16[32,1280]{1,0:T(8,128)(2,1)S(1)}, bf16[32,1280]{1,0:T(8,128)(2,1)S(1)}, u32[]{:S(2)}, u32[]{:S(2)}) collective-permute-start(bf16[32,1280]{1,0:T(8,128)(2,1)S(1)} %get-tuple-element.41), channel_id=1, source_target_pairs={{0,8},{4,12},{8,0},{12,4},{1,9},{5,13},{9,1},{13,5},{2,10},{6,14},... | collective-permute-start | bytes 245768 | tf_op jit(solution)/shard_map/ppermute | solution.py:206
  22.6 1.5 %collective-permute-start.10 = (bf16[32,128]{1,0:T(8,128)(2,1)S(1)}, bf16[32,128]{1,0:T(8,128)(2,1)S(1)}, u32[]{:S(2)}, u32[]{:S(2)}) collective-permute-start(bf16[32,128]{1,0:T(8,128)(2,1)S(1)} %get-tuple-element.45.refs_5_), channel_id=1, source_target_pairs={{0,2},{2,0},{1,3},{3,1},{4,6},{6,4},{5,7},{7,5},{8,10},{10,8},{9,1... | collective-permute-start | bytes 24584 | tf_op jit(solution)/shard_map/ppermute | solution.py:206
  24.1 0.4 collective-permute-start.8
  24.5 0.3 collective-permute-start.9
  24.9 1.4 %collective-permute-done.10.refs_0_.refs_6_ = bf16[32,128]{1,0:T(8,128)(2,1)S(1)} collective-permute-done((bf16[32,128]{1,0:T(8,128)(2,1)S(1)}, bf16[32,128]{1,0:T(8,128)(2,1)S(1)}, u32[]{:S(2)}, u32[]{:S(2)}) %collective-permute-start.10) | collective-permute-done | bytes 8224 | tf_op jit(solution)/shard_map/ppermute | solution.py:206
  26.3 0.9 %collective-permute-done.7.passed.refs_0_ = bf16[32,1280]{1,0:T(8,128)(2,1)S(1)} collective-permute-done((bf16[32,1280]{1,0:T(8,128)(2,1)S(1)}, bf16[32,1280]{1,0:T(8,128)(2,1)S(1)}, u32[]{:S(2)}, u32[]{:S(2)}) %collective-permute-start.7) | collective-permute-done | bytes 81952 | tf_op jit(solution)/shard_map/ppermute | solution.py:206
  27.2 2.6 %collective-permute-start.11 = (bf16[32,1280]{1,0:T(8,128)(2,1)S(1)}, bf16[32,1280]{1,0:T(8,128)(2,1)S(1)}, u32[]{:S(2)}, u32[]{:S(2)}) collective-permute-start(bf16[32,1280]{1,0:T(8,128)(2,1)S(1)} %shard_map.87), channel_id=1, source_target_pairs={{0,2},{2,0},{1,3},{3,1},{4,6},{6,4},{5,7},{7,5},{8,10},{10,8},{9,1... | collective-permute-start | bytes 245768 | tf_op jit(solution)/shard_map/ppermute | solution.py:206
  29.9 3.7 %shard_map.82 = (bf16[2048,1024]{1,0:T(8,128)(2,1)S(1)}, bf16[32,64,256]{2,1,0:T(8,128)(2,1)S(1)}, bf16[32,64,256]{2,1,0:T(8,128)(2,1)S(1)}, f32[32,128]{1,0:T(8...) custom-call(s32[32]{0:T(128)S(1)} %copy-done.3, bf16[4096,2048]{1,0:T(8,128)(2,1)} %weight.5, ...), custom_call_target="tpu_custom_call" | custom-call | bytes 6291456 | tf_op jit(solution)/shard_map/pallas_call | solution.py:642
  33.6 1.7 %shard_map.88 = (bf16[32,2048]{1,0:T(8,128)(2,1)S(1)}, bf16[16,2048]{1,0:T(8,128)(2,1)S(1)}, bf16[16,2048]{1,0:T(8,128)(2,1)S(1)}) custom-call(f32[32,128]{1,0:T(8,128)S(1)} %get-tuple-element.33.cosine, f32[32,128]{1,0:T(8,128)S(1)} %get-tuple-element.34.sine, s32[32,128]{1,0:T(8,128)S(1)} %get-tuple-element.35.lengths, ...), custom_call_target="tpu_custom_call" | custom-call | flops 16777216 | tf_op jit(solution)/shard_map/pallas_call | solution.py:658
  35.3 0.5 collective-permute-start.13
  35.8 2.5 %collective-permute-start.14 = (bf16[16,2048]{1,0:T(8,128)(2,1)S(1)}, bf16[16,2048]{1,0:T(8,128)(2,1)S(1)}, u32[]{:S(2)}, u32[]{:S(2)}) collective-permute-start(bf16[16,2048]{1,0:T(8,128)(2,1)S(1)} %get-tuple-element.51), channel_id=1, source_target_pairs={{0,8},{4,12},{8,0},{12,4},{1,9},{5,13},{9,1},{13,5},{2,10},{6,14},... | collective-permute-start | bytes 196616 | tf_op jit(solution)/shard_map/ppermute | solution.py:206
  38.3 1.1 %collective-permute-start.12 = (bf16[32,2048]{1,0:T(8,128)(2,1)S(1)}, bf16[32,2048]{1,0:T(8,128)(2,1)S(1)}, u32[]{:S(2)}, u32[]{:S(2)}) collective-permute-start(bf16[32,2048]{1,0:T(8,128)(2,1)S(1)} %get-tuple-element.48.attended.refs_0_), channel_id=1, source_target_pairs={{0,4},{4,0},{8,12},{12,8},{1,5},{5,1},{9,13},{13,9},{2,6},{6,2},{1... | collective-permute-start | bytes 393224 | tf_op jit(solution)/shard_map/ppermute | solution.py:206
  39.4 1.5 %collective-permute-done.13.refs_2_ = bf16[16,2048]{1,0:T(8,128)(2,1)S(1)} collective-permute-done((bf16[16,2048]{1,0:T(8,128)(2,1)S(1)}, bf16[16,2048]{1,0:T(8,128)(2,1)S(1)}, u32[]{:S(2)}, u32[]{:S(2)}) %collective-permute-start.13) | collective-permute-done | bytes 65568 | tf_op jit(solution)/shard_map/ppermute | solution.py:206
  41.0 1.3 %collective-permute-start.15 = (bf16[16,2048]{1,0:T(8,128)(2,1)S(1)}, bf16[16,2048]{1,0:T(8,128)(2,1)S(1)}, u32[]{:S(2)}, u32[]{:S(2)}) collective-permute-start(bf16[16,2048]{1,0:T(8,128)(2,1)S(1)} %collective-permute-done.13.refs_2_), channel_id=1, source_target_pairs={{0,4},{4,0},{8,12},{12,8},{1,5},{5,1},{9,13},{13,9},{2,6},{6,2},{1... | collective-permute-start | bytes 196616 | tf_op jit(solution)/shard_map/ppermute | solution.py:206
  42.3 2.9 %collective-permute-start.16 = (bf16[16,2048]{1,0:T(8,128)(2,1)S(1)}, bf16[16,2048]{1,0:T(8,128)(2,1)S(1)}, u32[]{:S(2)}, u32[]{:S(2)}) collective-permute-start(bf16[16,2048]{1,0:T(8,128)(2,1)S(1)} %collective-permute-done.14.refs_3_), channel_id=1, source_target_pairs={{0,4},{4,0},{8,12},{12,8},{1,5},{5,1},{9,13},{13,9},{2,6},{6,2},{1... | collective-permute-start | bytes 196616 | tf_op jit(solution)/shard_map/ppermute | solution.py:206
  45.2 2.2 %shard_map.89.refs_6_.weight = bf16[2048,1024]{1,0:T(8,128)(2,1)S(1)} custom-call(bf16[4096,2048]{1,0:T(8,128)(2,1)} %weight.5, bf16[32,2048]{1,0:T(8,128)(2,1)S(1)} %get-tuple-element.48.attended.refs_0_), custom_call_target="tpu_custom_call" | custom-call | bytes 4194304 | tf_op jit(solution)/shard_map/pallas_call | solution.py:675
  47.4 0.8 %shard_map.90 = (bf16[128,1024]{1,0:T(8,128)(2,1)S(1)}, bf16[128,2048]{1,0:T(8,128)(2,1)S(1)}) custom-call(bf16[128,128]{1,0:T(8,128)(2,1)S(1)} %get-tuple-element.49.chosen, bf16[32,2048]{1,0:T(8,128)(2,1)S(1)} %get-tuple-element.48.attended.refs_0_, bf16[32,2048]{1,0:T(8,128)(2,1)S(1)} %collective-permute-done.12.refs_1_, ...), custom_call_target="tpu_custom_call" | custom-call | flops 536870912 | bytes 4194304 | tf_op jit(solution)/shard_map/pallas_call | solution.py:392
  48.3 0.0 copy-start
  48.3 0.1 collective-permute-start.17
  48.4 0.7 %shard_map.91.own = f32[128,1024]{1,0:T(8,128)S(1)} custom-call(bf16[128,2048]{1,0:T(8,128)(2,1)S(1)} %get-tuple-element.53.permuted, bf16[2048,1024]{1,0:T(8,128)(2,1)S(1)} %shard_map.89.refs_6_.weight), custom_call_target="tpu_custom_call" | custom-call | flops 536870912 | bytes 4194304 | tf_op jit(solution)/shard_map/pallas_call | solution.py:401
  49.1 0.8 %collective-permute-done.17.received = bf16[128,1024]{1,0:T(8,128)(2,1)S(1)} collective-permute-done((bf16[128,1024]{1,0:T(8,128)(2,1)S(1)}, bf16[128,1024]{1,0:T(8,128)(2,1)S(1)}, u32[]{:S(2)}, u32[]{:S(2)}) %collective-permute-start.17) | collective-permute-done | bytes 262176 | tf_op jit(solution)/shard_map/ppermute | solution.py:206
  50.0 1.6 %collective-permute-start.18 = (bf16[32,1024]{1,0:T(8,128)(2,1)S(1)}, bf16[32,1024]{1,0:T(8,128)(2,1)S(1)}, u32[]{:S(2)}, u32[]{:S(2)}) collective-permute-start(bf16[32,1024]{1,0:T(8,128)(2,1)S(1)} %get-tuple-element.55), channel_id=1, source_target_pairs={{0,8},{4,12},{8,0},{12,4},{1,9},{5,13},{9,1},{13,5},{2,10},{6,14},... | collective-permute-start | bytes 196616 | tf_op jit(solution)/shard_map/ppermute | solution.py:206
  51.6 2.8 %collective-permute-start.19 = (bf16[32,1024]{1,0:T(8,128)(2,1)S(1)}, bf16[32,1024]{1,0:T(8,128)(2,1)S(1)}, u32[]{:S(2)}, u32[]{:S(2)}) collective-permute-start(bf16[32,1024]{1,0:T(8,128)(2,1)S(1)} %get-tuple-element.56), channel_id=1, source_target_pairs={{0,12},{2,4},{4,8},{6,0},{8,14},{10,6},{12,10},{14,2},{1,13},{3,5}... | collective-permute-start | bytes 196616 | tf_op jit(solution)/shard_map/ppermute | solution.py:453
  54.4 1.5 %collective-permute-done.18.passed.refs_0_ = bf16[32,1024]{1,0:T(8,128)(2,1)S(1)} collective-permute-done((bf16[32,1024]{1,0:T(8,128)(2,1)S(1)}, bf16[32,1024]{1,0:T(8,128)(2,1)S(1)}, u32[]{:S(2)}, u32[]{:S(2)}) %collective-permute-start.18) | collective-permute-done | bytes 65568 | tf_op jit(solution)/shard_map/ppermute | solution.py:206
  55.9 1.6 %collective-permute-start.21 = (bf16[32,1024]{1,0:T(8,128)(2,1)S(1)}, bf16[32,1024]{1,0:T(8,128)(2,1)S(1)}, u32[]{:S(2)}, u32[]{:S(2)}) collective-permute-start(bf16[32,1024]{1,0:T(8,128)(2,1)S(1)} %shard_map.93), channel_id=1, source_target_pairs={{0,2},{2,0},{1,3},{3,1},{4,6},{6,4},{5,7},{7,5},{8,10},{10,8},{9,1... | collective-permute-start | bytes 196616 | tf_op jit(solution)/shard_map/ppermute | solution.py:206
  57.5 2.4 %collective-permute-done.20.refs_2_ = bf16[32,1024]{1,0:T(8,128)(2,1)S(1)} collective-permute-done((bf16[32,1024]{1,0:T(8,128)(2,1)S(1)}, bf16[32,1024]{1,0:T(8,128)(2,1)S(1)}, u32[]{:S(2)}, u32[]{:S(2)}) %collective-permute-start.20) | collective-permute-done | bytes 65568 | tf_op jit(solution)/shard_map/ppermute | solution.py:453
  59.9 0.3 collective-permute-done.21.refs_4_
  60.2 0.1 shard_map.94
  60.3 0.1 collective-permute-start.22
  60.4 1.3 %collective-permute-done.22.received = bf16[32,2048]{1,0:T(8,128)(2,1)S(1)} collective-permute-done((bf16[32,2048]{1,0:T(8,128)(2,1)S(1)}, bf16[32,2048]{1,0:T(8,128)(2,1)S(1)}, u32[]{:S(2)}, u32[]{:S(2)}) %collective-permute-start.22) | collective-permute-done | bytes 131104 | tf_op jit(solution)/shard_map/ppermute | solution.py:206
  61.7 0.7 %shard_map.95 = bf16[1,32,4096]{2,1,0:T(8,128)(2,1)} custom-call(bf16[32,2048]{1,0:T(8,128)(2,1)S(1)} %get-tuple-element.59.keep, bf16[32,2048]{1,0:T(8,128)(2,1)S(1)} %collective-permute-done.22.received), custom_call_target="tpu_custom_call" | custom-call | bytes 524288 | tf_op jit(solution)/shard_map/pallas_call | solution.py:696
  (21 shorter events, 0.1 us)
Async XLA Ops:
  0.9 7.9 %collective-permute-start.2 = (bf16[16,2048]{1,0:T(8,128)(2,1)S(1)}, bf16[16,2048]{1,0:T(8,128)(2,1)S(1)}, u32[]{:S(2)}, u32[]{:S(2)}) collective-permute-start(bf16[16,2048]{1,0:T(8,128)(2,1)S(1)} %get-tuple-element.62.refs_0_), channel_id=1, source_target_pairs={{0,8},{4,12},{8,0},{12,4},{1,9},{5,13},{9,1},{13,5},{2,10},{6,14},... | collective-permute-start | bytes 196616 | tf_op jit(solution)/shard_map/ppermute | solution.py:206
  5.0 11.5 %copy-start.1 = (bf16[4096]{0:T(1024)(128)(2,1)S(1)}, bf16[4096]{0:T(1024)(128)(2,1)}, u32[]{:S(2)}) copy-start(bf16[4096]{0:T(1024)(128)(2,1)} %param.9) | copy-start | bytes 24580
  5.0 6.1 %collective-permute-start.3 = (bf16[16,2048]{1,0:T(8,128)(2,1)S(1)}, bf16[16,2048]{1,0:T(8,128)(2,1)S(1)}, u32[]{:S(2)}, u32[]{:S(2)}) collective-permute-start(bf16[16,2048]{1,0:T(8,128)(2,1)S(1)} %get-tuple-element.61.refs_1_), channel_id=1, source_target_pairs={{0,8},{4,12},{8,0},{12,4},{1,9},{5,13},{9,1},{13,5},{2,10},{6,14},... | collective-permute-start | bytes 196616 | tf_op jit(solution)/shard_map/ppermute | solution.py:206
  5.1 11.4 %collective-permute-start = (bf16[16,2048]{1,0:T(8,128)(2,1)S(1)}, bf16[16,2048]{1,0:T(8,128)(2,1)S(1)}, u32[]{:S(2)}, u32[]{:S(2)}) collective-permute-start(bf16[16,2048]{1,0:T(8,128)(2,1)S(1)} %get-tuple-element.62.refs_0_), channel_id=1, source_target_pairs={{0,4},{4,0},{8,12},{12,8},{1,5},{5,1},{9,13},{13,9},{2,6},{6,2},{1... | collective-permute-start | bytes 196616 | tf_op jit(solution)/shard_map/ppermute | solution.py:206
  6.9 9.6 %collective-permute-start.1 = (bf16[16,2048]{1,0:T(8,128)(2,1)S(1)}, bf16[16,2048]{1,0:T(8,128)(2,1)S(1)}, u32[]{:S(2)}, u32[]{:S(2)}) collective-permute-start(bf16[16,2048]{1,0:T(8,128)(2,1)S(1)} %get-tuple-element.61.refs_1_), channel_id=1, source_target_pairs={{0,4},{4,0},{8,12},{12,8},{1,5},{5,1},{9,13},{13,9},{2,6},{6,2},{1... | collective-permute-start | bytes 196616 | tf_op jit(solution)/shard_map/ppermute | solution.py:206
  8.7 7.8 %collective-permute-start.4 = (bf16[16,2048]{1,0:T(8,128)(2,1)S(1)}, bf16[16,2048]{1,0:T(8,128)(2,1)S(1)}, u32[]{:S(2)}, u32[]{:S(2)}) collective-permute-start(bf16[16,2048]{1,0:T(8,128)(2,1)S(1)} %collective-permute-done.2.refs_4_), channel_id=1, source_target_pairs={{0,4},{4,0},{8,12},{12,8},{1,5},{5,1},{9,13},{13,9},{2,6},{6,2},{1... | collective-permute-start | bytes 196616 | tf_op jit(solution)/shard_map/ppermute | solution.py:206
  11.1 5.4 %collective-permute-start.5 = (bf16[16,2048]{1,0:T(8,128)(2,1)S(1)}, bf16[16,2048]{1,0:T(8,128)(2,1)S(1)}, u32[]{:S(2)}, u32[]{:S(2)}) collective-permute-start(bf16[16,2048]{1,0:T(8,128)(2,1)S(1)} %collective-permute-done.3.refs_5_), channel_id=1, source_target_pairs={{0,4},{4,0},{8,12},{12,8},{1,5},{5,1},{9,13},{13,9},{2,6},{6,2},{1... | collective-permute-start | bytes 196616 | tf_op jit(solution)/shard_map/ppermute | solution.py:206
  17.6 12.2 %copy-start.2 = (s32[128]{0:T(128)S(1)}, s32[128]{0:T(128)}, u32[]{:S(2)}) copy-start(s32[128]{0:T(128)} %slots.3) | copy-start | bytes 1540
  17.6 12.2 %copy-start.3 = (s32[32]{0:T(128)S(1)}, s32[32]{0:T(128)}, u32[]{:S(2)}) copy-start(s32[32]{0:T(128)} %lengths.1) | copy-start | bytes 388
  17.6 1.7 %collective-permute-start.6 = (bf16[128,1408]{1,0:T(8,128)(2,1)S(1)}, bf16[128,1408]{1,0:T(8,128)(2,1)S(1)}, u32[]{:S(2)}, u32[]{:S(2)}) collective-permute-start(bf16[128,1408]{1,0:T(8,128)(2,1)S(1)} %get-tuple-element.40.given), channel_id=1, source_target_pairs={{0,1},{1,0},{2,3},{3,2},{4,5},{5,4},{6,7},{7,6},{8,9},{9,8},{10,11... | collective-permute-start | bytes 1081352 | tf_op jit(solution)/shard_map/ppermute | solution.py:206
  19.5 7.8 %collective-permute-start.7 = (bf16[32,1280]{1,0:T(8,128)(2,1)S(1)}, bf16[32,1280]{1,0:T(8,128)(2,1)S(1)}, u32[]{:S(2)}, u32[]{:S(2)}) collective-permute-start(bf16[32,1280]{1,0:T(8,128)(2,1)S(1)} %get-tuple-element.41), channel_id=1, source_target_pairs={{0,8},{4,12},{8,0},{12,4},{1,9},{5,13},{9,1},{13,5},{2,10},{6,14},... | collective-permute-start | bytes 245768 | tf_op jit(solution)/shard_map/ppermute | solution.py:206
  22.6 3.7 %collective-permute-start.10 = (bf16[32,128]{1,0:T(8,128)(2,1)S(1)}, bf16[32,128]{1,0:T(8,128)(2,1)S(1)}, u32[]{:S(2)}, u32[]{:S(2)}) collective-permute-start(bf16[32,128]{1,0:T(8,128)(2,1)S(1)} %get-tuple-element.45.refs_5_), channel_id=1, source_target_pairs={{0,2},{2,0},{1,3},{3,1},{4,6},{6,4},{5,7},{7,5},{8,10},{10,8},{9,1... | collective-permute-start | bytes 24584 | tf_op jit(solution)/shard_map/ppermute | solution.py:206
  24.1 9.4 %collective-permute-start.8 = (bf16[32,1280]{1,0:T(8,128)(2,1)S(1)}, bf16[32,1280]{1,0:T(8,128)(2,1)S(1)}, u32[]{:S(2)}, u32[]{:S(2)}) collective-permute-start(bf16[32,1280]{1,0:T(8,128)(2,1)S(1)} %get-tuple-element.42), channel_id=1, source_target_pairs={{0,12},{2,4},{4,8},{6,0},{8,14},{10,6},{12,10},{14,2},{1,13},{3,5}... | collective-permute-start | bytes 245768 | tf_op jit(solution)/shard_map/ppermute | solution.py:453
  24.5 9.1 %collective-permute-start.9 = (bf16[32,1280]{1,0:T(8,128)(2,1)S(1)}, bf16[32,1280]{1,0:T(8,128)(2,1)S(1)}, u32[]{:S(2)}, u32[]{:S(2)}) collective-permute-start(bf16[32,1280]{1,0:T(8,128)(2,1)S(1)} %get-tuple-element.43), channel_id=1, source_target_pairs={{0,4},{2,12},{4,0},{6,8},{8,6},{10,14},{12,2},{14,10},{1,5},{3,13}... | collective-permute-start | bytes 245768 | tf_op jit(solution)/shard_map/ppermute | solution.py:453
  27.2 6.4 %collective-permute-start.11 = (bf16[32,1280]{1,0:T(8,128)(2,1)S(1)}, bf16[32,1280]{1,0:T(8,128)(2,1)S(1)}, u32[]{:S(2)}, u32[]{:S(2)}) collective-permute-start(bf16[32,1280]{1,0:T(8,128)(2,1)S(1)} %shard_map.87), channel_id=1, source_target_pairs={{0,2},{2,0},{1,3},{3,1},{4,6},{6,4},{5,7},{7,5},{8,10},{10,8},{9,1... | collective-permute-start | bytes 245768 | tf_op jit(solution)/shard_map/ppermute | solution.py:206
  35.3 5.7 %collective-permute-start.13 = (bf16[16,2048]{1,0:T(8,128)(2,1)S(1)}, bf16[16,2048]{1,0:T(8,128)(2,1)S(1)}, u32[]{:S(2)}, u32[]{:S(2)}) collective-permute-start(bf16[16,2048]{1,0:T(8,128)(2,1)S(1)} %get-tuple-element.50), channel_id=1, source_target_pairs={{0,8},{4,12},{8,0},{12,4},{1,9},{5,13},{9,1},{13,5},{2,10},{6,14},... | collective-permute-start | bytes 196616 | tf_op jit(solution)/shard_map/ppermute | solution.py:206
  35.8 6.5 %collective-permute-start.14 = (bf16[16,2048]{1,0:T(8,128)(2,1)S(1)}, bf16[16,2048]{1,0:T(8,128)(2,1)S(1)}, u32[]{:S(2)}, u32[]{:S(2)}) collective-permute-start(bf16[16,2048]{1,0:T(8,128)(2,1)S(1)} %get-tuple-element.51), channel_id=1, source_target_pairs={{0,8},{4,12},{8,0},{12,4},{1,9},{5,13},{9,1},{13,5},{2,10},{6,14},... | collective-permute-start | bytes 196616 | tf_op jit(solution)/shard_map/ppermute | solution.py:206
  38.3 9.1 %collective-permute-start.12 = (bf16[32,2048]{1,0:T(8,128)(2,1)S(1)}, bf16[32,2048]{1,0:T(8,128)(2,1)S(1)}, u32[]{:S(2)}, u32[]{:S(2)}) collective-permute-start(bf16[32,2048]{1,0:T(8,128)(2,1)S(1)} %get-tuple-element.48.attended.refs_0_), channel_id=1, source_target_pairs={{0,4},{4,0},{8,12},{12,8},{1,5},{5,1},{9,13},{13,9},{2,6},{6,2},{1... | collective-permute-start | bytes 393224 | tf_op jit(solution)/shard_map/ppermute | solution.py:206
  41.0 6.5 %collective-permute-start.15 = (bf16[16,2048]{1,0:T(8,128)(2,1)S(1)}, bf16[16,2048]{1,0:T(8,128)(2,1)S(1)}, u32[]{:S(2)}, u32[]{:S(2)}) collective-permute-start(bf16[16,2048]{1,0:T(8,128)(2,1)S(1)} %collective-permute-done.13.refs_2_), channel_id=1, source_target_pairs={{0,4},{4,0},{8,12},{12,8},{1,5},{5,1},{9,13},{13,9},{2,6},{6,2},{1... | collective-permute-start | bytes 196616 | tf_op jit(solution)/shard_map/ppermute | solution.py:206
  42.3 5.1 %collective-permute-start.16 = (bf16[16,2048]{1,0:T(8,128)(2,1)S(1)}, bf16[16,2048]{1,0:T(8,128)(2,1)S(1)}, u32[]{:S(2)}, u32[]{:S(2)}) collective-permute-start(bf16[16,2048]{1,0:T(8,128)(2,1)S(1)} %collective-permute-done.14.refs_3_), channel_id=1, source_target_pairs={{0,4},{4,0},{8,12},{12,8},{1,5},{5,1},{9,13},{13,9},{2,6},{6,2},{1... | collective-permute-start | bytes 196616 | tf_op jit(solution)/shard_map/ppermute | solution.py:206
  48.3 11.9 %copy-start = (bf16[32,4096]{1,0:T(8,128)(2,1)S(1)}, bf16[32,4096]{1,0:T(8,128)(2,1)}, u32[]{:S(2)}) copy-start(bf16[32,4096]{1,0:T(8,128)(2,1)} %hidden.1) | copy-start | bytes 786436
  48.3 1.6 %collective-permute-start.17 = (bf16[128,1024]{1,0:T(8,128)(2,1)S(1)}, bf16[128,1024]{1,0:T(8,128)(2,1)S(1)}, u32[]{:S(2)}, u32[]{:S(2)}) collective-permute-start(bf16[128,1024]{1,0:T(8,128)(2,1)S(1)} %get-tuple-element.54.given), channel_id=1, source_target_pairs={{0,1},{1,0},{2,3},{3,2},{4,5},{5,4},{6,7},{7,6},{8,9},{9,8},{10,11... | collective-permute-start | bytes 786440 | tf_op jit(solution)/shard_map/ppermute | solution.py:206
  50.0 5.9 %collective-permute-start.18 = (bf16[32,1024]{1,0:T(8,128)(2,1)S(1)}, bf16[32,1024]{1,0:T(8,128)(2,1)S(1)}, u32[]{:S(2)}, u32[]{:S(2)}) collective-permute-start(bf16[32,1024]{1,0:T(8,128)(2,1)S(1)} %get-tuple-element.55), channel_id=1, source_target_pairs={{0,8},{4,12},{8,0},{12,4},{1,9},{5,13},{9,1},{13,5},{2,10},{6,14},... | collective-permute-start | bytes 196616 | tf_op jit(solution)/shard_map/ppermute | solution.py:206
  51.6 5.9 %collective-permute-start.19 = (bf16[32,1024]{1,0:T(8,128)(2,1)S(1)}, bf16[32,1024]{1,0:T(8,128)(2,1)S(1)}, u32[]{:S(2)}, u32[]{:S(2)}) collective-permute-start(bf16[32,1024]{1,0:T(8,128)(2,1)S(1)} %get-tuple-element.56), channel_id=1, source_target_pairs={{0,12},{2,4},{4,8},{6,0},{8,14},{10,6},{12,10},{14,2},{1,13},{3,5}... | collective-permute-start | bytes 196616 | tf_op jit(solution)/shard_map/ppermute | solution.py:453
  54.4 5.6 %collective-permute-start.20 = (bf16[32,1024]{1,0:T(8,128)(2,1)S(1)}, bf16[32,1024]{1,0:T(8,128)(2,1)S(1)}, u32[]{:S(2)}, u32[]{:S(2)}) collective-permute-start(bf16[32,1024]{1,0:T(8,128)(2,1)S(1)} %get-tuple-element.57), channel_id=1, source_target_pairs={{0,4},{2,12},{4,0},{6,8},{8,6},{10,14},{12,2},{14,10},{1,5},{3,13}... | collective-permute-start | bytes 196616 | tf_op jit(solution)/shard_map/ppermute | solution.py:453
  55.9 4.3 %collective-permute-start.21 = (bf16[32,1024]{1,0:T(8,128)(2,1)S(1)}, bf16[32,1024]{1,0:T(8,128)(2,1)S(1)}, u32[]{:S(2)}, u32[]{:S(2)}) collective-permute-start(bf16[32,1024]{1,0:T(8,128)(2,1)S(1)} %shard_map.93), channel_id=1, source_target_pairs={{0,2},{2,0},{1,3},{3,1},{4,6},{6,4},{5,7},{7,5},{8,10},{10,8},{9,1... | collective-permute-start | bytes 196616 | tf_op jit(solution)/shard_map/ppermute | solution.py:206
  60.3 1.4 %collective-permute-start.22 = (bf16[32,2048]{1,0:T(8,128)(2,1)S(1)}, bf16[32,2048]{1,0:T(8,128)(2,1)S(1)}, u32[]{:S(2)}, u32[]{:S(2)}) collective-permute-start(bf16[32,2048]{1,0:T(8,128)(2,1)S(1)} %get-tuple-element.60), channel_id=1, source_target_pairs={{0,1},{1,0},{2,3},{3,2},{4,5},{5,4},{6,7},{7,6},{8,9},{9,8},{10,11... | collective-permute-start | bytes 393224 | tf_op jit(solution)/shard_map/ppermute | solution.py:206

commit v19 on v18

--- a/solution.py
+++ b/solution.py
@@ -232,20 +232,14 @@
     return weight.at[rows, columns], target
 
 
-def stage_in_kernel(blocks, weight, slots, give_part, own_part, chosen, scratch, slot_part, sems):
+def stage_in_kernel(blocks, weight, slots, give_part, chosen, scratch, slot_part, sems):
     side, col = position()
-    slots_copy, *copies = started(
-        [
-            (slots, slot_part),
-            rows_copy(weight, give_part, 1 - side),
-            rows_copy(weight, own_part, side),
-        ],
-        sems,
+    slots_copy, copy = started(
+        [(slots, slot_part), rows_copy(weight, give_part, 1 - side)], sems
     )
     slots_copy.wait()
     chosen[...] = one_hot(slot_part, scratch, blocks, col, col).astype(jnp.bfloat16)
-    for copy in copies:
-        copy.wait()
+    copy.wait()
 
 
 def head_copies(weight, target, half):
@@ -318,7 +312,7 @@
 
 
 def in_kernel(count, chosen, *refs):
-    pieces_in, (_, gain, weight, give, permuted) = refs[:count], refs[count:]
+    pieces_in, (gain, weight, give, permuted) = refs[:count], refs[count:]
     depth = pieces_in[0].shape[1]
     half = weight.shape[1]
     runs = depth // HEAD_DIM
@@ -378,34 +372,57 @@
         out[...] = jnp.concatenate([given[:rows, lanes], received[:rows, lanes]], axis=1)
 
 
+def own_stream_kernel(permuted, weight, own, chunks, sems):
+    count, depth, width = chunks.shape
+    side = lax.axis_index("side")
+    rows = pl.ds(pl.multiple_of(side * depth, depth), depth)
+    copies = []
+    for i in range(count):
+        first = pl.multiple_of((side * count + i) * width, width)
+        copies.append((weight.at[rows, pl.ds(first, width)], chunks.at[i]))
+    for i, copy in enumerate(started(copies, sems)):
+        copy.wait()
+        own[:, i * width : (i + 1) * width] = jnp.dot(
+            permuted[...], chunks[i], preferred_element_type=jnp.float32
+        )
+
+
 def own_kernel(permuted, weight, own):
     dot_columns(permuted[...], weight, own)
 
 
-def project(kernel, chosen, pieces_in, extra, weights, more):
+def project(kernel, chosen, pieces_in, extra, give_weight, own_weight, more):
     count = lax.axis_size("col")
     parts = len(pieces_in)
     depth = pieces_in[0].shape[1]
     rows = sum(part.shape[0] for part in pieces_in)
-    half = weights[0].shape[1]
+    half = give_weight.shape[1]
     flops = 2 * rows * depth * half
     give, permuted = call(
         functools.partial(kernel, parts),
         [struct((rows, half + more)), struct((rows, depth))],
-        [VMEM] * (parts + len(extra) + 3),
+        [VMEM] * (parts + len(extra) + 2),
         [VMEM, VMEM],
         flops,
         depth * half * 2,
-    )(chosen, *pieces_in, in_vmem(weights[1]), *extra, in_vmem(weights[0]))
+    )(chosen, *pieces_in, *extra, in_vmem(give_weight))
     received = moved(give, "side", 1)
+    staged = own_weight.shape == give_weight.shape
+    width = 256
     own = call(
-        own_kernel,
+        own_kernel if staged else own_stream_kernel,
         struct((rows, half), jnp.float32),
-        [VMEM, VMEM],
+        [VMEM, VMEM if staged else HBM],
         VMEM,
         flops,
         depth * half * 2,
-    )(permuted, in_vmem(weights[1]))
+        []
+        if staged
+        else [
+            pltpu.VMEM((half // width, depth, width), jnp.bfloat16),
+            pltpu.SemaphoreType.DMA((half // width,)),
+        ],
+    )(permuted, in_vmem(own_weight) if staged else in_hbm(own_weight))
     outs = [struct((rows // count, half))] * count
     if more:
         outs = outs + [struct((rows // count, more))]
@@ -622,17 +639,17 @@
     half_in, half_out = qkv_weight.shape[1] // 2, out_weight.shape[1] // 2
     total = rows * col_count
     square = (total, total)
-    give_in, own_in, chosen_in = call(
+    give_in, chosen_in = call(
         functools.partial(stage_in_kernel, col_count),
-        [pltpu.VMEM((half, half_in), jnp.bfloat16)] * 2 + [struct(square)],
+        [pltpu.VMEM((half, half_in), jnp.bfloat16), struct(square)],
         [HBM, HBM],
-        [VMEM] * 3,
+        [VMEM] * 2,
         0,
-        half * half_in * 4,
+        half * half_in * 2,
         [
             pltpu.VMEM(square, jnp.float32),
             pltpu.VMEM((total,), jnp.int32),
-            pltpu.SemaphoreType.DMA((3,)),
+            pltpu.SemaphoreType.DMA((2,)),
         ],
     )(in_hbm(qkv_weight), in_hbm(slot_request))
     blocks = gathered(
@@ -650,7 +667,7 @@
         half * half_out * 2 + 4 * rows * cache * pairs * HEAD_DIM,
         [pltpu.VMEM(square, jnp.float32), pltpu.SemaphoreType.DMA((3 * pairs,))],
     )(cache_lengths, in_hbm(out_weight), in_hbm(key_cache), in_hbm(value_cache), slot_request)
-    products, sums = project(in_kernel, chosen_in, blocks, [gain], [give_in, own_in], HEAD_DIM)
+    products, sums = project(in_kernel, chosen_in, blocks, [gain], give_in, qkv_weight, HEAD_DIM)
     other_sums = moved(sums[0], "row", 1)
     products = spread(products, [other_sums])
 
@@ -682,7 +699,7 @@
         [pltpu.SemaphoreType.DMA((pairs,))],
     )(in_hbm(out_weight), attended)
     products, _ = project(
-        out_kernel, chosen_out, gathered(attended_parts, "col", attended), [], [give_out, own_out], 0
+        out_kernel, chosen_out, gathered(attended_parts, "col", attended), [in_vmem(own_out)], give_out, own_out, 0
     )
     products = spread(products, [])
     keep, send = call(
@@ -714,6 +731,7 @@
         and col_count > row_count
         and col_count & (col_count - 1) == 0
         and hidden_in.shape[0] % 32 == 0
+        and GROUP_WIDTH % 256 == 0
         and key_cache.shape[1] % 16 == 0
         and hidden_in.shape[1] == 2 * OUT_WIDTH * (col_count // row_count)
     )

time: 62.6 us -> 64.6 us (1.032)
  waiting for transfers between devices: 13.2 us -> 15 us
  Pallas kernels: 16.2 us -> 17.1 us
  starting transfers between devices: 32 us -> 31.3 us
    ppermute x19, waiting for transfers between devices: 10.7 us -> 15 us  [moved(): return lax.ppermute(value, axis, pairs)]
    pallas_call x2, Pallas kernels: 1.58 us -> 4.02 us  [project(): call(own_kernel if staged else own_stream_kernel, struct((rows, half), jn...]
    ppermute x4, waiting for transfers between devices: 2.44 us -> 0.01 us  [direct(): return lax.ppermute(value, ('col', 'row'), moves)]
    pallas_call x1, Pallas kernels: 4.09 us -> 2.52 us  [paired_plan(): call(functools.partial(stage_in_kernel, col_count), [pltpu.VMEM((half, ha...]
    ppermute x4, starting transfers between devices: 3.53 us -> 2.85 us  [direct(): return lax.ppermute(value, ('col', 'row'), moves)]
  transfers between devices with their start and end apart: 23 -> 23, of which waited for: 11 -> 12; matrix products, arithmetic and copies ran while one was open for 0% -> 0% of each run, Pallas kernels for 19% -> 19%
where the time goes in v19:
time: 64.6 us; the launch traced here: 64.4 us
  starting transfers between devices  31.3 us (48%)
  Pallas kernels  17.1 us (26%)
  waiting for transfers between devices  15 us (23%)
  local copies, waits for them, and re-layouts  0.9 us (1%)
    ppermute x19, starting transfers between devices, moved(): return lax.ppermute(value, axis, pairs)  28.4 us
    ppermute x19, waiting for transfers between devices, moved(): return lax.ppermute(value, axis, pairs)  15 us
    pallas_call x2, Pallas kernels, project(): call(own_kernel if staged else own_stream_kernel, struct((rows, half), jn...  4.02 us
    pallas_call x1, Pallas kernels, paired_plan(): call(functools.partial(stage_rest_kernel, col_count), [pltpu.VMEM((half,...  3.71 us
    ppermute x4, starting transfers between devices, direct(): return lax.ppermute(value, ('col', 'row'), moves)  2.85 us
    pallas_call x1, Pallas kernels, paired_plan(): call(functools.partial(stage_in_kernel, col_count), [pltpu.VMEM((half, ha...  2.52 us
    pallas_call x1, Pallas kernels, paired_plan(): call(stage_out_kernel, pltpu.VMEM((half, half_out), jnp.bfloat16), [HBM,...  2.24 us
    pallas_call x2, Pallas kernels, project(): call(functools.partial(kernel, parts), [struct((rows, half + more)), stru...  1.91 us
  transfers between devices with their start and end apart: 23, of which 12 were waited for; matrix products, arithmetic and copies ran while one was open for 0% of the time, Pallas kernels for 19%

profile of v19, /device:TPU:0, one launch (start us, length us, event | category | flops | bytes accessed | tf_op | source)
XLA Modules:
  0.0 64.4 jit_solution(3615862260222807038)
XLA Ops:
  0.0 0.9 %fusion = (bf16[16,2048]{1,0:T(8,128)(2,1)S(1)}, bf16[16,2048]{1,0:T(8,128)(2,1)S(1)}) fusion(bf16[32,4096]{1,0:T(8,128)(2,1)} %hidden.1, s32[]{:T(128)S(6)} %add.4, s32[]{:T(128)S(6)} %select_n.3), kind=kLoop, calls=%fused_computation.1 | loop fusion | bytes 262152 | tf_op jit(solution)/shard_map/slice | solution.py:656
  0.9 4.1 %collective-permute-start.3 = (bf16[16,2048]{1,0:T(8,128)(2,1)S(1)}, bf16[16,2048]{1,0:T(8,128)(2,1)S(1)}, u32[]{:S(2)}, u32[]{:S(2)}) collective-permute-start(bf16[16,2048]{1,0:T(8,128)(2,1)S(1)} %get-tuple-element.59.refs_1_), channel_id=1, source_target_pairs={{0,8},{4,12},{8,0},{12,4},{1,9},{5,13},{9,1},{13,5},{2,10},{6,14},... | collective-permute-start | bytes 196616 | tf_op jit(solution)/shard_map/ppermute | solution.py:206
  5.0 0.1 collective-permute-start.2
  5.1 1.8 %collective-permute-start.1 = (bf16[16,2048]{1,0:T(8,128)(2,1)S(1)}, bf16[16,2048]{1,0:T(8,128)(2,1)S(1)}, u32[]{:S(2)}, u32[]{:S(2)}) collective-permute-start(bf16[16,2048]{1,0:T(8,128)(2,1)S(1)} %get-tuple-element.59.refs_1_), channel_id=1, source_target_pairs={{0,4},{4,0},{8,12},{12,8},{1,5},{5,1},{9,13},{13,9},{2,6},{6,2},{1... | collective-permute-start | bytes 196616 | tf_op jit(solution)/shard_map/ppermute | solution.py:206
  6.9 0.2 collective-permute-start
  7.1 1.6 %collective-permute-done.3.refs_5_ = bf16[16,2048]{1,0:T(8,128)(2,1)S(1)} collective-permute-done((bf16[16,2048]{1,0:T(8,128)(2,1)S(1)}, bf16[16,2048]{1,0:T(8,128)(2,1)S(1)}, u32[]{:S(2)}, u32[]{:S(2)}) %collective-permute-start.3) | collective-permute-done | bytes 65568 | tf_op jit(solution)/shard_map/ppermute | solution.py:206
  8.7 1.9 %collective-permute-start.5 = (bf16[16,2048]{1,0:T(8,128)(2,1)S(1)}, bf16[16,2048]{1,0:T(8,128)(2,1)S(1)}, u32[]{:S(2)}, u32[]{:S(2)}) collective-permute-start(bf16[16,2048]{1,0:T(8,128)(2,1)S(1)} %collective-permute-done.3.refs_5_), channel_id=1, source_target_pairs={{0,4},{4,0},{8,12},{12,8},{1,5},{5,1},{9,13},{13,9},{2,6},{6,2},{1... | collective-permute-start | bytes 196616 | tf_op jit(solution)/shard_map/ppermute | solution.py:206
  10.6 0.4 collective-permute-done.2.refs_4_
  11.1 1.3 %collective-permute-start.4 = (bf16[16,2048]{1,0:T(8,128)(2,1)S(1)}, bf16[16,2048]{1,0:T(8,128)(2,1)S(1)}, u32[]{:S(2)}, u32[]{:S(2)}) collective-permute-start(bf16[16,2048]{1,0:T(8,128)(2,1)S(1)} %collective-permute-done.2.refs_4_), channel_id=1, source_target_pairs={{0,4},{4,0},{8,12},{12,8},{1,5},{5,1},{9,13},{13,9},{2,6},{6,2},{1... | collective-permute-start | bytes 196616 | tf_op jit(solution)/shard_map/ppermute | solution.py:206
  12.4 2.5 %shard_map.83 = (bf16[2048,1280]{1,0:T(8,128)(2,1)S(1)}, bf16[128,128]{1,0:T(8,128)(2,1)S(1)}) custom-call(bf16[4096,2560]{1,0:T(8,128)(2,1)} %weight.6, s32[128]{0:T(128)} %slots.3), custom_call_target="tpu_custom_call" | custom-call | bytes 5242880 | tf_op jit(solution)/shard_map/pallas_call | solution.py:642
  14.9 0.4 collective-permute-done.4.refs_6_
  15.3 1.1 %shard_map.84 = (bf16[128,1408]{1,0:T(8,128)(2,1)S(1)}, bf16[128,2048]{1,0:T(8,128)(2,1)S(1)}) custom-call(bf16[128,128]{1,0:T(8,128)(2,1)S(1)} %get-tuple-element.35.chosen, bf16[16,2048]{1,0:T(8,128)(2,1)S(1)} %get-tuple-element.60.refs_0_, bf16[16,2048]{1,0:T(8,128)(2,1)S(1)} %get-tuple-element.59.refs_1_, ...), custom_call_target="tpu_custom_call" | custom-call | flops 671088640 | bytes 5242880 | tf_op jit(solution)/shard_map/pallas_call | solution.py:401
  16.4 0.1 collective-permute-start.6
  16.5 0.0 copy-start.2
  16.5 0.0 copy-start.3
  16.5 3.3 %shard_map.85.own = f32[128,1280]{1,0:T(8,128)S(1)} custom-call(bf16[128,2048]{1,0:T(8,128)(2,1)S(1)} %get-tuple-element.37.permuted, bf16[4096,2560]{1,0:T(8,128)(2,1)} %weight.6), custom_call_target="tpu_custom_call" | custom-call | flops 671088640 | bytes 5242880 | tf_op jit(solution)/shard_map/pallas_call | solution.py:412
  19.8 0.1 shard_map.86
  19.9 3.2 %collective-permute-start.7 = (bf16[32,1280]{1,0:T(8,128)(2,1)S(1)}, bf16[32,1280]{1,0:T(8,128)(2,1)S(1)}, u32[]{:S(2)}, u32[]{:S(2)}) collective-permute-start(bf16[32,1280]{1,0:T(8,128)(2,1)S(1)} %get-tuple-element.39), channel_id=1, source_target_pairs={{0,8},{4,12},{8,0},{12,4},{1,9},{5,13},{9,1},{13,5},{2,10},{6,14},... | collective-permute-start | bytes 245768 | tf_op jit(solution)/shard_map/ppermute | solution.py:206
  23.1 1.5 %collective-permute-start.10 = (bf16[32,128]{1,0:T(8,128)(2,1)S(1)}, bf16[32,128]{1,0:T(8,128)(2,1)S(1)}, u32[]{:S(2)}, u32[]{:S(2)}) collective-permute-start(bf16[32,128]{1,0:T(8,128)(2,1)S(1)} %get-tuple-element.43.refs_5_), channel_id=1, source_target_pairs={{0,2},{2,0},{1,3},{3,1},{4,6},{6,4},{5,7},{7,5},{8,10},{10,8},{9,1... | collective-permute-start | bytes 24584 | tf_op jit(solution)/shard_map/ppermute | solution.py:206
  24.6 0.9 %collective-permute-start.8 = (bf16[32,1280]{1,0:T(8,128)(2,1)S(1)}, bf16[32,1280]{1,0:T(8,128)(2,1)S(1)}, u32[]{:S(2)}, u32[]{:S(2)}) collective-permute-start(bf16[32,1280]{1,0:T(8,128)(2,1)S(1)} %get-tuple-element.40), channel_id=1, source_target_pairs={{0,12},{2,4},{4,8},{6,0},{8,14},{10,6},{12,10},{14,2},{1,13},{3,5}... | collective-permute-start | bytes 245768 | tf_op jit(solution)/shard_map/ppermute | solution.py:470
  25.5 0.5 collective-permute-start.9
  26.0 0.8 %collective-permute-done.10.refs_0_.refs_6_ = bf16[32,128]{1,0:T(8,128)(2,1)S(1)} collective-permute-done((bf16[32,128]{1,0:T(8,128)(2,1)S(1)}, bf16[32,128]{1,0:T(8,128)(2,1)S(1)}, u32[]{:S(2)}, u32[]{:S(2)}) %collective-permute-start.10) | collective-permute-done | bytes 8224 | tf_op jit(solution)/shard_map/ppermute | solution.py:206
  26.8 1.2 %collective-permute-done.7.passed.refs_0_ = bf16[32,1280]{1,0:T(8,128)(2,1)S(1)} collective-permute-done((bf16[32,1280]{1,0:T(8,128)(2,1)S(1)}, bf16[32,1280]{1,0:T(8,128)(2,1)S(1)}, u32[]{:S(2)}, u32[]{:S(2)}) %collective-permute-start.7) | collective-permute-done | bytes 81952 | tf_op jit(solution)/shard_map/ppermute | solution.py:206
  28.0 2.9 %collective-permute-start.11 = (bf16[32,1280]{1,0:T(8,128)(2,1)S(1)}, bf16[32,1280]{1,0:T(8,128)(2,1)S(1)}, u32[]{:S(2)}, u32[]{:S(2)}) collective-permute-start(bf16[32,1280]{1,0:T(8,128)(2,1)S(1)} %shard_map.87), channel_id=1, source_target_pairs={{0,2},{2,0},{1,3},{3,1},{4,6},{6,4},{5,7},{7,5},{8,10},{10,8},{9,1... | collective-permute-start | bytes 245768 | tf_op jit(solution)/shard_map/ppermute | solution.py:206
  30.9 3.7 %shard_map.82 = (bf16[2048,1024]{1,0:T(8,128)(2,1)S(1)}, bf16[32,64,256]{2,1,0:T(8,128)(2,1)S(1)}, bf16[32,64,256]{2,1,0:T(8,128)(2,1)S(1)}, f32[32,128]{1,0:T(8...) custom-call(s32[32]{0:T(128)S(1)} %copy-done.3, bf16[4096,2048]{1,0:T(8,128)(2,1)} %weight.7, ...), custom_call_target="tpu_custom_call" | custom-call | bytes 6291456 | tf_op jit(solution)/shard_map/pallas_call | solution.py:659
  34.7 1.7 %shard_map.88 = (bf16[32,2048]{1,0:T(8,128)(2,1)S(1)}, bf16[16,2048]{1,0:T(8,128)(2,1)S(1)}, bf16[16,2048]{1,0:T(8,128)(2,1)S(1)}) custom-call(f32[32,128]{1,0:T(8,128)S(1)} %get-tuple-element.32.cosine, f32[32,128]{1,0:T(8,128)S(1)} %get-tuple-element.33.sine, s32[32,128]{1,0:T(8,128)S(1)} %get-tuple-element.34.lengths, ...), custom_call_target="tpu_custom_call" | custom-call | flops 16777216 | tf_op jit(solution)/shard_map/pallas_call | solution.py:675
  36.4 0.4 collective-permute-start.13
  36.8 2.6 %collective-permute-start.14 = (bf16[16,2048]{1,0:T(8,128)(2,1)S(1)}, bf16[16,2048]{1,0:T(8,128)(2,1)S(1)}, u32[]{:S(2)}, u32[]{:S(2)}) collective-permute-start(bf16[16,2048]{1,0:T(8,128)(2,1)S(1)} %get-tuple-element.49), channel_id=1, source_target_pairs={{0,8},{4,12},{8,0},{12,4},{1,9},{5,13},{9,1},{13,5},{2,10},{6,14},... | collective-permute-start | bytes 196616 | tf_op jit(solution)/shard_map/ppermute | solution.py:206
  39.4 1.0 %collective-permute-start.12 = (bf16[32,2048]{1,0:T(8,128)(2,1)S(1)}, bf16[32,2048]{1,0:T(8,128)(2,1)S(1)}, u32[]{:S(2)}, u32[]{:S(2)}) collective-permute-start(bf16[32,2048]{1,0:T(8,128)(2,1)S(1)} %get-tuple-element.46.attended.refs_0_), channel_id=1, source_target_pairs={{0,4},{4,0},{8,12},{12,8},{1,5},{5,1},{9,13},{13,9},{2,6},{6,2},{1... | collective-permute-start | bytes 393224 | tf_op jit(solution)/shard_map/ppermute | solution.py:206
  40.3 3.0 %collective-permute-done.13.refs_2_ = bf16[16,2048]{1,0:T(8,128)(2,1)S(1)} collective-permute-done((bf16[16,2048]{1,0:T(8,128)(2,1)S(1)}, bf16[16,2048]{1,0:T(8,128)(2,1)S(1)}, u32[]{:S(2)}, u32[]{:S(2)}) %collective-permute-start.13) | collective-permute-done | bytes 65568 | tf_op jit(solution)/shard_map/ppermute | solution.py:206
  43.3 0.7 %collective-permute-done.14.refs_3_ = bf16[16,2048]{1,0:T(8,128)(2,1)S(1)} collective-permute-done((bf16[16,2048]{1,0:T(8,128)(2,1)S(1)}, bf16[16,2048]{1,0:T(8,128)(2,1)S(1)}, u32[]{:S(2)}, u32[]{:S(2)}) %collective-permute-start.14) | collective-permute-done | bytes 65568 | tf_op jit(solution)/shard_map/ppermute | solution.py:206
  44.0 1.7 %collective-permute-start.16 = (bf16[16,2048]{1,0:T(8,128)(2,1)S(1)}, bf16[16,2048]{1,0:T(8,128)(2,1)S(1)}, u32[]{:S(2)}, u32[]{:S(2)}) collective-permute-start(bf16[16,2048]{1,0:T(8,128)(2,1)S(1)} %collective-permute-done.14.refs_3_), channel_id=1, source_target_pairs={{0,4},{4,0},{8,12},{12,8},{1,5},{5,1},{9,13},{13,9},{2,6},{6,2},{1... | collective-permute-start | bytes 196616 | tf_op jit(solution)/shard_map/ppermute | solution.py:206
  45.7 2.2 %shard_map.89.refs_6_.weight = bf16[2048,1024]{1,0:T(8,128)(2,1)S(1)} custom-call(bf16[4096,2048]{1,0:T(8,128)(2,1)} %weight.7, bf16[32,2048]{1,0:T(8,128)(2,1)S(1)} %get-tuple-element.46.attended.refs_0_), custom_call_target="tpu_custom_call" | custom-call | bytes 4194304 | tf_op jit(solution)/shard_map/pallas_call | solution.py:692
  48.0 0.3 collective-permute-done.16.refs_5_
  48.3 0.8 %shard_map.90 = (bf16[128,1024]{1,0:T(8,128)(2,1)S(1)}, bf16[128,2048]{1,0:T(8,128)(2,1)S(1)}) custom-call(bf16[128,128]{1,0:T(8,128)(2,1)S(1)} %get-tuple-element.47.chosen, bf16[32,2048]{1,0:T(8,128)(2,1)S(1)} %get-tuple-element.46.attended.refs_0_, bf16[32,2048]{1,0:T(8,128)(2,1)S(1)} %collective-permute-done.12.refs_1_, ...), custom_call_target="tpu_custom_call" | custom-call | flops 536870912 | bytes 4194304 | tf_op jit(solution)/shard_map/pallas_call | solution.py:401
  49.1 0.0 copy-start
  49.1 0.1 collective-permute-start.17
  49.2 0.7 %shard_map.91.own = f32[128,1024]{1,0:T(8,128)S(1)} custom-call(bf16[128,2048]{1,0:T(8,128)(2,1)S(1)} %get-tuple-element.51.permuted, bf16[2048,1024]{1,0:T(8,128)(2,1)S(1)} %shard_map.89.refs_6_.weight), custom_call_target="tpu_custom_call" | custom-call | flops 536870912 | bytes 4194304 | tf_op jit(solution)/shard_map/pallas_call | solution.py:412
  49.9 0.8 %collective-permute-done.17.received = bf16[128,1024]{1,0:T(8,128)(2,1)S(1)} collective-permute-done((bf16[128,1024]{1,0:T(8,128)(2,1)S(1)}, bf16[128,1024]{1,0:T(8,128)(2,1)S(1)}, u32[]{:S(2)}, u32[]{:S(2)}) %collective-permute-start.17) | collective-permute-done | bytes 262176 | tf_op jit(solution)/shard_map/ppermute | solution.py:206
  50.8 2.7 %collective-permute-start.18 = (bf16[32,1024]{1,0:T(8,128)(2,1)S(1)}, bf16[32,1024]{1,0:T(8,128)(2,1)S(1)}, u32[]{:S(2)}, u32[]{:S(2)}) collective-permute-start(bf16[32,1024]{1,0:T(8,128)(2,1)S(1)} %get-tuple-element.53), channel_id=1, source_target_pairs={{0,8},{4,12},{8,0},{12,4},{1,9},{5,13},{9,1},{13,5},{2,10},{6,14},... | collective-permute-start | bytes 196616 | tf_op jit(solution)/shard_map/ppermute | solution.py:206
  53.5 1.4 %collective-permute-start.19 = (bf16[32,1024]{1,0:T(8,128)(2,1)S(1)}, bf16[32,1024]{1,0:T(8,128)(2,1)S(1)}, u32[]{:S(2)}, u32[]{:S(2)}) collective-permute-start(bf16[32,1024]{1,0:T(8,128)(2,1)S(1)} %get-tuple-element.54), channel_id=1, source_target_pairs={{0,12},{2,4},{4,8},{6,0},{8,14},{10,6},{12,10},{14,2},{1,13},{3,5}... | collective-permute-start | bytes 196616 | tf_op jit(solution)/shard_map/ppermute | solution.py:470
  54.9 2.2 %collective-permute-done.18.passed.refs_0_ = bf16[32,1024]{1,0:T(8,128)(2,1)S(1)} collective-permute-done((bf16[32,1024]{1,0:T(8,128)(2,1)S(1)}, bf16[32,1024]{1,0:T(8,128)(2,1)S(1)}, u32[]{:S(2)}, u32[]{:S(2)}) %collective-permute-start.18) | collective-permute-done | bytes 65568 | tf_op jit(solution)/shard_map/ppermute | solution.py:206
  57.1 2.8 %collective-permute-start.21 = (bf16[32,1024]{1,0:T(8,128)(2,1)S(1)}, bf16[32,1024]{1,0:T(8,128)(2,1)S(1)}, u32[]{:S(2)}, u32[]{:S(2)}) collective-permute-start(bf16[32,1024]{1,0:T(8,128)(2,1)S(1)} %shard_map.93), channel_id=1, source_target_pairs={{0,2},{2,0},{1,3},{3,1},{4,6},{6,4},{5,7},{7,5},{8,10},{10,8},{9,1... | collective-permute-start | bytes 196616 | tf_op jit(solution)/shard_map/ppermute | solution.py:206
  59.9 2.2 %collective-permute-done.21.refs_4_ = bf16[32,1024]{1,0:T(8,128)(2,1)S(1)} collective-permute-done((bf16[32,1024]{1,0:T(8,128)(2,1)S(1)}, bf16[32,1024]{1,0:T(8,128)(2,1)S(1)}, u32[]{:S(2)}, u32[]{:S(2)}) %collective-permute-start.21) | collective-permute-done | bytes 65568 | tf_op jit(solution)/shard_map/ppermute | solution.py:206
  62.2 0.1 shard_map.94
  62.3 0.1 collective-permute-start.22
  62.3 1.3 %collective-permute-done.22.received = bf16[32,2048]{1,0:T(8,128)(2,1)S(1)} collective-permute-done((bf16[32,2048]{1,0:T(8,128)(2,1)S(1)}, bf16[32,2048]{1,0:T(8,128)(2,1)S(1)}, u32[]{:S(2)}, u32[]{:S(2)}) %collective-permute-start.22) | collective-permute-done | bytes 131104 | tf_op jit(solution)/shard_map/ppermute | solution.py:206
  63.7 0.7 %shard_map.95 = bf16[1,32,4096]{2,1,0:T(8,128)(2,1)} custom-call(bf16[32,2048]{1,0:T(8,128)(2,1)S(1)} %get-tuple-element.57.keep, bf16[32,2048]{1,0:T(8,128)(2,1)S(1)} %collective-permute-done.22.received), custom_call_target="tpu_custom_call" | custom-call | bytes 524288 | tf_op jit(solution)/shard_map/pallas_call | solution.py:713
  (21 shorter events, 0.1 us)
Async XLA Ops:
  0.9 7.9 %collective-permute-start.3 = (bf16[16,2048]{1,0:T(8,128)(2,1)S(1)}, bf16[16,2048]{1,0:T(8,128)(2,1)S(1)}, u32[]{:S(2)}, u32[]{:S(2)}) collective-permute-start(bf16[16,2048]{1,0:T(8,128)(2,1)S(1)} %get-tuple-element.59.refs_1_), channel_id=1, source_target_pairs={{0,8},{4,12},{8,0},{12,4},{1,9},{5,13},{9,1},{13,5},{2,10},{6,14},... | collective-permute-start | bytes 196616 | tf_op jit(solution)/shard_map/ppermute | solution.py:206
  5.0 10.4 %copy-start.1 = (bf16[4096]{0:T(1024)(128)(2,1)S(1)}, bf16[4096]{0:T(1024)(128)(2,1)}, u32[]{:S(2)}) copy-start(bf16[4096]{0:T(1024)(128)(2,1)} %param.9) | copy-start | bytes 24580
  5.0 6.1 %collective-permute-start.2 = (bf16[16,2048]{1,0:T(8,128)(2,1)S(1)}, bf16[16,2048]{1,0:T(8,128)(2,1)S(1)}, u32[]{:S(2)}, u32[]{:S(2)}) collective-permute-start(bf16[16,2048]{1,0:T(8,128)(2,1)S(1)} %get-tuple-element.60.refs_0_), channel_id=1, source_target_pairs={{0,8},{4,12},{8,0},{12,4},{1,9},{5,13},{9,1},{13,5},{2,10},{6,14},... | collective-permute-start | bytes 196616 | tf_op jit(solution)/shard_map/ppermute | solution.py:206
  5.1 9.8 %collective-permute-start.1 = (bf16[16,2048]{1,0:T(8,128)(2,1)S(1)}, bf16[16,2048]{1,0:T(8,128)(2,1)S(1)}, u32[]{:S(2)}, u32[]{:S(2)}) collective-permute-start(bf16[16,2048]{1,0:T(8,128)(2,1)S(1)} %get-tuple-element.59.refs_1_), channel_id=1, source_target_pairs={{0,4},{4,0},{8,12},{12,8},{1,5},{5,1},{9,13},{13,9},{2,6},{6,2},{1... | collective-permute-start | bytes 196616 | tf_op jit(solution)/shard_map/ppermute | solution.py:206
  6.9 8.0 %collective-permute-start = (bf16[16,2048]{1,0:T(8,128)(2,1)S(1)}, bf16[16,2048]{1,0:T(8,128)(2,1)S(1)}, u32[]{:S(2)}, u32[]{:S(2)}) collective-permute-start(bf16[16,2048]{1,0:T(8,128)(2,1)S(1)} %get-tuple-element.60.refs_0_), channel_id=1, source_target_pairs={{0,4},{4,0},{8,12},{12,8},{1,5},{5,1},{9,13},{13,9},{2,6},{6,2},{1... | collective-permute-start | bytes 196616 | tf_op jit(solution)/shard_map/ppermute | solution.py:206
  8.7 6.2 %collective-permute-start.5 = (bf16[16,2048]{1,0:T(8,128)(2,1)S(1)}, bf16[16,2048]{1,0:T(8,128)(2,1)S(1)}, u32[]{:S(2)}, u32[]{:S(2)}) collective-permute-start(bf16[16,2048]{1,0:T(8,128)(2,1)S(1)} %collective-permute-done.3.refs_5_), channel_id=1, source_target_pairs={{0,4},{4,0},{8,12},{12,8},{1,5},{5,1},{9,13},{13,9},{2,6},{6,2},{1... | collective-permute-start | bytes 196616 | tf_op jit(solution)/shard_map/ppermute | solution.py:206
  11.1 4.3 %collective-permute-start.4 = (bf16[16,2048]{1,0:T(8,128)(2,1)S(1)}, bf16[16,2048]{1,0:T(8,128)(2,1)S(1)}, u32[]{:S(2)}, u32[]{:S(2)}) collective-permute-start(bf16[16,2048]{1,0:T(8,128)(2,1)S(1)} %collective-permute-done.2.refs_4_), channel_id=1, source_target_pairs={{0,4},{4,0},{8,12},{12,8},{1,5},{5,1},{9,13},{13,9},{2,6},{6,2},{1... | collective-permute-start | bytes 196616 | tf_op jit(solution)/shard_map/ppermute | solution.py:206
  16.4 3.4 %collective-permute-start.6 = (bf16[128,1408]{1,0:T(8,128)(2,1)S(1)}, bf16[128,1408]{1,0:T(8,128)(2,1)S(1)}, u32[]{:S(2)}, u32[]{:S(2)}) collective-permute-start(bf16[128,1408]{1,0:T(8,128)(2,1)S(1)} %get-tuple-element.38.given), channel_id=1, source_target_pairs={{0,1},{1,0},{2,3},{3,2},{4,5},{5,4},{6,7},{7,6},{8,9},{9,8},{10,11... | collective-permute-start | bytes 1081352 | tf_op jit(solution)/shard_map/ppermute | solution.py:206
  16.5 14.4 %copy-start.2 = (s32[128]{0:T(128)S(1)}, s32[128]{0:T(128)}, u32[]{:S(2)}) copy-start(s32[128]{0:T(128)} %slots.3) | copy-start | bytes 1540
  16.5 14.4 %copy-start.3 = (s32[32]{0:T(128)S(1)}, s32[32]{0:T(128)}, u32[]{:S(2)}) copy-start(s32[32]{0:T(128)} %lengths.1) | copy-start | bytes 388
  19.9 8.0 %collective-permute-start.7 = (bf16[32,1280]{1,0:T(8,128)(2,1)S(1)}, bf16[32,1280]{1,0:T(8,128)(2,1)S(1)}, u32[]{:S(2)}, u32[]{:S(2)}) collective-permute-start(bf16[32,1280]{1,0:T(8,128)(2,1)S(1)} %get-tuple-element.39), channel_id=1, source_target_pairs={{0,8},{4,12},{8,0},{12,4},{1,9},{5,13},{9,1},{13,5},{2,10},{6,14},... | collective-permute-start | bytes 245768 | tf_op jit(solution)/shard_map/ppermute | solution.py:206
  23.1 3.7 %collective-permute-start.10 = (bf16[32,128]{1,0:T(8,128)(2,1)S(1)}, bf16[32,128]{1,0:T(8,128)(2,1)S(1)}, u32[]{:S(2)}, u32[]{:S(2)}) collective-permute-start(bf16[32,128]{1,0:T(8,128)(2,1)S(1)} %get-tuple-element.43.refs_5_), channel_id=1, source_target_pairs={{0,2},{2,0},{1,3},{3,1},{4,6},{6,4},{5,7},{7,5},{8,10},{10,8},{9,1... | collective-permute-start | bytes 24584 | tf_op jit(solution)/shard_map/ppermute | solution.py:206
  24.6 10.0 %collective-permute-start.8 = (bf16[32,1280]{1,0:T(8,128)(2,1)S(1)}, bf16[32,1280]{1,0:T(8,128)(2,1)S(1)}, u32[]{:S(2)}, u32[]{:S(2)}) collective-permute-start(bf16[32,1280]{1,0:T(8,128)(2,1)S(1)} %get-tuple-element.40), channel_id=1, source_target_pairs={{0,12},{2,4},{4,8},{6,0},{8,14},{10,6},{12,10},{14,2},{1,13},{3,5}... | collective-permute-start | bytes 245768 | tf_op jit(solution)/shard_map/ppermute | solution.py:470
  25.5 9.1 %collective-permute-start.9 = (bf16[32,1280]{1,0:T(8,128)(2,1)S(1)}, bf16[32,1280]{1,0:T(8,128)(2,1)S(1)}, u32[]{:S(2)}, u32[]{:S(2)}) collective-permute-start(bf16[32,1280]{1,0:T(8,128)(2,1)S(1)} %get-tuple-element.41), channel_id=1, source_target_pairs={{0,4},{2,12},{4,0},{6,8},{8,6},{10,14},{12,2},{14,10},{1,5},{3,13}... | collective-permute-start | bytes 245768 | tf_op jit(solution)/shard_map/ppermute | solution.py:470
  28.0 6.7 %collective-permute-start.11 = (bf16[32,1280]{1,0:T(8,128)(2,1)S(1)}, bf16[32,1280]{1,0:T(8,128)(2,1)S(1)}, u32[]{:S(2)}, u32[]{:S(2)}) collective-permute-start(bf16[32,1280]{1,0:T(8,128)(2,1)S(1)} %shard_map.87), channel_id=1, source_target_pairs={{0,2},{2,0},{1,3},{3,1},{4,6},{6,4},{5,7},{7,5},{8,10},{10,8},{9,1... | collective-permute-start | bytes 245768 | tf_op jit(solution)/shard_map/ppermute | solution.py:206
  36.4 6.9 %collective-permute-start.13 = (bf16[16,2048]{1,0:T(8,128)(2,1)S(1)}, bf16[16,2048]{1,0:T(8,128)(2,1)S(1)}, u32[]{:S(2)}, u32[]{:S(2)}) collective-permute-start(bf16[16,2048]{1,0:T(8,128)(2,1)S(1)} %get-tuple-element.48), channel_id=1, source_target_pairs={{0,8},{4,12},{8,0},{12,4},{1,9},{5,13},{9,1},{13,5},{2,10},{6,14},... | collective-permute-start | bytes 196616 | tf_op jit(solution)/shard_map/ppermute | solution.py:206
  36.8 7.2 %collective-permute-start.14 = (bf16[16,2048]{1,0:T(8,128)(2,1)S(1)}, bf16[16,2048]{1,0:T(8,128)(2,1)S(1)}, u32[]{:S(2)}, u32[]{:S(2)}) collective-permute-start(bf16[16,2048]{1,0:T(8,128)(2,1)S(1)} %get-tuple-element.49), channel_id=1, source_target_pairs={{0,8},{4,12},{8,0},{12,4},{1,9},{5,13},{9,1},{13,5},{2,10},{6,14},... | collective-permute-start | bytes 196616 | tf_op jit(solution)/shard_map/ppermute | solution.py:206
  39.4 8.9 %collective-permute-start.12 = (bf16[32,2048]{1,0:T(8,128)(2,1)S(1)}, bf16[32,2048]{1,0:T(8,128)(2,1)S(1)}, u32[]{:S(2)}, u32[]{:S(2)}) collective-permute-start(bf16[32,2048]{1,0:T(8,128)(2,1)S(1)} %get-tuple-element.46.attended.refs_0_), channel_id=1, source_target_pairs={{0,4},{4,0},{8,12},{12,8},{1,5},{5,1},{9,13},{13,9},{2,6},{6,2},{1... | collective-permute-start | bytes 393224 | tf_op jit(solution)/shard_map/ppermute | solution.py:206
  43.3 4.7 %collective-permute-start.15 = (bf16[16,2048]{1,0:T(8,128)(2,1)S(1)}, bf16[16,2048]{1,0:T(8,128)(2,1)S(1)}, u32[]{:S(2)}, u32[]{:S(2)}) collective-permute-start(bf16[16,2048]{1,0:T(8,128)(2,1)S(1)} %collective-permute-done.13.refs_2_), channel_id=1, source_target_pairs={{0,4},{4,0},{8,12},{12,8},{1,5},{5,1},{9,13},{13,9},{2,6},{6,2},{1... | collective-permute-start | bytes 196616 | tf_op jit(solution)/shard_map/ppermute | solution.py:206
  44.0 4.3 %collective-permute-start.16 = (bf16[16,2048]{1,0:T(8,128)(2,1)S(1)}, bf16[16,2048]{1,0:T(8,128)(2,1)S(1)}, u32[]{:S(2)}, u32[]{:S(2)}) collective-permute-start(bf16[16,2048]{1,0:T(8,128)(2,1)S(1)} %collective-permute-done.14.refs_3_), channel_id=1, source_target_pairs={{0,4},{4,0},{8,12},{12,8},{1,5},{5,1},{9,13},{13,9},{2,6},{6,2},{1... | collective-permute-start | bytes 196616 | tf_op jit(solution)/shard_map/ppermute | solution.py:206
  49.1 13.1 %copy-start = (bf16[32,4096]{1,0:T(8,128)(2,1)S(1)}, bf16[32,4096]{1,0:T(8,128)(2,1)}, u32[]{:S(2)}) copy-start(bf16[32,4096]{1,0:T(8,128)(2,1)} %hidden.1) | copy-start | bytes 786436
  49.1 1.6 %collective-permute-start.17 = (bf16[128,1024]{1,0:T(8,128)(2,1)S(1)}, bf16[128,1024]{1,0:T(8,128)(2,1)S(1)}, u32[]{:S(2)}, u32[]{:S(2)}) collective-permute-start(bf16[128,1024]{1,0:T(8,128)(2,1)S(1)} %get-tuple-element.52.given), channel_id=1, source_target_pairs={{0,1},{1,0},{2,3},{3,2},{4,5},{5,4},{6,7},{7,6},{8,9},{9,8},{10,11... | collective-permute-start | bytes 786440 | tf_op jit(solution)/shard_map/ppermute | solution.py:206
  50.8 6.3 %collective-permute-start.18 = (bf16[32,1024]{1,0:T(8,128)(2,1)S(1)}, bf16[32,1024]{1,0:T(8,128)(2,1)S(1)}, u32[]{:S(2)}, u32[]{:S(2)}) collective-permute-start(bf16[32,1024]{1,0:T(8,128)(2,1)S(1)} %get-tuple-element.53), channel_id=1, source_target_pairs={{0,8},{4,12},{8,0},{12,4},{1,9},{5,13},{9,1},{13,5},{2,10},{6,14},... | collective-permute-start | bytes 196616 | tf_op jit(solution)/shard_map/ppermute | solution.py:206
  53.5 6.4 %collective-permute-start.19 = (bf16[32,1024]{1,0:T(8,128)(2,1)S(1)}, bf16[32,1024]{1,0:T(8,128)(2,1)S(1)}, u32[]{:S(2)}, u32[]{:S(2)}) collective-permute-start(bf16[32,1024]{1,0:T(8,128)(2,1)S(1)} %get-tuple-element.54), channel_id=1, source_target_pairs={{0,12},{2,4},{4,8},{6,0},{8,14},{10,6},{12,10},{14,2},{1,13},{3,5}... | collective-permute-start | bytes 196616 | tf_op jit(solution)/shard_map/ppermute | solution.py:470
  54.9 5.0 %collective-permute-start.20 = (bf16[32,1024]{1,0:T(8,128)(2,1)S(1)}, bf16[32,1024]{1,0:T(8,128)(2,1)S(1)}, u32[]{:S(2)}, u32[]{:S(2)}) collective-permute-start(bf16[32,1024]{1,0:T(8,128)(2,1)S(1)} %get-tuple-element.55), channel_id=1, source_target_pairs={{0,4},{2,12},{4,0},{6,8},{8,6},{10,14},{12,2},{14,10},{1,5},{3,13}... | collective-permute-start | bytes 196616 | tf_op jit(solution)/shard_map/ppermute | solution.py:470
  57.1 5.0 %collective-permute-start.21 = (bf16[32,1024]{1,0:T(8,128)(2,1)S(1)}, bf16[32,1024]{1,0:T(8,128)(2,1)S(1)}, u32[]{:S(2)}, u32[]{:S(2)}) collective-permute-start(bf16[32,1024]{1,0:T(8,128)(2,1)S(1)} %shard_map.93), channel_id=1, source_target_pairs={{0,2},{2,0},{1,3},{3,1},{4,6},{6,4},{5,7},{7,5},{8,10},{10,8},{9,1... | collective-permute-start | bytes 196616 | tf_op jit(solution)/shard_map/ppermute | solution.py:206
  62.3 1.4 %collective-permute-start.22 = (bf16[32,2048]{1,0:T(8,128)(2,1)S(1)}, bf16[32,2048]{1,0:T(8,128)(2,1)S(1)}, u32[]{:S(2)}, u32[]{:S(2)}) collective-permute-start(bf16[32,2048]{1,0:T(8,128)(2,1)S(1)} %get-tuple-element.58), channel_id=1, source_target_pairs={{0,1},{1,0},{2,3},{3,2},{4,5},{5,4},{6,7},{7,6},{8,9},{9,8},{10,11... | collective-permute-start | bytes 393224 | tf_op jit(solution)/shard_map/ppermute | solution.py:206

commit v20 on v18

--- a/solution.py
+++ b/solution.py
@@ -172,7 +172,6 @@
 OUT_WIDTH = GROUP * HEAD_DIM
 SLOTS = 8
 VMEM = pl.BlockSpec(memory_space=pltpu.VMEM)
-SMEM = pl.BlockSpec(memory_space=pltpu.SMEM)
 HBM = pl.BlockSpec(memory_space=pl.ANY)
 MIB = 2**20
 
@@ -488,10 +487,11 @@
 
 
 def rope(lengths, rows):
-    slot = lax.broadcasted_iota(jnp.int32, (rows, HEAD_DIM), 0)
-    length_of = jnp.zeros((rows, HEAD_DIM), jnp.int32)
-    for i in range(rows):
-        length_of = jnp.where(slot == i, lengths[i], length_of)
+    row = lax.broadcasted_iota(jnp.int32, (rows, rows), 0)
+    slot = lax.broadcasted_iota(jnp.int32, (rows, rows), 1)
+    own = jnp.where(row == slot, lengths[...].reshape(1, rows), 0)
+    column = jnp.sum(own.astype(jnp.float32), axis=1, keepdims=True).astype(jnp.int32)
+    length_of = jnp.broadcast_to(column, (rows, HEAD_DIM))
     lane = lax.broadcasted_iota(jnp.int32, (rows, HEAD_DIM), 1)
     half = HEAD_DIM // 2
     step = lax.rem(lane, half).astype(jnp.float32)
@@ -550,19 +550,19 @@
             weights = jnp.exp(scores - highest)
             own_weight = jnp.exp(own_score - highest)
             inverse = 1.0 / (jnp.sum(weights, axis=2, keepdims=True) + own_weight)
-            probs = (weights * inverse).astype(jnp.bfloat16)
-            probs_of[pair, run] = probs.reshape(GROUP * SLOTS, SLOTS * cache)
-            own_probs.append((own_weight * inverse).astype(jnp.bfloat16).astype(jnp.float32))
+            probs_of[pair, run] = weights.astype(jnp.bfloat16).reshape(
+                GROUP * SLOTS, SLOTS * cache
+            )
+            own_probs.append((own_weight, inverse))
     for pair in range(pairs):
         lanes = pl.ds(pl.multiple_of((low ^ pair) * HEAD_DIM, HEAD_DIM), HEAD_DIM)
         results = []
         for run, part in enumerate(runs):
             value = values[part, :, lanes].reshape(SLOTS * cache, HEAD_DIM)
             mixed = jnp.dot(probs_of[pair, run], value, preferred_element_type=jnp.float32)
-            own_prob = own_probs[pair * len(runs) + run]
-            results.append(
-                mixed.reshape(GROUP, SLOTS, HEAD_DIM) + own_prob * new_values[pair][part][None]
-            )
+            own_weight, inverse = own_probs[pair * len(runs) + run]
+            mixed = mixed.reshape(GROUP, SLOTS, HEAD_DIM) + own_weight * new_values[pair][part][None]
+            results.append(mixed * inverse)
         for head in range(GROUP):
             at = pl.multiple_of((low ^ pair) * OUT_WIDTH + head * HEAD_DIM, HEAD_DIM)
             size = len(results) // parts
@@ -644,7 +644,7 @@
         [pltpu.VMEM((half, half_out), jnp.bfloat16)]
         + [pltpu.VMEM((rows, cache, pairs * HEAD_DIM), jnp.bfloat16)] * 2
         + [table, table, struct((rows, HEAD_DIM), jnp.int32), struct(square)],
-        [SMEM, HBM, HBM, HBM, VMEM],
+        [VMEM, HBM, HBM, HBM, VMEM],
         [VMEM] * 7,
         0,
         half * half_out * 2 + 4 * rows * cache * pairs * HEAD_DIM,

time: 62.6 us -> 63.5 us (1.014)
  starting transfers between devices: 32 us -> 34 us
  waiting for transfers between devices: 13.2 us -> 12.4 us
    ppermute x19, starting transfers between devices: 28.4 us -> 31 us  [moved(): return lax.ppermute(value, axis, pairs)]
    ppermute x4, waiting for transfers between devices: 2.44 us -> 0.75 us  [direct(): return lax.ppermute(value, ('col', 'row'), moves)]
    ppermute x19, waiting for transfers between devices: 10.7 us -> 11.7 us  [moved(): return lax.ppermute(value, axis, pairs)]
  transfers between devices with their start and end apart: 23 -> 23, of which waited for: 11 -> 11; matrix products, arithmetic and copies ran while one was open for 0% -> 0% of each run, Pallas kernels for 19% -> 17%
where the time goes in v20:
time: 63.5 us; the launch traced here: 63.4 us
  starting transfers between devices  34 us (54%)
  Pallas kernels  15.8 us (25%)
  waiting for transfers between devices  12.4 us (20%)
  local copies, waits for them, and re-layouts  0.9 us (1%)
    ppermute x19, starting transfers between devices, moved(): return lax.ppermute(value, axis, pairs)  31 us
    ppermute x19, waiting for transfers between devices, moved(): return lax.ppermute(value, axis, pairs)  11.7 us
    pallas_call x1, Pallas kernels, paired_plan(): call(functools.partial(stage_in_kernel, col_count), [pltpu.VMEM((half, ha...  4.09 us
    pallas_call x1, Pallas kernels, paired_plan(): call(functools.partial(stage_rest_kernel, col_count), [pltpu.VMEM((half,...  3.12 us
    ppermute x4, starting transfers between devices, direct(): return lax.ppermute(value, ('col', 'row'), moves)  2.96 us
    pallas_call x1, Pallas kernels, paired_plan(): call(stage_out_kernel, pltpu.VMEM((half, half_out), jnp.bfloat16), [HBM,...  2.24 us
    pallas_call x2, Pallas kernels, project(): call(functools.partial(kernel, parts), [struct((rows, half + more)), stru...  1.91 us
    pallas_call x1, Pallas kernels, paired_plan(): call(functools.partial(attend_all, len(products), parts), [struct((rows,...  1.88 us
  transfers between devices with their start and end apart: 23, of which 11 were waited for; matrix products, arithmetic and copies ran while one was open for 0% of the time, Pallas kernels for 17%

profile of v20, /device:TPU:0, one launch (start us, length us, event | category | flops | bytes accessed | tf_op | source)
XLA Modules:
  0.0 63.4 jit_solution(3468654778176215180)
XLA Ops:
  0.0 0.9 %fusion = (bf16[16,2048]{1,0:T(8,128)(2,1)S(1)}, bf16[16,2048]{1,0:T(8,128)(2,1)S(1)}) fusion(bf16[32,4096]{1,0:T(8,128)(2,1)} %hidden.1, s32[]{:T(128)S(6)} %add.4, s32[]{:T(128)S(6)} %select_n.3), kind=kLoop, calls=%fused_computation.1 | loop fusion | bytes 262152 | tf_op jit(solution)/shard_map/slice | solution.py:639
  0.9 4.1 %collective-permute-start.2 = (bf16[16,2048]{1,0:T(8,128)(2,1)S(1)}, bf16[16,2048]{1,0:T(8,128)(2,1)S(1)}, u32[]{:S(2)}, u32[]{:S(2)}) collective-permute-start(bf16[16,2048]{1,0:T(8,128)(2,1)S(1)} %get-tuple-element.62.refs_0_), channel_id=1, source_target_pairs={{0,8},{4,12},{8,0},{12,4},{1,9},{5,13},{9,1},{13,5},{2,10},{6,14},... | collective-permute-start | bytes 196616 | tf_op jit(solution)/shard_map/ppermute | solution.py:205
  5.0 0.1 collective-permute-start.3
  5.1 1.8 %collective-permute-start = (bf16[16,2048]{1,0:T(8,128)(2,1)S(1)}, bf16[16,2048]{1,0:T(8,128)(2,1)S(1)}, u32[]{:S(2)}, u32[]{:S(2)}) collective-permute-start(bf16[16,2048]{1,0:T(8,128)(2,1)S(1)} %get-tuple-element.62.refs_0_), channel_id=1, source_target_pairs={{0,4},{4,0},{8,12},{12,8},{1,5},{5,1},{9,13},{13,9},{2,6},{6,2},{1... | collective-permute-start | bytes 196616 | tf_op jit(solution)/shard_map/ppermute | solution.py:205
  6.9 0.2 collective-permute-start.1
  7.1 1.6 %collective-permute-done.2.refs_4_ = bf16[16,2048]{1,0:T(8,128)(2,1)S(1)} collective-permute-done((bf16[16,2048]{1,0:T(8,128)(2,1)S(1)}, bf16[16,2048]{1,0:T(8,128)(2,1)S(1)}, u32[]{:S(2)}, u32[]{:S(2)}) %collective-permute-start.2) | collective-permute-done | bytes 65568 | tf_op jit(solution)/shard_map/ppermute | solution.py:205
  8.7 1.9 %collective-permute-start.4 = (bf16[16,2048]{1,0:T(8,128)(2,1)S(1)}, bf16[16,2048]{1,0:T(8,128)(2,1)S(1)}, u32[]{:S(2)}, u32[]{:S(2)}) collective-permute-start(bf16[16,2048]{1,0:T(8,128)(2,1)S(1)} %collective-permute-done.2.refs_4_), channel_id=1, source_target_pairs={{0,4},{4,0},{8,12},{12,8},{1,5},{5,1},{9,13},{13,9},{2,6},{6,2},{1... | collective-permute-start | bytes 196616 | tf_op jit(solution)/shard_map/ppermute | solution.py:205
  10.6 0.4 collective-permute-done.3.refs_5_
  11.1 1.3 %collective-permute-start.5 = (bf16[16,2048]{1,0:T(8,128)(2,1)S(1)}, bf16[16,2048]{1,0:T(8,128)(2,1)S(1)}, u32[]{:S(2)}, u32[]{:S(2)}) collective-permute-start(bf16[16,2048]{1,0:T(8,128)(2,1)S(1)} %collective-permute-done.3.refs_5_), channel_id=1, source_target_pairs={{0,4},{4,0},{8,12},{12,8},{1,5},{5,1},{9,13},{13,9},{2,6},{6,2},{1... | collective-permute-start | bytes 196616 | tf_op jit(solution)/shard_map/ppermute | solution.py:205
  12.4 4.1 %shard_map.83 = (bf16[2048,1280]{1,0:T(8,128)(2,1)S(1)}, bf16[2048,1280]{1,0:T(8,128)(2,1)S(1)}, bf16[128,128]{1,0:T(8,128)(2,1)S(1)}) custom-call(bf16[4096,2560]{1,0:T(8,128)(2,1)} %weight.4, s32[128]{0:T(128)} %slots.3), custom_call_target="tpu_custom_call" | custom-call | bytes 10485760 | tf_op jit(solution)/shard_map/pallas_call | solution.py:625
  16.5 1.1 %shard_map.84 = (bf16[128,1408]{1,0:T(8,128)(2,1)S(1)}, bf16[128,2048]{1,0:T(8,128)(2,1)S(1)}) custom-call(bf16[128,128]{1,0:T(8,128)(2,1)S(1)} %get-tuple-element.36.chosen, bf16[16,2048]{1,0:T(8,128)(2,1)S(1)} %get-tuple-element.62.refs_0_, bf16[16,2048]{1,0:T(8,128)(2,1)S(1)} %get-tuple-element.61.refs_1_, ...), custom_call_target="tpu_custom_call" | custom-call | flops 671088640 | bytes 5242880 | tf_op jit(solution)/shard_map/pallas_call | solution.py:391
  17.6 0.0 copy-start.2
  17.6 0.0 copy-start.3
  17.6 0.1 collective-permute-start.6
  17.7 0.9 %shard_map.85.own = f32[128,1280]{1,0:T(8,128)S(1)} custom-call(bf16[128,2048]{1,0:T(8,128)(2,1)S(1)} %get-tuple-element.39.permuted, bf16[2048,1280]{1,0:T(8,128)(2,1)S(1)} %get-tuple-element.37.refs_8_.weight), custom_call_target="tpu_custom_call" | custom-call | flops 671088640 | bytes 5242880 | tf_op jit(solution)/shard_map/pallas_call | solution.py:400
  18.6 0.8 %collective-permute-done.6.received = bf16[128,1408]{1,0:T(8,128)(2,1)S(1)} collective-permute-done((bf16[128,1408]{1,0:T(8,128)(2,1)S(1)}, bf16[128,1408]{1,0:T(8,128)(2,1)S(1)}, u32[]{:S(2)}, u32[]{:S(2)}) %collective-permute-start.6) | collective-permute-done | bytes 360480 | tf_op jit(solution)/shard_map/ppermute | solution.py:205
  19.4 0.1 shard_map.86
  19.5 3.2 %collective-permute-start.7 = (bf16[32,1280]{1,0:T(8,128)(2,1)S(1)}, bf16[32,1280]{1,0:T(8,128)(2,1)S(1)}, u32[]{:S(2)}, u32[]{:S(2)}) collective-permute-start(bf16[32,1280]{1,0:T(8,128)(2,1)S(1)} %get-tuple-element.41), channel_id=1, source_target_pairs={{0,8},{4,12},{8,0},{12,4},{1,9},{5,13},{9,1},{13,5},{2,10},{6,14},... | collective-permute-start | bytes 245768 | tf_op jit(solution)/shard_map/ppermute | solution.py:205
  22.6 1.5 %collective-permute-start.10 = (bf16[32,128]{1,0:T(8,128)(2,1)S(1)}, bf16[32,128]{1,0:T(8,128)(2,1)S(1)}, u32[]{:S(2)}, u32[]{:S(2)}) collective-permute-start(bf16[32,128]{1,0:T(8,128)(2,1)S(1)} %get-tuple-element.45.refs_5_), channel_id=1, source_target_pairs={{0,2},{2,0},{1,3},{3,1},{4,6},{6,4},{5,7},{7,5},{8,10},{10,8},{9,1... | collective-permute-start | bytes 24584 | tf_op jit(solution)/shard_map/ppermute | solution.py:205
  24.1 0.4 collective-permute-start.8
  24.5 0.3 collective-permute-start.9
  24.9 1.4 %collective-permute-done.10.refs_0_.refs_6_ = bf16[32,128]{1,0:T(8,128)(2,1)S(1)} collective-permute-done((bf16[32,128]{1,0:T(8,128)(2,1)S(1)}, bf16[32,128]{1,0:T(8,128)(2,1)S(1)}, u32[]{:S(2)}, u32[]{:S(2)}) %collective-permute-start.10) | collective-permute-done | bytes 8224 | tf_op jit(solution)/shard_map/ppermute | solution.py:205
  26.3 0.9 %collective-permute-done.7.passed.refs_0_ = bf16[32,1280]{1,0:T(8,128)(2,1)S(1)} collective-permute-done((bf16[32,1280]{1,0:T(8,128)(2,1)S(1)}, bf16[32,1280]{1,0:T(8,128)(2,1)S(1)}, u32[]{:S(2)}, u32[]{:S(2)}) %collective-permute-start.7) | collective-permute-done | bytes 81952 | tf_op jit(solution)/shard_map/ppermute | solution.py:205
  27.2 2.6 %collective-permute-start.11 = (bf16[32,1280]{1,0:T(8,128)(2,1)S(1)}, bf16[32,1280]{1,0:T(8,128)(2,1)S(1)}, u32[]{:S(2)}, u32[]{:S(2)}) collective-permute-start(bf16[32,1280]{1,0:T(8,128)(2,1)S(1)} %shard_map.87), channel_id=1, source_target_pairs={{0,2},{2,0},{1,3},{3,1},{4,6},{6,4},{5,7},{7,5},{8,10},{10,8},{9,1... | collective-permute-start | bytes 245768 | tf_op jit(solution)/shard_map/ppermute | solution.py:205
  29.9 3.1 %shard_map.82 = (bf16[2048,1024]{1,0:T(8,128)(2,1)S(1)}, bf16[32,64,256]{2,1,0:T(8,128)(2,1)S(1)}, bf16[32,64,256]{2,1,0:T(8,128)(2,1)S(1)}, f32[32,128]{1,0:T(8...) custom-call(s32[32]{0:T(128)S(1)} %copy-done.3, bf16[4096,2048]{1,0:T(8,128)(2,1)} %weight.5, ...), custom_call_target="tpu_custom_call" | custom-call | bytes 6291456 | tf_op jit(solution)/shard_map/pallas_call | solution.py:642
  33.0 1.9 %shard_map.88 = (bf16[32,2048]{1,0:T(8,128)(2,1)S(1)}, bf16[16,2048]{1,0:T(8,128)(2,1)S(1)}, bf16[16,2048]{1,0:T(8,128)(2,1)S(1)}) custom-call(f32[32,128]{1,0:T(8,128)S(1)} %get-tuple-element.33.cosine, f32[32,128]{1,0:T(8,128)S(1)} %get-tuple-element.34.sine, s32[32,128]{1,0:T(8,128)S(1)} %get-tuple-element.35.lengths, ...), custom_call_target="tpu_custom_call" | custom-call | flops 16777216 | tf_op jit(solution)/shard_map/pallas_call | solution.py:658
  34.9 1.1 %collective-permute-start.13 = (bf16[16,2048]{1,0:T(8,128)(2,1)S(1)}, bf16[16,2048]{1,0:T(8,128)(2,1)S(1)}, u32[]{:S(2)}, u32[]{:S(2)}) collective-permute-start(bf16[16,2048]{1,0:T(8,128)(2,1)S(1)} %get-tuple-element.50), channel_id=1, source_target_pairs={{0,8},{4,12},{8,0},{12,4},{1,9},{5,13},{9,1},{13,5},{2,10},{6,14},... | collective-permute-start | bytes 196616 | tf_op jit(solution)/shard_map/ppermute | solution.py:205
  36.0 1.9 %collective-permute-start.14 = (bf16[16,2048]{1,0:T(8,128)(2,1)S(1)}, bf16[16,2048]{1,0:T(8,128)(2,1)S(1)}, u32[]{:S(2)}, u32[]{:S(2)}) collective-permute-start(bf16[16,2048]{1,0:T(8,128)(2,1)S(1)} %get-tuple-element.51), channel_id=1, source_target_pairs={{0,8},{4,12},{8,0},{12,4},{1,9},{5,13},{9,1},{13,5},{2,10},{6,14},... | collective-permute-start | bytes 196616 | tf_op jit(solution)/shard_map/ppermute | solution.py:205
  37.9 1.7 %collective-permute-start.12 = (bf16[32,2048]{1,0:T(8,128)(2,1)S(1)}, bf16[32,2048]{1,0:T(8,128)(2,1)S(1)}, u32[]{:S(2)}, u32[]{:S(2)}) collective-permute-start(bf16[32,2048]{1,0:T(8,128)(2,1)S(1)} %get-tuple-element.48.attended.refs_0_), channel_id=1, source_target_pairs={{0,4},{4,0},{8,12},{12,8},{1,5},{5,1},{9,13},{13,9},{2,6},{6,2},{1... | collective-permute-start | bytes 393224 | tf_op jit(solution)/shard_map/ppermute | solution.py:205
  39.6 1.3 %collective-permute-done.13.refs_2_ = bf16[16,2048]{1,0:T(8,128)(2,1)S(1)} collective-permute-done((bf16[16,2048]{1,0:T(8,128)(2,1)S(1)}, bf16[16,2048]{1,0:T(8,128)(2,1)S(1)}, u32[]{:S(2)}, u32[]{:S(2)}) %collective-permute-start.13) | collective-permute-done | bytes 65568 | tf_op jit(solution)/shard_map/ppermute | solution.py:205
  40.9 1.6 %collective-permute-start.15 = (bf16[16,2048]{1,0:T(8,128)(2,1)S(1)}, bf16[16,2048]{1,0:T(8,128)(2,1)S(1)}, u32[]{:S(2)}, u32[]{:S(2)}) collective-permute-start(bf16[16,2048]{1,0:T(8,128)(2,1)S(1)} %collective-permute-done.13.refs_2_), channel_id=1, source_target_pairs={{0,4},{4,0},{8,12},{12,8},{1,5},{5,1},{9,13},{13,9},{2,6},{6,2},{1... | collective-permute-start | bytes 196616 | tf_op jit(solution)/shard_map/ppermute | solution.py:205
  42.5 2.7 %collective-permute-start.16 = (bf16[16,2048]{1,0:T(8,128)(2,1)S(1)}, bf16[16,2048]{1,0:T(8,128)(2,1)S(1)}, u32[]{:S(2)}, u32[]{:S(2)}) collective-permute-start(bf16[16,2048]{1,0:T(8,128)(2,1)S(1)} %collective-permute-done.14.refs_3_), channel_id=1, source_target_pairs={{0,4},{4,0},{8,12},{12,8},{1,5},{5,1},{9,13},{13,9},{2,6},{6,2},{1... | collective-permute-start | bytes 196616 | tf_op jit(solution)/shard_map/ppermute | solution.py:205
  45.2 2.2 %shard_map.89.refs_6_.weight = bf16[2048,1024]{1,0:T(8,128)(2,1)S(1)} custom-call(bf16[4096,2048]{1,0:T(8,128)(2,1)} %weight.5, bf16[32,2048]{1,0:T(8,128)(2,1)S(1)} %get-tuple-element.48.attended.refs_0_), custom_call_target="tpu_custom_call" | custom-call | bytes 4194304 | tf_op jit(solution)/shard_map/pallas_call | solution.py:675
  47.5 0.8 %shard_map.90 = (bf16[128,1024]{1,0:T(8,128)(2,1)S(1)}, bf16[128,2048]{1,0:T(8,128)(2,1)S(1)}) custom-call(bf16[128,128]{1,0:T(8,128)(2,1)S(1)} %get-tuple-element.49.chosen, bf16[32,2048]{1,0:T(8,128)(2,1)S(1)} %get-tuple-element.48.attended.refs_0_, bf16[32,2048]{1,0:T(8,128)(2,1)S(1)} %collective-permute-done.12.refs_1_, ...), custom_call_target="tpu_custom_call" | custom-call | flops 536870912 | bytes 4194304 | tf_op jit(solution)/shard_map/pallas_call | solution.py:391
  48.3 0.0 copy-start
  48.4 0.1 collective-permute-start.17
  48.4 0.7 %shard_map.91.own = f32[128,1024]{1,0:T(8,128)S(1)} custom-call(bf16[128,2048]{1,0:T(8,128)(2,1)S(1)} %get-tuple-element.53.permuted, bf16[2048,1024]{1,0:T(8,128)(2,1)S(1)} %shard_map.89.refs_6_.weight), custom_call_target="tpu_custom_call" | custom-call | flops 536870912 | bytes 4194304 | tf_op jit(solution)/shard_map/pallas_call | solution.py:400
  49.2 0.8 %collective-permute-done.17.received = bf16[128,1024]{1,0:T(8,128)(2,1)S(1)} collective-permute-done((bf16[128,1024]{1,0:T(8,128)(2,1)S(1)}, bf16[128,1024]{1,0:T(8,128)(2,1)S(1)}, u32[]{:S(2)}, u32[]{:S(2)}) %collective-permute-start.17) | collective-permute-done | bytes 262176 | tf_op jit(solution)/shard_map/ppermute | solution.py:205
  50.0 2.2 %collective-permute-start.18 = (bf16[32,1024]{1,0:T(8,128)(2,1)S(1)}, bf16[32,1024]{1,0:T(8,128)(2,1)S(1)}, u32[]{:S(2)}, u32[]{:S(2)}) collective-permute-start(bf16[32,1024]{1,0:T(8,128)(2,1)S(1)} %get-tuple-element.55), channel_id=1, source_target_pairs={{0,8},{4,12},{8,0},{12,4},{1,9},{5,13},{9,1},{13,5},{2,10},{6,14},... | collective-permute-start | bytes 196616 | tf_op jit(solution)/shard_map/ppermute | solution.py:205
  52.2 2.2 %collective-permute-start.19 = (bf16[32,1024]{1,0:T(8,128)(2,1)S(1)}, bf16[32,1024]{1,0:T(8,128)(2,1)S(1)}, u32[]{:S(2)}, u32[]{:S(2)}) collective-permute-start(bf16[32,1024]{1,0:T(8,128)(2,1)S(1)} %get-tuple-element.56), channel_id=1, source_target_pairs={{0,12},{2,4},{4,8},{6,0},{8,14},{10,6},{12,10},{14,2},{1,13},{3,5}... | collective-permute-start | bytes 196616 | tf_op jit(solution)/shard_map/ppermute | solution.py:452
  54.4 1.5 %collective-permute-done.18.passed.refs_0_ = bf16[32,1024]{1,0:T(8,128)(2,1)S(1)} collective-permute-done((bf16[32,1024]{1,0:T(8,128)(2,1)S(1)}, bf16[32,1024]{1,0:T(8,128)(2,1)S(1)}, u32[]{:S(2)}, u32[]{:S(2)}) %collective-permute-start.18) | collective-permute-done | bytes 65568 | tf_op jit(solution)/shard_map/ppermute | solution.py:205
  56.0 2.9 %collective-permute-start.21 = (bf16[32,1024]{1,0:T(8,128)(2,1)S(1)}, bf16[32,1024]{1,0:T(8,128)(2,1)S(1)}, u32[]{:S(2)}, u32[]{:S(2)}) collective-permute-start(bf16[32,1024]{1,0:T(8,128)(2,1)S(1)} %shard_map.93), channel_id=1, source_target_pairs={{0,2},{2,0},{1,3},{3,1},{4,6},{6,4},{5,7},{7,5},{8,10},{10,8},{9,1... | collective-permute-start | bytes 196616 | tf_op jit(solution)/shard_map/ppermute | solution.py:205
  58.9 0.7 %collective-permute-done.20.refs_2_ = bf16[32,1024]{1,0:T(8,128)(2,1)S(1)} collective-permute-done((bf16[32,1024]{1,0:T(8,128)(2,1)S(1)}, bf16[32,1024]{1,0:T(8,128)(2,1)S(1)}, u32[]{:S(2)}, u32[]{:S(2)}) %collective-permute-start.20) | collective-permute-done | bytes 65568 | tf_op jit(solution)/shard_map/ppermute | solution.py:452
  59.6 1.5 %collective-permute-done.21.refs_4_ = bf16[32,1024]{1,0:T(8,128)(2,1)S(1)} collective-permute-done((bf16[32,1024]{1,0:T(8,128)(2,1)S(1)}, bf16[32,1024]{1,0:T(8,128)(2,1)S(1)}, u32[]{:S(2)}, u32[]{:S(2)}) %collective-permute-start.21) | collective-permute-done | bytes 65568 | tf_op jit(solution)/shard_map/ppermute | solution.py:205
  61.1 0.1 shard_map.94
  61.2 0.1 collective-permute-start.22
  61.3 1.3 %collective-permute-done.22.received = bf16[32,2048]{1,0:T(8,128)(2,1)S(1)} collective-permute-done((bf16[32,2048]{1,0:T(8,128)(2,1)S(1)}, bf16[32,2048]{1,0:T(8,128)(2,1)S(1)}, u32[]{:S(2)}, u32[]{:S(2)}) %collective-permute-start.22) | collective-permute-done | bytes 131104 | tf_op jit(solution)/shard_map/ppermute | solution.py:205
  62.6 0.7 %shard_map.95 = bf16[1,32,4096]{2,1,0:T(8,128)(2,1)} custom-call(bf16[32,2048]{1,0:T(8,128)(2,1)S(1)} %get-tuple-element.59.keep, bf16[32,2048]{1,0:T(8,128)(2,1)S(1)} %collective-permute-done.22.received), custom_call_target="tpu_custom_call" | custom-call | bytes 524288 | tf_op jit(solution)/shard_map/pallas_call | solution.py:696
  (21 shorter events, 0.1 us)
Async XLA Ops:
  0.9 7.9 %collective-permute-start.2 = (bf16[16,2048]{1,0:T(8,128)(2,1)S(1)}, bf16[16,2048]{1,0:T(8,128)(2,1)S(1)}, u32[]{:S(2)}, u32[]{:S(2)}) collective-permute-start(bf16[16,2048]{1,0:T(8,128)(2,1)S(1)} %get-tuple-element.62.refs_0_), channel_id=1, source_target_pairs={{0,8},{4,12},{8,0},{12,4},{1,9},{5,13},{9,1},{13,5},{2,10},{6,14},... | collective-permute-start | bytes 196616 | tf_op jit(solution)/shard_map/ppermute | solution.py:205
  5.0 11.5 %copy-start.1 = (bf16[4096]{0:T(1024)(128)(2,1)S(1)}, bf16[4096]{0:T(1024)(128)(2,1)}, u32[]{:S(2)}) copy-start(bf16[4096]{0:T(1024)(128)(2,1)} %param.9) | copy-start | bytes 24580
  5.0 6.1 %collective-permute-start.3 = (bf16[16,2048]{1,0:T(8,128)(2,1)S(1)}, bf16[16,2048]{1,0:T(8,128)(2,1)S(1)}, u32[]{:S(2)}, u32[]{:S(2)}) collective-permute-start(bf16[16,2048]{1,0:T(8,128)(2,1)S(1)} %get-tuple-element.61.refs_1_), channel_id=1, source_target_pairs={{0,8},{4,12},{8,0},{12,4},{1,9},{5,13},{9,1},{13,5},{2,10},{6,14},... | collective-permute-start | bytes 196616 | tf_op jit(solution)/shard_map/ppermute | solution.py:205
  5.1 11.4 %collective-permute-start = (bf16[16,2048]{1,0:T(8,128)(2,1)S(1)}, bf16[16,2048]{1,0:T(8,128)(2,1)S(1)}, u32[]{:S(2)}, u32[]{:S(2)}) collective-permute-start(bf16[16,2048]{1,0:T(8,128)(2,1)S(1)} %get-tuple-element.62.refs_0_), channel_id=1, source_target_pairs={{0,4},{4,0},{8,12},{12,8},{1,5},{5,1},{9,13},{13,9},{2,6},{6,2},{1... | collective-permute-start | bytes 196616 | tf_op jit(solution)/shard_map/ppermute | solution.py:205
  6.9 9.6 %collective-permute-start.1 = (bf16[16,2048]{1,0:T(8,128)(2,1)S(1)}, bf16[16,2048]{1,0:T(8,128)(2,1)S(1)}, u32[]{:S(2)}, u32[]{:S(2)}) collective-permute-start(bf16[16,2048]{1,0:T(8,128)(2,1)S(1)} %get-tuple-element.61.refs_1_), channel_id=1, source_target_pairs={{0,4},{4,0},{8,12},{12,8},{1,5},{5,1},{9,13},{13,9},{2,6},{6,2},{1... | collective-permute-start | bytes 196616 | tf_op jit(solution)/shard_map/ppermute | solution.py:205
  8.7 7.8 %collective-permute-start.4 = (bf16[16,2048]{1,0:T(8,128)(2,1)S(1)}, bf16[16,2048]{1,0:T(8,128)(2,1)S(1)}, u32[]{:S(2)}, u32[]{:S(2)}) collective-permute-start(bf16[16,2048]{1,0:T(8,128)(2,1)S(1)} %collective-permute-done.2.refs_4_), channel_id=1, source_target_pairs={{0,4},{4,0},{8,12},{12,8},{1,5},{5,1},{9,13},{13,9},{2,6},{6,2},{1... | collective-permute-start | bytes 196616 | tf_op jit(solution)/shard_map/ppermute | solution.py:205
  11.1 5.4 %collective-permute-start.5 = (bf16[16,2048]{1,0:T(8,128)(2,1)S(1)}, bf16[16,2048]{1,0:T(8,128)(2,1)S(1)}, u32[]{:S(2)}, u32[]{:S(2)}) collective-permute-start(bf16[16,2048]{1,0:T(8,128)(2,1)S(1)} %collective-permute-done.3.refs_5_), channel_id=1, source_target_pairs={{0,4},{4,0},{8,12},{12,8},{1,5},{5,1},{9,13},{13,9},{2,6},{6,2},{1... | collective-permute-start | bytes 196616 | tf_op jit(solution)/shard_map/ppermute | solution.py:205
  17.6 12.2 %copy-start.2 = (s32[128]{0:T(128)S(1)}, s32[128]{0:T(128)}, u32[]{:S(2)}) copy-start(s32[128]{0:T(128)} %slots.3) | copy-start | bytes 1540
  17.6 12.2 %copy-start.3 = (s32[32]{0:T(128)S(1)}, s32[32]{0:T(128)}, u32[]{:S(2)}) copy-start(s32[32]{0:T(128)} %lengths.1) | copy-start | bytes 388
  17.6 1.7 %collective-permute-start.6 = (bf16[128,1408]{1,0:T(8,128)(2,1)S(1)}, bf16[128,1408]{1,0:T(8,128)(2,1)S(1)}, u32[]{:S(2)}, u32[]{:S(2)}) collective-permute-start(bf16[128,1408]{1,0:T(8,128)(2,1)S(1)} %get-tuple-element.40.given), channel_id=1, source_target_pairs={{0,1},{1,0},{2,3},{3,2},{4,5},{5,4},{6,7},{7,6},{8,9},{9,8},{10,11... | collective-permute-start | bytes 1081352 | tf_op jit(solution)/shard_map/ppermute | solution.py:205
  19.5 7.8 %collective-permute-start.7 = (bf16[32,1280]{1,0:T(8,128)(2,1)S(1)}, bf16[32,1280]{1,0:T(8,128)(2,1)S(1)}, u32[]{:S(2)}, u32[]{:S(2)}) collective-permute-start(bf16[32,1280]{1,0:T(8,128)(2,1)S(1)} %get-tuple-element.41), channel_id=1, source_target_pairs={{0,8},{4,12},{8,0},{12,4},{1,9},{5,13},{9,1},{13,5},{2,10},{6,14},... | collective-permute-start | bytes 245768 | tf_op jit(solution)/shard_map/ppermute | solution.py:205
  22.6 3.7 %collective-permute-start.10 = (bf16[32,128]{1,0:T(8,128)(2,1)S(1)}, bf16[32,128]{1,0:T(8,128)(2,1)S(1)}, u32[]{:S(2)}, u32[]{:S(2)}) collective-permute-start(bf16[32,128]{1,0:T(8,128)(2,1)S(1)} %get-tuple-element.45.refs_5_), channel_id=1, source_target_pairs={{0,2},{2,0},{1,3},{3,1},{4,6},{6,4},{5,7},{7,5},{8,10},{10,8},{9,1... | collective-permute-start | bytes 24584 | tf_op jit(solution)/shard_map/ppermute | solution.py:205
  24.1 8.9 %collective-permute-start.8 = (bf16[32,1280]{1,0:T(8,128)(2,1)S(1)}, bf16[32,1280]{1,0:T(8,128)(2,1)S(1)}, u32[]{:S(2)}, u32[]{:S(2)}) collective-permute-start(bf16[32,1280]{1,0:T(8,128)(2,1)S(1)} %get-tuple-element.42), channel_id=1, source_target_pairs={{0,12},{2,4},{4,8},{6,0},{8,14},{10,6},{12,10},{14,2},{1,13},{3,5}... | collective-permute-start | bytes 245768 | tf_op jit(solution)/shard_map/ppermute | solution.py:452
  24.5 8.5 %collective-permute-start.9 = (bf16[32,1280]{1,0:T(8,128)(2,1)S(1)}, bf16[32,1280]{1,0:T(8,128)(2,1)S(1)}, u32[]{:S(2)}, u32[]{:S(2)}) collective-permute-start(bf16[32,1280]{1,0:T(8,128)(2,1)S(1)} %get-tuple-element.43), channel_id=1, source_target_pairs={{0,4},{2,12},{4,0},{6,8},{8,6},{10,14},{12,2},{14,10},{1,5},{3,13}... | collective-permute-start | bytes 245768 | tf_op jit(solution)/shard_map/ppermute | solution.py:452
  27.2 5.8 %collective-permute-start.11 = (bf16[32,1280]{1,0:T(8,128)(2,1)S(1)}, bf16[32,1280]{1,0:T(8,128)(2,1)S(1)}, u32[]{:S(2)}, u32[]{:S(2)}) collective-permute-start(bf16[32,1280]{1,0:T(8,128)(2,1)S(1)} %shard_map.87), channel_id=1, source_target_pairs={{0,2},{2,0},{1,3},{3,1},{4,6},{6,4},{5,7},{7,5},{8,10},{10,8},{9,1... | collective-permute-start | bytes 245768 | tf_op jit(solution)/shard_map/ppermute | solution.py:205
  34.9 6.0 %collective-permute-start.13 = (bf16[16,2048]{1,0:T(8,128)(2,1)S(1)}, bf16[16,2048]{1,0:T(8,128)(2,1)S(1)}, u32[]{:S(2)}, u32[]{:S(2)}) collective-permute-start(bf16[16,2048]{1,0:T(8,128)(2,1)S(1)} %get-tuple-element.50), channel_id=1, source_target_pairs={{0,8},{4,12},{8,0},{12,4},{1,9},{5,13},{9,1},{13,5},{2,10},{6,14},... | collective-permute-start | bytes 196616 | tf_op jit(solution)/shard_map/ppermute | solution.py:205
  36.0 6.5 %collective-permute-start.14 = (bf16[16,2048]{1,0:T(8,128)(2,1)S(1)}, bf16[16,2048]{1,0:T(8,128)(2,1)S(1)}, u32[]{:S(2)}, u32[]{:S(2)}) collective-permute-start(bf16[16,2048]{1,0:T(8,128)(2,1)S(1)} %get-tuple-element.51), channel_id=1, source_target_pairs={{0,8},{4,12},{8,0},{12,4},{1,9},{5,13},{9,1},{13,5},{2,10},{6,14},... | collective-permute-start | bytes 196616 | tf_op jit(solution)/shard_map/ppermute | solution.py:205
  37.9 9.6 %collective-permute-start.12 = (bf16[32,2048]{1,0:T(8,128)(2,1)S(1)}, bf16[32,2048]{1,0:T(8,128)(2,1)S(1)}, u32[]{:S(2)}, u32[]{:S(2)}) collective-permute-start(bf16[32,2048]{1,0:T(8,128)(2,1)S(1)} %get-tuple-element.48.attended.refs_0_), channel_id=1, source_target_pairs={{0,4},{4,0},{8,12},{12,8},{1,5},{5,1},{9,13},{13,9},{2,6},{6,2},{1... | collective-permute-start | bytes 393224 | tf_op jit(solution)/shard_map/ppermute | solution.py:205
  40.9 6.6 %collective-permute-start.15 = (bf16[16,2048]{1,0:T(8,128)(2,1)S(1)}, bf16[16,2048]{1,0:T(8,128)(2,1)S(1)}, u32[]{:S(2)}, u32[]{:S(2)}) collective-permute-start(bf16[16,2048]{1,0:T(8,128)(2,1)S(1)} %collective-permute-done.13.refs_2_), channel_id=1, source_target_pairs={{0,4},{4,0},{8,12},{12,8},{1,5},{5,1},{9,13},{13,9},{2,6},{6,2},{1... | collective-permute-start | bytes 196616 | tf_op jit(solution)/shard_map/ppermute | solution.py:205
  42.5 5.0 %collective-permute-start.16 = (bf16[16,2048]{1,0:T(8,128)(2,1)S(1)}, bf16[16,2048]{1,0:T(8,128)(2,1)S(1)}, u32[]{:S(2)}, u32[]{:S(2)}) collective-permute-start(bf16[16,2048]{1,0:T(8,128)(2,1)S(1)} %collective-permute-done.14.refs_3_), channel_id=1, source_target_pairs={{0,4},{4,0},{8,12},{12,8},{1,5},{5,1},{9,13},{13,9},{2,6},{6,2},{1... | collective-permute-start | bytes 196616 | tf_op jit(solution)/shard_map/ppermute | solution.py:205
  48.3 12.8 %copy-start = (bf16[32,4096]{1,0:T(8,128)(2,1)S(1)}, bf16[32,4096]{1,0:T(8,128)(2,1)}, u32[]{:S(2)}) copy-start(bf16[32,4096]{1,0:T(8,128)(2,1)} %hidden.1) | copy-start | bytes 786436
  48.4 1.6 %collective-permute-start.17 = (bf16[128,1024]{1,0:T(8,128)(2,1)S(1)}, bf16[128,1024]{1,0:T(8,128)(2,1)S(1)}, u32[]{:S(2)}, u32[]{:S(2)}) collective-permute-start(bf16[128,1024]{1,0:T(8,128)(2,1)S(1)} %get-tuple-element.54.given), channel_id=1, source_target_pairs={{0,1},{1,0},{2,3},{3,2},{4,5},{5,4},{6,7},{7,6},{8,9},{9,8},{10,11... | collective-permute-start | bytes 786440 | tf_op jit(solution)/shard_map/ppermute | solution.py:205
  50.0 5.9 %collective-permute-start.18 = (bf16[32,1024]{1,0:T(8,128)(2,1)S(1)}, bf16[32,1024]{1,0:T(8,128)(2,1)S(1)}, u32[]{:S(2)}, u32[]{:S(2)}) collective-permute-start(bf16[32,1024]{1,0:T(8,128)(2,1)S(1)} %get-tuple-element.55), channel_id=1, source_target_pairs={{0,8},{4,12},{8,0},{12,4},{1,9},{5,13},{9,1},{13,5},{2,10},{6,14},... | collective-permute-start | bytes 196616 | tf_op jit(solution)/shard_map/ppermute | solution.py:205
  52.2 6.7 %collective-permute-start.19 = (bf16[32,1024]{1,0:T(8,128)(2,1)S(1)}, bf16[32,1024]{1,0:T(8,128)(2,1)S(1)}, u32[]{:S(2)}, u32[]{:S(2)}) collective-permute-start(bf16[32,1024]{1,0:T(8,128)(2,1)S(1)} %get-tuple-element.56), channel_id=1, source_target_pairs={{0,12},{2,4},{4,8},{6,0},{8,14},{10,6},{12,10},{14,2},{1,13},{3,5}... | collective-permute-start | bytes 196616 | tf_op jit(solution)/shard_map/ppermute | solution.py:452
  54.4 5.2 %collective-permute-start.20 = (bf16[32,1024]{1,0:T(8,128)(2,1)S(1)}, bf16[32,1024]{1,0:T(8,128)(2,1)S(1)}, u32[]{:S(2)}, u32[]{:S(2)}) collective-permute-start(bf16[32,1024]{1,0:T(8,128)(2,1)S(1)} %get-tuple-element.57), channel_id=1, source_target_pairs={{0,4},{2,12},{4,0},{6,8},{8,6},{10,14},{12,2},{14,10},{1,5},{3,13}... | collective-permute-start | bytes 196616 | tf_op jit(solution)/shard_map/ppermute | solution.py:452
  56.0 5.2 %collective-permute-start.21 = (bf16[32,1024]{1,0:T(8,128)(2,1)S(1)}, bf16[32,1024]{1,0:T(8,128)(2,1)S(1)}, u32[]{:S(2)}, u32[]{:S(2)}) collective-permute-start(bf16[32,1024]{1,0:T(8,128)(2,1)S(1)} %shard_map.93), channel_id=1, source_target_pairs={{0,2},{2,0},{1,3},{3,1},{4,6},{6,4},{5,7},{7,5},{8,10},{10,8},{9,1... | collective-permute-start | bytes 196616 | tf_op jit(solution)/shard_map/ppermute | solution.py:205
  61.2 1.4 %collective-permute-start.22 = (bf16[32,2048]{1,0:T(8,128)(2,1)S(1)}, bf16[32,2048]{1,0:T(8,128)(2,1)S(1)}, u32[]{:S(2)}, u32[]{:S(2)}) collective-permute-start(bf16[32,2048]{1,0:T(8,128)(2,1)S(1)} %get-tuple-element.60), channel_id=1, source_target_pairs={{0,1},{1,0},{2,3},{3,2},{4,5},{5,4},{6,7},{7,6},{8,9},{9,8},{10,11... | collective-permute-start | bytes 393224 | tf_op jit(solution)/shard_map/ppermute | solution.py:205

commit v21 on v18

--- a/solution.py
+++ b/solution.py
@@ -172,7 +172,6 @@
 OUT_WIDTH = GROUP * HEAD_DIM
 SLOTS = 8
 VMEM = pl.BlockSpec(memory_space=pltpu.VMEM)
-SMEM = pl.BlockSpec(memory_space=pltpu.SMEM)
 HBM = pl.BlockSpec(memory_space=pl.ANY)
 MIB = 2**20
 
@@ -488,10 +487,11 @@
 
 
 def rope(lengths, rows):
-    slot = lax.broadcasted_iota(jnp.int32, (rows, HEAD_DIM), 0)
-    length_of = jnp.zeros((rows, HEAD_DIM), jnp.int32)
-    for i in range(rows):
-        length_of = jnp.where(slot == i, lengths[i], length_of)
+    row = lax.broadcasted_iota(jnp.int32, (rows, rows), 0)
+    slot = lax.broadcasted_iota(jnp.int32, (rows, rows), 1)
+    own = jnp.where(row == slot, lengths[...].reshape(1, rows), 0)
+    column = jnp.sum(own.astype(jnp.float32), axis=1, keepdims=True).astype(jnp.int32)
+    length_of = jnp.broadcast_to(column, (rows, HEAD_DIM))
     lane = lax.broadcasted_iota(jnp.int32, (rows, HEAD_DIM), 1)
     half = HEAD_DIM // 2
     step = lax.rem(lane, half).astype(jnp.float32)
@@ -644,7 +644,7 @@
         [pltpu.VMEM((half, half_out), jnp.bfloat16)]
         + [pltpu.VMEM((rows, cache, pairs * HEAD_DIM), jnp.bfloat16)] * 2
         + [table, table, struct((rows, HEAD_DIM), jnp.int32), struct(square)],
-        [SMEM, HBM, HBM, HBM, VMEM],
+        [VMEM, HBM, HBM, HBM, VMEM],
         [VMEM] * 7,
         0,
         half * half_out * 2 + 4 * rows * cache * pairs * HEAD_DIM,

time: 62.6 us -> 63.3 us (1.011)
  starting transfers between devices: 32 us -> 34 us
  waiting for transfers between devices: 13.2 us -> 12.4 us
    ppermute x19, starting transfers between devices: 28.4 us -> 31 us  [moved(): return lax.ppermute(value, axis, pairs)]
    ppermute x4, waiting for transfers between devices: 2.44 us -> 0.77 us  [direct(): return lax.ppermute(value, ('col', 'row'), moves)]
    ppermute x19, waiting for transfers between devices: 10.7 us -> 11.7 us  [moved(): return lax.ppermute(value, axis, pairs)]
  transfers between devices with their start and end apart: 23 -> 23, of which waited for: 11 -> 11; matrix products, arithmetic and copies ran while one was open for 0% -> 0% of each run, Pallas kernels for 19% -> 18%
where the time goes in v21:
time: 63.3 us; the launch traced here: 63.2 us
  starting transfers between devices  34 us (54%)
  Pallas kernels  15.6 us (25%)
  waiting for transfers between devices  12.4 us (20%)
  local copies, waits for them, and re-layouts  0.9 us (1%)
    ppermute x19, starting transfers between devices, moved(): return lax.ppermute(value, axis, pairs)  31 us
    ppermute x19, waiting for transfers between devices, moved(): return lax.ppermute(value, axis, pairs)  11.7 us
    pallas_call x1, Pallas kernels, paired_plan(): call(functools.partial(stage_in_kernel, col_count), [pltpu.VMEM((half, ha...  4.09 us
    pallas_call x1, Pallas kernels, paired_plan(): call(functools.partial(stage_rest_kernel, col_count), [pltpu.VMEM((half,...  3.12 us
    ppermute x4, starting transfers between devices, direct(): return lax.ppermute(value, ('col', 'row'), moves)  2.96 us
    pallas_call x1, Pallas kernels, paired_plan(): call(stage_out_kernel, pltpu.VMEM((half, half_out), jnp.bfloat16), [HBM,...  2.24 us
    pallas_call x2, Pallas kernels, project(): call(functools.partial(kernel, parts), [struct((rows, half + more)), stru...  1.91 us
    pallas_call x1, Pallas kernels, paired_plan(): call(functools.partial(attend_all, len(products), parts), [struct((rows,...  1.71 us
  transfers between devices with their start and end apart: 23, of which 11 were waited for; matrix products, arithmetic and copies ran while one was open for 0% of the time, Pallas kernels for 18%

profile of v21, /device:TPU:0, one launch (start us, length us, event | category | flops | bytes accessed | tf_op | source)
XLA Modules:
  0.0 63.2 jit_solution(14304470607803366698)
XLA Ops:
  0.0 0.9 %fusion = (bf16[16,2048]{1,0:T(8,128)(2,1)S(1)}, bf16[16,2048]{1,0:T(8,128)(2,1)S(1)}) fusion(bf16[32,4096]{1,0:T(8,128)(2,1)} %hidden.1, s32[]{:T(128)S(6)} %add.4, s32[]{:T(128)S(6)} %select_n.3), kind=kLoop, calls=%fused_computation.1 | loop fusion | bytes 262152 | tf_op jit(solution)/shard_map/slice | solution.py:639
  0.9 4.1 %collective-permute-start.2 = (bf16[16,2048]{1,0:T(8,128)(2,1)S(1)}, bf16[16,2048]{1,0:T(8,128)(2,1)S(1)}, u32[]{:S(2)}, u32[]{:S(2)}) collective-permute-start(bf16[16,2048]{1,0:T(8,128)(2,1)S(1)} %get-tuple-element.62.refs_0_), channel_id=1, source_target_pairs={{0,8},{4,12},{8,0},{12,4},{1,9},{5,13},{9,1},{13,5},{2,10},{6,14},... | collective-permute-start | bytes 196616 | tf_op jit(solution)/shard_map/ppermute | solution.py:205
  5.0 0.1 collective-permute-start.3
  5.1 1.8 %collective-permute-start = (bf16[16,2048]{1,0:T(8,128)(2,1)S(1)}, bf16[16,2048]{1,0:T(8,128)(2,1)S(1)}, u32[]{:S(2)}, u32[]{:S(2)}) collective-permute-start(bf16[16,2048]{1,0:T(8,128)(2,1)S(1)} %get-tuple-element.62.refs_0_), channel_id=1, source_target_pairs={{0,4},{4,0},{8,12},{12,8},{1,5},{5,1},{9,13},{13,9},{2,6},{6,2},{1... | collective-permute-start | bytes 196616 | tf_op jit(solution)/shard_map/ppermute | solution.py:205
  6.9 0.2 collective-permute-start.1
  7.1 1.6 %collective-permute-done.2.refs_4_ = bf16[16,2048]{1,0:T(8,128)(2,1)S(1)} collective-permute-done((bf16[16,2048]{1,0:T(8,128)(2,1)S(1)}, bf16[16,2048]{1,0:T(8,128)(2,1)S(1)}, u32[]{:S(2)}, u32[]{:S(2)}) %collective-permute-start.2) | collective-permute-done | bytes 65568 | tf_op jit(solution)/shard_map/ppermute | solution.py:205
  8.7 1.9 %collective-permute-start.4 = (bf16[16,2048]{1,0:T(8,128)(2,1)S(1)}, bf16[16,2048]{1,0:T(8,128)(2,1)S(1)}, u32[]{:S(2)}, u32[]{:S(2)}) collective-permute-start(bf16[16,2048]{1,0:T(8,128)(2,1)S(1)} %collective-permute-done.2.refs_4_), channel_id=1, source_target_pairs={{0,4},{4,0},{8,12},{12,8},{1,5},{5,1},{9,13},{13,9},{2,6},{6,2},{1... | collective-permute-start | bytes 196616 | tf_op jit(solution)/shard_map/ppermute | solution.py:205
  10.6 0.4 collective-permute-done.3.refs_5_
  11.1 1.3 %collective-permute-start.5 = (bf16[16,2048]{1,0:T(8,128)(2,1)S(1)}, bf16[16,2048]{1,0:T(8,128)(2,1)S(1)}, u32[]{:S(2)}, u32[]{:S(2)}) collective-permute-start(bf16[16,2048]{1,0:T(8,128)(2,1)S(1)} %collective-permute-done.3.refs_5_), channel_id=1, source_target_pairs={{0,4},{4,0},{8,12},{12,8},{1,5},{5,1},{9,13},{13,9},{2,6},{6,2},{1... | collective-permute-start | bytes 196616 | tf_op jit(solution)/shard_map/ppermute | solution.py:205
  12.4 4.1 %shard_map.83 = (bf16[2048,1280]{1,0:T(8,128)(2,1)S(1)}, bf16[2048,1280]{1,0:T(8,128)(2,1)S(1)}, bf16[128,128]{1,0:T(8,128)(2,1)S(1)}) custom-call(bf16[4096,2560]{1,0:T(8,128)(2,1)} %weight.4, s32[128]{0:T(128)} %slots.3), custom_call_target="tpu_custom_call" | custom-call | bytes 10485760 | tf_op jit(solution)/shard_map/pallas_call | solution.py:625
  16.5 1.1 %shard_map.84 = (bf16[128,1408]{1,0:T(8,128)(2,1)S(1)}, bf16[128,2048]{1,0:T(8,128)(2,1)S(1)}) custom-call(bf16[128,128]{1,0:T(8,128)(2,1)S(1)} %get-tuple-element.36.chosen, bf16[16,2048]{1,0:T(8,128)(2,1)S(1)} %get-tuple-element.62.refs_0_, bf16[16,2048]{1,0:T(8,128)(2,1)S(1)} %get-tuple-element.61.refs_1_, ...), custom_call_target="tpu_custom_call" | custom-call | flops 671088640 | bytes 5242880 | tf_op jit(solution)/shard_map/pallas_call | solution.py:391
  17.6 0.0 copy-start.2
  17.6 0.0 copy-start.3
  17.6 0.1 collective-permute-start.6
  17.7 0.9 %shard_map.85.own = f32[128,1280]{1,0:T(8,128)S(1)} custom-call(bf16[128,2048]{1,0:T(8,128)(2,1)S(1)} %get-tuple-element.39.permuted, bf16[2048,1280]{1,0:T(8,128)(2,1)S(1)} %get-tuple-element.37.refs_8_.weight), custom_call_target="tpu_custom_call" | custom-call | flops 671088640 | bytes 5242880 | tf_op jit(solution)/shard_map/pallas_call | solution.py:400
  18.6 0.8 %collective-permute-done.6.received = bf16[128,1408]{1,0:T(8,128)(2,1)S(1)} collective-permute-done((bf16[128,1408]{1,0:T(8,128)(2,1)S(1)}, bf16[128,1408]{1,0:T(8,128)(2,1)S(1)}, u32[]{:S(2)}, u32[]{:S(2)}) %collective-permute-start.6) | collective-permute-done | bytes 360480 | tf_op jit(solution)/shard_map/ppermute | solution.py:205
  19.4 0.1 shard_map.86
  19.5 3.2 %collective-permute-start.7 = (bf16[32,1280]{1,0:T(8,128)(2,1)S(1)}, bf16[32,1280]{1,0:T(8,128)(2,1)S(1)}, u32[]{:S(2)}, u32[]{:S(2)}) collective-permute-start(bf16[32,1280]{1,0:T(8,128)(2,1)S(1)} %get-tuple-element.41), channel_id=1, source_target_pairs={{0,8},{4,12},{8,0},{12,4},{1,9},{5,13},{9,1},{13,5},{2,10},{6,14},... | collective-permute-start | bytes 245768 | tf_op jit(solution)/shard_map/ppermute | solution.py:205
  22.6 1.5 %collective-permute-start.10 = (bf16[32,128]{1,0:T(8,128)(2,1)S(1)}, bf16[32,128]{1,0:T(8,128)(2,1)S(1)}, u32[]{:S(2)}, u32[]{:S(2)}) collective-permute-start(bf16[32,128]{1,0:T(8,128)(2,1)S(1)} %get-tuple-element.45.refs_5_), channel_id=1, source_target_pairs={{0,2},{2,0},{1,3},{3,1},{4,6},{6,4},{5,7},{7,5},{8,10},{10,8},{9,1... | collective-permute-start | bytes 24584 | tf_op jit(solution)/shard_map/ppermute | solution.py:205
  24.1 0.4 collective-permute-start.8
  24.5 0.3 collective-permute-start.9
  24.9 1.4 %collective-permute-done.10.refs_0_.refs_6_ = bf16[32,128]{1,0:T(8,128)(2,1)S(1)} collective-permute-done((bf16[32,128]{1,0:T(8,128)(2,1)S(1)}, bf16[32,128]{1,0:T(8,128)(2,1)S(1)}, u32[]{:S(2)}, u32[]{:S(2)}) %collective-permute-start.10) | collective-permute-done | bytes 8224 | tf_op jit(solution)/shard_map/ppermute | solution.py:205
  26.3 0.9 %collective-permute-done.7.passed.refs_0_ = bf16[32,1280]{1,0:T(8,128)(2,1)S(1)} collective-permute-done((bf16[32,1280]{1,0:T(8,128)(2,1)S(1)}, bf16[32,1280]{1,0:T(8,128)(2,1)S(1)}, u32[]{:S(2)}, u32[]{:S(2)}) %collective-permute-start.7) | collective-permute-done | bytes 81952 | tf_op jit(solution)/shard_map/ppermute | solution.py:205
  27.2 2.6 %collective-permute-start.11 = (bf16[32,1280]{1,0:T(8,128)(2,1)S(1)}, bf16[32,1280]{1,0:T(8,128)(2,1)S(1)}, u32[]{:S(2)}, u32[]{:S(2)}) collective-permute-start(bf16[32,1280]{1,0:T(8,128)(2,1)S(1)} %shard_map.87), channel_id=1, source_target_pairs={{0,2},{2,0},{1,3},{3,1},{4,6},{6,4},{5,7},{7,5},{8,10},{10,8},{9,1... | collective-permute-start | bytes 245768 | tf_op jit(solution)/shard_map/ppermute | solution.py:205
  29.9 3.1 %shard_map.82 = (bf16[2048,1024]{1,0:T(8,128)(2,1)S(1)}, bf16[32,64,256]{2,1,0:T(8,128)(2,1)S(1)}, bf16[32,64,256]{2,1,0:T(8,128)(2,1)S(1)}, f32[32,128]{1,0:T(8...) custom-call(s32[32]{0:T(128)S(1)} %copy-done.3, bf16[4096,2048]{1,0:T(8,128)(2,1)} %weight.5, ...), custom_call_target="tpu_custom_call" | custom-call | bytes 6291456 | tf_op jit(solution)/shard_map/pallas_call | solution.py:642
  33.0 1.7 %shard_map.88 = (bf16[32,2048]{1,0:T(8,128)(2,1)S(1)}, bf16[16,2048]{1,0:T(8,128)(2,1)S(1)}, bf16[16,2048]{1,0:T(8,128)(2,1)S(1)}) custom-call(f32[32,128]{1,0:T(8,128)S(1)} %get-tuple-element.33.cosine, f32[32,128]{1,0:T(8,128)S(1)} %get-tuple-element.34.sine, s32[32,128]{1,0:T(8,128)S(1)} %get-tuple-element.35.lengths, ...), custom_call_target="tpu_custom_call" | custom-call | flops 16777216 | tf_op jit(solution)/shard_map/pallas_call | solution.py:658
  34.7 1.1 %collective-permute-start.13 = (bf16[16,2048]{1,0:T(8,128)(2,1)S(1)}, bf16[16,2048]{1,0:T(8,128)(2,1)S(1)}, u32[]{:S(2)}, u32[]{:S(2)}) collective-permute-start(bf16[16,2048]{1,0:T(8,128)(2,1)S(1)} %get-tuple-element.50), channel_id=1, source_target_pairs={{0,8},{4,12},{8,0},{12,4},{1,9},{5,13},{9,1},{13,5},{2,10},{6,14},... | collective-permute-start | bytes 196616 | tf_op jit(solution)/shard_map/ppermute | solution.py:205
  35.8 1.9 %collective-permute-start.14 = (bf16[16,2048]{1,0:T(8,128)(2,1)S(1)}, bf16[16,2048]{1,0:T(8,128)(2,1)S(1)}, u32[]{:S(2)}, u32[]{:S(2)}) collective-permute-start(bf16[16,2048]{1,0:T(8,128)(2,1)S(1)} %get-tuple-element.51), channel_id=1, source_target_pairs={{0,8},{4,12},{8,0},{12,4},{1,9},{5,13},{9,1},{13,5},{2,10},{6,14},... | collective-permute-start | bytes 196616 | tf_op jit(solution)/shard_map/ppermute | solution.py:205
  37.7 1.7 %collective-permute-start.12 = (bf16[32,2048]{1,0:T(8,128)(2,1)S(1)}, bf16[32,2048]{1,0:T(8,128)(2,1)S(1)}, u32[]{:S(2)}, u32[]{:S(2)}) collective-permute-start(bf16[32,2048]{1,0:T(8,128)(2,1)S(1)} %get-tuple-element.48.attended.refs_0_), channel_id=1, source_target_pairs={{0,4},{4,0},{8,12},{12,8},{1,5},{5,1},{9,13},{13,9},{2,6},{6,2},{1... | collective-permute-start | bytes 393224 | tf_op jit(solution)/shard_map/ppermute | solution.py:205
  39.4 1.3 %collective-permute-done.13.refs_2_ = bf16[16,2048]{1,0:T(8,128)(2,1)S(1)} collective-permute-done((bf16[16,2048]{1,0:T(8,128)(2,1)S(1)}, bf16[16,2048]{1,0:T(8,128)(2,1)S(1)}, u32[]{:S(2)}, u32[]{:S(2)}) %collective-permute-start.13) | collective-permute-done | bytes 65568 | tf_op jit(solution)/shard_map/ppermute | solution.py:205
  40.7 1.6 %collective-permute-start.15 = (bf16[16,2048]{1,0:T(8,128)(2,1)S(1)}, bf16[16,2048]{1,0:T(8,128)(2,1)S(1)}, u32[]{:S(2)}, u32[]{:S(2)}) collective-permute-start(bf16[16,2048]{1,0:T(8,128)(2,1)S(1)} %collective-permute-done.13.refs_2_), channel_id=1, source_target_pairs={{0,4},{4,0},{8,12},{12,8},{1,5},{5,1},{9,13},{13,9},{2,6},{6,2},{1... | collective-permute-start | bytes 196616 | tf_op jit(solution)/shard_map/ppermute | solution.py:205
  42.3 2.7 %collective-permute-start.16 = (bf16[16,2048]{1,0:T(8,128)(2,1)S(1)}, bf16[16,2048]{1,0:T(8,128)(2,1)S(1)}, u32[]{:S(2)}, u32[]{:S(2)}) collective-permute-start(bf16[16,2048]{1,0:T(8,128)(2,1)S(1)} %collective-permute-done.14.refs_3_), channel_id=1, source_target_pairs={{0,4},{4,0},{8,12},{12,8},{1,5},{5,1},{9,13},{13,9},{2,6},{6,2},{1... | collective-permute-start | bytes 196616 | tf_op jit(solution)/shard_map/ppermute | solution.py:205
  45.0 2.2 %shard_map.89.refs_6_.weight = bf16[2048,1024]{1,0:T(8,128)(2,1)S(1)} custom-call(bf16[4096,2048]{1,0:T(8,128)(2,1)} %weight.5, bf16[32,2048]{1,0:T(8,128)(2,1)S(1)} %get-tuple-element.48.attended.refs_0_), custom_call_target="tpu_custom_call" | custom-call | bytes 4194304 | tf_op jit(solution)/shard_map/pallas_call | solution.py:675
  47.3 0.8 %shard_map.90 = (bf16[128,1024]{1,0:T(8,128)(2,1)S(1)}, bf16[128,2048]{1,0:T(8,128)(2,1)S(1)}) custom-call(bf16[128,128]{1,0:T(8,128)(2,1)S(1)} %get-tuple-element.49.chosen, bf16[32,2048]{1,0:T(8,128)(2,1)S(1)} %get-tuple-element.48.attended.refs_0_, bf16[32,2048]{1,0:T(8,128)(2,1)S(1)} %collective-permute-done.12.refs_1_, ...), custom_call_target="tpu_custom_call" | custom-call | flops 536870912 | bytes 4194304 | tf_op jit(solution)/shard_map/pallas_call | solution.py:391
  48.2 0.0 copy-start
  48.2 0.1 collective-permute-start.17
  48.3 0.7 %shard_map.91.own = f32[128,1024]{1,0:T(8,128)S(1)} custom-call(bf16[128,2048]{1,0:T(8,128)(2,1)S(1)} %get-tuple-element.53.permuted, bf16[2048,1024]{1,0:T(8,128)(2,1)S(1)} %shard_map.89.refs_6_.weight), custom_call_target="tpu_custom_call" | custom-call | flops 536870912 | bytes 4194304 | tf_op jit(solution)/shard_map/pallas_call | solution.py:400
  49.0 0.8 %collective-permute-done.17.received = bf16[128,1024]{1,0:T(8,128)(2,1)S(1)} collective-permute-done((bf16[128,1024]{1,0:T(8,128)(2,1)S(1)}, bf16[128,1024]{1,0:T(8,128)(2,1)S(1)}, u32[]{:S(2)}, u32[]{:S(2)}) %collective-permute-start.17) | collective-permute-done | bytes 262176 | tf_op jit(solution)/shard_map/ppermute | solution.py:205
  49.8 2.2 %collective-permute-start.18 = (bf16[32,1024]{1,0:T(8,128)(2,1)S(1)}, bf16[32,1024]{1,0:T(8,128)(2,1)S(1)}, u32[]{:S(2)}, u32[]{:S(2)}) collective-permute-start(bf16[32,1024]{1,0:T(8,128)(2,1)S(1)} %get-tuple-element.55), channel_id=1, source_target_pairs={{0,8},{4,12},{8,0},{12,4},{1,9},{5,13},{9,1},{13,5},{2,10},{6,14},... | collective-permute-start | bytes 196616 | tf_op jit(solution)/shard_map/ppermute | solution.py:205
  52.0 2.2 %collective-permute-start.19 = (bf16[32,1024]{1,0:T(8,128)(2,1)S(1)}, bf16[32,1024]{1,0:T(8,128)(2,1)S(1)}, u32[]{:S(2)}, u32[]{:S(2)}) collective-permute-start(bf16[32,1024]{1,0:T(8,128)(2,1)S(1)} %get-tuple-element.56), channel_id=1, source_target_pairs={{0,12},{2,4},{4,8},{6,0},{8,14},{10,6},{12,10},{14,2},{1,13},{3,5}... | collective-permute-start | bytes 196616 | tf_op jit(solution)/shard_map/ppermute | solution.py:452
  54.2 1.5 %collective-permute-done.18.passed.refs_0_ = bf16[32,1024]{1,0:T(8,128)(2,1)S(1)} collective-permute-done((bf16[32,1024]{1,0:T(8,128)(2,1)S(1)}, bf16[32,1024]{1,0:T(8,128)(2,1)S(1)}, u32[]{:S(2)}, u32[]{:S(2)}) %collective-permute-start.18) | collective-permute-done | bytes 65568 | tf_op jit(solution)/shard_map/ppermute | solution.py:205
  55.8 2.9 %collective-permute-start.21 = (bf16[32,1024]{1,0:T(8,128)(2,1)S(1)}, bf16[32,1024]{1,0:T(8,128)(2,1)S(1)}, u32[]{:S(2)}, u32[]{:S(2)}) collective-permute-start(bf16[32,1024]{1,0:T(8,128)(2,1)S(1)} %shard_map.93), channel_id=1, source_target_pairs={{0,2},{2,0},{1,3},{3,1},{4,6},{6,4},{5,7},{7,5},{8,10},{10,8},{9,1... | collective-permute-start | bytes 196616 | tf_op jit(solution)/shard_map/ppermute | solution.py:205
  58.7 0.8 %collective-permute-done.20.refs_2_ = bf16[32,1024]{1,0:T(8,128)(2,1)S(1)} collective-permute-done((bf16[32,1024]{1,0:T(8,128)(2,1)S(1)}, bf16[32,1024]{1,0:T(8,128)(2,1)S(1)}, u32[]{:S(2)}, u32[]{:S(2)}) %collective-permute-start.20) | collective-permute-done | bytes 65568 | tf_op jit(solution)/shard_map/ppermute | solution.py:452
  59.5 1.5 %collective-permute-done.21.refs_4_ = bf16[32,1024]{1,0:T(8,128)(2,1)S(1)} collective-permute-done((bf16[32,1024]{1,0:T(8,128)(2,1)S(1)}, bf16[32,1024]{1,0:T(8,128)(2,1)S(1)}, u32[]{:S(2)}, u32[]{:S(2)}) %collective-permute-start.21) | collective-permute-done | bytes 65568 | tf_op jit(solution)/shard_map/ppermute | solution.py:205
  60.9 0.1 shard_map.94
  61.0 0.1 collective-permute-start.22
  61.1 1.3 %collective-permute-done.22.received = bf16[32,2048]{1,0:T(8,128)(2,1)S(1)} collective-permute-done((bf16[32,2048]{1,0:T(8,128)(2,1)S(1)}, bf16[32,2048]{1,0:T(8,128)(2,1)S(1)}, u32[]{:S(2)}, u32[]{:S(2)}) %collective-permute-start.22) | collective-permute-done | bytes 131104 | tf_op jit(solution)/shard_map/ppermute | solution.py:205
  62.4 0.7 %shard_map.95 = bf16[1,32,4096]{2,1,0:T(8,128)(2,1)} custom-call(bf16[32,2048]{1,0:T(8,128)(2,1)S(1)} %get-tuple-element.59.keep, bf16[32,2048]{1,0:T(8,128)(2,1)S(1)} %collective-permute-done.22.received), custom_call_target="tpu_custom_call" | custom-call | bytes 524288 | tf_op jit(solution)/shard_map/pallas_call | solution.py:696
  (21 shorter events, 0.1 us)
Async XLA Ops:
  0.9 7.9 %collective-permute-start.2 = (bf16[16,2048]{1,0:T(8,128)(2,1)S(1)}, bf16[16,2048]{1,0:T(8,128)(2,1)S(1)}, u32[]{:S(2)}, u32[]{:S(2)}) collective-permute-start(bf16[16,2048]{1,0:T(8,128)(2,1)S(1)} %get-tuple-element.62.refs_0_), channel_id=1, source_target_pairs={{0,8},{4,12},{8,0},{12,4},{1,9},{5,13},{9,1},{13,5},{2,10},{6,14},... | collective-permute-start | bytes 196616 | tf_op jit(solution)/shard_map/ppermute | solution.py:205
  5.0 11.5 %copy-start.1 = (bf16[4096]{0:T(1024)(128)(2,1)S(1)}, bf16[4096]{0:T(1024)(128)(2,1)}, u32[]{:S(2)}) copy-start(bf16[4096]{0:T(1024)(128)(2,1)} %param.9) | copy-start | bytes 24580
  5.0 6.1 %collective-permute-start.3 = (bf16[16,2048]{1,0:T(8,128)(2,1)S(1)}, bf16[16,2048]{1,0:T(8,128)(2,1)S(1)}, u32[]{:S(2)}, u32[]{:S(2)}) collective-permute-start(bf16[16,2048]{1,0:T(8,128)(2,1)S(1)} %get-tuple-element.61.refs_1_), channel_id=1, source_target_pairs={{0,8},{4,12},{8,0},{12,4},{1,9},{5,13},{9,1},{13,5},{2,10},{6,14},... | collective-permute-start | bytes 196616 | tf_op jit(solution)/shard_map/ppermute | solution.py:205
  5.1 11.4 %collective-permute-start = (bf16[16,2048]{1,0:T(8,128)(2,1)S(1)}, bf16[16,2048]{1,0:T(8,128)(2,1)S(1)}, u32[]{:S(2)}, u32[]{:S(2)}) collective-permute-start(bf16[16,2048]{1,0:T(8,128)(2,1)S(1)} %get-tuple-element.62.refs_0_), channel_id=1, source_target_pairs={{0,4},{4,0},{8,12},{12,8},{1,5},{5,1},{9,13},{13,9},{2,6},{6,2},{1... | collective-permute-start | bytes 196616 | tf_op jit(solution)/shard_map/ppermute | solution.py:205
  6.9 9.6 %collective-permute-start.1 = (bf16[16,2048]{1,0:T(8,128)(2,1)S(1)}, bf16[16,2048]{1,0:T(8,128)(2,1)S(1)}, u32[]{:S(2)}, u32[]{:S(2)}) collective-permute-start(bf16[16,2048]{1,0:T(8,128)(2,1)S(1)} %get-tuple-element.61.refs_1_), channel_id=1, source_target_pairs={{0,4},{4,0},{8,12},{12,8},{1,5},{5,1},{9,13},{13,9},{2,6},{6,2},{1... | collective-permute-start | bytes 196616 | tf_op jit(solution)/shard_map/ppermute | solution.py:205
  8.7 7.8 %collective-permute-start.4 = (bf16[16,2048]{1,0:T(8,128)(2,1)S(1)}, bf16[16,2048]{1,0:T(8,128)(2,1)S(1)}, u32[]{:S(2)}, u32[]{:S(2)}) collective-permute-start(bf16[16,2048]{1,0:T(8,128)(2,1)S(1)} %collective-permute-done.2.refs_4_), channel_id=1, source_target_pairs={{0,4},{4,0},{8,12},{12,8},{1,5},{5,1},{9,13},{13,9},{2,6},{6,2},{1... | collective-permute-start | bytes 196616 | tf_op jit(solution)/shard_map/ppermute | solution.py:205
  11.1 5.4 %collective-permute-start.5 = (bf16[16,2048]{1,0:T(8,128)(2,1)S(1)}, bf16[16,2048]{1,0:T(8,128)(2,1)S(1)}, u32[]{:S(2)}, u32[]{:S(2)}) collective-permute-start(bf16[16,2048]{1,0:T(8,128)(2,1)S(1)} %collective-permute-done.3.refs_5_), channel_id=1, source_target_pairs={{0,4},{4,0},{8,12},{12,8},{1,5},{5,1},{9,13},{13,9},{2,6},{6,2},{1... | collective-permute-start | bytes 196616 | tf_op jit(solution)/shard_map/ppermute | solution.py:205
  17.6 12.2 %copy-start.2 = (s32[128]{0:T(128)S(1)}, s32[128]{0:T(128)}, u32[]{:S(2)}) copy-start(s32[128]{0:T(128)} %slots.3) | copy-start | bytes 1540
  17.6 12.2 %copy-start.3 = (s32[32]{0:T(128)S(1)}, s32[32]{0:T(128)}, u32[]{:S(2)}) copy-start(s32[32]{0:T(128)} %lengths.1) | copy-start | bytes 388
  17.6 1.7 %collective-permute-start.6 = (bf16[128,1408]{1,0:T(8,128)(2,1)S(1)}, bf16[128,1408]{1,0:T(8,128)(2,1)S(1)}, u32[]{:S(2)}, u32[]{:S(2)}) collective-permute-start(bf16[128,1408]{1,0:T(8,128)(2,1)S(1)} %get-tuple-element.40.given), channel_id=1, source_target_pairs={{0,1},{1,0},{2,3},{3,2},{4,5},{5,4},{6,7},{7,6},{8,9},{9,8},{10,11... | collective-permute-start | bytes 1081352 | tf_op jit(solution)/shard_map/ppermute | solution.py:205
  19.5 7.8 %collective-permute-start.7 = (bf16[32,1280]{1,0:T(8,128)(2,1)S(1)}, bf16[32,1280]{1,0:T(8,128)(2,1)S(1)}, u32[]{:S(2)}, u32[]{:S(2)}) collective-permute-start(bf16[32,1280]{1,0:T(8,128)(2,1)S(1)} %get-tuple-element.41), channel_id=1, source_target_pairs={{0,8},{4,12},{8,0},{12,4},{1,9},{5,13},{9,1},{13,5},{2,10},{6,14},... | collective-permute-start | bytes 245768 | tf_op jit(solution)/shard_map/ppermute | solution.py:205
  22.6 3.7 %collective-permute-start.10 = (bf16[32,128]{1,0:T(8,128)(2,1)S(1)}, bf16[32,128]{1,0:T(8,128)(2,1)S(1)}, u32[]{:S(2)}, u32[]{:S(2)}) collective-permute-start(bf16[32,128]{1,0:T(8,128)(2,1)S(1)} %get-tuple-element.45.refs_5_), channel_id=1, source_target_pairs={{0,2},{2,0},{1,3},{3,1},{4,6},{6,4},{5,7},{7,5},{8,10},{10,8},{9,1... | collective-permute-start | bytes 24584 | tf_op jit(solution)/shard_map/ppermute | solution.py:205
  24.1 8.9 %collective-permute-start.8 = (bf16[32,1280]{1,0:T(8,128)(2,1)S(1)}, bf16[32,1280]{1,0:T(8,128)(2,1)S(1)}, u32[]{:S(2)}, u32[]{:S(2)}) collective-permute-start(bf16[32,1280]{1,0:T(8,128)(2,1)S(1)} %get-tuple-element.42), channel_id=1, source_target_pairs={{0,12},{2,4},{4,8},{6,0},{8,14},{10,6},{12,10},{14,2},{1,13},{3,5}... | collective-permute-start | bytes 245768 | tf_op jit(solution)/shard_map/ppermute | solution.py:452
  24.5 8.5 %collective-permute-start.9 = (bf16[32,1280]{1,0:T(8,128)(2,1)S(1)}, bf16[32,1280]{1,0:T(8,128)(2,1)S(1)}, u32[]{:S(2)}, u32[]{:S(2)}) collective-permute-start(bf16[32,1280]{1,0:T(8,128)(2,1)S(1)} %get-tuple-element.43), channel_id=1, source_target_pairs={{0,4},{2,12},{4,0},{6,8},{8,6},{10,14},{12,2},{14,10},{1,5},{3,13}... | collective-permute-start | bytes 245768 | tf_op jit(solution)/shard_map/ppermute | solution.py:452
  27.2 5.8 %collective-permute-start.11 = (bf16[32,1280]{1,0:T(8,128)(2,1)S(1)}, bf16[32,1280]{1,0:T(8,128)(2,1)S(1)}, u32[]{:S(2)}, u32[]{:S(2)}) collective-permute-start(bf16[32,1280]{1,0:T(8,128)(2,1)S(1)} %shard_map.87), channel_id=1, source_target_pairs={{0,2},{2,0},{1,3},{3,1},{4,6},{6,4},{5,7},{7,5},{8,10},{10,8},{9,1... | collective-permute-start | bytes 245768 | tf_op jit(solution)/shard_map/ppermute | solution.py:205
  34.7 6.0 %collective-permute-start.13 = (bf16[16,2048]{1,0:T(8,128)(2,1)S(1)}, bf16[16,2048]{1,0:T(8,128)(2,1)S(1)}, u32[]{:S(2)}, u32[]{:S(2)}) collective-permute-start(bf16[16,2048]{1,0:T(8,128)(2,1)S(1)} %get-tuple-element.50), channel_id=1, source_target_pairs={{0,8},{4,12},{8,0},{12,4},{1,9},{5,13},{9,1},{13,5},{2,10},{6,14},... | collective-permute-start | bytes 196616 | tf_op jit(solution)/shard_map/ppermute | solution.py:205
  35.8 6.5 %collective-permute-start.14 = (bf16[16,2048]{1,0:T(8,128)(2,1)S(1)}, bf16[16,2048]{1,0:T(8,128)(2,1)S(1)}, u32[]{:S(2)}, u32[]{:S(2)}) collective-permute-start(bf16[16,2048]{1,0:T(8,128)(2,1)S(1)} %get-tuple-element.51), channel_id=1, source_target_pairs={{0,8},{4,12},{8,0},{12,4},{1,9},{5,13},{9,1},{13,5},{2,10},{6,14},... | collective-permute-start | bytes 196616 | tf_op jit(solution)/shard_map/ppermute | solution.py:205
  37.7 9.6 %collective-permute-start.12 = (bf16[32,2048]{1,0:T(8,128)(2,1)S(1)}, bf16[32,2048]{1,0:T(8,128)(2,1)S(1)}, u32[]{:S(2)}, u32[]{:S(2)}) collective-permute-start(bf16[32,2048]{1,0:T(8,128)(2,1)S(1)} %get-tuple-element.48.attended.refs_0_), channel_id=1, source_target_pairs={{0,4},{4,0},{8,12},{12,8},{1,5},{5,1},{9,13},{13,9},{2,6},{6,2},{1... | collective-permute-start | bytes 393224 | tf_op jit(solution)/shard_map/ppermute | solution.py:205
  40.7 6.6 %collective-permute-start.15 = (bf16[16,2048]{1,0:T(8,128)(2,1)S(1)}, bf16[16,2048]{1,0:T(8,128)(2,1)S(1)}, u32[]{:S(2)}, u32[]{:S(2)}) collective-permute-start(bf16[16,2048]{1,0:T(8,128)(2,1)S(1)} %collective-permute-done.13.refs_2_), channel_id=1, source_target_pairs={{0,4},{4,0},{8,12},{12,8},{1,5},{5,1},{9,13},{13,9},{2,6},{6,2},{1... | collective-permute-start | bytes 196616 | tf_op jit(solution)/shard_map/ppermute | solution.py:205
  42.3 5.0 %collective-permute-start.16 = (bf16[16,2048]{1,0:T(8,128)(2,1)S(1)}, bf16[16,2048]{1,0:T(8,128)(2,1)S(1)}, u32[]{:S(2)}, u32[]{:S(2)}) collective-permute-start(bf16[16,2048]{1,0:T(8,128)(2,1)S(1)} %collective-permute-done.14.refs_3_), channel_id=1, source_target_pairs={{0,4},{4,0},{8,12},{12,8},{1,5},{5,1},{9,13},{13,9},{2,6},{6,2},{1... | collective-permute-start | bytes 196616 | tf_op jit(solution)/shard_map/ppermute | solution.py:205
  48.2 12.8 %copy-start = (bf16[32,4096]{1,0:T(8,128)(2,1)S(1)}, bf16[32,4096]{1,0:T(8,128)(2,1)}, u32[]{:S(2)}) copy-start(bf16[32,4096]{1,0:T(8,128)(2,1)} %hidden.1) | copy-start | bytes 786436
  48.2 1.6 %collective-permute-start.17 = (bf16[128,1024]{1,0:T(8,128)(2,1)S(1)}, bf16[128,1024]{1,0:T(8,128)(2,1)S(1)}, u32[]{:S(2)}, u32[]{:S(2)}) collective-permute-start(bf16[128,1024]{1,0:T(8,128)(2,1)S(1)} %get-tuple-element.54.given), channel_id=1, source_target_pairs={{0,1},{1,0},{2,3},{3,2},{4,5},{5,4},{6,7},{7,6},{8,9},{9,8},{10,11... | collective-permute-start | bytes 786440 | tf_op jit(solution)/shard_map/ppermute | solution.py:205
  49.8 5.9 %collective-permute-start.18 = (bf16[32,1024]{1,0:T(8,128)(2,1)S(1)}, bf16[32,1024]{1,0:T(8,128)(2,1)S(1)}, u32[]{:S(2)}, u32[]{:S(2)}) collective-permute-start(bf16[32,1024]{1,0:T(8,128)(2,1)S(1)} %get-tuple-element.55), channel_id=1, source_target_pairs={{0,8},{4,12},{8,0},{12,4},{1,9},{5,13},{9,1},{13,5},{2,10},{6,14},... | collective-permute-start | bytes 196616 | tf_op jit(solution)/shard_map/ppermute | solution.py:205
  52.0 6.7 %collective-permute-start.19 = (bf16[32,1024]{1,0:T(8,128)(2,1)S(1)}, bf16[32,1024]{1,0:T(8,128)(2,1)S(1)}, u32[]{:S(2)}, u32[]{:S(2)}) collective-permute-start(bf16[32,1024]{1,0:T(8,128)(2,1)S(1)} %get-tuple-element.56), channel_id=1, source_target_pairs={{0,12},{2,4},{4,8},{6,0},{8,14},{10,6},{12,10},{14,2},{1,13},{3,5}... | collective-permute-start | bytes 196616 | tf_op jit(solution)/shard_map/ppermute | solution.py:452
  54.2 5.2 %collective-permute-start.20 = (bf16[32,1024]{1,0:T(8,128)(2,1)S(1)}, bf16[32,1024]{1,0:T(8,128)(2,1)S(1)}, u32[]{:S(2)}, u32[]{:S(2)}) collective-permute-start(bf16[32,1024]{1,0:T(8,128)(2,1)S(1)} %get-tuple-element.57), channel_id=1, source_target_pairs={{0,4},{2,12},{4,0},{6,8},{8,6},{10,14},{12,2},{14,10},{1,5},{3,13}... | collective-permute-start | bytes 196616 | tf_op jit(solution)/shard_map/ppermute | solution.py:452
  55.8 5.2 %collective-permute-start.21 = (bf16[32,1024]{1,0:T(8,128)(2,1)S(1)}, bf16[32,1024]{1,0:T(8,128)(2,1)S(1)}, u32[]{:S(2)}, u32[]{:S(2)}) collective-permute-start(bf16[32,1024]{1,0:T(8,128)(2,1)S(1)} %shard_map.93), channel_id=1, source_target_pairs={{0,2},{2,0},{1,3},{3,1},{4,6},{6,4},{5,7},{7,5},{8,10},{10,8},{9,1... | collective-permute-start | bytes 196616 | tf_op jit(solution)/shard_map/ppermute | solution.py:205
  61.0 1.4 %collective-permute-start.22 = (bf16[32,2048]{1,0:T(8,128)(2,1)S(1)}, bf16[32,2048]{1,0:T(8,128)(2,1)S(1)}, u32[]{:S(2)}, u32[]{:S(2)}) collective-permute-start(bf16[32,2048]{1,0:T(8,128)(2,1)S(1)} %get-tuple-element.60), channel_id=1, source_target_pairs={{0,1},{1,0},{2,3},{3,2},{4,5},{5,4},{6,7},{7,6},{8,9},{9,8},{10,11... | collective-permute-start | bytes 393224 | tf_op jit(solution)/shard_map/ppermute | solution.py:205

commit v22 on v18

--- a/solution.py
+++ b/solution.py
@@ -460,8 +460,8 @@
     blocks = []
     for pair in range(1, pairs):
         blocks += [
+            direct(rest[2 * pair - 1], False, pair),
             direct(rest[2 * pair - 2], True, pair),
-            direct(rest[2 * pair - 1], False, pair),
         ]
     crossing = call(
         choose_kernel,

time: 62.6 us -> 64.7 us (1.034)
  starting transfers between devices: 32 us -> 36.4 us
  waiting for transfers between devices: 13.2 us -> 10.8 us
    ppermute x4, starting transfers between devices: 3.53 us -> 7.88 us  [direct(): return lax.ppermute(value, ('col', 'row'), moves)]
    ppermute x4, waiting for transfers between devices: 2.44 us -> 0.37 us  [direct(): return lax.ppermute(value, ('col', 'row'), moves)]
  transfers between devices with their start and end apart: 23 -> 23, of which waited for: 11 -> 8; matrix products, arithmetic and copies ran while one was open for 0% -> 0% of each run, Pallas kernels for 19% -> 18%
where the time goes in v22:
time: 64.7 us; the launch traced here: 64.5 us
  starting transfers between devices  36.4 us (56%)
  Pallas kernels  16.2 us (25%)
  waiting for transfers between devices  10.8 us (17%)
  local copies, waits for them, and re-layouts  0.9 us (1%)
    ppermute x19, starting transfers between devices, moved(): return lax.ppermute(value, axis, pairs)  28.5 us
    ppermute x19, waiting for transfers between devices, moved(): return lax.ppermute(value, axis, pairs)  10.4 us
    ppermute x4, starting transfers between devices, direct(): return lax.ppermute(value, ('col', 'row'), moves)  7.88 us
    pallas_call x1, Pallas kernels, paired_plan(): call(functools.partial(stage_in_kernel, col_count), [pltpu.VMEM((half, ha...  4.09 us
    pallas_call x1, Pallas kernels, paired_plan(): call(functools.partial(stage_rest_kernel, col_count), [pltpu.VMEM((half,...  3.71 us
    pallas_call x1, Pallas kernels, paired_plan(): call(stage_out_kernel, pltpu.VMEM((half, half_out), jnp.bfloat16), [HBM,...  2.24 us
    pallas_call x2, Pallas kernels, project(): call(functools.partial(kernel, parts), [struct((rows, half + more)), stru...  1.92 us
    pallas_call x1, Pallas kernels, paired_plan(): call(functools.partial(attend_all, len(products), parts), [struct((rows,...  1.71 us
  transfers between devices with their start and end apart: 23, of which 8 were waited for; matrix products, arithmetic and copies ran while one was open for 0% of the time, Pallas kernels for 18%

profile of v22, /device:TPU:0, one launch (start us, length us, event | category | flops | bytes accessed | tf_op | source)
XLA Modules:
  0.0 64.5 jit_solution(14045769331972455525)
XLA Ops:
  0.0 0.9 %fusion = (bf16[16,2048]{1,0:T(8,128)(2,1)S(1)}, bf16[16,2048]{1,0:T(8,128)(2,1)S(1)}) fusion(bf16[32,4096]{1,0:T(8,128)(2,1)} %hidden.1, s32[]{:T(128)S(6)} %add.4, s32[]{:T(128)S(6)} %select_n.3), kind=kLoop, calls=%fused_computation.1 | loop fusion | bytes 262152 | tf_op jit(solution)/shard_map/slice | solution.py:639
  0.9 4.1 %collective-permute-start.2 = (bf16[16,2048]{1,0:T(8,128)(2,1)S(1)}, bf16[16,2048]{1,0:T(8,128)(2,1)S(1)}, u32[]{:S(2)}, u32[]{:S(2)}) collective-permute-start(bf16[16,2048]{1,0:T(8,128)(2,1)S(1)} %get-tuple-element.62.refs_0_), channel_id=1, source_target_pairs={{0,8},{4,12},{8,0},{12,4},{1,9},{5,13},{9,1},{13,5},{2,10},{6,14},... | collective-permute-start | bytes 196616 | tf_op jit(solution)/shard_map/ppermute | solution.py:206
  5.0 0.1 collective-permute-start.3
  5.1 1.8 %collective-permute-start = (bf16[16,2048]{1,0:T(8,128)(2,1)S(1)}, bf16[16,2048]{1,0:T(8,128)(2,1)S(1)}, u32[]{:S(2)}, u32[]{:S(2)}) collective-permute-start(bf16[16,2048]{1,0:T(8,128)(2,1)S(1)} %get-tuple-element.62.refs_0_), channel_id=1, source_target_pairs={{0,4},{4,0},{8,12},{12,8},{1,5},{5,1},{9,13},{13,9},{2,6},{6,2},{1... | collective-permute-start | bytes 196616 | tf_op jit(solution)/shard_map/ppermute | solution.py:206
  6.9 0.2 collective-permute-start.1
  7.1 1.6 %collective-permute-done.2.refs_4_ = bf16[16,2048]{1,0:T(8,128)(2,1)S(1)} collective-permute-done((bf16[16,2048]{1,0:T(8,128)(2,1)S(1)}, bf16[16,2048]{1,0:T(8,128)(2,1)S(1)}, u32[]{:S(2)}, u32[]{:S(2)}) %collective-permute-start.2) | collective-permute-done | bytes 65568 | tf_op jit(solution)/shard_map/ppermute | solution.py:206
  8.7 1.9 %collective-permute-start.4 = (bf16[16,2048]{1,0:T(8,128)(2,1)S(1)}, bf16[16,2048]{1,0:T(8,128)(2,1)S(1)}, u32[]{:S(2)}, u32[]{:S(2)}) collective-permute-start(bf16[16,2048]{1,0:T(8,128)(2,1)S(1)} %collective-permute-done.2.refs_4_), channel_id=1, source_target_pairs={{0,4},{4,0},{8,12},{12,8},{1,5},{5,1},{9,13},{13,9},{2,6},{6,2},{1... | collective-permute-start | bytes 196616 | tf_op jit(solution)/shard_map/ppermute | solution.py:206
  10.6 0.4 collective-permute-done.3.refs_5_
  11.1 1.3 %collective-permute-start.5 = (bf16[16,2048]{1,0:T(8,128)(2,1)S(1)}, bf16[16,2048]{1,0:T(8,128)(2,1)S(1)}, u32[]{:S(2)}, u32[]{:S(2)}) collective-permute-start(bf16[16,2048]{1,0:T(8,128)(2,1)S(1)} %collective-permute-done.3.refs_5_), channel_id=1, source_target_pairs={{0,4},{4,0},{8,12},{12,8},{1,5},{5,1},{9,13},{13,9},{2,6},{6,2},{1... | collective-permute-start | bytes 196616 | tf_op jit(solution)/shard_map/ppermute | solution.py:206
  12.4 4.1 %shard_map.83 = (bf16[2048,1280]{1,0:T(8,128)(2,1)S(1)}, bf16[2048,1280]{1,0:T(8,128)(2,1)S(1)}, bf16[128,128]{1,0:T(8,128)(2,1)S(1)}) custom-call(bf16[4096,2560]{1,0:T(8,128)(2,1)} %weight.4, s32[128]{0:T(128)} %slots.3), custom_call_target="tpu_custom_call" | custom-call | bytes 10485760 | tf_op jit(solution)/shard_map/pallas_call | solution.py:625
  16.5 0.0 collective-permute-done.1.refs_3_
  16.5 1.1 %shard_map.84 = (bf16[128,1408]{1,0:T(8,128)(2,1)S(1)}, bf16[128,2048]{1,0:T(8,128)(2,1)S(1)}) custom-call(bf16[128,128]{1,0:T(8,128)(2,1)S(1)} %get-tuple-element.36.chosen, bf16[16,2048]{1,0:T(8,128)(2,1)S(1)} %get-tuple-element.62.refs_0_, bf16[16,2048]{1,0:T(8,128)(2,1)S(1)} %get-tuple-element.61.refs_1_, ...), custom_call_target="tpu_custom_call" | custom-call | flops 671088640 | bytes 5242880 | tf_op jit(solution)/shard_map/pallas_call | solution.py:392
  17.6 0.0 copy-start.2
  17.6 0.0 copy-start.3
  17.6 0.1 collective-permute-start.6
  17.7 0.9 %shard_map.85.own = f32[128,1280]{1,0:T(8,128)S(1)} custom-call(bf16[128,2048]{1,0:T(8,128)(2,1)S(1)} %get-tuple-element.39.permuted, bf16[2048,1280]{1,0:T(8,128)(2,1)S(1)} %get-tuple-element.37.refs_8_.weight), custom_call_target="tpu_custom_call" | custom-call | flops 671088640 | bytes 5242880 | tf_op jit(solution)/shard_map/pallas_call | solution.py:401
  18.6 0.8 %collective-permute-done.6.received = bf16[128,1408]{1,0:T(8,128)(2,1)S(1)} collective-permute-done((bf16[128,1408]{1,0:T(8,128)(2,1)S(1)}, bf16[128,1408]{1,0:T(8,128)(2,1)S(1)}, u32[]{:S(2)}, u32[]{:S(2)}) %collective-permute-start.6) | collective-permute-done | bytes 360480 | tf_op jit(solution)/shard_map/ppermute | solution.py:206
  19.4 0.1 shard_map.86
  19.5 3.2 %collective-permute-start.7 = (bf16[32,1280]{1,0:T(8,128)(2,1)S(1)}, bf16[32,1280]{1,0:T(8,128)(2,1)S(1)}, u32[]{:S(2)}, u32[]{:S(2)}) collective-permute-start(bf16[32,1280]{1,0:T(8,128)(2,1)S(1)} %get-tuple-element.41), channel_id=1, source_target_pairs={{0,8},{4,12},{8,0},{12,4},{1,9},{5,13},{9,1},{13,5},{2,10},{6,14},... | collective-permute-start | bytes 245768 | tf_op jit(solution)/shard_map/ppermute | solution.py:206
  22.6 1.5 %collective-permute-start.10 = (bf16[32,128]{1,0:T(8,128)(2,1)S(1)}, bf16[32,128]{1,0:T(8,128)(2,1)S(1)}, u32[]{:S(2)}, u32[]{:S(2)}) collective-permute-start(bf16[32,128]{1,0:T(8,128)(2,1)S(1)} %get-tuple-element.45.refs_5_), channel_id=1, source_target_pairs={{0,2},{2,0},{1,3},{3,1},{4,6},{6,4},{5,7},{7,5},{8,10},{10,8},{9,1... | collective-permute-start | bytes 24584 | tf_op jit(solution)/shard_map/ppermute | solution.py:206
  24.1 0.7 %collective-permute-start.8 = (bf16[32,1280]{1,0:T(8,128)(2,1)S(1)}, bf16[32,1280]{1,0:T(8,128)(2,1)S(1)}, u32[]{:S(2)}, u32[]{:S(2)}) collective-permute-start(bf16[32,1280]{1,0:T(8,128)(2,1)S(1)} %get-tuple-element.42), channel_id=1, source_target_pairs={{0,4},{2,12},{4,0},{6,8},{8,6},{10,14},{12,2},{14,10},{1,5},{3,13}... | collective-permute-start | bytes 245768 | tf_op jit(solution)/shard_map/ppermute | solution.py:453
  24.8 3.1 %collective-permute-start.9 = (bf16[32,1280]{1,0:T(8,128)(2,1)S(1)}, bf16[32,1280]{1,0:T(8,128)(2,1)S(1)}, u32[]{:S(2)}, u32[]{:S(2)}) collective-permute-start(bf16[32,1280]{1,0:T(8,128)(2,1)S(1)} %get-tuple-element.43), channel_id=1, source_target_pairs={{0,12},{2,4},{4,8},{6,0},{8,14},{10,6},{12,10},{14,2},{1,13},{3,5}... | collective-permute-start | bytes 245768 | tf_op jit(solution)/shard_map/ppermute | solution.py:453
  28.0 1.0 %collective-permute-start.11 = (bf16[32,1280]{1,0:T(8,128)(2,1)S(1)}, bf16[32,1280]{1,0:T(8,128)(2,1)S(1)}, u32[]{:S(2)}, u32[]{:S(2)}) collective-permute-start(bf16[32,1280]{1,0:T(8,128)(2,1)S(1)} %shard_map.87), channel_id=1, source_target_pairs={{0,2},{2,0},{1,3},{3,1},{4,6},{6,4},{5,7},{7,5},{8,10},{10,8},{9,1... | collective-permute-start | bytes 245768 | tf_op jit(solution)/shard_map/ppermute | solution.py:206
  29.0 3.7 %shard_map.82 = (bf16[2048,1024]{1,0:T(8,128)(2,1)S(1)}, bf16[32,64,256]{2,1,0:T(8,128)(2,1)S(1)}, bf16[32,64,256]{2,1,0:T(8,128)(2,1)S(1)}, f32[32,128]{1,0:T(8...) custom-call(s32[32]{0:T(128)S(1)} %copy-done.3, bf16[4096,2048]{1,0:T(8,128)(2,1)} %weight.5, ...), custom_call_target="tpu_custom_call" | custom-call | bytes 6291456 | tf_op jit(solution)/shard_map/pallas_call | solution.py:642
  32.7 1.7 %shard_map.88 = (bf16[32,2048]{1,0:T(8,128)(2,1)S(1)}, bf16[16,2048]{1,0:T(8,128)(2,1)S(1)}, bf16[16,2048]{1,0:T(8,128)(2,1)S(1)}) custom-call(f32[32,128]{1,0:T(8,128)S(1)} %get-tuple-element.33.cosine, f32[32,128]{1,0:T(8,128)S(1)} %get-tuple-element.34.sine, s32[32,128]{1,0:T(8,128)S(1)} %get-tuple-element.35.lengths, ...), custom_call_target="tpu_custom_call" | custom-call | flops 16777216 | tf_op jit(solution)/shard_map/pallas_call | solution.py:658
  34.4 1.4 %collective-permute-start.13 = (bf16[16,2048]{1,0:T(8,128)(2,1)S(1)}, bf16[16,2048]{1,0:T(8,128)(2,1)S(1)}, u32[]{:S(2)}, u32[]{:S(2)}) collective-permute-start(bf16[16,2048]{1,0:T(8,128)(2,1)S(1)} %get-tuple-element.50), channel_id=1, source_target_pairs={{0,8},{4,12},{8,0},{12,4},{1,9},{5,13},{9,1},{13,5},{2,10},{6,14},... | collective-permute-start | bytes 196616 | tf_op jit(solution)/shard_map/ppermute | solution.py:206
  35.8 1.6 %collective-permute-start.14 = (bf16[16,2048]{1,0:T(8,128)(2,1)S(1)}, bf16[16,2048]{1,0:T(8,128)(2,1)S(1)}, u32[]{:S(2)}, u32[]{:S(2)}) collective-permute-start(bf16[16,2048]{1,0:T(8,128)(2,1)S(1)} %get-tuple-element.51), channel_id=1, source_target_pairs={{0,8},{4,12},{8,0},{12,4},{1,9},{5,13},{9,1},{13,5},{2,10},{6,14},... | collective-permute-start | bytes 196616 | tf_op jit(solution)/shard_map/ppermute | solution.py:206
  37.4 2.8 %collective-permute-start.12 = (bf16[32,2048]{1,0:T(8,128)(2,1)S(1)}, bf16[32,2048]{1,0:T(8,128)(2,1)S(1)}, u32[]{:S(2)}, u32[]{:S(2)}) collective-permute-start(bf16[32,2048]{1,0:T(8,128)(2,1)S(1)} %get-tuple-element.48.attended.refs_0_), channel_id=1, source_target_pairs={{0,4},{4,0},{8,12},{12,8},{1,5},{5,1},{9,13},{13,9},{2,6},{6,2},{1... | collective-permute-start | bytes 393224 | tf_op jit(solution)/shard_map/ppermute | solution.py:206
  40.2 0.0 collective-permute-done.13.refs_2_
  40.2 2.8 %collective-permute-start.15 = (bf16[16,2048]{1,0:T(8,128)(2,1)S(1)}, bf16[16,2048]{1,0:T(8,128)(2,1)S(1)}, u32[]{:S(2)}, u32[]{:S(2)}) collective-permute-start(bf16[16,2048]{1,0:T(8,128)(2,1)S(1)} %collective-permute-done.13.refs_2_), channel_id=1, source_target_pairs={{0,4},{4,0},{8,12},{12,8},{1,5},{5,1},{9,13},{13,9},{2,6},{6,2},{1... | collective-permute-start | bytes 196616 | tf_op jit(solution)/shard_map/ppermute | solution.py:206
  43.1 2.4 %collective-permute-start.16 = (bf16[16,2048]{1,0:T(8,128)(2,1)S(1)}, bf16[16,2048]{1,0:T(8,128)(2,1)S(1)}, u32[]{:S(2)}, u32[]{:S(2)}) collective-permute-start(bf16[16,2048]{1,0:T(8,128)(2,1)S(1)} %collective-permute-done.14.refs_3_), channel_id=1, source_target_pairs={{0,4},{4,0},{8,12},{12,8},{1,5},{5,1},{9,13},{13,9},{2,6},{6,2},{1... | collective-permute-start | bytes 196616 | tf_op jit(solution)/shard_map/ppermute | solution.py:206
  45.4 2.2 %shard_map.89.refs_6_.weight = bf16[2048,1024]{1,0:T(8,128)(2,1)S(1)} custom-call(bf16[4096,2048]{1,0:T(8,128)(2,1)} %weight.5, bf16[32,2048]{1,0:T(8,128)(2,1)S(1)} %get-tuple-element.48.attended.refs_0_), custom_call_target="tpu_custom_call" | custom-call | bytes 4194304 | tf_op jit(solution)/shard_map/pallas_call | solution.py:675
  47.7 0.8 %shard_map.90 = (bf16[128,1024]{1,0:T(8,128)(2,1)S(1)}, bf16[128,2048]{1,0:T(8,128)(2,1)S(1)}) custom-call(bf16[128,128]{1,0:T(8,128)(2,1)S(1)} %get-tuple-element.49.chosen, bf16[32,2048]{1,0:T(8,128)(2,1)S(1)} %get-tuple-element.48.attended.refs_0_, bf16[32,2048]{1,0:T(8,128)(2,1)S(1)} %collective-permute-done.12.refs_1_, ...), custom_call_target="tpu_custom_call" | custom-call | flops 536870912 | bytes 4194304 | tf_op jit(solution)/shard_map/pallas_call | solution.py:392
  48.6 0.0 copy-start
  48.6 0.1 collective-permute-start.17
  48.7 0.7 %shard_map.91.own = f32[128,1024]{1,0:T(8,128)S(1)} custom-call(bf16[128,2048]{1,0:T(8,128)(2,1)S(1)} %get-tuple-element.53.permuted, bf16[2048,1024]{1,0:T(8,128)(2,1)S(1)} %shard_map.89.refs_6_.weight), custom_call_target="tpu_custom_call" | custom-call | flops 536870912 | bytes 4194304 | tf_op jit(solution)/shard_map/pallas_call | solution.py:401
  49.4 0.8 %collective-permute-done.17.received = bf16[128,1024]{1,0:T(8,128)(2,1)S(1)} collective-permute-done((bf16[128,1024]{1,0:T(8,128)(2,1)S(1)}, bf16[128,1024]{1,0:T(8,128)(2,1)S(1)}, u32[]{:S(2)}, u32[]{:S(2)}) %collective-permute-start.17) | collective-permute-done | bytes 262176 | tf_op jit(solution)/shard_map/ppermute | solution.py:206
  50.2 2.1 %collective-permute-start.18 = (bf16[32,1024]{1,0:T(8,128)(2,1)S(1)}, bf16[32,1024]{1,0:T(8,128)(2,1)S(1)}, u32[]{:S(2)}, u32[]{:S(2)}) collective-permute-start(bf16[32,1024]{1,0:T(8,128)(2,1)S(1)} %get-tuple-element.55), channel_id=1, source_target_pairs={{0,8},{4,12},{8,0},{12,4},{1,9},{5,13},{9,1},{13,5},{2,10},{6,14},... | collective-permute-start | bytes 196616 | tf_op jit(solution)/shard_map/ppermute | solution.py:206
  52.3 0.9 %collective-permute-start.19 = (bf16[32,1024]{1,0:T(8,128)(2,1)S(1)}, bf16[32,1024]{1,0:T(8,128)(2,1)S(1)}, u32[]{:S(2)}, u32[]{:S(2)}) collective-permute-start(bf16[32,1024]{1,0:T(8,128)(2,1)S(1)} %get-tuple-element.56), channel_id=1, source_target_pairs={{0,4},{2,12},{4,0},{6,8},{8,6},{10,14},{12,2},{14,10},{1,5},{3,13}... | collective-permute-start | bytes 196616 | tf_op jit(solution)/shard_map/ppermute | solution.py:453
  53.3 3.2 %collective-permute-start.20 = (bf16[32,1024]{1,0:T(8,128)(2,1)S(1)}, bf16[32,1024]{1,0:T(8,128)(2,1)S(1)}, u32[]{:S(2)}, u32[]{:S(2)}) collective-permute-start(bf16[32,1024]{1,0:T(8,128)(2,1)S(1)} %get-tuple-element.57), channel_id=1, source_target_pairs={{0,12},{2,4},{4,8},{6,0},{8,14},{10,6},{12,10},{14,2},{1,13},{3,5}... | collective-permute-start | bytes 196616 | tf_op jit(solution)/shard_map/ppermute | solution.py:453
  56.4 1.5 %collective-permute-done.18.passed.refs_0_ = bf16[32,1024]{1,0:T(8,128)(2,1)S(1)} collective-permute-done((bf16[32,1024]{1,0:T(8,128)(2,1)S(1)}, bf16[32,1024]{1,0:T(8,128)(2,1)S(1)}, u32[]{:S(2)}, u32[]{:S(2)}) %collective-permute-start.18) | collective-permute-done | bytes 65568 | tf_op jit(solution)/shard_map/ppermute | solution.py:206
  58.0 0.1 collective-permute-start.21
  58.1 0.4 collective-permute-done.20.refs_2_
  58.4 3.9 %collective-permute-done.21.refs_4_ = bf16[32,1024]{1,0:T(8,128)(2,1)S(1)} collective-permute-done((bf16[32,1024]{1,0:T(8,128)(2,1)S(1)}, bf16[32,1024]{1,0:T(8,128)(2,1)S(1)}, u32[]{:S(2)}, u32[]{:S(2)}) %collective-permute-start.21) | collective-permute-done | bytes 65568 | tf_op jit(solution)/shard_map/ppermute | solution.py:206
  62.3 0.1 shard_map.94
  62.4 0.1 collective-permute-start.22
  62.5 1.3 %collective-permute-done.22.received = bf16[32,2048]{1,0:T(8,128)(2,1)S(1)} collective-permute-done((bf16[32,2048]{1,0:T(8,128)(2,1)S(1)}, bf16[32,2048]{1,0:T(8,128)(2,1)S(1)}, u32[]{:S(2)}, u32[]{:S(2)}) %collective-permute-start.22) | collective-permute-done | bytes 131104 | tf_op jit(solution)/shard_map/ppermute | solution.py:206
  63.8 0.7 %shard_map.95 = bf16[1,32,4096]{2,1,0:T(8,128)(2,1)} custom-call(bf16[32,2048]{1,0:T(8,128)(2,1)S(1)} %get-tuple-element.59.keep, bf16[32,2048]{1,0:T(8,128)(2,1)S(1)} %collective-permute-done.22.received), custom_call_target="tpu_custom_call" | custom-call | bytes 524288 | tf_op jit(solution)/shard_map/pallas_call | solution.py:696
  (21 shorter events, 0.1 us)
Async XLA Ops:
  0.9 7.9 %collective-permute-start.2 = (bf16[16,2048]{1,0:T(8,128)(2,1)S(1)}, bf16[16,2048]{1,0:T(8,128)(2,1)S(1)}, u32[]{:S(2)}, u32[]{:S(2)}) collective-permute-start(bf16[16,2048]{1,0:T(8,128)(2,1)S(1)} %get-tuple-element.62.refs_0_), channel_id=1, source_target_pairs={{0,8},{4,12},{8,0},{12,4},{1,9},{5,13},{9,1},{13,5},{2,10},{6,14},... | collective-permute-start | bytes 196616 | tf_op jit(solution)/shard_map/ppermute | solution.py:206
  5.0 11.5 %copy-start.1 = (bf16[4096]{0:T(1024)(128)(2,1)S(1)}, bf16[4096]{0:T(1024)(128)(2,1)}, u32[]{:S(2)}) copy-start(bf16[4096]{0:T(1024)(128)(2,1)} %param.9) | copy-start | bytes 24580
  5.0 6.1 %collective-permute-start.3 = (bf16[16,2048]{1,0:T(8,128)(2,1)S(1)}, bf16[16,2048]{1,0:T(8,128)(2,1)S(1)}, u32[]{:S(2)}, u32[]{:S(2)}) collective-permute-start(bf16[16,2048]{1,0:T(8,128)(2,1)S(1)} %get-tuple-element.61.refs_1_), channel_id=1, source_target_pairs={{0,8},{4,12},{8,0},{12,4},{1,9},{5,13},{9,1},{13,5},{2,10},{6,14},... | collective-permute-start | bytes 196616 | tf_op jit(solution)/shard_map/ppermute | solution.py:206
  5.1 11.4 %collective-permute-start = (bf16[16,2048]{1,0:T(8,128)(2,1)S(1)}, bf16[16,2048]{1,0:T(8,128)(2,1)S(1)}, u32[]{:S(2)}, u32[]{:S(2)}) collective-permute-start(bf16[16,2048]{1,0:T(8,128)(2,1)S(1)} %get-tuple-element.62.refs_0_), channel_id=1, source_target_pairs={{0,4},{4,0},{8,12},{12,8},{1,5},{5,1},{9,13},{13,9},{2,6},{6,2},{1... | collective-permute-start | bytes 196616 | tf_op jit(solution)/shard_map/ppermute | solution.py:206
  6.9 9.6 %collective-permute-start.1 = (bf16[16,2048]{1,0:T(8,128)(2,1)S(1)}, bf16[16,2048]{1,0:T(8,128)(2,1)S(1)}, u32[]{:S(2)}, u32[]{:S(2)}) collective-permute-start(bf16[16,2048]{1,0:T(8,128)(2,1)S(1)} %get-tuple-element.61.refs_1_), channel_id=1, source_target_pairs={{0,4},{4,0},{8,12},{12,8},{1,5},{5,1},{9,13},{13,9},{2,6},{6,2},{1... | collective-permute-start | bytes 196616 | tf_op jit(solution)/shard_map/ppermute | solution.py:206
  8.7 7.8 %collective-permute-start.4 = (bf16[16,2048]{1,0:T(8,128)(2,1)S(1)}, bf16[16,2048]{1,0:T(8,128)(2,1)S(1)}, u32[]{:S(2)}, u32[]{:S(2)}) collective-permute-start(bf16[16,2048]{1,0:T(8,128)(2,1)S(1)} %collective-permute-done.2.refs_4_), channel_id=1, source_target_pairs={{0,4},{4,0},{8,12},{12,8},{1,5},{5,1},{9,13},{13,9},{2,6},{6,2},{1... | collective-permute-start | bytes 196616 | tf_op jit(solution)/shard_map/ppermute | solution.py:206
  11.1 5.4 %collective-permute-start.5 = (bf16[16,2048]{1,0:T(8,128)(2,1)S(1)}, bf16[16,2048]{1,0:T(8,128)(2,1)S(1)}, u32[]{:S(2)}, u32[]{:S(2)}) collective-permute-start(bf16[16,2048]{1,0:T(8,128)(2,1)S(1)} %collective-permute-done.3.refs_5_), channel_id=1, source_target_pairs={{0,4},{4,0},{8,12},{12,8},{1,5},{5,1},{9,13},{13,9},{2,6},{6,2},{1... | collective-permute-start | bytes 196616 | tf_op jit(solution)/shard_map/ppermute | solution.py:206
  17.6 11.4 %copy-start.2 = (s32[128]{0:T(128)S(1)}, s32[128]{0:T(128)}, u32[]{:S(2)}) copy-start(s32[128]{0:T(128)} %slots.3) | copy-start | bytes 1540
  17.6 11.3 %copy-start.3 = (s32[32]{0:T(128)S(1)}, s32[32]{0:T(128)}, u32[]{:S(2)}) copy-start(s32[32]{0:T(128)} %lengths.1) | copy-start | bytes 388
  17.6 1.7 %collective-permute-start.6 = (bf16[128,1408]{1,0:T(8,128)(2,1)S(1)}, bf16[128,1408]{1,0:T(8,128)(2,1)S(1)}, u32[]{:S(2)}, u32[]{:S(2)}) collective-permute-start(bf16[128,1408]{1,0:T(8,128)(2,1)S(1)} %get-tuple-element.40.given), channel_id=1, source_target_pairs={{0,1},{1,0},{2,3},{3,2},{4,5},{5,4},{6,7},{7,6},{8,9},{9,8},{10,11... | collective-permute-start | bytes 1081352 | tf_op jit(solution)/shard_map/ppermute | solution.py:206
  19.5 8.5 %collective-permute-start.7 = (bf16[32,1280]{1,0:T(8,128)(2,1)S(1)}, bf16[32,1280]{1,0:T(8,128)(2,1)S(1)}, u32[]{:S(2)}, u32[]{:S(2)}) collective-permute-start(bf16[32,1280]{1,0:T(8,128)(2,1)S(1)} %get-tuple-element.41), channel_id=1, source_target_pairs={{0,8},{4,12},{8,0},{12,4},{1,9},{5,13},{9,1},{13,5},{2,10},{6,14},... | collective-permute-start | bytes 245768 | tf_op jit(solution)/shard_map/ppermute | solution.py:206
  22.6 5.3 %collective-permute-start.10 = (bf16[32,128]{1,0:T(8,128)(2,1)S(1)}, bf16[32,128]{1,0:T(8,128)(2,1)S(1)}, u32[]{:S(2)}, u32[]{:S(2)}) collective-permute-start(bf16[32,128]{1,0:T(8,128)(2,1)S(1)} %get-tuple-element.45.refs_5_), channel_id=1, source_target_pairs={{0,2},{2,0},{1,3},{3,1},{4,6},{6,4},{5,7},{7,5},{8,10},{10,8},{9,1... | collective-permute-start | bytes 24584 | tf_op jit(solution)/shard_map/ppermute | solution.py:206
  24.1 8.6 %collective-permute-start.8 = (bf16[32,1280]{1,0:T(8,128)(2,1)S(1)}, bf16[32,1280]{1,0:T(8,128)(2,1)S(1)}, u32[]{:S(2)}, u32[]{:S(2)}) collective-permute-start(bf16[32,1280]{1,0:T(8,128)(2,1)S(1)} %get-tuple-element.42), channel_id=1, source_target_pairs={{0,4},{2,12},{4,0},{6,8},{8,6},{10,14},{12,2},{14,10},{1,5},{3,13}... | collective-permute-start | bytes 245768 | tf_op jit(solution)/shard_map/ppermute | solution.py:453
  24.8 7.9 %collective-permute-start.9 = (bf16[32,1280]{1,0:T(8,128)(2,1)S(1)}, bf16[32,1280]{1,0:T(8,128)(2,1)S(1)}, u32[]{:S(2)}, u32[]{:S(2)}) collective-permute-start(bf16[32,1280]{1,0:T(8,128)(2,1)S(1)} %get-tuple-element.43), channel_id=1, source_target_pairs={{0,12},{2,4},{4,8},{6,0},{8,14},{10,6},{12,10},{14,2},{1,13},{3,5}... | collective-permute-start | bytes 245768 | tf_op jit(solution)/shard_map/ppermute | solution.py:453
  28.0 4.8 %collective-permute-start.11 = (bf16[32,1280]{1,0:T(8,128)(2,1)S(1)}, bf16[32,1280]{1,0:T(8,128)(2,1)S(1)}, u32[]{:S(2)}, u32[]{:S(2)}) collective-permute-start(bf16[32,1280]{1,0:T(8,128)(2,1)S(1)} %shard_map.87), channel_id=1, source_target_pairs={{0,2},{2,0},{1,3},{3,1},{4,6},{6,4},{5,7},{7,5},{8,10},{10,8},{9,1... | collective-permute-start | bytes 245768 | tf_op jit(solution)/shard_map/ppermute | solution.py:206
  34.4 5.8 %collective-permute-start.13 = (bf16[16,2048]{1,0:T(8,128)(2,1)S(1)}, bf16[16,2048]{1,0:T(8,128)(2,1)S(1)}, u32[]{:S(2)}, u32[]{:S(2)}) collective-permute-start(bf16[16,2048]{1,0:T(8,128)(2,1)S(1)} %get-tuple-element.50), channel_id=1, source_target_pairs={{0,8},{4,12},{8,0},{12,4},{1,9},{5,13},{9,1},{13,5},{2,10},{6,14},... | collective-permute-start | bytes 196616 | tf_op jit(solution)/shard_map/ppermute | solution.py:206
  35.8 7.3 %collective-permute-start.14 = (bf16[16,2048]{1,0:T(8,128)(2,1)S(1)}, bf16[16,2048]{1,0:T(8,128)(2,1)S(1)}, u32[]{:S(2)}, u32[]{:S(2)}) collective-permute-start(bf16[16,2048]{1,0:T(8,128)(2,1)S(1)} %get-tuple-element.51), channel_id=1, source_target_pairs={{0,8},{4,12},{8,0},{12,4},{1,9},{5,13},{9,1},{13,5},{2,10},{6,14},... | collective-permute-start | bytes 196616 | tf_op jit(solution)/shard_map/ppermute | solution.py:206
  37.4 10.3 %collective-permute-start.12 = (bf16[32,2048]{1,0:T(8,128)(2,1)S(1)}, bf16[32,2048]{1,0:T(8,128)(2,1)S(1)}, u32[]{:S(2)}, u32[]{:S(2)}) collective-permute-start(bf16[32,2048]{1,0:T(8,128)(2,1)S(1)} %get-tuple-element.48.attended.refs_0_), channel_id=1, source_target_pairs={{0,4},{4,0},{8,12},{12,8},{1,5},{5,1},{9,13},{13,9},{2,6},{6,2},{1... | collective-permute-start | bytes 393224 | tf_op jit(solution)/shard_map/ppermute | solution.py:206
  40.2 7.5 %collective-permute-start.15 = (bf16[16,2048]{1,0:T(8,128)(2,1)S(1)}, bf16[16,2048]{1,0:T(8,128)(2,1)S(1)}, u32[]{:S(2)}, u32[]{:S(2)}) collective-permute-start(bf16[16,2048]{1,0:T(8,128)(2,1)S(1)} %collective-permute-done.13.refs_2_), channel_id=1, source_target_pairs={{0,4},{4,0},{8,12},{12,8},{1,5},{5,1},{9,13},{13,9},{2,6},{6,2},{1... | collective-permute-start | bytes 196616 | tf_op jit(solution)/shard_map/ppermute | solution.py:206
  43.1 4.6 %collective-permute-start.16 = (bf16[16,2048]{1,0:T(8,128)(2,1)S(1)}, bf16[16,2048]{1,0:T(8,128)(2,1)S(1)}, u32[]{:S(2)}, u32[]{:S(2)}) collective-permute-start(bf16[16,2048]{1,0:T(8,128)(2,1)S(1)} %collective-permute-done.14.refs_3_), channel_id=1, source_target_pairs={{0,4},{4,0},{8,12},{12,8},{1,5},{5,1},{9,13},{13,9},{2,6},{6,2},{1... | collective-permute-start | bytes 196616 | tf_op jit(solution)/shard_map/ppermute | solution.py:206
  48.6 13.7 %copy-start = (bf16[32,4096]{1,0:T(8,128)(2,1)S(1)}, bf16[32,4096]{1,0:T(8,128)(2,1)}, u32[]{:S(2)}) copy-start(bf16[32,4096]{1,0:T(8,128)(2,1)} %hidden.1) | copy-start | bytes 786436
  48.6 1.6 %collective-permute-start.17 = (bf16[128,1024]{1,0:T(8,128)(2,1)S(1)}, bf16[128,1024]{1,0:T(8,128)(2,1)S(1)}, u32[]{:S(2)}, u32[]{:S(2)}) collective-permute-start(bf16[128,1024]{1,0:T(8,128)(2,1)S(1)} %get-tuple-element.54.given), channel_id=1, source_target_pairs={{0,1},{1,0},{2,3},{3,2},{4,5},{5,4},{6,7},{7,6},{8,9},{9,8},{10,11... | collective-permute-start | bytes 786440 | tf_op jit(solution)/shard_map/ppermute | solution.py:206
  50.2 7.7 %collective-permute-start.18 = (bf16[32,1024]{1,0:T(8,128)(2,1)S(1)}, bf16[32,1024]{1,0:T(8,128)(2,1)S(1)}, u32[]{:S(2)}, u32[]{:S(2)}) collective-permute-start(bf16[32,1024]{1,0:T(8,128)(2,1)S(1)} %get-tuple-element.55), channel_id=1, source_target_pairs={{0,8},{4,12},{8,0},{12,4},{1,9},{5,13},{9,1},{13,5},{2,10},{6,14},... | collective-permute-start | bytes 196616 | tf_op jit(solution)/shard_map/ppermute | solution.py:206
  52.3 5.7 %collective-permute-start.19 = (bf16[32,1024]{1,0:T(8,128)(2,1)S(1)}, bf16[32,1024]{1,0:T(8,128)(2,1)S(1)}, u32[]{:S(2)}, u32[]{:S(2)}) collective-permute-start(bf16[32,1024]{1,0:T(8,128)(2,1)S(1)} %get-tuple-element.56), channel_id=1, source_target_pairs={{0,4},{2,12},{4,0},{6,8},{8,6},{10,14},{12,2},{14,10},{1,5},{3,13}... | collective-permute-start | bytes 196616 | tf_op jit(solution)/shard_map/ppermute | solution.py:453
  53.3 5.2 %collective-permute-start.20 = (bf16[32,1024]{1,0:T(8,128)(2,1)S(1)}, bf16[32,1024]{1,0:T(8,128)(2,1)S(1)}, u32[]{:S(2)}, u32[]{:S(2)}) collective-permute-start(bf16[32,1024]{1,0:T(8,128)(2,1)S(1)} %get-tuple-element.57), channel_id=1, source_target_pairs={{0,12},{2,4},{4,8},{6,0},{8,14},{10,6},{12,10},{14,2},{1,13},{3,5}... | collective-permute-start | bytes 196616 | tf_op jit(solution)/shard_map/ppermute | solution.py:453
  58.0 4.3 %collective-permute-start.21 = (bf16[32,1024]{1,0:T(8,128)(2,1)S(1)}, bf16[32,1024]{1,0:T(8,128)(2,1)S(1)}, u32[]{:S(2)}, u32[]{:S(2)}) collective-permute-start(bf16[32,1024]{1,0:T(8,128)(2,1)S(1)} %shard_map.93), channel_id=1, source_target_pairs={{0,2},{2,0},{1,3},{3,1},{4,6},{6,4},{5,7},{7,5},{8,10},{10,8},{9,1... | collective-permute-start | bytes 196616 | tf_op jit(solution)/shard_map/ppermute | solution.py:206
  62.4 1.4 %collective-permute-start.22 = (bf16[32,2048]{1,0:T(8,128)(2,1)S(1)}, bf16[32,2048]{1,0:T(8,128)(2,1)S(1)}, u32[]{:S(2)}, u32[]{:S(2)}) collective-permute-start(bf16[32,2048]{1,0:T(8,128)(2,1)S(1)} %get-tuple-element.60), channel_id=1, source_target_pairs={{0,1},{1,0},{2,3},{3,2},{4,5},{5,4},{6,7},{7,6},{8,9},{9,8},{10,11... | collective-permute-start | bytes 393224 | tf_op jit(solution)/shard_map/ppermute | solution.py:206

commit v23 on v18

--- a/solution.py
+++ b/solution.py
@@ -682,7 +682,7 @@
         [pltpu.SemaphoreType.DMA((pairs,))],
     )(in_hbm(out_weight), attended)
     products, _ = project(
-        out_kernel, chosen_out, gathered(attended_parts, "col", attended), [], [give_out, own_out], 0
+        out_kernel, chosen_out, gathered(attended_parts, "col"), [], [give_out, own_out], 0
     )
     products = spread(products, [])
     keep, send = call(

time: 62.6 us -> 62.6 us (level)
  waiting for transfers between devices: 13.2 us -> 12.2 us
  starting transfers between devices: 32 us -> 32.9 us
    ppermute x19 -> x20, starting transfers between devices: 28.4 us -> 29.4 us  [moved(): return lax.ppermute(value, axis, pairs)]
    ppermute x19 -> x20, waiting for transfers between devices: 10.7 us -> 9.85 us  [moved(): return lax.ppermute(value, axis, pairs)]
  transfers between devices with their start and end apart: 23 -> 24, of which waited for: 11 -> 11; matrix products, arithmetic and copies ran while one was open for 0% -> 0% of each run, Pallas kernels for 19% -> 19%
where the time goes in v23:
time: 62.6 us; the launch traced here: 62.5 us
  starting transfers between devices  32.9 us (53%)
  Pallas kernels  16.2 us (26%)
  waiting for transfers between devices  12.2 us (19%)
  local copies, waits for them, and re-layouts  0.9 us (1%)
    ppermute x20, starting transfers between devices, moved(): return lax.ppermute(value, axis, pairs)  29.4 us
    ppermute x20, waiting for transfers between devices, moved(): return lax.ppermute(value, axis, pairs)  9.85 us
    pallas_call x1, Pallas kernels, paired_plan(): call(functools.partial(stage_in_kernel, col_count), [pltpu.VMEM((half, ha...  4.09 us
    pallas_call x1, Pallas kernels, paired_plan(): call(functools.partial(stage_rest_kernel, col_count), [pltpu.VMEM((half,...  3.71 us
    ppermute x4, starting transfers between devices, direct(): return lax.ppermute(value, ('col', 'row'), moves)  3.53 us
    ppermute x4, waiting for transfers between devices, direct(): return lax.ppermute(value, ('col', 'row'), moves)  2.4 us
    pallas_call x1, Pallas kernels, paired_plan(): call(stage_out_kernel, pltpu.VMEM((half, half_out), jnp.bfloat16), [HBM,...  2.24 us
    pallas_call x2, Pallas kernels, project(): call(functools.partial(kernel, parts), [struct((rows, half + more)), stru...  1.91 us
  transfers between devices with their start and end apart: 24, of which 11 were waited for; matrix products, arithmetic and copies ran while one was open for 0% of the time, Pallas kernels for 19%

profile of v23, /device:TPU:0, one launch (start us, length us, event | category | flops | bytes accessed | tf_op | source)
XLA Modules:
  0.0 62.5 jit_solution(11737494323617347617)
XLA Ops:
  0.0 0.9 %fusion = (bf16[16,2048]{1,0:T(8,128)(2,1)S(1)}, bf16[16,2048]{1,0:T(8,128)(2,1)S(1)}) fusion(bf16[32,4096]{1,0:T(8,128)(2,1)} %hidden.1, s32[]{:T(128)S(6)} %add.4, s32[]{:T(128)S(6)} %select_n.3), kind=kLoop, calls=%fused_computation.1 | loop fusion | bytes 262152 | tf_op jit(solution)/shard_map/slice | solution.py:639
  0.9 4.1 %collective-permute-start.2 = (bf16[16,2048]{1,0:T(8,128)(2,1)S(1)}, bf16[16,2048]{1,0:T(8,128)(2,1)S(1)}, u32[]{:S(2)}, u32[]{:S(2)}) collective-permute-start(bf16[16,2048]{1,0:T(8,128)(2,1)S(1)} %get-tuple-element.62.refs_0_), channel_id=1, source_target_pairs={{0,8},{4,12},{8,0},{12,4},{1,9},{5,13},{9,1},{13,5},{2,10},{6,14},... | collective-permute-start | bytes 196616 | tf_op jit(solution)/shard_map/ppermute | solution.py:206
  5.0 0.1 collective-permute-start.3
  5.1 1.8 %collective-permute-start = (bf16[16,2048]{1,0:T(8,128)(2,1)S(1)}, bf16[16,2048]{1,0:T(8,128)(2,1)S(1)}, u32[]{:S(2)}, u32[]{:S(2)}) collective-permute-start(bf16[16,2048]{1,0:T(8,128)(2,1)S(1)} %get-tuple-element.62.refs_0_), channel_id=1, source_target_pairs={{0,4},{4,0},{8,12},{12,8},{1,5},{5,1},{9,13},{13,9},{2,6},{6,2},{1... | collective-permute-start | bytes 196616 | tf_op jit(solution)/shard_map/ppermute | solution.py:206
  6.9 0.2 collective-permute-start.1
  7.1 1.6 %collective-permute-done.2.refs_4_ = bf16[16,2048]{1,0:T(8,128)(2,1)S(1)} collective-permute-done((bf16[16,2048]{1,0:T(8,128)(2,1)S(1)}, bf16[16,2048]{1,0:T(8,128)(2,1)S(1)}, u32[]{:S(2)}, u32[]{:S(2)}) %collective-permute-start.2) | collective-permute-done | bytes 65568 | tf_op jit(solution)/shard_map/ppermute | solution.py:206
  8.7 1.9 %collective-permute-start.4 = (bf16[16,2048]{1,0:T(8,128)(2,1)S(1)}, bf16[16,2048]{1,0:T(8,128)(2,1)S(1)}, u32[]{:S(2)}, u32[]{:S(2)}) collective-permute-start(bf16[16,2048]{1,0:T(8,128)(2,1)S(1)} %collective-permute-done.2.refs_4_), channel_id=1, source_target_pairs={{0,4},{4,0},{8,12},{12,8},{1,5},{5,1},{9,13},{13,9},{2,6},{6,2},{1... | collective-permute-start | bytes 196616 | tf_op jit(solution)/shard_map/ppermute | solution.py:206
  10.6 0.4 collective-permute-done.3.refs_5_
  11.1 1.3 %collective-permute-start.5 = (bf16[16,2048]{1,0:T(8,128)(2,1)S(1)}, bf16[16,2048]{1,0:T(8,128)(2,1)S(1)}, u32[]{:S(2)}, u32[]{:S(2)}) collective-permute-start(bf16[16,2048]{1,0:T(8,128)(2,1)S(1)} %collective-permute-done.3.refs_5_), channel_id=1, source_target_pairs={{0,4},{4,0},{8,12},{12,8},{1,5},{5,1},{9,13},{13,9},{2,6},{6,2},{1... | collective-permute-start | bytes 196616 | tf_op jit(solution)/shard_map/ppermute | solution.py:206
  12.4 4.1 %shard_map.83 = (bf16[2048,1280]{1,0:T(8,128)(2,1)S(1)}, bf16[2048,1280]{1,0:T(8,128)(2,1)S(1)}, bf16[128,128]{1,0:T(8,128)(2,1)S(1)}) custom-call(bf16[4096,2560]{1,0:T(8,128)(2,1)} %weight.4, s32[128]{0:T(128)} %slots.3), custom_call_target="tpu_custom_call" | custom-call | bytes 10485760 | tf_op jit(solution)/shard_map/pallas_call | solution.py:625
  16.5 1.1 %shard_map.84 = (bf16[128,1408]{1,0:T(8,128)(2,1)S(1)}, bf16[128,2048]{1,0:T(8,128)(2,1)S(1)}) custom-call(bf16[128,128]{1,0:T(8,128)(2,1)S(1)} %get-tuple-element.36.chosen, bf16[16,2048]{1,0:T(8,128)(2,1)S(1)} %get-tuple-element.62.refs_0_, bf16[16,2048]{1,0:T(8,128)(2,1)S(1)} %get-tuple-element.61.refs_1_, ...), custom_call_target="tpu_custom_call" | custom-call | flops 671088640 | bytes 5242880 | tf_op jit(solution)/shard_map/pallas_call | solution.py:392
  17.6 0.0 copy-start.3
  17.6 0.1 collective-permute-start.6
  17.7 0.9 %shard_map.85.own = f32[128,1280]{1,0:T(8,128)S(1)} custom-call(bf16[128,2048]{1,0:T(8,128)(2,1)S(1)} %get-tuple-element.39.permuted, bf16[2048,1280]{1,0:T(8,128)(2,1)S(1)} %get-tuple-element.37.refs_8_.weight), custom_call_target="tpu_custom_call" | custom-call | flops 671088640 | bytes 5242880 | tf_op jit(solution)/shard_map/pallas_call | solution.py:401
  18.6 0.8 %collective-permute-done.6.received = bf16[128,1408]{1,0:T(8,128)(2,1)S(1)} collective-permute-done((bf16[128,1408]{1,0:T(8,128)(2,1)S(1)}, bf16[128,1408]{1,0:T(8,128)(2,1)S(1)}, u32[]{:S(2)}, u32[]{:S(2)}) %collective-permute-start.6) | collective-permute-done | bytes 360480 | tf_op jit(solution)/shard_map/ppermute | solution.py:206
  19.4 0.1 shard_map.86
  19.5 3.2 %collective-permute-start.7 = (bf16[32,1280]{1,0:T(8,128)(2,1)S(1)}, bf16[32,1280]{1,0:T(8,128)(2,1)S(1)}, u32[]{:S(2)}, u32[]{:S(2)}) collective-permute-start(bf16[32,1280]{1,0:T(8,128)(2,1)S(1)} %get-tuple-element.41), channel_id=1, source_target_pairs={{0,8},{4,12},{8,0},{12,4},{1,9},{5,13},{9,1},{13,5},{2,10},{6,14},... | collective-permute-start | bytes 245768 | tf_op jit(solution)/shard_map/ppermute | solution.py:206
  22.6 1.5 %collective-permute-start.10 = (bf16[32,128]{1,0:T(8,128)(2,1)S(1)}, bf16[32,128]{1,0:T(8,128)(2,1)S(1)}, u32[]{:S(2)}, u32[]{:S(2)}) collective-permute-start(bf16[32,128]{1,0:T(8,128)(2,1)S(1)} %get-tuple-element.45.refs_5_), channel_id=1, source_target_pairs={{0,2},{2,0},{1,3},{3,1},{4,6},{6,4},{5,7},{7,5},{8,10},{10,8},{9,1... | collective-permute-start | bytes 24584 | tf_op jit(solution)/shard_map/ppermute | solution.py:206
  24.1 0.4 collective-permute-start.8
  24.5 0.3 collective-permute-start.9
  24.9 1.4 %collective-permute-done.10.refs_0_.refs_6_ = bf16[32,128]{1,0:T(8,128)(2,1)S(1)} collective-permute-done((bf16[32,128]{1,0:T(8,128)(2,1)S(1)}, bf16[32,128]{1,0:T(8,128)(2,1)S(1)}, u32[]{:S(2)}, u32[]{:S(2)}) %collective-permute-start.10) | collective-permute-done | bytes 8224 | tf_op jit(solution)/shard_map/ppermute | solution.py:206
  26.3 0.9 %collective-permute-done.7.passed.refs_0_ = bf16[32,1280]{1,0:T(8,128)(2,1)S(1)} collective-permute-done((bf16[32,1280]{1,0:T(8,128)(2,1)S(1)}, bf16[32,1280]{1,0:T(8,128)(2,1)S(1)}, u32[]{:S(2)}, u32[]{:S(2)}) %collective-permute-start.7) | collective-permute-done | bytes 81952 | tf_op jit(solution)/shard_map/ppermute | solution.py:206
  27.2 2.6 %collective-permute-start.11 = (bf16[32,1280]{1,0:T(8,128)(2,1)S(1)}, bf16[32,1280]{1,0:T(8,128)(2,1)S(1)}, u32[]{:S(2)}, u32[]{:S(2)}) collective-permute-start(bf16[32,1280]{1,0:T(8,128)(2,1)S(1)} %shard_map.87), channel_id=1, source_target_pairs={{0,2},{2,0},{1,3},{3,1},{4,6},{6,4},{5,7},{7,5},{8,10},{10,8},{9,1... | collective-permute-start | bytes 245768 | tf_op jit(solution)/shard_map/ppermute | solution.py:206
  29.9 3.7 %shard_map.82 = (bf16[2048,1024]{1,0:T(8,128)(2,1)S(1)}, bf16[32,64,256]{2,1,0:T(8,128)(2,1)S(1)}, bf16[32,64,256]{2,1,0:T(8,128)(2,1)S(1)}, f32[32,128]{1,0:T(8...) custom-call(s32[32]{0:T(128)S(1)} %copy-done.3, bf16[4096,2048]{1,0:T(8,128)(2,1)} %weight.5, ...), custom_call_target="tpu_custom_call" | custom-call | bytes 6291456 | tf_op jit(solution)/shard_map/pallas_call | solution.py:642
  33.6 1.7 %shard_map.88 = (bf16[32,2048]{1,0:T(8,128)(2,1)S(1)}, bf16[16,2048]{1,0:T(8,128)(2,1)S(1)}, bf16[16,2048]{1,0:T(8,128)(2,1)S(1)}) custom-call(f32[32,128]{1,0:T(8,128)S(1)} %get-tuple-element.33.cosine, f32[32,128]{1,0:T(8,128)S(1)} %get-tuple-element.34.sine, s32[32,128]{1,0:T(8,128)S(1)} %get-tuple-element.35.lengths, ...), custom_call_target="tpu_custom_call" | custom-call | flops 16777216 | tf_op jit(solution)/shard_map/pallas_call | solution.py:658
  35.3 0.5 collective-permute-start.14
  35.8 2.5 %collective-permute-start.15 = (bf16[16,2048]{1,0:T(8,128)(2,1)S(1)}, bf16[16,2048]{1,0:T(8,128)(2,1)S(1)}, u32[]{:S(2)}, u32[]{:S(2)}) collective-permute-start(bf16[16,2048]{1,0:T(8,128)(2,1)S(1)} %get-tuple-element.51.refs_1_), channel_id=1, source_target_pairs={{0,8},{4,12},{8,0},{12,4},{1,9},{5,13},{9,1},{13,5},{2,10},{6,14},... | collective-permute-start | bytes 196616 | tf_op jit(solution)/shard_map/ppermute | solution.py:206
  38.3 1.1 %collective-permute-start.12 = (bf16[16,2048]{1,0:T(8,128)(2,1)S(1)}, bf16[16,2048]{1,0:T(8,128)(2,1)S(1)}, u32[]{:S(2)}, u32[]{:S(2)}) collective-permute-start(bf16[16,2048]{1,0:T(8,128)(2,1)S(1)} %get-tuple-element.50.refs_0_), channel_id=1, source_target_pairs={{0,4},{4,0},{8,12},{12,8},{1,5},{5,1},{9,13},{13,9},{2,6},{6,2},{1... | collective-permute-start | bytes 196616 | tf_op jit(solution)/shard_map/ppermute | solution.py:206
  39.4 0.9 %collective-permute-start.13 = (bf16[16,2048]{1,0:T(8,128)(2,1)S(1)}, bf16[16,2048]{1,0:T(8,128)(2,1)S(1)}, u32[]{:S(2)}, u32[]{:S(2)}) collective-permute-start(bf16[16,2048]{1,0:T(8,128)(2,1)S(1)} %get-tuple-element.51.refs_1_), channel_id=1, source_target_pairs={{0,4},{4,0},{8,12},{12,8},{1,5},{5,1},{9,13},{13,9},{2,6},{6,2},{1... | collective-permute-start | bytes 196616 | tf_op jit(solution)/shard_map/ppermute | solution.py:206
  40.3 0.6 %collective-permute-done.14.refs_4_ = bf16[16,2048]{1,0:T(8,128)(2,1)S(1)} collective-permute-done((bf16[16,2048]{1,0:T(8,128)(2,1)S(1)}, bf16[16,2048]{1,0:T(8,128)(2,1)S(1)}, u32[]{:S(2)}, u32[]{:S(2)}) %collective-permute-start.14) | collective-permute-done | bytes 65568 | tf_op jit(solution)/shard_map/ppermute | solution.py:206
  41.0 1.3 %collective-permute-start.16 = (bf16[16,2048]{1,0:T(8,128)(2,1)S(1)}, bf16[16,2048]{1,0:T(8,128)(2,1)S(1)}, u32[]{:S(2)}, u32[]{:S(2)}) collective-permute-start(bf16[16,2048]{1,0:T(8,128)(2,1)S(1)} %collective-permute-done.14.refs_4_), channel_id=1, source_target_pairs={{0,4},{4,0},{8,12},{12,8},{1,5},{5,1},{9,13},{13,9},{2,6},{6,2},{1... | collective-permute-start | bytes 196616 | tf_op jit(solution)/shard_map/ppermute | solution.py:206
  42.3 2.9 %collective-permute-start.17 = (bf16[16,2048]{1,0:T(8,128)(2,1)S(1)}, bf16[16,2048]{1,0:T(8,128)(2,1)S(1)}, u32[]{:S(2)}, u32[]{:S(2)}) collective-permute-start(bf16[16,2048]{1,0:T(8,128)(2,1)S(1)} %collective-permute-done.15.refs_5_), channel_id=1, source_target_pairs={{0,4},{4,0},{8,12},{12,8},{1,5},{5,1},{9,13},{13,9},{2,6},{6,2},{1... | collective-permute-start | bytes 196616 | tf_op jit(solution)/shard_map/ppermute | solution.py:206
  45.2 2.2 %shard_map.89.refs_8_.weight = bf16[2048,1024]{1,0:T(8,128)(2,1)S(1)} custom-call(bf16[4096,2048]{1,0:T(8,128)(2,1)} %weight.5, bf16[32,2048]{1,0:T(8,128)(2,1)S(1)} %get-tuple-element.48.attended), custom_call_target="tpu_custom_call" | custom-call | bytes 4194304 | tf_op jit(solution)/shard_map/pallas_call | solution.py:675
  47.5 0.8 %shard_map.90 = (bf16[128,1024]{1,0:T(8,128)(2,1)S(1)}, bf16[128,2048]{1,0:T(8,128)(2,1)S(1)}) custom-call(bf16[128,128]{1,0:T(8,128)(2,1)S(1)} %get-tuple-element.49.chosen, bf16[16,2048]{1,0:T(8,128)(2,1)S(1)} %get-tuple-element.50.refs_0_, bf16[16,2048]{1,0:T(8,128)(2,1)S(1)} %get-tuple-element.51.refs_1_, ...), custom_call_target="tpu_custom_call" | custom-call | flops 536870912 | bytes 4194304 | tf_op jit(solution)/shard_map/pallas_call | solution.py:392
  48.3 0.0 copy-start
  48.3 0.1 collective-permute-start.18
  48.4 0.7 %shard_map.91.own = f32[128,1024]{1,0:T(8,128)S(1)} custom-call(bf16[128,2048]{1,0:T(8,128)(2,1)S(1)} %get-tuple-element.53.permuted, bf16[2048,1024]{1,0:T(8,128)(2,1)S(1)} %shard_map.89.refs_8_.weight), custom_call_target="tpu_custom_call" | custom-call | flops 536870912 | bytes 4194304 | tf_op jit(solution)/shard_map/pallas_call | solution.py:401
  49.1 0.8 %collective-permute-done.18.received = bf16[128,1024]{1,0:T(8,128)(2,1)S(1)} collective-permute-done((bf16[128,1024]{1,0:T(8,128)(2,1)S(1)}, bf16[128,1024]{1,0:T(8,128)(2,1)S(1)}, u32[]{:S(2)}, u32[]{:S(2)}) %collective-permute-start.18) | collective-permute-done | bytes 262176 | tf_op jit(solution)/shard_map/ppermute | solution.py:206
  50.0 1.6 %collective-permute-start.19 = (bf16[32,1024]{1,0:T(8,128)(2,1)S(1)}, bf16[32,1024]{1,0:T(8,128)(2,1)S(1)}, u32[]{:S(2)}, u32[]{:S(2)}) collective-permute-start(bf16[32,1024]{1,0:T(8,128)(2,1)S(1)} %get-tuple-element.55), channel_id=1, source_target_pairs={{0,8},{4,12},{8,0},{12,4},{1,9},{5,13},{9,1},{13,5},{2,10},{6,14},... | collective-permute-start | bytes 196616 | tf_op jit(solution)/shard_map/ppermute | solution.py:206
  51.6 2.8 %collective-permute-start.20 = (bf16[32,1024]{1,0:T(8,128)(2,1)S(1)}, bf16[32,1024]{1,0:T(8,128)(2,1)S(1)}, u32[]{:S(2)}, u32[]{:S(2)}) collective-permute-start(bf16[32,1024]{1,0:T(8,128)(2,1)S(1)} %get-tuple-element.56), channel_id=1, source_target_pairs={{0,12},{2,4},{4,8},{6,0},{8,14},{10,6},{12,10},{14,2},{1,13},{3,5}... | collective-permute-start | bytes 196616 | tf_op jit(solution)/shard_map/ppermute | solution.py:453
  54.4 1.5 %collective-permute-done.19.passed.refs_0_ = bf16[32,1024]{1,0:T(8,128)(2,1)S(1)} collective-permute-done((bf16[32,1024]{1,0:T(8,128)(2,1)S(1)}, bf16[32,1024]{1,0:T(8,128)(2,1)S(1)}, u32[]{:S(2)}, u32[]{:S(2)}) %collective-permute-start.19) | collective-permute-done | bytes 65568 | tf_op jit(solution)/shard_map/ppermute | solution.py:206
  55.9 1.6 %collective-permute-start.22 = (bf16[32,1024]{1,0:T(8,128)(2,1)S(1)}, bf16[32,1024]{1,0:T(8,128)(2,1)S(1)}, u32[]{:S(2)}, u32[]{:S(2)}) collective-permute-start(bf16[32,1024]{1,0:T(8,128)(2,1)S(1)} %shard_map.93), channel_id=1, source_target_pairs={{0,2},{2,0},{1,3},{3,1},{4,6},{6,4},{5,7},{7,5},{8,10},{10,8},{9,1... | collective-permute-start | bytes 196616 | tf_op jit(solution)/shard_map/ppermute | solution.py:206
  57.5 2.4 %collective-permute-done.21.refs_2_ = bf16[32,1024]{1,0:T(8,128)(2,1)S(1)} collective-permute-done((bf16[32,1024]{1,0:T(8,128)(2,1)S(1)}, bf16[32,1024]{1,0:T(8,128)(2,1)S(1)}, u32[]{:S(2)}, u32[]{:S(2)}) %collective-permute-start.21) | collective-permute-done | bytes 65568 | tf_op jit(solution)/shard_map/ppermute | solution.py:453
  59.9 0.3 collective-permute-done.22.refs_4_
  60.3 0.1 shard_map.94
  60.3 0.1 collective-permute-start.23
  60.4 1.3 %collective-permute-done.23.received = bf16[32,2048]{1,0:T(8,128)(2,1)S(1)} collective-permute-done((bf16[32,2048]{1,0:T(8,128)(2,1)S(1)}, bf16[32,2048]{1,0:T(8,128)(2,1)S(1)}, u32[]{:S(2)}, u32[]{:S(2)}) %collective-permute-start.23) | collective-permute-done | bytes 131104 | tf_op jit(solution)/shard_map/ppermute | solution.py:206
  61.8 0.7 %shard_map.95 = bf16[1,32,4096]{2,1,0:T(8,128)(2,1)} custom-call(bf16[32,2048]{1,0:T(8,128)(2,1)S(1)} %get-tuple-element.59.keep, bf16[32,2048]{1,0:T(8,128)(2,1)S(1)} %collective-permute-done.23.received), custom_call_target="tpu_custom_call" | custom-call | bytes 524288 | tf_op jit(solution)/shard_map/pallas_call | solution.py:696
  (23 shorter events, 0.1 us)
Async XLA Ops:
  0.9 7.9 %collective-permute-start.2 = (bf16[16,2048]{1,0:T(8,128)(2,1)S(1)}, bf16[16,2048]{1,0:T(8,128)(2,1)S(1)}, u32[]{:S(2)}, u32[]{:S(2)}) collective-permute-start(bf16[16,2048]{1,0:T(8,128)(2,1)S(1)} %get-tuple-element.62.refs_0_), channel_id=1, source_target_pairs={{0,8},{4,12},{8,0},{12,4},{1,9},{5,13},{9,1},{13,5},{2,10},{6,14},... | collective-permute-start | bytes 196616 | tf_op jit(solution)/shard_map/ppermute | solution.py:206
  5.0 11.5 %copy-start.1 = (bf16[4096]{0:T(1024)(128)(2,1)S(1)}, bf16[4096]{0:T(1024)(128)(2,1)}, u32[]{:S(2)}) copy-start(bf16[4096]{0:T(1024)(128)(2,1)} %param.9) | copy-start | bytes 24580
  5.0 6.1 %collective-permute-start.3 = (bf16[16,2048]{1,0:T(8,128)(2,1)S(1)}, bf16[16,2048]{1,0:T(8,128)(2,1)S(1)}, u32[]{:S(2)}, u32[]{:S(2)}) collective-permute-start(bf16[16,2048]{1,0:T(8,128)(2,1)S(1)} %get-tuple-element.61.refs_1_), channel_id=1, source_target_pairs={{0,8},{4,12},{8,0},{12,4},{1,9},{5,13},{9,1},{13,5},{2,10},{6,14},... | collective-permute-start | bytes 196616 | tf_op jit(solution)/shard_map/ppermute | solution.py:206
  5.1 11.4 %collective-permute-start = (bf16[16,2048]{1,0:T(8,128)(2,1)S(1)}, bf16[16,2048]{1,0:T(8,128)(2,1)S(1)}, u32[]{:S(2)}, u32[]{:S(2)}) collective-permute-start(bf16[16,2048]{1,0:T(8,128)(2,1)S(1)} %get-tuple-element.62.refs_0_), channel_id=1, source_target_pairs={{0,4},{4,0},{8,12},{12,8},{1,5},{5,1},{9,13},{13,9},{2,6},{6,2},{1... | collective-permute-start | bytes 196616 | tf_op jit(solution)/shard_map/ppermute | solution.py:206
  6.9 9.6 %collective-permute-start.1 = (bf16[16,2048]{1,0:T(8,128)(2,1)S(1)}, bf16[16,2048]{1,0:T(8,128)(2,1)S(1)}, u32[]{:S(2)}, u32[]{:S(2)}) collective-permute-start(bf16[16,2048]{1,0:T(8,128)(2,1)S(1)} %get-tuple-element.61.refs_1_), channel_id=1, source_target_pairs={{0,4},{4,0},{8,12},{12,8},{1,5},{5,1},{9,13},{13,9},{2,6},{6,2},{1... | collective-permute-start | bytes 196616 | tf_op jit(solution)/shard_map/ppermute | solution.py:206
  8.7 7.8 %collective-permute-start.4 = (bf16[16,2048]{1,0:T(8,128)(2,1)S(1)}, bf16[16,2048]{1,0:T(8,128)(2,1)S(1)}, u32[]{:S(2)}, u32[]{:S(2)}) collective-permute-start(bf16[16,2048]{1,0:T(8,128)(2,1)S(1)} %collective-permute-done.2.refs_4_), channel_id=1, source_target_pairs={{0,4},{4,0},{8,12},{12,8},{1,5},{5,1},{9,13},{13,9},{2,6},{6,2},{1... | collective-permute-start | bytes 196616 | tf_op jit(solution)/shard_map/ppermute | solution.py:206
  11.1 5.4 %collective-permute-start.5 = (bf16[16,2048]{1,0:T(8,128)(2,1)S(1)}, bf16[16,2048]{1,0:T(8,128)(2,1)S(1)}, u32[]{:S(2)}, u32[]{:S(2)}) collective-permute-start(bf16[16,2048]{1,0:T(8,128)(2,1)S(1)} %collective-permute-done.3.refs_5_), channel_id=1, source_target_pairs={{0,4},{4,0},{8,12},{12,8},{1,5},{5,1},{9,13},{13,9},{2,6},{6,2},{1... | collective-permute-start | bytes 196616 | tf_op jit(solution)/shard_map/ppermute | solution.py:206
  17.6 12.2 %copy-start.2 = (s32[128]{0:T(128)S(1)}, s32[128]{0:T(128)}, u32[]{:S(2)}) copy-start(s32[128]{0:T(128)} %slots.3) | copy-start | bytes 1540
  17.6 12.2 %copy-start.3 = (s32[32]{0:T(128)S(1)}, s32[32]{0:T(128)}, u32[]{:S(2)}) copy-start(s32[32]{0:T(128)} %lengths.1) | copy-start | bytes 388
  17.6 1.7 %collective-permute-start.6 = (bf16[128,1408]{1,0:T(8,128)(2,1)S(1)}, bf16[128,1408]{1,0:T(8,128)(2,1)S(1)}, u32[]{:S(2)}, u32[]{:S(2)}) collective-permute-start(bf16[128,1408]{1,0:T(8,128)(2,1)S(1)} %get-tuple-element.40.given), channel_id=1, source_target_pairs={{0,1},{1,0},{2,3},{3,2},{4,5},{5,4},{6,7},{7,6},{8,9},{9,8},{10,11... | collective-permute-start | bytes 1081352 | tf_op jit(solution)/shard_map/ppermute | solution.py:206
  19.5 7.8 %collective-permute-start.7 = (bf16[32,1280]{1,0:T(8,128)(2,1)S(1)}, bf16[32,1280]{1,0:T(8,128)(2,1)S(1)}, u32[]{:S(2)}, u32[]{:S(2)}) collective-permute-start(bf16[32,1280]{1,0:T(8,128)(2,1)S(1)} %get-tuple-element.41), channel_id=1, source_target_pairs={{0,8},{4,12},{8,0},{12,4},{1,9},{5,13},{9,1},{13,5},{2,10},{6,14},... | collective-permute-start | bytes 245768 | tf_op jit(solution)/shard_map/ppermute | solution.py:206
  22.6 3.7 %collective-permute-start.10 = (bf16[32,128]{1,0:T(8,128)(2,1)S(1)}, bf16[32,128]{1,0:T(8,128)(2,1)S(1)}, u32[]{:S(2)}, u32[]{:S(2)}) collective-permute-start(bf16[32,128]{1,0:T(8,128)(2,1)S(1)} %get-tuple-element.45.refs_5_), channel_id=1, source_target_pairs={{0,2},{2,0},{1,3},{3,1},{4,6},{6,4},{5,7},{7,5},{8,10},{10,8},{9,1... | collective-permute-start | bytes 24584 | tf_op jit(solution)/shard_map/ppermute | solution.py:206
  24.1 9.4 %collective-permute-start.8 = (bf16[32,1280]{1,0:T(8,128)(2,1)S(1)}, bf16[32,1280]{1,0:T(8,128)(2,1)S(1)}, u32[]{:S(2)}, u32[]{:S(2)}) collective-permute-start(bf16[32,1280]{1,0:T(8,128)(2,1)S(1)} %get-tuple-element.42), channel_id=1, source_target_pairs={{0,12},{2,4},{4,8},{6,0},{8,14},{10,6},{12,10},{14,2},{1,13},{3,5}... | collective-permute-start | bytes 245768 | tf_op jit(solution)/shard_map/ppermute | solution.py:453
  24.5 9.1 %collective-permute-start.9 = (bf16[32,1280]{1,0:T(8,128)(2,1)S(1)}, bf16[32,1280]{1,0:T(8,128)(2,1)S(1)}, u32[]{:S(2)}, u32[]{:S(2)}) collective-permute-start(bf16[32,1280]{1,0:T(8,128)(2,1)S(1)} %get-tuple-element.43), channel_id=1, source_target_pairs={{0,4},{2,12},{4,0},{6,8},{8,6},{10,14},{12,2},{14,10},{1,5},{3,13}... | collective-permute-start | bytes 245768 | tf_op jit(solution)/shard_map/ppermute | solution.py:453
  27.2 6.4 %collective-permute-start.11 = (bf16[32,1280]{1,0:T(8,128)(2,1)S(1)}, bf16[32,1280]{1,0:T(8,128)(2,1)S(1)}, u32[]{:S(2)}, u32[]{:S(2)}) collective-permute-start(bf16[32,1280]{1,0:T(8,128)(2,1)S(1)} %shard_map.87), channel_id=1, source_target_pairs={{0,2},{2,0},{1,3},{3,1},{4,6},{6,4},{5,7},{7,5},{8,10},{10,8},{9,1... | collective-permute-start | bytes 245768 | tf_op jit(solution)/shard_map/ppermute | solution.py:206
  35.3 5.7 %collective-permute-start.14 = (bf16[16,2048]{1,0:T(8,128)(2,1)S(1)}, bf16[16,2048]{1,0:T(8,128)(2,1)S(1)}, u32[]{:S(2)}, u32[]{:S(2)}) collective-permute-start(bf16[16,2048]{1,0:T(8,128)(2,1)S(1)} %get-tuple-element.50.refs_0_), channel_id=1, source_target_pairs={{0,8},{4,12},{8,0},{12,4},{1,9},{5,13},{9,1},{13,5},{2,10},{6,14},... | collective-permute-start | bytes 196616 | tf_op jit(solution)/shard_map/ppermute | solution.py:206
  35.8 6.5 %collective-permute-start.15 = (bf16[16,2048]{1,0:T(8,128)(2,1)S(1)}, bf16[16,2048]{1,0:T(8,128)(2,1)S(1)}, u32[]{:S(2)}, u32[]{:S(2)}) collective-permute-start(bf16[16,2048]{1,0:T(8,128)(2,1)S(1)} %get-tuple-element.51.refs_1_), channel_id=1, source_target_pairs={{0,8},{4,12},{8,0},{12,4},{1,9},{5,13},{9,1},{13,5},{2,10},{6,14},... | collective-permute-start | bytes 196616 | tf_op jit(solution)/shard_map/ppermute | solution.py:206
  38.3 9.1 %collective-permute-start.12 = (bf16[16,2048]{1,0:T(8,128)(2,1)S(1)}, bf16[16,2048]{1,0:T(8,128)(2,1)S(1)}, u32[]{:S(2)}, u32[]{:S(2)}) collective-permute-start(bf16[16,2048]{1,0:T(8,128)(2,1)S(1)} %get-tuple-element.50.refs_0_), channel_id=1, source_target_pairs={{0,4},{4,0},{8,12},{12,8},{1,5},{5,1},{9,13},{13,9},{2,6},{6,2},{1... | collective-permute-start | bytes 196616 | tf_op jit(solution)/shard_map/ppermute | solution.py:206
  39.4 8.0 %collective-permute-start.13 = (bf16[16,2048]{1,0:T(8,128)(2,1)S(1)}, bf16[16,2048]{1,0:T(8,128)(2,1)S(1)}, u32[]{:S(2)}, u32[]{:S(2)}) collective-permute-start(bf16[16,2048]{1,0:T(8,128)(2,1)S(1)} %get-tuple-element.51.refs_1_), channel_id=1, source_target_pairs={{0,4},{4,0},{8,12},{12,8},{1,5},{5,1},{9,13},{13,9},{2,6},{6,2},{1... | collective-permute-start | bytes 196616 | tf_op jit(solution)/shard_map/ppermute | solution.py:206
  41.0 6.5 %collective-permute-start.16 = (bf16[16,2048]{1,0:T(8,128)(2,1)S(1)}, bf16[16,2048]{1,0:T(8,128)(2,1)S(1)}, u32[]{:S(2)}, u32[]{:S(2)}) collective-permute-start(bf16[16,2048]{1,0:T(8,128)(2,1)S(1)} %collective-permute-done.14.refs_4_), channel_id=1, source_target_pairs={{0,4},{4,0},{8,12},{12,8},{1,5},{5,1},{9,13},{13,9},{2,6},{6,2},{1... | collective-permute-start | bytes 196616 | tf_op jit(solution)/shard_map/ppermute | solution.py:206
  42.3 5.2 %collective-permute-start.17 = (bf16[16,2048]{1,0:T(8,128)(2,1)S(1)}, bf16[16,2048]{1,0:T(8,128)(2,1)S(1)}, u32[]{:S(2)}, u32[]{:S(2)}) collective-permute-start(bf16[16,2048]{1,0:T(8,128)(2,1)S(1)} %collective-permute-done.15.refs_5_), channel_id=1, source_target_pairs={{0,4},{4,0},{8,12},{12,8},{1,5},{5,1},{9,13},{13,9},{2,6},{6,2},{1... | collective-permute-start | bytes 196616 | tf_op jit(solution)/shard_map/ppermute | solution.py:206
  48.3 11.9 %copy-start = (bf16[32,4096]{1,0:T(8,128)(2,1)S(1)}, bf16[32,4096]{1,0:T(8,128)(2,1)}, u32[]{:S(2)}) copy-start(bf16[32,4096]{1,0:T(8,128)(2,1)} %hidden.1) | copy-start | bytes 786436
  48.3 1.6 %collective-permute-start.18 = (bf16[128,1024]{1,0:T(8,128)(2,1)S(1)}, bf16[128,1024]{1,0:T(8,128)(2,1)S(1)}, u32[]{:S(2)}, u32[]{:S(2)}) collective-permute-start(bf16[128,1024]{1,0:T(8,128)(2,1)S(1)} %get-tuple-element.54.given), channel_id=1, source_target_pairs={{0,1},{1,0},{2,3},{3,2},{4,5},{5,4},{6,7},{7,6},{8,9},{9,8},{10,11... | collective-permute-start | bytes 786440 | tf_op jit(solution)/shard_map/ppermute | solution.py:206
  50.0 5.9 %collective-permute-start.19 = (bf16[32,1024]{1,0:T(8,128)(2,1)S(1)}, bf16[32,1024]{1,0:T(8,128)(2,1)S(1)}, u32[]{:S(2)}, u32[]{:S(2)}) collective-permute-start(bf16[32,1024]{1,0:T(8,128)(2,1)S(1)} %get-tuple-element.55), channel_id=1, source_target_pairs={{0,8},{4,12},{8,0},{12,4},{1,9},{5,13},{9,1},{13,5},{2,10},{6,14},... | collective-permute-start | bytes 196616 | tf_op jit(solution)/shard_map/ppermute | solution.py:206
  51.6 6.0 %collective-permute-start.20 = (bf16[32,1024]{1,0:T(8,128)(2,1)S(1)}, bf16[32,1024]{1,0:T(8,128)(2,1)S(1)}, u32[]{:S(2)}, u32[]{:S(2)}) collective-permute-start(bf16[32,1024]{1,0:T(8,128)(2,1)S(1)} %get-tuple-element.56), channel_id=1, source_target_pairs={{0,12},{2,4},{4,8},{6,0},{8,14},{10,6},{12,10},{14,2},{1,13},{3,5}... | collective-permute-start | bytes 196616 | tf_op jit(solution)/shard_map/ppermute | solution.py:453
  54.4 5.6 %collective-permute-start.21 = (bf16[32,1024]{1,0:T(8,128)(2,1)S(1)}, bf16[32,1024]{1,0:T(8,128)(2,1)S(1)}, u32[]{:S(2)}, u32[]{:S(2)}) collective-permute-start(bf16[32,1024]{1,0:T(8,128)(2,1)S(1)} %get-tuple-element.57), channel_id=1, source_target_pairs={{0,4},{2,12},{4,0},{6,8},{8,6},{10,14},{12,2},{14,10},{1,5},{3,13}... | collective-permute-start | bytes 196616 | tf_op jit(solution)/shard_map/ppermute | solution.py:453
  55.9 4.3 %collective-permute-start.22 = (bf16[32,1024]{1,0:T(8,128)(2,1)S(1)}, bf16[32,1024]{1,0:T(8,128)(2,1)S(1)}, u32[]{:S(2)}, u32[]{:S(2)}) collective-permute-start(bf16[32,1024]{1,0:T(8,128)(2,1)S(1)} %shard_map.93), channel_id=1, source_target_pairs={{0,2},{2,0},{1,3},{3,1},{4,6},{6,4},{5,7},{7,5},{8,10},{10,8},{9,1... | collective-permute-start | bytes 196616 | tf_op jit(solution)/shard_map/ppermute | solution.py:206
  60.3 1.4 %collective-permute-start.23 = (bf16[32,2048]{1,0:T(8,128)(2,1)S(1)}, bf16[32,2048]{1,0:T(8,128)(2,1)S(1)}, u32[]{:S(2)}, u32[]{:S(2)}) collective-permute-start(bf16[32,2048]{1,0:T(8,128)(2,1)S(1)} %get-tuple-element.60), channel_id=1, source_target_pairs={{0,1},{1,0},{2,3},{3,2},{4,5},{5,4},{6,7},{7,6},{8,9},{9,8},{10,11... | collective-permute-start | bytes 393224 | tf_op jit(solution)/shard_map/ppermute | solution.py:206

commit v24 on v23

--- a/solution.py
+++ b/solution.py
@@ -310,7 +310,7 @@
 
 
 def dot_columns(rows, weight, out):
-    size, width = weight.shape[1], 512
+    size, width = weight.shape[1], 1024
     for start in range(0, size, width):
         part = slice(start, min(start + width, size))
         product = jnp.dot(rows, weight[:, part], preferred_element_type=jnp.float32)

time: 62.6 us -> 62.6 us (level)
  no operation moved by 1% of the time
where the time goes in v24:
time: 62.6 us; the launch traced here: 62.5 us
  starting transfers between devices  32.9 us (53%)
  Pallas kernels  16.2 us (26%)
  waiting for transfers between devices  12.2 us (19%)
  local copies, waits for them, and re-layouts  0.9 us (1%)
    ppermute x20, starting transfers between devices, moved(): return lax.ppermute(value, axis, pairs)  29.4 us
    ppermute x20, waiting for transfers between devices, moved(): return lax.ppermute(value, axis, pairs)  9.85 us
    pallas_call x1, Pallas kernels, paired_plan(): call(functools.partial(stage_in_kernel, col_count), [pltpu.VMEM((half, ha...  4.09 us
    pallas_call x1, Pallas kernels, paired_plan(): call(functools.partial(stage_rest_kernel, col_count), [pltpu.VMEM((half,...  3.71 us
    ppermute x4, starting transfers between devices, direct(): return lax.ppermute(value, ('col', 'row'), moves)  3.53 us
    ppermute x4, waiting for transfers between devices, direct(): return lax.ppermute(value, ('col', 'row'), moves)  2.4 us
    pallas_call x1, Pallas kernels, paired_plan(): call(stage_out_kernel, pltpu.VMEM((half, half_out), jnp.bfloat16), [HBM,...  2.24 us
    pallas_call x2, Pallas kernels, project(): call(functools.partial(kernel, parts), [struct((rows, half + more)), stru...  1.91 us
  transfers between devices with their start and end apart: 24, of which 11 were waited for; matrix products, arithmetic and copies ran while one was open for 0% of the time, Pallas kernels for 19%

profile of v24, /device:TPU:0, one launch (start us, length us, event | category | flops | bytes accessed | tf_op | source)
XLA Modules:
  0.0 62.5 jit_solution(11737494323617347617)
XLA Ops:
  0.0 0.9 %fusion = (bf16[16,2048]{1,0:T(8,128)(2,1)S(1)}, bf16[16,2048]{1,0:T(8,128)(2,1)S(1)}) fusion(bf16[32,4096]{1,0:T(8,128)(2,1)} %hidden.1, s32[]{:T(128)S(6)} %add.4, s32[]{:T(128)S(6)} %select_n.3), kind=kLoop, calls=%fused_computation.1 | loop fusion | bytes 262152 | tf_op jit(solution)/shard_map/slice | solution.py:639
  0.9 4.1 %collective-permute-start.2 = (bf16[16,2048]{1,0:T(8,128)(2,1)S(1)}, bf16[16,2048]{1,0:T(8,128)(2,1)S(1)}, u32[]{:S(2)}, u32[]{:S(2)}) collective-permute-start(bf16[16,2048]{1,0:T(8,128)(2,1)S(1)} %get-tuple-element.62.refs_0_), channel_id=1, source_target_pairs={{0,8},{4,12},{8,0},{12,4},{1,9},{5,13},{9,1},{13,5},{2,10},{6,14},... | collective-permute-start | bytes 196616 | tf_op jit(solution)/shard_map/ppermute | solution.py:206
  5.0 0.1 collective-permute-start.3
  5.1 1.8 %collective-permute-start = (bf16[16,2048]{1,0:T(8,128)(2,1)S(1)}, bf16[16,2048]{1,0:T(8,128)(2,1)S(1)}, u32[]{:S(2)}, u32[]{:S(2)}) collective-permute-start(bf16[16,2048]{1,0:T(8,128)(2,1)S(1)} %get-tuple-element.62.refs_0_), channel_id=1, source_target_pairs={{0,4},{4,0},{8,12},{12,8},{1,5},{5,1},{9,13},{13,9},{2,6},{6,2},{1... | collective-permute-start | bytes 196616 | tf_op jit(solution)/shard_map/ppermute | solution.py:206
  6.9 0.2 collective-permute-start.1
  7.1 1.6 %collective-permute-done.2.refs_4_ = bf16[16,2048]{1,0:T(8,128)(2,1)S(1)} collective-permute-done((bf16[16,2048]{1,0:T(8,128)(2,1)S(1)}, bf16[16,2048]{1,0:T(8,128)(2,1)S(1)}, u32[]{:S(2)}, u32[]{:S(2)}) %collective-permute-start.2) | collective-permute-done | bytes 65568 | tf_op jit(solution)/shard_map/ppermute | solution.py:206
  8.7 1.9 %collective-permute-start.4 = (bf16[16,2048]{1,0:T(8,128)(2,1)S(1)}, bf16[16,2048]{1,0:T(8,128)(2,1)S(1)}, u32[]{:S(2)}, u32[]{:S(2)}) collective-permute-start(bf16[16,2048]{1,0:T(8,128)(2,1)S(1)} %collective-permute-done.2.refs_4_), channel_id=1, source_target_pairs={{0,4},{4,0},{8,12},{12,8},{1,5},{5,1},{9,13},{13,9},{2,6},{6,2},{1... | collective-permute-start | bytes 196616 | tf_op jit(solution)/shard_map/ppermute | solution.py:206
  10.6 0.4 collective-permute-done.3.refs_5_
  11.1 1.3 %collective-permute-start.5 = (bf16[16,2048]{1,0:T(8,128)(2,1)S(1)}, bf16[16,2048]{1,0:T(8,128)(2,1)S(1)}, u32[]{:S(2)}, u32[]{:S(2)}) collective-permute-start(bf16[16,2048]{1,0:T(8,128)(2,1)S(1)} %collective-permute-done.3.refs_5_), channel_id=1, source_target_pairs={{0,4},{4,0},{8,12},{12,8},{1,5},{5,1},{9,13},{13,9},{2,6},{6,2},{1... | collective-permute-start | bytes 196616 | tf_op jit(solution)/shard_map/ppermute | solution.py:206
  12.4 4.1 %shard_map.83 = (bf16[2048,1280]{1,0:T(8,128)(2,1)S(1)}, bf16[2048,1280]{1,0:T(8,128)(2,1)S(1)}, bf16[128,128]{1,0:T(8,128)(2,1)S(1)}) custom-call(bf16[4096,2560]{1,0:T(8,128)(2,1)} %weight.4, s32[128]{0:T(128)} %slots.3), custom_call_target="tpu_custom_call" | custom-call | bytes 10485760 | tf_op jit(solution)/shard_map/pallas_call | solution.py:625
  16.5 1.1 %shard_map.84 = (bf16[128,1408]{1,0:T(8,128)(2,1)S(1)}, bf16[128,2048]{1,0:T(8,128)(2,1)S(1)}) custom-call(bf16[128,128]{1,0:T(8,128)(2,1)S(1)} %get-tuple-element.36.chosen, bf16[16,2048]{1,0:T(8,128)(2,1)S(1)} %get-tuple-element.62.refs_0_, bf16[16,2048]{1,0:T(8,128)(2,1)S(1)} %get-tuple-element.61.refs_1_, ...), custom_call_target="tpu_custom_call" | custom-call | flops 671088640 | bytes 5242880 | tf_op jit(solution)/shard_map/pallas_call | solution.py:392
  17.6 0.0 copy-start.3
  17.6 0.1 collective-permute-start.6
  17.7 0.9 %shard_map.85.own = f32[128,1280]{1,0:T(8,128)S(1)} custom-call(bf16[128,2048]{1,0:T(8,128)(2,1)S(1)} %get-tuple-element.39.permuted, bf16[2048,1280]{1,0:T(8,128)(2,1)S(1)} %get-tuple-element.37.refs_8_.weight), custom_call_target="tpu_custom_call" | custom-call | flops 671088640 | bytes 5242880 | tf_op jit(solution)/shard_map/pallas_call | solution.py:401
  18.6 0.8 %collective-permute-done.6.received = bf16[128,1408]{1,0:T(8,128)(2,1)S(1)} collective-permute-done((bf16[128,1408]{1,0:T(8,128)(2,1)S(1)}, bf16[128,1408]{1,0:T(8,128)(2,1)S(1)}, u32[]{:S(2)}, u32[]{:S(2)}) %collective-permute-start.6) | collective-permute-done | bytes 360480 | tf_op jit(solution)/shard_map/ppermute | solution.py:206
  19.4 0.1 shard_map.86
  19.5 3.2 %collective-permute-start.7 = (bf16[32,1280]{1,0:T(8,128)(2,1)S(1)}, bf16[32,1280]{1,0:T(8,128)(2,1)S(1)}, u32[]{:S(2)}, u32[]{:S(2)}) collective-permute-start(bf16[32,1280]{1,0:T(8,128)(2,1)S(1)} %get-tuple-element.41), channel_id=1, source_target_pairs={{0,8},{4,12},{8,0},{12,4},{1,9},{5,13},{9,1},{13,5},{2,10},{6,14},... | collective-permute-start | bytes 245768 | tf_op jit(solution)/shard_map/ppermute | solution.py:206
  22.6 1.5 %collective-permute-start.10 = (bf16[32,128]{1,0:T(8,128)(2,1)S(1)}, bf16[32,128]{1,0:T(8,128)(2,1)S(1)}, u32[]{:S(2)}, u32[]{:S(2)}) collective-permute-start(bf16[32,128]{1,0:T(8,128)(2,1)S(1)} %get-tuple-element.45.refs_5_), channel_id=1, source_target_pairs={{0,2},{2,0},{1,3},{3,1},{4,6},{6,4},{5,7},{7,5},{8,10},{10,8},{9,1... | collective-permute-start | bytes 24584 | tf_op jit(solution)/shard_map/ppermute | solution.py:206
  24.1 0.4 collective-permute-start.8
  24.5 0.3 collective-permute-start.9
  24.9 1.4 %collective-permute-done.10.refs_0_.refs_6_ = bf16[32,128]{1,0:T(8,128)(2,1)S(1)} collective-permute-done((bf16[32,128]{1,0:T(8,128)(2,1)S(1)}, bf16[32,128]{1,0:T(8,128)(2,1)S(1)}, u32[]{:S(2)}, u32[]{:S(2)}) %collective-permute-start.10) | collective-permute-done | bytes 8224 | tf_op jit(solution)/shard_map/ppermute | solution.py:206
  26.3 0.9 %collective-permute-done.7.passed.refs_0_ = bf16[32,1280]{1,0:T(8,128)(2,1)S(1)} collective-permute-done((bf16[32,1280]{1,0:T(8,128)(2,1)S(1)}, bf16[32,1280]{1,0:T(8,128)(2,1)S(1)}, u32[]{:S(2)}, u32[]{:S(2)}) %collective-permute-start.7) | collective-permute-done | bytes 81952 | tf_op jit(solution)/shard_map/ppermute | solution.py:206
  27.2 2.6 %collective-permute-start.11 = (bf16[32,1280]{1,0:T(8,128)(2,1)S(1)}, bf16[32,1280]{1,0:T(8,128)(2,1)S(1)}, u32[]{:S(2)}, u32[]{:S(2)}) collective-permute-start(bf16[32,1280]{1,0:T(8,128)(2,1)S(1)} %shard_map.87), channel_id=1, source_target_pairs={{0,2},{2,0},{1,3},{3,1},{4,6},{6,4},{5,7},{7,5},{8,10},{10,8},{9,1... | collective-permute-start | bytes 245768 | tf_op jit(solution)/shard_map/ppermute | solution.py:206
  29.9 3.7 %shard_map.82 = (bf16[2048,1024]{1,0:T(8,128)(2,1)S(1)}, bf16[32,64,256]{2,1,0:T(8,128)(2,1)S(1)}, bf16[32,64,256]{2,1,0:T(8,128)(2,1)S(1)}, f32[32,128]{1,0:T(8...) custom-call(s32[32]{0:T(128)S(1)} %copy-done.3, bf16[4096,2048]{1,0:T(8,128)(2,1)} %weight.5, ...), custom_call_target="tpu_custom_call" | custom-call | bytes 6291456 | tf_op jit(solution)/shard_map/pallas_call | solution.py:642
  33.6 1.7 %shard_map.88 = (bf16[32,2048]{1,0:T(8,128)(2,1)S(1)}, bf16[16,2048]{1,0:T(8,128)(2,1)S(1)}, bf16[16,2048]{1,0:T(8,128)(2,1)S(1)}) custom-call(f32[32,128]{1,0:T(8,128)S(1)} %get-tuple-element.33.cosine, f32[32,128]{1,0:T(8,128)S(1)} %get-tuple-element.34.sine, s32[32,128]{1,0:T(8,128)S(1)} %get-tuple-element.35.lengths, ...), custom_call_target="tpu_custom_call" | custom-call | flops 16777216 | tf_op jit(solution)/shard_map/pallas_call | solution.py:658
  35.3 0.5 collective-permute-start.14
  35.8 2.5 %collective-permute-start.15 = (bf16[16,2048]{1,0:T(8,128)(2,1)S(1)}, bf16[16,2048]{1,0:T(8,128)(2,1)S(1)}, u32[]{:S(2)}, u32[]{:S(2)}) collective-permute-start(bf16[16,2048]{1,0:T(8,128)(2,1)S(1)} %get-tuple-element.51.refs_1_), channel_id=1, source_target_pairs={{0,8},{4,12},{8,0},{12,4},{1,9},{5,13},{9,1},{13,5},{2,10},{6,14},... | collective-permute-start | bytes 196616 | tf_op jit(solution)/shard_map/ppermute | solution.py:206
  38.3 1.1 %collective-permute-start.12 = (bf16[16,2048]{1,0:T(8,128)(2,1)S(1)}, bf16[16,2048]{1,0:T(8,128)(2,1)S(1)}, u32[]{:S(2)}, u32[]{:S(2)}) collective-permute-start(bf16[16,2048]{1,0:T(8,128)(2,1)S(1)} %get-tuple-element.50.refs_0_), channel_id=1, source_target_pairs={{0,4},{4,0},{8,12},{12,8},{1,5},{5,1},{9,13},{13,9},{2,6},{6,2},{1... | collective-permute-start | bytes 196616 | tf_op jit(solution)/shard_map/ppermute | solution.py:206
  39.4 0.9 %collective-permute-start.13 = (bf16[16,2048]{1,0:T(8,128)(2,1)S(1)}, bf16[16,2048]{1,0:T(8,128)(2,1)S(1)}, u32[]{:S(2)}, u32[]{:S(2)}) collective-permute-start(bf16[16,2048]{1,0:T(8,128)(2,1)S(1)} %get-tuple-element.51.refs_1_), channel_id=1, source_target_pairs={{0,4},{4,0},{8,12},{12,8},{1,5},{5,1},{9,13},{13,9},{2,6},{6,2},{1... | collective-permute-start | bytes 196616 | tf_op jit(solution)/shard_map/ppermute | solution.py:206
  40.3 0.6 %collective-permute-done.14.refs_4_ = bf16[16,2048]{1,0:T(8,128)(2,1)S(1)} collective-permute-done((bf16[16,2048]{1,0:T(8,128)(2,1)S(1)}, bf16[16,2048]{1,0:T(8,128)(2,1)S(1)}, u32[]{:S(2)}, u32[]{:S(2)}) %collective-permute-start.14) | collective-permute-done | bytes 65568 | tf_op jit(solution)/shard_map/ppermute | solution.py:206
  41.0 1.3 %collective-permute-start.16 = (bf16[16,2048]{1,0:T(8,128)(2,1)S(1)}, bf16[16,2048]{1,0:T(8,128)(2,1)S(1)}, u32[]{:S(2)}, u32[]{:S(2)}) collective-permute-start(bf16[16,2048]{1,0:T(8,128)(2,1)S(1)} %collective-permute-done.14.refs_4_), channel_id=1, source_target_pairs={{0,4},{4,0},{8,12},{12,8},{1,5},{5,1},{9,13},{13,9},{2,6},{6,2},{1... | collective-permute-start | bytes 196616 | tf_op jit(solution)/shard_map/ppermute | solution.py:206
  42.3 2.9 %collective-permute-start.17 = (bf16[16,2048]{1,0:T(8,128)(2,1)S(1)}, bf16[16,2048]{1,0:T(8,128)(2,1)S(1)}, u32[]{:S(2)}, u32[]{:S(2)}) collective-permute-start(bf16[16,2048]{1,0:T(8,128)(2,1)S(1)} %collective-permute-done.15.refs_5_), channel_id=1, source_target_pairs={{0,4},{4,0},{8,12},{12,8},{1,5},{5,1},{9,13},{13,9},{2,6},{6,2},{1... | collective-permute-start | bytes 196616 | tf_op jit(solution)/shard_map/ppermute | solution.py:206
  45.2 2.2 %shard_map.89.refs_8_.weight = bf16[2048,1024]{1,0:T(8,128)(2,1)S(1)} custom-call(bf16[4096,2048]{1,0:T(8,128)(2,1)} %weight.5, bf16[32,2048]{1,0:T(8,128)(2,1)S(1)} %get-tuple-element.48.attended), custom_call_target="tpu_custom_call" | custom-call | bytes 4194304 | tf_op jit(solution)/shard_map/pallas_call | solution.py:675
  47.5 0.8 %shard_map.90 = (bf16[128,1024]{1,0:T(8,128)(2,1)S(1)}, bf16[128,2048]{1,0:T(8,128)(2,1)S(1)}) custom-call(bf16[128,128]{1,0:T(8,128)(2,1)S(1)} %get-tuple-element.49.chosen, bf16[16,2048]{1,0:T(8,128)(2,1)S(1)} %get-tuple-element.50.refs_0_, bf16[16,2048]{1,0:T(8,128)(2,1)S(1)} %get-tuple-element.51.refs_1_, ...), custom_call_target="tpu_custom_call" | custom-call | flops 536870912 | bytes 4194304 | tf_op jit(solution)/shard_map/pallas_call | solution.py:392
  48.3 0.0 copy-start
  48.3 0.1 collective-permute-start.18
  48.4 0.7 %shard_map.91.own = f32[128,1024]{1,0:T(8,128)S(1)} custom-call(bf16[128,2048]{1,0:T(8,128)(2,1)S(1)} %get-tuple-element.53.permuted, bf16[2048,1024]{1,0:T(8,128)(2,1)S(1)} %shard_map.89.refs_8_.weight), custom_call_target="tpu_custom_call" | custom-call | flops 536870912 | bytes 4194304 | tf_op jit(solution)/shard_map/pallas_call | solution.py:401
  49.1 0.8 %collective-permute-done.18.received = bf16[128,1024]{1,0:T(8,128)(2,1)S(1)} collective-permute-done((bf16[128,1024]{1,0:T(8,128)(2,1)S(1)}, bf16[128,1024]{1,0:T(8,128)(2,1)S(1)}, u32[]{:S(2)}, u32[]{:S(2)}) %collective-permute-start.18) | collective-permute-done | bytes 262176 | tf_op jit(solution)/shard_map/ppermute | solution.py:206
  50.0 1.6 %collective-permute-start.19 = (bf16[32,1024]{1,0:T(8,128)(2,1)S(1)}, bf16[32,1024]{1,0:T(8,128)(2,1)S(1)}, u32[]{:S(2)}, u32[]{:S(2)}) collective-permute-start(bf16[32,1024]{1,0:T(8,128)(2,1)S(1)} %get-tuple-element.55), channel_id=1, source_target_pairs={{0,8},{4,12},{8,0},{12,4},{1,9},{5,13},{9,1},{13,5},{2,10},{6,14},... | collective-permute-start | bytes 196616 | tf_op jit(solution)/shard_map/ppermute | solution.py:206
  51.6 2.8 %collective-permute-start.20 = (bf16[32,1024]{1,0:T(8,128)(2,1)S(1)}, bf16[32,1024]{1,0:T(8,128)(2,1)S(1)}, u32[]{:S(2)}, u32[]{:S(2)}) collective-permute-start(bf16[32,1024]{1,0:T(8,128)(2,1)S(1)} %get-tuple-element.56), channel_id=1, source_target_pairs={{0,12},{2,4},{4,8},{6,0},{8,14},{10,6},{12,10},{14,2},{1,13},{3,5}... | collective-permute-start | bytes 196616 | tf_op jit(solution)/shard_map/ppermute | solution.py:453
  54.4 1.5 %collective-permute-done.19.passed.refs_0_ = bf16[32,1024]{1,0:T(8,128)(2,1)S(1)} collective-permute-done((bf16[32,1024]{1,0:T(8,128)(2,1)S(1)}, bf16[32,1024]{1,0:T(8,128)(2,1)S(1)}, u32[]{:S(2)}, u32[]{:S(2)}) %collective-permute-start.19) | collective-permute-done | bytes 65568 | tf_op jit(solution)/shard_map/ppermute | solution.py:206
  55.9 1.6 %collective-permute-start.22 = (bf16[32,1024]{1,0:T(8,128)(2,1)S(1)}, bf16[32,1024]{1,0:T(8,128)(2,1)S(1)}, u32[]{:S(2)}, u32[]{:S(2)}) collective-permute-start(bf16[32,1024]{1,0:T(8,128)(2,1)S(1)} %shard_map.93), channel_id=1, source_target_pairs={{0,2},{2,0},{1,3},{3,1},{4,6},{6,4},{5,7},{7,5},{8,10},{10,8},{9,1... | collective-permute-start | bytes 196616 | tf_op jit(solution)/shard_map/ppermute | solution.py:206
  57.5 2.4 %collective-permute-done.21.refs_2_ = bf16[32,1024]{1,0:T(8,128)(2,1)S(1)} collective-permute-done((bf16[32,1024]{1,0:T(8,128)(2,1)S(1)}, bf16[32,1024]{1,0:T(8,128)(2,1)S(1)}, u32[]{:S(2)}, u32[]{:S(2)}) %collective-permute-start.21) | collective-permute-done | bytes 65568 | tf_op jit(solution)/shard_map/ppermute | solution.py:453
  59.9 0.3 collective-permute-done.22.refs_4_
  60.3 0.1 shard_map.94
  60.3 0.1 collective-permute-start.23
  60.4 1.3 %collective-permute-done.23.received = bf16[32,2048]{1,0:T(8,128)(2,1)S(1)} collective-permute-done((bf16[32,2048]{1,0:T(8,128)(2,1)S(1)}, bf16[32,2048]{1,0:T(8,128)(2,1)S(1)}, u32[]{:S(2)}, u32[]{:S(2)}) %collective-permute-start.23) | collective-permute-done | bytes 131104 | tf_op jit(solution)/shard_map/ppermute | solution.py:206
  61.8 0.7 %shard_map.95 = bf16[1,32,4096]{2,1,0:T(8,128)(2,1)} custom-call(bf16[32,2048]{1,0:T(8,128)(2,1)S(1)} %get-tuple-element.59.keep, bf16[32,2048]{1,0:T(8,128)(2,1)S(1)} %collective-permute-done.23.received), custom_call_target="tpu_custom_call" | custom-call | bytes 524288 | tf_op jit(solution)/shard_map/pallas_call | solution.py:696
  (23 shorter events, 0.1 us)
Async XLA Ops:
  0.9 7.9 %collective-permute-start.2 = (bf16[16,2048]{1,0:T(8,128)(2,1)S(1)}, bf16[16,2048]{1,0:T(8,128)(2,1)S(1)}, u32[]{:S(2)}, u32[]{:S(2)}) collective-permute-start(bf16[16,2048]{1,0:T(8,128)(2,1)S(1)} %get-tuple-element.62.refs_0_), channel_id=1, source_target_pairs={{0,8},{4,12},{8,0},{12,4},{1,9},{5,13},{9,1},{13,5},{2,10},{6,14},... | collective-permute-start | bytes 196616 | tf_op jit(solution)/shard_map/ppermute | solution.py:206
  5.0 11.5 %copy-start.1 = (bf16[4096]{0:T(1024)(128)(2,1)S(1)}, bf16[4096]{0:T(1024)(128)(2,1)}, u32[]{:S(2)}) copy-start(bf16[4096]{0:T(1024)(128)(2,1)} %param.9) | copy-start | bytes 24580
  5.0 6.1 %collective-permute-start.3 = (bf16[16,2048]{1,0:T(8,128)(2,1)S(1)}, bf16[16,2048]{1,0:T(8,128)(2,1)S(1)}, u32[]{:S(2)}, u32[]{:S(2)}) collective-permute-start(bf16[16,2048]{1,0:T(8,128)(2,1)S(1)} %get-tuple-element.61.refs_1_), channel_id=1, source_target_pairs={{0,8},{4,12},{8,0},{12,4},{1,9},{5,13},{9,1},{13,5},{2,10},{6,14},... | collective-permute-start | bytes 196616 | tf_op jit(solution)/shard_map/ppermute | solution.py:206
  5.1 11.4 %collective-permute-start = (bf16[16,2048]{1,0:T(8,128)(2,1)S(1)}, bf16[16,2048]{1,0:T(8,128)(2,1)S(1)}, u32[]{:S(2)}, u32[]{:S(2)}) collective-permute-start(bf16[16,2048]{1,0:T(8,128)(2,1)S(1)} %get-tuple-element.62.refs_0_), channel_id=1, source_target_pairs={{0,4},{4,0},{8,12},{12,8},{1,5},{5,1},{9,13},{13,9},{2,6},{6,2},{1... | collective-permute-start | bytes 196616 | tf_op jit(solution)/shard_map/ppermute | solution.py:206
  6.9 9.6 %collective-permute-start.1 = (bf16[16,2048]{1,0:T(8,128)(2,1)S(1)}, bf16[16,2048]{1,0:T(8,128)(2,1)S(1)}, u32[]{:S(2)}, u32[]{:S(2)}) collective-permute-start(bf16[16,2048]{1,0:T(8,128)(2,1)S(1)} %get-tuple-element.61.refs_1_), channel_id=1, source_target_pairs={{0,4},{4,0},{8,12},{12,8},{1,5},{5,1},{9,13},{13,9},{2,6},{6,2},{1... | collective-permute-start | bytes 196616 | tf_op jit(solution)/shard_map/ppermute | solution.py:206
  8.7 7.8 %collective-permute-start.4 = (bf16[16,2048]{1,0:T(8,128)(2,1)S(1)}, bf16[16,2048]{1,0:T(8,128)(2,1)S(1)}, u32[]{:S(2)}, u32[]{:S(2)}) collective-permute-start(bf16[16,2048]{1,0:T(8,128)(2,1)S(1)} %collective-permute-done.2.refs_4_), channel_id=1, source_target_pairs={{0,4},{4,0},{8,12},{12,8},{1,5},{5,1},{9,13},{13,9},{2,6},{6,2},{1... | collective-permute-start | bytes 196616 | tf_op jit(solution)/shard_map/ppermute | solution.py:206
  11.1 5.4 %collective-permute-start.5 = (bf16[16,2048]{1,0:T(8,128)(2,1)S(1)}, bf16[16,2048]{1,0:T(8,128)(2,1)S(1)}, u32[]{:S(2)}, u32[]{:S(2)}) collective-permute-start(bf16[16,2048]{1,0:T(8,128)(2,1)S(1)} %collective-permute-done.3.refs_5_), channel_id=1, source_target_pairs={{0,4},{4,0},{8,12},{12,8},{1,5},{5,1},{9,13},{13,9},{2,6},{6,2},{1... | collective-permute-start | bytes 196616 | tf_op jit(solution)/shard_map/ppermute | solution.py:206
  17.6 12.2 %copy-start.2 = (s32[128]{0:T(128)S(1)}, s32[128]{0:T(128)}, u32[]{:S(2)}) copy-start(s32[128]{0:T(128)} %slots.3) | copy-start | bytes 1540
  17.6 12.2 %copy-start.3 = (s32[32]{0:T(128)S(1)}, s32[32]{0:T(128)}, u32[]{:S(2)}) copy-start(s32[32]{0:T(128)} %lengths.1) | copy-start | bytes 388
  17.6 1.7 %collective-permute-start.6 = (bf16[128,1408]{1,0:T(8,128)(2,1)S(1)}, bf16[128,1408]{1,0:T(8,128)(2,1)S(1)}, u32[]{:S(2)}, u32[]{:S(2)}) collective-permute-start(bf16[128,1408]{1,0:T(8,128)(2,1)S(1)} %get-tuple-element.40.given), channel_id=1, source_target_pairs={{0,1},{1,0},{2,3},{3,2},{4,5},{5,4},{6,7},{7,6},{8,9},{9,8},{10,11... | collective-permute-start | bytes 1081352 | tf_op jit(solution)/shard_map/ppermute | solution.py:206
  19.5 7.8 %collective-permute-start.7 = (bf16[32,1280]{1,0:T(8,128)(2,1)S(1)}, bf16[32,1280]{1,0:T(8,128)(2,1)S(1)}, u32[]{:S(2)}, u32[]{:S(2)}) collective-permute-start(bf16[32,1280]{1,0:T(8,128)(2,1)S(1)} %get-tuple-element.41), channel_id=1, source_target_pairs={{0,8},{4,12},{8,0},{12,4},{1,9},{5,13},{9,1},{13,5},{2,10},{6,14},... | collective-permute-start | bytes 245768 | tf_op jit(solution)/shard_map/ppermute | solution.py:206
  22.6 3.7 %collective-permute-start.10 = (bf16[32,128]{1,0:T(8,128)(2,1)S(1)}, bf16[32,128]{1,0:T(8,128)(2,1)S(1)}, u32[]{:S(2)}, u32[]{:S(2)}) collective-permute-start(bf16[32,128]{1,0:T(8,128)(2,1)S(1)} %get-tuple-element.45.refs_5_), channel_id=1, source_target_pairs={{0,2},{2,0},{1,3},{3,1},{4,6},{6,4},{5,7},{7,5},{8,10},{10,8},{9,1... | collective-permute-start | bytes 24584 | tf_op jit(solution)/shard_map/ppermute | solution.py:206
  24.1 9.4 %collective-permute-start.8 = (bf16[32,1280]{1,0:T(8,128)(2,1)S(1)}, bf16[32,1280]{1,0:T(8,128)(2,1)S(1)}, u32[]{:S(2)}, u32[]{:S(2)}) collective-permute-start(bf16[32,1280]{1,0:T(8,128)(2,1)S(1)} %get-tuple-element.42), channel_id=1, source_target_pairs={{0,12},{2,4},{4,8},{6,0},{8,14},{10,6},{12,10},{14,2},{1,13},{3,5}... | collective-permute-start | bytes 245768 | tf_op jit(solution)/shard_map/ppermute | solution.py:453
  24.5 9.1 %collective-permute-start.9 = (bf16[32,1280]{1,0:T(8,128)(2,1)S(1)}, bf16[32,1280]{1,0:T(8,128)(2,1)S(1)}, u32[]{:S(2)}, u32[]{:S(2)}) collective-permute-start(bf16[32,1280]{1,0:T(8,128)(2,1)S(1)} %get-tuple-element.43), channel_id=1, source_target_pairs={{0,4},{2,12},{4,0},{6,8},{8,6},{10,14},{12,2},{14,10},{1,5},{3,13}... | collective-permute-start | bytes 245768 | tf_op jit(solution)/shard_map/ppermute | solution.py:453
  27.2 6.4 %collective-permute-start.11 = (bf16[32,1280]{1,0:T(8,128)(2,1)S(1)}, bf16[32,1280]{1,0:T(8,128)(2,1)S(1)}, u32[]{:S(2)}, u32[]{:S(2)}) collective-permute-start(bf16[32,1280]{1,0:T(8,128)(2,1)S(1)} %shard_map.87), channel_id=1, source_target_pairs={{0,2},{2,0},{1,3},{3,1},{4,6},{6,4},{5,7},{7,5},{8,10},{10,8},{9,1... | collective-permute-start | bytes 245768 | tf_op jit(solution)/shard_map/ppermute | solution.py:206
  35.3 5.7 %collective-permute-start.14 = (bf16[16,2048]{1,0:T(8,128)(2,1)S(1)}, bf16[16,2048]{1,0:T(8,128)(2,1)S(1)}, u32[]{:S(2)}, u32[]{:S(2)}) collective-permute-start(bf16[16,2048]{1,0:T(8,128)(2,1)S(1)} %get-tuple-element.50.refs_0_), channel_id=1, source_target_pairs={{0,8},{4,12},{8,0},{12,4},{1,9},{5,13},{9,1},{13,5},{2,10},{6,14},... | collective-permute-start | bytes 196616 | tf_op jit(solution)/shard_map/ppermute | solution.py:206
  35.8 6.5 %collective-permute-start.15 = (bf16[16,2048]{1,0:T(8,128)(2,1)S(1)}, bf16[16,2048]{1,0:T(8,128)(2,1)S(1)}, u32[]{:S(2)}, u32[]{:S(2)}) collective-permute-start(bf16[16,2048]{1,0:T(8,128)(2,1)S(1)} %get-tuple-element.51.refs_1_), channel_id=1, source_target_pairs={{0,8},{4,12},{8,0},{12,4},{1,9},{5,13},{9,1},{13,5},{2,10},{6,14},... | collective-permute-start | bytes 196616 | tf_op jit(solution)/shard_map/ppermute | solution.py:206
  38.3 9.1 %collective-permute-start.12 = (bf16[16,2048]{1,0:T(8,128)(2,1)S(1)}, bf16[16,2048]{1,0:T(8,128)(2,1)S(1)}, u32[]{:S(2)}, u32[]{:S(2)}) collective-permute-start(bf16[16,2048]{1,0:T(8,128)(2,1)S(1)} %get-tuple-element.50.refs_0_), channel_id=1, source_target_pairs={{0,4},{4,0},{8,12},{12,8},{1,5},{5,1},{9,13},{13,9},{2,6},{6,2},{1... | collective-permute-start | bytes 196616 | tf_op jit(solution)/shard_map/ppermute | solution.py:206
  39.4 8.0 %collective-permute-start.13 = (bf16[16,2048]{1,0:T(8,128)(2,1)S(1)}, bf16[16,2048]{1,0:T(8,128)(2,1)S(1)}, u32[]{:S(2)}, u32[]{:S(2)}) collective-permute-start(bf16[16,2048]{1,0:T(8,128)(2,1)S(1)} %get-tuple-element.51.refs_1_), channel_id=1, source_target_pairs={{0,4},{4,0},{8,12},{12,8},{1,5},{5,1},{9,13},{13,9},{2,6},{6,2},{1... | collective-permute-start | bytes 196616 | tf_op jit(solution)/shard_map/ppermute | solution.py:206
  41.0 6.5 %collective-permute-start.16 = (bf16[16,2048]{1,0:T(8,128)(2,1)S(1)}, bf16[16,2048]{1,0:T(8,128)(2,1)S(1)}, u32[]{:S(2)}, u32[]{:S(2)}) collective-permute-start(bf16[16,2048]{1,0:T(8,128)(2,1)S(1)} %collective-permute-done.14.refs_4_), channel_id=1, source_target_pairs={{0,4},{4,0},{8,12},{12,8},{1,5},{5,1},{9,13},{13,9},{2,6},{6,2},{1... | collective-permute-start | bytes 196616 | tf_op jit(solution)/shard_map/ppermute | solution.py:206
  42.3 5.2 %collective-permute-start.17 = (bf16[16,2048]{1,0:T(8,128)(2,1)S(1)}, bf16[16,2048]{1,0:T(8,128)(2,1)S(1)}, u32[]{:S(2)}, u32[]{:S(2)}) collective-permute-start(bf16[16,2048]{1,0:T(8,128)(2,1)S(1)} %collective-permute-done.15.refs_5_), channel_id=1, source_target_pairs={{0,4},{4,0},{8,12},{12,8},{1,5},{5,1},{9,13},{13,9},{2,6},{6,2},{1... | collective-permute-start | bytes 196616 | tf_op jit(solution)/shard_map/ppermute | solution.py:206
  48.3 11.9 %copy-start = (bf16[32,4096]{1,0:T(8,128)(2,1)S(1)}, bf16[32,4096]{1,0:T(8,128)(2,1)}, u32[]{:S(2)}) copy-start(bf16[32,4096]{1,0:T(8,128)(2,1)} %hidden.1) | copy-start | bytes 786436
  48.3 1.6 %collective-permute-start.18 = (bf16[128,1024]{1,0:T(8,128)(2,1)S(1)}, bf16[128,1024]{1,0:T(8,128)(2,1)S(1)}, u32[]{:S(2)}, u32[]{:S(2)}) collective-permute-start(bf16[128,1024]{1,0:T(8,128)(2,1)S(1)} %get-tuple-element.54.given), channel_id=1, source_target_pairs={{0,1},{1,0},{2,3},{3,2},{4,5},{5,4},{6,7},{7,6},{8,9},{9,8},{10,11... | collective-permute-start | bytes 786440 | tf_op jit(solution)/shard_map/ppermute | solution.py:206
  50.0 5.9 %collective-permute-start.19 = (bf16[32,1024]{1,0:T(8,128)(2,1)S(1)}, bf16[32,1024]{1,0:T(8,128)(2,1)S(1)}, u32[]{:S(2)}, u32[]{:S(2)}) collective-permute-start(bf16[32,1024]{1,0:T(8,128)(2,1)S(1)} %get-tuple-element.55), channel_id=1, source_target_pairs={{0,8},{4,12},{8,0},{12,4},{1,9},{5,13},{9,1},{13,5},{2,10},{6,14},... | collective-permute-start | bytes 196616 | tf_op jit(solution)/shard_map/ppermute | solution.py:206
  51.6 6.0 %collective-permute-start.20 = (bf16[32,1024]{1,0:T(8,128)(2,1)S(1)}, bf16[32,1024]{1,0:T(8,128)(2,1)S(1)}, u32[]{:S(2)}, u32[]{:S(2)}) collective-permute-start(bf16[32,1024]{1,0:T(8,128)(2,1)S(1)} %get-tuple-element.56), channel_id=1, source_target_pairs={{0,12},{2,4},{4,8},{6,0},{8,14},{10,6},{12,10},{14,2},{1,13},{3,5}... | collective-permute-start | bytes 196616 | tf_op jit(solution)/shard_map/ppermute | solution.py:453
  54.4 5.6 %collective-permute-start.21 = (bf16[32,1024]{1,0:T(8,128)(2,1)S(1)}, bf16[32,1024]{1,0:T(8,128)(2,1)S(1)}, u32[]{:S(2)}, u32[]{:S(2)}) collective-permute-start(bf16[32,1024]{1,0:T(8,128)(2,1)S(1)} %get-tuple-element.57), channel_id=1, source_target_pairs={{0,4},{2,12},{4,0},{6,8},{8,6},{10,14},{12,2},{14,10},{1,5},{3,13}... | collective-permute-start | bytes 196616 | tf_op jit(solution)/shard_map/ppermute | solution.py:453
  55.9 4.3 %collective-permute-start.22 = (bf16[32,1024]{1,0:T(8,128)(2,1)S(1)}, bf16[32,1024]{1,0:T(8,128)(2,1)S(1)}, u32[]{:S(2)}, u32[]{:S(2)}) collective-permute-start(bf16[32,1024]{1,0:T(8,128)(2,1)S(1)} %shard_map.93), channel_id=1, source_target_pairs={{0,2},{2,0},{1,3},{3,1},{4,6},{6,4},{5,7},{7,5},{8,10},{10,8},{9,1... | collective-permute-start | bytes 196616 | tf_op jit(solution)/shard_map/ppermute | solution.py:206
  60.3 1.4 %collective-permute-start.23 = (bf16[32,2048]{1,0:T(8,128)(2,1)S(1)}, bf16[32,2048]{1,0:T(8,128)(2,1)S(1)}, u32[]{:S(2)}, u32[]{:S(2)}) collective-permute-start(bf16[32,2048]{1,0:T(8,128)(2,1)S(1)} %get-tuple-element.60), channel_id=1, source_target_pairs={{0,1},{1,0},{2,3},{3,2},{4,5},{5,4},{6,7},{7,6},{8,9},{9,8},{10,11... | collective-permute-start | bytes 393224 | tf_op jit(solution)/shard_map/ppermute | solution.py:206
